TPU v7x, 32 devices: a whole 2x2x4 slice. The times are simulated.
32 devices in a mesh: groups: 2 (over x), patch: 16 (over z, y, core).
Axes of the slice: x: 2, y: 2, z: 4, core: 2. Of those that a mesh axis runs over, the one named last changes fastest.
Arguments:
- node_features: bfloat16 [4, 2048, 512], P('groups', 'patch'), parts along dimension 0, may hold values from -6 to 6
- out_grad: bfloat16 [4, 2048, 512], P('groups', 'patch'), parts along dimension 0, may hold values from -6 to 6
- w_query: bfloat16 [512, 512], replicated, may hold values from -0.25 to 0.25
- w_key: bfloat16 [512, 512], replicated, may hold values from -0.25 to 0.25
- w_value: bfloat16 [512, 512], replicated, may hold values from -0.25 to 0.25
- w_out: bfloat16 [512, 512], replicated, may hold values from -0.25 to 0.25
- neighbours: int32 [2048, 256], P('patch'), may hold values from 0 to 255, as said below
- neighbour_count: int32 [2048], P('patch'), may hold values from 128 to 256
- send_rows: int32 [16, 8, 16], P('patch'), may hold values from 0 to 127, as said below
Outputs:
- node_grad: bfloat16 [4, 2048, 512], P('groups', 'patch'), parts along dimension 0
- weight_grad: float32 [1024, 2048], P(('groups', 'patch')), parts along dimension 0
There are 2 independent parts, one for each index of `groups`. A program takes and returns all parts, laid end to end along the dimension named above; an argument that names none is the same for every part. Nothing has to cross between parts.
Inputs may be any that keep to these rules, and one draw needn't show every extreme that they name: Each row holds 256 distinct columns of its patch's extended table; only the first neighbour_count entries are neighbours. `send_rows`: entry [q, k, s] is a row of patch q's block of nodes; the 16 rows for one pair (q, k) are distinct.
All inputs are finite; a program needn't handle non-finite values.
Results may differ from a plain program's by a relative error of at most 0.0086.
Values may be sent and summed in bfloat16 or wider, within the bound.
No kernel may reach another device: no remote copies, remote signals or barrier semaphores. Data moves between devices by JAX's collectives and lax.ppermute only.
A program may use at most 64 MiB of HBM per device.

v0:
```python
import math

import jax
import jax.numpy as jnp
from jax import lax
from jax.sharding import PartitionSpec as P

HEADS = 16


score_cap = 5.0


def shifted(shard, axis, by):
    count = lax.axis_size(axis)
    return lax.ppermute(shard, axis, [(i, (i + by) % count) for i in range(count)])


def times_transpose(left_rows, weight):
    return lax.dot_general(
        left_rows, weight, (((1,), (1,)), ((), ())), preferred_element_type=jnp.float32
    )


def project(inputs_rows, weight):
    return jnp.dot(inputs_rows, weight, preferred_element_type=jnp.float32).astype(jnp.bfloat16)


def build_mask(neighbours, neighbour_count, table_size):
    is_valid = jnp.arange(neighbours.shape[1], dtype=jnp.int32)[None, :] < neighbour_count[:, None]
    target = jnp.where(is_valid, neighbours, table_size)
    columns = jnp.arange(table_size, dtype=jnp.int32)[None, None, :]
    return jnp.any(target[:, :, None] == columns, axis=1).astype(jnp.float32)


def member_backward(query_rows, key_table, value_table, grad_rows, neighbour_mask):
    node_rows, model_width = query_rows.shape
    table_size = key_table.shape[0]
    head_size = model_width // HEADS
    query_heads = query_rows.reshape(node_rows, HEADS, head_size)
    key_heads = key_table.reshape(table_size, HEADS, head_size)
    value_heads = value_table.reshape(table_size, HEADS, head_size)
    grad_heads = grad_rows.reshape(node_rows, HEADS, head_size)
    raw_scores = jnp.einsum(
        "rhd,chd->hrc", query_heads, key_heads, preferred_element_type=jnp.float32
    ) / math.sqrt(head_size)
    capped = score_cap * jnp.tanh(raw_scores / score_cap)
    score_exp = jnp.exp(capped) * neighbour_mask[None]
    attn_prob = score_exp / jnp.sum(score_exp, axis=-1, keepdims=True)
    attn_prob_b = attn_prob.astype(jnp.bfloat16)
    attended = (
        jnp.einsum("hrc,chd->rhd", attn_prob_b, value_heads, preferred_element_type=jnp.float32)
        .reshape(node_rows, model_width)
        .astype(jnp.bfloat16)
    )
    prob_grad = jnp.einsum(
        "rhd,chd->hrc", grad_heads, value_heads, preferred_element_type=jnp.float32
    )
    row_inner = jnp.sum(attn_prob * prob_grad, axis=-1, keepdims=True)
    slope = 1.0 - capped / score_cap * (capped / score_cap)
    score_grad = (attn_prob * (prob_grad - row_inner) * slope / math.sqrt(head_size)).astype(
        jnp.bfloat16
    )
    d_query = (
        jnp.einsum("hrc,chd->rhd", score_grad, key_heads, preferred_element_type=jnp.float32)
        .reshape(node_rows, model_width)
        .astype(jnp.bfloat16)
    )
    d_key = (
        jnp.einsum("hrc,rhd->chd", score_grad, query_heads, preferred_element_type=jnp.float32)
        .reshape(table_size, model_width)
        .astype(jnp.bfloat16)
    )
    d_value = (
        jnp.einsum("hrc,rhd->chd", attn_prob_b, grad_heads, preferred_element_type=jnp.float32)
        .reshape(table_size, model_width)
        .astype(jnp.bfloat16)
    )
    return (attended, d_query, d_key, d_value)


def weight_block(operand_pairs):
    blocks = []
    for inputs_side, grads_side in operand_pairs:
        blocks.append(
            lax.dot_general(
                inputs_side,
                grads_side,
                (((0,), (0,)), ((), ())),
                preferred_element_type=jnp.float32,
            )
        )
    return jnp.concatenate(blocks, axis=1)


def body(
    node_features, out_grad, w_query, w_key, w_value, w_out, neighbours, neighbour_count, send_rows
):
    members, node_rows, model_width = node_features.shape
    patch_count = lax.axis_size("patch")
    row_width = min(8, patch_count // 4)
    offsets = [
        1,
        -1,
        row_width,
        -row_width,
        row_width - 1,
        1 - row_width,
        row_width + 1,
        -row_width - 1,
    ]
    adjacent = send_rows.shape[1]
    slot_count = send_rows.shape[2]
    halo_rows = adjacent * slot_count
    table_size = node_rows + halo_rows
    flat_nodes = node_features.reshape(members * node_rows, model_width)
    out_flat = out_grad.reshape(members * node_rows, model_width)
    query_rows = project(flat_nodes, w_query).reshape(members, node_rows, model_width)
    key_rows = project(flat_nodes, w_key).reshape(members, node_rows, model_width)
    value_rows = project(flat_nodes, w_value).reshape(members, node_rows, model_width)
    sent_index = send_rows[0].reshape(halo_rows)
    sent_nodes = node_features[:, sent_index]
    outgoing = jnp.stack([key_rows[:, sent_index], value_rows[:, sent_index]]).reshape(
        2, members, adjacent, slot_count, model_width
    )
    incoming = jnp.stack(
        [
            shifted(outgoing[:, :, direction], "patch", offsets[direction])
            for direction in range(adjacent)
        ],
        axis=2,
    )
    halo_key = incoming[0].reshape(members, halo_rows, model_width)
    halo_value = incoming[1].reshape(members, halo_rows, model_width)
    halo_inputs = sent_nodes.reshape(members * halo_rows, model_width)
    key_table = jnp.concatenate([key_rows, halo_key], axis=1)
    value_table = jnp.concatenate([value_rows, halo_value], axis=1)
    neighbour_mask = build_mask(neighbours, neighbour_count, table_size)
    grad_attended = (
        times_transpose(out_flat, w_out)
        .astype(jnp.bfloat16)
        .reshape(members, node_rows, model_width)
    )
    results = [
        member_backward(
            query_rows[member],
            key_table[member],
            value_table[member],
            grad_attended[member],
            neighbour_mask,
        )
        for member in range(members)
    ]
    attended = jnp.concatenate([result[0] for result in results], axis=0)
    d_query = jnp.concatenate([result[1] for result in results], axis=0)
    d_key = jnp.stack([result[2] for result in results])
    d_value = jnp.stack([result[3] for result in results])
    local_key_grad = d_key[:, :node_rows].reshape(members * node_rows, model_width)
    local_value_grad = d_value[:, :node_rows].reshape(members * node_rows, model_width)
    halo_key_grad = d_key[:, node_rows:]
    halo_value_grad = d_value[:, node_rows:]
    node_grad = (
        times_transpose(d_query, w_query)
        + times_transpose(local_key_grad, w_key)
        + times_transpose(local_value_grad, w_value)
    )
    leaving = jnp.stack([halo_key_grad, halo_value_grad]).reshape(
        2, members, adjacent, slot_count, model_width
    )
    back = jnp.stack(
        [
            shifted(leaving[:, :, direction], "patch", -offsets[direction])
            for direction in range(adjacent)
        ],
        axis=2,
    )
    returned_key = back[0].reshape(members * halo_rows, model_width)
    returned_value = back[1].reshape(members * halo_rows, model_width)
    arriving = times_transpose(returned_key, w_key) + times_transpose(returned_value, w_value)
    kv_key_grad = jnp.concatenate([local_key_grad, returned_key], axis=0)
    kv_value_grad = jnp.concatenate([local_value_grad, returned_value], axis=0)
    kv_inputs = jnp.concatenate([flat_nodes, halo_inputs], axis=0)
    node_total = (
        node_grad.reshape(members, node_rows, model_width)
        .at[:, sent_index]
        .add(arriving.reshape(members, halo_rows, model_width))
    )
    weight_grad = lax.psum_scatter(
        weight_block(
            (
                (flat_nodes, d_query),
                (kv_inputs, kv_key_grad),
                (kv_inputs, kv_value_grad),
                (attended, out_flat),
            )
        ),
        "patch",
        scatter_dimension=0,
        tiled=True,
    )
    return (node_total.astype(jnp.bfloat16), weight_grad)


def solution(mesh):
    in_specs = (
        P("groups", "patch", None),
        P("groups", "patch", None),
        P(),
        P(),
        P(),
        P(),
        P("patch", None),
        P("patch"),
        P("patch", None, None),
    )
    out_specs = (P("groups", "patch", None), P(("groups", "patch"), None))
    return jax.shard_map(body, mesh=mesh, in_specs=in_specs, out_specs=out_specs, check_vma=False)
```

profile of v0, /device:TPU:0, one launch (start us, length us, event | category | flops | bytes accessed | tf_op | source)
XLA Modules:
  0.0 240.2 jit_solution(13959889902285776275)
XLA Ops:
  7.2 0.8 reshape_squeeze.39
  8.1 1.4 convolution_convert_fusion.6
  9.8 1.3 convolution_convert_fusion.7
  11.4 1.1 gather_fusion.1
  12.6 1.1 gather_fusion
  13.7 0.9 maximum_bitcast_fusion
  14.7 2.5 %collective-permute-start.6 = (bf16[2,2,16,512]{3,1,2,0:T(2,128)(2,1)}, bf16[2,2,16,512]{3,1,2,0:T(2,128)(2,1)S(1)}, u32[]{:S(2)}, u32[]{:S(2)}) collective-permute-start(bf16[2,2,16,512]{3,1,2,0:T(2,128)(2,1)} %get-tuple-element.37), channel_id=1, source_target_pairs={{0,5},{1,6},{2,7},{3,8},{4,9},{5,10},{6,11},{7,12},{8,13},{9,14},{... | collective-permute-start | bytes 196616 | tf_op jit(solution)/shard_map/ppermute | solution.py:16
  17.1 2.8 %collective-permute-start.4 = (bf16[2,2,16,512]{3,1,2,0:T(2,128)(2,1)}, bf16[2,2,16,512]{3,1,2,0:T(2,128)(2,1)}, u32[]{:S(2)}, u32[]{:S(2)}) collective-permute-start(bf16[2,2,16,512]{3,1,2,0:T(2,128)(2,1)} %get-tuple-element.38), channel_id=1, source_target_pairs={{0,3},{1,4},{2,5},{3,6},{4,7},{5,8},{6,9},{7,10},{8,11},{9,12},{10... | collective-permute-start | bytes 196616 | tf_op jit(solution)/shard_map/ppermute | solution.py:16
  19.9 0.8 collective-permute-start.5
  20.7 1.1 fusion.59
  22.1 2.2 collective-permute-start
  24.4 5.7 %fusion.2 = pred[128,256]{1,0:T(8,128)(4,1)S(1)} fusion(s32[128,256]{1,0:T(8,128)S(1)} %fusion.50), kind=kLoop, calls=%fused_computation.7 | loop fusion | flops 16744448 | bytes 163840 | tf_op jit(solution)/shard_map/reduce_or | solution.py:33
  30.9 2.2 gather_fusion.2
  33.8 0.8 copy.125
  34.7 0.8 copy.124
  35.5 0.8 copy.129
  36.3 2.2 collective-permute-start.1
  38.5 0.9 bitcast_dynamic-update-slice_fusion.15
  39.3 1.0 collective-permute-done.1
  40.6 6.2 %collective-permute-done.2 = bf16[2,2,16,512]{3,1,2,0:T(2,128)(2,1)S(1)} collective-permute-done((bf16[2,2,16,512]{3,1,2,0:T(2,128)(2,1)S(1)}, bf16[2,2,16,512]{3,1,2,0:T(2,128)(2,1)S(1)}, u32[]{:S(2)}, u32[]{:S(2)}) %collective-permute-start.2) | collective-permute-done | bytes 65568 | tf_op jit(solution)/shard_map/ppermute | solution.py:16
  47.4 3.7 %collective-permute-done.3 = bf16[2,2,16,512]{3,1,2,0:T(2,128)(2,1)S(1)} collective-permute-done((bf16[2,2,16,512]{3,1,2,0:T(2,128)(2,1)S(1)}, bf16[2,2,16,512]{3,1,2,0:T(2,128)(2,1)S(1)}, u32[]{:S(2)}, u32[]{:S(2)}) %collective-permute-start.3) | collective-permute-done | bytes 65568 | tf_op jit(solution)/shard_map/ppermute | solution.py:16
  51.2 0.9 bitcast_dynamic-update-slice_fusion.11
  52.8 0.7 fusion.43
  53.5 0.8 copy.131
  54.4 0.9 copy.123
  55.3 0.8 copy.128
  56.2 1.6 fusion.106
  57.7 2.7 %fusion.107 = f32[16,128,256]{2,1,0:T(8,128)} fusion(bf16[128,16,32]{0,2,1:T(8,128)(2,1)S(1)} %bitcast.231, bf16[256,16,32]{0,2,1:T(8,128)(2,1)} %bitcast.209), kind=kOutput, calls=%fused_computation.170 | convolution fusion | flops 33554432 | bytes 2490368 | tf_op jit(solution)/shard_map/rhd,chd->hrc/dot_general | solution.py:56
  60.5 2.6 %fusion.10 = (f32[16,128]{1,0:T(8,128)S(1)}, f32[16,128]{1,0:T(8,128)S(1)}, f32[16,128,256]{2,1,0:T(8,128)}) fusion(f32[128,256]{1,0:T(8,128)S(1)} %copy-done.18, f32[16,128,256]{2,1,0:T(8,128)S(1)} %fusion.106, bf16[128,16,32]{0,2,1:T(8,128)(2,1)S(1)} %bitcast.246, bf16[256,16,32]{0,2,1:T(8,128)(2,1)S(1)} %bitcast.239), kind=kOutput, calls=%fused_computation.20 | convolution fusion | flops 37744640 | bytes 4734976 | tf_op jit(solution)/shard_map/rhd,chd->hrc/dot_general | solution.py:44
  63.7 1.6 convolution_convert_fusion.8
  65.3 13.5 %convolution_convert_fusion.10 = bf16[16,32,128]{2,1,0:T(8,128)(2,1)S(1)} fusion(bf16[256,16,32]{0,2,1:T(8,128)(2,1)} %bitcast.212, f32[16,128,256]{2,1,0:T(8,128)} %fusion.107, f32[16,128,256]{2,1,0:T(8,128)S(1)} %fusion.106, f32[16,128]{1,0:T(8,128)} %copy-done.25, f32[128,256]{1,0:T(8,128)} %convert_element_type.137), kind=kOutput, calls=%fused_computation.37 | convolution fusion | flops 42010880 | bytes 4726784 | tf_op jit(solution)/shard_map/hrc,chd->rhd/dot_general | solution.py:65
  78.8 14.3 %convolution_convert_fusion.2 = bf16[16,32,256]{2,1,0:T(8,128)(2,1)} fusion(bf16[128,16,32]{0,2,1:T(8,128)(2,1)} %bitcast.234, f32[16,128,256]{2,1,0:T(8,128)} %fusion.107, f32[16,128,256]{2,1,0:T(8,128)S(1)} %fusion.106, f32[16,128]{1,0:T(8,128)} %copy-done.25, f32[128,256]{1,0:T(8,128)} %convert_element_type.137), kind=kOutput, calls=%fused_computation.29 | convolution fusion | flops 42076416 | bytes 4726784 | tf_op jit(solution)/shard_map/hrc,rhd->chd/dot_general | solution.py:70
  93.0 2.5 %convolution_convert_fusion = bf16[16,32,256]{2,1,0:T(8,128)(2,1)} fusion(bf16[128,16,32]{0,2,1:T(8,128)(2,1)} %bitcast.232, f32[16,128,256]{2,1,0:T(8,128)S(1)} %fusion.106, f32[16,128]{1,0:T(8,128)} %copy-done.25, f32[128,256]{1,0:T(8,128)} %convert_element_type.137), kind=kOutput, calls=%fused_computation.27 | convolution fusion | flops 36306944 | bytes 2629632 | tf_op jit(solution)/shard_map/hrc,rhd->chd/dot_general | solution.py:75
  95.6 1.8 copy.127
  97.4 1.8 fusion.105
  99.1 3.2 %convolution_convert_fusion.9 = bf16[16,32,128]{2,1,0:T(8,128)(2,1)} fusion(bf16[256,16,32]{0,2,1:T(8,128)(2,1)S(1)} %bitcast.214, f32[16,128,256]{2,1,0:T(8,128)} %get-tuple-element.44, f32[16,128]{1,0:T(8,128)S(1)} %get-tuple-element.10, f32[128,256]{1,0:T(8,128)} %convert_element_type.137), kind=kOutput, calls=%fused_computation.36 | convolution fusion | flops 36241408 | bytes 2629632 | tf_op jit(solution)/shard_map/hrc,chd->rhd/dot_general | solution.py:52
  102.4 14.2 %convolution_convert_fusion.11 = bf16[16,32,128]{2,1,0:T(8,128)(2,1)} fusion(bf16[256,16,32]{0,2,1:T(8,128)(2,1)} %bitcast.238, f32[16,128,256]{2,1,0:T(8,128)S(1)} %fusion.105, f32[16,128,256]{2,1,0:T(8,128)} %get-tuple-element.44, f32[16,128]{1,0:T(8,128)S(1)} %get-tuple-element.10, f32[128,256]{1,0:T(8,128)} %convert_element_type.137), kind=kOutput, calls=%fused_computation.38 | convolution fusion | flops 42010880 | bytes 4726784 | tf_op jit(solution)/shard_map/hrc,chd->rhd/dot_general | solution.py:65
  116.5 14.2 %convolution_convert_fusion.3 = bf16[16,32,256]{2,1,0:T(8,128)(2,1)} fusion(bf16[128,16,32]{0,2,1:T(8,128)(2,1)} %bitcast.245, f32[16,128,256]{2,1,0:T(8,128)S(1)} %fusion.105, f32[16,128,256]{2,1,0:T(8,128)} %get-tuple-element.44, f32[16,128]{1,0:T(8,128)S(1)} %get-tuple-element.10, f32[128,256]{1,0:T(8,128)} %convert_element_type.137), kind=kOutput, calls=%fused_computation.30 | convolution fusion | flops 42076416 | bytes 4726784 | tf_op jit(solution)/shard_map/hrc,rhd->chd/dot_general | solution.py:70
  130.8 2.6 %convolution_convert_fusion.1 = bf16[16,32,256]{2,1,0:T(8,128)(2,1)S(1)} fusion(bf16[128,16,32]{0,2,1:T(8,128)(2,1)} %bitcast.230, f32[16,128,256]{2,1,0:T(8,128)} %get-tuple-element.44, f32[16,128]{1,0:T(8,128)S(1)} %get-tuple-element.10, f32[128,256]{1,0:T(8,128)} %convert_element_type.137), kind=kOutput, calls=%fused_computation.28 | convolution fusion | flops 36306944 | bytes 2629632 | tf_op jit(solution)/shard_map/hrc,rhd->chd/dot_general | solution.py:75
  134.3 2.7 %collective-permute-start.8 = (bf16[2,2,16,512]{3,2,1,0:T(8,128)(2,1)S(1)}, bf16[2,2,16,512]{3,2,1,0:T(8,128)(2,1)S(1)}, u32[]{:S(2)}, u32[]{:S(2)}) collective-permute-start(bf16[2,2,16,512]{3,2,1,0:T(8,128)(2,1)S(1)} %get-tuple-element.15), channel_id=1, source_target_pairs={{0,15},{1,0},{2,1},{3,2},{4,3},{5,4},{6,5},{7,6},{8,7},{9,8},{10,9... | collective-permute-start | bytes 196616 | tf_op jit(solution)/shard_map/ppermute | solution.py:16
  137.0 2.3 collective-permute-start.10
  140.0 4.2 %collective-permute-start.12 = (bf16[2,2,16,512]{3,2,1,0:T(8,128)(2,1)S(1)}, bf16[2,2,16,512]{3,2,1,0:T(8,128)(2,1)S(1)}, u32[]{:S(2)}, u32[]{:S(2)}) collective-permute-start(bf16[2,2,16,512]{3,2,1,0:T(8,128)(2,1)S(1)} %get-tuple-element.19), channel_id=1, source_target_pairs={{0,13},{1,14},{2,15},{3,0},{4,1},{5,2},{6,3},{7,4},{8,5},{9,6},{10... | collective-permute-start | bytes 196616 | tf_op jit(solution)/shard_map/ppermute | solution.py:16
  144.9 1.2 collective-permute-done.11
  146.7 3.4 %collective-permute-done.13 = bf16[2,2,16,512]{3,2,1,0:T(8,128)(2,1)S(1)} collective-permute-done((bf16[2,2,16,512]{3,2,1,0:T(8,128)(2,1)S(1)}, bf16[2,2,16,512]{3,2,1,0:T(8,128)(2,1)S(1)}, u32[]{:S(2)}, u32[]{:S(2)}) %collective-permute-start.13) | collective-permute-done | bytes 65568 | tf_op jit(solution)/shard_map/ppermute | solution.py:16
  151.3 2.4 pad_maximum_fusion
  153.7 5.4 %copy.148 = f32[512,2048]{1,0:T(8,128)} copy(f32[512,2048]{0,1:T(8,128)} %pad_maximum_fusion) | data formatting | bytes 8388608
  162.0 5.5 %scatter_fusion = f32[2,128,512]{2,0,1:T(2,128)S(1)} fusion(f32[2,128,512]{2,0,1:T(2,128)S(1)} %copy.145, s32[128]{0:T(128)S(1)} %fusion.67, f32[128,2,512]{2,1,0:T(2,128)S(1)} %bitcast.204), kind=kCustom, calls=%fused_computation.3 | custom fusion | flops 131072 | bytes 1573376 | tf_op jit(solution)/shard_map/scatter-add | solution.py:186
  168.5 64.9 %reduce-scatter.4.cloned.1.call-done = f32[32,2048]{1,0:T(8,128)} async-done(((f32[512,2048]{1,0:T(8,128)}), f32[32,2048]{1,0:T(8,128)}) %reduce-scatter.4.cloned.1.call-update) | async-done | bytes 262160
  (125 shorter events, 12.1 us)
Async XLA Ops:
  7.2 2.6 %copy-start = (bf16[512,512]{1,0:T(8,128)(2,1)S(1)}, bf16[512,512]{1,0:T(8,128)(2,1)}, u32[]{:S(2)}) copy-start(bf16[512,512]{1,0:T(8,128)(2,1)} %param.12) | copy-start | bytes 1572868
  7.2 226.2 %reduce-scatter.4.cloned.1.call-start = ((), (), s32[]{:S(2)}) async-start(), calls=%async_computation.1 | async-start | bytes 4456448
  9.8 14.6 %copy-start.19 = (s32[128,256]{1,0:T(8,128)S(1)}, s32[128,256]{1,0:T(8,128)}, u32[]{:S(2)}) copy-start(s32[128,256]{1,0:T(8,128)} %param.15) | copy-start | bytes 393220
  9.8 14.6 %copy-start.24 = (s32[128]{0:T(128)S(1)}, s32[128]{0:T(128)}, u32[]{:S(2)}) copy-start(s32[128]{0:T(128)} %param.16) | copy-start | bytes 1540
  9.8 20.4 %copy-start.6 = (bf16[2,128,512]{2,1,0:T(8,128)(2,1)S(1)}, bf16[2,128,512]{2,1,0:T(8,128)(2,1)}, u32[]{:S(2)}) copy-start(bf16[2,128,512]{2,1,0:T(8,128)(2,1)} %param.10) | copy-start | bytes 786436
  9.8 20.4 %copy-start.10 = (bf16[512,512]{1,0:T(8,128)(2,1)S(1)}, bf16[512,512]{1,0:T(8,128)(2,1)}, u32[]{:S(2)}) copy-start(bf16[512,512]{1,0:T(8,128)(2,1)} %param.14) | copy-start | bytes 1572868
  12.6 18.0 %copy-start.1 = (bf16[2,128,512]{2,1,0:T(8,128)(2,1)S(1)}, bf16[2,128,512]{2,1,0:T(8,128)(2,1)}, u32[]{:S(2)}) copy-start(bf16[2,128,512]{2,1,0:T(8,128)(2,1)} %param.9) | copy-start | bytes 786436
  12.6 18.0 %copy-start.3 = (bf16[512,512]{1,0:T(8,128)(2,1)S(1)}, bf16[512,512]{1,0:T(8,128)(2,1)}, u32[]{:S(2)}) copy-start(bf16[512,512]{1,0:T(8,128)(2,1)} %param.11) | copy-start | bytes 1572868
  14.7 37.5 %collective-permute-start.6 = (bf16[2,2,16,512]{3,1,2,0:T(2,128)(2,1)}, bf16[2,2,16,512]{3,1,2,0:T(2,128)(2,1)S(1)}, u32[]{:S(2)}, u32[]{:S(2)}) collective-permute-start(bf16[2,2,16,512]{3,1,2,0:T(2,128)(2,1)} %get-tuple-element.37), channel_id=1, source_target_pairs={{0,5},{1,6},{2,7},{3,8},{4,9},{5,10},{6,11},{7,12},{8,13},{9,14},{... | collective-permute-start | bytes 196616 | tf_op jit(solution)/shard_map/ppermute | solution.py:16
  17.1 34.1 %collective-permute-start.4 = (bf16[2,2,16,512]{3,1,2,0:T(2,128)(2,1)}, bf16[2,2,16,512]{3,1,2,0:T(2,128)(2,1)}, u32[]{:S(2)}, u32[]{:S(2)}) collective-permute-start(bf16[2,2,16,512]{3,1,2,0:T(2,128)(2,1)} %get-tuple-element.38), channel_id=1, source_target_pairs={{0,3},{1,4},{2,5},{3,6},{4,7},{5,8},{6,9},{7,10},{8,11},{9,12},{10... | collective-permute-start | bytes 196616 | tf_op jit(solution)/shard_map/ppermute | solution.py:16
  19.9 32.2 %collective-permute-start.5 = (bf16[2,2,16,512]{3,1,2,0:T(2,128)(2,1)}, bf16[2,2,16,512]{3,1,2,0:T(2,128)(2,1)S(1)}, u32[]{:S(2)}, u32[]{:S(2)}) collective-permute-start(bf16[2,2,16,512]{3,1,2,0:T(2,128)(2,1)} %get-tuple-element.39), channel_id=1, source_target_pairs={{0,13},{1,14},{2,15},{3,0},{4,1},{5,2},{6,3},{7,4},{8,5},{9,6},{10... | collective-permute-start | bytes 196616 | tf_op jit(solution)/shard_map/ppermute | solution.py:16
  21.8 30.5 %collective-permute-start.7 = (bf16[2,2,16,512]{3,1,2,0:T(2,128)(2,1)}, bf16[2,2,16,512]{3,1,2,0:T(2,128)(2,1)S(1)}, u32[]{:S(2)}, u32[]{:S(2)}) collective-permute-start(bf16[2,2,16,512]{3,1,2,0:T(2,128)(2,1)} %get-tuple-element.32), channel_id=1, source_target_pairs={{0,11},{1,12},{2,13},{3,14},{4,15},{5,0},{6,1},{7,2},{8,3},{9,4},{... | collective-permute-start | bytes 196616 | tf_op jit(solution)/shard_map/ppermute | solution.py:16
  22.1 14.2 %collective-permute-start = (bf16[2,2,16,512]{3,1,2,0:T(2,128)(2,1)}, bf16[2,2,16,512]{3,1,2,0:T(2,128)(2,1)}, u32[]{:S(2)}, u32[]{:S(2)}) collective-permute-start(bf16[2,2,16,512]{3,1,2,0:T(2,128)(2,1)} %get-tuple-element.33), channel_id=1, source_target_pairs={{0,1},{1,2},{2,3},{3,4},{4,5},{5,6},{6,7},{7,8},{8,9},{9,10},{10,1... | collective-permute-start | bytes 196616 | tf_op jit(solution)/shard_map/ppermute | solution.py:16
  30.9 5.4 %copy-start.23 = (bf16[2,2,16,512]{3,1,2,0:T(2,128)(2,1)S(1)}, bf16[2,2,16,512]{3,1,2,0:T(2,128)(2,1)}, u32[]{:S(2)}) copy-start(bf16[2,2,16,512]{3,1,2,0:T(2,128)(2,1)} %get-tuple-element.34) | copy-start | bytes 196612
  30.9 9.5 %copy-start.22 = (bf16[2,2,16,512]{3,1,2,0:T(2,128)(2,1)S(1)}, bf16[2,2,16,512]{3,1,2,0:T(2,128)(2,1)}, u32[]{:S(2)}) copy-start(bf16[2,2,16,512]{3,1,2,0:T(2,128)(2,1)} %get-tuple-element.35) | copy-start | bytes 196612
  30.9 16.0 %copy-start.21 = (bf16[2,2,16,512]{3,1,2,0:T(2,128)(2,1)S(1)}, bf16[2,2,16,512]{3,1,2,0:T(2,128)(2,1)}, u32[]{:S(2)}) copy-start(bf16[2,2,16,512]{3,1,2,0:T(2,128)(2,1)} %get-tuple-element.36) | copy-start | bytes 196612
  34.7 23.0 %copy-start.9 = (bf16[128,512]{0,1:T(8,128)(2,1)}, bf16[128,512]{0,1:T(8,128)(2,1)S(1)}, u32[]{:S(2)}) copy-start(bf16[128,512]{0,1:T(8,128)(2,1)S(1)} %copy.130) | copy-start | bytes 393220
  36.3 4.1 %collective-permute-start.1 = (bf16[2,2,16,512]{3,1,2,0:T(2,128)(2,1)S(1)}, bf16[2,2,16,512]{3,1,2,0:T(2,128)(2,1)S(1)}, u32[]{:S(2)}, u32[]{:S(2)}) collective-permute-start(bf16[2,2,16,512]{3,1,2,0:T(2,128)(2,1)S(1)} %copy-done.23), channel_id=1, source_target_pairs={{0,15},{1,0},{2,1},{3,2},{4,3},{5,4},{6,5},{7,6},{8,7},{9,8},{10,9... | collective-permute-start | bytes 196616 | tf_op jit(solution)/shard_map/ppermute | solution.py:16
  40.4 6.5 %collective-permute-start.2 = (bf16[2,2,16,512]{3,1,2,0:T(2,128)(2,1)S(1)}, bf16[2,2,16,512]{3,1,2,0:T(2,128)(2,1)S(1)}, u32[]{:S(2)}, u32[]{:S(2)}) collective-permute-start(bf16[2,2,16,512]{3,1,2,0:T(2,128)(2,1)S(1)} %copy-done.22), channel_id=1, source_target_pairs={{0,4},{1,5},{2,6},{3,7},{4,8},{5,9},{6,10},{7,11},{8,12},{9,13},{1... | collective-permute-start | bytes 196616 | tf_op jit(solution)/shard_map/ppermute | solution.py:16
  46.9 4.3 %collective-permute-start.3 = (bf16[2,2,16,512]{3,1,2,0:T(2,128)(2,1)S(1)}, bf16[2,2,16,512]{3,1,2,0:T(2,128)(2,1)S(1)}, u32[]{:S(2)}, u32[]{:S(2)}) collective-permute-start(bf16[2,2,16,512]{3,1,2,0:T(2,128)(2,1)S(1)} %copy-done.21), channel_id=1, source_target_pairs={{0,12},{1,13},{2,14},{3,15},{4,0},{5,1},{6,2},{7,3},{8,4},{9,5},{1... | collective-permute-start | bytes 196616 | tf_op jit(solution)/shard_map/ppermute | solution.py:16
  56.1 4.3 %copy-start.13 = (bf16[1,256,512]{1,2,0:T(8,128)(2,1)S(1)}, bf16[1,256,512]{1,2,0:T(8,128)(2,1)}, u32[]{:S(2)}) copy-start(bf16[1,256,512]{1,2,0:T(8,128)(2,1)} %copy.123) | copy-start | bytes 786436
  56.1 4.3 %copy-start.18 = (f32[128,256]{1,0:T(8,128)S(1)}, f32[128,256]{1,0:T(8,128)}, u32[]{:S(2)}) copy-start(f32[128,256]{1,0:T(8,128)} %convert_element_type.137) | copy-start | bytes 393220
  56.2 4.3 %copy-start.20 = (bf16[128,512]{0,1:T(8,128)(2,1)S(1)}, bf16[128,512]{0,1:T(8,128)(2,1)}, u32[]{:S(2)}) copy-start(bf16[128,512]{0,1:T(8,128)(2,1)} %copy.124) | copy-start | bytes 393220
  60.5 3.2 %copy-start.4 = (bf16[1,256,512]{1,2,0:T(8,128)(2,1)S(1)}, bf16[1,256,512]{1,2,0:T(8,128)(2,1)}, u32[]{:S(2)}) copy-start(bf16[1,256,512]{1,2,0:T(8,128)(2,1)} %copy.131) | copy-start | bytes 786436
  63.1 0.6 copy-start.25
  97.4 1.8 copy-start.5
  130.8 2.8 %copy-start.15 = (bf16[16,32,256]{2,1,0:T(8,128)(2,1)S(1)}, bf16[16,32,256]{2,1,0:T(8,128)(2,1)}, u32[]{:S(2)}) copy-start(bf16[16,32,256]{2,1,0:T(8,128)(2,1)} %convolution_convert_fusion.3) | copy-start | bytes 786436
  130.8 3.0 %copy-start.14 = (bf16[16,32,256]{2,1,0:T(8,128)(2,1)S(1)}, bf16[16,32,256]{2,1,0:T(8,128)(2,1)}, u32[]{:S(2)}) copy-start(bf16[16,32,256]{2,1,0:T(8,128)(2,1)} %convolution_convert_fusion) | copy-start | bytes 786436
  130.8 3.1 %copy-start.12 = (bf16[16,32,256]{2,1,0:T(8,128)(2,1)S(1)}, bf16[16,32,256]{2,1,0:T(8,128)(2,1)}, u32[]{:S(2)}) copy-start(bf16[16,32,256]{2,1,0:T(8,128)(2,1)} %convolution_convert_fusion.2) | copy-start | bytes 786436
  133.7 5.6 %copy-start.8 = (bf16[16,32,128]{2,1,0:T(8,128)(2,1)S(1)}, bf16[16,32,128]{2,1,0:T(8,128)(2,1)}, u32[]{:S(2)}) copy-start(bf16[16,32,128]{2,1,0:T(8,128)(2,1)} %convolution_convert_fusion.11) | copy-start | bytes 393220
  134.1 5.5 %copy-start.7 = (bf16[2,128,512]{2,1,0:T(8,128)(2,1)S(1)}, bf16[2,128,512]{2,1,0:T(8,128)(2,1)}, u32[]{:S(2)}) copy-start(bf16[2,128,512]{2,1,0:T(8,128)(2,1)} %param.10) | copy-start | bytes 786436
  134.1 5.5 %copy-start.16 = (bf16[16,32,128]{2,1,0:T(8,128)(2,1)S(1)}, bf16[16,32,128]{2,1,0:T(8,128)(2,1)}, u32[]{:S(2)}) copy-start(bf16[16,32,128]{2,1,0:T(8,128)(2,1)} %convolution_convert_fusion.8) | copy-start | bytes 393220
  134.1 5.5 %copy-start.17 = (bf16[16,32,128]{2,1,0:T(8,128)(2,1)S(1)}, bf16[16,32,128]{2,1,0:T(8,128)(2,1)}, u32[]{:S(2)}) copy-start(bf16[16,32,128]{2,1,0:T(8,128)(2,1)} %convolution_convert_fusion.9) | copy-start | bytes 393220
  134.2 15.9 %collective-permute-start.15 = (bf16[2,2,16,512]{3,2,1,0:T(8,128)(2,1)S(1)}, bf16[2,2,16,512]{3,2,1,0:T(8,128)(2,1)S(1)}, u32[]{:S(2)}, u32[]{:S(2)}) collective-permute-start(bf16[2,2,16,512]{3,2,1,0:T(8,128)(2,1)S(1)} %get-tuple-element.14), channel_id=1, source_target_pairs={{0,5},{1,6},{2,7},{3,8},{4,9},{5,10},{6,11},{7,12},{8,13},{9,14},{... | collective-permute-start | bytes 196616 | tf_op jit(solution)/shard_map/ppermute | solution.py:16
  134.3 5.7 %collective-permute-start.8 = (bf16[2,2,16,512]{3,2,1,0:T(8,128)(2,1)S(1)}, bf16[2,2,16,512]{3,2,1,0:T(8,128)(2,1)S(1)}, u32[]{:S(2)}, u32[]{:S(2)}) collective-permute-start(bf16[2,2,16,512]{3,2,1,0:T(8,128)(2,1)S(1)} %get-tuple-element.15), channel_id=1, source_target_pairs={{0,15},{1,0},{2,1},{3,2},{4,3},{5,4},{6,5},{7,6},{8,7},{9,8},{10,9... | collective-permute-start | bytes 196616 | tf_op jit(solution)/shard_map/ppermute | solution.py:16
  137.0 7.2 %collective-permute-start.9 = (bf16[2,2,16,512]{3,2,1,0:T(8,128)(2,1)S(1)}, bf16[2,2,16,512]{3,2,1,0:T(8,128)(2,1)S(1)}, u32[]{:S(2)}, u32[]{:S(2)}) collective-permute-start(bf16[2,2,16,512]{3,2,1,0:T(8,128)(2,1)S(1)} %get-tuple-element.16), channel_id=1, source_target_pairs={{0,1},{1,2},{2,3},{3,4},{4,5},{5,6},{6,7},{7,8},{8,9},{9,10},{10,1... | collective-permute-start | bytes 196616 | tf_op jit(solution)/shard_map/ppermute | solution.py:16
  137.0 7.3 %collective-permute-start.10 = (bf16[2,2,16,512]{3,2,1,0:T(8,128)(2,1)S(1)}, bf16[2,2,16,512]{3,2,1,0:T(8,128)(2,1)S(1)}, u32[]{:S(2)}, u32[]{:S(2)}) collective-permute-start(bf16[2,2,16,512]{3,2,1,0:T(8,128)(2,1)S(1)} %get-tuple-element.17), channel_id=1, source_target_pairs={{0,12},{1,13},{2,14},{3,15},{4,0},{5,1},{6,2},{7,3},{8,4},{9,5},{1... | collective-permute-start | bytes 196616 | tf_op jit(solution)/shard_map/ppermute | solution.py:16
  139.3 6.9 %collective-permute-start.11 = (bf16[2,2,16,512]{3,2,1,0:T(8,128)(2,1)S(1)}, bf16[2,2,16,512]{3,2,1,0:T(8,128)(2,1)S(1)}, u32[]{:S(2)}, u32[]{:S(2)}) collective-permute-start(bf16[2,2,16,512]{3,2,1,0:T(8,128)(2,1)S(1)} %get-tuple-element.18), channel_id=1, source_target_pairs={{0,4},{1,5},{2,6},{3,7},{4,8},{5,9},{6,10},{7,11},{8,12},{9,13},{1... | collective-permute-start | bytes 196616 | tf_op jit(solution)/shard_map/ppermute | solution.py:16
  139.6 10.7 %copy-start.11 = (bf16[128,2,512]{2,0,1:T(8,128)(2,1)S(1)}, bf16[128,2,512]{2,0,1:T(8,128)(2,1)}, u32[]{:S(2)}) copy-start(bf16[128,2,512]{2,0,1:T(8,128)(2,1)} %gather_fusion.2) | copy-start | bytes 786436
  140.0 6.7 %collective-permute-start.12 = (bf16[2,2,16,512]{3,2,1,0:T(8,128)(2,1)S(1)}, bf16[2,2,16,512]{3,2,1,0:T(8,128)(2,1)S(1)}, u32[]{:S(2)}, u32[]{:S(2)}) collective-permute-start(bf16[2,2,16,512]{3,2,1,0:T(8,128)(2,1)S(1)} %get-tuple-element.19), channel_id=1, source_target_pairs={{0,13},{1,14},{2,15},{3,0},{4,1},{5,2},{6,3},{7,4},{8,5},{9,6},{10... | collective-permute-start | bytes 196616 | tf_op jit(solution)/shard_map/ppermute | solution.py:16
  144.2 5.9 %collective-permute-start.13 = (bf16[2,2,16,512]{3,2,1,0:T(8,128)(2,1)S(1)}, bf16[2,2,16,512]{3,2,1,0:T(8,128)(2,1)S(1)}, u32[]{:S(2)}, u32[]{:S(2)}) collective-permute-start(bf16[2,2,16,512]{3,2,1,0:T(8,128)(2,1)S(1)} %get-tuple-element.20), channel_id=1, source_target_pairs={{0,3},{1,4},{2,5},{3,6},{4,7},{5,8},{6,9},{7,10},{8,11},{9,12},{10... | collective-permute-start | bytes 196616 | tf_op jit(solution)/shard_map/ppermute | solution.py:16
  144.3 5.8 %collective-permute-start.14 = (bf16[2,2,16,512]{3,2,1,0:T(8,128)(2,1)S(1)}, bf16[2,2,16,512]{3,2,1,0:T(8,128)(2,1)S(1)}, u32[]{:S(2)}, u32[]{:S(2)}) collective-permute-start(bf16[2,2,16,512]{3,2,1,0:T(8,128)(2,1)S(1)} %get-tuple-element.21), channel_id=1, source_target_pairs={{0,11},{1,12},{2,13},{3,14},{4,15},{5,0},{6,1},{7,2},{8,3},{9,4},{... | collective-permute-start | bytes 196616 | tf_op jit(solution)/shard_map/ppermute | solution.py:16
  159.1 1.0 copy-start.2
Sparse Core Ops, SparseCore 0:
  159.2 74.0 reduce-scatter.3
where the time goes:
time: 241 us; the launch traced here: 240 us
  matrix products  81.4 us (34%)
  waiting for transfers between devices  81.1 us (34%)
  local copies, waits for them, and re-layouts  23.9 us (10%)
  starting transfers between devices  21.4 us (9%)
  other arithmetic  17.6 us (7%)
  between operations  14.7 us (6%)
    unnamed x2, waiting for transfers between devices  64.9 us
    dot_general x2, matrix products, member_backward(): jnp.einsum('hrc,rhd->chd', score_grad, query_heads, preferred_element_typ...  28.5 us
    dot_general x2, matrix products, member_backward(): jnp.einsum('hrc,chd->rhd', score_grad, key_heads, preferred_element_type=...  27.6 us
    ppermute x16, starting transfers between devices, shifted(): lax.ppermute(shard, axis, [(i, (i + by) % count) for i in range(count)])  21.4 us
    ppermute x16, waiting for transfers between devices, shifted(): lax.ppermute(shard, axis, [(i, (i + by) % count) for i in range(count)])  16.2 us
    unnamed x68, local copies, waits for them, and re-layouts  9.33 us
    reduce_or x1, other arithmetic, build_mask(): return jnp.any(target[:, :, None] == columns, axis=1).astype(jnp.float32)  5.74 us
    scatter-add x1, other arithmetic, body(): node_total = node_grad.reshape(members, node_rows, model_width).at[:, sen...  5.54 us
  transfers between devices with their start and end apart: 17, of which 7 were waited for; matrix products, arithmetic and copies ran while one was open for 10% of the time, Pallas kernels for 0%

commit v1 on v0

v1 whole, which is shorter than its diff:
```python
import functools
import math

import jax
import jax.numpy as jnp
from jax import lax
from jax.experimental import pallas as pl
from jax.experimental.pallas import tpu as pltpu
from jax.sharding import PartitionSpec as P

HEADS = 16
score_cap = 5.0
VMEM = pltpu.CompilerParams(vmem_limit_bytes=56 * 1024 * 1024)
f32 = jnp.float32
bf16 = jnp.bfloat16


def nn(a, b):
    return lax.dot_general(a, b, (((1,), (0,)), ((), ())), preferred_element_type=f32)


def nt(a, b):
    return lax.dot_general(a, b, (((1,), (1,)), ((), ())), preferred_element_type=f32)


def shifted(shard, by):
    count = lax.axis_size("patch")
    return lax.ppermute(shard, "patch", [(i, (i + by) % count) for i in range(count)])


def sent_selector(send_rows, node_rows):
    adjacent, slots = send_rows.shape
    halo = adjacent * slots
    wide = jnp.concatenate([send_rows] * adjacent, axis=1)
    own = lax.broadcasted_iota(jnp.int32, (adjacent, halo), 1) // slots == lax.broadcasted_iota(
        jnp.int32, (adjacent, halo), 0
    )
    ids = jnp.sum(jnp.where(own, wide, 0), axis=0, keepdims=True)
    nodes = lax.broadcasted_iota(jnp.int32, (node_rows, halo), 0)
    return jnp.where(nodes == ids, 1.0, 0.0).astype(f32)


def gather_kernel(slots, send_ref, x_ref, plus_ref, minus_ref, right_ref, left_ref):
    members, node_rows, _ = x_ref.shape
    pick = sent_selector(send_ref[0], node_rows).T.astype(bf16)
    for m in range(members):
        rows = nn(pick, x_ref[m]).astype(bf16)

        def part(k):
            return rows[k * slots : (k + 1) * slots]

        for i, k in enumerate((2, 6, 4)):
            plus_ref[m, i] = part(k)
        for i, k in enumerate((3, 5, 7)):
            minus_ref[m, i] = part(k)
        right_ref[m, 0] = part(0)
        left_ref[m, 0] = part(1)


def local_kernel(
    x_ref, og_ref, wq_ref, wk_ref, wv_ref, wo_ref, neigh_ref, count_ref,
    q_ref, qt_ref, k_ref, kt_ref, v_ref, vt_ref, g_ref, gt_ref, xt_ref, mask_ref,
):
    members, node_rows, width = x_ref.shape
    groups = width // 128
    x = x_ref[...].reshape(members * node_rows, width)
    og = og_ref[...].reshape(members * node_rows, width)

    def put(rows, nat_ref, t_ref):
        for m in range(members):
            for g in range(groups):
                block = rows[m * node_rows : (m + 1) * node_rows, g * 128 : (g + 1) * 128]
                nat_ref[m, g] = block
                t_ref[m, g] = block.T

    put(nn(x, wq_ref[...]).astype(bf16), q_ref, qt_ref)
    put(nn(x, wk_ref[...]).astype(bf16), k_ref, kt_ref)
    put(nn(x, wv_ref[...]).astype(bf16), v_ref, vt_ref)
    put(nt(og, wo_ref[...]).astype(bf16), g_ref, gt_ref)
    for m in range(members):
        xt_ref[m] = x_ref[m].T

    neigh = neigh_ref[...].T
    slots = neigh.shape[0]
    table = mask_ref.shape[0]
    order = lax.broadcasted_iota(jnp.int32, neigh.shape, 0)
    tail = jnp.where(order >= count_ref[...], neigh, -1)[slots // 2 :]
    half = table // 2
    for part in range(2):
        columns = lax.broadcasted_iota(jnp.int32, (half, node_rows), 0) + part * half
        kept = jnp.ones((half, node_rows), f32)
        for j in range(slots // 2):
            kept = jnp.where(tail[j : j + 1] == columns, 0.0, kept)
        mask_ref[part * half : (part + 1) * half] = kept


def attention_kernel(
    me_ref, x_ref, og_ref, xt_ref, q_ref, qt_ref, k_ref, kt_ref, v_ref, vt_ref, g_ref, gt_ref, mask_ref,
    plus_ref, minus_ref, right_ref, left_ref, wq_ref, wk_ref, wv_ref,
    keep_ref, send_ref, node_ref, back_left_ref, back_right_ref, back_minus_ref, back_plus_ref,
    kf, ktf, vf, vtf, xtf, att, dq, dk, dv, score, grad, dw,
):
    members, node_rows, width = x_ref.shape
    groups = width // 128
    slots = plus_ref.shape[2]
    table = mask_ref.shape[0]
    head = width // HEADS
    per = 128 // head
    scale = 1.0 / math.sqrt(head)

    for m in range(members):
        pieces = [None] * 8
        for ref, order in (
            (right_ref, (0, 6, 5)),
            (left_ref, (1, 4, 7)),
            (plus_ref, (2,)),
            (minus_ref, (3,)),
        ):
            for i, k in enumerate(order):
                pieces[k] = ref[m, i]
        halo = jnp.concatenate(pieces, axis=0)
        xtf[m, :, :node_rows] = xt_ref[m]
        xtf[m, :, node_rows:] = halo.T
        for w_ref, nat, trans, lnat, ltrans in (
            (wk_ref, kf, ktf, k_ref, kt_ref),
            (wv_ref, vf, vtf, v_ref, vt_ref),
        ):
            rows = nn(halo, w_ref[...]).astype(bf16)
            for g in range(groups):
                block = rows[:, g * 128 : (g + 1) * 128]
                nat[m, g, :node_rows] = lnat[m, g]
                nat[m, g, node_rows:] = block
                trans[m, g, :, :node_rows] = ltrans[m, g]
                trans[m, g, :, node_rows:] = block.T

    row_head = lax.broadcasted_iota(jnp.int32, (128, node_rows), 0) // head
    lane_head = lax.broadcasted_iota(jnp.int32, (node_rows, 128), 1) // head

    def spread_t(block):
        zero = jnp.zeros_like(block)
        return jnp.concatenate([jnp.where(row_head == h, block, zero) for h in range(per)], axis=1)

    def spread_n(block):
        zero = jnp.zeros_like(block)
        return jnp.concatenate([jnp.where(lane_head == h, block, zero) for h in range(per)], axis=0)

    strip = 64

    def step(i, _):
        m = i // groups
        g = i % groups
        kg, vg = kf[m, g], vf[m, g]
        score[...] = nn(kg, spread_t(qt_ref[m, g]))
        grad[...] = nn(vg, spread_t(gt_ref[m, g]))
        probs = []
        slopes = []
        for h in range(per):
            lanes = slice(h * node_rows, (h + 1) * node_rows)
            den = jnp.zeros((8, node_rows), f32)
            inner = jnp.zeros((8, node_rows), f32)
            for c in range(0, table, strip):
                t = jnp.tanh(score[c : c + strip, lanes] * (scale / score_cap))
                e = jnp.exp(t * score_cap) * mask_ref[c : c + strip]
                den = den + jnp.sum(e.reshape(strip // 8, 8, node_rows), axis=0)
                inner = inner + jnp.sum(
                    (e * grad[c : c + strip, lanes]).reshape(strip // 8, 8, node_rows), axis=0
                )
                score[c : c + strip, lanes] = e
                slopes.append(e * (scale - scale * (t * t)))
            r = 1.0 / jnp.sum(den, axis=0, keepdims=True)
            inner = jnp.sum(inner, axis=0, keepdims=True) * r
            column = []
            scores = []
            for j, c in enumerate(range(0, table, strip)):
                column.append((score[c : c + strip, lanes] * r).astype(bf16))
                w = slopes[h * (table // strip) + j]
                scores.append(((w * r) * (grad[c : c + strip, lanes] - inner)).astype(bf16))
            probs.append((jnp.concatenate(column, axis=0), jnp.concatenate(scores, axis=0)))
        pb = jnp.concatenate([p for p, _ in probs], axis=1)
        ds = jnp.concatenate([s for _, s in probs], axis=1)
        ktg, vtg = ktf[m, g], vtf[m, g]
        for h in range(0, per, 2):
            lanes = slice(h * node_rows, (h + 2) * node_rows)
            rows = slice(h * head, (h + 2) * head)
            a = nn(vtg[rows], pb[:, lanes])
            b = nn(ktg[rows], ds[:, lanes])
            for j in range(2):
                inside = (slice(j * head, (j + 1) * head), slice(j * node_rows, (j + 1) * node_rows))
                att[m, g, (h + j) * head : (h + j + 1) * head, :] = a[inside].astype(bf16)
                dq[m, g, (h + j) * head : (h + j + 1) * head, :] = b[inside].astype(bf16)
        dk[m, g] = nn(ds, spread_n(q_ref[m, g])).astype(bf16)
        dv[m, g] = nn(pb, spread_n(g_ref[m, g])).astype(bf16)
        return 0

    lax.fori_loop(0, members * groups, step, 0)

    def whole(ref, m):
        return jnp.concatenate([ref[m, g] for g in range(groups)], axis=1)

    blocks, rows = dw.shape[0] * 2, dw.shape[2]
    c = me_ref[0] % 2
    dqs = [jnp.concatenate([dq[m, g].T for g in range(groups)], axis=1) for m in range(members)]
    dks = [whole(dk, m) for m in range(members)]
    dvs = [whole(dv, m) for m in range(members)]
    atts = [att[m].reshape(width, node_rows) for m in range(members)]

    def emit(n, pairs):
        total = None
        for a, b in pairs:
            term = nn(a, b)
            total = term if total is None else total + term
        dw[...] = total.reshape(blocks // 2, 2, rows, width)
        lanes = slice(n * width, (n + 1) * width)
        keep_ref[:, :, lanes] = dw[:, pl.ds(c, 1)][:, 0]
        send_ref[:, :, lanes] = dw[:, pl.ds(1 - c, 1)][:, 0].astype(bf16)

    emit(0, [(xt_ref[m], dqs[m]) for m in range(members)])
    emit(1, [(xtf[m], dks[m]) for m in range(members)])
    emit(2, [(xtf[m], dvs[m]) for m in range(members)])
    emit(3, [(atts[m], og_ref[m]) for m in range(members)])
    for m in range(members):
        spread = nt(dks[m], wk_ref[...]) + nt(dvs[m], wv_ref[...])
        node_ref[m] = spread[:node_rows] + nt(dqs[m], wq_ref[...])
        halo = spread[node_rows:].astype(bf16)
        for ref, order in (
            (back_left_ref, (0, 6, 5)),
            (back_right_ref, (1, 4, 7)),
            (back_minus_ref, (2,)),
            (back_plus_ref, (3,)),
        ):
            for i, k in enumerate(order):
                ref[m, i] = halo[k * slots : (k + 1) * slots]


def finish_kernel(send_ref, node_ref, left_ref, right_ref, minus_ref, plus_ref, out_ref):
    members, node_rows, _ = node_ref.shape
    pick = sent_selector(send_ref[0], node_rows).astype(bf16)
    for m in range(members):
        pieces = [None] * 8
        for ref, order in (
            (left_ref, (0,)),
            (right_ref, (1,)),
            (minus_ref, (2, 6, 4)),
            (plus_ref, (3, 5, 7)),
        ):
            for i, k in enumerate(order):
                pieces[k] = ref[m, i]
        arriving = jnp.concatenate(pieces, axis=0)
        out_ref[m] = (node_ref[m] + nn(pick, arriving)).astype(bf16)


def call(kernel, outs, scratch=(), smem=0, cost=None):
    return pl.pallas_call(
        kernel,
        out_shape=[jax.ShapeDtypeStruct(*o) for o in outs],
        scratch_shapes=list(scratch),
        compiler_params=VMEM,
        cost_estimate=cost,
        **smem_specs(smem),
    )


def smem_specs(count):
    if not count:
        return {}
    return {
        "in_specs": [pl.BlockSpec(memory_space=pltpu.SMEM)]
        + [pl.BlockSpec(memory_space=pltpu.VMEM)] * count
    }


def scatter_sum(keep, received, me, count):
    stride, left = 2, count // 2
    while left > 1:
        radix = 2 if stride == 2 or left % 4 else 4
        total = (keep + received.astype(f32)) if received is not None else keep
        view = total.reshape(left // radix, radix, *total.shape[1:])
        digit = (me // stride) % radix
        own = lax.dynamic_index_in_dim(view, digit, 1, keepdims=False)
        arrived = []
        for k in range(1, radix):
            outgoing = lax.dynamic_index_in_dim(
                view, (digit + k) % radix, 1, keepdims=False
            ).astype(bf16)
            pairs = []
            for i in range(count):
                d = (i // stride) % radix
                pairs.append((i, i + ((d + k) % radix - d) * stride))
            arrived.append(lax.ppermute(outgoing, "patch", pairs))
        keep = own
        for a in arrived:
            keep = keep + a.astype(f32)
        received = None
        stride, left = stride * radix, left // radix
    return keep


def body(
    node_features, out_grad, w_query, w_key, w_value, w_out, neighbours, neighbour_count, send_rows
):
    members, node_rows, width = node_features.shape
    count = lax.axis_size("patch")
    row_width = min(8, count // 4)
    _, adjacent, slots = send_rows.shape
    table = node_rows + adjacent * slots
    groups = width // 128
    me = lax.axis_index("patch")
    three = ((members, 3, slots, width), bf16)
    one = ((members, 1, slots, width), bf16)

    to_plus, to_minus, own_right, own_left = call(
        functools.partial(gather_kernel, slots), [three, three, one, one]
    )(send_rows, node_features)
    plus = shifted(to_plus, row_width)
    minus = shifted(to_minus, -row_width)
    right = shifted(jnp.concatenate([own_right, plus[:, 1:2], minus[:, 1:2]], axis=1), 1)
    left = shifted(jnp.concatenate([own_left, plus[:, 2:3], minus[:, 2:3]], axis=1), -1)

    nat = ((members, groups, node_rows, 128), bf16)
    trans = ((members, groups, 128, node_rows), bf16)
    q, qt, k, kt, v, vt, g, gt, xt, mask = call(
        local_kernel,
        [nat, trans] * 4 + [((members, width, node_rows), bf16), ((table, node_rows), f32)],
        cost=pl.CostEstimate(flops=10**9, bytes_accessed=6 * 10**6, transcendentals=0),
    )(
        node_features, out_grad, w_query, w_key, w_value, w_out, neighbours,
        neighbour_count.reshape(1, node_rows),
    )

    blocks, rows = count // 2, width // count
    keep, send, node, back_left, back_right, back_minus, back_plus = call(
        attention_kernel,
        [
            ((blocks, rows, 4 * width), f32),
            ((blocks, rows, 4 * width), bf16),
            ((members, node_rows, width), f32),
            three, three, one, one,
        ],
        scratch=[
            pltpu.VMEM((members, groups, table, 128), bf16),
            pltpu.VMEM((members, groups, 128, table), bf16),
            pltpu.VMEM((members, groups, table, 128), bf16),
            pltpu.VMEM((members, groups, 128, table), bf16),
            pltpu.VMEM((members, width, table), bf16),
            pltpu.VMEM((members, groups, 128, node_rows), bf16),
            pltpu.VMEM((members, groups, 128, node_rows), bf16),
            pltpu.VMEM((members, groups, table, 128), bf16),
            pltpu.VMEM((members, groups, table, 128), bf16),
            pltpu.VMEM((table, 512), f32),
            pltpu.VMEM((table, 512), f32),
            pltpu.VMEM((blocks, 2, rows, width), f32),
        ],
        smem=19,
        cost=pl.CostEstimate(flops=3 * 10**9, bytes_accessed=10**7, transcendentals=2 * 10**6),
    )(
        me.reshape(1), node_features, out_grad, xt, q, qt, k, kt, v, vt, g, gt, mask,
        plus, minus, right, left, w_query, w_key, w_value,
    )

    received = lax.ppermute(send, "patch", [(i, i ^ 1) for i in range(count)])
    from_right = shifted(back_left, -1)
    from_left = shifted(back_right, 1)
    weight_grad = scatter_sum(keep, received, me, count)
    from_plus = shifted(
        jnp.concatenate([back_minus, from_right[:, 1:2], from_left[:, 1:2]], axis=1), -row_width
    )
    from_minus = shifted(
        jnp.concatenate([back_plus, from_right[:, 2:3], from_left[:, 2:3]], axis=1), row_width
    )
    (node_grad,) = call(finish_kernel, [((members, node_rows, width), bf16)])(
        send_rows, node, from_right[:, :1], from_left[:, :1], from_plus, from_minus
    )
    return (node_grad, weight_grad.reshape(rows, 4 * width))


def solution(mesh):
    in_specs = (
        P("groups", "patch", None),
        P("groups", "patch", None),
        P(),
        P(),
        P(),
        P(),
        P("patch", None),
        P("patch"),
        P("patch", None, None),
    )
    out_specs = (P("groups", "patch", None), P(("groups", "patch"), None))
    return jax.shard_map(body, mesh=mesh, in_specs=in_specs, out_specs=out_specs, check_vma=False)
```

time: 241 us -> 76.6 us (0.32)
  the two profiles are of different devices: /device:TPU:0 before, /device:TPU:21 now
where the time goes in v1:
time: 76.6 us; the launch traced here: 76.2 us
  waiting for transfers between devices  26 us (34%)
  Pallas kernels  22.2 us (29%)
  starting transfers between devices  20.1 us (26%)
  other arithmetic  4.36 us (6%)
  local copies, waits for them, and re-layouts  2.69 us (4%)
  between operations  0.88 us (1%)
    ppermute x8, waiting for transfers between devices, shifted(): lax.ppermute(shard, 'patch', [(i, (i + by) % count) for i in range(count)])  16.2 us
    pallas_call x1, Pallas kernels, body(): call(attention_kernel, [((blocks, rows, 4 * width), f32), ((blocks, rows,...  13.7 us
    ppermute x8, starting transfers between devices, shifted(): lax.ppermute(shard, 'patch', [(i, (i + by) % count) for i in range(count)])  12.6 us
    ppermute x4, waiting for transfers between devices, scatter_sum(): arrived.append(lax.ppermute(outgoing, 'patch', pairs))  9.81 us
    ppermute x4, starting transfers between devices, scatter_sum(): arrived.append(lax.ppermute(outgoing, 'patch', pairs))  7.46 us
    pallas_call x1, Pallas kernels, body(): call(local_kernel, [nat, trans] * 4 + [((members, width, node_rows), bf16...  4.35 us
    pallas_call x1, Pallas kernels, body(): call(finish_kernel, [((members, node_rows, width), bf16)])  2.11 us
    pallas_call x1, Pallas kernels, body(): call(functools.partial(gather_kernel, slots), [three, three, one, one])  1.99 us
  transfers between devices with their start and end apart: 13, of which 6 were waited for; matrix products, arithmetic and copies ran while one was open for 5% of the time, Pallas kernels for 8%

profile of v1, /device:TPU:21, one launch (start us, length us, event | category | flops | bytes accessed | tf_op | source)
XLA Modules:
  0.0 76.2 jit_solution(1795274162343635186)
XLA Ops:
  0.6 2.0 %shard_map.105 = (bf16[2,3,16,512]{3,2,1,0:T(8,128)(2,1)}, bf16[2,3,16,512]{3,2,1,0:T(8,128)(2,1)}, bf16[2,1,16,512]{3,2,1,0:T(8,128)(2,1)}, bf16[2,1,16,512]{3,2,1,0:T(8,128)(2,1)}) custom-call(s32[1,8,16]{2,1,0:T(8,128)} %send_ref.3, bf16[2,128,512]{2,1,0:T(8,128)(2,1)} %x_ref.5), custom_call_target="tpu_custom_call" | custom-call | tf_op jit(solution)/shard_map/pallas_call | solution.py:311
  2.6 0.2 collective-permute-start.1
  2.8 1.3 %collective-permute-start = (bf16[2,3,16,512]{3,2,1,0:T(8,128)(2,1)}, bf16[2,3,16,512]{3,2,1,0:T(8,128)(2,1)S(1)}, u32[]{:S(2)}, u32[]{:S(2)}) collective-permute-start(bf16[2,3,16,512]{3,2,1,0:T(8,128)(2,1)} %get-tuple-element.33), channel_id=1, source_target_pairs={{0,4},{1,5},{2,6},{3,7},{4,8},{5,9},{6,10},{7,11},{8,12},{9,13},{1... | collective-permute-start | bytes 294920 | tf_op jit(solution)/shard_map/ppermute | solution.py:28
  4.1 2.2 %collective-permute-done.1.minus_ref = bf16[2,3,16,512]{3,2,1,0:T(8,128)(2,1)S(1)} collective-permute-done((bf16[2,3,16,512]{3,2,1,0:T(8,128)(2,1)}, bf16[2,3,16,512]{3,2,1,0:T(8,128)(2,1)S(1)}, u32[]{:S(2)}, u32[]{:S(2)}) %collective-permute-start.1) | collective-permute-done | bytes 98336 | tf_op jit(solution)/shard_map/ppermute | solution.py:28
  6.3 0.5 collective-permute-done.plus_ref
  6.8 0.8 %pad_maximum_fusion = bf16[2,3,16,512]{3,2,1,0:T(8,128)(2,1)S(1)} fusion(bf16[2,1,16,512]{3,2,1,0:T(8,128)(2,1)S(1)} %get-tuple-element.56, bf16[2,1,16,512]{3,2,1,0:T(8,128)(2,1)S(1)} %get-tuple-element.54, bf16[2,1,16,512]{3,2,1,0:T(8,128)(2,1)} %get-tuple-element.35), kind=kLoop, calls=%fused_computation.8 | loop fusion | flops 98304 | bytes 196608 | tf_op jit(solution)/shard_map/concatenate | solution.py:316
  7.6 5.4 %collective-permute-start.2 = (bf16[2,3,16,512]{3,2,1,0:T(8,128)(2,1)S(1)}, bf16[2,3,16,512]{3,2,1,0:T(8,128)(2,1)S(1)}, u32[]{:S(2)}, u32[]{:S(2)}) collective-permute-start(bf16[2,3,16,512]{3,2,1,0:T(8,128)(2,1)S(1)} %pad_maximum_fusion), channel_id=1, source_target_pairs={{0,1},{1,2},{2,3},{3,4},{4,5},{5,6},{6,7},{7,8},{8,9},{9,10},{10,1... | collective-permute-start | bytes 294920 | tf_op jit(solution)/shard_map/ppermute | solution.py:28
  13.0 0.8 %pad_maximum_fusion.1 = bf16[2,3,16,512]{3,2,1,0:T(8,128)(2,1)S(1)} fusion(bf16[2,1,16,512]{3,2,1,0:T(8,128)(2,1)S(1)} %get-tuple-element.55, bf16[2,1,16,512]{3,2,1,0:T(8,128)(2,1)S(1)} %get-tuple-element.53, bf16[2,1,16,512]{3,2,1,0:T(8,128)(2,1)} %get-tuple-element.36), kind=kLoop, calls=%fused_computation.9 | loop fusion | flops 98304 | bytes 196608 | tf_op jit(solution)/shard_map/concatenate | solution.py:317
  13.7 0.1 collective-permute-start.3
  13.8 4.3 %shard_map.104 = (bf16[2,4,128,128]{3,2,1,0:T(8,128)(2,1)}, bf16[2,4,128,128]{3,2,1,0:T(8,128)(2,1)}, bf16[2,4,128,128]{3,2,1,0:T(8,128)(2,1)}, bf16[2,4,128,128...) custom-call(bf16[2,128,512]{2,1,0:T(8,128)(2,1)} %x_ref.5, ...), custom_call_target="tpu_custom_call" | custom-call | flops 1000000000 | bytes 6000000 | tf_op jit(solution)/shard_map/pallas_call | solution.py:321
  18.2 0.0 copy-done.2
  18.2 0.0 copy-done.3
  18.2 0.0 collective-permute-done.2.right_ref
  18.2 0.0 copy-start.6
  18.2 0.5 collective-permute-done.3.left_ref
  18.7 0.1 copy-done.6
  18.8 0.6 copy-done.7
  19.4 13.7 %shard_map.106 = (f32[8,32,2048]{2,1,0:T(8,128)}, bf16[8,32,2048]{2,1,0:T(8,128)(2,1)}, f32[2,128,512]{2,1,0:T(8,128)}, bf16[2,3,16,512]{3,2,1,0:T(8,128)(2,1)},...) custom-call(s32[1]{0:T(128)} %bitcast.me_ref, ...), custom_call_target="tpu_custom_call" | custom-call | flops 3000000000 | bytes 10000000 | tf_op jit(solution)/shard_map/pallas_call | solution.py:331
  33.1 0.1 collective-permute-start.8
  33.3 0.4 collective-permute-start.4
  33.7 2.3 %collective-permute-start.5 = (bf16[2,3,16,512]{3,2,1,0:T(8,128)(2,1)}, bf16[2,3,16,512]{3,2,1,0:T(8,128)(2,1)S(1)}, u32[]{:S(2)}, u32[]{:S(2)}) collective-permute-start(bf16[2,3,16,512]{3,2,1,0:T(8,128)(2,1)} %get-tuple-element.39), channel_id=1, source_target_pairs={{0,1},{1,2},{2,3},{3,4},{4,5},{5,6},{6,7},{7,8},{8,9},{9,10},{10,1... | collective-permute-start | bytes 294920 | tf_op jit(solution)/shard_map/ppermute | solution.py:28
  36.0 0.0 collective-permute-done.8
  36.0 1.9 %convert_add_fusion = f32[8,32,2048]{2,1,0:T(8,128)S(1)} fusion(f32[8,32,2048]{2,1,0:T(8,128)} %get-tuple-element.42, bf16[8,32,2048]{2,1,0:T(8,128)(2,1)S(1)} %collective-permute-done.8), kind=kLoop, calls=%fused_computation | loop fusion | flops 1048576 | bytes 5242880 | tf_op jit(solution)/shard_map/add | solution.py:276
  37.9 0.1 fusion
  38.0 0.0 copy-start.4
  38.0 0.2 collective-permute-start.9
  38.2 0.4 collective-permute-done.4
  38.6 0.6 fusion.1
  39.2 0.0 collective-permute-done.5
  39.2 0.6 fusion.2
  39.9 0.0 copy-done.5
  39.9 1.7 %collective-permute-start.6 = (bf16[2,3,16,512]{3,2,1,0:T(8,128)(2,1)S(1)}, bf16[2,3,16,512]{3,2,1,0:T(8,128)(2,1)S(1)}, u32[]{:S(2)}, u32[]{:S(2)}) collective-permute-start(bf16[2,3,16,512]{3,2,1,0:T(8,128)(2,1)S(1)} %pad_maximum_fusion.2), channel_id=1, source_target_pairs={{0,12},{1,13},{2,14},{3,15},{4,0},{5,1},{6,2},{7,3},{8,4},{9,5},{1... | collective-permute-start | bytes 294920 | tf_op jit(solution)/shard_map/ppermute | solution.py:28
  41.6 9.8 %collective-permute-done.9 = bf16[4,32,2048]{2,1,0:T(8,128)(2,1)S(1)} collective-permute-done((bf16[4,32,2048]{2,1,0:T(8,128)(2,1)S(1)}, bf16[4,32,2048]{2,1,0:T(8,128)(2,1)S(1)}, u32[]{:S(2)}, u32[]{:S(2)}) %collective-permute-start.9) | collective-permute-done | bytes 524320 | tf_op jit(solution)/shard_map/ppermute | solution.py:289
  51.4 0.1 bitcast_add_fusion
  51.6 0.1 dynamic-slice_convert_fusion.2
  51.6 1.2 %collective-permute-start.12 = (bf16[1,32,2048]{2,1,0:T(8,128)(2,1)S(1)}, bf16[1,32,2048]{2,1,0:T(8,128)(2,1)S(1)}, u32[]{:S(2)}, u32[]{:S(2)}) collective-permute-start(bf16[1,32,2048]{2,1,0:T(8,128)(2,1)S(1)} %get-tuple-element.45), channel_id=1, source_target_pairs={{0,12},{1,13},{2,14},{3,15},{4,0},{5,1},{6,2},{7,3},{8,4},{9,5},{1... | collective-permute-start | bytes 393224 | tf_op jit(solution)/shard_map/ppermute | solution.py:289
  52.9 6.0 %collective-permute-start.11 = (bf16[1,32,2048]{2,1,0:T(8,128)(2,1)S(1)}, bf16[1,32,2048]{2,1,0:T(8,128)(2,1)S(1)}, u32[]{:S(2)}, u32[]{:S(2)}) collective-permute-start(bf16[1,32,2048]{2,1,0:T(8,128)(2,1)S(1)} %get-tuple-element.46), channel_id=1, source_target_pairs={{0,8},{1,9},{2,10},{3,11},{4,12},{5,13},{6,14},{7,15},{8,0},{9,1},... | collective-permute-start | bytes 393224 | tf_op jit(solution)/shard_map/ppermute | solution.py:289
  58.9 0.0 collective-permute-start.10
  58.9 1.2 %collective-permute-start.7 = (bf16[2,3,16,512]{3,2,1,0:T(8,128)(2,1)S(1)}, bf16[2,3,16,512]{3,2,1,0:T(8,128)(2,1)S(1)}, u32[]{:S(2)}, u32[]{:S(2)}) collective-permute-start(bf16[2,3,16,512]{3,2,1,0:T(8,128)(2,1)S(1)} %pad_maximum_fusion.3), channel_id=1, source_target_pairs={{0,4},{1,5},{2,6},{3,7},{4,8},{5,9},{6,10},{7,11},{8,12},{9,13},{1... | collective-permute-start | bytes 294920 | tf_op jit(solution)/shard_map/ppermute | solution.py:28
  60.2 0.0 collective-permute-done.6.minus_ref
  60.2 12.5 %collective-permute-done.7.plus_ref = bf16[2,3,16,512]{3,2,1,0:T(8,128)(2,1)S(1)} collective-permute-done((bf16[2,3,16,512]{3,2,1,0:T(8,128)(2,1)S(1)}, bf16[2,3,16,512]{3,2,1,0:T(8,128)(2,1)S(1)}, u32[]{:S(2)}, u32[]{:S(2)}) %collective-permute-start.7) | collective-permute-done | bytes 98336 | tf_op jit(solution)/shard_map/ppermute | solution.py:28
  72.7 0.0 copy-done
  72.7 0.6 copy-done.1
  73.3 2.1 %shard_map.107 = bf16[2,128,512]{2,1,0:T(8,128)(2,1)} custom-call(s32[1,8,16]{2,1,0:T(8,128)} %send_ref.3, f32[2,128,512]{2,1,0:T(8,128)} %get-tuple-element.37.node_ref, bf16[2,1,16,512]{3,2,1,0:T(8,128)(2,1)} %get-tuple-element.49.left_ref, bf16[2,1,16,512]{3,2,1,0:T(8,128)(2,1)} %get-tuple-element.52.right_ref, bf16[2,3,16,512]{3,2,1,0:T(8,128)(2,1)} %copy-done, ...), custom_call_target="tpu_custom_call" | custom-call | tf_op jit(solution)/shard_map/pallas_call | solution.py:370
  75.4 0.0 collective-permute-done.12
  75.4 0.0 collective-permute-done.11
  75.4 0.0 collective-permute-done.10
  75.5 0.8 %add_bitcast_fusion = f32[32,2048]{1,0:T(8,128)} fusion(bf16[1,32,2048]{2,1,0:T(8,128)(2,1)S(1)} %collective-permute-done.12, bf16[1,32,2048]{2,1,0:T(8,128)(2,1)S(1)} %collective-permute-done.11, bf16[1,32,2048]{2,1,0:T(8,128)(2,1)S(1)} %collective-permute-done.10, f32[4,32,2048]{2,1,0:T(8,128)S(1)} %bitcast_add_fusion, s32[]{:T(128)S(6)} %select_n.61), kind=kLoop, calls=%fused_computation.4 | loop fusion | flops 393216 | bytes 917508 | tf_op jit(solution)/shard_map/reshape | solution.py:373
  (11 shorter events, 0.0 us)
Async XLA Ops:
  2.6 3.7 %collective-permute-start.1 = (bf16[2,3,16,512]{3,2,1,0:T(8,128)(2,1)}, bf16[2,3,16,512]{3,2,1,0:T(8,128)(2,1)S(1)}, u32[]{:S(2)}, u32[]{:S(2)}) collective-permute-start(bf16[2,3,16,512]{3,2,1,0:T(8,128)(2,1)} %get-tuple-element.34), channel_id=1, source_target_pairs={{0,12},{1,13},{2,14},{3,15},{4,0},{5,1},{6,2},{7,3},{8,4},{9,5},{1... | collective-permute-start | bytes 294920 | tf_op jit(solution)/shard_map/ppermute | solution.py:28
  2.8 4.0 %collective-permute-start = (bf16[2,3,16,512]{3,2,1,0:T(8,128)(2,1)}, bf16[2,3,16,512]{3,2,1,0:T(8,128)(2,1)S(1)}, u32[]{:S(2)}, u32[]{:S(2)}) collective-permute-start(bf16[2,3,16,512]{3,2,1,0:T(8,128)(2,1)} %get-tuple-element.33), channel_id=1, source_target_pairs={{0,4},{1,5},{2,6},{3,7},{4,8},{5,9},{6,10},{7,11},{8,12},{9,13},{1... | collective-permute-start | bytes 294920 | tf_op jit(solution)/shard_map/ppermute | solution.py:28
  6.3 11.9 %copy-start.2 = (bf16[2,3,16,512]{3,2,1,0:T(8,128)(2,1)}, bf16[2,3,16,512]{3,2,1,0:T(8,128)(2,1)S(1)}, u32[]{:S(2)}) copy-start(bf16[2,3,16,512]{3,2,1,0:T(8,128)(2,1)S(1)} %collective-permute-done.1.minus_ref) | copy-start | bytes 294916
  6.8 11.4 %copy-start.3 = (bf16[2,3,16,512]{3,2,1,0:T(8,128)(2,1)}, bf16[2,3,16,512]{3,2,1,0:T(8,128)(2,1)S(1)}, u32[]{:S(2)}) copy-start(bf16[2,3,16,512]{3,2,1,0:T(8,128)(2,1)S(1)} %collective-permute-done.plus_ref) | copy-start | bytes 294916
  7.6 10.6 %collective-permute-start.2 = (bf16[2,3,16,512]{3,2,1,0:T(8,128)(2,1)S(1)}, bf16[2,3,16,512]{3,2,1,0:T(8,128)(2,1)S(1)}, u32[]{:S(2)}, u32[]{:S(2)}) collective-permute-start(bf16[2,3,16,512]{3,2,1,0:T(8,128)(2,1)S(1)} %pad_maximum_fusion), channel_id=1, source_target_pairs={{0,1},{1,2},{2,3},{3,4},{4,5},{5,6},{6,7},{7,8},{8,9},{9,10},{10,1... | collective-permute-start | bytes 294920 | tf_op jit(solution)/shard_map/ppermute | solution.py:28
  13.7 5.0 %collective-permute-start.3 = (bf16[2,3,16,512]{3,2,1,0:T(8,128)(2,1)S(1)}, bf16[2,3,16,512]{3,2,1,0:T(8,128)(2,1)S(1)}, u32[]{:S(2)}, u32[]{:S(2)}) collective-permute-start(bf16[2,3,16,512]{3,2,1,0:T(8,128)(2,1)S(1)} %pad_maximum_fusion.1), channel_id=1, source_target_pairs={{0,15},{1,0},{2,1},{3,2},{4,3},{5,4},{6,5},{7,6},{8,7},{9,8},{10,9... | collective-permute-start | bytes 294920 | tf_op jit(solution)/shard_map/ppermute | solution.py:28
  18.2 0.6 copy-start.6
  18.7 0.6 copy-start.7
  33.1 2.9 %collective-permute-start.8 = (bf16[8,32,2048]{2,1,0:T(8,128)(2,1)}, bf16[8,32,2048]{2,1,0:T(8,128)(2,1)S(1)}, u32[]{:S(2)}, u32[]{:S(2)}) collective-permute-start(bf16[8,32,2048]{2,1,0:T(8,128)(2,1)} %get-tuple-element.43), channel_id=1, source_target_pairs={{0,1},{1,0},{2,3},{3,2},{4,5},{5,4},{6,7},{7,6},{8,9},{9,8},{10,11... | collective-permute-start | bytes 3145736 | tf_op jit(solution)/shard_map/ppermute | solution.py:360
  33.3 5.3 %collective-permute-start.4 = (bf16[2,3,16,512]{3,2,1,0:T(8,128)(2,1)}, bf16[2,3,16,512]{3,2,1,0:T(8,128)(2,1)S(1)}, u32[]{:S(2)}, u32[]{:S(2)}) collective-permute-start(bf16[2,3,16,512]{3,2,1,0:T(8,128)(2,1)} %get-tuple-element.38), channel_id=1, source_target_pairs={{0,15},{1,0},{2,1},{3,2},{4,3},{5,4},{6,5},{7,6},{8,7},{9,8},{10,9... | collective-permute-start | bytes 294920 | tf_op jit(solution)/shard_map/ppermute | solution.py:28
  33.7 5.6 %collective-permute-start.5 = (bf16[2,3,16,512]{3,2,1,0:T(8,128)(2,1)}, bf16[2,3,16,512]{3,2,1,0:T(8,128)(2,1)S(1)}, u32[]{:S(2)}, u32[]{:S(2)}) collective-permute-start(bf16[2,3,16,512]{3,2,1,0:T(8,128)(2,1)} %get-tuple-element.39), channel_id=1, source_target_pairs={{0,1},{1,2},{2,3},{3,4},{4,5},{5,6},{6,7},{7,8},{8,9},{9,10},{10,1... | collective-permute-start | bytes 294920 | tf_op jit(solution)/shard_map/ppermute | solution.py:28
  36.0 3.8 %copy-start.5 = (bf16[2,1,16,512]{3,2,1,0:T(8,128)(2,1)S(1)}, bf16[2,1,16,512]{3,2,1,0:T(8,128)(2,1)}, u32[]{:S(2)}) copy-start(bf16[2,1,16,512]{3,2,1,0:T(8,128)(2,1)} %get-tuple-element.40) | copy-start | bytes 98308
  38.0 20.9 %copy-start.4 = (bf16[2,1,16,512]{3,2,1,0:T(8,128)(2,1)S(1)}, bf16[2,1,16,512]{3,2,1,0:T(8,128)(2,1)}, u32[]{:S(2)}) copy-start(bf16[2,1,16,512]{3,2,1,0:T(8,128)(2,1)} %get-tuple-element.41) | copy-start | bytes 98308
  38.0 13.4 %collective-permute-start.9 = (bf16[4,32,2048]{2,1,0:T(8,128)(2,1)S(1)}, bf16[4,32,2048]{2,1,0:T(8,128)(2,1)S(1)}, u32[]{:S(2)}, u32[]{:S(2)}) collective-permute-start(bf16[4,32,2048]{2,1,0:T(8,128)(2,1)S(1)} %fusion), channel_id=1, source_target_pairs={{0,2},{1,3},{2,0},{3,1},{4,6},{5,7},{6,4},{7,5},{8,10},{9,11},{10,... | collective-permute-start | bytes 1572872 | tf_op jit(solution)/shard_map/ppermute | solution.py:289
  39.9 20.3 %collective-permute-start.6 = (bf16[2,3,16,512]{3,2,1,0:T(8,128)(2,1)S(1)}, bf16[2,3,16,512]{3,2,1,0:T(8,128)(2,1)S(1)}, u32[]{:S(2)}, u32[]{:S(2)}) collective-permute-start(bf16[2,3,16,512]{3,2,1,0:T(8,128)(2,1)S(1)} %pad_maximum_fusion.2), channel_id=1, source_target_pairs={{0,12},{1,13},{2,14},{3,15},{4,0},{5,1},{6,2},{7,3},{8,4},{9,5},{1... | collective-permute-start | bytes 294920 | tf_op jit(solution)/shard_map/ppermute | solution.py:28
  51.6 23.8 %collective-permute-start.12 = (bf16[1,32,2048]{2,1,0:T(8,128)(2,1)S(1)}, bf16[1,32,2048]{2,1,0:T(8,128)(2,1)S(1)}, u32[]{:S(2)}, u32[]{:S(2)}) collective-permute-start(bf16[1,32,2048]{2,1,0:T(8,128)(2,1)S(1)} %get-tuple-element.45), channel_id=1, source_target_pairs={{0,12},{1,13},{2,14},{3,15},{4,0},{5,1},{6,2},{7,3},{8,4},{9,5},{1... | collective-permute-start | bytes 393224 | tf_op jit(solution)/shard_map/ppermute | solution.py:289
  52.9 22.6 %collective-permute-start.11 = (bf16[1,32,2048]{2,1,0:T(8,128)(2,1)S(1)}, bf16[1,32,2048]{2,1,0:T(8,128)(2,1)S(1)}, u32[]{:S(2)}, u32[]{:S(2)}) collective-permute-start(bf16[1,32,2048]{2,1,0:T(8,128)(2,1)S(1)} %get-tuple-element.46), channel_id=1, source_target_pairs={{0,8},{1,9},{2,10},{3,11},{4,12},{5,13},{6,14},{7,15},{8,0},{9,1},... | collective-permute-start | bytes 393224 | tf_op jit(solution)/shard_map/ppermute | solution.py:289
  58.9 16.5 %collective-permute-start.10 = (bf16[1,32,2048]{2,1,0:T(8,128)(2,1)S(1)}, bf16[1,32,2048]{2,1,0:T(8,128)(2,1)S(1)}, u32[]{:S(2)}, u32[]{:S(2)}) collective-permute-start(bf16[1,32,2048]{2,1,0:T(8,128)(2,1)S(1)} %get-tuple-element.44), channel_id=1, source_target_pairs={{0,4},{1,5},{2,6},{3,7},{4,8},{5,9},{6,10},{7,11},{8,12},{9,13},{1... | collective-permute-start | bytes 393224 | tf_op jit(solution)/shard_map/ppermute | solution.py:289
  58.9 13.7 %collective-permute-start.7 = (bf16[2,3,16,512]{3,2,1,0:T(8,128)(2,1)S(1)}, bf16[2,3,16,512]{3,2,1,0:T(8,128)(2,1)S(1)}, u32[]{:S(2)}, u32[]{:S(2)}) collective-permute-start(bf16[2,3,16,512]{3,2,1,0:T(8,128)(2,1)S(1)} %pad_maximum_fusion.3), channel_id=1, source_target_pairs={{0,4},{1,5},{2,6},{3,7},{4,8},{5,9},{6,10},{7,11},{8,12},{9,13},{1... | collective-permute-start | bytes 294920 | tf_op jit(solution)/shard_map/ppermute | solution.py:28
  60.2 12.5 %copy-start = (bf16[2,3,16,512]{3,2,1,0:T(8,128)(2,1)}, bf16[2,3,16,512]{3,2,1,0:T(8,128)(2,1)S(1)}, u32[]{:S(2)}) copy-start(bf16[2,3,16,512]{3,2,1,0:T(8,128)(2,1)S(1)} %collective-permute-done.6.minus_ref) | copy-start | bytes 294916
  72.7 0.6 copy-start.1

commit v2 on v1

v2 whole, which is shorter than its diff:
```python
import functools
import math

import jax
import jax.numpy as jnp
from jax import lax
from jax.experimental import pallas as pl
from jax.experimental.pallas import tpu as pltpu
from jax.sharding import PartitionSpec as P

HEADS = 16
score_cap = 5.0
MIB = 1024 * 1024
f32 = jnp.float32
bf16 = jnp.bfloat16


def nn(a, b):
    return lax.dot_general(a, b, (((1,), (0,)), ((), ())), preferred_element_type=f32)


def nt(a, b):
    return lax.dot_general(a, b, (((1,), (1,)), ((), ())), preferred_element_type=f32)


def shifted(shard, by):
    count = lax.axis_size("patch")
    return lax.ppermute(shard, "patch", [(i, (i + by) % count) for i in range(count)])


def sent_selector(send_rows, node_rows):
    adjacent, slots = send_rows.shape
    halo = adjacent * slots
    wide = jnp.concatenate([send_rows] * adjacent, axis=1)
    own = lax.broadcasted_iota(jnp.int32, (adjacent, halo), 1) // slots == lax.broadcasted_iota(
        jnp.int32, (adjacent, halo), 0
    )
    ids = jnp.sum(jnp.where(own, wide, 0), axis=0, keepdims=True)
    nodes = lax.broadcasted_iota(jnp.int32, (node_rows, halo), 0)
    return jnp.where(nodes == ids, 1.0, 0.0).astype(f32)


def gather_kernel(slots, send_ref, x_ref, plus_ref, minus_ref, right_ref, left_ref):
    members, node_rows, _ = x_ref.shape
    pick = sent_selector(send_ref[0], node_rows).T.astype(bf16)
    for m in range(members):
        rows = nn(pick, x_ref[m]).astype(bf16)

        def part(k):
            return rows[k * slots : (k + 1) * slots]

        for i, k in enumerate((2, 6, 4)):
            plus_ref[m, i] = part(k)
        for i, k in enumerate((3, 5, 7)):
            minus_ref[m, i] = part(k)
        right_ref[m, 0] = part(0)
        left_ref[m, 0] = part(1)


def relay_kernel(after_ref, own_a, own_b, plus_ref, minus_ref, a_ref, b_ref):
    a_ref[:, 0:1] = own_a[...]
    a_ref[:, 1:2] = plus_ref[:, 1:2]
    a_ref[:, 2:3] = minus_ref[:, 1:2]
    b_ref[:, 0:1] = own_b[...]
    b_ref[:, 1:2] = plus_ref[:, 2:3]
    b_ref[:, 2:3] = minus_ref[:, 2:3]


def back_relay_kernel(after_ref, own_minus, own_plus, right_ref, left_ref, minus_ref, plus_ref):
    minus_ref[:, 0:1] = own_minus[...]
    minus_ref[:, 1:2] = right_ref[:, 1:2]
    minus_ref[:, 2:3] = left_ref[:, 1:2]
    plus_ref[:, 0:1] = own_plus[...]
    plus_ref[:, 1:2] = right_ref[:, 2:3]
    plus_ref[:, 2:3] = left_ref[:, 2:3]


Q, K, V, G, QT, KT, VT, GT = range(8)


def local_kernel(after_ref, x_ref, og_ref, wq_ref, wk_ref, wv_ref, wo_ref, *out_refs):
    loc_refs, xt_ref = out_refs[:-1], out_refs[-1]
    members, node_rows, width = x_ref.shape
    x = x_ref[...].reshape(members * node_rows, width)
    og = og_ref[...].reshape(members * node_rows, width)

    def put(rows, kind):
        for m in range(members):
            for g, ref in enumerate(loc_refs):
                block = rows[m * node_rows : (m + 1) * node_rows, g * 128 : (g + 1) * 128]
                ref[kind, m] = block
                ref[kind + 4, m] = block.T

    put(nn(x, wq_ref[...]).astype(bf16), Q)
    put(nn(x, wk_ref[...]).astype(bf16), K)
    put(nn(x, wv_ref[...]).astype(bf16), V)
    put(nt(og, wo_ref[...]).astype(bf16), G)
    for m in range(members):
        xt_ref[m] = x_ref[m].T


def mask_kernel(after_ref, neigh_ref, count_ref, mask_ref):
    neigh = neigh_ref[...].T
    slots, node_rows = neigh.shape
    table = mask_ref.shape[0]
    order = lax.broadcasted_iota(jnp.int32, neigh.shape, 0)
    tail = jnp.where(order >= count_ref[...], neigh, -1)[slots // 2 :]
    half = table // 2
    for part in range(2):
        columns = lax.broadcasted_iota(jnp.int32, (half, node_rows), 0) + part * half
        kept = jnp.ones((half, node_rows), f32)
        for j in range(slots // 2):
            kept = jnp.where(tail[j : j + 1] == columns, 0.0, kept)
        mask_ref[part * half : (part + 1) * half] = kept


def halo_kernel(plus_ref, minus_ref, right_ref, left_ref, xt_ref, wk_ref, wv_ref, *out_refs):
    halo_refs, xtf_ref = out_refs[:-1], out_refs[-1]
    members, _, node_rows = xt_ref.shape
    for m in range(members):
        pieces = [None] * 8
        for ref, order in (
            (right_ref, (0, 6, 5)),
            (left_ref, (1, 4, 7)),
            (plus_ref, (2,)),
            (minus_ref, (3,)),
        ):
            for i, k in enumerate(order):
                pieces[k] = ref[m, i]
        halo = jnp.concatenate(pieces, axis=0)
        xtf_ref[m, :, :node_rows] = xt_ref[m]
        xtf_ref[m, :, node_rows:] = halo.T
        for kind, w_ref in enumerate((wk_ref, wv_ref)):
            rows = nn(halo, w_ref[...]).astype(bf16)
            for g, ref in enumerate(halo_refs):
                block = rows[:, g * 128 : (g + 1) * 128]
                ref[kind, m] = block
                ref[kind + 2, m] = block.T


def attention_kernel(
    extra, me_ref, *refs,
):
    refs = refs[extra:]
    loc, halo, mask_ref, xtf, og_ref = refs[:5]
    own_ref, other_ref, send_ref, dq_ref, dk_ref, dv_ref = refs[5:11]
    score, grad, slope, dw, wos = refs[11:]
    _, members, node_rows, _ = loc.shape
    table = mask_ref.shape[0]
    width = og_ref.shape[2]
    head = width // HEADS
    per = 128 // head
    scale = 1.0 / math.sqrt(head)

    row_head = lax.broadcasted_iota(jnp.int32, (128, node_rows), 0) // head
    lane_head = lax.broadcasted_iota(jnp.int32, (node_rows, 128), 1) // head

    def spread_t(block):
        zero = jnp.zeros_like(block)
        return jnp.concatenate([jnp.where(row_head == h, block, zero) for h in range(per)], axis=1)

    def spread_n(block):
        zero = jnp.zeros_like(block)
        return jnp.concatenate([jnp.where(lane_head == h, block, zero) for h in range(per)], axis=0)

    strip = 64
    for m in range(members):
        kg = jnp.concatenate([loc[K, m], halo[0, m]], axis=0)
        vg = jnp.concatenate([loc[V, m], halo[1, m]], axis=0)
        score[m] = nn(kg, spread_t(loc[QT, m]))
        grad[m] = nn(vg, spread_t(loc[GT, m]))

    wo_total = None
    kv_total = None
    q_total = None
    for m in range(members):
        probs = []
        for h in range(per):
            lanes = slice(h * node_rows, (h + 1) * node_rows)
            den = jnp.zeros((8, node_rows), f32)
            inner = jnp.zeros((8, node_rows), f32)
            for c in range(0, table, strip):
                at = (m, slice(c, c + strip), lanes)
                t = jnp.tanh(score[at] * (scale / score_cap))
                e = jnp.exp2(t * (score_cap / math.log(2.0))) * mask_ref[c : c + strip]
                den = den + jnp.sum(e.reshape(strip // 8, 8, node_rows), axis=0)
                inner = inner + jnp.sum((e * grad[at]).reshape(strip // 8, 8, node_rows), axis=0)
                score[at] = e
                slope[at] = e * (scale - scale * (t * t))
            r = 1.0 / jnp.sum(den, axis=0, keepdims=True)
            inner = jnp.sum(inner, axis=0, keepdims=True) * r
            column = []
            scores = []
            for c in range(0, table, strip):
                at = (m, slice(c, c + strip), lanes)
                column.append((score[at] * r).astype(bf16))
                scores.append(((slope[at] * r) * (grad[at] - inner)).astype(bf16))
            probs.append((jnp.concatenate(column, axis=0), jnp.concatenate(scores, axis=0)))
        pb = jnp.concatenate([p for p, _ in probs], axis=1)
        ds = jnp.concatenate([s for _, s in probs], axis=1)
        ktg = jnp.concatenate([loc[KT, m], halo[2, m]], axis=1)
        vtg = jnp.concatenate([loc[VT, m], halo[3, m]], axis=1)
        att, dqt = [], []
        for h in range(0, per, 2):
            lanes = slice(h * node_rows, (h + 2) * node_rows)
            rows = slice(h * head, (h + 2) * head)
            a = nn(vtg[rows], pb[:, lanes])
            b = nn(ktg[rows], ds[:, lanes])
            for j in range(2):
                inside = (slice(j * head, (j + 1) * head), slice(j * node_rows, (j + 1) * node_rows))
                att.append(a[inside].astype(bf16))
                dqt.append(b[inside].astype(bf16))
        att = jnp.concatenate(att, axis=0)
        dq = jnp.concatenate(dqt, axis=0).T
        dk = nn(ds, spread_n(loc[Q, m])).astype(bf16)
        dv = nn(pb, spread_n(loc[G, m])).astype(bf16)
        dq_ref[m], dk_ref[m], dv_ref[m] = dq, dk, dv
        wo_term = nn(att, og_ref[m])
        kv_term = nn(xtf[m], jnp.concatenate([dk, dv], axis=1))
        q_term = nn(xtf[m, :, :node_rows], dq)
        wo_total = wo_term if m == 0 else wo_total + wo_term
        kv_total = kv_term if m == 0 else kv_total + kv_term
        q_total = q_term if m == 0 else q_total + q_term

    planes, _, _, rows, _ = dw.shape
    inner_planes = wos.shape[0]
    dw[:, :, :, :, :128] = q_total.reshape(planes, 2, 2, rows, 128)
    dw[:, :, :, :, 128:] = kv_total.reshape(planes, 2, 2, rows, 256)
    wos[...] = wo_total.reshape(inner_planes, 2, 2, rows, width)
    me = me_ref[0]
    c, y, z = me % 2, (me // 2) % 2, me // 4
    for k in range(planes):
        zk = (z + k) % planes
        own_ref[k, :, :384] = dw[zk, y, c]
        other_ref[k, :, :384] = dw[zk, 1 - y, c]
        send_ref[0, k, :, :384] = dw[zk, 1 - y, 1 - c].astype(bf16)
        send_ref[1, k, :, :384] = dw[zk, y, 1 - c].astype(bf16)
    for i in range(inner_planes):
        for n in range(width // 128):
            k = n * inner_planes + i
            lanes = slice(n * 128, (n + 1) * 128)
            own_ref[k, :, 384:] = wos[i, y, c, :, lanes]
            other_ref[k, :, 384:] = wos[i, 1 - y, c, :, lanes]
            send_ref[0, k, :, 384:] = wos[i, 1 - y, 1 - c, :, lanes].astype(bf16)
            send_ref[1, k, :, 384:] = wos[i, y, 1 - c, :, lanes].astype(bf16)


def node_kernel(groups, skip, *refs):
    refs = refs[skip:]
    dqs, dks, dvs = refs[:groups], refs[groups : 2 * groups], refs[2 * groups : 3 * groups]
    wq_ref, wk_ref, wv_ref, node_ref, left_ref, right_ref, minus_ref, plus_ref = refs[3 * groups :]
    members, node_rows, _ = dqs[0].shape
    slots = left_ref.shape[2]

    def whole(parts, m):
        return jnp.concatenate([part[m] for part in parts], axis=1)

    for m in range(members):
        spread = nt(whole(dks, m), wk_ref[...]) + nt(whole(dvs, m), wv_ref[...])
        node_ref[m] = spread[:node_rows] + nt(whole(dqs, m), wq_ref[...])
        halo = spread[node_rows:].astype(bf16)
        for ref, order in (
            (left_ref, (0, 6, 5)),
            (right_ref, (1, 4, 7)),
            (minus_ref, (2,)),
            (plus_ref, (3,)),
        ):
            for i, k in enumerate(order):
                ref[m, i] = halo[k * slots : (k + 1) * slots]


def sums(half, refs, k):
    owns, core_in, y_in = refs[:half], refs[half : 2 * half], refs[2 * half : 3 * half]
    return [
        own[k] + core[1, k].astype(f32) + y[k].astype(f32)
        for own, core, y in zip(owns, core_in, y_in)
    ]


def first_kernel(half, skip, *refs):
    ins, outs = refs[skip : skip + 3 * half], refs[skip + 3 * half :]
    own_ref, projection_ref, *sent = outs
    planes = len(sent) + 1
    for k in range(planes):
        parts = sums(half, ins, k)
        gather_projection(parts, k, planes, projection_ref, 0)
        row = jnp.concatenate([part[:, :384] for part in parts], axis=1)
        if k:
            sent[k - 1][...] = row.astype(bf16)
        else:
            own_ref[...] = row


def gather_projection(parts, k, planes, projection_ref, start):
    inner_planes = planes * 128 // projection_ref.shape[2]
    quarter, inner = divmod(k, inner_planes)
    for i, part in enumerate(parts):
        plane = start + i * inner_planes + inner
        projection_ref[plane, :, quarter * 128 : (quarter + 1) * 128] = part[:, 384:]


def second_kernel(half, planes, me_ref, *refs):
    refs = refs[planes:]
    first_ref, ins = refs[0], refs[1 : 1 + 3 * half]
    own_ref, *sent = refs[1 + 3 * half : -1]
    projection_ref = refs[-1]
    done = first_ref.shape[0]
    projection_ref[:done] = first_ref[...]
    rows = []
    for k in range(planes):
        parts = sums(half, ins, k)
        gather_projection(parts, k, planes, projection_ref, done)
        rows.append(jnp.concatenate([part[:, :384] for part in parts], axis=1))
    wide = 384 * half
    z = me_ref[0] // 4
    for k in range(planes):
        projection = projection_ref[(z + k) % planes]
        if k:
            sent[k - 1][:, :wide] = rows[k].astype(bf16)
            sent[k - 1][:, wide:] = projection.astype(bf16)
        else:
            own_ref[:, :wide] = rows[k]
            own_ref[:, wide:] = projection


def weight_kernel(half, planes, after_ref, own_a, own_b, *refs):
    z_a, z_b, out_ref = refs[: planes - 1], refs[planes - 1 : -1], refs[-1]
    a, b = own_a[...], own_b[...]
    for ref in z_a:
        a = a + ref[...].astype(f32)
    for ref in z_b:
        b = b + ref[...].astype(f32)
    width = 256 * half
    for i, part in enumerate((a, b)):
        for j in range(half):
            for n in range(3):
                at = n * width + (i * half + j) * 128
                out_ref[:, at : at + 128] = part[:, j * 384 + n * 128 : j * 384 + (n + 1) * 128]
    out_ref[:, 3 * width :] = b[:, 384 * half :]


def finish_kernel(send_ref, node_ref, left_ref, right_ref, minus_ref, plus_ref, out_ref):
    members, node_rows, _ = node_ref.shape
    pick = sent_selector(send_ref[0], node_rows).astype(bf16)
    for m in range(members):
        pieces = [None] * 8
        for ref, order in (
            (left_ref, (0,)),
            (right_ref, (1,)),
            (minus_ref, (2, 6, 4)),
            (plus_ref, (3, 5, 7)),
        ):
            for i, k in enumerate(order):
                pieces[k] = ref[m, i]
        arriving = jnp.concatenate(pieces, axis=0)
        out_ref[m] = (node_ref[m] + nn(pick, arriving)).astype(bf16)


def call(kernel, outs, operands, specs=None, scratch=(), flops=10**8, limit=12):
    specs = list(specs or ())
    specs += [pltpu.VMEM] * (len(operands) - len(specs))
    return pl.pallas_call(
        kernel,
        out_shape=[jax.ShapeDtypeStruct(*o) for o in outs],
        in_specs=[pl.BlockSpec(memory_space=s) for s in specs],
        scratch_shapes=list(scratch),
        compiler_params=pltpu.CompilerParams(vmem_limit_bytes=limit * MIB),
        cost_estimate=pl.CostEstimate(flops=flops, bytes_accessed=10**6, transcendentals=0),
    )(*operands)


def body(
    node_features, out_grad, w_query, w_key, w_value, w_out, neighbours, neighbour_count, send_rows
):
    members, node_rows, width = node_features.shape
    count = lax.axis_size("patch")
    row_width = min(8, count // 4)
    _, adjacent, slots = send_rows.shape
    table = node_rows + adjacent * slots
    groups = width // 128
    me = lax.axis_index("patch")
    three = ((members, 3, slots, width), bf16)
    one = ((members, 1, slots, width), bf16)

    to_plus, to_minus, own_right, own_left = call(
        functools.partial(gather_kernel, slots), [three, three, one, one],
        (send_rows, node_features),
    )
    plus = shifted(to_plus, row_width)
    minus = shifted(to_minus, -row_width)
    *loc, xt = call(
        local_kernel,
        [((8, members, node_rows, 128), bf16)] * groups + [((members, width, node_rows), bf16)],
        (own_right, node_features, out_grad, w_query, w_key, w_value, w_out),
        specs=[pl.ANY], flops=3 * 10**9, limit=16,
    )
    to_right, to_left = call(
        relay_kernel, [three, three], (loc[0], own_right, own_left, plus, minus), specs=[pl.ANY]
    )
    right = shifted(to_right, 1)
    left = shifted(to_left, -1)
    (mask,) = call(
        mask_kernel, [((table, node_rows), f32)],
        (to_right, neighbours, neighbour_count.reshape(1, node_rows)),
        specs=[pl.ANY], flops=2 * 10**9,
    )
    *halo, xtf = call(
        halo_kernel,
        [((4, members, node_rows, 128), bf16)] * groups + [((members, width, table), bf16)],
        (plus, minus, right, left, xt, w_key, w_value), flops=10**9,
    )

    planes, rows = count // 4, width // count
    inner_planes = planes * 128 // width
    keep = ((planes, rows, 512), f32)
    flip = [(i, i ^ 1) for i in range(count)]
    flop = [(i, i ^ 2) for i in range(count)]
    place = me.reshape(1)
    dqs, dks, dvs, owns, others, core_in, y_out, y_in = [], [], [], [], [], [], [], []

    def pass_y():
        i = len(y_out)
        y_out.append((others[i] + core_in[i][0].astype(f32)).astype(bf16))
        y_in.append(lax.ppermute(y_out[i], "patch", flop))

    for g in range(groups):
        extra = ()
        if g >= 2:
            pass_y()
            extra = tuple(y_out[-1:] + y_in[:-1][-1:])
        own, other, send, dq, dk, dv = call(
            functools.partial(attention_kernel, len(extra)),
            [
                keep, keep, ((2, planes, rows, 512), bf16),
                ((members, node_rows, 128), bf16),
                ((members, table, 128), bf16),
                ((members, table, 128), bf16),
            ],
            (place, *extra, loc[g], halo[g], mask, xtf, out_grad),
            specs=[pltpu.SMEM] + [pl.ANY] * len(extra),
            scratch=[pltpu.VMEM((members, table, 512), f32)] * 3
            + [
                pltpu.VMEM((planes, 2, 2, rows, 384), f32),
                pltpu.VMEM((inner_planes, 2, 2, rows, width), f32),
            ],
            flops=35 * 10**8, limit=20,
        )
        dqs.append(dq)
        dks.append(dk)
        dvs.append(dv)
        owns.append(own)
        others.append(other)
        core_in.append(lax.ppermute(send, "patch", flip))

    def along_z(sent):
        return [
            lax.ppermute(s, "patch", [(i, (i + 4 * k) % count) for i in range(count)])
            for k, s in enumerate(sent, 1)
        ]

    half = groups // 2
    wide = 384 * half
    projection = ((half * inner_planes, rows, width), f32)
    own_a, out_a, *sent = call(
        functools.partial(first_kernel, half, 1),
        [((rows, wide), f32), projection] + [((rows, wide), bf16)] * (planes - 1),
        (owns[-1], *owns[:half], *core_in[:half], *y_in[:half]),
        specs=[pl.ANY],
    )
    z_a = along_z(sent)
    while len(y_out) < groups:
        pass_y()
    node, back_left, back_right, back_minus, back_plus = call(
        functools.partial(node_kernel, groups, planes + 1),
        [((members, node_rows, width), f32), three, three, one, one],
        (*sent, *y_out[half:], *dqs, *dks, *dvs, w_query, w_key, w_value),
        specs=[pl.ANY] * (planes + 1), flops=2 * 10**9,
    )
    from_right = shifted(back_left, -1)
    from_left = shifted(back_right, 1)
    own_b, *sent = call(
        functools.partial(second_kernel, half, planes),
        [((rows, wide + width), f32)] + [((rows, wide + width), bf16)] * (planes - 1),
        (place, node, *z_a, out_a, *owns[half:], *core_in[half:], *y_in[half:]),
        specs=[pltpu.SMEM] + [pl.ANY] * planes,
        scratch=[pltpu.VMEM((planes, rows, width), f32)],
    )
    z_b = along_z(sent)
    to_minus, to_plus = call(
        back_relay_kernel, [three, three],
        (own_b, back_minus, back_plus, from_right, from_left), specs=[pl.ANY],
    )
    from_plus = shifted(to_minus, -row_width)
    from_minus = shifted(to_plus, row_width)
    (node_grad,) = call(
        finish_kernel, [((members, node_rows, width), bf16)],
        (send_rows, node, from_right, from_left, from_plus, from_minus), flops=10**9,
    )
    (weight_grad,) = call(
        functools.partial(weight_kernel, half, planes), [((rows, 4 * width), f32)],
        (node_grad, own_a, own_b, *z_a, *z_b), specs=[pl.ANY],
    )
    return (node_grad, weight_grad)


def solution(mesh):
    in_specs = (
        P("groups", "patch", None),
        P("groups", "patch", None),
        P(),
        P(),
        P(),
        P(),
        P("patch", None),
        P("patch"),
        P("patch", None, None),
    )
    out_specs = (P("groups", "patch", None), P(("groups", "patch"), None))
    return jax.shard_map(body, mesh=mesh, in_specs=in_specs, out_specs=out_specs, check_vma=False)
```

time: 76.6 us -> 63.8 us (0.83)
  the two profiles are of different devices: /device:TPU:21 before, /device:TPU:0 now
where the time goes in v2:
time: 63.8 us; the launch traced here: 62.8 us
  starting transfers between devices  25.5 us (40%)
  waiting for transfers between devices  15.4 us (24%)
  Pallas kernels  12.9 us (20%)
  local copies, waits for them, and re-layouts  8.07 us (13%)
  between operations  0.88 us (1%)
    pallas_call x15, Pallas kernels, call(): pl.pallas_call(kernel, out_shape=[jax.ShapeDtypeStruct(*o) for o in outs]...  12.9 us
    ppermute x8, starting transfers between devices, shifted(): lax.ppermute(shard, 'patch', [(i, (i + by) % count) for i in range(count)])  12.3 us
    ppermute x6, starting transfers between devices, along_z(): lax.ppermute(s, 'patch', [(i, (i + 4 * k) % count) for i in range(count)])  9.19 us
    unnamed x32, local copies, waits for them, and re-layouts  8.07 us
    ppermute x6, waiting for transfers between devices, along_z(): lax.ppermute(s, 'patch', [(i, (i + 4 * k) % count) for i in range(count)])  5.9 us
    ppermute x8, waiting for transfers between devices, shifted(): lax.ppermute(shard, 'patch', [(i, (i + by) % count) for i in range(count)])  4.98 us
    ppermute x4, waiting for transfers between devices, pass_y(): y_in.append(lax.ppermute(y_out[i], 'patch', flop))  3.44 us
    ppermute x4, starting transfers between devices, pass_y(): y_in.append(lax.ppermute(y_out[i], 'patch', flop))  3.26 us
  transfers between devices with their start and end apart: 22, of which 10 were waited for; matrix products, arithmetic and copies ran while one was open for 0% of the time, Pallas kernels for 15%

profile of v2, /device:TPU:0, one launch (start us, length us, event | category | flops | bytes accessed | tf_op | source)
XLA Modules:
  0.0 62.8 jit_solution(8314862494838409833)
XLA Ops:
  0.6 0.9 %copy-done.8 = bf16[2,128,512]{2,1,0:T(8,128)(2,1)S(1)} copy-done((bf16[2,128,512]{2,1,0:T(8,128)(2,1)S(1)}, bf16[2,128,512]{2,1,0:T(8,128)(2,1)}, u32[]{:S(2)}) %copy-start.8) | copy-done | bytes 262168
  1.6 0.7 %copy-done.13 = s32[1,8,16]{2,1,0:T(8,128)S(1)} copy-done((s32[1,8,16]{2,1,0:T(8,128)S(1)}, s32[1,8,16]{2,1,0:T(8,128)}, u32[]{:S(2)}) %copy-start.13) | copy-done | bytes 536
  2.3 0.3 shard_map.104
  2.6 3.1 %collective-permute-start = (bf16[2,3,16,512]{3,2,1,0:T(8,128)(2,1)S(1)}, bf16[2,3,16,512]{3,2,1,0:T(8,128)(2,1)S(1)}, u32[]{:S(2)}, u32[]{:S(2)}) collective-permute-start(bf16[2,3,16,512]{3,2,1,0:T(8,128)(2,1)S(1)} %get-tuple-element.60), channel_id=1, source_target_pairs={{0,4},{1,5},{2,6},{3,7},{4,8},{5,9},{6,10},{7,11},{8,12},{9,13},{1... | collective-permute-start | bytes 294920 | tf_op jit(solution)/shard_map/ppermute | solution.py:28
  5.7 2.1 %collective-permute-start.1 = (bf16[2,3,16,512]{3,2,1,0:T(8,128)(2,1)S(1)}, bf16[2,3,16,512]{3,2,1,0:T(8,128)(2,1)S(1)}, u32[]{:S(2)}, u32[]{:S(2)}) collective-permute-start(bf16[2,3,16,512]{3,2,1,0:T(8,128)(2,1)S(1)} %get-tuple-element.61), channel_id=1, source_target_pairs={{0,12},{1,13},{2,14},{3,15},{4,0},{5,1},{6,2},{7,3},{8,4},{9,5},{1... | collective-permute-start | bytes 294920 | tf_op jit(solution)/shard_map/ppermute | solution.py:28
  7.8 1.0 %copy-done.1 = bf16[512,512]{1,0:T(8,128)(2,1)S(1)} copy-done((bf16[512,512]{1,0:T(8,128)(2,1)S(1)}, bf16[512,512]{1,0:T(8,128)(2,1)}, u32[]{:S(2)}) %copy-start.1) | copy-done | bytes 524312
  8.8 1.0 %copy-done.2 = bf16[512,512]{1,0:T(8,128)(2,1)S(1)} copy-done((bf16[512,512]{1,0:T(8,128)(2,1)S(1)}, bf16[512,512]{1,0:T(8,128)(2,1)}, u32[]{:S(2)}) %copy-start.2) | copy-done | bytes 524312
  9.9 1.0 %copy-done.4 = bf16[512,512]{1,0:T(8,128)(2,1)S(1)} copy-done((bf16[512,512]{1,0:T(8,128)(2,1)S(1)}, bf16[512,512]{1,0:T(8,128)(2,1)}, u32[]{:S(2)}) %copy-start.4) | copy-done | bytes 524312
  10.9 1.0 %copy-done.6 = bf16[512,512]{1,0:T(8,128)(2,1)S(1)} copy-done((bf16[512,512]{1,0:T(8,128)(2,1)S(1)}, bf16[512,512]{1,0:T(8,128)(2,1)}, u32[]{:S(2)}) %copy-start.6) | copy-done | bytes 524312
  12.0 0.9 %copy-done.10 = bf16[2,128,512]{2,1,0:T(8,128)(2,1)S(1)} copy-done((bf16[2,128,512]{2,1,0:T(8,128)(2,1)S(1)}, bf16[2,128,512]{2,1,0:T(8,128)(2,1)}, u32[]{:S(2)}) %copy-start.10) | copy-done | bytes 262168
  12.9 0.8 %shard_map.105 = (bf16[8,2,128,128]{3,2,1,0:T(8,128)(2,1)S(1)}, bf16[8,2,128,128]{3,2,1,0:T(8,128)(2,1)S(1)}, bf16[8,2,128,128]{3,2,1,0:T(8,128)(2,1)S(1)}, bf16...) custom-call(bf16[2,1,16,512]{3,2,1,0:T(8,128)(2,1)S(1)} %get-tuple-element.58.after_ref.own_a, ...), custom_call_target="tpu_custom_call" | custom-call | flops 3000000000 | bytes 1000000 | tf_op jit(solution)/shard_map/pallas_call | solution.py:362
  13.9 4.4 %collective-permute-start.3 = (bf16[2,3,16,512]{3,2,1,0:T(8,128)(2,1)S(1)}, bf16[2,3,16,512]{3,2,1,0:T(8,128)(2,1)S(1)}, u32[]{:S(2)}, u32[]{:S(2)}) collective-permute-start(bf16[2,3,16,512]{3,2,1,0:T(8,128)(2,1)S(1)} %get-tuple-element.65), channel_id=1, source_target_pairs={{0,15},{1,0},{2,1},{3,2},{4,3},{5,4},{6,5},{7,6},{8,7},{9,8},{10,9... | collective-permute-start | bytes 294920 | tf_op jit(solution)/shard_map/ppermute | solution.py:28
  18.3 1.4 %shard_map.108.refs_2_.refs_4_.refs_3_ = f32[256,128]{1,0:T(8,128)S(1)} custom-call(bf16[2,3,16,512]{3,2,1,0:T(8,128)(2,1)S(1)} %get-tuple-element.64.after_ref, s32[128,256]{1,0:T(8,128)S(1)} %copy-done.12, s32[1,128]{1,0:T(1,128)S(1)} %bitcast.22), custom_call_target="tpu_custom_call" | custom-call | flops 2000000000 | bytes 1000000 | tf_op jit(solution)/shard_map/pallas_call | solution.py:362
  19.7 0.9 %collective-permute-done.2.right_ref = bf16[2,3,16,512]{3,2,1,0:T(8,128)(2,1)S(1)} collective-permute-done((bf16[2,3,16,512]{3,2,1,0:T(8,128)(2,1)S(1)}, bf16[2,3,16,512]{3,2,1,0:T(8,128)(2,1)S(1)}, u32[]{:S(2)}, u32[]{:S(2)}) %collective-permute-start.2) | collective-permute-done | bytes 98336 | tf_op jit(solution)/shard_map/ppermute | solution.py:28
  20.7 0.6 shard_map.107
  21.3 0.3 copy-done.11
  21.6 1.7 %shard_map.110 = (f32[4,32,512]{2,1,0:T(8,128)S(1)}, f32[4,32,512]{2,1,0:T(8,128)S(1)}, bf16[2,4,32,512]{3,2,1,0:T(8,128)(2,1)S(1)}, bf16[2,128,128]{2,1,0:T(8,1...) custom-call(s32[1]{0:T(128)} %bitcast.me_ref, ...), custom_call_target="tpu_custom_call" | custom-call | flops 3500000000 | bytes 1000000 | tf_op jit(solution)/shard_map/pallas_call | solution.py:362
  23.3 0.1 collective-permute-start.5
  23.4 1.7 %shard_map.109 = (f32[4,32,512]{2,1,0:T(8,128)S(1)}, f32[4,32,512]{2,1,0:T(8,128)S(1)}, bf16[2,4,32,512]{3,2,1,0:T(8,128)(2,1)S(1)}, bf16[2,128,128]{2,1,0:T(8,1...) custom-call(s32[1]{0:T(128)} %bitcast.me_ref, ...), custom_call_target="tpu_custom_call" | custom-call | flops 3500000000 | bytes 1000000 | tf_op jit(solution)/shard_map/pallas_call | solution.py:362
  25.1 0.5 collective-permute-start.4
  25.7 0.1 collective-permute-start.6
  25.8 1.0 %collective-permute-done.4.refs_4_ = bf16[2,4,32,512]{3,2,1,0:T(8,128)(2,1)S(1)} collective-permute-done((bf16[2,4,32,512]{3,2,1,0:T(8,128)(2,1)S(1)}, bf16[2,4,32,512]{3,2,1,0:T(8,128)(2,1)S(1)}, u32[]{:S(2)}, u32[]{:S(2)}) %collective-permute-start.4) | collective-permute-done | bytes 262176 | tf_op jit(solution)/shard_map/ppermute | solution.py:453
  26.9 1.0 %collective-permute-start.7 = (bf16[4,32,512]{2,1,0:T(8,128)(2,1)S(1)}, bf16[4,32,512]{2,1,0:T(8,128)(2,1)S(1)}, u32[]{:S(2)}, u32[]{:S(2)}) collective-permute-start(bf16[4,32,512]{2,1,0:T(8,128)(2,1)S(1)} %fusion.3.refs_0_), channel_id=1, source_target_pairs={{0,2},{1,3},{2,0},{3,1},{4,6},{5,7},{6,4},{7,5},{8,10},{9,11},{10,... | collective-permute-start | bytes 393224 | tf_op jit(solution)/shard_map/ppermute | solution.py:424
  27.9 1.7 %shard_map.113 = (f32[4,32,512]{2,1,0:T(8,128)S(1)}, f32[4,32,512]{2,1,0:T(8,128)S(1)}, bf16[2,4,32,512]{3,2,1,0:T(8,128)(2,1)S(1)}, bf16[2,128,128]{2,1,0:T(8,1...) custom-call(s32[1]{0:T(128)} %bitcast.me_ref, bf16[4,32,512]{2,1,0:T(8,128)(2,1)S(1)} %fusion.2.refs_0_, ...), custom_call_target="tpu_custom_call" | custom-call | flops 3500000000 | bytes 1000000 | tf_op jit(solution)/shard_map/pallas_call | solution.py:362
  29.6 2.5 %collective-permute-done.6.refs_1_.refs_5_ = bf16[4,32,512]{2,1,0:T(8,128)(2,1)S(1)} collective-permute-done((bf16[4,32,512]{2,1,0:T(8,128)(2,1)S(1)}, bf16[4,32,512]{2,1,0:T(8,128)(2,1)S(1)}, u32[]{:S(2)}, u32[]{:S(2)}) %collective-permute-start.6) | collective-permute-done | bytes 131104 | tf_op jit(solution)/shard_map/ppermute | solution.py:424
  32.1 1.7 %shard_map.111 = (f32[4,32,512]{2,1,0:T(8,128)S(1)}, f32[4,32,512]{2,1,0:T(8,128)S(1)}, bf16[2,4,32,512]{3,2,1,0:T(8,128)(2,1)S(1)}, bf16[2,128,128]{2,1,0:T(8,1...) custom-call(s32[1]{0:T(128)} %bitcast.me_ref, bf16[4,32,512]{2,1,0:T(8,128)(2,1)S(1)} %fusion.3.refs_0_, ...), custom_call_target="tpu_custom_call" | custom-call | flops 3500000000 | bytes 1000000 | tf_op jit(solution)/shard_map/pallas_call | solution.py:362
  33.9 0.1 collective-permute-done.7.refs_6_
  34.0 0.1 shard_map.112
  34.2 4.1 %collective-permute-start.13 = (bf16[32,768]{1,0:T(8,128)(2,1)S(1)}, bf16[32,768]{1,0:T(8,128)(2,1)S(1)}, u32[]{:S(2)}, u32[]{:S(2)}) collective-permute-start(bf16[32,768]{1,0:T(8,128)(2,1)S(1)} %get-tuple-element.80.refs_1_), channel_id=1, source_target_pairs={{0,8},{1,9},{2,10},{3,11},{4,12},{5,13},{6,14},{7,15},{8,0},{9,1},... | collective-permute-start | bytes 147464 | tf_op jit(solution)/shard_map/ppermute | solution.py:457
  38.3 1.8 %collective-permute-start.15 = (bf16[4,32,512]{2,1,0:T(8,128)(2,1)S(1)}, bf16[4,32,512]{2,1,0:T(8,128)(2,1)S(1)}, u32[]{:S(2)}, u32[]{:S(2)}) collective-permute-start(bf16[4,32,512]{2,1,0:T(8,128)(2,1)S(1)} %fusion.1.refs_3_), channel_id=1, source_target_pairs={{0,2},{1,3},{2,0},{3,1},{4,6},{5,7},{6,4},{7,5},{8,10},{9,11},{10,... | collective-permute-start | bytes 393224 | tf_op jit(solution)/shard_map/ppermute | solution.py:424
  40.1 0.4 collective-permute-start.16
  40.5 1.0 %shard_map.114 = (f32[2,128,512]{2,1,0:T(8,128)S(1)}, bf16[2,3,16,512]{3,2,1,0:T(8,128)(2,1)S(1)}, bf16[2,3,16,512]{3,2,1,0:T(8,128)(2,1)S(1)}, bf16[2,1,16,512]...) custom-call(bf16[32,768]{1,0:T(8,128)(2,1)S(1)} %get-tuple-element.79.refs_0_, ...), custom_call_target="tpu_custom_call" | custom-call | flops 2000000000 | bytes 1000000 | tf_op jit(solution)/shard_map/pallas_call | solution.py:362
  41.6 0.5 collective-permute-start.11
  42.1 1.2 %collective-permute-start.14 = (bf16[32,768]{1,0:T(8,128)(2,1)S(1)}, bf16[32,768]{1,0:T(8,128)(2,1)S(1)}, u32[]{:S(2)}, u32[]{:S(2)}) collective-permute-start(bf16[32,768]{1,0:T(8,128)(2,1)S(1)} %get-tuple-element.81.refs_2_), channel_id=1, source_target_pairs={{0,12},{1,13},{2,14},{3,15},{4,0},{5,1},{6,2},{7,3},{8,4},{9,5},{1... | collective-permute-start | bytes 147464 | tf_op jit(solution)/shard_map/ppermute | solution.py:457
  43.3 3.1 %collective-permute-done.14.refs_3_.refs_2_ = bf16[32,768]{1,0:T(8,128)(2,1)S(1)} collective-permute-done((bf16[32,768]{1,0:T(8,128)(2,1)S(1)}, bf16[32,768]{1,0:T(8,128)(2,1)S(1)}, u32[]{:S(2)}, u32[]{:S(2)}) %collective-permute-start.14) | collective-permute-done | bytes 49184 | tf_op jit(solution)/shard_map/ppermute | solution.py:457
  46.4 0.8 %collective-permute-done.16.refs_10_ = bf16[4,32,512]{2,1,0:T(8,128)(2,1)S(1)} collective-permute-done((bf16[4,32,512]{2,1,0:T(8,128)(2,1)S(1)}, bf16[4,32,512]{2,1,0:T(8,128)(2,1)S(1)}, u32[]{:S(2)}, u32[]{:S(2)}) %collective-permute-start.16) | collective-permute-done | bytes 131104 | tf_op jit(solution)/shard_map/ppermute | solution.py:424
  47.2 0.1 shard_map.115
  47.3 1.6 %collective-permute-done.11.left_ref.right_ref = bf16[2,3,16,512]{3,2,1,0:T(8,128)(2,1)S(1)} collective-permute-done((bf16[2,3,16,512]{3,2,1,0:T(8,128)(2,1)S(1)}, bf16[2,3,16,512]{3,2,1,0:T(8,128)(2,1)S(1)}, u32[]{:S(2)}, u32[]{:S(2)}) %collective-permute-start.11) | collective-permute-done | bytes 98336 | tf_op jit(solution)/shard_map/ppermute | solution.py:28
  48.9 0.8 %collective-permute-start.17 = (bf16[2,3,16,512]{3,2,1,0:T(8,128)(2,1)S(1)}, bf16[2,3,16,512]{3,2,1,0:T(8,128)(2,1)S(1)}, u32[]{:S(2)}, u32[]{:S(2)}) collective-permute-start(bf16[2,3,16,512]{3,2,1,0:T(8,128)(2,1)S(1)} %get-tuple-element.108), channel_id=1, source_target_pairs={{0,12},{1,13},{2,14},{3,15},{4,0},{5,1},{6,2},{7,3},{8,4},{9,5},{1... | collective-permute-start | bytes 294920 | tf_op jit(solution)/shard_map/ppermute | solution.py:28
  49.7 1.3 %collective-permute-start.18 = (bf16[2,3,16,512]{3,2,1,0:T(8,128)(2,1)S(1)}, bf16[2,3,16,512]{3,2,1,0:T(8,128)(2,1)S(1)}, u32[]{:S(2)}, u32[]{:S(2)}) collective-permute-start(bf16[2,3,16,512]{3,2,1,0:T(8,128)(2,1)S(1)} %get-tuple-element.109), channel_id=1, source_target_pairs={{0,4},{1,5},{2,6},{3,7},{4,8},{5,9},{6,10},{7,11},{8,12},{9,13},{1... | collective-permute-start | bytes 294920 | tf_op jit(solution)/shard_map/ppermute | solution.py:28
  51.0 3.0 %collective-permute-start.20 = (bf16[32,1280]{1,0:T(8,128)(2,1)S(1)}, bf16[32,1280]{1,0:T(8,128)(2,1)S(1)}, u32[]{:S(2)}, u32[]{:S(2)}) collective-permute-start(bf16[32,1280]{1,0:T(8,128)(2,1)S(1)} %get-tuple-element.112), channel_id=1, source_target_pairs={{0,8},{1,9},{2,10},{3,11},{4,12},{5,13},{6,14},{7,15},{8,0},{9,1},... | collective-permute-start | bytes 245768 | tf_op jit(solution)/shard_map/ppermute | solution.py:457
  54.1 0.8 %collective-permute-start.21 = (bf16[32,1280]{1,0:T(8,128)(2,1)S(1)}, bf16[32,1280]{1,0:T(8,128)(2,1)S(1)}, u32[]{:S(2)}, u32[]{:S(2)}) collective-permute-start(bf16[32,1280]{1,0:T(8,128)(2,1)S(1)} %get-tuple-element.113), channel_id=1, source_target_pairs={{0,12},{1,13},{2,14},{3,15},{4,0},{5,1},{6,2},{7,3},{8,4},{9,5},{1... | collective-permute-start | bytes 245768 | tf_op jit(solution)/shard_map/ppermute | solution.py:457
  54.8 2.5 %collective-permute-done.18.plus_ref = bf16[2,3,16,512]{3,2,1,0:T(8,128)(2,1)S(1)} collective-permute-done((bf16[2,3,16,512]{3,2,1,0:T(8,128)(2,1)S(1)}, bf16[2,3,16,512]{3,2,1,0:T(8,128)(2,1)S(1)}, u32[]{:S(2)}, u32[]{:S(2)}) %collective-permute-start.18) | collective-permute-done | bytes 98336 | tf_op jit(solution)/shard_map/ppermute | solution.py:28
  57.3 1.0 %shard_map.117.after_ref = bf16[2,128,512]{2,1,0:T(8,128)(2,1)} custom-call(s32[1,8,16]{2,1,0:T(8,128)S(1)} %copy-done.14, f32[2,128,512]{2,1,0:T(8,128)S(1)} %get-tuple-element.100.refs_0_.node_ref, bf16[2,3,16,512]{3,2,1,0:T(8,128)(2,1)S(1)} %collective-permute-done.10.right_ref.left_ref, ...), custom_call_target="tpu_custom_call" | custom-call | flops 1000000000 | bytes 1000000 | tf_op jit(solution)/shard_map/pallas_call | solution.py:362
  58.3 0.8 %collective-permute-done.19.refs_3_ = bf16[32,1280]{1,0:T(8,128)(2,1)S(1)} collective-permute-done((bf16[32,1280]{1,0:T(8,128)(2,1)S(1)}, bf16[32,1280]{1,0:T(8,128)(2,1)S(1)}, u32[]{:S(2)}, u32[]{:S(2)}) %collective-permute-start.19) | collective-permute-done | bytes 81952 | tf_op jit(solution)/shard_map/ppermute | solution.py:457
  59.0 2.1 %collective-permute-done.20.refs_4_ = bf16[32,1280]{1,0:T(8,128)(2,1)S(1)} collective-permute-done((bf16[32,1280]{1,0:T(8,128)(2,1)S(1)}, bf16[32,1280]{1,0:T(8,128)(2,1)S(1)}, u32[]{:S(2)}, u32[]{:S(2)}) %collective-permute-start.20) | collective-permute-done | bytes 81952 | tf_op jit(solution)/shard_map/ppermute | solution.py:457
  61.1 0.9 %copy-done = bf16[2,128,512]{2,1,0:T(8,128)(2,1)S(1)} copy-done((bf16[2,128,512]{2,1,0:T(8,128)(2,1)S(1)}, bf16[2,128,512]{2,1,0:T(8,128)(2,1)}, u32[]{:S(2)}) %copy-start) | copy-done | bytes 262168
  62.1 0.8 %shard_map.118 = f32[32,2048]{1,0:T(8,128)} custom-call(bf16[2,128,512]{2,1,0:T(8,128)(2,1)S(1)} %copy-done, f32[32,768]{1,0:T(8,128)S(1)} %get-tuple-element.110.own_a, f32[32,1280]{1,0:T(8,128)S(1)} %get-tuple-element.105.after_ref.own_b, bf16[32,768]{1,0:T(8,128)(2,1)S(1)} %collective-permute-done.12.refs_1_.refs_0_, ...), custom_call_target="tpu_custom_call" | custom-call | flops 100000000 | bytes 1000000 | tf_op jit(solution)/shard_map/pallas_call | solution.py:362
  (47 shorter events, 0.6 us)
Async XLA Ops:
  0.6 1.0 %copy-start.8 = (bf16[2,128,512]{2,1,0:T(8,128)(2,1)S(1)}, bf16[2,128,512]{2,1,0:T(8,128)(2,1)}, u32[]{:S(2)}) copy-start(bf16[2,128,512]{2,1,0:T(8,128)(2,1)} %x_ref.3) | copy-start | bytes 786436
  1.6 0.7 %copy-start.13 = (s32[1,8,16]{2,1,0:T(8,128)S(1)}, s32[1,8,16]{2,1,0:T(8,128)}, u32[]{:S(2)}) copy-start(s32[1,8,16]{2,1,0:T(8,128)} %send_ref.3) | copy-start | bytes 1540
  2.3 5.5 %copy-start.9 = (bf16[2,128,512]{2,1,0:T(8,128)(2,1)S(1)}, bf16[2,128,512]{2,1,0:T(8,128)(2,1)}, u32[]{:S(2)}) copy-start(bf16[2,128,512]{2,1,0:T(8,128)(2,1)} %x_ref.3) | copy-start | bytes 786436
  2.6 11.1 %collective-permute-start = (bf16[2,3,16,512]{3,2,1,0:T(8,128)(2,1)S(1)}, bf16[2,3,16,512]{3,2,1,0:T(8,128)(2,1)S(1)}, u32[]{:S(2)}, u32[]{:S(2)}) collective-permute-start(bf16[2,3,16,512]{3,2,1,0:T(8,128)(2,1)S(1)} %get-tuple-element.60), channel_id=1, source_target_pairs={{0,4},{1,5},{2,6},{3,7},{4,8},{5,9},{6,10},{7,11},{8,12},{9,13},{1... | collective-permute-start | bytes 294920 | tf_op jit(solution)/shard_map/ppermute | solution.py:28
  5.7 8.0 %collective-permute-start.1 = (bf16[2,3,16,512]{3,2,1,0:T(8,128)(2,1)S(1)}, bf16[2,3,16,512]{3,2,1,0:T(8,128)(2,1)S(1)}, u32[]{:S(2)}, u32[]{:S(2)}) collective-permute-start(bf16[2,3,16,512]{3,2,1,0:T(8,128)(2,1)S(1)} %get-tuple-element.61), channel_id=1, source_target_pairs={{0,12},{1,13},{2,14},{3,15},{4,0},{5,1},{6,2},{7,3},{8,4},{9,5},{1... | collective-permute-start | bytes 294920 | tf_op jit(solution)/shard_map/ppermute | solution.py:28
  7.8 1.0 %copy-start.1 = (bf16[512,512]{1,0:T(8,128)(2,1)S(1)}, bf16[512,512]{1,0:T(8,128)(2,1)}, u32[]{:S(2)}) copy-start(bf16[512,512]{1,0:T(8,128)(2,1)} %wo_ref.1) | copy-start | bytes 1572868
  8.8 1.0 %copy-start.2 = (bf16[512,512]{1,0:T(8,128)(2,1)S(1)}, bf16[512,512]{1,0:T(8,128)(2,1)}, u32[]{:S(2)}) copy-start(bf16[512,512]{1,0:T(8,128)(2,1)} %refs_17_.1) | copy-start | bytes 1572868
  9.9 1.0 %copy-start.4 = (bf16[512,512]{1,0:T(8,128)(2,1)S(1)}, bf16[512,512]{1,0:T(8,128)(2,1)}, u32[]{:S(2)}) copy-start(bf16[512,512]{1,0:T(8,128)(2,1)} %refs_18_.1) | copy-start | bytes 1572868
  10.9 1.0 %copy-start.6 = (bf16[512,512]{1,0:T(8,128)(2,1)S(1)}, bf16[512,512]{1,0:T(8,128)(2,1)}, u32[]{:S(2)}) copy-start(bf16[512,512]{1,0:T(8,128)(2,1)} %refs_19_.1) | copy-start | bytes 1572868
  12.0 0.9 %copy-start.10 = (bf16[2,128,512]{2,1,0:T(8,128)(2,1)S(1)}, bf16[2,128,512]{2,1,0:T(8,128)(2,1)}, u32[]{:S(2)}) copy-start(bf16[2,128,512]{2,1,0:T(8,128)(2,1)} %refs_5_.1) | copy-start | bytes 786436
  13.7 4.5 %copy-start.12 = (s32[128,256]{1,0:T(8,128)S(1)}, s32[128,256]{1,0:T(8,128)}, u32[]{:S(2)}) copy-start(s32[128,256]{1,0:T(8,128)} %neigh_ref.1) | copy-start | bytes 393220
  13.8 6.9 %collective-permute-start.2 = (bf16[2,3,16,512]{3,2,1,0:T(8,128)(2,1)S(1)}, bf16[2,3,16,512]{3,2,1,0:T(8,128)(2,1)S(1)}, u32[]{:S(2)}, u32[]{:S(2)}) collective-permute-start(bf16[2,3,16,512]{3,2,1,0:T(8,128)(2,1)S(1)} %get-tuple-element.64.after_ref), channel_id=1, source_target_pairs={{0,1},{1,2},{2,3},{3,4},{4,5},{5,6},{6,7},{7,8},{8,9},{9,10},{10,1... | collective-permute-start | bytes 294920 | tf_op jit(solution)/shard_map/ppermute | solution.py:28
  13.8 4.4 %copy-start.15 = (s32[128]{0:T(128)S(1)}, s32[128]{0:T(128)}, u32[]{:S(2)}) copy-start(s32[128]{0:T(128)} %param.16) | copy-start | bytes 1540
  13.9 6.8 %collective-permute-start.3 = (bf16[2,3,16,512]{3,2,1,0:T(8,128)(2,1)S(1)}, bf16[2,3,16,512]{3,2,1,0:T(8,128)(2,1)S(1)}, u32[]{:S(2)}, u32[]{:S(2)}) collective-permute-start(bf16[2,3,16,512]{3,2,1,0:T(8,128)(2,1)S(1)} %get-tuple-element.65), channel_id=1, source_target_pairs={{0,15},{1,0},{2,1},{3,2},{4,3},{5,4},{6,5},{7,6},{8,7},{9,8},{10,9... | collective-permute-start | bytes 294920 | tf_op jit(solution)/shard_map/ppermute | solution.py:28
  18.3 2.4 %copy-start.5 = (bf16[512,512]{1,0:T(8,128)(2,1)S(1)}, bf16[512,512]{1,0:T(8,128)(2,1)}, u32[]{:S(2)}) copy-start(bf16[512,512]{1,0:T(8,128)(2,1)} %refs_18_.1) | copy-start | bytes 1572868
  18.3 2.4 %copy-start.7 = (bf16[512,512]{1,0:T(8,128)(2,1)S(1)}, bf16[512,512]{1,0:T(8,128)(2,1)}, u32[]{:S(2)}) copy-start(bf16[512,512]{1,0:T(8,128)(2,1)} %refs_19_.1) | copy-start | bytes 1572868
  20.7 1.0 %copy-start.11 = (bf16[2,128,512]{2,1,0:T(8,128)(2,1)S(1)}, bf16[2,128,512]{2,1,0:T(8,128)(2,1)}, u32[]{:S(2)}) copy-start(bf16[2,128,512]{2,1,0:T(8,128)(2,1)} %refs_5_.1) | copy-start | bytes 786436
  23.3 2.3 %collective-permute-start.5 = (bf16[2,4,32,512]{3,2,1,0:T(8,128)(2,1)S(1)}, bf16[2,4,32,512]{3,2,1,0:T(8,128)(2,1)S(1)}, u32[]{:S(2)}, u32[]{:S(2)}) collective-permute-start(bf16[2,4,32,512]{3,2,1,0:T(8,128)(2,1)S(1)} %get-tuple-element.73), channel_id=1, source_target_pairs={{0,1},{1,0},{2,3},{3,2},{4,5},{5,4},{6,7},{7,6},{8,9},{9,8},{10,11... | collective-permute-start | bytes 786440 | tf_op jit(solution)/shard_map/ppermute | solution.py:453
  25.1 1.7 %collective-permute-start.4 = (bf16[2,4,32,512]{3,2,1,0:T(8,128)(2,1)S(1)}, bf16[2,4,32,512]{3,2,1,0:T(8,128)(2,1)S(1)}, u32[]{:S(2)}, u32[]{:S(2)}) collective-permute-start(bf16[2,4,32,512]{3,2,1,0:T(8,128)(2,1)S(1)} %get-tuple-element.70), channel_id=1, source_target_pairs={{0,1},{1,0},{2,3},{3,2},{4,5},{5,4},{6,7},{7,6},{8,9},{9,8},{10,11... | collective-permute-start | bytes 786440 | tf_op jit(solution)/shard_map/ppermute | solution.py:453
  25.7 6.4 %collective-permute-start.6 = (bf16[4,32,512]{2,1,0:T(8,128)(2,1)S(1)}, bf16[4,32,512]{2,1,0:T(8,128)(2,1)S(1)}, u32[]{:S(2)}, u32[]{:S(2)}) collective-permute-start(bf16[4,32,512]{2,1,0:T(8,128)(2,1)S(1)} %fusion.2.refs_0_), channel_id=1, source_target_pairs={{0,2},{1,3},{2,0},{3,1},{4,6},{5,7},{6,4},{7,5},{8,10},{9,11},{10,... | collective-permute-start | bytes 393224 | tf_op jit(solution)/shard_map/ppermute | solution.py:424
  26.9 7.2 %collective-permute-start.7 = (bf16[4,32,512]{2,1,0:T(8,128)(2,1)S(1)}, bf16[4,32,512]{2,1,0:T(8,128)(2,1)S(1)}, u32[]{:S(2)}, u32[]{:S(2)}) collective-permute-start(bf16[4,32,512]{2,1,0:T(8,128)(2,1)S(1)} %fusion.3.refs_0_), channel_id=1, source_target_pairs={{0,2},{1,3},{2,0},{3,1},{4,6},{5,7},{6,4},{7,5},{8,10},{9,11},{10,... | collective-permute-start | bytes 393224 | tf_op jit(solution)/shard_map/ppermute | solution.py:424
  29.6 8.7 %collective-permute-start.8 = (bf16[2,4,32,512]{3,2,1,0:T(8,128)(2,1)S(1)}, bf16[2,4,32,512]{3,2,1,0:T(8,128)(2,1)S(1)}, u32[]{:S(2)}, u32[]{:S(2)}) collective-permute-start(bf16[2,4,32,512]{3,2,1,0:T(8,128)(2,1)S(1)} %get-tuple-element.85), channel_id=1, source_target_pairs={{0,1},{1,0},{2,3},{3,2},{4,5},{5,4},{6,7},{7,6},{8,9},{9,8},{10,11... | collective-permute-start | bytes 786440 | tf_op jit(solution)/shard_map/ppermute | solution.py:453
  33.8 6.3 %collective-permute-start.9 = (bf16[2,4,32,512]{3,2,1,0:T(8,128)(2,1)S(1)}, bf16[2,4,32,512]{3,2,1,0:T(8,128)(2,1)S(1)}, u32[]{:S(2)}, u32[]{:S(2)}) collective-permute-start(bf16[2,4,32,512]{3,2,1,0:T(8,128)(2,1)S(1)} %get-tuple-element.87), channel_id=1, source_target_pairs={{0,1},{1,0},{2,3},{3,2},{4,5},{5,4},{6,7},{7,6},{8,9},{9,8},{10,11... | collective-permute-start | bytes 786440 | tf_op jit(solution)/shard_map/ppermute | solution.py:453
  34.1 7.5 %collective-permute-start.12 = (bf16[32,768]{1,0:T(8,128)(2,1)S(1)}, bf16[32,768]{1,0:T(8,128)(2,1)S(1)}, u32[]{:S(2)}, u32[]{:S(2)}) collective-permute-start(bf16[32,768]{1,0:T(8,128)(2,1)S(1)} %get-tuple-element.79.refs_0_), channel_id=1, source_target_pairs={{0,4},{1,5},{2,6},{3,7},{4,8},{5,9},{6,10},{7,11},{8,12},{9,13},{1... | collective-permute-start | bytes 147464 | tf_op jit(solution)/shard_map/ppermute | solution.py:457
  34.2 7.9 %collective-permute-start.13 = (bf16[32,768]{1,0:T(8,128)(2,1)S(1)}, bf16[32,768]{1,0:T(8,128)(2,1)S(1)}, u32[]{:S(2)}, u32[]{:S(2)}) collective-permute-start(bf16[32,768]{1,0:T(8,128)(2,1)S(1)} %get-tuple-element.80.refs_1_), channel_id=1, source_target_pairs={{0,8},{1,9},{2,10},{3,11},{4,12},{5,13},{6,14},{7,15},{8,0},{9,1},... | collective-permute-start | bytes 147464 | tf_op jit(solution)/shard_map/ppermute | solution.py:457
  38.2 2.2 %copy-start.3 = (bf16[512,512]{1,0:T(8,128)(2,1)S(1)}, bf16[512,512]{1,0:T(8,128)(2,1)}, u32[]{:S(2)}) copy-start(bf16[512,512]{1,0:T(8,128)(2,1)} %refs_17_.1) | copy-start | bytes 1572868
  38.3 8.1 %collective-permute-start.15 = (bf16[4,32,512]{2,1,0:T(8,128)(2,1)S(1)}, bf16[4,32,512]{2,1,0:T(8,128)(2,1)S(1)}, u32[]{:S(2)}, u32[]{:S(2)}) collective-permute-start(bf16[4,32,512]{2,1,0:T(8,128)(2,1)S(1)} %fusion.1.refs_3_), channel_id=1, source_target_pairs={{0,2},{1,3},{2,0},{3,1},{4,6},{5,7},{6,4},{7,5},{8,10},{9,11},{10,... | collective-permute-start | bytes 393224 | tf_op jit(solution)/shard_map/ppermute | solution.py:424
  40.1 7.1 %collective-permute-start.16 = (bf16[4,32,512]{2,1,0:T(8,128)(2,1)S(1)}, bf16[4,32,512]{2,1,0:T(8,128)(2,1)S(1)}, u32[]{:S(2)}, u32[]{:S(2)}) collective-permute-start(bf16[4,32,512]{2,1,0:T(8,128)(2,1)S(1)} %fusion.refs_4_), channel_id=1, source_target_pairs={{0,2},{1,3},{2,0},{3,1},{4,6},{5,7},{6,4},{7,5},{8,10},{9,11},{10,... | collective-permute-start | bytes 393224 | tf_op jit(solution)/shard_map/ppermute | solution.py:424
  41.5 5.8 %collective-permute-start.10 = (bf16[2,3,16,512]{3,2,1,0:T(8,128)(2,1)S(1)}, bf16[2,3,16,512]{3,2,1,0:T(8,128)(2,1)S(1)}, u32[]{:S(2)}, u32[]{:S(2)}) collective-permute-start(bf16[2,3,16,512]{3,2,1,0:T(8,128)(2,1)S(1)} %get-tuple-element.101), channel_id=1, source_target_pairs={{0,15},{1,0},{2,1},{3,2},{4,3},{5,4},{6,5},{7,6},{8,7},{9,8},{10,9... | collective-permute-start | bytes 294920 | tf_op jit(solution)/shard_map/ppermute | solution.py:28
  41.6 7.3 %collective-permute-start.11 = (bf16[2,3,16,512]{3,2,1,0:T(8,128)(2,1)S(1)}, bf16[2,3,16,512]{3,2,1,0:T(8,128)(2,1)S(1)}, u32[]{:S(2)}, u32[]{:S(2)}) collective-permute-start(bf16[2,3,16,512]{3,2,1,0:T(8,128)(2,1)S(1)} %get-tuple-element.102), channel_id=1, source_target_pairs={{0,1},{1,2},{2,3},{3,4},{4,5},{5,6},{6,7},{7,8},{8,9},{9,10},{10,1... | collective-permute-start | bytes 294920 | tf_op jit(solution)/shard_map/ppermute | solution.py:28
  42.1 4.3 %collective-permute-start.14 = (bf16[32,768]{1,0:T(8,128)(2,1)S(1)}, bf16[32,768]{1,0:T(8,128)(2,1)S(1)}, u32[]{:S(2)}, u32[]{:S(2)}) collective-permute-start(bf16[32,768]{1,0:T(8,128)(2,1)S(1)} %get-tuple-element.81.refs_2_), channel_id=1, source_target_pairs={{0,12},{1,13},{2,14},{3,15},{4,0},{5,1},{6,2},{7,3},{8,4},{9,5},{1... | collective-permute-start | bytes 147464 | tf_op jit(solution)/shard_map/ppermute | solution.py:457
  48.9 8.4 %copy-start.14 = (s32[1,8,16]{2,1,0:T(8,128)S(1)}, s32[1,8,16]{2,1,0:T(8,128)}, u32[]{:S(2)}) copy-start(s32[1,8,16]{2,1,0:T(8,128)} %send_ref.3) | copy-start | bytes 1540
  48.9 5.9 %collective-permute-start.17 = (bf16[2,3,16,512]{3,2,1,0:T(8,128)(2,1)S(1)}, bf16[2,3,16,512]{3,2,1,0:T(8,128)(2,1)S(1)}, u32[]{:S(2)}, u32[]{:S(2)}) collective-permute-start(bf16[2,3,16,512]{3,2,1,0:T(8,128)(2,1)S(1)} %get-tuple-element.108), channel_id=1, source_target_pairs={{0,12},{1,13},{2,14},{3,15},{4,0},{5,1},{6,2},{7,3},{8,4},{9,5},{1... | collective-permute-start | bytes 294920 | tf_op jit(solution)/shard_map/ppermute | solution.py:28
  49.7 7.6 %collective-permute-start.18 = (bf16[2,3,16,512]{3,2,1,0:T(8,128)(2,1)S(1)}, bf16[2,3,16,512]{3,2,1,0:T(8,128)(2,1)S(1)}, u32[]{:S(2)}, u32[]{:S(2)}) collective-permute-start(bf16[2,3,16,512]{3,2,1,0:T(8,128)(2,1)S(1)} %get-tuple-element.109), channel_id=1, source_target_pairs={{0,4},{1,5},{2,6},{3,7},{4,8},{5,9},{6,10},{7,11},{8,12},{9,13},{1... | collective-permute-start | bytes 294920 | tf_op jit(solution)/shard_map/ppermute | solution.py:28
  51.0 8.1 %collective-permute-start.19 = (bf16[32,1280]{1,0:T(8,128)(2,1)S(1)}, bf16[32,1280]{1,0:T(8,128)(2,1)S(1)}, u32[]{:S(2)}, u32[]{:S(2)}) collective-permute-start(bf16[32,1280]{1,0:T(8,128)(2,1)S(1)} %get-tuple-element.111), channel_id=1, source_target_pairs={{0,4},{1,5},{2,6},{3,7},{4,8},{5,9},{6,10},{7,11},{8,12},{9,13},{1... | collective-permute-start | bytes 245768 | tf_op jit(solution)/shard_map/ppermute | solution.py:457
  51.0 10.1 %collective-permute-start.20 = (bf16[32,1280]{1,0:T(8,128)(2,1)S(1)}, bf16[32,1280]{1,0:T(8,128)(2,1)S(1)}, u32[]{:S(2)}, u32[]{:S(2)}) collective-permute-start(bf16[32,1280]{1,0:T(8,128)(2,1)S(1)} %get-tuple-element.112), channel_id=1, source_target_pairs={{0,8},{1,9},{2,10},{3,11},{4,12},{5,13},{6,14},{7,15},{8,0},{9,1},... | collective-permute-start | bytes 245768 | tf_op jit(solution)/shard_map/ppermute | solution.py:457
  54.1 7.0 %collective-permute-start.21 = (bf16[32,1280]{1,0:T(8,128)(2,1)S(1)}, bf16[32,1280]{1,0:T(8,128)(2,1)S(1)}, u32[]{:S(2)}, u32[]{:S(2)}) collective-permute-start(bf16[32,1280]{1,0:T(8,128)(2,1)S(1)} %get-tuple-element.113), channel_id=1, source_target_pairs={{0,12},{1,13},{2,14},{3,15},{4,0},{5,1},{6,2},{7,3},{8,4},{9,5},{1... | collective-permute-start | bytes 245768 | tf_op jit(solution)/shard_map/ppermute | solution.py:457
  61.1 1.0 %copy-start = (bf16[2,128,512]{2,1,0:T(8,128)(2,1)S(1)}, bf16[2,128,512]{2,1,0:T(8,128)(2,1)}, u32[]{:S(2)}) copy-start(bf16[2,128,512]{2,1,0:T(8,128)(2,1)} %shard_map.117.after_ref) | copy-start | bytes 786436

commit v3 on v2

v3 whole, which is shorter than its diff:
```python
import functools
import math

import jax
import jax.numpy as jnp
from jax import lax
from jax.experimental import pallas as pl
from jax.experimental.pallas import tpu as pltpu
from jax.sharding import PartitionSpec as P

HEADS = 16
score_cap = 5.0
MIB = 1024 * 1024
f32 = jnp.float32
bf16 = jnp.bfloat16


def nn(a, b):
    return lax.dot_general(a, b, (((1,), (0,)), ((), ())), preferred_element_type=f32)


def nt(a, b):
    return lax.dot_general(a, b, (((1,), (1,)), ((), ())), preferred_element_type=f32)


def shifted(shard, by):
    count = lax.axis_size("patch")
    return lax.ppermute(shard, "patch", [(i, (i + by) % count) for i in range(count)])


def sent_selector(send_rows, node_rows):
    adjacent, slots = send_rows.shape
    halo = adjacent * slots
    wide = jnp.concatenate([send_rows] * adjacent, axis=1)
    own = lax.broadcasted_iota(jnp.int32, (adjacent, halo), 1) // slots == lax.broadcasted_iota(
        jnp.int32, (adjacent, halo), 0
    )
    ids = jnp.sum(jnp.where(own, wide, 0), axis=0, keepdims=True)
    nodes = lax.broadcasted_iota(jnp.int32, (node_rows, halo), 0)
    return jnp.where(nodes == ids, 1.0, 0.0).astype(f32)


def gather_kernel(slots, send_hbm, x_hbm, plus_ref, minus_ref, right_ref, left_ref, x_ref, send_ref, sem):
    copies = [
        pltpu.make_async_copy(send_hbm, send_ref, sem.at[0]),
        pltpu.make_async_copy(x_hbm, x_ref, sem.at[1]),
    ]
    for copy in copies:
        copy.start()
    copies[0].wait()
    members, node_rows, _ = x_ref.shape
    pick = sent_selector(send_ref[0], node_rows).T.astype(bf16)
    copies[1].wait()
    for m in range(members):
        rows = nn(pick, x_ref[m]).astype(bf16)

        def part(k):
            return rows[k * slots : (k + 1) * slots]

        for i, k in enumerate((2, 6, 4)):
            plus_ref[m, i] = part(k)
        for i, k in enumerate((3, 5, 7)):
            minus_ref[m, i] = part(k)
        right_ref[m, 0] = part(0)
        left_ref[m, 0] = part(1)


def relay_kernel(after_ref, own_a, own_b, plus_ref, minus_ref, a_ref, b_ref):
    a_ref[:, 0:1] = own_a[...]
    a_ref[:, 1:2] = plus_ref[:, 1:2]
    a_ref[:, 2:3] = minus_ref[:, 1:2]
    b_ref[:, 0:1] = own_b[...]
    b_ref[:, 1:2] = plus_ref[:, 2:3]
    b_ref[:, 2:3] = minus_ref[:, 2:3]


Q, K, V, G, QT, KT, VT, GT = range(8)


def local_kernel(groups, after_ref, x_ref, *refs):
    sources, loc_refs, xt_ref = refs[:5], refs[5 : 5 + groups], refs[5 + groups]
    copied, sem = refs[6 + groups : 11 + groups], refs[-1]
    copies = [
        pltpu.make_async_copy(source, target, sem.at[i])
        for i, (source, target) in enumerate(zip(sources, copied))
    ]
    for copy in copies:
        copy.start()
    members, node_rows, width = x_ref.shape
    x = x_ref[...].reshape(members * node_rows, width)
    for m in range(members):
        xt_ref[m] = x_ref[m].T

    def put(rows, kind):
        for m in range(members):
            for g, ref in enumerate(loc_refs):
                block = rows[m * node_rows : (m + 1) * node_rows, g * 128 : (g + 1) * 128]
                ref[kind, m] = block
                ref[kind + 4, m] = block.T

    wq_ref, wk_ref, wv_ref, og_ref, wo_ref = copied
    for kind, ref in enumerate((wq_ref, wk_ref, wv_ref)):
        copies[kind].wait()
        put(nn(x, ref[...]).astype(bf16), kind)
    copies[3].wait()
    copies[4].wait()
    og = og_ref[...].reshape(members * node_rows, width)
    put(nt(og, wo_ref[...]).astype(bf16), G)


def mask_kernel(after_ref, neigh_ref, count_ref, mask_ref):
    neigh = neigh_ref[...].T
    slots, node_rows = neigh.shape
    table = mask_ref.shape[0]
    order = lax.broadcasted_iota(jnp.int32, neigh.shape, 0)
    tail = jnp.where(order >= count_ref[...], neigh, -1)[slots // 2 :]
    half = table // 2
    for part in range(2):
        columns = lax.broadcasted_iota(jnp.int32, (half, node_rows), 0) + part * half
        kept = jnp.ones((half, node_rows), f32)
        for j in range(slots // 2):
            kept = jnp.where(tail[j : j + 1] == columns, 0.0, kept)
        mask_ref[part * half : (part + 1) * half] = kept


def halo_kernel(plus_ref, minus_ref, right_ref, left_ref, xt_ref, wk_ref, wv_ref, *out_refs):
    halo_refs, xtf_ref = out_refs[:-1], out_refs[-1]
    members, _, node_rows = xt_ref.shape
    for m in range(members):
        pieces = [None] * 8
        for ref, order in (
            (right_ref, (0, 6, 5)),
            (left_ref, (1, 4, 7)),
            (plus_ref, (2,)),
            (minus_ref, (3,)),
        ):
            for i, k in enumerate(order):
                pieces[k] = ref[m, i]
        halo = jnp.concatenate(pieces, axis=0)
        xtf_ref[m, :, :node_rows] = xt_ref[m]
        xtf_ref[m, :, node_rows:] = halo.T
        for kind, w_ref in enumerate((wk_ref, wv_ref)):
            rows = nn(halo, w_ref[...]).astype(bf16)
            for g, ref in enumerate(halo_refs):
                block = rows[:, g * 128 : (g + 1) * 128]
                ref[kind, m] = block
                ref[kind + 2, m] = block.T


def attention_kernel(extra, here, me_ref, *refs):
    refs = refs[extra:]
    locs, halos, refs = refs[:here], refs[here : 2 * here], refs[2 * here :]
    mask_ref, xtf, og_ref = refs[:3]
    outs, grads, scratch = refs[3:7], refs[7 : 7 + 3 * here], refs[7 + 3 * here :]
    for i in range(here):
        attend(
            me_ref, locs[i], halos[i], mask_ref, xtf, og_ref, outs, 512 * i,
            grads[3 * i : 3 * i + 3], scratch,
        )


def attend(me_ref, loc, halo, mask_ref, xtf, og_ref, out_refs, at, grad_refs, scratch):
    own_ref, other_ref, send_other, send_own = out_refs
    dq_ref, dk_ref, dv_ref = grad_refs
    score, grad, slope, dw, wos = scratch
    _, members, node_rows, _ = loc.shape
    table = mask_ref.shape[0]
    width = og_ref.shape[2]
    head = width // HEADS
    per = 128 // head
    scale = 1.0 / math.sqrt(head)

    row_head = lax.broadcasted_iota(jnp.int32, (128, node_rows), 0) // head
    lane_head = lax.broadcasted_iota(jnp.int32, (node_rows, 128), 1) // head

    def spread_t(block):
        zero = jnp.zeros_like(block)
        return jnp.concatenate([jnp.where(row_head == h, block, zero) for h in range(per)], axis=1)

    def spread_n(block):
        zero = jnp.zeros_like(block)
        return jnp.concatenate([jnp.where(lane_head == h, block, zero) for h in range(per)], axis=0)

    strip = 64
    for m in range(members):
        kg = jnp.concatenate([loc[K, m], halo[0, m]], axis=0)
        vg = jnp.concatenate([loc[V, m], halo[1, m]], axis=0)
        score[m] = nn(kg, spread_t(loc[QT, m]))
        grad[m] = nn(vg, spread_t(loc[GT, m]))

    wo_total = None
    kv_total = None
    q_total = None
    for m in range(members):
        probs = []
        for h in range(per):
            lanes = slice(h * node_rows, (h + 1) * node_rows)
            den = jnp.zeros((8, node_rows), f32)
            inner = jnp.zeros((8, node_rows), f32)
            for c in range(0, table, strip):
                box = (m, slice(c, c + strip), lanes)
                t = jnp.tanh(score[box] * (scale / score_cap))
                e = jnp.exp2(t * (score_cap / math.log(2.0))) * mask_ref[c : c + strip]
                den = den + jnp.sum(e.reshape(strip // 8, 8, node_rows), axis=0)
                inner = inner + jnp.sum((e * grad[box]).reshape(strip // 8, 8, node_rows), axis=0)
                score[box] = e
                slope[box] = e * (scale - scale * (t * t))
            r = 1.0 / jnp.sum(den, axis=0, keepdims=True)
            inner = jnp.sum(inner, axis=0, keepdims=True) * r
            column = []
            scores = []
            for c in range(0, table, strip):
                box = (m, slice(c, c + strip), lanes)
                column.append((score[box] * r).astype(bf16))
                scores.append(((slope[box] * r) * (grad[box] - inner)).astype(bf16))
            probs.append((jnp.concatenate(column, axis=0), jnp.concatenate(scores, axis=0)))
        pb = jnp.concatenate([p for p, _ in probs], axis=1)
        ds = jnp.concatenate([s for _, s in probs], axis=1)
        ktg = jnp.concatenate([loc[KT, m], halo[2, m]], axis=1)
        vtg = jnp.concatenate([loc[VT, m], halo[3, m]], axis=1)
        att, dqt = [], []
        for h in range(0, per, 2):
            lanes = slice(h * node_rows, (h + 2) * node_rows)
            rows = slice(h * head, (h + 2) * head)
            a = nn(vtg[rows], pb[:, lanes])
            b = nn(ktg[rows], ds[:, lanes])
            for j in range(2):
                inside = (slice(j * head, (j + 1) * head), slice(j * node_rows, (j + 1) * node_rows))
                att.append(a[inside].astype(bf16))
                dqt.append(b[inside].astype(bf16))
        att = jnp.concatenate(att, axis=0)
        dq = jnp.concatenate(dqt, axis=0).T
        dk = nn(ds, spread_n(loc[Q, m])).astype(bf16)
        dv = nn(pb, spread_n(loc[G, m])).astype(bf16)
        dq_ref[m], dk_ref[m], dv_ref[m] = dq, dk, dv
        wo_term = nn(att, og_ref[m])
        kv_term = nn(xtf[m], jnp.concatenate([dk, dv], axis=1))
        q_term = nn(xtf[m, :, :node_rows], dq)
        wo_total = wo_term if m == 0 else wo_total + wo_term
        kv_total = kv_term if m == 0 else kv_total + kv_term
        q_total = q_term if m == 0 else q_total + q_term

    planes, _, _, rows, _ = dw.shape
    inner_planes = wos.shape[0]
    dw[:, :, :, :, :128] = q_total.reshape(planes, 2, 2, rows, 128)
    dw[:, :, :, :, 128:] = kv_total.reshape(planes, 2, 2, rows, 256)
    wos[...] = wo_total.reshape(inner_planes, 2, 2, rows, width)
    me = me_ref[0]
    c, y, z = me % 2, (me // 2) % 2, me // 4
    qkv = slice(at, at + 384)
    for k in range(planes):
        zk = (z + k) % planes
        own_ref[k, :, qkv] = dw[zk, y, c]
        other_ref[k, :, qkv] = dw[zk, 1 - y, c]
        send_other[k, :, qkv] = dw[zk, 1 - y, 1 - c].astype(bf16)
        send_own[k, :, qkv] = dw[zk, y, 1 - c].astype(bf16)
    last = slice(at + 384, at + 512)
    for i in range(inner_planes):
        for n in range(width // 128):
            k = n * inner_planes + i
            lanes = slice(n * 128, (n + 1) * 128)
            own_ref[k, :, last] = wos[i, y, c, :, lanes]
            other_ref[k, :, last] = wos[i, 1 - y, c, :, lanes]
            send_other[k, :, last] = wos[i, 1 - y, 1 - c, :, lanes].astype(bf16)
            send_own[k, :, last] = wos[i, y, 1 - c, :, lanes].astype(bf16)


def node_kernel(groups, skip, *refs):
    refs = refs[skip:]
    dqs, dks, dvs = refs[:groups], refs[groups : 2 * groups], refs[2 * groups : 3 * groups]
    wq_ref, wk_ref, wv_ref, node_ref, left_ref, right_ref, minus_ref, plus_ref = refs[3 * groups :]
    members, node_rows, _ = dqs[0].shape
    slots = left_ref.shape[2]

    def whole(parts, m):
        return jnp.concatenate([part[m] for part in parts], axis=1)

    for m in range(members):
        spread = nt(whole(dks, m), wk_ref[...]) + nt(whole(dvs, m), wv_ref[...])
        node_ref[m] = spread[:node_rows] + nt(whole(dqs, m), wq_ref[...])
        halo = spread[node_rows:].astype(bf16)
        for ref, order in (
            (left_ref, (0, 6, 5)),
            (right_ref, (1, 4, 7)),
            (minus_ref, (2,)),
            (plus_ref, (3,)),
        ):
            for i, k in enumerate(order):
                ref[m, i] = halo[k * slots : (k + 1) * slots]


def sums(owns, core_in, y_in, k):
    total = jnp.concatenate(
        [own[k] + core[k].astype(f32) for own, core in zip(owns, core_in)], axis=1
    ) + y_in[k].astype(f32)
    return [total[:, at : at + 512] for at in range(0, total.shape[1], 512)]


def gather_projection(parts, k, planes, projection_ref, start):
    inner_planes = planes * 128 // projection_ref.shape[2]
    quarter, inner = divmod(k, inner_planes)
    for i, part in enumerate(parts):
        plane = start + i * inner_planes + inner
        projection_ref[plane, :, quarter * 128 : (quarter + 1) * 128] = part[:, 384:]


def first_kernel(pieces, *refs):
    later, later_core, refs = refs[:pieces], refs[pieces : 2 * pieces], refs[2 * pieces :]
    own, core_in, y_in, next_ref, own_ref, projection_ref, *sent = refs
    for i, (ref, core) in enumerate(zip(later, later_core)):
        next_ref[:, :, i * 512 : (i + 1) * 512] = (ref[...] + core[...].astype(f32)).astype(bf16)
    planes = len(sent) + 1
    for k in range(planes):
        parts = sums([own], [core_in], y_in, k)
        gather_projection(parts, k, planes, projection_ref, 0)
        row = jnp.concatenate([part[:, :384] for part in parts], axis=1)
        if k:
            sent[k - 1][...] = row.astype(bf16)
        else:
            own_ref[...] = row


def second_kernel(planes, pieces, near, me_ref, *refs):
    refs = refs[planes:]
    first_ref, back_plus, back_minus, from_right, from_left, y_in = refs[:6]
    owns, core_in = refs[6 : 6 + pieces], refs[6 + pieces : 6 + 2 * pieces]
    own_ref, *sent = refs[6 + 2 * pieces : -1]
    projection_ref = refs[-1]
    done, rows, width = first_ref.shape
    members = back_plus.shape[0]
    projection_ref[:done] = first_ref[...]
    held = []
    for k in range(planes):
        parts = sums(owns, core_in, y_in, k)
        gather_projection(parts, k, planes, projection_ref, done)
        held.append(jnp.concatenate([part[:, :384] for part in parts], axis=1))
    z = me_ref[0] // 4
    for k in range(planes):
        row = jnp.concatenate([held[k], projection_ref[(z + k) % planes]], axis=1)
        if not k:
            own_ref[...] = row
            continue
        row = row.astype(bf16)
        blocks = row.shape[1] // 256
        for n in range(blocks):
            sent[k - 1][n] = row[:, n * 256 : (n + 1) * 256]
        if k not in near:
            continue
        side = near.index(k)
        relayed = 2 - side
        for m in range(members):
            trio = ((back_plus, back_minus)[side][m, 0], from_right[m, relayed], from_left[m, relayed])
            for i, part in enumerate(trio):
                flat = jnp.concatenate([part[:, :256], part[:, 256:]], axis=0)
                pieces = flat.shape[0] // rows
                at = blocks + (m * 3 + i) * pieces
                sent[k - 1][at : at + pieces] = flat.reshape(pieces, rows, 256)


def finish_kernel(blocks, send_ref, node_ref, left_ref, right_ref, plus_ref, minus_ref, out_ref):
    members, node_rows, _ = node_ref.shape
    slots = left_ref.shape[2]
    pick = sent_selector(send_ref[0], node_rows).astype(bf16)
    rows = plus_ref.shape[1]
    each = 2 * slots // rows

    def arrived(ref, m, i):
        at = blocks + (m * 3 + i) * each
        flat = ref[at : at + each].reshape(2 * slots, 256)
        return jnp.concatenate([flat[:slots], flat[slots:]], axis=1)

    for m in range(members):
        pieces = [None] * 8
        pieces[0] = left_ref[m, 0]
        pieces[1] = right_ref[m, 0]
        for i, k in enumerate((2, 6, 4)):
            pieces[k] = arrived(minus_ref, m, i)
        for i, k in enumerate((3, 5, 7)):
            pieces[k] = arrived(plus_ref, m, i)
        arriving = jnp.concatenate(pieces, axis=0)
        out_ref[m] = (node_ref[m] + nn(pick, arriving)).astype(bf16)


def weight_kernel(planes, after_ref, own_a, own_b, *refs):
    z_a, z_b, out_ref = refs[: planes - 1], refs[planes - 1 : -1], refs[-1]
    a, b = own_a[...], own_b[...]
    blocks = b.shape[1] // 256
    for ref in z_a:
        a = a + ref[...].astype(f32)
    for ref in z_b:
        b = b + jnp.concatenate([ref[n].astype(f32) for n in range(blocks)], axis=1)
    half = a.shape[1] // 384
    width = 256 * half
    for i, part in enumerate((a, b)):
        for j in range(half):
            for n in range(3):
                at = n * width + (i * half + j) * 128
                out_ref[:, at : at + 128] = part[:, j * 384 + n * 128 : j * 384 + (n + 1) * 128]
    out_ref[:, 3 * width :] = b[:, 384 * half :]


def call(kernel, outs, operands, specs=None, scratch=(), flops=10**6, limit=12):
    specs = list(specs or ())
    specs += [pltpu.VMEM] * (len(operands) - len(specs))
    operands = [
        pltpu.with_memory_space_constraint(o, s) if s is pltpu.HBM else o
        for o, s in zip(operands, specs)
    ]
    return pl.pallas_call(
        kernel,
        out_shape=[jax.ShapeDtypeStruct(*o) for o in outs],
        in_specs=[pl.BlockSpec(memory_space=s) for s in specs],
        scratch_shapes=list(scratch),
        compiler_params=pltpu.CompilerParams(vmem_limit_bytes=limit * MIB),
        cost_estimate=pl.CostEstimate(flops=flops, bytes_accessed=10**4, transcendentals=0),
    )(*operands)


def body(
    node_features, out_grad, w_query, w_key, w_value, w_out, neighbours, neighbour_count, send_rows
):
    members, node_rows, width = node_features.shape
    count = lax.axis_size("patch")
    row_width = min(8, count // 4)
    _, adjacent, slots = send_rows.shape
    table = node_rows + adjacent * slots
    groups = width // 128
    me = lax.axis_index("patch")
    three = ((members, 3, slots, width), bf16)
    one = ((members, 1, slots, width), bf16)

    to_plus, to_minus, own_right, own_left, x = call(
        functools.partial(gather_kernel, slots),
        [three, three, one, one, (node_features.shape, bf16)],
        (send_rows, node_features),
        specs=[pltpu.HBM] * 2,
        scratch=[pltpu.VMEM(send_rows.shape, jnp.int32), pltpu.SemaphoreType.DMA((2,))],
    )
    plus = shifted(to_plus, row_width)
    minus = shifted(to_minus, -row_width)
    square = ((width, width), bf16)
    *loc, xt, wq, wk, wv, og = call(
        functools.partial(local_kernel, groups),
        [((8, members, node_rows, 128), bf16)] * groups
        + [((members, width, node_rows), bf16), square, square, square, (out_grad.shape, bf16)],
        (own_right, x, w_query, w_key, w_value, out_grad, w_out),
        specs=[pl.ANY, pltpu.VMEM] + [pltpu.HBM] * 5,
        scratch=[pltpu.VMEM((width, width), bf16), pltpu.SemaphoreType.DMA((5,))],
        limit=16,
    )
    to_right, to_left = call(
        relay_kernel, [three, three], (loc[0], own_right, own_left, plus, minus), specs=[pl.ANY]
    )
    right = shifted(to_right, 1)
    left = shifted(to_left, -1)
    (mask,) = call(
        mask_kernel, [((table, node_rows), f32)],
        (to_right, neighbours, neighbour_count.reshape(1, node_rows)),
        specs=[pl.ANY],
    )
    *halo, xtf = call(
        halo_kernel,
        [((4, members, node_rows, 128), bf16)] * groups + [((members, width, table), bf16)],
        (plus, minus, right, left, xt, wk, wv),
    )

    planes, rows = count // 4, width // count
    inner_planes = planes * 128 // width
    flip = [(i, i ^ 1) for i in range(count)]
    flop = [(i, i ^ 2) for i in range(count)]
    place = me.reshape(1)
    grads = []

    def attention(extra, which):
        wide = 512 * len(which)
        outs = call(
            functools.partial(attention_kernel, len(extra), len(which)),
            [((planes, rows, wide), kind) for kind in (f32, f32, bf16, bf16)]
            + [
                ((members, node_rows, 128), bf16),
                ((members, table, 128), bf16),
                ((members, table, 128), bf16),
            ]
            * len(which),
            (
                place, *extra, *[loc[g] for g in which], *[halo[g] for g in which], mask, xtf, og,
            ),
            specs=[pltpu.SMEM] + [pl.ANY] * len(extra),
            scratch=[pltpu.VMEM((members, table, 512), f32)] * 3
            + [
                pltpu.VMEM((planes, 2, 2, rows, 384), f32),
                pltpu.VMEM((inner_planes, 2, 2, rows, width), f32),
            ],
            limit=24,
        )
        grads.extend(outs[4:])
        own, other, send_other, send_own = outs[:4]
        return own, other, lax.ppermute(send_other, "patch", flip), lax.ppermute(send_own, "patch", flip)

    def along_z(sent):
        return [
            lax.ppermute(s, "patch", [(i, (i + 4 * k) % count) for i in range(count)])
            for k, s in enumerate(sent, 1)
        ]

    half = groups // 2
    wide = 384 * half
    own_a, other, core_other, core_own = attention((), range(half))
    y_sent = (other + core_other.astype(f32)).astype(bf16)
    y_a = lax.ppermute(y_sent, "patch", flop)
    later = []
    for g in range(half, groups):
        later.append(attention((y_sent,) if g == groups - 1 else (), range(g, g + 1)))
    own_b, other_b, core_other_b, core_own_b = zip(*later)
    y_sent, own_a, out_a, *sent = call(
        functools.partial(first_kernel, len(later)),
        [(y_sent.shape, bf16), ((rows, wide), f32), ((half * inner_planes, rows, width), f32)]
        + [((rows, wide), bf16)] * (planes - 1),
        (*other_b, *core_other_b, own_a, core_own, y_a),
    )
    y_b = lax.ppermute(y_sent, "patch", flop)
    node, back_left, back_right, back_minus, back_plus = call(
        functools.partial(node_kernel, groups, planes),
        [((members, node_rows, width), f32), three, three, one, one],
        (y_sent, *sent, *grads[0::3], *grads[1::3], *grads[2::3], wq, wk, wv),
        specs=[pl.ANY] * planes,
    )
    from_right = shifted(back_left, -1)
    from_left = shifted(back_right, 1)
    z_a = along_z(sent)
    near = (row_width // 4, planes - row_width // 4)
    blocks = (wide + width) // 256
    more = members * 6 * slots // rows
    own_b, *sent = call(
        functools.partial(second_kernel, planes, len(later), near),
        [((rows, wide + width), f32)]
        + [((blocks + (more if k in near else 0), rows, 256), bf16) for k in range(1, planes)],
        (
            place, node, *z_a, out_a, back_plus, back_minus, from_right, from_left, y_b,
            *own_b, *core_own_b,
        ),
        specs=[pltpu.SMEM] + [pl.ANY] * planes,
        scratch=[pltpu.VMEM((planes, rows, width), f32)],
    )
    z_b = along_z(sent)
    (node_grad,) = call(
        functools.partial(finish_kernel, blocks), [((members, node_rows, width), bf16)],
        (send_rows, node, from_right, from_left, z_b[near[0] - 1], z_b[near[1] - 1]),
    )
    (weight_grad,) = call(
        functools.partial(weight_kernel, planes), [((rows, 4 * width), f32)],
        (node_grad, own_a, own_b, *z_a, *z_b), specs=[pl.ANY],
    )
    return (node_grad, weight_grad)


def solution(mesh):
    in_specs = (
        P("groups", "patch", None),
        P("groups", "patch", None),
        P(),
        P(),
        P(),
        P(),
        P("patch", None),
        P("patch"),
        P("patch", None, None),
    )
    out_specs = (P("groups", "patch", None), P(("groups", "patch"), None))
    return jax.shard_map(body, mesh=mesh, in_specs=in_specs, out_specs=out_specs, check_vma=False)
```

time: 63.8 us -> 62.6 us (0.981); the launches traced: 62.8 us -> 62.4 us
  local copies, waits for them, and re-layouts: 8.07 us -> 2.71 us
  Pallas kernels: 12.9 us -> 17 us
  waiting for transfers between devices: 15.4 us -> 17.7 us
  starting transfers between devices: 25.5 us -> 24.2 us
    ppermute x6, waiting for transfers between devices: 5.9 us -> 11.6 us  [along_z(): lax.ppermute(s, 'patch', [(i, (i + 4 * k) % count) for i in range(count)])]
    unnamed x32 -> x20, local copies, waits for them, and re-layouts: 8.07 us -> 2.71 us
    pallas_call x15 -> x13, Pallas kernels: 12.9 us -> 17 us  [call(): pl.pallas_call(kernel, out_shape=[jax.ShapeDtypeStruct(*o) for o in outs]...]
    ppermute x8 -> x6, waiting for transfers between devices: 4.98 us -> 1.17 us  [shifted(): lax.ppermute(shard, 'patch', [(i, (i + by) % count) for i in range(count)])]
    ppermute x6, starting transfers between devices: 9.19 us -> 7.14 us  [along_z(): lax.ppermute(s, 'patch', [(i, (i + 4 * k) % count) for i in range(count)])]
    ppermute x8 -> x6, starting transfers between devices: 12.3 us -> 14.1 us  [shifted(): lax.ppermute(shard, 'patch', [(i, (i + by) % count) for i in range(count)])]
    ppermute x8, starting transfers between devices: 4.04 us -> 2.94 us  [the longest x3 1.01 us: attention(): lax.ppermute(send_own, 'patch', flip)]
  transfers between devices with their start and end apart: 22 -> 20, of which waited for: 10 -> 10; matrix products, arithmetic and copies ran while one was open for 0% -> 0% of each run, Pallas kernels for 15% -> 15%
where the time goes in v3:
time: 62.6 us; the launch traced here: 62.4 us
  starting transfers between devices  24.2 us (39%)
  waiting for transfers between devices  17.7 us (28%)
  Pallas kernels  17 us (27%)
  local copies, waits for them, and re-layouts  2.71 us (4%)
  between operations  0.79 us (1%)
    pallas_call x13, Pallas kernels, call(): pl.pallas_call(kernel, out_shape=[jax.ShapeDtypeStruct(*o) for o in outs]...  17 us
    ppermute x6, starting transfers between devices, shifted(): lax.ppermute(shard, 'patch', [(i, (i + by) % count) for i in range(count)])  14.1 us
    ppermute x6, waiting for transfers between devices, along_z(): lax.ppermute(s, 'patch', [(i, (i + 4 * k) % count) for i in range(count)])  11.6 us
    ppermute x6, starting transfers between devices, along_z(): lax.ppermute(s, 'patch', [(i, (i + 4 * k) % count) for i in range(count)])  7.14 us
    ppermute x1, waiting for transfers between devices, body(): y_a = lax.ppermute(y_sent, 'patch', flop)  2.92 us
    unnamed x20, local copies, waits for them, and re-layouts  2.71 us
    ppermute x3, waiting for transfers between devices, attention(): lax.ppermute(send_other, 'patch', flip)  2.01 us
  transfers between devices with their start and end apart: 20, of which 10 were waited for; matrix products, arithmetic and copies ran while one was open for 0% of the time, Pallas kernels for 15%

profile of v3, /device:TPU:0, one launch (start us, length us, event | category | flops | bytes accessed | tf_op | source)
XLA Modules:
  0.0 62.4 jit_solution(9403366435893817337)
XLA Ops:
  0.6 1.2 %shard_map.104 = (bf16[2,3,16,512]{3,2,1,0:T(8,128)(2,1)S(1)}, bf16[2,3,16,512]{3,2,1,0:T(8,128)(2,1)S(1)}, bf16[2,1,16,512]{3,2,1,0:T(8,128)(2,1)S(1)}, bf16[2,...) custom-call(s32[1,8,16]{2,1,0:T(8,128)} %send_ref.1, bf16[2,128,512]{2,1,0:T(8,128)(2,1)} %x_hbm.1), custom_call_target="tpu_custom_call" | custom-call | flops 1000000 | bytes 10000 | tf_op jit(solution)/shard_map/pallas_call | solution.py:409
  1.8 3.1 %collective-permute-start = (bf16[2,3,16,512]{3,2,1,0:T(8,128)(2,1)S(1)}, bf16[2,3,16,512]{3,2,1,0:T(8,128)(2,1)S(1)}, u32[]{:S(2)}, u32[]{:S(2)}) collective-permute-start(bf16[2,3,16,512]{3,2,1,0:T(8,128)(2,1)S(1)} %get-tuple-element.65), channel_id=1, source_target_pairs={{0,4},{1,5},{2,6},{3,7},{4,8},{5,9},{6,10},{7,11},{8,12},{9,13},{1... | collective-permute-start | bytes 294920 | tf_op jit(solution)/shard_map/ppermute | solution.py:28
  4.9 2.1 %collective-permute-start.1 = (bf16[2,3,16,512]{3,2,1,0:T(8,128)(2,1)S(1)}, bf16[2,3,16,512]{3,2,1,0:T(8,128)(2,1)S(1)}, u32[]{:S(2)}, u32[]{:S(2)}) collective-permute-start(bf16[2,3,16,512]{3,2,1,0:T(8,128)(2,1)S(1)} %get-tuple-element.66), channel_id=1, source_target_pairs={{0,12},{1,13},{2,14},{3,15},{4,0},{5,1},{6,2},{7,3},{8,4},{9,5},{1... | collective-permute-start | bytes 294920 | tf_op jit(solution)/shard_map/ppermute | solution.py:28
  7.0 2.6 %shard_map.105 = (bf16[8,2,128,128]{3,2,1,0:T(8,128)(2,1)S(1)}, bf16[8,2,128,128]{3,2,1,0:T(8,128)(2,1)S(1)}, bf16[8,2,128,128]{3,2,1,0:T(8,128)(2,1)S(1)}, bf16...) custom-call(bf16[2,1,16,512]{3,2,1,0:T(8,128)(2,1)S(1)} %get-tuple-e, ...), custom_call_target="tpu_custom_call" | custom-call | flops 1000000 | bytes 10000 | tf_op jit(solution)/shard_map/pallas_call | solution.py:409
  9.6 0.8 %copy-done.1 = bf16[8,2,128,128]{3,2,1,0:T(8,128)(2,1)} copy-done((bf16[8,2,128,128]{3,2,1,0:T(8,128)(2,1)}, bf16[8,2,128,128]{3,2,1,0:T(8,128)(2,1)S(1)}, u32[]{:S(2)}) %copy-start.1) | copy-done | bytes 524312
  10.4 0.0 collective-permute-done.plus_ref
  10.4 0.8 %collective-permute-done.1.minus_ref = bf16[2,3,16,512]{3,2,1,0:T(8,128)(2,1)S(1)} collective-permute-done((bf16[2,3,16,512]{3,2,1,0:T(8,128)(2,1)S(1)}, bf16[2,3,16,512]{3,2,1,0:T(8,128)(2,1)S(1)}, u32[]{:S(2)}, u32[]{:S(2)}) %collective-permute-start.1) | collective-permute-done | bytes 98336 | tf_op jit(solution)/shard_map/ppermute | solution.py:28
  11.3 0.7 %shard_map.106 = (bf16[2,3,16,512]{3,2,1,0:T(8,128)(2,1)}, bf16[2,3,16,512]{3,2,1,0:T(8,128)(2,1)}) custom-call(bf16[8,2,128,128]{3,2,1,0:T(8,128)(2,1)S(1)} %get-tuple-element.67.after_ref.refs_0_, bf16[2,1,16,512]{3,2,1,0:T(8,128)(2,1)S(1)} %get-tuple-element.62.after_ref.own_a, bf16[2,1,16,512]{3,2,1,0:T(8,128)(2,1)S(1)} %get-tuple-element.68.own_b, ...), custom_call_target="tpu_custom_call" | custom-call | flops 1000000 | bytes 10000 | tf_op jit(solution)/shard_map/pallas_call | solution.py:409
  12.0 0.0 collective-permute-start.2
  12.0 4.4 %collective-permute-start.3 = (bf16[2,3,16,512]{3,2,1,0:T(8,128)(2,1)}, bf16[2,3,16,512]{3,2,1,0:T(8,128)(2,1)}, u32[]{:S(2)}, u32[]{:S(2)}) collective-permute-start(bf16[2,3,16,512]{3,2,1,0:T(8,128)(2,1)} %get-tuple-element.70), channel_id=1, source_target_pairs={{0,15},{1,0},{2,1},{3,2},{4,3},{5,4},{6,5},{7,6},{8,7},{9,8},{10,9... | collective-permute-start | bytes 294920 | tf_op jit(solution)/shard_map/ppermute | solution.py:28
  16.4 0.9 %copy-done.7 = s32[128,256]{1,0:T(8,128)S(1)} copy-done((s32[128,256]{1,0:T(8,128)S(1)}, s32[128,256]{1,0:T(8,128)}, u32[]{:S(2)}) %copy-start.7) | copy-done | bytes 131096
  17.4 1.4 %shard_map.108.refs_2_.refs_4_.refs_3_ = f32[256,128]{1,0:T(8,128)S(1)} custom-call(bf16[2,3,16,512]{3,2,1,0:T(8,128)(2,1)} %get-tuple-element.69.after_ref, s32[128,256]{1,0:T(8,128)S(1)} %copy-done.7, s32[1,128]{1,0:T(1,128)S(1)} %bitcast.2), custom_call_target="tpu_custom_call" | custom-call | flops 1000000 | bytes 10000 | tf_op jit(solution)/shard_map/pallas_call | solution.py:409
  18.8 0.3 collective-permute-done.2.right_ref
  19.1 0.0 collective-permute-done.3.left_ref
  19.2 1.6 %shard_map.107 = (bf16[4,2,128,128]{3,2,1,0:T(8,128)(2,1)S(1)}, bf16[4,2,128,128]{3,2,1,0:T(8,128)(2,1)S(1)}, bf16[4,2,128,128]{3,2,1,0:T(8,128)(2,1)S(1)}, bf16...) custom-call(bf16[2,3,16,512]{3,2,1,0:T(8,128)(2,1)S(1)} %collective-permute-done.plus_ref, ...), custom_call_target="tpu_custom_call" | custom-call | flops 1000000 | bytes 10000 | tf_op jit(solution)/shard_map/pallas_call | solution.py:409
  20.7 3.1 %shard_map.110 = (f32[4,32,1024]{2,1,0:T(8,128)S(1)}, f32[4,32,1024]{2,1,0:T(8,128)S(1)}, bf16[4,32,1024]{2,1,0:T(8,128)(2,1)S(1)}, bf16[4,32,1024]{2,1,0:T(8,12...) custom-call(s32[1]{0:T(128)} %bitcast.me_ref, ...), custom_call_target="tpu_custom_call" | custom-call | flops 1000000 | bytes 10000 | tf_op jit(solution)/shard_map/pallas_call | solution.py:409
  23.8 0.1 collective-permute-start.4
  23.9 0.5 collective-permute-start.7
  24.4 1.0 %collective-permute-done.4 = bf16[4,32,1024]{2,1,0:T(8,128)(2,1)S(1)} collective-permute-done((bf16[4,32,1024]{2,1,0:T(8,128)(2,1)S(1)}, bf16[4,32,1024]{2,1,0:T(8,128)(2,1)S(1)}, u32[]{:S(2)}, u32[]{:S(2)}) %collective-permute-start.4) | collective-permute-done | bytes 262176 | tf_op jit(solution)/shard_map/ppermute | solution.py:498
  25.4 0.1 add_convert_fusion.refs_0_
  25.5 0.5 collective-permute-start.8
  26.0 1.7 %shard_map.109 = (f32[4,32,512]{2,1,0:T(8,128)S(1)}, f32[4,32,512]{2,1,0:T(8,128)S(1)}, bf16[4,32,512]{2,1,0:T(8,128)(2,1)S(1)}, bf16[4,32,512]{2,1,0:T(8,128)(2...) custom-call(s32[1]{0:T(128)} %bitcast.me_ref, ...), custom_call_target="tpu_custom_call" | custom-call | flops 1000000 | bytes 10000 | tf_op jit(solution)/shard_map/pallas_call | solution.py:409
  27.7 0.1 collective-permute-start.5
  27.8 1.7 %shard_map.111 = (f32[4,32,512]{2,1,0:T(8,128)S(1)}, f32[4,32,512]{2,1,0:T(8,128)S(1)}, bf16[4,32,512]{2,1,0:T(8,128)(2,1)S(1)}, bf16[4,32,512]{2,1,0:T(8,128)(2...) custom-call(s32[1]{0:T(128)} %bitcast.me_ref, ...), custom_call_target="tpu_custom_call" | custom-call | flops 1000000 | bytes 10000 | tf_op jit(solution)/shard_map/pallas_call | solution.py:409
  29.5 0.5 collective-permute-start.6
  30.0 0.0 collective-permute-done.5.refs_2_
  30.0 1.0 %collective-permute-done.6.refs_3_ = bf16[4,32,512]{2,1,0:T(8,128)(2,1)S(1)} collective-permute-done((bf16[4,32,512]{2,1,0:T(8,128)(2,1)S(1)}, bf16[4,32,512]{2,1,0:T(8,128)(2,1)S(1)}, u32[]{:S(2)}, u32[]{:S(2)}) %collective-permute-start.6) | collective-permute-done | bytes 131104 | tf_op jit(solution)/shard_map/ppermute | solution.py:498
  31.0 2.9 %collective-permute-done.8.refs_6_ = bf16[4,32,1024]{2,1,0:T(8,128)(2,1)S(1)} collective-permute-done((bf16[4,32,1024]{2,1,0:T(8,128)(2,1)S(1)}, bf16[4,32,1024]{2,1,0:T(8,128)(2,1)S(1)}, u32[]{:S(2)}, u32[]{:S(2)}) %collective-permute-start.8) | collective-permute-done | bytes 262176 | tf_op jit(solution)/shard_map/ppermute | solution.py:510
  33.9 0.1 shard_map.112
  34.0 0.7 %collective-permute-start.14 = (bf16[4,32,1024]{2,1,0:T(8,128)(2,1)S(1)}, bf16[4,32,1024]{2,1,0:T(8,128)(2,1)S(1)}, u32[]{:S(2)}, u32[]{:S(2)}) collective-permute-start(bf16[4,32,1024]{2,1,0:T(8,128)(2,1)S(1)} %get-tuple-element.90.refs_0_), channel_id=1, source_target_pairs={{0,2},{1,3},{2,0},{3,1},{4,6},{5,7},{6,4},{7,5},{8,10},{9,11},{10,... | collective-permute-start | bytes 786440 | tf_op jit(solution)/shard_map/ppermute | solution.py:521
  34.7 0.5 collective-permute-start.16
  35.2 0.8 %collective-permute-start.11 = (bf16[32,768]{1,0:T(8,128)(2,1)S(1)}, bf16[32,768]{1,0:T(8,128)(2,1)S(1)}, u32[]{:S(2)}, u32[]{:S(2)}) collective-permute-start(bf16[32,768]{1,0:T(8,128)(2,1)S(1)} %get-tuple-element.91.refs_1_), channel_id=1, source_target_pairs={{0,4},{1,5},{2,6},{3,7},{4,8},{5,9},{6,10},{7,11},{8,12},{9,13},{1... | collective-permute-start | bytes 147464 | tf_op jit(solution)/shard_map/ppermute | solution.py:502
  36.1 1.0 %shard_map.113 = (f32[2,128,512]{2,1,0:T(8,128)S(1)}, bf16[2,3,16,512]{3,2,1,0:T(8,128)(2,1)S(1)}, bf16[2,3,16,512]{3,2,1,0:T(8,128)(2,1)S(1)}, bf16[2,1,16,512]...) custom-call(bf16[4,32,1024]{2,1,0:T(8,128)(2,1)S(1)} %get-tuple-element.90.refs_0_, ...), custom_call_target="tpu_custom_call" | custom-call | flops 1000000 | bytes 10000 | tf_op jit(solution)/shard_map/pallas_call | solution.py:409
  37.1 0.1 collective-permute-start.10
  37.2 4.4 %collective-permute-start.9 = (bf16[2,3,16,512]{3,2,1,0:T(8,128)(2,1)S(1)}, bf16[2,3,16,512]{3,2,1,0:T(8,128)(2,1)S(1)}, u32[]{:S(2)}, u32[]{:S(2)}) collective-permute-start(bf16[2,3,16,512]{3,2,1,0:T(8,128)(2,1)S(1)} %get-tuple-element.108), channel_id=1, source_target_pairs={{0,15},{1,0},{2,1},{3,2},{4,3},{5,4},{6,5},{7,6},{8,7},{9,8},{10,9... | collective-permute-start | bytes 294920 | tf_op jit(solution)/shard_map/ppermute | solution.py:28
  41.6 2.4 %collective-permute-start.12 = (bf16[32,768]{1,0:T(8,128)(2,1)S(1)}, bf16[32,768]{1,0:T(8,128)(2,1)S(1)}, u32[]{:S(2)}, u32[]{:S(2)}) collective-permute-start(bf16[32,768]{1,0:T(8,128)(2,1)S(1)} %get-tuple-element.92.refs_2_), channel_id=1, source_target_pairs={{0,8},{1,9},{2,10},{3,11},{4,12},{5,13},{6,14},{7,15},{8,0},{9,1},... | collective-permute-start | bytes 147464 | tf_op jit(solution)/shard_map/ppermute | solution.py:502
  44.1 3.6 %collective-permute-done.12.refs_2_.refs_1_ = bf16[32,768]{1,0:T(8,128)(2,1)S(1)} collective-permute-done((bf16[32,768]{1,0:T(8,128)(2,1)S(1)}, bf16[32,768]{1,0:T(8,128)(2,1)S(1)}, u32[]{:S(2)}, u32[]{:S(2)}) %collective-permute-start.12) | collective-permute-done | bytes 49184 | tf_op jit(solution)/shard_map/ppermute | solution.py:502
  47.7 0.5 collective-permute-done.13.refs_3_.refs_2_
  48.2 0.1 shard_map.114
  48.4 0.0 copy-start.8
  48.4 0.6 collective-permute-start.17
  49.0 3.3 %collective-permute-start.18 = (bf16[11,32,256]{2,1,0:T(8,128)(2,1)S(1)}, bf16[11,32,256]{2,1,0:T(8,128)(2,1)S(1)}, u32[]{:S(2)}, u32[]{:S(2)}) collective-permute-start(bf16[11,32,256]{2,1,0:T(8,128)(2,1)S(1)} %get-tuple-element.118), channel_id=1, source_target_pairs={{0,12},{1,13},{2,14},{3,15},{4,0},{5,1},{6,2},{7,3},{8,4},{9,5},{1... | collective-permute-start | bytes 540680 | tf_op jit(solution)/shard_map/ppermute | solution.py:502
  52.3 4.0 %collective-permute-done.17.plus_ref.refs_3_ = bf16[11,32,256]{2,1,0:T(8,128)(2,1)S(1)} collective-permute-done((bf16[11,32,256]{2,1,0:T(8,128)(2,1)S(1)}, bf16[11,32,256]{2,1,0:T(8,128)(2,1)S(1)}, u32[]{:S(2)}, u32[]{:S(2)}) %collective-permute-start.17) | collective-permute-done | bytes 180256 | tf_op jit(solution)/shard_map/ppermute | solution.py:502
  56.3 0.6 collective-permute-done.18.minus_ref.refs_5_
  56.9 1.0 %shard_map.115.after_ref = bf16[2,128,512]{2,1,0:T(8,128)(2,1)} custom-call(s32[1,8,16]{2,1,0:T(8,128)S(1)} %copy-done.8, f32[2,128,512]{2,1,0:T(8,128)S(1)} %get-tuple-element.107.refs_0_.node_ref, bf16[2,3,16,512]{3,2,1,0:T(8,128)(2,1)S(1)} %collective-permute-done.9.refs_7_.left_ref, ...), custom_call_target="tpu_custom_call" | custom-call | flops 1000000 | bytes 10000 | tf_op jit(solution)/shard_map/pallas_call | solution.py:409
  57.9 2.8 %collective-permute-done.19.refs_4_ = bf16[5,32,256]{2,1,0:T(8,128)(2,1)S(1)} collective-permute-done((bf16[5,32,256]{2,1,0:T(8,128)(2,1)S(1)}, bf16[5,32,256]{2,1,0:T(8,128)(2,1)S(1)}, u32[]{:S(2)}, u32[]{:S(2)}) %collective-permute-start.19) | collective-permute-done | bytes 81952 | tf_op jit(solution)/shard_map/ppermute | solution.py:502
  60.7 0.9 %copy-done = bf16[2,128,512]{2,1,0:T(8,128)(2,1)S(1)} copy-done((bf16[2,128,512]{2,1,0:T(8,128)(2,1)S(1)}, bf16[2,128,512]{2,1,0:T(8,128)(2,1)}, u32[]{:S(2)}) %copy-start) | copy-done | bytes 262168
  61.6 0.8 %shard_map.116 = f32[32,2048]{1,0:T(8,128)} custom-call(bf16[2,128,512]{2,1,0:T(8,128)(2,1)S(1)} %copy-done, f32[32,768]{1,0:T(8,128)S(1)} %get-tuple-element.119.own_a, f32[32,1280]{1,0:T(8,128)S(1)} %get-tuple-element.120.own_b, bf16[32,768]{1,0:T(8,128)(2,1)S(1)} %collective-permute-done.11.refs_1_.refs_0_, ...), custom_call_target="tpu_custom_call" | custom-call | flops 1000000 | bytes 10000 | tf_op jit(solution)/shard_map/pallas_call | solution.py:409
  (26 shorter events, 0.1 us)
Async XLA Ops:
  1.8 8.6 %collective-permute-start = (bf16[2,3,16,512]{3,2,1,0:T(8,128)(2,1)S(1)}, bf16[2,3,16,512]{3,2,1,0:T(8,128)(2,1)S(1)}, u32[]{:S(2)}, u32[]{:S(2)}) collective-permute-start(bf16[2,3,16,512]{3,2,1,0:T(8,128)(2,1)S(1)} %get-tuple-element.65), channel_id=1, source_target_pairs={{0,4},{1,5},{2,6},{3,7},{4,8},{5,9},{6,10},{7,11},{8,12},{9,13},{1... | collective-permute-start | bytes 294920 | tf_op jit(solution)/shard_map/ppermute | solution.py:28
  4.9 6.4 %collective-permute-start.1 = (bf16[2,3,16,512]{3,2,1,0:T(8,128)(2,1)S(1)}, bf16[2,3,16,512]{3,2,1,0:T(8,128)(2,1)S(1)}, u32[]{:S(2)}, u32[]{:S(2)}) collective-permute-start(bf16[2,3,16,512]{3,2,1,0:T(8,128)(2,1)S(1)} %get-tuple-element.66), channel_id=1, source_target_pairs={{0,12},{1,13},{2,14},{3,15},{4,0},{5,1},{6,2},{7,3},{8,4},{9,5},{1... | collective-permute-start | bytes 294920 | tf_op jit(solution)/shard_map/ppermute | solution.py:28
  9.6 0.8 %copy-start.1 = (bf16[8,2,128,128]{3,2,1,0:T(8,128)(2,1)}, bf16[8,2,128,128]{3,2,1,0:T(8,128)(2,1)S(1)}, u32[]{:S(2)}) copy-start(bf16[8,2,128,128]{3,2,1,0:T(8,128)(2,1)S(1)} %get-tuple-element.78.refs_1_) | copy-start | bytes 1572868
  10.4 1.5 %copy-start.5 = (bf16[2,512,128]{2,1,0:T(8,128)(2,1)}, bf16[2,512,128]{2,1,0:T(8,128)(2,1)S(1)}, u32[]{:S(2)}) copy-start(bf16[2,512,128]{2,1,0:T(8,128)(2,1)S(1)} %get-tuple-element.71.xt_ref) | copy-start | bytes 786436
  11.3 0.7 %copy-start.3 = (bf16[2,3,16,512]{3,2,1,0:T(8,128)(2,1)}, bf16[2,3,16,512]{3,2,1,0:T(8,128)(2,1)S(1)}, u32[]{:S(2)}) copy-start(bf16[2,3,16,512]{3,2,1,0:T(8,128)(2,1)S(1)} %collective-permute-done.1.minus_ref) | copy-start | bytes 294916
  11.3 5.1 %copy-start.9 = (s32[128]{0:T(128)S(1)}, s32[128]{0:T(128)}, u32[]{:S(2)}) copy-start(s32[128]{0:T(128)} %param.16) | copy-start | bytes 1540
  12.0 7.2 %collective-permute-start.2 = (bf16[2,3,16,512]{3,2,1,0:T(8,128)(2,1)}, bf16[2,3,16,512]{3,2,1,0:T(8,128)(2,1)}, u32[]{:S(2)}, u32[]{:S(2)}) collective-permute-start(bf16[2,3,16,512]{3,2,1,0:T(8,128)(2,1)} %get-tuple-element.69.after_ref), channel_id=1, source_target_pairs={{0,1},{1,2},{2,3},{3,4},{4,5},{5,6},{6,7},{7,8},{8,9},{9,10},{10,1... | collective-permute-start | bytes 294920 | tf_op jit(solution)/shard_map/ppermute | solution.py:28
  12.0 7.2 %collective-permute-start.3 = (bf16[2,3,16,512]{3,2,1,0:T(8,128)(2,1)}, bf16[2,3,16,512]{3,2,1,0:T(8,128)(2,1)}, u32[]{:S(2)}, u32[]{:S(2)}) collective-permute-start(bf16[2,3,16,512]{3,2,1,0:T(8,128)(2,1)} %get-tuple-element.70), channel_id=1, source_target_pairs={{0,15},{1,0},{2,1},{3,2},{4,3},{5,4},{6,5},{7,6},{8,7},{9,8},{10,9... | collective-permute-start | bytes 294920 | tf_op jit(solution)/shard_map/ppermute | solution.py:28
  16.4 2.7 %copy-start.6 = (bf16[2,512,128]{2,1,0:T(8,128)(2,1)S(1)}, bf16[2,512,128]{2,1,0:T(8,128)(2,1)}, u32[]{:S(2)}) copy-start(bf16[2,512,128]{2,1,0:T(8,128)(2,1)} %copy-done.5) | copy-start | bytes 786436
  16.4 0.9 %copy-start.7 = (s32[128,256]{1,0:T(8,128)S(1)}, s32[128,256]{1,0:T(8,128)}, u32[]{:S(2)}) copy-start(s32[128,256]{1,0:T(8,128)} %neigh_ref.1) | copy-start | bytes 393220
  17.4 1.8 %copy-start.4 = (bf16[2,3,16,512]{3,2,1,0:T(8,128)(2,1)S(1)}, bf16[2,3,16,512]{3,2,1,0:T(8,128)(2,1)}, u32[]{:S(2)}) copy-start(bf16[2,3,16,512]{3,2,1,0:T(8,128)(2,1)} %copy-done.3) | copy-start | bytes 294916
  19.1 1.6 %copy-start.2 = (bf16[8,2,128,128]{3,2,1,0:T(8,128)(2,1)S(1)}, bf16[8,2,128,128]{3,2,1,0:T(8,128)(2,1)}, u32[]{:S(2)}) copy-start(bf16[8,2,128,128]{3,2,1,0:T(8,128)(2,1)} %copy-done.1) | copy-start | bytes 1572868
  23.8 1.6 %collective-permute-start.4 = (bf16[4,32,1024]{2,1,0:T(8,128)(2,1)S(1)}, bf16[4,32,1024]{2,1,0:T(8,128)(2,1)S(1)}, u32[]{:S(2)}, u32[]{:S(2)}) collective-permute-start(bf16[4,32,1024]{2,1,0:T(8,128)(2,1)S(1)} %get-tuple-element.82), channel_id=1, source_target_pairs={{0,1},{1,0},{2,3},{3,2},{4,5},{5,4},{6,7},{7,6},{8,9},{9,8},{10,11... | collective-permute-start | bytes 786440 | tf_op jit(solution)/shard_map/ppermute | solution.py:498
  23.9 6.1 %collective-permute-start.7 = (bf16[4,32,1024]{2,1,0:T(8,128)(2,1)S(1)}, bf16[4,32,1024]{2,1,0:T(8,128)(2,1)S(1)}, u32[]{:S(2)}, u32[]{:S(2)}) collective-permute-start(bf16[4,32,1024]{2,1,0:T(8,128)(2,1)S(1)} %get-tuple-element.89), channel_id=1, source_target_pairs={{0,1},{1,0},{2,3},{3,2},{4,5},{5,4},{6,7},{7,6},{8,9},{9,8},{10,11... | collective-permute-start | bytes 786440 | tf_op jit(solution)/shard_map/ppermute | solution.py:498
  25.5 8.4 %collective-permute-start.8 = (bf16[4,32,1024]{2,1,0:T(8,128)(2,1)S(1)}, bf16[4,32,1024]{2,1,0:T(8,128)(2,1)S(1)}, u32[]{:S(2)}, u32[]{:S(2)}) collective-permute-start(bf16[4,32,1024]{2,1,0:T(8,128)(2,1)S(1)} %add_convert_fusion.refs_0_), channel_id=1, source_target_pairs={{0,2},{1,3},{2,0},{3,1},{4,6},{5,7},{6,4},{7,5},{8,10},{9,11},{10,... | collective-permute-start | bytes 786440 | tf_op jit(solution)/shard_map/ppermute | solution.py:510
  27.7 2.3 %collective-permute-start.5 = (bf16[4,32,512]{2,1,0:T(8,128)(2,1)S(1)}, bf16[4,32,512]{2,1,0:T(8,128)(2,1)S(1)}, u32[]{:S(2)}, u32[]{:S(2)}) collective-permute-start(bf16[4,32,512]{2,1,0:T(8,128)(2,1)S(1)} %get-tuple-element.86), channel_id=1, source_target_pairs={{0,1},{1,0},{2,3},{3,2},{4,5},{5,4},{6,7},{7,6},{8,9},{9,8},{10,11... | collective-permute-start | bytes 393224 | tf_op jit(solution)/shard_map/ppermute | solution.py:498
  29.5 1.5 %collective-permute-start.6 = (bf16[4,32,512]{2,1,0:T(8,128)(2,1)S(1)}, bf16[4,32,512]{2,1,0:T(8,128)(2,1)S(1)}, u32[]{:S(2)}, u32[]{:S(2)}) collective-permute-start(bf16[4,32,512]{2,1,0:T(8,128)(2,1)S(1)} %get-tuple-element.87), channel_id=1, source_target_pairs={{0,1},{1,0},{2,3},{3,2},{4,5},{5,4},{6,7},{7,6},{8,9},{9,8},{10,11... | collective-permute-start | bytes 393224 | tf_op jit(solution)/shard_map/ppermute | solution.py:498
  34.0 14.2 %collective-permute-start.14 = (bf16[4,32,1024]{2,1,0:T(8,128)(2,1)S(1)}, bf16[4,32,1024]{2,1,0:T(8,128)(2,1)S(1)}, u32[]{:S(2)}, u32[]{:S(2)}) collective-permute-start(bf16[4,32,1024]{2,1,0:T(8,128)(2,1)S(1)} %get-tuple-element.90.refs_0_), channel_id=1, source_target_pairs={{0,2},{1,3},{2,0},{3,1},{4,6},{5,7},{6,4},{7,5},{8,10},{9,11},{10,... | collective-permute-start | bytes 786440 | tf_op jit(solution)/shard_map/ppermute | solution.py:521
  34.7 2.4 %collective-permute-start.15 = (bf16[4,32,512]{2,1,0:T(8,128)(2,1)S(1)}, bf16[4,32,512]{2,1,0:T(8,128)(2,1)S(1)}, u32[]{:S(2)}, u32[]{:S(2)}) collective-permute-start(bf16[4,32,512]{2,1,0:T(8,128)(2,1)S(1)} %get-tuple-element.115), channel_id=1, source_target_pairs={{0,1},{1,0},{2,3},{3,2},{4,5},{5,4},{6,7},{7,6},{8,9},{9,8},{10,11... | collective-permute-start | bytes 393224 | tf_op jit(solution)/shard_map/ppermute | solution.py:498
  34.7 6.9 %collective-permute-start.16 = (bf16[4,32,512]{2,1,0:T(8,128)(2,1)S(1)}, bf16[4,32,512]{2,1,0:T(8,128)(2,1)S(1)}, u32[]{:S(2)}, u32[]{:S(2)}) collective-permute-start(bf16[4,32,512]{2,1,0:T(8,128)(2,1)S(1)} %get-tuple-element.116), channel_id=1, source_target_pairs={{0,1},{1,0},{2,3},{3,2},{4,5},{5,4},{6,7},{7,6},{8,9},{9,8},{10,11... | collective-permute-start | bytes 393224 | tf_op jit(solution)/shard_map/ppermute | solution.py:498
  35.2 8.8 %collective-permute-start.11 = (bf16[32,768]{1,0:T(8,128)(2,1)S(1)}, bf16[32,768]{1,0:T(8,128)(2,1)S(1)}, u32[]{:S(2)}, u32[]{:S(2)}) collective-permute-start(bf16[32,768]{1,0:T(8,128)(2,1)S(1)} %get-tuple-element.91.refs_1_), channel_id=1, source_target_pairs={{0,4},{1,5},{2,6},{3,7},{4,8},{5,9},{6,10},{7,11},{8,12},{9,13},{1... | collective-permute-start | bytes 147464 | tf_op jit(solution)/shard_map/ppermute | solution.py:502
  37.1 11.1 %collective-permute-start.10 = (bf16[2,3,16,512]{3,2,1,0:T(8,128)(2,1)S(1)}, bf16[2,3,16,512]{3,2,1,0:T(8,128)(2,1)S(1)}, u32[]{:S(2)}, u32[]{:S(2)}) collective-permute-start(bf16[2,3,16,512]{3,2,1,0:T(8,128)(2,1)S(1)} %get-tuple-element.109), channel_id=1, source_target_pairs={{0,1},{1,2},{2,3},{3,4},{4,5},{5,6},{6,7},{7,8},{8,9},{9,10},{10,1... | collective-permute-start | bytes 294920 | tf_op jit(solution)/shard_map/ppermute | solution.py:28
  37.2 11.0 %collective-permute-start.9 = (bf16[2,3,16,512]{3,2,1,0:T(8,128)(2,1)S(1)}, bf16[2,3,16,512]{3,2,1,0:T(8,128)(2,1)S(1)}, u32[]{:S(2)}, u32[]{:S(2)}) collective-permute-start(bf16[2,3,16,512]{3,2,1,0:T(8,128)(2,1)S(1)} %get-tuple-element.108), channel_id=1, source_target_pairs={{0,15},{1,0},{2,1},{3,2},{4,3},{5,4},{6,5},{7,6},{8,7},{9,8},{10,9... | collective-permute-start | bytes 294920 | tf_op jit(solution)/shard_map/ppermute | solution.py:28
  41.6 6.1 %collective-permute-start.12 = (bf16[32,768]{1,0:T(8,128)(2,1)S(1)}, bf16[32,768]{1,0:T(8,128)(2,1)S(1)}, u32[]{:S(2)}, u32[]{:S(2)}) collective-permute-start(bf16[32,768]{1,0:T(8,128)(2,1)S(1)} %get-tuple-element.92.refs_2_), channel_id=1, source_target_pairs={{0,8},{1,9},{2,10},{3,11},{4,12},{5,13},{6,14},{7,15},{8,0},{9,1},... | collective-permute-start | bytes 147464 | tf_op jit(solution)/shard_map/ppermute | solution.py:502
  44.0 4.2 %collective-permute-start.13 = (bf16[32,768]{1,0:T(8,128)(2,1)S(1)}, bf16[32,768]{1,0:T(8,128)(2,1)S(1)}, u32[]{:S(2)}, u32[]{:S(2)}) collective-permute-start(bf16[32,768]{1,0:T(8,128)(2,1)S(1)} %get-tuple-element.93.refs_3_), channel_id=1, source_target_pairs={{0,12},{1,13},{2,14},{3,15},{4,0},{5,1},{6,2},{7,3},{8,4},{9,5},{1... | collective-permute-start | bytes 147464 | tf_op jit(solution)/shard_map/ppermute | solution.py:502
  48.4 8.5 %copy-start.8 = (s32[1,8,16]{2,1,0:T(8,128)S(1)}, s32[1,8,16]{2,1,0:T(8,128)}, u32[]{:S(2)}) copy-start(s32[1,8,16]{2,1,0:T(8,128)} %send_ref.1) | copy-start | bytes 1540
  48.4 7.9 %collective-permute-start.17 = (bf16[11,32,256]{2,1,0:T(8,128)(2,1)S(1)}, bf16[11,32,256]{2,1,0:T(8,128)(2,1)S(1)}, u32[]{:S(2)}, u32[]{:S(2)}) collective-permute-start(bf16[11,32,256]{2,1,0:T(8,128)(2,1)S(1)} %get-tuple-element.117), channel_id=1, source_target_pairs={{0,4},{1,5},{2,6},{3,7},{4,8},{5,9},{6,10},{7,11},{8,12},{9,13},{1... | collective-permute-start | bytes 540680 | tf_op jit(solution)/shard_map/ppermute | solution.py:502
  49.0 7.9 %collective-permute-start.18 = (bf16[11,32,256]{2,1,0:T(8,128)(2,1)S(1)}, bf16[11,32,256]{2,1,0:T(8,128)(2,1)S(1)}, u32[]{:S(2)}, u32[]{:S(2)}) collective-permute-start(bf16[11,32,256]{2,1,0:T(8,128)(2,1)S(1)} %get-tuple-element.118), channel_id=1, source_target_pairs={{0,12},{1,13},{2,14},{3,15},{4,0},{5,1},{6,2},{7,3},{8,4},{9,5},{1... | collective-permute-start | bytes 540680 | tf_op jit(solution)/shard_map/ppermute | solution.py:502
  52.3 8.4 %collective-permute-start.19 = (bf16[5,32,256]{2,1,0:T(8,128)(2,1)S(1)}, bf16[5,32,256]{2,1,0:T(8,128)(2,1)S(1)}, u32[]{:S(2)}, u32[]{:S(2)}) collective-permute-start(bf16[5,32,256]{2,1,0:T(8,128)(2,1)S(1)} %get-tuple-element.121), channel_id=1, source_target_pairs={{0,8},{1,9},{2,10},{3,11},{4,12},{5,13},{6,14},{7,15},{8,0},{9,1},... | collective-permute-start | bytes 245768 | tf_op jit(solution)/shard_map/ppermute | solution.py:502
  60.7 1.0 %copy-start = (bf16[2,128,512]{2,1,0:T(8,128)(2,1)S(1)}, bf16[2,128,512]{2,1,0:T(8,128)(2,1)}, u32[]{:S(2)}) copy-start(bf16[2,128,512]{2,1,0:T(8,128)(2,1)} %shard_map.115.after_ref) | copy-start | bytes 786436

commit v4 on v3

--- a/solution.py
+++ b/solution.py
@@ -23,9 +23,31 @@
     return lax.dot_general(a, b, (((1,), (1,)), ((), ())), preferred_element_type=f32)
 
 
-def shifted(shard, by):
-    count = lax.axis_size("patch")
-    return lax.ppermute(shard, "patch", [(i, (i + by) % count) for i in range(count)])
+def neighbours_apart(count, stride):
+    first, second = [], []
+    for i in range(count):
+        up, down = (i + stride) % count, (i - stride) % count
+        even = i // stride % 2 == 0
+        first.append((i, up if even else down))
+        second.append((i, down if even else up))
+    return first, second
+
+
+def swap(pair, stride):
+    return [
+        lax.ppermute(shard, "patch", perm)
+        for shard, perm in zip(pair, neighbours_apart(lax.axis_size("patch"), stride))
+    ]
+
+
+def to_swaps(both, odd, first_ref, second_ref):
+    first_ref[...] = both[odd]
+    second_ref[...] = both[1 - odd]
+
+
+def from_swaps(both, odd, first_ref, second_ref):
+    both[1 - odd] = first_ref[...]
+    both[odd] = second_ref[...]
 
 
 def sent_selector(send_rows, node_rows):
@@ -40,7 +62,10 @@
     return jnp.where(nodes == ids, 1.0, 0.0).astype(f32)
 
 
-def gather_kernel(slots, send_hbm, x_hbm, plus_ref, minus_ref, right_ref, left_ref, x_ref, send_ref, sem):
+def gather_kernel(
+    slots, stride, me_ref, send_hbm, x_hbm, first_ref, second_ref, right_ref, left_ref, x_ref,
+    send_ref, both, sem,
+):
     copies = [
         pltpu.make_async_copy(send_hbm, send_ref, sem.at[0]),
         pltpu.make_async_copy(x_hbm, x_ref, sem.at[1]),
@@ -57,29 +82,34 @@
         def part(k):
             return rows[k * slots : (k + 1) * slots]
 
-        for i, k in enumerate((2, 6, 4)):
-            plus_ref[m, i] = part(k)
-        for i, k in enumerate((3, 5, 7)):
-            minus_ref[m, i] = part(k)
+        for side, order in enumerate(((2, 6, 4), (3, 5, 7))):
+            for i, k in enumerate(order):
+                both[side, m, i] = part(k)
         right_ref[m, 0] = part(0)
         left_ref[m, 0] = part(1)
-
-
-def relay_kernel(after_ref, own_a, own_b, plus_ref, minus_ref, a_ref, b_ref):
-    a_ref[:, 0:1] = own_a[...]
-    a_ref[:, 1:2] = plus_ref[:, 1:2]
-    a_ref[:, 2:3] = minus_ref[:, 1:2]
-    b_ref[:, 0:1] = own_b[...]
-    b_ref[:, 1:2] = plus_ref[:, 2:3]
-    b_ref[:, 2:3] = minus_ref[:, 2:3]
+    to_swaps(both, me_ref[0] // stride % 2, first_ref, second_ref)
+
+
+def relay_kernel(
+    stride, me_ref, after_ref, own_right, own_left, first_in, second_in, first_ref, second_ref,
+    plus_ref, minus_ref, came, both,
+):
+    from_swaps(came, me_ref[0] // stride % 2, first_in, second_in)
+    for side, own in enumerate((own_right, own_left)):
+        both[side, :, 0:1] = own[...]
+        both[side, :, 1:2] = came[0, :, 1 + side : 2 + side]
+        both[side, :, 2:3] = came[1, :, 1 + side : 2 + side]
+    to_swaps(both, me_ref[0] % 2, first_ref, second_ref)
+    plus_ref[...] = came[0, :, 0:1]
+    minus_ref[...] = came[1, :, 0:1]
 
 
 Q, K, V, G, QT, KT, VT, GT = range(8)
 
 
 def local_kernel(groups, after_ref, x_ref, *refs):
-    sources, loc_refs, xt_ref = refs[:5], refs[5 : 5 + groups], refs[5 + groups]
-    copied, sem = refs[6 + groups : 11 + groups], refs[-1]
+    sources, loc_refs, xt_ref = refs[:7], refs[7 : 7 + groups], refs[7 + groups]
+    copied, sem = refs[8 + groups : 15 + groups], refs[-1]
     copies = [
         pltpu.make_async_copy(source, target, sem.at[i])
         for i, (source, target) in enumerate(zip(sources, copied))
@@ -98,12 +128,12 @@
                 ref[kind, m] = block
                 ref[kind + 4, m] = block.T
 
-    wq_ref, wk_ref, wv_ref, og_ref, wo_ref = copied
+    wq_ref, wk_ref, wv_ref, og_ref, _, _, wo_ref = copied
     for kind, ref in enumerate((wq_ref, wk_ref, wv_ref)):
         copies[kind].wait()
         put(nn(x, ref[...]).astype(bf16), kind)
-    copies[3].wait()
-    copies[4].wait()
+    for copy in copies[3:]:
+        copy.wait()
     og = og_ref[...].reshape(members * node_rows, width)
     put(nt(og, wo_ref[...]).astype(bf16), G)
 
@@ -123,19 +153,19 @@
         mask_ref[part * half : (part + 1) * half] = kept
 
 
-def halo_kernel(plus_ref, minus_ref, right_ref, left_ref, xt_ref, wk_ref, wv_ref, *out_refs):
-    halo_refs, xtf_ref = out_refs[:-1], out_refs[-1]
+def halo_kernel(
+    me_ref, plus_ref, minus_ref, first_in, second_in, xt_ref, wk_ref, wv_ref, *refs
+):
+    halo_refs, xtf_ref, both = refs[:-2], refs[-2], refs[-1]
     members, _, node_rows = xt_ref.shape
+    from_swaps(both, me_ref[0] % 2, first_in, second_in)
     for m in range(members):
         pieces = [None] * 8
-        for ref, order in (
-            (right_ref, (0, 6, 5)),
-            (left_ref, (1, 4, 7)),
-            (plus_ref, (2,)),
-            (minus_ref, (3,)),
-        ):
+        for side, order in enumerate(((0, 6, 5), (1, 4, 7))):
             for i, k in enumerate(order):
-                pieces[k] = ref[m, i]
+                pieces[k] = both[side, m, i]
+        pieces[2] = plus_ref[m, 0]
+        pieces[3] = minus_ref[m, 0]
         halo = jnp.concatenate(pieces, axis=0)
         xtf_ref[m, :, :node_rows] = xt_ref[m]
         xtf_ref[m, :, node_rows:] = halo.T
@@ -265,12 +295,12 @@
             send_own[k, :, last] = wos[i, y, 1 - c, :, lanes].astype(bf16)
 
 
-def node_kernel(groups, skip, *refs):
+def node_kernel(groups, skip, me_ref, *refs):
     refs = refs[skip:]
     dqs, dks, dvs = refs[:groups], refs[groups : 2 * groups], refs[2 * groups : 3 * groups]
-    wq_ref, wk_ref, wv_ref, node_ref, left_ref, right_ref, minus_ref, plus_ref = refs[3 * groups :]
+    wq_ref, wk_ref, wv_ref, node_ref, first_ref, second_ref, plus_ref, minus_ref, both = refs[3 * groups :]
     members, node_rows, _ = dqs[0].shape
-    slots = left_ref.shape[2]
+    slots = plus_ref.shape[2]
 
     def whole(parts, m):
         return jnp.concatenate([part[m] for part in parts], axis=1)
@@ -280,13 +310,14 @@
         node_ref[m] = spread[:node_rows] + nt(whole(dqs, m), wq_ref[...])
         halo = spread[node_rows:].astype(bf16)
         for ref, order in (
-            (left_ref, (0, 6, 5)),
-            (right_ref, (1, 4, 7)),
+            (both.at[0], (1, 4, 7)),
+            (both.at[1], (0, 6, 5)),
+            (plus_ref, (3,)),
             (minus_ref, (2,)),
-            (plus_ref, (3,)),
         ):
             for i, k in enumerate(order):
                 ref[m, i] = halo[k * slots : (k + 1) * slots]
+    to_swaps(both, me_ref[0] % 2, first_ref, second_ref)
 
 
 def sums(owns, core_in, y_in, k):
@@ -304,30 +335,30 @@
         projection_ref[plane, :, quarter * 128 : (quarter + 1) * 128] = part[:, 384:]
 
 
-def first_kernel(pieces, *refs):
+def first_kernel(pieces, me_ref, *refs):
     later, later_core, refs = refs[:pieces], refs[pieces : 2 * pieces], refs[2 * pieces :]
-    own, core_in, y_in, next_ref, own_ref, projection_ref, *sent = refs
+    own, core_in, y_in, next_ref, own_ref, projection_ref, sent = refs
     for i, (ref, core) in enumerate(zip(later, later_core)):
         next_ref[:, :, i * 512 : (i + 1) * 512] = (ref[...] + core[...].astype(f32)).astype(bf16)
-    planes = len(sent) + 1
+    planes = sent.shape[0]
+    z = me_ref[0] // 4
     for k in range(planes):
         parts = sums([own], [core_in], y_in, k)
         gather_projection(parts, k, planes, projection_ref, 0)
         row = jnp.concatenate([part[:, :384] for part in parts], axis=1)
-        if k:
-            sent[k - 1][...] = row.astype(bf16)
-        else:
+        sent[(z + k) % planes] = row.astype(bf16)
+        if k == 0:
             own_ref[...] = row
 
 
-def second_kernel(planes, pieces, near, me_ref, *refs):
-    refs = refs[planes:]
-    first_ref, back_plus, back_minus, from_right, from_left, y_in = refs[:6]
+def second_kernel(skip, pieces, stride, me_ref, *refs):
+    refs = refs[skip:]
+    first_ref, back_plus, back_minus, first_in, second_in, y_in = refs[:6]
     owns, core_in = refs[6 : 6 + pieces], refs[6 + pieces : 6 + 2 * pieces]
-    own_ref, *sent = refs[6 + 2 * pieces : -1]
-    projection_ref = refs[-1]
-    done, rows, width = first_ref.shape
-    members = back_plus.shape[0]
+    own_ref, sent, home_first, home_second = refs[6 + 2 * pieces : -3]
+    projection_ref, came, both = refs[-3:]
+    done = first_ref.shape[0]
+    planes = sent.shape[0]
     projection_ref[:done] = first_ref[...]
     held = []
     for k in range(planes):
@@ -336,59 +367,44 @@
         held.append(jnp.concatenate([part[:, :384] for part in parts], axis=1))
     z = me_ref[0] // 4
     for k in range(planes):
-        row = jnp.concatenate([held[k], projection_ref[(z + k) % planes]], axis=1)
-        if not k:
+        zk = (z + k) % planes
+        row = jnp.concatenate([held[k], projection_ref[zk]], axis=1)
+        sent[zk] = row.astype(bf16)
+        if k == 0:
             own_ref[...] = row
-            continue
-        row = row.astype(bf16)
-        blocks = row.shape[1] // 256
-        for n in range(blocks):
-            sent[k - 1][n] = row[:, n * 256 : (n + 1) * 256]
-        if k not in near:
-            continue
-        side = near.index(k)
-        relayed = 2 - side
-        for m in range(members):
-            trio = ((back_plus, back_minus)[side][m, 0], from_right[m, relayed], from_left[m, relayed])
-            for i, part in enumerate(trio):
-                flat = jnp.concatenate([part[:, :256], part[:, 256:]], axis=0)
-                pieces = flat.shape[0] // rows
-                at = blocks + (m * 3 + i) * pieces
-                sent[k - 1][at : at + pieces] = flat.reshape(pieces, rows, 256)
-
-
-def finish_kernel(blocks, send_ref, node_ref, left_ref, right_ref, plus_ref, minus_ref, out_ref):
+    from_swaps(came, me_ref[0] % 2, first_in, second_in)
+    for side, own in enumerate((back_plus, back_minus)):
+        both[side, :, 0:1] = own[...]
+        both[side, :, 1:2] = came[1, :, 2 - side : 3 - side]
+        both[side, :, 2:3] = came[0, :, 2 - side : 3 - side]
+    to_swaps(both, me_ref[0] // stride % 2, home_first, home_second)
+
+
+def finish_kernel(
+    stride, me_ref, send_ref, node_ref, first_in, second_in, home_first, home_second, out_ref,
+    came, home,
+):
     members, node_rows, _ = node_ref.shape
-    slots = left_ref.shape[2]
     pick = sent_selector(send_ref[0], node_rows).astype(bf16)
-    rows = plus_ref.shape[1]
-    each = 2 * slots // rows
-
-    def arrived(ref, m, i):
-        at = blocks + (m * 3 + i) * each
-        flat = ref[at : at + each].reshape(2 * slots, 256)
-        return jnp.concatenate([flat[:slots], flat[slots:]], axis=1)
-
+    from_swaps(came, me_ref[0] % 2, first_in, second_in)
+    from_swaps(home, me_ref[0] // stride % 2, home_first, home_second)
     for m in range(members):
         pieces = [None] * 8
-        pieces[0] = left_ref[m, 0]
-        pieces[1] = right_ref[m, 0]
-        for i, k in enumerate((2, 6, 4)):
-            pieces[k] = arrived(minus_ref, m, i)
-        for i, k in enumerate((3, 5, 7)):
-            pieces[k] = arrived(plus_ref, m, i)
+        pieces[0], pieces[1] = came[1, m, 0], came[0, m, 0]
+        for side, order in enumerate(((3, 5, 7), (2, 6, 4))):
+            for i, k in enumerate(order):
+                pieces[k] = home[side, m, i]
         arriving = jnp.concatenate(pieces, axis=0)
         out_ref[m] = (node_ref[m] + nn(pick, arriving)).astype(bf16)
 
 
-def weight_kernel(planes, after_ref, own_a, own_b, *refs):
-    z_a, z_b, out_ref = refs[: planes - 1], refs[planes - 1 : -1], refs[-1]
+def weight_kernel(me_ref, after_ref, own_a, own_b, z_a, z_b, out_ref):
+    planes = z_a.shape[0]
+    z = me_ref[0] // 4
     a, b = own_a[...], own_b[...]
-    blocks = b.shape[1] // 256
-    for ref in z_a:
-        a = a + ref[...].astype(f32)
-    for ref in z_b:
-        b = b + jnp.concatenate([ref[n].astype(f32) for n in range(blocks)], axis=1)
+    for k in range(1, planes):
+        a = a + z_a[(z + k) % planes].astype(f32)
+        b = b + z_b[(z + k) % planes].astype(f32)
     half = a.shape[1] // 384
     width = 256 * half
     for i, part in enumerate((a, b)):
@@ -399,20 +415,20 @@
     out_ref[:, 3 * width :] = b[:, 384 * half :]
 
 
-def call(kernel, outs, operands, specs=None, scratch=(), flops=10**6, limit=12):
+def call(kernel, outs, operands, specs=None, scratch=(), limit=12, final=False):
     specs = list(specs or ())
     specs += [pltpu.VMEM] * (len(operands) - len(specs))
     operands = [
-        pltpu.with_memory_space_constraint(o, s) if s is pltpu.HBM else o
+        pltpu.with_memory_space_constraint(o, s) if s in (pltpu.HBM, pltpu.VMEM) else o
         for o, s in zip(operands, specs)
     ]
     return pl.pallas_call(
         kernel,
-        out_shape=[jax.ShapeDtypeStruct(*o) for o in outs],
+        out_shape=[jax.ShapeDtypeStruct(*o) if final else pltpu.VMEM(*o) for o in outs],
         in_specs=[pl.BlockSpec(memory_space=s) for s in specs],
         scratch_shapes=list(scratch),
         compiler_params=pltpu.CompilerParams(vmem_limit_bytes=limit * MIB),
-        cost_estimate=pl.CostEstimate(flops=flops, bytes_accessed=10**4, transcendentals=0),
+        cost_estimate=pl.CostEstimate(flops=10**6, bytes_accessed=10**4, transcendentals=0),
     )(*operands)
 
 
@@ -429,46 +445,47 @@
     three = ((members, 3, slots, width), bf16)
     one = ((members, 1, slots, width), bf16)
 
-    to_plus, to_minus, own_right, own_left, x = call(
-        functools.partial(gather_kernel, slots),
+    place = me.reshape(1)
+    trio = pltpu.VMEM((2, *three[0]), bf16)
+    *outgoing, own_right, own_left, x = call(
+        functools.partial(gather_kernel, slots, row_width),
         [three, three, one, one, (node_features.shape, bf16)],
-        (send_rows, node_features),
-        specs=[pltpu.HBM] * 2,
-        scratch=[pltpu.VMEM(send_rows.shape, jnp.int32), pltpu.SemaphoreType.DMA((2,))],
-    )
-    plus = shifted(to_plus, row_width)
-    minus = shifted(to_minus, -row_width)
+        (place, send_rows, node_features),
+        specs=[pltpu.SMEM] + [pltpu.HBM] * 2,
+        scratch=[pltpu.VMEM(send_rows.shape, jnp.int32), trio, pltpu.SemaphoreType.DMA((2,))],
+    )
+    arrived = swap(outgoing, row_width)
     square = ((width, width), bf16)
-    *loc, xt, wq, wk, wv, og = call(
+    counts = neighbour_count.reshape(1, node_rows)
+    *loc, xt, wq, wk, wv, og, neigh, counts = call(
         functools.partial(local_kernel, groups),
         [((8, members, node_rows, 128), bf16)] * groups
-        + [((members, width, node_rows), bf16), square, square, square, (out_grad.shape, bf16)],
-        (own_right, x, w_query, w_key, w_value, out_grad, w_out),
-        specs=[pl.ANY, pltpu.VMEM] + [pltpu.HBM] * 5,
-        scratch=[pltpu.VMEM((width, width), bf16), pltpu.SemaphoreType.DMA((5,))],
+        + [((members, width, node_rows), bf16), square, square, square, (out_grad.shape, bf16)]
+        + [(neighbours.shape, jnp.int32), (counts.shape, jnp.int32)],
+        (own_right, x, w_query, w_key, w_value, out_grad, neighbours, counts, w_out),
+        specs=[pl.ANY, pltpu.VMEM] + [pltpu.HBM] * 7,
+        scratch=[pltpu.VMEM((width, width), bf16), pltpu.SemaphoreType.DMA((7,))],
         limit=16,
     )
-    to_right, to_left = call(
-        relay_kernel, [three, three], (loc[0], own_right, own_left, plus, minus), specs=[pl.ANY]
-    )
-    right = shifted(to_right, 1)
-    left = shifted(to_left, -1)
+    *outgoing, plus, minus = call(
+        functools.partial(relay_kernel, row_width), [three, three, one, one],
+        (place, loc[0], own_right, own_left, *arrived), specs=[pltpu.SMEM, pl.ANY],
+        scratch=[trio, trio],
+    )
+    arrived = swap(outgoing, 1)
     (mask,) = call(
-        mask_kernel, [((table, node_rows), f32)],
-        (to_right, neighbours, neighbour_count.reshape(1, node_rows)),
-        specs=[pl.ANY],
+        mask_kernel, [((table, node_rows), f32)], (outgoing[0], neigh, counts), specs=[pl.ANY]
     )
     *halo, xtf = call(
         halo_kernel,
         [((4, members, node_rows, 128), bf16)] * groups + [((members, width, table), bf16)],
-        (plus, minus, right, left, xt, wk, wv),
+        (place, plus, minus, *arrived, xt, wk, wv), specs=[pltpu.SMEM], scratch=[trio],
     )
 
     planes, rows = count // 4, width // count
     inner_planes = planes * 128 // width
     flip = [(i, i ^ 1) for i in range(count)]
     flop = [(i, i ^ 2) for i in range(count)]
-    place = me.reshape(1)
     grads = []
 
     def attention(extra, which):
@@ -498,10 +515,8 @@
         return own, other, lax.ppermute(send_other, "patch", flip), lax.ppermute(send_own, "patch", flip)
 
     def along_z(sent):
-        return [
-            lax.ppermute(s, "patch", [(i, (i + 4 * k) % count) for i in range(count)])
-            for k, s in enumerate(sent, 1)
-        ]
+        lines = [[w + 4 * z for z in range(planes)] for w in range(4)]
+        return lax.all_to_all(sent, "patch", 0, 0, axis_index_groups=lines, tiled=True)
 
     half = groups // 2
     wide = 384 * half
@@ -512,44 +527,40 @@
     for g in range(half, groups):
         later.append(attention((y_sent,) if g == groups - 1 else (), range(g, g + 1)))
     own_b, other_b, core_other_b, core_own_b = zip(*later)
-    y_sent, own_a, out_a, *sent = call(
+    y_sent, own_a, out_a, sent = call(
         functools.partial(first_kernel, len(later)),
         [(y_sent.shape, bf16), ((rows, wide), f32), ((half * inner_planes, rows, width), f32)]
-        + [((rows, wide), bf16)] * (planes - 1),
-        (*other_b, *core_other_b, own_a, core_own, y_a),
+        + [((planes, rows, wide), bf16)],
+        (place, *other_b, *core_other_b, own_a, core_own, y_a), specs=[pltpu.SMEM],
     )
     y_b = lax.ppermute(y_sent, "patch", flop)
-    node, back_left, back_right, back_minus, back_plus = call(
-        functools.partial(node_kernel, groups, planes),
+    z_a = along_z(sent)
+    node, *outgoing, back_plus, back_minus = call(
+        functools.partial(node_kernel, groups, 2),
         [((members, node_rows, width), f32), three, three, one, one],
-        (y_sent, *sent, *grads[0::3], *grads[1::3], *grads[2::3], wq, wk, wv),
-        specs=[pl.ANY] * planes,
-    )
-    from_right = shifted(back_left, -1)
-    from_left = shifted(back_right, 1)
-    z_a = along_z(sent)
-    near = (row_width // 4, planes - row_width // 4)
-    blocks = (wide + width) // 256
-    more = members * 6 * slots // rows
-    own_b, *sent = call(
-        functools.partial(second_kernel, planes, len(later), near),
-        [((rows, wide + width), f32)]
-        + [((blocks + (more if k in near else 0), rows, 256), bf16) for k in range(1, planes)],
+        (place, y_sent, sent, *grads[0::3], *grads[1::3], *grads[2::3], wq, wk, wv),
+        specs=[pltpu.SMEM] + [pl.ANY] * 2, scratch=[trio],
+    )
+    back = swap(outgoing, 1)
+    own_b, sent, *outgoing = call(
+        functools.partial(second_kernel, 2, len(later), row_width),
+        [((rows, wide + width), f32), ((planes, rows, wide + width), bf16), three, three],
         (
-            place, node, *z_a, out_a, back_plus, back_minus, from_right, from_left, y_b,
-            *own_b, *core_own_b,
+            place, node, z_a, out_a, back_plus, back_minus, *back, y_b, *own_b, *core_own_b,
         ),
-        specs=[pltpu.SMEM] + [pl.ANY] * planes,
-        scratch=[pltpu.VMEM((planes, rows, width), f32)],
+        specs=[pltpu.SMEM] + [pl.ANY] * 2,
+        scratch=[pltpu.VMEM((planes, rows, width), f32), trio, trio],
     )
     z_b = along_z(sent)
+    home = swap(outgoing, row_width)
     (node_grad,) = call(
-        functools.partial(finish_kernel, blocks), [((members, node_rows, width), bf16)],
-        (send_rows, node, from_right, from_left, z_b[near[0] - 1], z_b[near[1] - 1]),
+        functools.partial(finish_kernel, row_width), [((members, node_rows, width), bf16)],
+        (place, send_rows, node, *back, *home), specs=[pltpu.SMEM], scratch=[trio, trio],
+        final=True,
     )
     (weight_grad,) = call(
-        functools.partial(weight_kernel, planes), [((rows, 4 * width), f32)],
-        (node_grad, own_a, own_b, *z_a, *z_b), specs=[pl.ANY],
+        weight_kernel, [((rows, 4 * width), f32)],
+        (place, node_grad, own_a, own_b, z_a, z_b), specs=[pltpu.SMEM, pl.ANY], final=True,
     )
     return (node_grad, weight_grad)
 

time: 62.6 us -> 84.3 us (1.35)
  local copies, waits for them, and re-layouts: 2.71 us -> 19.1 us
  starting transfers between devices: 24.2 us -> 26.9 us
  Pallas kernels: 17 us -> 18.2 us
    unnamed x20 -> x68, local copies, waits for them, and re-layouts: 2.71 us -> 19.1 us
    all_to_all x0 -> x2, starting transfers between devices: none -> 7.46 us  [along_z(): lax.all_to_all(sent, 'patch', 0, 0, axis_index_groups=lines, tiled=True)]
    ppermute x12 -> x8, starting transfers between devices: 21.2 us -> 16.7 us  [swap(): lax.ppermute(shard, 'patch', perm)]
    ppermute x12 -> x8, waiting for transfers between devices: 12.8 us -> 15.6 us  [swap(): lax.ppermute(shard, 'patch', perm)]
    ppermute x1, waiting for transfers between devices: 2.92 us -> 0.77 us  [body(): y_a = lax.ppermute(y_sent, 'patch', flop)]
    pallas_call x13, Pallas kernels: 17 us -> 18.2 us  [call(): pl.pallas_call(kernel, out_shape=[jax.ShapeDtypeStruct(*o) if final else...]
  transfers between devices with their start and end apart: 20 -> 18, of which waited for: 10 -> 8; matrix products, arithmetic and copies ran while one was open for 0% -> 0% of each run, Pallas kernels for 15% -> 13%
where the time goes in v4:
time: 84.3 us; the launch traced here: 83.5 us
  starting transfers between devices  26.9 us (32%)
  local copies, waits for them, and re-layouts  19.1 us (23%)
  waiting for transfers between devices  18.4 us (22%)
  Pallas kernels  18.2 us (22%)
  between operations  0.87 us (1%)
    unnamed x68, local copies, waits for them, and re-layouts  19.1 us
    pallas_call x13, Pallas kernels, call(): pl.pallas_call(kernel, out_shape=[jax.ShapeDtypeStruct(*o) if final else...  18.2 us
    ppermute x8, starting transfers between devices, swap(): lax.ppermute(shard, 'patch', perm)  16.7 us
    ppermute x8, waiting for transfers between devices, swap(): lax.ppermute(shard, 'patch', perm)  15.6 us
    all_to_all x2, starting transfers between devices, along_z(): lax.all_to_all(sent, 'patch', 0, 0, axis_index_groups=lines, tiled=True)  7.46 us
    ppermute x3, waiting for transfers between devices, attention(): lax.ppermute(send_other, 'patch', flip)  2.01 us
  transfers between devices with their start and end apart: 18, of which 8 were waited for; matrix products, arithmetic and copies ran while one was open for 0% of the time, Pallas kernels for 13%

profile of v4, /device:TPU:0, one launch (start us, length us, event | category | flops | bytes accessed | tf_op | source)
XLA Modules:
  0.0 83.5 jit_solution(3636783469468265927)
XLA Ops:
  0.6 1.2 %shard_map.104 = (bf16[2,3,16,512]{3,2,1,0:T(8,128)(2,1)S(1)}, bf16[2,3,16,512]{3,2,1,0:T(8,128)(2,1)S(1)}, bf16[2,1,16,512]{3,2,1,0:T(8,128)(2,1)S(1)}, bf16[2,...) custom-call(s32[1]{0:T(128)} %bitcast.me_ref, s32[1,8,16]{2,1,0:T(8,128)} %send_ref.1, bf16[2,128,512]{2,1,0:T(8,128)(2,1)} %x_hbm.1), custom_call_target="tpu_custom_call" | custom-call | flops 1000000 | bytes 10000 | tf_op jit(solution)/shard_map/pallas_call | solution.py:425
  1.9 3.1 %collective-permute-start = (bf16[2,3,16,512]{3,2,1,0:T(8,128)(2,1)S(1)}, bf16[2,3,16,512]{3,2,1,0:T(8,128)(2,1)S(1)}, u32[]{:S(2)}, u32[]{:S(2)}) collective-permute-start(bf16[2,3,16,512]{3,2,1,0:T(8,128)(2,1)S(1)} %get-tuple-element.69), channel_id=1, source_target_pairs={{0,4},{1,5},{2,6},{3,7},{4,0},{5,1},{6,2},{7,3},{8,12},{9,13},{10,... | collective-permute-start | bytes 294920 | tf_op jit(solution)/shard_map/ppermute | solution.py:38
  4.9 2.5 %collective-permute-start.1 = (bf16[2,3,16,512]{3,2,1,0:T(8,128)(2,1)S(1)}, bf16[2,3,16,512]{3,2,1,0:T(8,128)(2,1)S(1)}, u32[]{:S(2)}, u32[]{:S(2)}) collective-permute-start(bf16[2,3,16,512]{3,2,1,0:T(8,128)(2,1)S(1)} %get-tuple-element.70), channel_id=1, source_target_pairs={{0,12},{1,13},{2,14},{3,15},{4,8},{5,9},{6,10},{7,11},{8,4},{9,5},... | collective-permute-start | bytes 294920 | tf_op jit(solution)/shard_map/ppermute | solution.py:38
  7.4 2.6 %shard_map.105 = (bf16[8,2,128,128]{3,2,1,0:T(8,128)(2,1)S(1)}, bf16[8,2,128,128]{3,2,1,0:T(8,128)(2,1)S(1)}, bf16[8,2,128,128]{3,2,1,0:T(8,128)(2,1)S(1)}, bf16...) custom-call(bf16[2,1,16,512]{3,2,1,0:T(8,128)(2,1)S(1)} %get-tuple-e, ...), custom_call_target="tpu_custom_call" | custom-call | flops 1000000 | bytes 10000 | tf_op jit(solution)/shard_map/pallas_call | solution.py:425
  10.1 2.0 %collective-permute-done.1.second_in = bf16[2,3,16,512]{3,2,1,0:T(8,128)(2,1)S(1)} collective-permute-done((bf16[2,3,16,512]{3,2,1,0:T(8,128)(2,1)S(1)}, bf16[2,3,16,512]{3,2,1,0:T(8,128)(2,1)S(1)}, u32[]{:S(2)}, u32[]{:S(2)}) %collective-permute-start.1) | collective-permute-done | bytes 98336 | tf_op jit(solution)/shard_map/ppermute | solution.py:38
  12.2 2.8 %collective-permute-start.3 = (bf16[2,3,16,512]{3,2,1,0:T(8,128)(2,1)S(1)}, bf16[2,3,16,512]{3,2,1,0:T(8,128)(2,1)S(1)}, u32[]{:S(2)}, u32[]{:S(2)}) collective-permute-start(bf16[2,3,16,512]{3,2,1,0:T(8,128)(2,1)S(1)} %get-tuple-element.74), channel_id=1, source_target_pairs={{0,15},{1,2},{2,1},{3,4},{4,3},{5,6},{6,5},{7,8},{8,7},{9,10},{10,... | collective-permute-start | bytes 294920 | tf_op jit(solution)/shard_map/ppermute | solution.py:38
  15.1 1.4 %shard_map.108.refs_2_.refs_4_.refs_3_ = f32[256,128]{1,0:T(8,128)S(1)} custom-call(bf16[2,3,16,512]{3,2,1,0:T(8,128)(2,1)S(1)} %get-tuple-element.73.after_ref, s32[128,256]{1,0:T(8,128)S(1)} %get-tuple-element.79.neigh_ref, s32[1,128]{1,0:T(1,128)S(1)} %get-tuple-element.80.count_ref), custom_call_target="tpu_custom_call" | custom-call | flops 1000000 | bytes 10000 | tf_op jit(solution)/shard_map/pallas_call | solution.py:425
  16.5 2.5 %collective-permute-done.3.second_in = bf16[2,3,16,512]{3,2,1,0:T(8,128)(2,1)S(1)} collective-permute-done((bf16[2,3,16,512]{3,2,1,0:T(8,128)(2,1)S(1)}, bf16[2,3,16,512]{3,2,1,0:T(8,128)(2,1)S(1)}, u32[]{:S(2)}, u32[]{:S(2)}) %collective-permute-start.3) | collective-permute-done | bytes 98336 | tf_op jit(solution)/shard_map/ppermute | solution.py:38
  19.7 3.1 %shard_map.110 = (f32[4,32,1024]{2,1,0:T(8,128)S(1)}, f32[4,32,1024]{2,1,0:T(8,128)S(1)}, bf16[4,32,1024]{2,1,0:T(8,128)(2,1)S(1)}, bf16[4,32,1024]{2,1,0:T(8,12...) custom-call(s32[1]{0:T(128)} %bitcast.me_ref, ...), custom_call_target="tpu_custom_call" | custom-call | flops 1000000 | bytes 10000 | tf_op jit(solution)/shard_map/pallas_call | solution.py:425
  23.4 1.0 %collective-permute-done.4 = bf16[4,32,1024]{2,1,0:T(8,128)(2,1)S(1)} collective-permute-done((bf16[4,32,1024]{2,1,0:T(8,128)(2,1)S(1)}, bf16[4,32,1024]{2,1,0:T(8,128)(2,1)S(1)}, u32[]{:S(2)}, u32[]{:S(2)}) %collective-permute-start.4) | collective-permute-done | bytes 262176 | tf_op jit(solution)/shard_map/ppermute | solution.py:515
  24.6 2.4 %shard_map.109 = (f32[4,32,512]{2,1,0:T(8,128)S(1)}, f32[4,32,512]{2,1,0:T(8,128)S(1)}, bf16[4,32,512]{2,1,0:T(8,128)(2,1)S(1)}, bf16[4,32,512]{2,1,0:T(8,128)(2...) custom-call(s32[1]{0:T(128)} %bitcast.me_ref, ...), custom_call_target="tpu_custom_call" | custom-call | flops 1000000 | bytes 10000 | tf_op jit(solution)/shard_map/pallas_call | solution.py:425
  27.0 0.6 copy-done.9
  28.4 2.3 %shard_map.111 = (f32[4,32,512]{2,1,0:T(8,128)S(1)}, f32[4,32,512]{2,1,0:T(8,128)S(1)}, bf16[4,32,512]{2,1,0:T(8,128)(2,1)S(1)}, bf16[4,32,512]{2,1,0:T(8,128)(2...) custom-call(s32[1]{0:T(128)} %bitcast.me_ref, ...), custom_call_target="tpu_custom_call" | custom-call | flops 1000000 | bytes 10000 | tf_op jit(solution)/shard_map/pallas_call | solution.py:425
  31.2 1.0 %collective-permute-done.6.refs_3_ = bf16[4,32,512]{2,1,0:T(8,128)(2,1)S(1)} collective-permute-done((bf16[4,32,512]{2,1,0:T(8,128)(2,1)S(1)}, bf16[4,32,512]{2,1,0:T(8,128)(2,1)S(1)}, u32[]{:S(2)}, u32[]{:S(2)}) %collective-permute-start.6) | collective-permute-done | bytes 131104 | tf_op jit(solution)/shard_map/ppermute | solution.py:515
  32.2 0.8 collective-permute-done.8.refs_6_
  33.0 0.8 shard_map.112
  33.7 0.6 copy-done.7
  35.0 3.9 %all-to-all-start = ((bf16[4,32,768]{2,1,0:T(8,128)(2,1)}), bf16[4,32,768]{2,1,0:T(8,128)(2,1)S(1)}, u32[]{:S(2)}, u32[]{:S(2)}) async-start(bf16[4,32,768]{2,1,0:T(8,128)(2,1)} %get-tuple-element.97.refs_1_), calls=%async_computation | async-start | bytes 393216 | tf_op jit(solution)/shard_map/all_to_all | solution.py:519
  38.9 1.0 %collective-permute-start.11 = (bf16[4,32,1024]{2,1,0:T(8,128)(2,1)S(1)}, bf16[4,32,1024]{2,1,0:T(8,128)(2,1)S(1)}, u32[]{:S(2)}, u32[]{:S(2)}) collective-permute-start(bf16[4,32,1024]{2,1,0:T(8,128)(2,1)S(1)} %get-tuple-element.96.refs_0_), channel_id=1, source_target_pairs={{0,2},{1,3},{2,0},{3,1},{4,6},{5,7},{6,4},{7,5},{8,10},{9,11},{10,... | collective-permute-start | bytes 786440 | tf_op jit(solution)/shard_map/ppermute | solution.py:536
  40.4 0.9 %copy-done.2 = bf16[2,256,128]{2,1,0:T(8,128)(2,1)S(1)} copy-done((bf16[2,256,128]{2,1,0:T(8,128)(2,1)S(1)}, bf16[2,256,128]{2,1,0:T(8,128)(2,1)}, u32[]{:S(2)}) %copy-start.2) | copy-done | bytes 131096
  41.3 0.9 %copy-done.4 = bf16[2,256,128]{2,1,0:T(8,128)(2,1)S(1)} copy-done((bf16[2,256,128]{2,1,0:T(8,128)(2,1)S(1)}, bf16[2,256,128]{2,1,0:T(8,128)(2,1)}, u32[]{:S(2)}) %copy-start.4) | copy-done | bytes 131096
  42.2 0.9 %copy-done.6 = bf16[2,256,128]{2,1,0:T(8,128)(2,1)S(1)} copy-done((bf16[2,256,128]{2,1,0:T(8,128)(2,1)S(1)}, bf16[2,256,128]{2,1,0:T(8,128)(2,1)}, u32[]{:S(2)}) %copy-start.6) | copy-done | bytes 131096
  43.1 0.9 %copy-done.10 = bf16[2,256,128]{2,1,0:T(8,128)(2,1)S(1)} copy-done((bf16[2,256,128]{2,1,0:T(8,128)(2,1)S(1)}, bf16[2,256,128]{2,1,0:T(8,128)(2,1)}, u32[]{:S(2)}) %copy-start.10) | copy-done | bytes 131096
  44.0 0.9 %copy-done.12 = bf16[2,256,128]{2,1,0:T(8,128)(2,1)S(1)} copy-done((bf16[2,256,128]{2,1,0:T(8,128)(2,1)S(1)}, bf16[2,256,128]{2,1,0:T(8,128)(2,1)}, u32[]{:S(2)}) %copy-start.12) | copy-done | bytes 131096
  44.9 0.9 %copy-done.14 = bf16[2,256,128]{2,1,0:T(8,128)(2,1)S(1)} copy-done((bf16[2,256,128]{2,1,0:T(8,128)(2,1)S(1)}, bf16[2,256,128]{2,1,0:T(8,128)(2,1)}, u32[]{:S(2)}) %copy-start.14) | copy-done | bytes 131096
  45.8 0.9 %copy-done.16 = bf16[2,256,128]{2,1,0:T(8,128)(2,1)S(1)} copy-done((bf16[2,256,128]{2,1,0:T(8,128)(2,1)S(1)}, bf16[2,256,128]{2,1,0:T(8,128)(2,1)}, u32[]{:S(2)}) %copy-start.16) | copy-done | bytes 131096
  46.7 0.8 %copy-done.24 = bf16[2,128,128]{2,1,0:T(8,128)(2,1)S(1)} copy-done((bf16[2,128,128]{2,1,0:T(8,128)(2,1)S(1)}, bf16[2,128,128]{2,1,0:T(8,128)(2,1)}, u32[]{:S(2)}) %copy-start.24) | copy-done | bytes 65560
  47.6 0.8 %copy-done.26 = bf16[2,128,128]{2,1,0:T(8,128)(2,1)S(1)} copy-done((bf16[2,128,128]{2,1,0:T(8,128)(2,1)S(1)}, bf16[2,128,128]{2,1,0:T(8,128)(2,1)}, u32[]{:S(2)}) %copy-start.26) | copy-done | bytes 65560
  48.4 0.8 %copy-done.28 = bf16[2,128,128]{2,1,0:T(8,128)(2,1)S(1)} copy-done((bf16[2,128,128]{2,1,0:T(8,128)(2,1)S(1)}, bf16[2,128,128]{2,1,0:T(8,128)(2,1)}, u32[]{:S(2)}) %copy-start.28) | copy-done | bytes 65560
  49.3 1.0 %shard_map.113 = (f32[2,128,512]{2,1,0:T(8,128)S(1)}, bf16[2,3,16,512]{3,2,1,0:T(8,128)(2,1)S(1)}, bf16[2,3,16,512]{3,2,1,0:T(8,128)(2,1)S(1)}, bf16[2,1,16,512]...) custom-call(s32[1]{0:T(128)} %bitcast.me_ref, bf16[4,32,1024]{2,1,0:T(8,128)(2,1)S(1)} %get-tuple-element.96.refs_0_, ...), custom_call_target="tpu_custom_call" | custom-call | flops 1000000 | bytes 10000 | tf_op jit(solution)/shard_map/pallas_call | solution.py:425
  51.5 3.9 %collective-permute-start.10 = (bf16[2,3,16,512]{3,2,1,0:T(8,128)(2,1)S(1)}, bf16[2,3,16,512]{3,2,1,0:T(8,128)(2,1)S(1)}, u32[]{:S(2)}, u32[]{:S(2)}) collective-permute-start(bf16[2,3,16,512]{3,2,1,0:T(8,128)(2,1)S(1)} %get-tuple-element.113), channel_id=1, source_target_pairs={{0,15},{1,2},{2,1},{3,4},{4,3},{5,6},{6,5},{7,8},{8,7},{9,10},{10,... | collective-permute-start | bytes 294920 | tf_op jit(solution)/shard_map/ppermute | solution.py:38
  55.4 0.7 copy-done.17
  56.1 0.6 copy-done.19
  56.7 1.5 %collective-permute-done.10.refs_6_.second_in = bf16[2,3,16,512]{3,2,1,0:T(8,128)(2,1)S(1)} collective-permute-done((bf16[2,3,16,512]{3,2,1,0:T(8,128)(2,1)S(1)}, bf16[2,3,16,512]{3,2,1,0:T(8,128)(2,1)S(1)}, u32[]{:S(2)}, u32[]{:S(2)}) %collective-permute-start.10) | collective-permute-done | bytes 98336 | tf_op jit(solution)/shard_map/ppermute | solution.py:38
  58.3 0.9 %copy-done.8 = f32[2,32,512]{2,1,0:T(8,128)S(1)} copy-done((f32[2,32,512]{2,1,0:T(8,128)S(1)}, f32[2,32,512]{2,1,0:T(8,128)}, u32[]{:S(2)}) %copy-start.8) | copy-done | bytes 131096
  59.2 0.9 %copy-done.18 = bf16[4,32,512]{2,1,0:T(8,128)(2,1)S(1)} copy-done((bf16[4,32,512]{2,1,0:T(8,128)(2,1)S(1)}, bf16[4,32,512]{2,1,0:T(8,128)(2,1)}, u32[]{:S(2)}) %copy-start.18) | copy-done | bytes 131096
  60.1 0.9 %copy-done.20 = bf16[4,32,512]{2,1,0:T(8,128)(2,1)S(1)} copy-done((bf16[4,32,512]{2,1,0:T(8,128)(2,1)S(1)}, bf16[4,32,512]{2,1,0:T(8,128)(2,1)}, u32[]{:S(2)}) %copy-start.20) | copy-done | bytes 131096
  61.0 0.8 copy-done.30
  61.7 0.8 copy-done.32
  62.5 0.9 %shard_map.114 = (f32[32,1280]{1,0:T(8,128)S(1)}, bf16[4,32,1280]{2,1,0:T(8,128)(2,1)}, bf16[2,3,16,512]{3,2,1,0:T(8,128)(2,1)S(1)}, bf16[2,3,16,512]{3,2,1,0:T(8,128)(2,1)S(1)}) custom-call(s32[1]{0:T(128)} %bitcast.me_ref, f32[2,128,512]{2,1,0:T(8,128)S(1)} %get-tuple-element.111.refs_0_.node_ref, bf16[4,32,768]{2,1,0:T(8,128)(2,1)S(1)} %all-to-all-done.refs_1_.z_a, ...), custom_call_target="tpu_custom_call" | custom-call | flops 1000000 | bytes 10000 | tf_op jit(solution)/shard_map/pallas_call | solution.py:425
  63.4 3.6 %all-to-all-start.1 = ((bf16[4,32,1280]{2,1,0:T(8,128)(2,1)}), bf16[4,32,1280]{2,1,0:T(8,128)(2,1)S(1)}, u32[]{:S(2)}, u32[]{:S(2)}) async-start(bf16[4,32,1280]{2,1,0:T(8,128)(2,1)} %get-tuple-element.125), calls=%async_computation.1 | async-start | bytes 655360 | tf_op jit(solution)/shard_map/all_to_all | solution.py:519
  67.0 2.0 %collective-permute-start.14 = (bf16[2,3,16,512]{3,2,1,0:T(8,128)(2,1)S(1)}, bf16[2,3,16,512]{3,2,1,0:T(8,128)(2,1)S(1)}, u32[]{:S(2)}, u32[]{:S(2)}) collective-permute-start(bf16[2,3,16,512]{3,2,1,0:T(8,128)(2,1)S(1)} %get-tuple-element.121), channel_id=1, source_target_pairs={{0,4},{1,5},{2,6},{3,7},{4,0},{5,1},{6,2},{7,3},{8,12},{9,13},{10,... | collective-permute-start | bytes 294920 | tf_op jit(solution)/shard_map/ppermute | solution.py:38
  69.0 2.4 %collective-permute-start.15 = (bf16[2,3,16,512]{3,2,1,0:T(8,128)(2,1)S(1)}, bf16[2,3,16,512]{3,2,1,0:T(8,128)(2,1)S(1)}, u32[]{:S(2)}, u32[]{:S(2)}) collective-permute-start(bf16[2,3,16,512]{3,2,1,0:T(8,128)(2,1)S(1)} %get-tuple-element.122), channel_id=1, source_target_pairs={{0,12},{1,13},{2,14},{3,15},{4,8},{5,9},{6,10},{7,11},{8,4},{9,5},... | collective-permute-start | bytes 294920 | tf_op jit(solution)/shard_map/ppermute | solution.py:38
  71.3 4.8 %collective-permute-done.14.home_first = bf16[2,3,16,512]{3,2,1,0:T(8,128)(2,1)S(1)} collective-permute-done((bf16[2,3,16,512]{3,2,1,0:T(8,128)(2,1)S(1)}, bf16[2,3,16,512]{3,2,1,0:T(8,128)(2,1)S(1)}, u32[]{:S(2)}, u32[]{:S(2)}) %collective-permute-start.14) | collective-permute-done | bytes 98336 | tf_op jit(solution)/shard_map/ppermute | solution.py:38
  76.1 4.7 %collective-permute-done.15.home_second = bf16[2,3,16,512]{3,2,1,0:T(8,128)(2,1)S(1)} collective-permute-done((bf16[2,3,16,512]{3,2,1,0:T(8,128)(2,1)S(1)}, bf16[2,3,16,512]{3,2,1,0:T(8,128)(2,1)S(1)}, u32[]{:S(2)}, u32[]{:S(2)}) %collective-permute-start.15) | collective-permute-done | bytes 98336 | tf_op jit(solution)/shard_map/ppermute | solution.py:38
  80.8 1.0 %shard_map.115.after_ref = bf16[2,128,512]{2,1,0:T(8,128)(2,1)} custom-call(s32[1]{0:T(128)} %bitcast.me_ref, s32[1,8,16]{2,1,0:T(8,128)S(1)} %copy-done.33, f32[2,128,512]{2,1,0:T(8,128)S(1)} %get-tuple-element.111.refs_0_.node_ref, bf16[2,3,16,512]{3,2,1,0:T(8,128)(2,1)S(1)} %collective-permute-done.9.refs_5_.first_in, ...), custom_call_target="tpu_custom_call" | custom-call | flops 1000000 | bytes 10000 | tf_op jit(solution)/shard_map/pallas_call | solution.py:425
  81.8 0.9 %copy-done = bf16[2,128,512]{2,1,0:T(8,128)(2,1)S(1)} copy-done((bf16[2,128,512]{2,1,0:T(8,128)(2,1)S(1)}, bf16[2,128,512]{2,1,0:T(8,128)(2,1)}, u32[]{:S(2)}) %copy-start) | copy-done | bytes 262168
  82.8 0.8 shard_map.116
  (70 shorter events, 5.1 us)
Async XLA Ops:
  1.9 8.2 %collective-permute-start = (bf16[2,3,16,512]{3,2,1,0:T(8,128)(2,1)S(1)}, bf16[2,3,16,512]{3,2,1,0:T(8,128)(2,1)S(1)}, u32[]{:S(2)}, u32[]{:S(2)}) collective-permute-start(bf16[2,3,16,512]{3,2,1,0:T(8,128)(2,1)S(1)} %get-tuple-element.69), channel_id=1, source_target_pairs={{0,4},{1,5},{2,6},{3,7},{4,0},{5,1},{6,2},{7,3},{8,12},{9,13},{10,... | collective-permute-start | bytes 294920 | tf_op jit(solution)/shard_map/ppermute | solution.py:38
  4.9 7.2 %collective-permute-start.1 = (bf16[2,3,16,512]{3,2,1,0:T(8,128)(2,1)S(1)}, bf16[2,3,16,512]{3,2,1,0:T(8,128)(2,1)S(1)}, u32[]{:S(2)}, u32[]{:S(2)}) collective-permute-start(bf16[2,3,16,512]{3,2,1,0:T(8,128)(2,1)S(1)} %get-tuple-element.70), channel_id=1, source_target_pairs={{0,12},{1,13},{2,14},{3,15},{4,8},{5,9},{6,10},{7,11},{8,4},{9,5},... | collective-permute-start | bytes 294920 | tf_op jit(solution)/shard_map/ppermute | solution.py:38
  12.2 4.4 %collective-permute-start.2 = (bf16[2,3,16,512]{3,2,1,0:T(8,128)(2,1)S(1)}, bf16[2,3,16,512]{3,2,1,0:T(8,128)(2,1)S(1)}, u32[]{:S(2)}, u32[]{:S(2)}) collective-permute-start(bf16[2,3,16,512]{3,2,1,0:T(8,128)(2,1)S(1)} %get-tuple-element.73.after_ref), channel_id=1, source_target_pairs={{0,1},{1,0},{2,3},{3,2},{4,5},{5,4},{6,7},{7,6},{8,9},{9,8},{10,11... | collective-permute-start | bytes 294920 | tf_op jit(solution)/shard_map/ppermute | solution.py:38
  12.2 6.8 %collective-permute-start.3 = (bf16[2,3,16,512]{3,2,1,0:T(8,128)(2,1)S(1)}, bf16[2,3,16,512]{3,2,1,0:T(8,128)(2,1)S(1)}, u32[]{:S(2)}, u32[]{:S(2)}) collective-permute-start(bf16[2,3,16,512]{3,2,1,0:T(8,128)(2,1)S(1)} %get-tuple-element.74), channel_id=1, source_target_pairs={{0,15},{1,2},{2,1},{3,4},{4,3},{5,6},{6,5},{7,8},{8,7},{9,10},{10,... | collective-permute-start | bytes 294920 | tf_op jit(solution)/shard_map/ppermute | solution.py:38
  22.8 1.7 %copy-start.1 = (bf16[2,256,128]{2,1,0:T(8,128)(2,1)}, bf16[2,256,128]{2,1,0:T(8,128)(2,1)S(1)}, u32[]{:S(2)}) copy-start(bf16[2,256,128]{2,1,0:T(8,128)(2,1)S(1)} %get-tuple-element.106.refs_10_) | copy-start | bytes 393220
  22.8 1.7 %copy-start.3 = (bf16[2,256,128]{2,1,0:T(8,128)(2,1)}, bf16[2,256,128]{2,1,0:T(8,128)(2,1)S(1)}, u32[]{:S(2)}) copy-start(bf16[2,256,128]{2,1,0:T(8,128)(2,1)S(1)} %get-tuple-element.103.refs_7_) | copy-start | bytes 393220
  22.8 1.7 %copy-start.5 = (bf16[2,256,128]{2,1,0:T(8,128)(2,1)}, bf16[2,256,128]{2,1,0:T(8,128)(2,1)S(1)}, u32[]{:S(2)}) copy-start(bf16[2,256,128]{2,1,0:T(8,128)(2,1)S(1)} %get-tuple-element.107.refs_11_) | copy-start | bytes 393220
  22.8 1.7 %copy-start.23 = (bf16[2,128,128]{2,1,0:T(8,128)(2,1)}, bf16[2,128,128]{2,1,0:T(8,128)(2,1)S(1)}, u32[]{:S(2)}) copy-start(bf16[2,128,128]{2,1,0:T(8,128)(2,1)S(1)} %get-tuple-element.99.refs_3_) | copy-start | bytes 196612
  22.8 1.6 %collective-permute-start.4 = (bf16[4,32,1024]{2,1,0:T(8,128)(2,1)S(1)}, bf16[4,32,1024]{2,1,0:T(8,128)(2,1)S(1)}, u32[]{:S(2)}, u32[]{:S(2)}) collective-permute-start(bf16[4,32,1024]{2,1,0:T(8,128)(2,1)S(1)} %get-tuple-element.88), channel_id=1, source_target_pairs={{0,1},{1,0},{2,3},{3,2},{4,5},{5,4},{6,7},{7,6},{8,9},{9,8},{10,11... | collective-permute-start | bytes 786440 | tf_op jit(solution)/shard_map/ppermute | solution.py:515
  22.9 8.3 %collective-permute-start.7 = (bf16[4,32,1024]{2,1,0:T(8,128)(2,1)S(1)}, bf16[4,32,1024]{2,1,0:T(8,128)(2,1)S(1)}, u32[]{:S(2)}, u32[]{:S(2)}) collective-permute-start(bf16[4,32,1024]{2,1,0:T(8,128)(2,1)S(1)} %get-tuple-element.95), channel_id=1, source_target_pairs={{0,1},{1,0},{2,3},{3,2},{4,5},{5,4},{6,7},{7,6},{8,9},{9,8},{10,11... | collective-permute-start | bytes 786440 | tf_op jit(solution)/shard_map/ppermute | solution.py:515
  24.6 8.4 %collective-permute-start.8 = (bf16[4,32,1024]{2,1,0:T(8,128)(2,1)S(1)}, bf16[4,32,1024]{2,1,0:T(8,128)(2,1)S(1)}, u32[]{:S(2)}, u32[]{:S(2)}) collective-permute-start(bf16[4,32,1024]{2,1,0:T(8,128)(2,1)S(1)} %add_convert_fusion.refs_0_), channel_id=1, source_target_pairs={{0,2},{1,3},{2,0},{3,1},{4,6},{5,7},{6,4},{7,5},{8,10},{9,11},{10,... | collective-permute-start | bytes 786440 | tf_op jit(solution)/shard_map/ppermute | solution.py:525
  27.0 0.6 copy-start.9
  28.3 2.5 %copy-start.11 = (bf16[2,256,128]{2,1,0:T(8,128)(2,1)}, bf16[2,256,128]{2,1,0:T(8,128)(2,1)S(1)}, u32[]{:S(2)}) copy-start(bf16[2,256,128]{2,1,0:T(8,128)(2,1)S(1)} %get-tuple-element.108.refs_12_) | copy-start | bytes 393220
  28.3 2.9 %collective-permute-start.5 = (bf16[4,32,512]{2,1,0:T(8,128)(2,1)S(1)}, bf16[4,32,512]{2,1,0:T(8,128)(2,1)S(1)}, u32[]{:S(2)}, u32[]{:S(2)}) collective-permute-start(bf16[4,32,512]{2,1,0:T(8,128)(2,1)S(1)} %get-tuple-element.92), channel_id=1, source_target_pairs={{0,1},{1,0},{2,3},{3,2},{4,5},{5,4},{6,7},{7,6},{8,9},{9,8},{10,11... | collective-permute-start | bytes 393224 | tf_op jit(solution)/shard_map/ppermute | solution.py:515
  30.8 3.0 %copy-start.13 = (bf16[2,256,128]{2,1,0:T(8,128)(2,1)}, bf16[2,256,128]{2,1,0:T(8,128)(2,1)S(1)}, u32[]{:S(2)}) copy-start(bf16[2,256,128]{2,1,0:T(8,128)(2,1)S(1)} %get-tuple-element.105.refs_9_) | copy-start | bytes 393220
  30.8 3.0 %copy-start.15 = (bf16[2,256,128]{2,1,0:T(8,128)(2,1)}, bf16[2,256,128]{2,1,0:T(8,128)(2,1)S(1)}, u32[]{:S(2)}) copy-start(bf16[2,256,128]{2,1,0:T(8,128)(2,1)S(1)} %get-tuple-element.109.refs_13_) | copy-start | bytes 393220
  30.8 3.0 %copy-start.27 = (bf16[2,128,128]{2,1,0:T(8,128)(2,1)}, bf16[2,128,128]{2,1,0:T(8,128)(2,1)S(1)}, u32[]{:S(2)}) copy-start(bf16[2,128,128]{2,1,0:T(8,128)(2,1)S(1)} %get-tuple-element.101.refs_5_) | copy-start | bytes 196612
  30.8 1.4 %collective-permute-start.6 = (bf16[4,32,512]{2,1,0:T(8,128)(2,1)S(1)}, bf16[4,32,512]{2,1,0:T(8,128)(2,1)S(1)}, u32[]{:S(2)}, u32[]{:S(2)}) collective-permute-start(bf16[4,32,512]{2,1,0:T(8,128)(2,1)S(1)} %get-tuple-element.93), channel_id=1, source_target_pairs={{0,1},{1,0},{2,3},{3,2},{4,5},{5,4},{6,7},{7,6},{8,9},{9,8},{10,11... | collective-permute-start | bytes 393224 | tf_op jit(solution)/shard_map/ppermute | solution.py:515
  33.7 0.7 copy-start.7
  35.0 23.2 %all-to-all-start = ((bf16[4,32,768]{2,1,0:T(8,128)(2,1)}), bf16[4,32,768]{2,1,0:T(8,128)(2,1)S(1)}, u32[]{:S(2)}, u32[]{:S(2)}) async-start(bf16[4,32,768]{2,1,0:T(8,128)(2,1)} %get-tuple-element.97.refs_1_), calls=%async_computation | async-start | bytes 393216 | tf_op jit(solution)/shard_map/all_to_all | solution.py:519
  38.9 19.4 %collective-permute-start.11 = (bf16[4,32,1024]{2,1,0:T(8,128)(2,1)S(1)}, bf16[4,32,1024]{2,1,0:T(8,128)(2,1)S(1)}, u32[]{:S(2)}, u32[]{:S(2)}) collective-permute-start(bf16[4,32,1024]{2,1,0:T(8,128)(2,1)S(1)} %get-tuple-element.96.refs_0_), channel_id=1, source_target_pairs={{0,2},{1,3},{2,0},{3,1},{4,6},{5,7},{6,4},{7,5},{8,10},{9,11},{10,... | collective-permute-start | bytes 786440 | tf_op jit(solution)/shard_map/ppermute | solution.py:536
  39.9 15.5 %collective-permute-start.12 = (bf16[4,32,512]{2,1,0:T(8,128)(2,1)}, bf16[4,32,512]{2,1,0:T(8,128)(2,1)S(1)}, u32[]{:S(2)}, u32[]{:S(2)}) collective-permute-start(bf16[4,32,512]{2,1,0:T(8,128)(2,1)} %get-tuple-element.119), channel_id=1, source_target_pairs={{0,1},{1,0},{2,3},{3,2},{4,5},{5,4},{6,7},{7,6},{8,9},{9,8},{10,11... | collective-permute-start | bytes 393224 | tf_op jit(solution)/shard_map/ppermute | solution.py:515
  39.9 16.2 %collective-permute-start.13 = (bf16[4,32,512]{2,1,0:T(8,128)(2,1)}, bf16[4,32,512]{2,1,0:T(8,128)(2,1)S(1)}, u32[]{:S(2)}, u32[]{:S(2)}) collective-permute-start(bf16[4,32,512]{2,1,0:T(8,128)(2,1)} %get-tuple-element.120), channel_id=1, source_target_pairs={{0,1},{1,0},{2,3},{3,2},{4,5},{5,4},{6,7},{7,6},{8,9},{9,8},{10,11... | collective-permute-start | bytes 393224 | tf_op jit(solution)/shard_map/ppermute | solution.py:515
  40.4 0.9 %copy-start.2 = (bf16[2,256,128]{2,1,0:T(8,128)(2,1)S(1)}, bf16[2,256,128]{2,1,0:T(8,128)(2,1)}, u32[]{:S(2)}) copy-start(bf16[2,256,128]{2,1,0:T(8,128)(2,1)} %copy-done.1) | copy-start | bytes 393220
  41.3 0.9 %copy-start.4 = (bf16[2,256,128]{2,1,0:T(8,128)(2,1)S(1)}, bf16[2,256,128]{2,1,0:T(8,128)(2,1)}, u32[]{:S(2)}) copy-start(bf16[2,256,128]{2,1,0:T(8,128)(2,1)} %copy-done.3) | copy-start | bytes 393220
  42.2 0.9 %copy-start.6 = (bf16[2,256,128]{2,1,0:T(8,128)(2,1)S(1)}, bf16[2,256,128]{2,1,0:T(8,128)(2,1)}, u32[]{:S(2)}) copy-start(bf16[2,256,128]{2,1,0:T(8,128)(2,1)} %copy-done.5) | copy-start | bytes 393220
  43.1 0.9 %copy-start.10 = (bf16[2,256,128]{2,1,0:T(8,128)(2,1)S(1)}, bf16[2,256,128]{2,1,0:T(8,128)(2,1)}, u32[]{:S(2)}) copy-start(bf16[2,256,128]{2,1,0:T(8,128)(2,1)} %copy-done.9) | copy-start | bytes 393220
  44.0 0.9 %copy-start.12 = (bf16[2,256,128]{2,1,0:T(8,128)(2,1)S(1)}, bf16[2,256,128]{2,1,0:T(8,128)(2,1)}, u32[]{:S(2)}) copy-start(bf16[2,256,128]{2,1,0:T(8,128)(2,1)} %copy-done.11) | copy-start | bytes 393220
  44.9 0.9 %copy-start.14 = (bf16[2,256,128]{2,1,0:T(8,128)(2,1)S(1)}, bf16[2,256,128]{2,1,0:T(8,128)(2,1)}, u32[]{:S(2)}) copy-start(bf16[2,256,128]{2,1,0:T(8,128)(2,1)} %copy-done.13) | copy-start | bytes 393220
  45.8 0.9 %copy-start.16 = (bf16[2,256,128]{2,1,0:T(8,128)(2,1)S(1)}, bf16[2,256,128]{2,1,0:T(8,128)(2,1)}, u32[]{:S(2)}) copy-start(bf16[2,256,128]{2,1,0:T(8,128)(2,1)} %copy-done.15) | copy-start | bytes 393220
  46.7 0.8 %copy-start.24 = (bf16[2,128,128]{2,1,0:T(8,128)(2,1)S(1)}, bf16[2,128,128]{2,1,0:T(8,128)(2,1)}, u32[]{:S(2)}) copy-start(bf16[2,128,128]{2,1,0:T(8,128)(2,1)} %copy-done.23) | copy-start | bytes 196612
  47.6 0.8 %copy-start.26 = (bf16[2,128,128]{2,1,0:T(8,128)(2,1)S(1)}, bf16[2,128,128]{2,1,0:T(8,128)(2,1)}, u32[]{:S(2)}) copy-start(bf16[2,128,128]{2,1,0:T(8,128)(2,1)} %copy-done.25) | copy-start | bytes 196612
  48.4 0.8 %copy-start.28 = (bf16[2,128,128]{2,1,0:T(8,128)(2,1)S(1)}, bf16[2,128,128]{2,1,0:T(8,128)(2,1)}, u32[]{:S(2)}) copy-start(bf16[2,128,128]{2,1,0:T(8,128)(2,1)} %copy-done.27) | copy-start | bytes 196612
  51.5 6.7 %collective-permute-start.10 = (bf16[2,3,16,512]{3,2,1,0:T(8,128)(2,1)S(1)}, bf16[2,3,16,512]{3,2,1,0:T(8,128)(2,1)S(1)}, u32[]{:S(2)}, u32[]{:S(2)}) collective-permute-start(bf16[2,3,16,512]{3,2,1,0:T(8,128)(2,1)S(1)} %get-tuple-element.113), channel_id=1, source_target_pairs={{0,15},{1,2},{2,1},{3,4},{4,3},{5,6},{6,5},{7,8},{8,7},{9,10},{10,... | collective-permute-start | bytes 294920 | tf_op jit(solution)/shard_map/ppermute | solution.py:38
  55.4 2.9 %collective-permute-start.9 = (bf16[2,3,16,512]{3,2,1,0:T(8,128)(2,1)S(1)}, bf16[2,3,16,512]{3,2,1,0:T(8,128)(2,1)S(1)}, u32[]{:S(2)}, u32[]{:S(2)}) collective-permute-start(bf16[2,3,16,512]{3,2,1,0:T(8,128)(2,1)S(1)} %get-tuple-element.112), channel_id=1, source_target_pairs={{0,1},{1,0},{2,3},{3,2},{4,5},{5,4},{6,7},{7,6},{8,9},{9,8},{10,11... | collective-permute-start | bytes 294920 | tf_op jit(solution)/shard_map/ppermute | solution.py:38
  55.4 0.7 copy-start.17
  56.1 0.6 copy-start.19
  58.3 0.9 %copy-start.8 = (f32[2,32,512]{2,1,0:T(8,128)S(1)}, f32[2,32,512]{2,1,0:T(8,128)}, u32[]{:S(2)}) copy-start(f32[2,32,512]{2,1,0:T(8,128)} %copy-done.7) | copy-start | bytes 393220
  59.2 0.9 %copy-start.18 = (bf16[4,32,512]{2,1,0:T(8,128)(2,1)S(1)}, bf16[4,32,512]{2,1,0:T(8,128)(2,1)}, u32[]{:S(2)}) copy-start(bf16[4,32,512]{2,1,0:T(8,128)(2,1)} %copy-done.17) | copy-start | bytes 393220
  60.1 0.9 %copy-start.20 = (bf16[4,32,512]{2,1,0:T(8,128)(2,1)S(1)}, bf16[4,32,512]{2,1,0:T(8,128)(2,1)}, u32[]{:S(2)}) copy-start(bf16[4,32,512]{2,1,0:T(8,128)(2,1)} %copy-done.19) | copy-start | bytes 393220
  61.0 0.8 copy-start.30
  61.7 0.8 copy-start.32
  63.4 17.4 %copy-start.33 = (s32[1,8,16]{2,1,0:T(8,128)S(1)}, s32[1,8,16]{2,1,0:T(8,128)}, u32[]{:S(2)}) copy-start(s32[1,8,16]{2,1,0:T(8,128)} %send_ref.1) | copy-start | bytes 1540
  63.4 18.4 %all-to-all-start.1 = ((bf16[4,32,1280]{2,1,0:T(8,128)(2,1)}), bf16[4,32,1280]{2,1,0:T(8,128)(2,1)S(1)}, u32[]{:S(2)}, u32[]{:S(2)}) async-start(bf16[4,32,1280]{2,1,0:T(8,128)(2,1)} %get-tuple-element.125), calls=%async_computation.1 | async-start | bytes 655360 | tf_op jit(solution)/shard_map/all_to_all | solution.py:519
  67.0 9.1 %collective-permute-start.14 = (bf16[2,3,16,512]{3,2,1,0:T(8,128)(2,1)S(1)}, bf16[2,3,16,512]{3,2,1,0:T(8,128)(2,1)S(1)}, u32[]{:S(2)}, u32[]{:S(2)}) collective-permute-start(bf16[2,3,16,512]{3,2,1,0:T(8,128)(2,1)S(1)} %get-tuple-element.121), channel_id=1, source_target_pairs={{0,4},{1,5},{2,6},{3,7},{4,0},{5,1},{6,2},{7,3},{8,12},{9,13},{10,... | collective-permute-start | bytes 294920 | tf_op jit(solution)/shard_map/ppermute | solution.py:38
  69.0 12.8 %copy-start.22 = (f32[32,768]{1,0:T(8,128)S(1)}, f32[32,768]{1,0:T(8,128)}, u32[]{:S(2)}) copy-start(f32[32,768]{1,0:T(8,128)} %copy-done.21) | copy-start | bytes 294916
  69.0 11.9 %collective-permute-start.15 = (bf16[2,3,16,512]{3,2,1,0:T(8,128)(2,1)S(1)}, bf16[2,3,16,512]{3,2,1,0:T(8,128)(2,1)S(1)}, u32[]{:S(2)}, u32[]{:S(2)}) collective-permute-start(bf16[2,3,16,512]{3,2,1,0:T(8,128)(2,1)S(1)} %get-tuple-element.122), channel_id=1, source_target_pairs={{0,12},{1,13},{2,14},{3,15},{4,8},{5,9},{6,10},{7,11},{8,4},{9,5},... | collective-permute-start | bytes 294920 | tf_op jit(solution)/shard_map/ppermute | solution.py:38
  81.8 1.0 %copy-start = (bf16[2,128,512]{2,1,0:T(8,128)(2,1)S(1)}, bf16[2,128,512]{2,1,0:T(8,128)(2,1)}, u32[]{:S(2)}) copy-start(bf16[2,128,512]{2,1,0:T(8,128)(2,1)} %shard_map.115.after_ref) | copy-start | bytes 786436
  (4 other events, 2.5 us)

commit v5 on v4

--- a/solution.py
+++ b/solution.py
@@ -21,6 +21,11 @@
 
 def nt(a, b):
     return lax.dot_general(a, b, (((1,), (1,)), ((), ())), preferred_element_type=f32)
+
+
+def shifted(shard, by):
+    count = lax.axis_size("patch")
+    return lax.ppermute(shard, "patch", [(i, (i + by) % count) for i in range(count)])
 
 
 def neighbours_apart(count, stride):
@@ -63,8 +68,7 @@
 
 
 def gather_kernel(
-    slots, stride, me_ref, send_hbm, x_hbm, first_ref, second_ref, right_ref, left_ref, x_ref,
-    send_ref, both, sem,
+    slots, send_hbm, x_hbm, plus_ref, minus_ref, right_ref, left_ref, x_ref, send_ref, sem
 ):
     copies = [
         pltpu.make_async_copy(send_hbm, send_ref, sem.at[0]),
@@ -82,26 +86,37 @@
         def part(k):
             return rows[k * slots : (k + 1) * slots]
 
-        for side, order in enumerate(((2, 6, 4), (3, 5, 7))):
+        for ref, order in ((plus_ref, (2, 6, 4)), (minus_ref, (3, 5, 7))):
             for i, k in enumerate(order):
-                both[side, m, i] = part(k)
+                ref[m, i] = part(k)
         right_ref[m, 0] = part(0)
         left_ref[m, 0] = part(1)
-    to_swaps(both, me_ref[0] // stride % 2, first_ref, second_ref)
 
 
 def relay_kernel(
-    stride, me_ref, after_ref, own_right, own_left, first_in, second_in, first_ref, second_ref,
-    plus_ref, minus_ref, came, both,
+    me_ref, after_ref, own_right, own_left, plus_ref, minus_ref, first_ref, second_ref, both
 ):
-    from_swaps(came, me_ref[0] // stride % 2, first_in, second_in)
     for side, own in enumerate((own_right, own_left)):
         both[side, :, 0:1] = own[...]
-        both[side, :, 1:2] = came[0, :, 1 + side : 2 + side]
-        both[side, :, 2:3] = came[1, :, 1 + side : 2 + side]
+        both[side, :, 1:2] = plus_ref[:, 1 + side : 2 + side]
+        both[side, :, 2:3] = minus_ref[:, 1 + side : 2 + side]
     to_swaps(both, me_ref[0] % 2, first_ref, second_ref)
-    plus_ref[...] = came[0, :, 0:1]
-    minus_ref[...] = came[1, :, 0:1]
+
+
+def gray(z):
+    return z ^ (z >> 1)
+
+
+def plane_of(code):
+    z = code
+    for shift in range(1, 8):
+        z = z ^ (code >> shift)
+    return z
+
+
+def along_z(count, bit):
+    planes = count // 4
+    return [(i, plane_of(gray(i // 4) ^ (1 << bit)) * 4 + i % 4) for i in range(planes * 4)]
 
 
 Q, K, V, G, QT, KT, VT, GT = range(8)
@@ -279,7 +294,7 @@
     c, y, z = me % 2, (me // 2) % 2, me // 4
     qkv = slice(at, at + 384)
     for k in range(planes):
-        zk = (z + k) % planes
+        zk = plane_of(gray(z) ^ k)
         own_ref[k, :, qkv] = dw[zk, y, c]
         other_ref[k, :, qkv] = dw[zk, 1 - y, c]
         send_other[k, :, qkv] = dw[zk, 1 - y, 1 - c].astype(bf16)
@@ -335,30 +350,79 @@
         projection_ref[plane, :, quarter * 128 : (quarter + 1) * 128] = part[:, 384:]
 
 
-def first_kernel(pieces, me_ref, *refs):
-    later, later_core, refs = refs[:pieces], refs[pieces : 2 * pieces], refs[2 * pieces :]
-    own, core_in, y_in, next_ref, own_ref, projection_ref, sent = refs
-    for i, (ref, core) in enumerate(zip(later, later_core)):
-        next_ref[:, :, i * 512 : (i + 1) * 512] = (ref[...] + core[...].astype(f32)).astype(bf16)
-    planes = sent.shape[0]
-    z = me_ref[0] // 4
+def pack_kernel(pieces, after_ref, *refs):
+    for i, (ref, core) in enumerate(zip(refs[:pieces], refs[pieces:-1])):
+        refs[-1][:, :, i * 512 : (i + 1) * 512] = (ref[...] + core[...].astype(f32)).astype(bf16)
+
+
+def halve(rows, kept_ref, sent_ref):
+    for i, row in enumerate(rows):
+        if i % 2 == 0:
+            kept_ref[i // 2] = row
+            continue
+        pieces = row.shape[1] // 256
+        for n in range(pieces):
+            sent_ref[i // 2 * pieces + n] = row[:, n * 256 : (n + 1) * 256].astype(bf16)
+
+
+def add_received(kept_ref, received_ref):
+    planes, _, wide = kept_ref.shape
+    pieces = wide // 256
+    return [
+        kept_ref[i]
+        + jnp.concatenate([received_ref[i * pieces + n] for n in range(pieces)], axis=1).astype(f32)
+        for i in range(planes)
+    ]
+
+
+def flatten(rows, ref, at):
+    members = rows.shape[0]
+    height = ref.shape[1]
+    for m in range(members):
+        for i in range(3):
+            flat = jnp.concatenate([rows[m, i, :, :256], rows[m, i, :, 256:]], axis=0)
+            each = flat.shape[0] // height
+            start = at + (m * 3 + i) * each
+            ref[start : start + each] = flat.reshape(each, height, 256)
+
+
+def unflatten(ref, at, m, i, slots):
+    each = 2 * slots // ref.shape[1]
+    start = at + (m * 3 + i) * each
+    flat = ref[start : start + each].reshape(2 * slots, 256)
+    return jnp.concatenate([flat[:slots], flat[slots:]], axis=1)
+
+
+def first_kernel(
+    stride, skip, me_ref, *refs
+):
+    refs = refs[skip:]
+    own, core_in, y_in, back_plus, back_minus, first_in, second_in = refs[:7]
+    kept_ref, projection_ref, sent_ref, home_second, came, both = refs[7:]
+    planes = own.shape[0]
+    rows = []
     for k in range(planes):
         parts = sums([own], [core_in], y_in, k)
         gather_projection(parts, k, planes, projection_ref, 0)
-        row = jnp.concatenate([part[:, :384] for part in parts], axis=1)
-        sent[(z + k) % planes] = row.astype(bf16)
-        if k == 0:
-            own_ref[...] = row
-
-
-def second_kernel(skip, pieces, stride, me_ref, *refs):
+        rows.append(jnp.concatenate([part[:, :384] for part in parts], axis=1))
+    halve(rows, kept_ref, sent_ref)
+    from_swaps(came, me_ref[0] % 2, first_in, second_in)
+    for side, own_rows in enumerate((back_plus, back_minus)):
+        both[side, :, 0:1] = own_rows[...]
+        both[side, :, 1:2] = came[1, :, 2 - side : 3 - side]
+        both[side, :, 2:3] = came[0, :, 2 - side : 3 - side]
+    odd = me_ref[0] // stride % 2
+    flatten(both[odd], sent_ref, planes // 2 * rows[0].shape[1] // 256)
+    flatten(both[1 - odd], home_second, 0)
+
+
+def second_kernel(skip, pieces, me_ref, *refs):
     refs = refs[skip:]
-    first_ref, back_plus, back_minus, first_in, second_in, y_in = refs[:6]
-    owns, core_in = refs[6 : 6 + pieces], refs[6 + pieces : 6 + 2 * pieces]
-    own_ref, sent, home_first, home_second = refs[6 + 2 * pieces : -3]
-    projection_ref, came, both = refs[-3:]
+    first_ref, y_in = refs[:2]
+    owns, core_in = refs[2 : 2 + pieces], refs[2 + pieces : 2 + 2 * pieces]
+    kept_ref, sent_ref, projection_ref = refs[2 + 2 * pieces :]
     done = first_ref.shape[0]
-    planes = sent.shape[0]
+    planes = projection_ref.shape[0]
     projection_ref[:done] = first_ref[...]
     held = []
     for k in range(planes):
@@ -366,28 +430,35 @@
         gather_projection(parts, k, planes, projection_ref, done)
         held.append(jnp.concatenate([part[:, :384] for part in parts], axis=1))
     z = me_ref[0] // 4
-    for k in range(planes):
-        zk = (z + k) % planes
-        row = jnp.concatenate([held[k], projection_ref[zk]], axis=1)
-        sent[zk] = row.astype(bf16)
-        if k == 0:
-            own_ref[...] = row
-    from_swaps(came, me_ref[0] % 2, first_in, second_in)
-    for side, own in enumerate((back_plus, back_minus)):
-        both[side, :, 0:1] = own[...]
-        both[side, :, 1:2] = came[1, :, 2 - side : 3 - side]
-        both[side, :, 2:3] = came[0, :, 2 - side : 3 - side]
-    to_swaps(both, me_ref[0] // stride % 2, home_first, home_second)
+    halve(
+        [
+            jnp.concatenate([held[k], projection_ref[plane_of(gray(z) ^ k)]], axis=1)
+            for k in range(planes)
+        ],
+        kept_ref, sent_ref,
+    )
+
+
+def step_kernel(extra, after_ref, kept_in, received, *refs):
+    kept_ref, sent_ref = refs[-2:]
+    halve(add_received(kept_in, received), kept_ref, sent_ref)
+    if extra:
+        sent_ref[sent_ref.shape[0] - extra :] = refs[0][...]
 
 
 def finish_kernel(
-    stride, me_ref, send_ref, node_ref, first_in, second_in, home_first, home_second, out_ref,
-    came, home,
+    stride, at_first, at_second, me_ref, after_ref, send_ref, node_ref, first_in, second_in,
+    home_first, home_second, out_ref, came, home,
 ):
     members, node_rows, _ = node_ref.shape
+    slots = first_in.shape[2]
     pick = sent_selector(send_ref[0], node_rows).astype(bf16)
     from_swaps(came, me_ref[0] % 2, first_in, second_in)
-    from_swaps(home, me_ref[0] // stride % 2, home_first, home_second)
+    odd = me_ref[0] // stride % 2
+    for m in range(members):
+        for i in range(3):
+            home[1 - odd, m, i] = unflatten(home_first, at_first, m, i, slots)
+            home[odd, m, i] = unflatten(home_second, at_second, m, i, slots)
     for m in range(members):
         pieces = [None] * 8
         pieces[0], pieces[1] = came[1, m, 0], came[0, m, 0]
@@ -398,13 +469,9 @@
         out_ref[m] = (node_ref[m] + nn(pick, arriving)).astype(bf16)
 
 
-def weight_kernel(me_ref, after_ref, own_a, own_b, z_a, z_b, out_ref):
-    planes = z_a.shape[0]
-    z = me_ref[0] // 4
-    a, b = own_a[...], own_b[...]
-    for k in range(1, planes):
-        a = a + z_a[(z + k) % planes].astype(f32)
-        b = b + z_b[(z + k) % planes].astype(f32)
+def weight_kernel(after_ref, kept_a, in_a, kept_b, in_b, out_ref):
+    (a,) = add_received(kept_a, in_a)
+    (b,) = add_received(kept_b, in_b)
     half = a.shape[1] // 384
     width = 256 * half
     for i, part in enumerate((a, b)):
@@ -447,14 +514,15 @@
 
     place = me.reshape(1)
     trio = pltpu.VMEM((2, *three[0]), bf16)
-    *outgoing, own_right, own_left, x = call(
-        functools.partial(gather_kernel, slots, row_width),
+    to_plus, to_minus, own_right, own_left, x = call(
+        functools.partial(gather_kernel, slots),
         [three, three, one, one, (node_features.shape, bf16)],
-        (place, send_rows, node_features),
-        specs=[pltpu.SMEM] + [pltpu.HBM] * 2,
-        scratch=[pltpu.VMEM(send_rows.shape, jnp.int32), trio, pltpu.SemaphoreType.DMA((2,))],
-    )
-    arrived = swap(outgoing, row_width)
+        (send_rows, node_features),
+        specs=[pltpu.HBM] * 2,
+        scratch=[pltpu.VMEM(send_rows.shape, jnp.int32), pltpu.SemaphoreType.DMA((2,))],
+    )
+    plus = shifted(to_plus, row_width)
+    minus = shifted(to_minus, -row_width)
     square = ((width, width), bf16)
     counts = neighbour_count.reshape(1, node_rows)
     *loc, xt, wq, wk, wv, og, neigh, counts = call(
@@ -467,10 +535,9 @@
         scratch=[pltpu.VMEM((width, width), bf16), pltpu.SemaphoreType.DMA((7,))],
         limit=16,
     )
-    *outgoing, plus, minus = call(
-        functools.partial(relay_kernel, row_width), [three, three, one, one],
-        (place, loc[0], own_right, own_left, *arrived), specs=[pltpu.SMEM, pl.ANY],
-        scratch=[trio, trio],
+    outgoing = call(
+        relay_kernel, [three, three], (place, loc[0], own_right, own_left, plus, minus),
+        specs=[pltpu.SMEM, pl.ANY], scratch=[trio],
     )
     arrived = swap(outgoing, 1)
     (mask,) = call(
@@ -514,10 +581,6 @@
         own, other, send_other, send_own = outs[:4]
         return own, other, lax.ppermute(send_other, "patch", flip), lax.ppermute(send_own, "patch", flip)
 
-    def along_z(sent):
-        lines = [[w + 4 * z for z in range(planes)] for w in range(4)]
-        return lax.all_to_all(sent, "patch", 0, 0, axis_index_groups=lines, tiled=True)
-
     half = groups // 2
     wide = 384 * half
     own_a, other, core_other, core_own = attention((), range(half))
@@ -527,40 +590,77 @@
     for g in range(half, groups):
         later.append(attention((y_sent,) if g == groups - 1 else (), range(g, g + 1)))
     own_b, other_b, core_other_b, core_own_b = zip(*later)
-    y_sent, own_a, out_a, sent = call(
-        functools.partial(first_kernel, len(later)),
-        [(y_sent.shape, bf16), ((rows, wide), f32), ((half * inner_planes, rows, width), f32)]
-        + [((planes, rows, wide), bf16)],
-        (place, *other_b, *core_other_b, own_a, core_own, y_a), specs=[pltpu.SMEM],
+    (y_sent,) = call(
+        functools.partial(pack_kernel, len(later)), [(y_sent.shape, bf16)],
+        (y_a, *other_b, *core_other_b), specs=[pl.ANY],
     )
     y_b = lax.ppermute(y_sent, "patch", flop)
-    z_a = along_z(sent)
     node, *outgoing, back_plus, back_minus = call(
-        functools.partial(node_kernel, groups, 2),
+        functools.partial(node_kernel, groups, 1),
         [((members, node_rows, width), f32), three, three, one, one],
-        (place, y_sent, sent, *grads[0::3], *grads[1::3], *grads[2::3], wq, wk, wv),
-        specs=[pltpu.SMEM] + [pl.ANY] * 2, scratch=[trio],
+        (place, y_sent, *grads[0::3], *grads[1::3], *grads[2::3], wq, wk, wv),
+        specs=[pltpu.SMEM, pl.ANY], scratch=[trio],
     )
     back = swap(outgoing, 1)
-    own_b, sent, *outgoing = call(
-        functools.partial(second_kernel, 2, len(later), row_width),
-        [((rows, wide + width), f32), ((planes, rows, wide + width), bf16), three, three],
-        (
-            place, node, z_a, out_a, back_plus, back_minus, *back, y_b, *own_b, *core_own_b,
-        ),
-        specs=[pltpu.SMEM] + [pl.ANY] * 2,
-        scratch=[pltpu.VMEM((planes, rows, width), f32), trio, trio],
-    )
-    z_b = along_z(sent)
-    home = swap(outgoing, row_width)
+
+    steps = planes.bit_length() - 1
+    homeward = neighbours_apart(count, row_width)
+    more = members * 6 * slots // rows
+    rides = [along_z(count, i) == homeward[i] if i < steps else False for i in range(2)]
+
+    def exchange(sent, bit):
+        return lax.ppermute(sent, "patch", along_z(count, bit))
+
+    def halves(wide, bit, riders=0):
+        left = planes >> (bit + 1)
+        return [((left, rows, wide), f32), ((left * wide // 256 + riders, rows, 256), bf16)]
+
+    kept_a, projected = halves(wide, 0, more)
+    kept_a, out_a, sent, home_second = call(
+        functools.partial(first_kernel, row_width, 1),
+        [kept_a, ((half * inner_planes, rows, width), f32), projected, ((more, rows, 256), bf16)],
+        (place, y_sent, own_a, core_own, y_a, back_plus, back_minus, *back),
+        specs=[pltpu.SMEM, pl.ANY], scratch=[trio, trio],
+    )
+    in_a = exchange(sent, 0)
+    home_first = in_a if rides[0] else lax.ppermute(sent, "patch", homeward[0])
+    at_first, at_second = planes // 2 * wide // 256, 0
+    kept_b, sent_b = call(
+        functools.partial(second_kernel, 1, len(later)), halves(wide + width, 0),
+        (place, sent, out_a, y_b, *own_b, *core_own_b),
+        specs=[pltpu.SMEM, pl.ANY],
+        scratch=[pltpu.VMEM((planes, rows, width), f32)],
+    )
+    in_b = exchange(sent_b, 0)
+    after = sent_b
+    for bit in range(1, steps):
+        riding = bit == 1 and rides[1]
+        kept_a, after = call(
+            functools.partial(step_kernel, more if riding else 0),
+            halves(wide, bit, more if riding else 0),
+            (after, kept_a, in_a) + ((home_second,) if riding else ()),
+            specs=[pl.ANY],
+        )
+        in_a = exchange(after, bit)
+        if riding:
+            home_second = in_a
+            at_second = (planes >> (bit + 1)) * wide // 256
+        kept_b, after = call(
+            functools.partial(step_kernel, 0), halves(wide + width, bit),
+            (after, kept_b, in_b), specs=[pl.ANY],
+        )
+        in_b = exchange(after, bit)
+    if not rides[1]:
+        home_second = lax.ppermute(home_second, "patch", homeward[1])
     (node_grad,) = call(
-        functools.partial(finish_kernel, row_width), [((members, node_rows, width), bf16)],
-        (place, send_rows, node, *back, *home), specs=[pltpu.SMEM], scratch=[trio, trio],
-        final=True,
+        functools.partial(finish_kernel, row_width, at_first, at_second),
+        [((members, node_rows, width), bf16)],
+        (place, after, send_rows, node, *back, home_first, home_second),
+        specs=[pltpu.SMEM, pl.ANY], scratch=[trio, trio], final=True,
     )
     (weight_grad,) = call(
-        weight_kernel, [((rows, 4 * width), f32)],
-        (place, node_grad, own_a, own_b, z_a, z_b), specs=[pltpu.SMEM, pl.ANY], final=True,
+        weight_kernel, [((rows, 4 * width), f32)], (node_grad, kept_a, in_a, kept_b, in_b),
+        specs=[pl.ANY], final=True,
     )
     return (node_grad, weight_grad)
 

time: 84.3 us -> 60.2 us (0.71)
  local copies, waits for them, and re-layouts: 19.1 us -> 0.95 us
  starting transfers between devices: 26.9 us -> 18 us
  waiting for transfers between devices: 18.4 us -> 24.5 us
  Pallas kernels: 18.2 us -> 15.6 us
    unnamed x68 -> x4, local copies, waits for them, and re-layouts: 19.1 us -> 0.95 us
    ppermute x0 -> x6, waiting for transfers between devices: none -> 13.3 us  [the longest x4 11.7 us: exchange(): return lax.ppermute(sent, 'patch', along_z(count, bit))]
    ppermute x8 -> x4, starting transfers between devices: 16.7 us -> 6.35 us  [swap(): lax.ppermute(shard, 'patch', perm)]
    ppermute x8 -> x4, waiting for transfers between devices: 15.6 us -> 5.47 us  [swap(): lax.ppermute(shard, 'patch', perm)]
    ppermute x0 -> x6, starting transfers between devices: none -> 9.89 us  [the longest x2 5.17 us: shifted(): lax.ppermute(shard, 'patch', [(i, (i + by) % count) for i in range(count)])]
    all_to_all x2 -> x0, starting transfers between devices: 7.46 us -> none  [along_z(): lax.all_to_all(sent, 'patch', 0, 0, axis_index_groups=lines, tiled=True)]
    pallas_call x13 -> x16, Pallas kernels: 18.2 us -> 15.6 us  [call(): pl.pallas_call(kernel, out_shape=[jax.ShapeDtypeStruct(*o) if final else...]
    ppermute x1, waiting for transfers between devices: 0.77 us -> 3.29 us  [body(): y_a = lax.ppermute(y_sent, 'patch', flop)]
  transfers between devices with their start and end apart: 18 -> 18, of which waited for: 8 -> 12; matrix products, arithmetic and copies ran while one was open for 0% -> 0% of each run, Pallas kernels for 13% -> 16%
where the time goes in v5:
time: 60.2 us; the launch traced here: 59.9 us
  waiting for transfers between devices  24.5 us (41%)
  starting transfers between devices  18 us (30%)
  Pallas kernels  15.6 us (26%)
  local copies, waits for them, and re-layouts  0.95 us (2%)
  between operations  0.78 us (1%)
    pallas_call x16, Pallas kernels, call(): pl.pallas_call(kernel, out_shape=[jax.ShapeDtypeStruct(*o) if final else...  15.6 us
    ppermute x4, waiting for transfers between devices, exchange(): return lax.ppermute(sent, 'patch', along_z(count, bit))  11.7 us
    ppermute x4, starting transfers between devices, swap(): lax.ppermute(shard, 'patch', perm)  6.35 us
    ppermute x4, waiting for transfers between devices, swap(): lax.ppermute(shard, 'patch', perm)  5.47 us
    ppermute x2, starting transfers between devices, shifted(): lax.ppermute(shard, 'patch', [(i, (i + by) % count) for i in range(count)])  5.17 us
    ppermute x4, starting transfers between devices, exchange(): return lax.ppermute(sent, 'patch', along_z(count, bit))  4.72 us
    ppermute x1, waiting for transfers between devices, body(): y_a = lax.ppermute(y_sent, 'patch', flop)  3.29 us
    ppermute x3, waiting for transfers between devices, attention(): lax.ppermute(send_other, 'patch', flip)  2.37 us
  transfers between devices with their start and end apart: 18, of which 12 were waited for; matrix products, arithmetic and copies ran while one was open for 0% of the time, Pallas kernels for 16%

profile of v5, /device:TPU:0, one launch (start us, length us, event | category | flops | bytes accessed | tf_op | source)
XLA Modules:
  0.0 59.9 jit_solution(2331414397139726232)
XLA Ops:
  0.6 1.2 %shard_map.104 = (bf16[2,3,16,512]{3,2,1,0:T(8,128)(2,1)S(1)}, bf16[2,3,16,512]{3,2,1,0:T(8,128)(2,1)S(1)}, bf16[2,1,16,512]{3,2,1,0:T(8,128)(2,1)S(1)}, bf16[2,...) custom-call(s32[1,8,16]{2,1,0:T(8,128)} %send_ref.1, bf16[2,128,512]{2,1,0:T(8,128)(2,1)} %x_hbm.1), custom_call_target="tpu_custom_call" | custom-call | flops 1000000 | bytes 10000 | tf_op jit(solution)/shard_map/pallas_call | solution.py:492
  1.8 3.1 %collective-permute-start = (bf16[2,3,16,512]{3,2,1,0:T(8,128)(2,1)S(1)}, bf16[2,3,16,512]{3,2,1,0:T(8,128)(2,1)S(1)}, u32[]{:S(2)}, u32[]{:S(2)}) collective-permute-start(bf16[2,3,16,512]{3,2,1,0:T(8,128)(2,1)S(1)} %get-tuple-element.68), channel_id=1, source_target_pairs={{0,4},{1,5},{2,6},{3,7},{4,8},{5,9},{6,10},{7,11},{8,12},{9,13},{1... | collective-permute-start | bytes 294920 | tf_op jit(solution)/shard_map/ppermute | solution.py:28
  4.9 2.1 %collective-permute-start.1 = (bf16[2,3,16,512]{3,2,1,0:T(8,128)(2,1)S(1)}, bf16[2,3,16,512]{3,2,1,0:T(8,128)(2,1)S(1)}, u32[]{:S(2)}, u32[]{:S(2)}) collective-permute-start(bf16[2,3,16,512]{3,2,1,0:T(8,128)(2,1)S(1)} %get-tuple-element.69), channel_id=1, source_target_pairs={{0,12},{1,13},{2,14},{3,15},{4,0},{5,1},{6,2},{7,3},{8,4},{9,5},{1... | collective-permute-start | bytes 294920 | tf_op jit(solution)/shard_map/ppermute | solution.py:28
  7.0 2.6 %shard_map.105 = (bf16[8,2,128,128]{3,2,1,0:T(8,128)(2,1)S(1)}, bf16[8,2,128,128]{3,2,1,0:T(8,128)(2,1)S(1)}, bf16[8,2,128,128]{3,2,1,0:T(8,128)(2,1)S(1)}, bf16...) custom-call(bf16[2,1,16,512]{3,2,1,0:T(8,128)(2,1)S(1)} %get-tuple-e, ...), custom_call_target="tpu_custom_call" | custom-call | flops 1000000 | bytes 10000 | tf_op jit(solution)/shard_map/pallas_call | solution.py:492
  9.7 0.8 %collective-permute-done.plus_ref = bf16[2,3,16,512]{3,2,1,0:T(8,128)(2,1)S(1)} collective-permute-done((bf16[2,3,16,512]{3,2,1,0:T(8,128)(2,1)S(1)}, bf16[2,3,16,512]{3,2,1,0:T(8,128)(2,1)S(1)}, u32[]{:S(2)}, u32[]{:S(2)}) %collective-permute-start) | collective-permute-done | bytes 98336 | tf_op jit(solution)/shard_map/ppermute | solution.py:28
  10.4 0.8 %collective-permute-done.1.minus_ref = bf16[2,3,16,512]{3,2,1,0:T(8,128)(2,1)S(1)} collective-permute-done((bf16[2,3,16,512]{3,2,1,0:T(8,128)(2,1)S(1)}, bf16[2,3,16,512]{3,2,1,0:T(8,128)(2,1)S(1)}, u32[]{:S(2)}, u32[]{:S(2)}) %collective-permute-start.1) | collective-permute-done | bytes 98336 | tf_op jit(solution)/shard_map/ppermute | solution.py:28
  11.3 0.1 collective-permute-start.2
  11.4 3.4 %collective-permute-start.3 = (bf16[2,3,16,512]{3,2,1,0:T(8,128)(2,1)S(1)}, bf16[2,3,16,512]{3,2,1,0:T(8,128)(2,1)S(1)}, u32[]{:S(2)}, u32[]{:S(2)}) collective-permute-start(bf16[2,3,16,512]{3,2,1,0:T(8,128)(2,1)S(1)} %get-tuple-element.72), channel_id=1, source_target_pairs={{0,15},{1,2},{2,1},{3,4},{4,3},{5,6},{6,5},{7,8},{8,7},{9,10},{10,... | collective-permute-start | bytes 294920 | tf_op jit(solution)/shard_map/ppermute | solution.py:43
  14.8 1.4 %shard_map.108.refs_4_.refs_2_.refs_3_ = f32[256,128]{1,0:T(8,128)S(1)} custom-call(bf16[2,3,16,512]{3,2,1,0:T(8,128)(2,1)S(1)} %get-tuple-element.71.after_ref, s32[128,256]{1,0:T(8,128)S(1)} %get-tuple-element.78.neigh_ref, s32[1,128]{1,0:T(1,128)S(1)} %get-tuple-element.79.count_ref), custom_call_target="tpu_custom_call" | custom-call | flops 1000000 | bytes 10000 | tf_op jit(solution)/shard_map/pallas_call | solution.py:492
  16.3 1.9 %collective-permute-done.3.second_in = bf16[2,3,16,512]{3,2,1,0:T(8,128)(2,1)S(1)} collective-permute-done((bf16[2,3,16,512]{3,2,1,0:T(8,128)(2,1)S(1)}, bf16[2,3,16,512]{3,2,1,0:T(8,128)(2,1)S(1)}, u32[]{:S(2)}, u32[]{:S(2)}) %collective-permute-start.3) | collective-permute-done | bytes 98336 | tf_op jit(solution)/shard_map/ppermute | solution.py:43
  18.2 0.6 %shard_map.107 = (bf16[4,2,128,128]{3,2,1,0:T(8,128)(2,1)S(1)}, bf16[4,2,128,128]{3,2,1,0:T(8,128)(2,1)S(1)}, bf16[4,2,128,128]{3,2,1,0:T(8,128)(2,1)S(1)}, bf16...) custom-call(s32[1]{0:T(128)} %bitcast.me_ref, bf16[2,3,16,512]{3,2,1,0:T(8,128)(2,1)S(1)} %collective-permute-done.plus_ref, ...), custom_call_target="tpu_custom_call" | custom-call | flops 1000000 | bytes 10000 | tf_op jit(solution)/shard_map/pallas_call | solution.py:492
  18.8 3.1 %shard_map.109 = (f32[4,32,1024]{2,1,0:T(8,128)S(1)}, f32[4,32,1024]{2,1,0:T(8,128)S(1)}, bf16[4,32,1024]{2,1,0:T(8,128)(2,1)S(1)}, bf16[4,32,1024]{2,1,0:T(8,12...) custom-call(s32[1]{0:T(128)} %bitcast.me_ref, ...), custom_call_target="tpu_custom_call" | custom-call | flops 1000000 | bytes 10000 | tf_op jit(solution)/shard_map/pallas_call | solution.py:492
  22.0 0.1 collective-permute-start.4
  22.0 1.5 %collective-permute-done.4 = bf16[4,32,1024]{2,1,0:T(8,128)(2,1)S(1)} collective-permute-done((bf16[4,32,1024]{2,1,0:T(8,128)(2,1)S(1)}, bf16[4,32,1024]{2,1,0:T(8,128)(2,1)S(1)}, u32[]{:S(2)}, u32[]{:S(2)}) %collective-permute-start.4) | collective-permute-done | bytes 262176 | tf_op jit(solution)/shard_map/ppermute | solution.py:582
  23.6 0.1 add_convert_fusion.refs_0_
  23.6 0.1 collective-permute-start.5
  23.7 1.7 %shard_map.110 = (f32[4,32,512]{2,1,0:T(8,128)S(1)}, f32[4,32,512]{2,1,0:T(8,128)S(1)}, bf16[4,32,512]{2,1,0:T(8,128)(2,1)S(1)}, bf16[4,32,512]{2,1,0:T(8,128)(2...) custom-call(s32[1]{0:T(128)} %bitcast.me_ref, ...), custom_call_target="tpu_custom_call" | custom-call | flops 1000000 | bytes 10000 | tf_op jit(solution)/shard_map/pallas_call | solution.py:492
  25.4 0.2 collective-permute-start.6
  25.6 1.7 %shard_map.111 = (f32[4,32,512]{2,1,0:T(8,128)S(1)}, f32[4,32,512]{2,1,0:T(8,128)S(1)}, bf16[4,32,512]{2,1,0:T(8,128)(2,1)S(1)}, bf16[4,32,512]{2,1,0:T(8,128)(2...) custom-call(s32[1]{0:T(128)} %bitcast.me_ref, ...), custom_call_target="tpu_custom_call" | custom-call | flops 1000000 | bytes 10000 | tf_op jit(solution)/shard_map/pallas_call | solution.py:492
  27.3 0.4 collective-permute-start.7
  27.8 0.1 collective-permute-start.8
  27.9 0.0 collective-permute-done.6.refs_2_
  27.9 0.8 %collective-permute-done.7.refs_3_ = bf16[4,32,512]{2,1,0:T(8,128)(2,1)S(1)} collective-permute-done((bf16[4,32,512]{2,1,0:T(8,128)(2,1)S(1)}, bf16[4,32,512]{2,1,0:T(8,128)(2,1)S(1)}, u32[]{:S(2)}, u32[]{:S(2)}) %collective-permute-start.7) | collective-permute-done | bytes 131104 | tf_op jit(solution)/shard_map/ppermute | solution.py:582
  28.8 3.3 %collective-permute-done.5.after_ref.refs_3_ = bf16[4,32,1024]{2,1,0:T(8,128)(2,1)S(1)} collective-permute-done((bf16[4,32,1024]{2,1,0:T(8,128)(2,1)S(1)}, bf16[4,32,1024]{2,1,0:T(8,128)(2,1)S(1)}, u32[]{:S(2)}, u32[]{:S(2)}) %collective-permute-start.5) | collective-permute-done | bytes 262176 | tf_op jit(solution)/shard_map/ppermute | solution.py:588
  32.0 0.1 shard_map.112.refs_0_
  32.1 0.4 collective-permute-start.11
  32.5 1.0 %shard_map.113 = (f32[2,128,512]{2,1,0:T(8,128)S(1)}, bf16[2,3,16,512]{3,2,1,0:T(8,128)(2,1)S(1)}, bf16[2,3,16,512]{3,2,1,0:T(8,128)(2,1)S(1)}, bf16[2,1,16,512]...) custom-call(s32[1]{0:T(128)} %bitcast.me_ref, bf16[4,32,1024]{2,1,0:T(8,128)(2,1)S(1)} %shard_map.112.refs_0_, ...), custom_call_target="tpu_custom_call" | custom-call | flops 1000000 | bytes 10000 | tf_op jit(solution)/shard_map/pallas_call | solution.py:492
  33.5 2.8 %collective-permute-start.10 = (bf16[2,3,16,512]{3,2,1,0:T(8,128)(2,1)S(1)}, bf16[2,3,16,512]{3,2,1,0:T(8,128)(2,1)S(1)}, u32[]{:S(2)}, u32[]{:S(2)}) collective-permute-start(bf16[2,3,16,512]{3,2,1,0:T(8,128)(2,1)S(1)} %get-tuple-element.110), channel_id=1, source_target_pairs={{0,15},{1,2},{2,1},{3,4},{4,3},{5,6},{6,5},{7,8},{8,7},{9,10},{10,... | collective-permute-start | bytes 294920 | tf_op jit(solution)/shard_map/ppermute | solution.py:43
  36.3 0.0 collective-permute-start.9
  36.3 0.5 collective-permute-start.12
  36.8 0.0 collective-permute-done.8.refs_2_
  36.8 0.0 collective-permute-start.13
  36.8 3.6 %collective-permute-done.10.refs_7_.second_in = bf16[2,3,16,512]{3,2,1,0:T(8,128)(2,1)S(1)} collective-permute-done((bf16[2,3,16,512]{3,2,1,0:T(8,128)(2,1)S(1)}, bf16[2,3,16,512]{3,2,1,0:T(8,128)(2,1)S(1)}, u32[]{:S(2)}, u32[]{:S(2)}) %collective-permute-start.10) | collective-permute-done | bytes 98336 | tf_op jit(solution)/shard_map/ppermute | solution.py:43
  40.4 0.0 collective-permute-done.9.refs_6_.first_in
  40.4 0.1 shard_map.114
  40.5 0.1 collective-permute-start.14
  40.6 0.1 collective-permute-done.11.refs_2_
  40.8 0.1 shard_map.115
  40.9 2.0 %collective-permute-start.15 = (bf16[10,32,256]{2,1,0:T(8,128)(2,1)S(1)}, bf16[10,32,256]{2,1,0:T(8,128)(2,1)S(1)}, u32[]{:S(2)}, u32[]{:S(2)}) collective-permute-start(bf16[10,32,256]{2,1,0:T(8,128)(2,1)S(1)} %get-tuple-element.117.after_ref), channel_id=1, source_target_pairs={{0,4},{1,5},{2,6},{3,7},{4,0},{5,1},{6,2},{7,3},{8,12},{9,13},{10,... | collective-permute-start | bytes 491528 | tf_op jit(solution)/shard_map/ppermute | solution.py:612
  42.8 5.3 %collective-permute-done.14.received.home_first = bf16[12,32,256]{2,1,0:T(8,128)(2,1)S(1)} collective-permute-done((bf16[12,32,256]{2,1,0:T(8,128)(2,1)S(1)}, bf16[12,32,256]{2,1,0:T(8,128)(2,1)S(1)}, u32[]{:S(2)}, u32[]{:S(2)}) %collective-permute-start.14) | collective-permute-done | bytes 196640 | tf_op jit(solution)/shard_map/ppermute | solution.py:612
  48.2 1.3 %collective-permute-start.16 = (bf16[9,32,256]{2,1,0:T(8,128)(2,1)S(1)}, bf16[9,32,256]{2,1,0:T(8,128)(2,1)S(1)}, u32[]{:S(2)}, u32[]{:S(2)}) collective-permute-start(bf16[9,32,256]{2,1,0:T(8,128)(2,1)S(1)} %get-tuple-element.120.after_ref), channel_id=1, source_target_pairs={{0,12},{1,13},{2,14},{3,15},{4,8},{5,9},{6,10},{7,11},{8,4},{9,5},... | collective-permute-start | bytes 442376 | tf_op jit(solution)/shard_map/ppermute | solution.py:612
  49.5 2.1 %collective-permute-done.15.received = bf16[10,32,256]{2,1,0:T(8,128)(2,1)S(1)} collective-permute-done((bf16[10,32,256]{2,1,0:T(8,128)(2,1)S(1)}, bf16[10,32,256]{2,1,0:T(8,128)(2,1)S(1)}, u32[]{:S(2)}, u32[]{:S(2)}) %collective-permute-start.15) | collective-permute-done | bytes 163872 | tf_op jit(solution)/shard_map/ppermute | solution.py:612
  51.7 1.3 %collective-permute-start.17 = (bf16[5,32,256]{2,1,0:T(8,128)(2,1)S(1)}, bf16[5,32,256]{2,1,0:T(8,128)(2,1)S(1)}, u32[]{:S(2)}, u32[]{:S(2)}) collective-permute-start(bf16[5,32,256]{2,1,0:T(8,128)(2,1)S(1)} %get-tuple-element.122.after_ref), channel_id=1, source_target_pairs={{0,12},{1,13},{2,14},{3,15},{4,8},{5,9},{6,10},{7,11},{8,4},{9,5},... | collective-permute-start | bytes 245768 | tf_op jit(solution)/shard_map/ppermute | solution.py:612
  53.0 3.6 %collective-permute-done.16.home_second.in_a = bf16[9,32,256]{2,1,0:T(8,128)(2,1)S(1)} collective-permute-done((bf16[9,32,256]{2,1,0:T(8,128)(2,1)S(1)}, bf16[9,32,256]{2,1,0:T(8,128)(2,1)S(1)}, u32[]{:S(2)}, u32[]{:S(2)}) %collective-permute-start.16) | collective-permute-done | bytes 147488 | tf_op jit(solution)/shard_map/ppermute | solution.py:612
  56.6 1.0 %shard_map.118.after_ref = bf16[2,128,512]{2,1,0:T(8,128)(2,1)} custom-call(s32[1]{0:T(128)} %bitcast.me_ref, bf16[5,32,256]{2,1,0:T(8,128)(2,1)S(1)} %get-tuple-element.122.after_ref, s32[1,8,16]{2,1,0:T(8,128)S(1)} %copy-done.1, f32[2,128,512]{2,1,0:T(8,128)S(1)} %get-tuple-element.123.node_ref, ...), custom_call_target="tpu_custom_call" | custom-call | flops 1000000 | bytes 10000 | tf_op jit(solution)/shard_map/pallas_call | solution.py:492
  57.6 0.7 %collective-permute-done.17.in_b = bf16[5,32,256]{2,1,0:T(8,128)(2,1)S(1)} collective-permute-done((bf16[5,32,256]{2,1,0:T(8,128)(2,1)S(1)}, bf16[5,32,256]{2,1,0:T(8,128)(2,1)S(1)}, u32[]{:S(2)}, u32[]{:S(2)}) %collective-permute-start.17) | collective-permute-done | bytes 81952 | tf_op jit(solution)/shard_map/ppermute | solution.py:612
  58.2 0.9 %copy-done = bf16[2,128,512]{2,1,0:T(8,128)(2,1)S(1)} copy-done((bf16[2,128,512]{2,1,0:T(8,128)(2,1)S(1)}, bf16[2,128,512]{2,1,0:T(8,128)(2,1)}, u32[]{:S(2)}) %copy-start) | copy-done | bytes 262168
  59.2 0.7 %shard_map.119 = f32[32,2048]{1,0:T(8,128)} custom-call(bf16[2,128,512]{2,1,0:T(8,128)(2,1)S(1)} %copy-done, f32[1,32,768]{2,1,0:T(8,128)S(1)} %get-tuple-element.124.kept_a, bf16[9,32,256]{2,1,0:T(8,128)(2,1)S(1)} %collective-permute-done.16.home_second.in_a, f32[1,32,1280]{2,1,0:T(8,128)S(1)} %get-tuple-element.125.kept_b, ...), custom_call_target="tpu_custom_call" | custom-call | flops 1000000 | bytes 10000 | tf_op jit(solution)/shard_map/pallas_call | solution.py:492
  (9 shorter events, 0.1 us)
Async XLA Ops:
  1.8 8.6 %collective-permute-start = (bf16[2,3,16,512]{3,2,1,0:T(8,128)(2,1)S(1)}, bf16[2,3,16,512]{3,2,1,0:T(8,128)(2,1)S(1)}, u32[]{:S(2)}, u32[]{:S(2)}) collective-permute-start(bf16[2,3,16,512]{3,2,1,0:T(8,128)(2,1)S(1)} %get-tuple-element.68), channel_id=1, source_target_pairs={{0,4},{1,5},{2,6},{3,7},{4,8},{5,9},{6,10},{7,11},{8,12},{9,13},{1... | collective-permute-start | bytes 294920 | tf_op jit(solution)/shard_map/ppermute | solution.py:28
  4.9 6.4 %collective-permute-start.1 = (bf16[2,3,16,512]{3,2,1,0:T(8,128)(2,1)S(1)}, bf16[2,3,16,512]{3,2,1,0:T(8,128)(2,1)S(1)}, u32[]{:S(2)}, u32[]{:S(2)}) collective-permute-start(bf16[2,3,16,512]{3,2,1,0:T(8,128)(2,1)S(1)} %get-tuple-element.69), channel_id=1, source_target_pairs={{0,12},{1,13},{2,14},{3,15},{4,0},{5,1},{6,2},{7,3},{8,4},{9,5},{1... | collective-permute-start | bytes 294920 | tf_op jit(solution)/shard_map/ppermute | solution.py:28
  11.3 5.0 %collective-permute-start.2 = (bf16[2,3,16,512]{3,2,1,0:T(8,128)(2,1)S(1)}, bf16[2,3,16,512]{3,2,1,0:T(8,128)(2,1)S(1)}, u32[]{:S(2)}, u32[]{:S(2)}) collective-permute-start(bf16[2,3,16,512]{3,2,1,0:T(8,128)(2,1)S(1)} %get-tuple-element.71.after_ref), channel_id=1, source_target_pairs={{0,1},{1,0},{2,3},{3,2},{4,5},{5,4},{6,7},{7,6},{8,9},{9,8},{10,11... | collective-permute-start | bytes 294920 | tf_op jit(solution)/shard_map/ppermute | solution.py:43
  11.4 6.8 %collective-permute-start.3 = (bf16[2,3,16,512]{3,2,1,0:T(8,128)(2,1)S(1)}, bf16[2,3,16,512]{3,2,1,0:T(8,128)(2,1)S(1)}, u32[]{:S(2)}, u32[]{:S(2)}) collective-permute-start(bf16[2,3,16,512]{3,2,1,0:T(8,128)(2,1)S(1)} %get-tuple-element.72), channel_id=1, source_target_pairs={{0,15},{1,2},{2,1},{3,4},{4,3},{5,6},{6,5},{7,8},{8,7},{9,10},{10,... | collective-permute-start | bytes 294920 | tf_op jit(solution)/shard_map/ppermute | solution.py:43
  22.0 1.6 %collective-permute-start.4 = (bf16[4,32,1024]{2,1,0:T(8,128)(2,1)S(1)}, bf16[4,32,1024]{2,1,0:T(8,128)(2,1)S(1)}, u32[]{:S(2)}, u32[]{:S(2)}) collective-permute-start(bf16[4,32,1024]{2,1,0:T(8,128)(2,1)S(1)} %get-tuple-element.83), channel_id=1, source_target_pairs={{0,1},{1,0},{2,3},{3,2},{4,5},{5,4},{6,7},{7,6},{8,9},{9,8},{10,11... | collective-permute-start | bytes 786440 | tf_op jit(solution)/shard_map/ppermute | solution.py:582
  23.6 8.4 %collective-permute-start.5 = (bf16[4,32,1024]{2,1,0:T(8,128)(2,1)S(1)}, bf16[4,32,1024]{2,1,0:T(8,128)(2,1)S(1)}, u32[]{:S(2)}, u32[]{:S(2)}) collective-permute-start(bf16[4,32,1024]{2,1,0:T(8,128)(2,1)S(1)} %add_convert_fusion.refs_0_), channel_id=1, source_target_pairs={{0,2},{1,3},{2,0},{3,1},{4,6},{5,7},{6,4},{7,5},{8,10},{9,11},{10,... | collective-permute-start | bytes 786440 | tf_op jit(solution)/shard_map/ppermute | solution.py:588
  25.4 2.5 %collective-permute-start.6 = (bf16[4,32,512]{2,1,0:T(8,128)(2,1)S(1)}, bf16[4,32,512]{2,1,0:T(8,128)(2,1)S(1)}, u32[]{:S(2)}, u32[]{:S(2)}) collective-permute-start(bf16[4,32,512]{2,1,0:T(8,128)(2,1)S(1)} %get-tuple-element.90), channel_id=1, source_target_pairs={{0,1},{1,0},{2,3},{3,2},{4,5},{5,4},{6,7},{7,6},{8,9},{9,8},{10,11... | collective-permute-start | bytes 393224 | tf_op jit(solution)/shard_map/ppermute | solution.py:582
  27.3 1.4 %collective-permute-start.7 = (bf16[4,32,512]{2,1,0:T(8,128)(2,1)S(1)}, bf16[4,32,512]{2,1,0:T(8,128)(2,1)S(1)}, u32[]{:S(2)}, u32[]{:S(2)}) collective-permute-start(bf16[4,32,512]{2,1,0:T(8,128)(2,1)S(1)} %get-tuple-element.91), channel_id=1, source_target_pairs={{0,1},{1,0},{2,3},{3,2},{4,5},{5,4},{6,7},{7,6},{8,9},{9,8},{10,11... | collective-permute-start | bytes 393224 | tf_op jit(solution)/shard_map/ppermute | solution.py:582
  27.8 9.1 %collective-permute-start.8 = (bf16[4,32,1024]{2,1,0:T(8,128)(2,1)S(1)}, bf16[4,32,1024]{2,1,0:T(8,128)(2,1)S(1)}, u32[]{:S(2)}, u32[]{:S(2)}) collective-permute-start(bf16[4,32,1024]{2,1,0:T(8,128)(2,1)S(1)} %get-tuple-element.93), channel_id=1, source_target_pairs={{0,1},{1,0},{2,3},{3,2},{4,5},{5,4},{6,7},{7,6},{8,9},{9,8},{10,11... | collective-permute-start | bytes 786440 | tf_op jit(solution)/shard_map/ppermute | solution.py:582
  32.1 8.6 %collective-permute-start.11 = (bf16[4,32,1024]{2,1,0:T(8,128)(2,1)S(1)}, bf16[4,32,1024]{2,1,0:T(8,128)(2,1)S(1)}, u32[]{:S(2)}, u32[]{:S(2)}) collective-permute-start(bf16[4,32,1024]{2,1,0:T(8,128)(2,1)S(1)} %shard_map.112.refs_0_), channel_id=1, source_target_pairs={{0,2},{1,3},{2,0},{3,1},{4,6},{5,7},{6,4},{7,5},{8,10},{9,11},{10,... | collective-permute-start | bytes 786440 | tf_op jit(solution)/shard_map/ppermute | solution.py:597
  33.5 6.9 %collective-permute-start.10 = (bf16[2,3,16,512]{3,2,1,0:T(8,128)(2,1)S(1)}, bf16[2,3,16,512]{3,2,1,0:T(8,128)(2,1)S(1)}, u32[]{:S(2)}, u32[]{:S(2)}) collective-permute-start(bf16[2,3,16,512]{3,2,1,0:T(8,128)(2,1)S(1)} %get-tuple-element.110), channel_id=1, source_target_pairs={{0,15},{1,2},{2,1},{3,4},{4,3},{5,6},{6,5},{7,8},{8,7},{9,10},{10,... | collective-permute-start | bytes 294920 | tf_op jit(solution)/shard_map/ppermute | solution.py:43
  36.3 4.1 %collective-permute-start.9 = (bf16[2,3,16,512]{3,2,1,0:T(8,128)(2,1)S(1)}, bf16[2,3,16,512]{3,2,1,0:T(8,128)(2,1)S(1)}, u32[]{:S(2)}, u32[]{:S(2)}) collective-permute-start(bf16[2,3,16,512]{3,2,1,0:T(8,128)(2,1)S(1)} %get-tuple-element.109), channel_id=1, source_target_pairs={{0,1},{1,0},{2,3},{3,2},{4,5},{5,4},{6,7},{7,6},{8,9},{9,8},{10,11... | collective-permute-start | bytes 294920 | tf_op jit(solution)/shard_map/ppermute | solution.py:43
  36.3 4.3 %collective-permute-start.12 = (bf16[4,32,512]{2,1,0:T(8,128)(2,1)S(1)}, bf16[4,32,512]{2,1,0:T(8,128)(2,1)S(1)}, u32[]{:S(2)}, u32[]{:S(2)}) collective-permute-start(bf16[4,32,512]{2,1,0:T(8,128)(2,1)S(1)} %get-tuple-element.115), channel_id=1, source_target_pairs={{0,1},{1,0},{2,3},{3,2},{4,5},{5,4},{6,7},{7,6},{8,9},{9,8},{10,11... | collective-permute-start | bytes 393224 | tf_op jit(solution)/shard_map/ppermute | solution.py:582
  36.8 3.8 %collective-permute-start.13 = (bf16[4,32,512]{2,1,0:T(8,128)(2,1)S(1)}, bf16[4,32,512]{2,1,0:T(8,128)(2,1)S(1)}, u32[]{:S(2)}, u32[]{:S(2)}) collective-permute-start(bf16[4,32,512]{2,1,0:T(8,128)(2,1)S(1)} %get-tuple-element.116), channel_id=1, source_target_pairs={{0,1},{1,0},{2,3},{3,2},{4,5},{5,4},{6,7},{7,6},{8,9},{9,8},{10,11... | collective-permute-start | bytes 393224 | tf_op jit(solution)/shard_map/ppermute | solution.py:582
  40.5 7.6 %collective-permute-start.14 = (bf16[12,32,256]{2,1,0:T(8,128)(2,1)S(1)}, bf16[12,32,256]{2,1,0:T(8,128)(2,1)S(1)}, u32[]{:S(2)}, u32[]{:S(2)}) collective-permute-start(bf16[12,32,256]{2,1,0:T(8,128)(2,1)S(1)} %get-tuple-element.111.refs_0_), channel_id=1, source_target_pairs={{0,4},{1,5},{2,6},{3,7},{4,0},{5,1},{6,2},{7,3},{8,12},{9,13},{10,... | collective-permute-start | bytes 589832 | tf_op jit(solution)/shard_map/ppermute | solution.py:612
  40.9 10.8 %collective-permute-start.15 = (bf16[10,32,256]{2,1,0:T(8,128)(2,1)S(1)}, bf16[10,32,256]{2,1,0:T(8,128)(2,1)S(1)}, u32[]{:S(2)}, u32[]{:S(2)}) collective-permute-start(bf16[10,32,256]{2,1,0:T(8,128)(2,1)S(1)} %get-tuple-element.117.after_ref), channel_id=1, source_target_pairs={{0,4},{1,5},{2,6},{3,7},{4,0},{5,1},{6,2},{7,3},{8,12},{9,13},{10,... | collective-permute-start | bytes 491528 | tf_op jit(solution)/shard_map/ppermute | solution.py:612
  48.2 8.4 %collective-permute-start.16 = (bf16[9,32,256]{2,1,0:T(8,128)(2,1)S(1)}, bf16[9,32,256]{2,1,0:T(8,128)(2,1)S(1)}, u32[]{:S(2)}, u32[]{:S(2)}) collective-permute-start(bf16[9,32,256]{2,1,0:T(8,128)(2,1)S(1)} %get-tuple-element.120.after_ref), channel_id=1, source_target_pairs={{0,12},{1,13},{2,14},{3,15},{4,8},{5,9},{6,10},{7,11},{8,4},{9,5},... | collective-permute-start | bytes 442376 | tf_op jit(solution)/shard_map/ppermute | solution.py:612
  51.6 5.0 %copy-start.1 = (s32[1,8,16]{2,1,0:T(8,128)S(1)}, s32[1,8,16]{2,1,0:T(8,128)}, u32[]{:S(2)}) copy-start(s32[1,8,16]{2,1,0:T(8,128)} %send_ref.1) | copy-start | bytes 1540
  51.7 6.6 %collective-permute-start.17 = (bf16[5,32,256]{2,1,0:T(8,128)(2,1)S(1)}, bf16[5,32,256]{2,1,0:T(8,128)(2,1)S(1)}, u32[]{:S(2)}, u32[]{:S(2)}) collective-permute-start(bf16[5,32,256]{2,1,0:T(8,128)(2,1)S(1)} %get-tuple-element.122.after_ref), channel_id=1, source_target_pairs={{0,12},{1,13},{2,14},{3,15},{4,8},{5,9},{6,10},{7,11},{8,4},{9,5},... | collective-permute-start | bytes 245768 | tf_op jit(solution)/shard_map/ppermute | solution.py:612
  58.2 1.0 %copy-start = (bf16[2,128,512]{2,1,0:T(8,128)(2,1)S(1)}, bf16[2,128,512]{2,1,0:T(8,128)(2,1)}, u32[]{:S(2)}) copy-start(bf16[2,128,512]{2,1,0:T(8,128)(2,1)} %shard_map.118.after_ref) | copy-start | bytes 786436

commit v6 on v5

--- a/solution.py
+++ b/solution.py
@@ -196,7 +196,10 @@
     refs = refs[extra:]
     locs, halos, refs = refs[:here], refs[here : 2 * here], refs[2 * here :]
     mask_ref, xtf, og_ref = refs[:3]
-    outs, grads, scratch = refs[3:7], refs[7 : 7 + 3 * here], refs[7 + 3 * here :]
+    split = 7 if len(refs) == 15 + 3 * (here - 1) else 6
+    outs, grads, scratch = refs[3:split], refs[split : split + 3 * here], refs[split + 3 * here :]
+    if split == 6:
+        outs = (*outs[:2], outs[2].at[0], outs[2].at[1])
     for i in range(here):
         attend(
             me_ref, locs[i], halos[i], mask_ref, xtf, og_ref, outs, 512 * i,
@@ -310,10 +313,10 @@
             send_own[k, :, last] = wos[i, y, 1 - c, :, lanes].astype(bf16)
 
 
-def node_kernel(groups, skip, me_ref, *refs):
+def node_kernel(groups, skip, *refs):
     refs = refs[skip:]
     dqs, dks, dvs = refs[:groups], refs[groups : 2 * groups], refs[2 * groups : 3 * groups]
-    wq_ref, wk_ref, wv_ref, node_ref, first_ref, second_ref, plus_ref, minus_ref, both = refs[3 * groups :]
+    wq_ref, wk_ref, wv_ref, node_ref, plus_ref, minus_ref, right_ref, left_ref = refs[3 * groups :]
     members, node_rows, _ = dqs[0].shape
     slots = plus_ref.shape[2]
 
@@ -325,19 +328,22 @@
         node_ref[m] = spread[:node_rows] + nt(whole(dqs, m), wq_ref[...])
         halo = spread[node_rows:].astype(bf16)
         for ref, order in (
-            (both.at[0], (1, 4, 7)),
-            (both.at[1], (0, 6, 5)),
-            (plus_ref, (3,)),
-            (minus_ref, (2,)),
+            (plus_ref, (3, 7, 5)),
+            (minus_ref, (2, 4, 6)),
+            (right_ref, (1,)),
+            (left_ref, (0,)),
         ):
             for i, k in enumerate(order):
                 ref[m, i] = halo[k * slots : (k + 1) * slots]
-    to_swaps(both, me_ref[0] % 2, first_ref, second_ref)
 
 
 def sums(owns, core_in, y_in, k):
     total = jnp.concatenate(
-        [own[k] + core[k].astype(f32) for own, core in zip(owns, core_in)], axis=1
+        [
+            own[k] + (core[1, k] if len(core.shape) == 4 else core[k]).astype(f32)
+            for own, core in zip(owns, core_in)
+        ],
+        axis=1,
     ) + y_in[k].astype(f32)
     return [total[:, at : at + 512] for at in range(0, total.shape[1], 512)]
 
@@ -350,9 +356,10 @@
         projection_ref[plane, :, quarter * 128 : (quarter + 1) * 128] = part[:, 384:]
 
 
-def pack_kernel(pieces, after_ref, *refs):
+def pack_kernel(pieces, *refs):
     for i, (ref, core) in enumerate(zip(refs[:pieces], refs[pieces:-1])):
-        refs[-1][:, :, i * 512 : (i + 1) * 512] = (ref[...] + core[...].astype(f32)).astype(bf16)
+        arrived = core[0] if len(core.shape) == 4 else core[...]
+        refs[-1][:, :, i * 512 : (i + 1) * 512] = (ref[...] + arrived.astype(f32)).astype(bf16)
 
 
 def halve(rows, kept_ref, sent_ref):
@@ -375,30 +382,7 @@
     ]
 
 
-def flatten(rows, ref, at):
-    members = rows.shape[0]
-    height = ref.shape[1]
-    for m in range(members):
-        for i in range(3):
-            flat = jnp.concatenate([rows[m, i, :, :256], rows[m, i, :, 256:]], axis=0)
-            each = flat.shape[0] // height
-            start = at + (m * 3 + i) * each
-            ref[start : start + each] = flat.reshape(each, height, 256)
-
-
-def unflatten(ref, at, m, i, slots):
-    each = 2 * slots // ref.shape[1]
-    start = at + (m * 3 + i) * each
-    flat = ref[start : start + each].reshape(2 * slots, 256)
-    return jnp.concatenate([flat[:slots], flat[slots:]], axis=1)
-
-
-def first_kernel(
-    stride, skip, me_ref, *refs
-):
-    refs = refs[skip:]
-    own, core_in, y_in, back_plus, back_minus, first_in, second_in = refs[:7]
-    kept_ref, projection_ref, sent_ref, home_second, came, both = refs[7:]
+def first_kernel(after_ref, own, core_in, y_in, kept_ref, projection_ref, sent_ref):
     planes = own.shape[0]
     rows = []
     for k in range(planes):
@@ -406,14 +390,6 @@
         gather_projection(parts, k, planes, projection_ref, 0)
         rows.append(jnp.concatenate([part[:, :384] for part in parts], axis=1))
     halve(rows, kept_ref, sent_ref)
-    from_swaps(came, me_ref[0] % 2, first_in, second_in)
-    for side, own_rows in enumerate((back_plus, back_minus)):
-        both[side, :, 0:1] = own_rows[...]
-        both[side, :, 1:2] = came[1, :, 2 - side : 3 - side]
-        both[side, :, 2:3] = came[0, :, 2 - side : 3 - side]
-    odd = me_ref[0] // stride % 2
-    flatten(both[odd], sent_ref, planes // 2 * rows[0].shape[1] // 256)
-    flatten(both[1 - odd], home_second, 0)
 
 
 def second_kernel(skip, pieces, me_ref, *refs):
@@ -439,32 +415,22 @@
     )
 
 
-def step_kernel(extra, after_ref, kept_in, received, *refs):
-    kept_ref, sent_ref = refs[-2:]
+def step_kernel(after_ref, kept_in, received, kept_ref, sent_ref):
     halve(add_received(kept_in, received), kept_ref, sent_ref)
-    if extra:
-        sent_ref[sent_ref.shape[0] - extra :] = refs[0][...]
 
 
 def finish_kernel(
-    stride, at_first, at_second, me_ref, after_ref, send_ref, node_ref, first_in, second_in,
-    home_first, home_second, out_ref, came, home,
+    me_ref, after_ref, send_ref, node_ref, plus_ref, minus_ref, first_in, second_in, out_ref, came
 ):
     members, node_rows, _ = node_ref.shape
-    slots = first_in.shape[2]
     pick = sent_selector(send_ref[0], node_rows).astype(bf16)
     from_swaps(came, me_ref[0] % 2, first_in, second_in)
-    odd = me_ref[0] // stride % 2
-    for m in range(members):
-        for i in range(3):
-            home[1 - odd, m, i] = unflatten(home_first, at_first, m, i, slots)
-            home[odd, m, i] = unflatten(home_second, at_second, m, i, slots)
     for m in range(members):
         pieces = [None] * 8
-        pieces[0], pieces[1] = came[1, m, 0], came[0, m, 0]
-        for side, order in enumerate(((3, 5, 7), (2, 6, 4))):
+        for side, order in enumerate(((1, 4, 7), (0, 6, 5))):
             for i, k in enumerate(order):
-                pieces[k] = home[side, m, i]
+                pieces[k] = came[side, m, i]
+        pieces[2], pieces[3] = plus_ref[m, 0], minus_ref[m, 0]
         arriving = jnp.concatenate(pieces, axis=0)
         out_ref[m] = (node_ref[m] + nn(pick, arriving)).astype(bf16)
 
@@ -482,7 +448,7 @@
     out_ref[:, 3 * width :] = b[:, 384 * half :]
 
 
-def call(kernel, outs, operands, specs=None, scratch=(), limit=12, final=False):
+def call(kernel, outs, operands, specs=None, scratch=(), limit=12, final=False, flops=10**6):
     specs = list(specs or ())
     specs += [pltpu.VMEM] * (len(operands) - len(specs))
     operands = [
@@ -495,7 +461,7 @@
         in_specs=[pl.BlockSpec(memory_space=s) for s in specs],
         scratch_shapes=list(scratch),
         compiler_params=pltpu.CompilerParams(vmem_limit_bytes=limit * MIB),
-        cost_estimate=pl.CostEstimate(flops=10**6, bytes_accessed=10**4, transcendentals=0),
+        cost_estimate=pl.CostEstimate(flops=flops, bytes_accessed=10**4, transcendentals=0),
     )(*operands)
 
 
@@ -555,11 +521,13 @@
     flop = [(i, i ^ 2) for i in range(count)]
     grads = []
 
-    def attention(extra, which):
+    def attention(extra, which, together):
         wide = 512 * len(which)
+        sends = [((2, planes, rows, wide), bf16)] if together else [((planes, rows, wide), bf16)] * 2
         outs = call(
             functools.partial(attention_kernel, len(extra), len(which)),
-            [((planes, rows, wide), kind) for kind in (f32, f32, bf16, bf16)]
+            [((planes, rows, wide), f32)] * 2
+            + sends
             + [
                 ((members, node_rows, 128), bf16),
                 ((members, table, 128), bf16),
@@ -577,90 +545,80 @@
             ],
             limit=24,
         )
-        grads.extend(outs[4:])
-        own, other, send_other, send_own = outs[:4]
-        return own, other, lax.ppermute(send_other, "patch", flip), lax.ppermute(send_own, "patch", flip)
+        sent = outs[2 : 2 + len(sends)]
+        grads.extend(outs[2 + len(sends) :])
+        arrived = [lax.ppermute(shard, "patch", flip) for shard in sent]
+        return outs[0], outs[1], arrived[0], arrived[-1]
 
     half = groups // 2
     wide = 384 * half
-    own_a, other, core_other, core_own = attention((), range(half))
+    own_a, other, core_other, core_own = attention((), range(half), False)
     y_sent = (other + core_other.astype(f32)).astype(bf16)
     y_a = lax.ppermute(y_sent, "patch", flop)
     later = []
     for g in range(half, groups):
-        later.append(attention((y_sent,) if g == groups - 1 else (), range(g, g + 1)))
+        last = g == groups - 1
+        later.append(attention((y_sent,) if last else (), range(g, g + 1), not last))
     own_b, other_b, core_other_b, core_own_b = zip(*later)
     (y_sent,) = call(
         functools.partial(pack_kernel, len(later)), [(y_sent.shape, bf16)],
-        (y_a, *other_b, *core_other_b), specs=[pl.ANY],
+        (*other_b, *core_other_b),
     )
     y_b = lax.ppermute(y_sent, "patch", flop)
-    node, *outgoing, back_plus, back_minus = call(
+    def exchange(sent, bit):
+        return lax.ppermute(sent, "patch", along_z(count, bit))
+
+    def halves(wide, bit):
+        left = planes >> (bit + 1)
+        return [((left, rows, wide), f32), ((left * wide // 256, rows, 256), bf16)]
+
+    kept_a, sent_a = halves(wide, 0)
+    kept_a, out_a, sent_a = call(
+        first_kernel, [kept_a, ((half * inner_planes, rows, width), f32), sent_a],
+        (y_sent, own_a, core_own, y_a), specs=[pl.ANY],
+    )
+    in_a = exchange(sent_a, 0)
+    node, to_plus, to_minus, own_right, own_left = call(
         functools.partial(node_kernel, groups, 1),
         [((members, node_rows, width), f32), three, three, one, one],
-        (place, y_sent, *grads[0::3], *grads[1::3], *grads[2::3], wq, wk, wv),
+        (sent_a, *grads[0::3], *grads[1::3], *grads[2::3], wq, wk, wv),
+        specs=[pl.ANY], flops=2 * 10**10,
+    )
+    from_plus = shifted(to_minus, -row_width)
+    from_minus = shifted(to_plus, row_width)
+    outgoing = call(
+        relay_kernel, [three, three],
+        (place, in_a, own_right, own_left, from_plus, from_minus),
         specs=[pltpu.SMEM, pl.ANY], scratch=[trio],
     )
     back = swap(outgoing, 1)
-
-    steps = planes.bit_length() - 1
-    homeward = neighbours_apart(count, row_width)
-    more = members * 6 * slots // rows
-    rides = [along_z(count, i) == homeward[i] if i < steps else False for i in range(2)]
-
-    def exchange(sent, bit):
-        return lax.ppermute(sent, "patch", along_z(count, bit))
-
-    def halves(wide, bit, riders=0):
-        left = planes >> (bit + 1)
-        return [((left, rows, wide), f32), ((left * wide // 256 + riders, rows, 256), bf16)]
-
-    kept_a, projected = halves(wide, 0, more)
-    kept_a, out_a, sent, home_second = call(
-        functools.partial(first_kernel, row_width, 1),
-        [kept_a, ((half * inner_planes, rows, width), f32), projected, ((more, rows, 256), bf16)],
-        (place, y_sent, own_a, core_own, y_a, back_plus, back_minus, *back),
-        specs=[pltpu.SMEM, pl.ANY], scratch=[trio, trio],
-    )
-    in_a = exchange(sent, 0)
-    home_first = in_a if rides[0] else lax.ppermute(sent, "patch", homeward[0])
-    at_first, at_second = planes // 2 * wide // 256, 0
-    kept_b, sent_b = call(
-        functools.partial(second_kernel, 1, len(later)), halves(wide + width, 0),
-        (place, sent, out_a, y_b, *own_b, *core_own_b),
-        specs=[pltpu.SMEM, pl.ANY],
-        scratch=[pltpu.VMEM((planes, rows, width), f32)],
-    )
-    in_b = exchange(sent_b, 0)
-    after = sent_b
-    for bit in range(1, steps):
-        riding = bit == 1 and rides[1]
-        kept_a, after = call(
-            functools.partial(step_kernel, more if riding else 0),
-            halves(wide, bit, more if riding else 0),
-            (after, kept_a, in_a) + ((home_second,) if riding else ()),
-            specs=[pl.ANY],
-        )
-        in_a = exchange(after, bit)
-        if riding:
-            home_second = in_a
-            at_second = (planes >> (bit + 1)) * wide // 256
-        kept_b, after = call(
-            functools.partial(step_kernel, 0), halves(wide + width, bit),
-            (after, kept_b, in_b), specs=[pl.ANY],
-        )
-        in_b = exchange(after, bit)
-    if not rides[1]:
-        home_second = lax.ppermute(home_second, "patch", homeward[1])
+    after = outgoing[0]
+    for bit in range(1, planes.bit_length()):
+        if bit < planes.bit_length() - 1:
+            kept_a, after = call(
+                step_kernel, halves(wide, bit), (after, kept_a, in_a), specs=[pl.ANY]
+            )
+            in_a = exchange(after, bit)
+        if bit == 1:
+            kept_b, after = call(
+                functools.partial(second_kernel, 1, len(later)), halves(wide + width, 0),
+                (place, after, out_a, y_b, *own_b, *core_own_b),
+                specs=[pltpu.SMEM, pl.ANY],
+                scratch=[pltpu.VMEM((planes, rows, width), f32)],
+            )
+        else:
+            kept_b, after = call(
+                step_kernel, halves(wide + width, bit - 1), (after, kept_b, in_b), specs=[pl.ANY]
+            )
+        in_b = exchange(after, bit - 1)
     (node_grad,) = call(
-        functools.partial(finish_kernel, row_width, at_first, at_second),
-        [((members, node_rows, width), bf16)],
-        (place, after, send_rows, node, *back, home_first, home_second),
-        specs=[pltpu.SMEM, pl.ANY], scratch=[trio, trio], final=True,
+        finish_kernel, [((members, node_rows, width), bf16)],
+        (place, after, send_rows, node, from_plus, from_minus, *back),
+        specs=[pltpu.SMEM, pl.ANY], scratch=[trio], final=True,
     )
     (weight_grad,) = call(
         weight_kernel, [((rows, 4 * width), f32)], (node_grad, kept_a, in_a, kept_b, in_b),
-        specs=[pl.ANY], final=True,
+        specs=[pltpu.HBM], final=True,
     )
     return (node_grad, weight_grad)
 

time: 60.2 us -> 58.2 us (0.967)
  waiting for transfers between devices: 24.5 us -> 18.8 us
  starting transfers between devices: 18 us -> 22.8 us
  local copies, waits for them, and re-layouts: 0.95 us -> 0.01 us
    ppermute x4, waiting for transfers between devices: 11.7 us -> 4.05 us  [exchange(): return lax.ppermute(sent, 'patch', along_z(count, bit))]
    ppermute x2 -> x4, waiting for transfers between devices: 1.62 us -> 8.13 us  [shifted(): lax.ppermute(shard, 'patch', [(i, (i + by) % count) for i in range(count)])]
    ppermute x4, waiting for transfers between devices: 5.47 us -> 1.91 us  [swap(): lax.ppermute(shard, 'patch', perm)]
    ppermute x2 -> x4, starting transfers between devices: 5.17 us -> 7.42 us  [shifted(): lax.ppermute(shard, 'patch', [(i, (i + by) % count) for i in range(count)])]
    ppermute x1, starting transfers between devices: 0.35 us -> 2 us  [body(): y_b = lax.ppermute(y_sent, 'patch', flop)]
    ppermute x6 -> x5, waiting for transfers between devices: 2.38 us -> 0.88 us  [attention(): arrived = [lax.ppermute(shard, 'patch', flip) for shard in sent]]
    unnamed x4 -> x2, local copies, waits for them, and re-layouts: 0.95 us -> 0.01 us
    ppermute x6 -> x5, starting transfers between devices: 1.36 us -> 1.28 us  [attention(): arrived = [lax.ppermute(shard, 'patch', flip) for shard in sent]]
  transfers between devices with their start and end apart: 18 -> 19, of which waited for: 12 -> 10; matrix products, arithmetic and copies ran while one was open for 0% -> 0% of each run, Pallas kernels for 16% -> 17%
where the time goes in v6:
time: 58.2 us; the launch traced here: 58 us
  starting transfers between devices  22.8 us (39%)
  waiting for transfers between devices  18.8 us (32%)
  Pallas kernels  15.6 us (27%)
  between operations  0.78 us (1%)
    pallas_call x17, Pallas kernels, call(): pl.pallas_call(kernel, out_shape=[jax.ShapeDtypeStruct(*o) if final else...  15.6 us
    ppermute x4, waiting for transfers between devices, shifted(): lax.ppermute(shard, 'patch', [(i, (i + by) % count) for i in range(count)])  8.13 us
    ppermute x4, starting transfers between devices, shifted(): lax.ppermute(shard, 'patch', [(i, (i + by) % count) for i in range(count)])  7.42 us
    ppermute x4, starting transfers between devices, swap(): lax.ppermute(shard, 'patch', perm)  6.71 us
    ppermute x4, starting transfers between devices, exchange(): return lax.ppermute(sent, 'patch', along_z(count, bit))  5.3 us
    ppermute x4, waiting for transfers between devices, exchange(): return lax.ppermute(sent, 'patch', along_z(count, bit))  4.05 us
    ppermute x1, waiting for transfers between devices, body(): y_a = lax.ppermute(y_sent, 'patch', flop)  3.83 us
    ppermute x1, starting transfers between devices, body(): y_b = lax.ppermute(y_sent, 'patch', flop)  2 us
  transfers between devices with their start and end apart: 19, of which 10 were waited for; matrix products, arithmetic and copies ran while one was open for 0% of the time, Pallas kernels for 17%

profile of v6, /device:TPU:0, one launch (start us, length us, event | category | flops | bytes accessed | tf_op | source)
XLA Modules:
  0.0 58.0 jit_solution(13980681736539754327)
XLA Ops:
  0.6 1.2 %shard_map.104 = (bf16[2,3,16,512]{3,2,1,0:T(8,128)(2,1)S(1)}, bf16[2,3,16,512]{3,2,1,0:T(8,128)(2,1)S(1)}, bf16[2,1,16,512]{3,2,1,0:T(8,128)(2,1)S(1)}, bf16[2,...) custom-call(s32[1,8,16]{2,1,0:T(8,128)} %send_ref.1, bf16[2,128,512]{2,1,0:T(8,128)(2,1)} %x_hbm.1), custom_call_target="tpu_custom_call" | custom-call | flops 1000000 | bytes 10000 | tf_op jit(solution)/shard_map/pallas_call | solution.py:458
  1.8 3.1 %collective-permute-start = (bf16[2,3,16,512]{3,2,1,0:T(8,128)(2,1)S(1)}, bf16[2,3,16,512]{3,2,1,0:T(8,128)(2,1)S(1)}, u32[]{:S(2)}, u32[]{:S(2)}) collective-permute-start(bf16[2,3,16,512]{3,2,1,0:T(8,128)(2,1)S(1)} %get-tuple-element.67), channel_id=1, source_target_pairs={{0,4},{1,5},{2,6},{3,7},{4,8},{5,9},{6,10},{7,11},{8,12},{9,13},{1... | collective-permute-start | bytes 294920 | tf_op jit(solution)/shard_map/ppermute | solution.py:28
  4.9 2.1 %collective-permute-start.1 = (bf16[2,3,16,512]{3,2,1,0:T(8,128)(2,1)S(1)}, bf16[2,3,16,512]{3,2,1,0:T(8,128)(2,1)S(1)}, u32[]{:S(2)}, u32[]{:S(2)}) collective-permute-start(bf16[2,3,16,512]{3,2,1,0:T(8,128)(2,1)S(1)} %get-tuple-element.68), channel_id=1, source_target_pairs={{0,12},{1,13},{2,14},{3,15},{4,0},{5,1},{6,2},{7,3},{8,4},{9,5},{1... | collective-permute-start | bytes 294920 | tf_op jit(solution)/shard_map/ppermute | solution.py:28
  7.0 2.6 %shard_map.105 = (bf16[8,2,128,128]{3,2,1,0:T(8,128)(2,1)S(1)}, bf16[8,2,128,128]{3,2,1,0:T(8,128)(2,1)S(1)}, bf16[8,2,128,128]{3,2,1,0:T(8,128)(2,1)S(1)}, bf16...) custom-call(bf16[2,1,16,512]{3,2,1,0:T(8,128)(2,1)S(1)} %get-tuple-e, ...), custom_call_target="tpu_custom_call" | custom-call | flops 1000000 | bytes 10000 | tf_op jit(solution)/shard_map/pallas_call | solution.py:458
  9.7 0.8 %collective-permute-done.plus_ref = bf16[2,3,16,512]{3,2,1,0:T(8,128)(2,1)S(1)} collective-permute-done((bf16[2,3,16,512]{3,2,1,0:T(8,128)(2,1)S(1)}, bf16[2,3,16,512]{3,2,1,0:T(8,128)(2,1)S(1)}, u32[]{:S(2)}, u32[]{:S(2)}) %collective-permute-start) | collective-permute-done | bytes 98336 | tf_op jit(solution)/shard_map/ppermute | solution.py:28
  10.4 0.8 %collective-permute-done.1.minus_ref = bf16[2,3,16,512]{3,2,1,0:T(8,128)(2,1)S(1)} collective-permute-done((bf16[2,3,16,512]{3,2,1,0:T(8,128)(2,1)S(1)}, bf16[2,3,16,512]{3,2,1,0:T(8,128)(2,1)S(1)}, u32[]{:S(2)}, u32[]{:S(2)}) %collective-permute-start.1) | collective-permute-done | bytes 98336 | tf_op jit(solution)/shard_map/ppermute | solution.py:28
  11.3 0.1 collective-permute-start.2
  11.4 3.4 %collective-permute-start.3 = (bf16[2,3,16,512]{3,2,1,0:T(8,128)(2,1)S(1)}, bf16[2,3,16,512]{3,2,1,0:T(8,128)(2,1)S(1)}, u32[]{:S(2)}, u32[]{:S(2)}) collective-permute-start(bf16[2,3,16,512]{3,2,1,0:T(8,128)(2,1)S(1)} %get-tuple-element.72), channel_id=1, source_target_pairs={{0,15},{1,2},{2,1},{3,4},{4,3},{5,6},{6,5},{7,8},{8,7},{9,10},{10,... | collective-permute-start | bytes 294920 | tf_op jit(solution)/shard_map/ppermute | solution.py:43
  14.8 1.4 %shard_map.108.refs_2_.refs_4_.refs_3_ = f32[256,128]{1,0:T(8,128)S(1)} custom-call(bf16[2,3,16,512]{3,2,1,0:T(8,128)(2,1)S(1)} %get-tuple-element.71.after_ref, s32[128,256]{1,0:T(8,128)S(1)} %get-tuple-element.77.neigh_ref, s32[1,128]{1,0:T(1,128)S(1)} %get-tuple-element.78.count_ref), custom_call_target="tpu_custom_call" | custom-call | flops 1000000 | bytes 10000 | tf_op jit(solution)/shard_map/pallas_call | solution.py:458
  16.3 0.0 collective-permute-done.2.first_in
  16.3 1.9 %collective-permute-done.3.second_in = bf16[2,3,16,512]{3,2,1,0:T(8,128)(2,1)S(1)} collective-permute-done((bf16[2,3,16,512]{3,2,1,0:T(8,128)(2,1)S(1)}, bf16[2,3,16,512]{3,2,1,0:T(8,128)(2,1)S(1)}, u32[]{:S(2)}, u32[]{:S(2)}) %collective-permute-start.3) | collective-permute-done | bytes 98336 | tf_op jit(solution)/shard_map/ppermute | solution.py:43
  18.2 0.6 %shard_map.107 = (bf16[4,2,128,128]{3,2,1,0:T(8,128)(2,1)S(1)}, bf16[4,2,128,128]{3,2,1,0:T(8,128)(2,1)S(1)}, bf16[4,2,128,128]{3,2,1,0:T(8,128)(2,1)S(1)}, bf16...) custom-call(s32[1]{0:T(128)} %bitcast.me_ref, bf16[2,3,16,512]{3,2,1,0:T(8,128)(2,1)S(1)} %collective-permute-done.plus_ref, ...), custom_call_target="tpu_custom_call" | custom-call | flops 1000000 | bytes 10000 | tf_op jit(solution)/shard_map/pallas_call | solution.py:458
  18.8 3.1 %shard_map.110 = (f32[4,32,1024]{2,1,0:T(8,128)S(1)}, f32[4,32,1024]{2,1,0:T(8,128)S(1)}, bf16[4,32,1024]{2,1,0:T(8,128)(2,1)S(1)}, bf16[4,32,1024]{2,1,0:T(8,12...) custom-call(s32[1]{0:T(128)} %bitcast.me_ref, ...), custom_call_target="tpu_custom_call" | custom-call | flops 1000000 | bytes 10000 | tf_op jit(solution)/shard_map/pallas_call | solution.py:458
  22.0 0.1 collective-permute-start.4
  22.0 1.7 %shard_map.109 = (f32[4,32,512]{2,1,0:T(8,128)S(1)}, f32[4,32,512]{2,1,0:T(8,128)S(1)}, bf16[2,4,32,512]{3,2,1,0:T(8,128)(2,1)S(1)}, bf16[2,128,128]{2,1,0:T(8,1...) custom-call(s32[1]{0:T(128)} %bitcast.me_ref, ...), custom_call_target="tpu_custom_call" | custom-call | flops 1000000 | bytes 10000 | tf_op jit(solution)/shard_map/pallas_call | solution.py:458
  23.7 0.6 collective-permute-start.5
  24.3 0.1 collective-permute-start.7
  24.4 0.0 collective-permute-done.4
  24.4 0.1 add_convert_fusion.refs_0_
  24.5 0.1 collective-permute-start.8
  24.6 1.7 %shard_map.111 = (f32[4,32,512]{2,1,0:T(8,128)S(1)}, f32[4,32,512]{2,1,0:T(8,128)S(1)}, bf16[4,32,512]{2,1,0:T(8,128)(2,1)S(1)}, bf16[4,32,512]{2,1,0:T(8,128)(2...) custom-call(s32[1]{0:T(128)} %bitcast.me_ref, ...), custom_call_target="tpu_custom_call" | custom-call | flops 1000000 | bytes 10000 | tf_op jit(solution)/shard_map/pallas_call | solution.py:458
  26.3 0.5 collective-permute-start.6
  26.7 0.1 collective-permute-start.13
  26.9 0.0 collective-permute-done.5.refs_2_.refs_5_
  26.9 0.9 %collective-permute-done.6.refs_3_ = bf16[4,32,512]{2,1,0:T(8,128)(2,1)S(1)} collective-permute-done((bf16[4,32,512]{2,1,0:T(8,128)(2,1)S(1)}, bf16[4,32,512]{2,1,0:T(8,128)(2,1)S(1)}, u32[]{:S(2)}, u32[]{:S(2)}) %collective-permute-start.6) | collective-permute-done | bytes 131104 | tf_op jit(solution)/shard_map/ppermute | solution.py:550
  27.7 0.1 shard_map.112.after_ref
  27.8 2.0 %collective-permute-start.12 = (bf16[4,32,1024]{2,1,0:T(8,128)(2,1)S(1)}, bf16[4,32,1024]{2,1,0:T(8,128)(2,1)S(1)}, u32[]{:S(2)}, u32[]{:S(2)}) collective-permute-start(bf16[4,32,1024]{2,1,0:T(8,128)(2,1)S(1)} %shard_map.112.after_ref), channel_id=1, source_target_pairs={{0,2},{1,3},{2,0},{3,1},{4,6},{5,7},{6,4},{7,5},{8,10},{9,11},{10,... | collective-permute-start | bytes 786440 | tf_op jit(solution)/shard_map/ppermute | solution.py:567
  29.8 0.0 collective-permute-done.7.core_in
  29.8 3.8 %collective-permute-done.8.y_in = bf16[4,32,1024]{2,1,0:T(8,128)(2,1)S(1)} collective-permute-done((bf16[4,32,1024]{2,1,0:T(8,128)(2,1)S(1)}, bf16[4,32,1024]{2,1,0:T(8,128)(2,1)S(1)}, u32[]{:S(2)}, u32[]{:S(2)}) %collective-permute-start.8) | collective-permute-done | bytes 262176 | tf_op jit(solution)/shard_map/ppermute | solution.py:557
  33.6 0.1 shard_map.113
  33.7 1.0 %shard_map.114 = (f32[2,128,512]{2,1,0:T(8,128)S(1)}, bf16[2,3,16,512]{3,2,1,0:T(8,128)(2,1)S(1)}, bf16[2,3,16,512]{3,2,1,0:T(8,128)(2,1)S(1)}, bf16[2,1,16,512]...) custom-call(bf16[6,32,256]{2,1,0:T(8,128)(2,1)S(1)} %get-tuple-element.94.refs_0_, ...), custom_call_target="tpu_custom_call" | custom-call | flops 20000000000 | bytes 10000 | tf_op jit(solution)/shard_map/pallas_call | solution.py:458
  34.8 2.2 %collective-permute-start.10 = (bf16[2,3,16,512]{3,2,1,0:T(8,128)(2,1)S(1)}, bf16[2,3,16,512]{3,2,1,0:T(8,128)(2,1)S(1)}, u32[]{:S(2)}, u32[]{:S(2)}) collective-permute-start(bf16[2,3,16,512]{3,2,1,0:T(8,128)(2,1)S(1)} %get-tuple-element.110), channel_id=1, source_target_pairs={{0,12},{1,13},{2,14},{3,15},{4,0},{5,1},{6,2},{7,3},{8,4},{9,5},{1... | collective-permute-start | bytes 294920 | tf_op jit(solution)/shard_map/ppermute | solution.py:28
  37.0 0.0 collective-permute-start.9
  37.0 4.5 %collective-permute-done.10.plus_ref = bf16[2,3,16,512]{3,2,1,0:T(8,128)(2,1)S(1)} collective-permute-done((bf16[2,3,16,512]{3,2,1,0:T(8,128)(2,1)S(1)}, bf16[2,3,16,512]{3,2,1,0:T(8,128)(2,1)S(1)}, u32[]{:S(2)}, u32[]{:S(2)}) %collective-permute-start.10) | collective-permute-done | bytes 98336 | tf_op jit(solution)/shard_map/ppermute | solution.py:28
  41.5 2.0 %collective-permute-done.11.minus_ref = bf16[2,3,16,512]{3,2,1,0:T(8,128)(2,1)S(1)} collective-permute-done((bf16[2,3,16,512]{3,2,1,0:T(8,128)(2,1)S(1)}, bf16[2,3,16,512]{3,2,1,0:T(8,128)(2,1)S(1)}, u32[]{:S(2)}, u32[]{:S(2)}) %collective-permute-start.11) | collective-permute-done | bytes 98336 | tf_op jit(solution)/shard_map/ppermute | solution.py:28
  43.5 0.1 collective-permute-done.9.after_ref.received
  43.7 0.0 collective-permute-done.12.refs_2_
  43.7 0.1 shard_map.117
  43.8 1.4 %collective-permute-start.14 = (bf16[10,32,256]{2,1,0:T(8,128)(2,1)S(1)}, bf16[10,32,256]{2,1,0:T(8,128)(2,1)S(1)}, u32[]{:S(2)}, u32[]{:S(2)}) collective-permute-start(bf16[10,32,256]{2,1,0:T(8,128)(2,1)S(1)} %get-tuple-element.119.after_ref), channel_id=1, source_target_pairs={{0,4},{1,5},{2,6},{3,7},{4,0},{5,1},{6,2},{7,3},{8,12},{9,13},{10,... | collective-permute-start | bytes 491528 | tf_op jit(solution)/shard_map/ppermute | solution.py:569
  45.2 3.2 %collective-permute-start.16 = (bf16[2,3,16,512]{3,2,1,0:T(8,128)(2,1)S(1)}, bf16[2,3,16,512]{3,2,1,0:T(8,128)(2,1)S(1)}, u32[]{:S(2)}, u32[]{:S(2)}) collective-permute-start(bf16[2,3,16,512]{3,2,1,0:T(8,128)(2,1)S(1)} %get-tuple-element.123), channel_id=1, source_target_pairs={{0,15},{1,2},{2,1},{3,4},{4,3},{5,6},{6,5},{7,8},{8,7},{9,10},{10,... | collective-permute-start | bytes 294920 | tf_op jit(solution)/shard_map/ppermute | solution.py:43
  48.4 0.8 %collective-permute-done.14.received = bf16[10,32,256]{2,1,0:T(8,128)(2,1)S(1)} collective-permute-done((bf16[10,32,256]{2,1,0:T(8,128)(2,1)S(1)}, bf16[10,32,256]{2,1,0:T(8,128)(2,1)S(1)}, u32[]{:S(2)}, u32[]{:S(2)}) %collective-permute-start.14) | collective-permute-done | bytes 163872 | tf_op jit(solution)/shard_map/ppermute | solution.py:569
  49.3 2.1 %collective-permute-start.18 = (bf16[5,32,256]{2,1,0:T(8,128)(2,1)S(1)}, bf16[5,32,256]{2,1,0:T(8,128)(2,1)S(1)}, u32[]{:S(2)}, u32[]{:S(2)}) collective-permute-start(bf16[5,32,256]{2,1,0:T(8,128)(2,1)S(1)} %get-tuple-element.121.after_ref), channel_id=1, source_target_pairs={{0,12},{1,13},{2,14},{3,15},{4,8},{5,9},{6,10},{7,11},{8,4},{9,5},... | collective-permute-start | bytes 245768 | tf_op jit(solution)/shard_map/ppermute | solution.py:569
  51.4 1.7 %collective-permute-start.17 = (bf16[3,32,256]{2,1,0:T(8,128)(2,1)S(1)}, bf16[3,32,256]{2,1,0:T(8,128)(2,1)S(1)}, u32[]{:S(2)}, u32[]{:S(2)}) collective-permute-start(bf16[3,32,256]{2,1,0:T(8,128)(2,1)S(1)} %get-tuple-element.114.refs_0_), channel_id=1, source_target_pairs={{0,12},{1,13},{2,14},{3,15},{4,8},{5,9},{6,10},{7,11},{8,4},{9,5},... | collective-permute-start | bytes 147464 | tf_op jit(solution)/shard_map/ppermute | solution.py:569
  53.2 0.0 collective-permute-done.16.second_in
  53.2 1.0 %shard_map.119.after_ref = bf16[2,128,512]{2,1,0:T(8,128)(2,1)} custom-call(s32[1]{0:T(128)} %bitcast.me_ref, bf16[5,32,256]{2,1,0:T(8,128)(2,1)S(1)} %get-tuple-element.121.after_ref, s32[1,8,16]{2,1,0:T(8,128)S(1)} %copy-done, f32[2,128,512]{2,1,0:T(8,128)S(1)} %get-tuple-element.122.node_ref, ...), custom_call_target="tpu_custom_call" | custom-call | flops 1000000 | bytes 10000 | tf_op jit(solution)/shard_map/pallas_call | solution.py:458
  54.2 3.1 %collective-permute-done.17.in_a = bf16[3,32,256]{2,1,0:T(8,128)(2,1)S(1)} collective-permute-done((bf16[3,32,256]{2,1,0:T(8,128)(2,1)S(1)}, bf16[3,32,256]{2,1,0:T(8,128)(2,1)S(1)}, u32[]{:S(2)}, u32[]{:S(2)}) %collective-permute-start.17) | collective-permute-done | bytes 49184 | tf_op jit(solution)/shard_map/ppermute | solution.py:569
  57.3 0.0 collective-permute-done.18.in_b
  57.3 0.7 %shard_map.120 = f32[32,2048]{1,0:T(8,128)} custom-call(bf16[2,128,512]{2,1,0:T(8,128)(2,1)} %shard_map.119.after_ref, f32[1,32,768]{2,1,0:T(8,128)S(1)} %get-tuple-element.124.kept_a, bf16[3,32,256]{2,1,0:T(8,128)(2,1)S(1)} %collective-permute-done.17.in_a, f32[1,32,1280]{2,1,0:T(8,128)S(1)} %get-tuple-element.125.kept_b, ...), custom_call_target="tpu_custom_call" | custom-call | flops 1000000 | bytes 10000 | tf_op jit(solution)/shard_map/pallas_call | solution.py:458
  (10 shorter events, 0.1 us)
Async XLA Ops:
  1.8 8.6 %collective-permute-start = (bf16[2,3,16,512]{3,2,1,0:T(8,128)(2,1)S(1)}, bf16[2,3,16,512]{3,2,1,0:T(8,128)(2,1)S(1)}, u32[]{:S(2)}, u32[]{:S(2)}) collective-permute-start(bf16[2,3,16,512]{3,2,1,0:T(8,128)(2,1)S(1)} %get-tuple-element.67), channel_id=1, source_target_pairs={{0,4},{1,5},{2,6},{3,7},{4,8},{5,9},{6,10},{7,11},{8,12},{9,13},{1... | collective-permute-start | bytes 294920 | tf_op jit(solution)/shard_map/ppermute | solution.py:28
  4.9 6.4 %collective-permute-start.1 = (bf16[2,3,16,512]{3,2,1,0:T(8,128)(2,1)S(1)}, bf16[2,3,16,512]{3,2,1,0:T(8,128)(2,1)S(1)}, u32[]{:S(2)}, u32[]{:S(2)}) collective-permute-start(bf16[2,3,16,512]{3,2,1,0:T(8,128)(2,1)S(1)} %get-tuple-element.68), channel_id=1, source_target_pairs={{0,12},{1,13},{2,14},{3,15},{4,0},{5,1},{6,2},{7,3},{8,4},{9,5},{1... | collective-permute-start | bytes 294920 | tf_op jit(solution)/shard_map/ppermute | solution.py:28
  11.3 5.0 %collective-permute-start.2 = (bf16[2,3,16,512]{3,2,1,0:T(8,128)(2,1)S(1)}, bf16[2,3,16,512]{3,2,1,0:T(8,128)(2,1)S(1)}, u32[]{:S(2)}, u32[]{:S(2)}) collective-permute-start(bf16[2,3,16,512]{3,2,1,0:T(8,128)(2,1)S(1)} %get-tuple-element.71.after_ref), channel_id=1, source_target_pairs={{0,1},{1,0},{2,3},{3,2},{4,5},{5,4},{6,7},{7,6},{8,9},{9,8},{10,11... | collective-permute-start | bytes 294920 | tf_op jit(solution)/shard_map/ppermute | solution.py:43
  11.4 6.8 %collective-permute-start.3 = (bf16[2,3,16,512]{3,2,1,0:T(8,128)(2,1)S(1)}, bf16[2,3,16,512]{3,2,1,0:T(8,128)(2,1)S(1)}, u32[]{:S(2)}, u32[]{:S(2)}) collective-permute-start(bf16[2,3,16,512]{3,2,1,0:T(8,128)(2,1)S(1)} %get-tuple-element.72), channel_id=1, source_target_pairs={{0,15},{1,2},{2,1},{3,4},{4,3},{5,6},{6,5},{7,8},{8,7},{9,10},{10,... | collective-permute-start | bytes 294920 | tf_op jit(solution)/shard_map/ppermute | solution.py:43
  22.0 2.4 %collective-permute-start.4 = (bf16[4,32,1024]{2,1,0:T(8,128)(2,1)S(1)}, bf16[4,32,1024]{2,1,0:T(8,128)(2,1)S(1)}, u32[]{:S(2)}, u32[]{:S(2)}) collective-permute-start(bf16[4,32,1024]{2,1,0:T(8,128)(2,1)S(1)} %get-tuple-element.86), channel_id=1, source_target_pairs={{0,1},{1,0},{2,3},{3,2},{4,5},{5,4},{6,7},{7,6},{8,9},{9,8},{10,11... | collective-permute-start | bytes 786440 | tf_op jit(solution)/shard_map/ppermute | solution.py:550
  23.7 3.1 %collective-permute-start.5 = (bf16[2,4,32,512]{3,2,1,0:T(8,128)(2,1)S(1)}, bf16[2,4,32,512]{3,2,1,0:T(8,128)(2,1)S(1)}, u32[]{:S(2)}, u32[]{:S(2)}) collective-permute-start(bf16[2,4,32,512]{3,2,1,0:T(8,128)(2,1)S(1)} %get-tuple-element.90), channel_id=1, source_target_pairs={{0,1},{1,0},{2,3},{3,2},{4,5},{5,4},{6,7},{7,6},{8,9},{9,8},{10,11... | collective-permute-start | bytes 786440 | tf_op jit(solution)/shard_map/ppermute | solution.py:550
  24.3 5.5 %collective-permute-start.7 = (bf16[4,32,1024]{2,1,0:T(8,128)(2,1)S(1)}, bf16[4,32,1024]{2,1,0:T(8,128)(2,1)S(1)}, u32[]{:S(2)}, u32[]{:S(2)}) collective-permute-start(bf16[4,32,1024]{2,1,0:T(8,128)(2,1)S(1)} %get-tuple-element.93), channel_id=1, source_target_pairs={{0,1},{1,0},{2,3},{3,2},{4,5},{5,4},{6,7},{7,6},{8,9},{9,8},{10,11... | collective-permute-start | bytes 786440 | tf_op jit(solution)/shard_map/ppermute | solution.py:550
  24.5 9.2 %collective-permute-start.8 = (bf16[4,32,1024]{2,1,0:T(8,128)(2,1)S(1)}, bf16[4,32,1024]{2,1,0:T(8,128)(2,1)S(1)}, u32[]{:S(2)}, u32[]{:S(2)}) collective-permute-start(bf16[4,32,1024]{2,1,0:T(8,128)(2,1)S(1)} %add_convert_fusion.refs_0_), channel_id=1, source_target_pairs={{0,2},{1,3},{2,0},{3,1},{4,6},{5,7},{6,4},{7,5},{8,10},{9,11},{10,... | collective-permute-start | bytes 786440 | tf_op jit(solution)/shard_map/ppermute | solution.py:557
  26.3 1.4 %collective-permute-start.6 = (bf16[4,32,512]{2,1,0:T(8,128)(2,1)S(1)}, bf16[4,32,512]{2,1,0:T(8,128)(2,1)S(1)}, u32[]{:S(2)}, u32[]{:S(2)}) collective-permute-start(bf16[4,32,512]{2,1,0:T(8,128)(2,1)S(1)} %get-tuple-element.91), channel_id=1, source_target_pairs={{0,1},{1,0},{2,3},{3,2},{4,5},{5,4},{6,7},{7,6},{8,9},{9,8},{10,11... | collective-permute-start | bytes 393224 | tf_op jit(solution)/shard_map/ppermute | solution.py:550
  26.7 17.0 %collective-permute-start.13 = (bf16[4,32,512]{2,1,0:T(8,128)(2,1)S(1)}, bf16[4,32,512]{2,1,0:T(8,128)(2,1)S(1)}, u32[]{:S(2)}, u32[]{:S(2)}) collective-permute-start(bf16[4,32,512]{2,1,0:T(8,128)(2,1)S(1)} %get-tuple-element.118), channel_id=1, source_target_pairs={{0,1},{1,0},{2,3},{3,2},{4,5},{5,4},{6,7},{7,6},{8,9},{9,8},{10,11... | collective-permute-start | bytes 393224 | tf_op jit(solution)/shard_map/ppermute | solution.py:550
  27.8 15.9 %collective-permute-start.12 = (bf16[4,32,1024]{2,1,0:T(8,128)(2,1)S(1)}, bf16[4,32,1024]{2,1,0:T(8,128)(2,1)S(1)}, u32[]{:S(2)}, u32[]{:S(2)}) collective-permute-start(bf16[4,32,1024]{2,1,0:T(8,128)(2,1)S(1)} %shard_map.112.after_ref), channel_id=1, source_target_pairs={{0,2},{1,3},{2,0},{3,1},{4,6},{5,7},{6,4},{7,5},{8,10},{9,11},{10,... | collective-permute-start | bytes 786440 | tf_op jit(solution)/shard_map/ppermute | solution.py:567
  34.8 6.8 %collective-permute-start.10 = (bf16[2,3,16,512]{3,2,1,0:T(8,128)(2,1)S(1)}, bf16[2,3,16,512]{3,2,1,0:T(8,128)(2,1)S(1)}, u32[]{:S(2)}, u32[]{:S(2)}) collective-permute-start(bf16[2,3,16,512]{3,2,1,0:T(8,128)(2,1)S(1)} %get-tuple-element.110), channel_id=1, source_target_pairs={{0,12},{1,13},{2,14},{3,15},{4,0},{5,1},{6,2},{7,3},{8,4},{9,5},{1... | collective-permute-start | bytes 294920 | tf_op jit(solution)/shard_map/ppermute | solution.py:28
  37.0 6.5 %collective-permute-start.11 = (bf16[2,3,16,512]{3,2,1,0:T(8,128)(2,1)S(1)}, bf16[2,3,16,512]{3,2,1,0:T(8,128)(2,1)S(1)}, u32[]{:S(2)}, u32[]{:S(2)}) collective-permute-start(bf16[2,3,16,512]{3,2,1,0:T(8,128)(2,1)S(1)} %get-tuple-element.111), channel_id=1, source_target_pairs={{0,4},{1,5},{2,6},{3,7},{4,8},{5,9},{6,10},{7,11},{8,12},{9,13},{1... | collective-permute-start | bytes 294920 | tf_op jit(solution)/shard_map/ppermute | solution.py:28
  37.0 6.6 %collective-permute-start.9 = (bf16[6,32,256]{2,1,0:T(8,128)(2,1)S(1)}, bf16[6,32,256]{2,1,0:T(8,128)(2,1)S(1)}, u32[]{:S(2)}, u32[]{:S(2)}) collective-permute-start(bf16[6,32,256]{2,1,0:T(8,128)(2,1)S(1)} %get-tuple-element.94.refs_0_), channel_id=1, source_target_pairs={{0,4},{1,5},{2,6},{3,7},{4,0},{5,1},{6,2},{7,3},{8,12},{9,13},{10,... | collective-permute-start | bytes 294920 | tf_op jit(solution)/shard_map/ppermute | solution.py:569
  43.8 5.4 %collective-permute-start.14 = (bf16[10,32,256]{2,1,0:T(8,128)(2,1)S(1)}, bf16[10,32,256]{2,1,0:T(8,128)(2,1)S(1)}, u32[]{:S(2)}, u32[]{:S(2)}) collective-permute-start(bf16[10,32,256]{2,1,0:T(8,128)(2,1)S(1)} %get-tuple-element.119.after_ref), channel_id=1, source_target_pairs={{0,4},{1,5},{2,6},{3,7},{4,0},{5,1},{6,2},{7,3},{8,12},{9,13},{10,... | collective-permute-start | bytes 491528 | tf_op jit(solution)/shard_map/ppermute | solution.py:569
  45.2 7.9 %collective-permute-start.15 = (bf16[2,3,16,512]{3,2,1,0:T(8,128)(2,1)S(1)}, bf16[2,3,16,512]{3,2,1,0:T(8,128)(2,1)S(1)}, u32[]{:S(2)}, u32[]{:S(2)}) collective-permute-start(bf16[2,3,16,512]{3,2,1,0:T(8,128)(2,1)S(1)} %get-tuple-element.112.after_ref), channel_id=1, source_target_pairs={{0,1},{1,0},{2,3},{3,2},{4,5},{5,4},{6,7},{7,6},{8,9},{9,8},{10,11... | collective-permute-start | bytes 294920 | tf_op jit(solution)/shard_map/ppermute | solution.py:43
  45.2 7.9 %collective-permute-start.16 = (bf16[2,3,16,512]{3,2,1,0:T(8,128)(2,1)S(1)}, bf16[2,3,16,512]{3,2,1,0:T(8,128)(2,1)S(1)}, u32[]{:S(2)}, u32[]{:S(2)}) collective-permute-start(bf16[2,3,16,512]{3,2,1,0:T(8,128)(2,1)S(1)} %get-tuple-element.123), channel_id=1, source_target_pairs={{0,15},{1,2},{2,1},{3,4},{4,3},{5,6},{6,5},{7,8},{8,7},{9,10},{10,... | collective-permute-start | bytes 294920 | tf_op jit(solution)/shard_map/ppermute | solution.py:43
  49.2 3.9 %copy-start = (s32[1,8,16]{2,1,0:T(8,128)S(1)}, s32[1,8,16]{2,1,0:T(8,128)}, u32[]{:S(2)}) copy-start(s32[1,8,16]{2,1,0:T(8,128)} %send_ref.1) | copy-start | bytes 1540
  49.3 8.0 %collective-permute-start.18 = (bf16[5,32,256]{2,1,0:T(8,128)(2,1)S(1)}, bf16[5,32,256]{2,1,0:T(8,128)(2,1)S(1)}, u32[]{:S(2)}, u32[]{:S(2)}) collective-permute-start(bf16[5,32,256]{2,1,0:T(8,128)(2,1)S(1)} %get-tuple-element.121.after_ref), channel_id=1, source_target_pairs={{0,12},{1,13},{2,14},{3,15},{4,8},{5,9},{6,10},{7,11},{8,4},{9,5},... | collective-permute-start | bytes 245768 | tf_op jit(solution)/shard_map/ppermute | solution.py:569
  51.4 5.9 %collective-permute-start.17 = (bf16[3,32,256]{2,1,0:T(8,128)(2,1)S(1)}, bf16[3,32,256]{2,1,0:T(8,128)(2,1)S(1)}, u32[]{:S(2)}, u32[]{:S(2)}) collective-permute-start(bf16[3,32,256]{2,1,0:T(8,128)(2,1)S(1)} %get-tuple-element.114.refs_0_), channel_id=1, source_target_pairs={{0,12},{1,13},{2,14},{3,15},{4,8},{5,9},{6,10},{7,11},{8,4},{9,5},... | collective-permute-start | bytes 147464 | tf_op jit(solution)/shard_map/ppermute | solution.py:569

commit v7 on v6

--- a/solution.py
+++ b/solution.py
@@ -394,9 +394,9 @@
 
 def second_kernel(skip, pieces, me_ref, *refs):
     refs = refs[skip:]
-    first_ref, y_in = refs[:2]
-    owns, core_in = refs[2 : 2 + pieces], refs[2 + pieces : 2 + 2 * pieces]
-    kept_ref, sent_ref, projection_ref = refs[2 + 2 * pieces :]
+    kept_a, in_a, first_ref, y_in = refs[:4]
+    owns, core_in = refs[4 : 4 + pieces], refs[4 + pieces : 4 + 2 * pieces]
+    kept_ref, sent_ref, next_kept, next_sent, projection_ref = refs[4 + 2 * pieces :]
     done = first_ref.shape[0]
     planes = projection_ref.shape[0]
     projection_ref[:done] = first_ref[...]
@@ -413,6 +413,7 @@
         ],
         kept_ref, sent_ref,
     )
+    halve(add_received(kept_a, in_a), next_kept, next_sent)
 
 
 def step_kernel(after_ref, kept_in, received, kept_ref, sent_ref):
@@ -565,6 +566,14 @@
         (*other_b, *core_other_b),
     )
     y_b = lax.ppermute(y_sent, "patch", flop)
+    node, to_plus, to_minus, own_right, own_left = call(
+        functools.partial(node_kernel, groups, 1),
+        [((members, node_rows, width), f32), three, three, one, one],
+        (y_sent, *grads[0::3], *grads[1::3], *grads[2::3], wq, wk, wv),
+        specs=[pl.ANY],
+    )
+    from_plus = shifted(to_minus, -row_width)
+    from_minus = shifted(to_plus, row_width)
     def exchange(sent, bit):
         return lax.ppermute(sent, "patch", along_z(count, bit))
 
@@ -575,42 +584,34 @@
     kept_a, sent_a = halves(wide, 0)
     kept_a, out_a, sent_a = call(
         first_kernel, [kept_a, ((half * inner_planes, rows, width), f32), sent_a],
-        (y_sent, own_a, core_own, y_a), specs=[pl.ANY],
+        (y_sent, own_a, core_own, y_a), specs=[pl.ANY], flops=2 * 10**10,
     )
     in_a = exchange(sent_a, 0)
-    node, to_plus, to_minus, own_right, own_left = call(
-        functools.partial(node_kernel, groups, 1),
-        [((members, node_rows, width), f32), three, three, one, one],
-        (sent_a, *grads[0::3], *grads[1::3], *grads[2::3], wq, wk, wv),
-        specs=[pl.ANY], flops=2 * 10**10,
-    )
-    from_plus = shifted(to_minus, -row_width)
-    from_minus = shifted(to_plus, row_width)
     outgoing = call(
         relay_kernel, [three, three],
-        (place, in_a, own_right, own_left, from_plus, from_minus),
+        (place, sent_a, own_right, own_left, from_plus, from_minus),
         specs=[pltpu.SMEM, pl.ANY], scratch=[trio],
     )
     back = swap(outgoing, 1)
-    after = outgoing[0]
-    for bit in range(1, planes.bit_length()):
-        if bit < planes.bit_length() - 1:
+    kept_b, after, kept_a, sent_a = call(
+        functools.partial(second_kernel, 1, len(later)),
+        halves(wide + width, 0) + halves(wide, 1),
+        (place, outgoing[0], kept_a, in_a, out_a, y_b, *own_b, *core_own_b),
+        specs=[pltpu.SMEM, pl.ANY],
+        scratch=[pltpu.VMEM((planes, rows, width), f32)],
+    )
+    in_b = exchange(after, 0)
+    in_a = exchange(sent_a, 1)
+    for bit in range(1, planes.bit_length() - 1):
+        kept_b, after = call(
+            step_kernel, halves(wide + width, bit), (in_a, kept_b, in_b), specs=[pl.ANY]
+        )
+        in_b = exchange(after, bit)
+        if bit < planes.bit_length() - 2:
             kept_a, after = call(
-                step_kernel, halves(wide, bit), (after, kept_a, in_a), specs=[pl.ANY]
+                step_kernel, halves(wide, bit + 1), (after, kept_a, in_a), specs=[pl.ANY]
             )
-            in_a = exchange(after, bit)
-        if bit == 1:
-            kept_b, after = call(
-                functools.partial(second_kernel, 1, len(later)), halves(wide + width, 0),
-                (place, after, out_a, y_b, *own_b, *core_own_b),
-                specs=[pltpu.SMEM, pl.ANY],
-                scratch=[pltpu.VMEM((planes, rows, width), f32)],
-            )
-        else:
-            kept_b, after = call(
-                step_kernel, halves(wide + width, bit - 1), (after, kept_b, in_b), specs=[pl.ANY]
-            )
-        in_b = exchange(after, bit - 1)
+            in_a = exchange(after, bit + 1)
     (node_grad,) = call(
         finish_kernel, [((members, node_rows, width), bf16)],
         (place, after, send_rows, node, from_plus, from_minus, *back),

time: 58.2 us -> 55.3 us (0.950)
  waiting for transfers between devices: 18.8 us -> 15.3 us
    ppermute x1, waiting for transfers between devices: 3.83 us -> 0.01 us  [body(): y_a = lax.ppermute(y_sent, 'patch', flop)]
    ppermute x4, waiting for transfers between devices: 8.13 us -> 5.1 us  [shifted(): lax.ppermute(shard, 'patch', [(i, (i + by) % count) for i in range(count)])]
    ppermute x4, waiting for transfers between devices: 4.05 us -> 6.78 us  [exchange(): return lax.ppermute(sent, 'patch', along_z(count, bit))]
    ppermute x4, starting transfers between devices: 7.42 us -> 9.03 us  [shifted(): lax.ppermute(shard, 'patch', [(i, (i + by) % count) for i in range(count)])]
    ppermute x4, starting transfers between devices: 6.71 us -> 5.23 us  [swap(): lax.ppermute(shard, 'patch', perm)]
    ppermute x4, waiting for transfers between devices: 1.91 us -> 2.59 us  [swap(): lax.ppermute(shard, 'patch', perm)]
    pallas_call x17 -> x16, Pallas kernels: 15.6 us -> 15.5 us  [call(): pl.pallas_call(kernel, out_shape=[jax.ShapeDtypeStruct(*o) if final else...]
  transfers between devices with their start and end apart: 19 -> 19, of which waited for: 10 -> 9; matrix products, arithmetic and copies ran while one was open for 0% -> 0% of each run, Pallas kernels for 17% -> 18%
where the time goes in v7:
time: 55.3 us; the launch traced here: 55.1 us
  starting transfers between devices  23.3 us (42%)
  Pallas kernels  15.5 us (28%)
  waiting for transfers between devices  15.3 us (28%)
  between operations  0.79 us (1%)
    pallas_call x16, Pallas kernels, call(): pl.pallas_call(kernel, out_shape=[jax.ShapeDtypeStruct(*o) if final else...  15.5 us
    ppermute x4, starting transfers between devices, shifted(): lax.ppermute(shard, 'patch', [(i, (i + by) % count) for i in range(count)])  9.03 us
    ppermute x4, waiting for transfers between devices, exchange(): return lax.ppermute(sent, 'patch', along_z(count, bit))  6.78 us
    ppermute x4, starting transfers between devices, exchange(): return lax.ppermute(sent, 'patch', along_z(count, bit))  5.67 us
    ppermute x4, starting transfers between devices, swap(): lax.ppermute(shard, 'patch', perm)  5.23 us
    ppermute x4, waiting for transfers between devices, shifted(): lax.ppermute(shard, 'patch', [(i, (i + by) % count) for i in range(count)])  5.1 us
    ppermute x4, waiting for transfers between devices, swap(): lax.ppermute(shard, 'patch', perm)  2.59 us
    ppermute x1, starting transfers between devices, body(): y_b = lax.ppermute(y_sent, 'patch', flop)  2 us
  transfers between devices with their start and end apart: 19, of which 9 were waited for; matrix products, arithmetic and copies ran while one was open for 0% of the time, Pallas kernels for 18%

profile of v7, /device:TPU:0, one launch (start us, length us, event | category | flops | bytes accessed | tf_op | source)
XLA Modules:
  0.0 55.1 jit_solution(10158320453132964783)
XLA Ops:
  0.6 1.2 %shard_map.104 = (bf16[2,3,16,512]{3,2,1,0:T(8,128)(2,1)S(1)}, bf16[2,3,16,512]{3,2,1,0:T(8,128)(2,1)S(1)}, bf16[2,1,16,512]{3,2,1,0:T(8,128)(2,1)S(1)}, bf16[2,...) custom-call(s32[1,8,16]{2,1,0:T(8,128)} %send_ref.1, bf16[2,128,512]{2,1,0:T(8,128)(2,1)} %x_hbm.1), custom_call_target="tpu_custom_call" | custom-call | flops 1000000 | bytes 10000 | tf_op jit(solution)/shard_map/pallas_call | solution.py:459
  1.8 3.1 %collective-permute-start = (bf16[2,3,16,512]{3,2,1,0:T(8,128)(2,1)S(1)}, bf16[2,3,16,512]{3,2,1,0:T(8,128)(2,1)S(1)}, u32[]{:S(2)}, u32[]{:S(2)}) collective-permute-start(bf16[2,3,16,512]{3,2,1,0:T(8,128)(2,1)S(1)} %get-tuple-element.67), channel_id=1, source_target_pairs={{0,4},{1,5},{2,6},{3,7},{4,8},{5,9},{6,10},{7,11},{8,12},{9,13},{1... | collective-permute-start | bytes 294920 | tf_op jit(solution)/shard_map/ppermute | solution.py:28
  4.9 2.1 %collective-permute-start.1 = (bf16[2,3,16,512]{3,2,1,0:T(8,128)(2,1)S(1)}, bf16[2,3,16,512]{3,2,1,0:T(8,128)(2,1)S(1)}, u32[]{:S(2)}, u32[]{:S(2)}) collective-permute-start(bf16[2,3,16,512]{3,2,1,0:T(8,128)(2,1)S(1)} %get-tuple-element.68), channel_id=1, source_target_pairs={{0,12},{1,13},{2,14},{3,15},{4,0},{5,1},{6,2},{7,3},{8,4},{9,5},{1... | collective-permute-start | bytes 294920 | tf_op jit(solution)/shard_map/ppermute | solution.py:28
  7.0 2.6 %shard_map.105 = (bf16[8,2,128,128]{3,2,1,0:T(8,128)(2,1)S(1)}, bf16[8,2,128,128]{3,2,1,0:T(8,128)(2,1)S(1)}, bf16[8,2,128,128]{3,2,1,0:T(8,128)(2,1)S(1)}, bf16...) custom-call(bf16[2,1,16,512]{3,2,1,0:T(8,128)(2,1)S(1)} %get-tuple-e, ...), custom_call_target="tpu_custom_call" | custom-call | flops 1000000 | bytes 10000 | tf_op jit(solution)/shard_map/pallas_call | solution.py:459
  9.7 0.8 %collective-permute-done.plus_ref = bf16[2,3,16,512]{3,2,1,0:T(8,128)(2,1)S(1)} collective-permute-done((bf16[2,3,16,512]{3,2,1,0:T(8,128)(2,1)S(1)}, bf16[2,3,16,512]{3,2,1,0:T(8,128)(2,1)S(1)}, u32[]{:S(2)}, u32[]{:S(2)}) %collective-permute-start) | collective-permute-done | bytes 98336 | tf_op jit(solution)/shard_map/ppermute | solution.py:28
  10.4 0.8 %collective-permute-done.1.minus_ref = bf16[2,3,16,512]{3,2,1,0:T(8,128)(2,1)S(1)} collective-permute-done((bf16[2,3,16,512]{3,2,1,0:T(8,128)(2,1)S(1)}, bf16[2,3,16,512]{3,2,1,0:T(8,128)(2,1)S(1)}, u32[]{:S(2)}, u32[]{:S(2)}) %collective-permute-start.1) | collective-permute-done | bytes 98336 | tf_op jit(solution)/shard_map/ppermute | solution.py:28
  11.3 0.1 collective-permute-start.2
  11.4 3.4 %collective-permute-start.3 = (bf16[2,3,16,512]{3,2,1,0:T(8,128)(2,1)S(1)}, bf16[2,3,16,512]{3,2,1,0:T(8,128)(2,1)S(1)}, u32[]{:S(2)}, u32[]{:S(2)}) collective-permute-start(bf16[2,3,16,512]{3,2,1,0:T(8,128)(2,1)S(1)} %get-tuple-element.72), channel_id=1, source_target_pairs={{0,15},{1,2},{2,1},{3,4},{4,3},{5,6},{6,5},{7,8},{8,7},{9,10},{10,... | collective-permute-start | bytes 294920 | tf_op jit(solution)/shard_map/ppermute | solution.py:43
  14.8 1.4 %shard_map.108.refs_2_.refs_4_.refs_3_ = f32[256,128]{1,0:T(8,128)S(1)} custom-call(bf16[2,3,16,512]{3,2,1,0:T(8,128)(2,1)S(1)} %get-tuple-element.71.after_ref, s32[128,256]{1,0:T(8,128)S(1)} %get-tuple-element.77.neigh_ref, s32[1,128]{1,0:T(1,128)S(1)} %get-tuple-element.78.count_ref), custom_call_target="tpu_custom_call" | custom-call | flops 1000000 | bytes 10000 | tf_op jit(solution)/shard_map/pallas_call | solution.py:459
  16.3 0.0 collective-permute-done.2.first_in
  16.3 1.9 %collective-permute-done.3.second_in = bf16[2,3,16,512]{3,2,1,0:T(8,128)(2,1)S(1)} collective-permute-done((bf16[2,3,16,512]{3,2,1,0:T(8,128)(2,1)S(1)}, bf16[2,3,16,512]{3,2,1,0:T(8,128)(2,1)S(1)}, u32[]{:S(2)}, u32[]{:S(2)}) %collective-permute-start.3) | collective-permute-done | bytes 98336 | tf_op jit(solution)/shard_map/ppermute | solution.py:43
  18.2 0.6 %shard_map.107 = (bf16[4,2,128,128]{3,2,1,0:T(8,128)(2,1)S(1)}, bf16[4,2,128,128]{3,2,1,0:T(8,128)(2,1)S(1)}, bf16[4,2,128,128]{3,2,1,0:T(8,128)(2,1)S(1)}, bf16...) custom-call(s32[1]{0:T(128)} %bitcast.me_ref, bf16[2,3,16,512]{3,2,1,0:T(8,128)(2,1)S(1)} %collective-permute-done.plus_ref, ...), custom_call_target="tpu_custom_call" | custom-call | flops 1000000 | bytes 10000 | tf_op jit(solution)/shard_map/pallas_call | solution.py:459
  18.8 3.1 %shard_map.110 = (f32[4,32,1024]{2,1,0:T(8,128)S(1)}, f32[4,32,1024]{2,1,0:T(8,128)S(1)}, bf16[4,32,1024]{2,1,0:T(8,128)(2,1)S(1)}, bf16[4,32,1024]{2,1,0:T(8,12...) custom-call(s32[1]{0:T(128)} %bitcast.me_ref, ...), custom_call_target="tpu_custom_call" | custom-call | flops 1000000 | bytes 10000 | tf_op jit(solution)/shard_map/pallas_call | solution.py:459
  22.0 0.1 collective-permute-start.4
  22.0 1.7 %shard_map.109 = (f32[4,32,512]{2,1,0:T(8,128)S(1)}, f32[4,32,512]{2,1,0:T(8,128)S(1)}, bf16[2,4,32,512]{3,2,1,0:T(8,128)(2,1)S(1)}, bf16[2,128,128]{2,1,0:T(8,1...) custom-call(s32[1]{0:T(128)} %bitcast.me_ref, ...), custom_call_target="tpu_custom_call" | custom-call | flops 1000000 | bytes 10000 | tf_op jit(solution)/shard_map/pallas_call | solution.py:459
  23.7 0.6 %collective-permute-start.5 = (bf16[2,4,32,512]{3,2,1,0:T(8,128)(2,1)S(1)}, bf16[2,4,32,512]{3,2,1,0:T(8,128)(2,1)S(1)}, u32[]{:S(2)}, u32[]{:S(2)}) collective-permute-start(bf16[2,4,32,512]{3,2,1,0:T(8,128)(2,1)S(1)} %get-tuple-element.90), channel_id=1, source_target_pairs={{0,1},{1,0},{2,3},{3,2},{4,5},{5,4},{6,7},{7,6},{8,9},{9,8},{10,11... | collective-permute-start | bytes 786440 | tf_op jit(solution)/shard_map/ppermute | solution.py:551
  24.3 0.1 collective-permute-start.7
  24.4 0.0 collective-permute-done.4
  24.4 0.1 add_convert_fusion.refs_0_
  24.5 0.1 collective-permute-start.8
  24.6 1.7 %shard_map.111 = (f32[4,32,512]{2,1,0:T(8,128)S(1)}, f32[4,32,512]{2,1,0:T(8,128)S(1)}, bf16[4,32,512]{2,1,0:T(8,128)(2,1)S(1)}, bf16[4,32,512]{2,1,0:T(8,128)(2...) custom-call(s32[1]{0:T(128)} %bitcast.me_ref, ...), custom_call_target="tpu_custom_call" | custom-call | flops 1000000 | bytes 10000 | tf_op jit(solution)/shard_map/pallas_call | solution.py:459
  26.3 0.5 collective-permute-start.6
  26.7 0.1 collective-permute-start.13
  26.9 0.0 collective-permute-done.5.refs_2_.refs_7_
  26.9 0.9 %collective-permute-done.6.refs_3_ = bf16[4,32,512]{2,1,0:T(8,128)(2,1)S(1)} collective-permute-done((bf16[4,32,512]{2,1,0:T(8,128)(2,1)S(1)}, bf16[4,32,512]{2,1,0:T(8,128)(2,1)S(1)}, u32[]{:S(2)}, u32[]{:S(2)}) %collective-permute-start.6) | collective-permute-done | bytes 131104 | tf_op jit(solution)/shard_map/ppermute | solution.py:551
  27.7 0.1 shard_map.112.after_ref.refs_0_
  27.8 2.0 %collective-permute-start.12 = (bf16[4,32,1024]{2,1,0:T(8,128)(2,1)S(1)}, bf16[4,32,1024]{2,1,0:T(8,128)(2,1)S(1)}, u32[]{:S(2)}, u32[]{:S(2)}) collective-permute-start(bf16[4,32,1024]{2,1,0:T(8,128)(2,1)S(1)} %shard_map.112.after_ref.refs_0_), channel_id=1, source_target_pairs={{0,2},{1,3},{2,0},{3,1},{4,6},{5,7},{6,4},{7,5},{8,10},{9,11},{10,... | collective-permute-start | bytes 786440 | tf_op jit(solution)/shard_map/ppermute | solution.py:568
  29.8 1.0 %shard_map.114 = (f32[2,128,512]{2,1,0:T(8,128)S(1)}, bf16[2,3,16,512]{3,2,1,0:T(8,128)(2,1)S(1)}, bf16[2,3,16,512]{3,2,1,0:T(8,128)(2,1)S(1)}, bf16[2,1,16,512]...) custom-call(bf16[4,32,1024]{2,1,0:T(8,128)(2,1)S(1)} %shard_map.112.after_ref.refs_0_, ...), custom_call_target="tpu_custom_call" | custom-call | flops 1000000 | bytes 10000 | tf_op jit(solution)/shard_map/pallas_call | solution.py:459
  30.8 0.1 collective-permute-start.10
  30.9 3.8 %collective-permute-start.9 = (bf16[2,3,16,512]{3,2,1,0:T(8,128)(2,1)S(1)}, bf16[2,3,16,512]{3,2,1,0:T(8,128)(2,1)S(1)}, u32[]{:S(2)}, u32[]{:S(2)}) collective-permute-start(bf16[2,3,16,512]{3,2,1,0:T(8,128)(2,1)S(1)} %get-tuple-element.110), channel_id=1, source_target_pairs={{0,12},{1,13},{2,14},{3,15},{4,0},{5,1},{6,2},{7,3},{8,4},{9,5},{1... | collective-permute-start | bytes 294920 | tf_op jit(solution)/shard_map/ppermute | solution.py:28
  34.7 0.1 shard_map.113
  34.8 0.1 collective-permute-start.11
  34.9 3.5 %collective-permute-done.10.minus_ref = bf16[2,3,16,512]{3,2,1,0:T(8,128)(2,1)S(1)} collective-permute-done((bf16[2,3,16,512]{3,2,1,0:T(8,128)(2,1)S(1)}, bf16[2,3,16,512]{3,2,1,0:T(8,128)(2,1)S(1)}, u32[]{:S(2)}, u32[]{:S(2)}) %collective-permute-start.10) | collective-permute-done | bytes 98336 | tf_op jit(solution)/shard_map/ppermute | solution.py:28
  38.3 0.0 collective-permute-done.9.plus_ref
  38.4 1.4 %collective-permute-done.11.refs_2_ = bf16[6,32,256]{2,1,0:T(8,128)(2,1)S(1)} collective-permute-done((bf16[6,32,256]{2,1,0:T(8,128)(2,1)S(1)}, bf16[6,32,256]{2,1,0:T(8,128)(2,1)S(1)}, u32[]{:S(2)}, u32[]{:S(2)}) %collective-permute-start.11) | collective-permute-done | bytes 98336 | tf_op jit(solution)/shard_map/ppermute | solution.py:578
  39.8 0.0 collective-permute-done.12.refs_4_
  39.8 0.1 shard_map.116
  39.9 1.4 %collective-permute-start.15 = (bf16[10,32,256]{2,1,0:T(8,128)(2,1)S(1)}, bf16[10,32,256]{2,1,0:T(8,128)(2,1)S(1)}, u32[]{:S(2)}, u32[]{:S(2)}) collective-permute-start(bf16[10,32,256]{2,1,0:T(8,128)(2,1)S(1)} %get-tuple-element.120), channel_id=1, source_target_pairs={{0,4},{1,5},{2,6},{3,7},{4,0},{5,1},{6,2},{7,3},{8,12},{9,13},{10,... | collective-permute-start | bytes 491528 | tf_op jit(solution)/shard_map/ppermute | solution.py:578
  41.3 2.4 %collective-permute-start.14 = (bf16[3,32,256]{2,1,0:T(8,128)(2,1)S(1)}, bf16[3,32,256]{2,1,0:T(8,128)(2,1)S(1)}, u32[]{:S(2)}, u32[]{:S(2)}) collective-permute-start(bf16[3,32,256]{2,1,0:T(8,128)(2,1)S(1)} %get-tuple-element.118), channel_id=1, source_target_pairs={{0,12},{1,13},{2,14},{3,15},{4,8},{5,9},{6,10},{7,11},{8,4},{9,5},... | collective-permute-start | bytes 147464 | tf_op jit(solution)/shard_map/ppermute | solution.py:578
  43.7 0.0 collective-permute-start.16
  43.7 1.7 %collective-permute-start.17 = (bf16[2,3,16,512]{3,2,1,0:T(8,128)(2,1)S(1)}, bf16[2,3,16,512]{3,2,1,0:T(8,128)(2,1)S(1)}, u32[]{:S(2)}, u32[]{:S(2)}) collective-permute-start(bf16[2,3,16,512]{3,2,1,0:T(8,128)(2,1)S(1)} %get-tuple-element.123), channel_id=1, source_target_pairs={{0,15},{1,2},{2,1},{3,4},{4,3},{5,6},{6,5},{7,8},{8,7},{9,10},{10,... | collective-permute-start | bytes 294920 | tf_op jit(solution)/shard_map/ppermute | solution.py:43
  45.5 2.5 %collective-permute-done.14.after_ref.in_a = bf16[3,32,256]{2,1,0:T(8,128)(2,1)S(1)} collective-permute-done((bf16[3,32,256]{2,1,0:T(8,128)(2,1)S(1)}, bf16[3,32,256]{2,1,0:T(8,128)(2,1)S(1)}, u32[]{:S(2)}, u32[]{:S(2)}) %collective-permute-start.14) | collective-permute-done | bytes 49184 | tf_op jit(solution)/shard_map/ppermute | solution.py:578
  48.0 0.0 collective-permute-done.15.received
  48.0 1.8 %collective-permute-start.18 = (bf16[5,32,256]{2,1,0:T(8,128)(2,1)S(1)}, bf16[5,32,256]{2,1,0:T(8,128)(2,1)S(1)}, u32[]{:S(2)}, u32[]{:S(2)}) collective-permute-start(bf16[5,32,256]{2,1,0:T(8,128)(2,1)S(1)} %get-tuple-element.121.after_ref), channel_id=1, source_target_pairs={{0,12},{1,13},{2,14},{3,15},{4,8},{5,9},{6,10},{7,11},{8,4},{9,5},... | collective-permute-start | bytes 245768 | tf_op jit(solution)/shard_map/ppermute | solution.py:578
  49.8 0.7 %collective-permute-done.17.second_in = bf16[2,3,16,512]{3,2,1,0:T(8,128)(2,1)S(1)} collective-permute-done((bf16[2,3,16,512]{3,2,1,0:T(8,128)(2,1)S(1)}, bf16[2,3,16,512]{3,2,1,0:T(8,128)(2,1)S(1)}, u32[]{:S(2)}, u32[]{:S(2)}) %collective-permute-start.17) | collective-permute-done | bytes 98336 | tf_op jit(solution)/shard_map/ppermute | solution.py:43
  50.5 1.0 %shard_map.118.after_ref = bf16[2,128,512]{2,1,0:T(8,128)(2,1)} custom-call(s32[1]{0:T(128)} %bitcast.me_ref, bf16[5,32,256]{2,1,0:T(8,128)(2,1)S(1)} %get-tuple-element.121.after_ref, s32[1,8,16]{2,1,0:T(8,128)S(1)} %copy-done, f32[2,128,512]{2,1,0:T(8,128)S(1)} %get-tuple-element.122.node_ref, bf16[2,3,16,512]{3,2,1,0:T(8,128)(2,1)S(1)} %collective-permute-done.9.plus_ref, ...), custom_call_target="tpu_custom_call" | custom-call | flops 1000000 | bytes 10000 | tf_op jit(solution)/shard_map/pallas_call | solution.py:459
  51.5 2.9 %collective-permute-done.18.in_b = bf16[5,32,256]{2,1,0:T(8,128)(2,1)S(1)} collective-permute-done((bf16[5,32,256]{2,1,0:T(8,128)(2,1)S(1)}, bf16[5,32,256]{2,1,0:T(8,128)(2,1)S(1)}, u32[]{:S(2)}, u32[]{:S(2)}) %collective-permute-start.18) | collective-permute-done | bytes 81952 | tf_op jit(solution)/shard_map/ppermute | solution.py:578
  54.3 0.7 %shard_map.119 = f32[32,2048]{1,0:T(8,128)} custom-call(bf16[2,128,512]{2,1,0:T(8,128)(2,1)} %shard_map.118.after_ref, f32[1,32,768]{2,1,0:T(8,128)S(1)} %get-tuple-element.124.kept_a, bf16[3,32,256]{2,1,0:T(8,128)(2,1)S(1)} %collective-permute-done.14.after_ref.in_a, f32[1,32,1280]{2,1,0:T(8,128)S(1)} %get-tuple-element.125.kept_b, ...), custom_call_target="tpu_custom_call" | custom-call | flops 1000000 | bytes 10000 | tf_op jit(solution)/shard_map/pallas_call | solution.py:459
  (9 shorter events, 0.1 us)
Async XLA Ops:
  1.8 8.6 %collective-permute-start = (bf16[2,3,16,512]{3,2,1,0:T(8,128)(2,1)S(1)}, bf16[2,3,16,512]{3,2,1,0:T(8,128)(2,1)S(1)}, u32[]{:S(2)}, u32[]{:S(2)}) collective-permute-start(bf16[2,3,16,512]{3,2,1,0:T(8,128)(2,1)S(1)} %get-tuple-element.67), channel_id=1, source_target_pairs={{0,4},{1,5},{2,6},{3,7},{4,8},{5,9},{6,10},{7,11},{8,12},{9,13},{1... | collective-permute-start | bytes 294920 | tf_op jit(solution)/shard_map/ppermute | solution.py:28
  4.9 6.4 %collective-permute-start.1 = (bf16[2,3,16,512]{3,2,1,0:T(8,128)(2,1)S(1)}, bf16[2,3,16,512]{3,2,1,0:T(8,128)(2,1)S(1)}, u32[]{:S(2)}, u32[]{:S(2)}) collective-permute-start(bf16[2,3,16,512]{3,2,1,0:T(8,128)(2,1)S(1)} %get-tuple-element.68), channel_id=1, source_target_pairs={{0,12},{1,13},{2,14},{3,15},{4,0},{5,1},{6,2},{7,3},{8,4},{9,5},{1... | collective-permute-start | bytes 294920 | tf_op jit(solution)/shard_map/ppermute | solution.py:28
  11.3 5.0 %collective-permute-start.2 = (bf16[2,3,16,512]{3,2,1,0:T(8,128)(2,1)S(1)}, bf16[2,3,16,512]{3,2,1,0:T(8,128)(2,1)S(1)}, u32[]{:S(2)}, u32[]{:S(2)}) collective-permute-start(bf16[2,3,16,512]{3,2,1,0:T(8,128)(2,1)S(1)} %get-tuple-element.71.after_ref), channel_id=1, source_target_pairs={{0,1},{1,0},{2,3},{3,2},{4,5},{5,4},{6,7},{7,6},{8,9},{9,8},{10,11... | collective-permute-start | bytes 294920 | tf_op jit(solution)/shard_map/ppermute | solution.py:43
  11.4 6.8 %collective-permute-start.3 = (bf16[2,3,16,512]{3,2,1,0:T(8,128)(2,1)S(1)}, bf16[2,3,16,512]{3,2,1,0:T(8,128)(2,1)S(1)}, u32[]{:S(2)}, u32[]{:S(2)}) collective-permute-start(bf16[2,3,16,512]{3,2,1,0:T(8,128)(2,1)S(1)} %get-tuple-element.72), channel_id=1, source_target_pairs={{0,15},{1,2},{2,1},{3,4},{4,3},{5,6},{6,5},{7,8},{8,7},{9,10},{10,... | collective-permute-start | bytes 294920 | tf_op jit(solution)/shard_map/ppermute | solution.py:43
  22.0 2.4 %collective-permute-start.4 = (bf16[4,32,1024]{2,1,0:T(8,128)(2,1)S(1)}, bf16[4,32,1024]{2,1,0:T(8,128)(2,1)S(1)}, u32[]{:S(2)}, u32[]{:S(2)}) collective-permute-start(bf16[4,32,1024]{2,1,0:T(8,128)(2,1)S(1)} %get-tuple-element.86), channel_id=1, source_target_pairs={{0,1},{1,0},{2,3},{3,2},{4,5},{5,4},{6,7},{7,6},{8,9},{9,8},{10,11... | collective-permute-start | bytes 786440 | tf_op jit(solution)/shard_map/ppermute | solution.py:551
  23.7 3.1 %collective-permute-start.5 = (bf16[2,4,32,512]{3,2,1,0:T(8,128)(2,1)S(1)}, bf16[2,4,32,512]{3,2,1,0:T(8,128)(2,1)S(1)}, u32[]{:S(2)}, u32[]{:S(2)}) collective-permute-start(bf16[2,4,32,512]{3,2,1,0:T(8,128)(2,1)S(1)} %get-tuple-element.90), channel_id=1, source_target_pairs={{0,1},{1,0},{2,3},{3,2},{4,5},{5,4},{6,7},{7,6},{8,9},{9,8},{10,11... | collective-permute-start | bytes 786440 | tf_op jit(solution)/shard_map/ppermute | solution.py:551
  24.3 6.6 %collective-permute-start.7 = (bf16[4,32,1024]{2,1,0:T(8,128)(2,1)S(1)}, bf16[4,32,1024]{2,1,0:T(8,128)(2,1)S(1)}, u32[]{:S(2)}, u32[]{:S(2)}) collective-permute-start(bf16[4,32,1024]{2,1,0:T(8,128)(2,1)S(1)} %get-tuple-element.93), channel_id=1, source_target_pairs={{0,1},{1,0},{2,3},{3,2},{4,5},{5,4},{6,7},{7,6},{8,9},{9,8},{10,11... | collective-permute-start | bytes 786440 | tf_op jit(solution)/shard_map/ppermute | solution.py:551
  24.5 10.2 %collective-permute-start.8 = (bf16[4,32,1024]{2,1,0:T(8,128)(2,1)S(1)}, bf16[4,32,1024]{2,1,0:T(8,128)(2,1)S(1)}, u32[]{:S(2)}, u32[]{:S(2)}) collective-permute-start(bf16[4,32,1024]{2,1,0:T(8,128)(2,1)S(1)} %add_convert_fusion.refs_0_), channel_id=1, source_target_pairs={{0,2},{1,3},{2,0},{3,1},{4,6},{5,7},{6,4},{7,5},{8,10},{9,11},{10,... | collective-permute-start | bytes 786440 | tf_op jit(solution)/shard_map/ppermute | solution.py:558
  26.3 1.4 %collective-permute-start.6 = (bf16[4,32,512]{2,1,0:T(8,128)(2,1)S(1)}, bf16[4,32,512]{2,1,0:T(8,128)(2,1)S(1)}, u32[]{:S(2)}, u32[]{:S(2)}) collective-permute-start(bf16[4,32,512]{2,1,0:T(8,128)(2,1)S(1)} %get-tuple-element.91), channel_id=1, source_target_pairs={{0,1},{1,0},{2,3},{3,2},{4,5},{5,4},{6,7},{7,6},{8,9},{9,8},{10,11... | collective-permute-start | bytes 393224 | tf_op jit(solution)/shard_map/ppermute | solution.py:551
  26.7 11.6 %collective-permute-start.13 = (bf16[4,32,512]{2,1,0:T(8,128)(2,1)S(1)}, bf16[4,32,512]{2,1,0:T(8,128)(2,1)S(1)}, u32[]{:S(2)}, u32[]{:S(2)}) collective-permute-start(bf16[4,32,512]{2,1,0:T(8,128)(2,1)S(1)} %get-tuple-element.117), channel_id=1, source_target_pairs={{0,1},{1,0},{2,3},{3,2},{4,5},{5,4},{6,7},{7,6},{8,9},{9,8},{10,11... | collective-permute-start | bytes 393224 | tf_op jit(solution)/shard_map/ppermute | solution.py:551
  27.8 12.0 %collective-permute-start.12 = (bf16[4,32,1024]{2,1,0:T(8,128)(2,1)S(1)}, bf16[4,32,1024]{2,1,0:T(8,128)(2,1)S(1)}, u32[]{:S(2)}, u32[]{:S(2)}) collective-permute-start(bf16[4,32,1024]{2,1,0:T(8,128)(2,1)S(1)} %shard_map.112.after_ref.refs_0_), channel_id=1, source_target_pairs={{0,2},{1,3},{2,0},{3,1},{4,6},{5,7},{6,4},{7,5},{8,10},{9,11},{10,... | collective-permute-start | bytes 786440 | tf_op jit(solution)/shard_map/ppermute | solution.py:568
  30.8 7.5 %collective-permute-start.10 = (bf16[2,3,16,512]{3,2,1,0:T(8,128)(2,1)S(1)}, bf16[2,3,16,512]{3,2,1,0:T(8,128)(2,1)S(1)}, u32[]{:S(2)}, u32[]{:S(2)}) collective-permute-start(bf16[2,3,16,512]{3,2,1,0:T(8,128)(2,1)S(1)} %get-tuple-element.111), channel_id=1, source_target_pairs={{0,4},{1,5},{2,6},{3,7},{4,8},{5,9},{6,10},{7,11},{8,12},{9,13},{1... | collective-permute-start | bytes 294920 | tf_op jit(solution)/shard_map/ppermute | solution.py:28
  30.9 7.5 %collective-permute-start.9 = (bf16[2,3,16,512]{3,2,1,0:T(8,128)(2,1)S(1)}, bf16[2,3,16,512]{3,2,1,0:T(8,128)(2,1)S(1)}, u32[]{:S(2)}, u32[]{:S(2)}) collective-permute-start(bf16[2,3,16,512]{3,2,1,0:T(8,128)(2,1)S(1)} %get-tuple-element.110), channel_id=1, source_target_pairs={{0,12},{1,13},{2,14},{3,15},{4,0},{5,1},{6,2},{7,3},{8,4},{9,5},{1... | collective-permute-start | bytes 294920 | tf_op jit(solution)/shard_map/ppermute | solution.py:28
  34.8 5.0 %collective-permute-start.11 = (bf16[6,32,256]{2,1,0:T(8,128)(2,1)S(1)}, bf16[6,32,256]{2,1,0:T(8,128)(2,1)S(1)}, u32[]{:S(2)}, u32[]{:S(2)}) collective-permute-start(bf16[6,32,256]{2,1,0:T(8,128)(2,1)S(1)} %get-tuple-element.94.after_ref), channel_id=1, source_target_pairs={{0,4},{1,5},{2,6},{3,7},{4,0},{5,1},{6,2},{7,3},{8,12},{9,13},{10,... | collective-permute-start | bytes 294920 | tf_op jit(solution)/shard_map/ppermute | solution.py:578
  39.9 8.1 %collective-permute-start.15 = (bf16[10,32,256]{2,1,0:T(8,128)(2,1)S(1)}, bf16[10,32,256]{2,1,0:T(8,128)(2,1)S(1)}, u32[]{:S(2)}, u32[]{:S(2)}) collective-permute-start(bf16[10,32,256]{2,1,0:T(8,128)(2,1)S(1)} %get-tuple-element.120), channel_id=1, source_target_pairs={{0,4},{1,5},{2,6},{3,7},{4,0},{5,1},{6,2},{7,3},{8,12},{9,13},{10,... | collective-permute-start | bytes 491528 | tf_op jit(solution)/shard_map/ppermute | solution.py:578
  41.3 6.7 %collective-permute-start.14 = (bf16[3,32,256]{2,1,0:T(8,128)(2,1)S(1)}, bf16[3,32,256]{2,1,0:T(8,128)(2,1)S(1)}, u32[]{:S(2)}, u32[]{:S(2)}) collective-permute-start(bf16[3,32,256]{2,1,0:T(8,128)(2,1)S(1)} %get-tuple-element.118), channel_id=1, source_target_pairs={{0,12},{1,13},{2,14},{3,15},{4,8},{5,9},{6,10},{7,11},{8,4},{9,5},... | collective-permute-start | bytes 147464 | tf_op jit(solution)/shard_map/ppermute | solution.py:578
  43.7 6.1 %collective-permute-start.16 = (bf16[2,3,16,512]{3,2,1,0:T(8,128)(2,1)S(1)}, bf16[2,3,16,512]{3,2,1,0:T(8,128)(2,1)S(1)}, u32[]{:S(2)}, u32[]{:S(2)}) collective-permute-start(bf16[2,3,16,512]{3,2,1,0:T(8,128)(2,1)S(1)} %get-tuple-element.112.refs_0_), channel_id=1, source_target_pairs={{0,1},{1,0},{2,3},{3,2},{4,5},{5,4},{6,7},{7,6},{8,9},{9,8},{10,11... | collective-permute-start | bytes 294920 | tf_op jit(solution)/shard_map/ppermute | solution.py:43
  43.7 6.7 %collective-permute-start.17 = (bf16[2,3,16,512]{3,2,1,0:T(8,128)(2,1)S(1)}, bf16[2,3,16,512]{3,2,1,0:T(8,128)(2,1)S(1)}, u32[]{:S(2)}, u32[]{:S(2)}) collective-permute-start(bf16[2,3,16,512]{3,2,1,0:T(8,128)(2,1)S(1)} %get-tuple-element.123), channel_id=1, source_target_pairs={{0,15},{1,2},{2,1},{3,4},{4,3},{5,6},{6,5},{7,8},{8,7},{9,10},{10,... | collective-permute-start | bytes 294920 | tf_op jit(solution)/shard_map/ppermute | solution.py:43
  48.0 2.5 %copy-start = (s32[1,8,16]{2,1,0:T(8,128)S(1)}, s32[1,8,16]{2,1,0:T(8,128)}, u32[]{:S(2)}) copy-start(s32[1,8,16]{2,1,0:T(8,128)} %send_ref.1) | copy-start | bytes 1540
  48.0 6.3 %collective-permute-start.18 = (bf16[5,32,256]{2,1,0:T(8,128)(2,1)S(1)}, bf16[5,32,256]{2,1,0:T(8,128)(2,1)S(1)}, u32[]{:S(2)}, u32[]{:S(2)}) collective-permute-start(bf16[5,32,256]{2,1,0:T(8,128)(2,1)S(1)} %get-tuple-element.121.after_ref), channel_id=1, source_target_pairs={{0,12},{1,13},{2,14},{3,15},{4,8},{5,9},{6,10},{7,11},{8,4},{9,5},... | collective-permute-start | bytes 245768 | tf_op jit(solution)/shard_map/ppermute | solution.py:578

commit v8 on v7

--- a/solution.py
+++ b/solution.py
@@ -114,9 +114,9 @@
     return z
 
 
-def along_z(count, bit):
+def along_z(count, distance):
     planes = count // 4
-    return [(i, plane_of(gray(i // 4) ^ (1 << bit)) * 4 + i % 4) for i in range(planes * 4)]
+    return [(i, plane_of(gray(i // 4) ^ distance) * 4 + i % 4) for i in range(planes * 4)]
 
 
 Q, K, V, G, QT, KT, VT, GT = range(8)
@@ -392,11 +392,17 @@
     halve(rows, kept_ref, sent_ref)
 
 
+def put(row, ref, at):
+    for n in range(row.shape[1] // 256):
+        ref[at + n] = row[:, n * 256 : (n + 1) * 256].astype(bf16)
+
+
 def second_kernel(skip, pieces, me_ref, *refs):
     refs = refs[skip:]
     kept_a, in_a, first_ref, y_in = refs[:4]
     owns, core_in = refs[4 : 4 + pieces], refs[4 + pieces : 4 + 2 * pieces]
-    kept_ref, sent_ref, next_kept, next_sent, projection_ref = refs[4 + 2 * pieces :]
+    own_a, own_b, *sent = refs[4 + 2 * pieces : -1]
+    projection_ref = refs[-1]
     done = first_ref.shape[0]
     planes = projection_ref.shape[0]
     projection_ref[:done] = first_ref[...]
@@ -405,19 +411,17 @@
         parts = sums(owns, core_in, y_in, k)
         gather_projection(parts, k, planes, projection_ref, done)
         held.append(jnp.concatenate([part[:, :384] for part in parts], axis=1))
+    first = add_received(kept_a, in_a)
+    own_a[...] = first[0]
     z = me_ref[0] // 4
-    halve(
-        [
-            jnp.concatenate([held[k], projection_ref[plane_of(gray(z) ^ k)]], axis=1)
-            for k in range(planes)
-        ],
-        kept_ref, sent_ref,
-    )
-    halve(add_received(kept_a, in_a), next_kept, next_sent)
-
-
-def step_kernel(after_ref, kept_in, received, kept_ref, sent_ref):
-    halve(add_received(kept_in, received), kept_ref, sent_ref)
+    for k in range(planes):
+        row = jnp.concatenate([held[k], projection_ref[plane_of(gray(z) ^ k)]], axis=1)
+        if k == 0:
+            own_b[...] = row
+            continue
+        put(row, sent[k - 1], 0)
+        if k % 2 == 0:
+            put(first[k // 2], sent[k - 1], row.shape[1] // 256)
 
 
 def finish_kernel(
@@ -436,9 +440,14 @@
         out_ref[m] = (node_ref[m] + nn(pick, arriving)).astype(bf16)
 
 
-def weight_kernel(after_ref, kept_a, in_a, kept_b, in_b, out_ref):
-    (a,) = add_received(kept_a, in_a)
-    (b,) = add_received(kept_b, in_b)
+def weight_kernel(after_ref, own_a, own_b, *refs):
+    received, out_ref = refs[:-1], refs[-1]
+    a, b = own_a[...], own_b[...]
+    blocks, more = b.shape[1] // 256, a.shape[1] // 256
+    for k, ref in enumerate(received, 1):
+        b = b + jnp.concatenate([ref[n] for n in range(blocks)], axis=1).astype(f32)
+        if k % 2 == 0:
+            a = a + jnp.concatenate([ref[blocks + n] for n in range(more)], axis=1).astype(f32)
     half = a.shape[1] // 384
     width = 256 * half
     for i, part in enumerate((a, b)):
@@ -574,51 +583,42 @@
     )
     from_plus = shifted(to_minus, -row_width)
     from_minus = shifted(to_plus, row_width)
-    def exchange(sent, bit):
-        return lax.ppermute(sent, "patch", along_z(count, bit))
-
-    def halves(wide, bit):
-        left = planes >> (bit + 1)
-        return [((left, rows, wide), f32), ((left * wide // 256, rows, 256), bf16)]
-
-    kept_a, sent_a = halves(wide, 0)
+    def exchange(sent, distance):
+        return lax.ppermute(sent, "patch", along_z(count, distance))
+
     kept_a, out_a, sent_a = call(
-        first_kernel, [kept_a, ((half * inner_planes, rows, width), f32), sent_a],
+        first_kernel,
+        [
+            ((planes // 2, rows, wide), f32),
+            ((half * inner_planes, rows, width), f32),
+            ((planes // 2 * wide // 256, rows, 256), bf16),
+        ],
         (y_sent, own_a, core_own, y_a), specs=[pl.ANY], flops=2 * 10**10,
     )
-    in_a = exchange(sent_a, 0)
+    in_a = exchange(sent_a, 1)
     outgoing = call(
         relay_kernel, [three, three],
         (place, sent_a, own_right, own_left, from_plus, from_minus),
         specs=[pltpu.SMEM, pl.ANY], scratch=[trio],
     )
     back = swap(outgoing, 1)
-    kept_b, after, kept_a, sent_a = call(
+    more, blocks = wide // 256, (wide + width) // 256
+    own_a, own_b, *sent = call(
         functools.partial(second_kernel, 1, len(later)),
-        halves(wide + width, 0) + halves(wide, 1),
+        [((rows, wide), f32), ((rows, wide + width), f32)]
+        + [((blocks + (0 if k % 2 else more), rows, 256), bf16) for k in range(1, planes)],
         (place, outgoing[0], kept_a, in_a, out_a, y_b, *own_b, *core_own_b),
         specs=[pltpu.SMEM, pl.ANY],
         scratch=[pltpu.VMEM((planes, rows, width), f32)],
     )
-    in_b = exchange(after, 0)
-    in_a = exchange(sent_a, 1)
-    for bit in range(1, planes.bit_length() - 1):
-        kept_b, after = call(
-            step_kernel, halves(wide + width, bit), (in_a, kept_b, in_b), specs=[pl.ANY]
-        )
-        in_b = exchange(after, bit)
-        if bit < planes.bit_length() - 2:
-            kept_a, after = call(
-                step_kernel, halves(wide, bit + 1), (after, kept_a, in_a), specs=[pl.ANY]
-            )
-            in_a = exchange(after, bit + 1)
+    received = [exchange(shard, k) for k, shard in enumerate(sent, 1)]
     (node_grad,) = call(
         finish_kernel, [((members, node_rows, width), bf16)],
-        (place, after, send_rows, node, from_plus, from_minus, *back),
+        (place, sent[0], send_rows, node, from_plus, from_minus, *back),
         specs=[pltpu.SMEM, pl.ANY], scratch=[trio], final=True,
     )
     (weight_grad,) = call(
-        weight_kernel, [((rows, 4 * width), f32)], (node_grad, kept_a, in_a, kept_b, in_b),
+        weight_kernel, [((rows, 4 * width), f32)], (node_grad, own_a, own_b, *received),
         specs=[pltpu.HBM], final=True,
     )
     return (node_grad, weight_grad)

time: 55.3 us -> 53.4 us (0.966)
  starting transfers between devices: 23.3 us -> 21.9 us
    ppermute x4, waiting for transfers between devices: 6.78 us -> 3.49 us  [exchange(): return lax.ppermute(sent, 'patch', along_z(count, distance))]
    ppermute x4, waiting for transfers between devices: 2.59 us -> 5.51 us  [swap(): lax.ppermute(shard, 'patch', perm)]
    ppermute x4, starting transfers between devices: 5.67 us -> 3.82 us  [exchange(): return lax.ppermute(sent, 'patch', along_z(count, distance))]
    pallas_call x16 -> x15, Pallas kernels: 15.5 us -> 15.5 us  [call(): pl.pallas_call(kernel, out_shape=[jax.ShapeDtypeStruct(*o) if final else...]
where the time goes in v8:
time: 53.4 us; the launch traced here: 53.2 us
  starting transfers between devices  21.9 us (41%)
  Pallas kernels  15.5 us (29%)
  waiting for transfers between devices  15 us (28%)
  between operations  0.79 us (1%)
    pallas_call x15, Pallas kernels, call(): pl.pallas_call(kernel, out_shape=[jax.ShapeDtypeStruct(*o) if final else...  15.5 us
    ppermute x4, starting transfers between devices, shifted(): lax.ppermute(shard, 'patch', [(i, (i + by) % count) for i in range(count)])  9.03 us
    ppermute x4, starting transfers between devices, swap(): lax.ppermute(shard, 'patch', perm)  5.6 us
    ppermute x4, waiting for transfers between devices, swap(): lax.ppermute(shard, 'patch', perm)  5.51 us
    ppermute x4, waiting for transfers between devices, shifted(): lax.ppermute(shard, 'patch', [(i, (i + by) % count) for i in range(count)])  5.1 us
    ppermute x4, starting transfers between devices, exchange(): return lax.ppermute(sent, 'patch', along_z(count, distance))  3.82 us
    ppermute x4, waiting for transfers between devices, exchange(): return lax.ppermute(sent, 'patch', along_z(count, distance))  3.49 us
    ppermute x1, starting transfers between devices, body(): y_b = lax.ppermute(y_sent, 'patch', flop)  2 us
  transfers between devices with their start and end apart: 19, of which 9 were waited for; matrix products, arithmetic and copies ran while one was open for 0% of the time, Pallas kernels for 18%

profile of v8, /device:TPU:0, one launch (start us, length us, event | category | flops | bytes accessed | tf_op | source)
XLA Modules:
  0.0 53.2 jit_solution(4007814626698977355)
XLA Ops:
  0.6 1.2 %shard_map.104 = (bf16[2,3,16,512]{3,2,1,0:T(8,128)(2,1)S(1)}, bf16[2,3,16,512]{3,2,1,0:T(8,128)(2,1)S(1)}, bf16[2,1,16,512]{3,2,1,0:T(8,128)(2,1)S(1)}, bf16[2,...) custom-call(s32[1,8,16]{2,1,0:T(8,128)} %send_ref.1, bf16[2,128,512]{2,1,0:T(8,128)(2,1)} %x_hbm.1), custom_call_target="tpu_custom_call" | custom-call | flops 1000000 | bytes 10000 | tf_op jit(solution)/shard_map/pallas_call | solution.py:468
  1.8 3.1 %collective-permute-start = (bf16[2,3,16,512]{3,2,1,0:T(8,128)(2,1)S(1)}, bf16[2,3,16,512]{3,2,1,0:T(8,128)(2,1)S(1)}, u32[]{:S(2)}, u32[]{:S(2)}) collective-permute-start(bf16[2,3,16,512]{3,2,1,0:T(8,128)(2,1)S(1)} %get-tuple-element.66), channel_id=1, source_target_pairs={{0,4},{1,5},{2,6},{3,7},{4,8},{5,9},{6,10},{7,11},{8,12},{9,13},{1... | collective-permute-start | bytes 294920 | tf_op jit(solution)/shard_map/ppermute | solution.py:28
  4.9 2.1 %collective-permute-start.1 = (bf16[2,3,16,512]{3,2,1,0:T(8,128)(2,1)S(1)}, bf16[2,3,16,512]{3,2,1,0:T(8,128)(2,1)S(1)}, u32[]{:S(2)}, u32[]{:S(2)}) collective-permute-start(bf16[2,3,16,512]{3,2,1,0:T(8,128)(2,1)S(1)} %get-tuple-element.67), channel_id=1, source_target_pairs={{0,12},{1,13},{2,14},{3,15},{4,0},{5,1},{6,2},{7,3},{8,4},{9,5},{1... | collective-permute-start | bytes 294920 | tf_op jit(solution)/shard_map/ppermute | solution.py:28
  7.0 2.6 %shard_map.105 = (bf16[8,2,128,128]{3,2,1,0:T(8,128)(2,1)S(1)}, bf16[8,2,128,128]{3,2,1,0:T(8,128)(2,1)S(1)}, bf16[8,2,128,128]{3,2,1,0:T(8,128)(2,1)S(1)}, bf16...) custom-call(bf16[2,1,16,512]{3,2,1,0:T(8,128)(2,1)S(1)} %get-tuple-e, ...), custom_call_target="tpu_custom_call" | custom-call | flops 1000000 | bytes 10000 | tf_op jit(solution)/shard_map/pallas_call | solution.py:468
  9.7 0.8 %collective-permute-done.plus_ref = bf16[2,3,16,512]{3,2,1,0:T(8,128)(2,1)S(1)} collective-permute-done((bf16[2,3,16,512]{3,2,1,0:T(8,128)(2,1)S(1)}, bf16[2,3,16,512]{3,2,1,0:T(8,128)(2,1)S(1)}, u32[]{:S(2)}, u32[]{:S(2)}) %collective-permute-start) | collective-permute-done | bytes 98336 | tf_op jit(solution)/shard_map/ppermute | solution.py:28
  10.4 0.8 %collective-permute-done.1.minus_ref = bf16[2,3,16,512]{3,2,1,0:T(8,128)(2,1)S(1)} collective-permute-done((bf16[2,3,16,512]{3,2,1,0:T(8,128)(2,1)S(1)}, bf16[2,3,16,512]{3,2,1,0:T(8,128)(2,1)S(1)}, u32[]{:S(2)}, u32[]{:S(2)}) %collective-permute-start.1) | collective-permute-done | bytes 98336 | tf_op jit(solution)/shard_map/ppermute | solution.py:28
  11.3 0.1 collective-permute-start.2
  11.4 3.4 %collective-permute-start.3 = (bf16[2,3,16,512]{3,2,1,0:T(8,128)(2,1)S(1)}, bf16[2,3,16,512]{3,2,1,0:T(8,128)(2,1)S(1)}, u32[]{:S(2)}, u32[]{:S(2)}) collective-permute-start(bf16[2,3,16,512]{3,2,1,0:T(8,128)(2,1)S(1)} %get-tuple-element.71), channel_id=1, source_target_pairs={{0,15},{1,2},{2,1},{3,4},{4,3},{5,6},{6,5},{7,8},{8,7},{9,10},{10,... | collective-permute-start | bytes 294920 | tf_op jit(solution)/shard_map/ppermute | solution.py:43
  14.8 1.4 %shard_map.108.refs_2_.refs_4_.refs_3_ = f32[256,128]{1,0:T(8,128)S(1)} custom-call(bf16[2,3,16,512]{3,2,1,0:T(8,128)(2,1)S(1)} %get-tuple-element.70.after_ref, s32[128,256]{1,0:T(8,128)S(1)} %get-tuple-element.76.neigh_ref, s32[1,128]{1,0:T(1,128)S(1)} %get-tuple-element.77.count_ref), custom_call_target="tpu_custom_call" | custom-call | flops 1000000 | bytes 10000 | tf_op jit(solution)/shard_map/pallas_call | solution.py:468
  16.3 0.0 collective-permute-done.2.first_in
  16.3 1.9 %collective-permute-done.3.second_in = bf16[2,3,16,512]{3,2,1,0:T(8,128)(2,1)S(1)} collective-permute-done((bf16[2,3,16,512]{3,2,1,0:T(8,128)(2,1)S(1)}, bf16[2,3,16,512]{3,2,1,0:T(8,128)(2,1)S(1)}, u32[]{:S(2)}, u32[]{:S(2)}) %collective-permute-start.3) | collective-permute-done | bytes 98336 | tf_op jit(solution)/shard_map/ppermute | solution.py:43
  18.2 0.6 %shard_map.107 = (bf16[4,2,128,128]{3,2,1,0:T(8,128)(2,1)S(1)}, bf16[4,2,128,128]{3,2,1,0:T(8,128)(2,1)S(1)}, bf16[4,2,128,128]{3,2,1,0:T(8,128)(2,1)S(1)}, bf16...) custom-call(s32[1]{0:T(128)} %bitcast.me_ref, bf16[2,3,16,512]{3,2,1,0:T(8,128)(2,1)S(1)} %collective-permute-done.plus_ref, ...), custom_call_target="tpu_custom_call" | custom-call | flops 1000000 | bytes 10000 | tf_op jit(solution)/shard_map/pallas_call | solution.py:468
  18.8 3.1 %shard_map.110 = (f32[4,32,1024]{2,1,0:T(8,128)S(1)}, f32[4,32,1024]{2,1,0:T(8,128)S(1)}, bf16[4,32,1024]{2,1,0:T(8,128)(2,1)S(1)}, bf16[4,32,1024]{2,1,0:T(8,12...) custom-call(s32[1]{0:T(128)} %bitcast.me_ref, ...), custom_call_target="tpu_custom_call" | custom-call | flops 1000000 | bytes 10000 | tf_op jit(solution)/shard_map/pallas_call | solution.py:468
  22.0 0.1 collective-permute-start.4
  22.0 1.7 %shard_map.109 = (f32[4,32,512]{2,1,0:T(8,128)S(1)}, f32[4,32,512]{2,1,0:T(8,128)S(1)}, bf16[2,4,32,512]{3,2,1,0:T(8,128)(2,1)S(1)}, bf16[2,128,128]{2,1,0:T(8,1...) custom-call(s32[1]{0:T(128)} %bitcast.me_ref, ...), custom_call_target="tpu_custom_call" | custom-call | flops 1000000 | bytes 10000 | tf_op jit(solution)/shard_map/pallas_call | solution.py:468
  23.7 0.6 %collective-permute-start.5 = (bf16[2,4,32,512]{3,2,1,0:T(8,128)(2,1)S(1)}, bf16[2,4,32,512]{3,2,1,0:T(8,128)(2,1)S(1)}, u32[]{:S(2)}, u32[]{:S(2)}) collective-permute-start(bf16[2,4,32,512]{3,2,1,0:T(8,128)(2,1)S(1)} %get-tuple-element.89), channel_id=1, source_target_pairs={{0,1},{1,0},{2,3},{3,2},{4,5},{5,4},{6,7},{7,6},{8,9},{9,8},{10,11... | collective-permute-start | bytes 786440 | tf_op jit(solution)/shard_map/ppermute | solution.py:560
  24.3 0.1 collective-permute-start.7
  24.4 0.0 collective-permute-done.4
  24.4 0.1 add_convert_fusion.refs_0_
  24.5 0.1 collective-permute-start.8
  24.6 1.7 %shard_map.111 = (f32[4,32,512]{2,1,0:T(8,128)S(1)}, f32[4,32,512]{2,1,0:T(8,128)S(1)}, bf16[4,32,512]{2,1,0:T(8,128)(2,1)S(1)}, bf16[4,32,512]{2,1,0:T(8,128)(2...) custom-call(s32[1]{0:T(128)} %bitcast.me_ref, ...), custom_call_target="tpu_custom_call" | custom-call | flops 1000000 | bytes 10000 | tf_op jit(solution)/shard_map/pallas_call | solution.py:468
  26.3 0.5 collective-permute-start.6
  26.7 0.1 collective-permute-start.13
  26.9 0.0 collective-permute-done.5.refs_2_.refs_7_
  26.9 0.9 %collective-permute-done.6.refs_3_ = bf16[4,32,512]{2,1,0:T(8,128)(2,1)S(1)} collective-permute-done((bf16[4,32,512]{2,1,0:T(8,128)(2,1)S(1)}, bf16[4,32,512]{2,1,0:T(8,128)(2,1)S(1)}, u32[]{:S(2)}, u32[]{:S(2)}) %collective-permute-start.6) | collective-permute-done | bytes 131104 | tf_op jit(solution)/shard_map/ppermute | solution.py:560
  27.7 0.1 shard_map.112.after_ref.refs_0_
  27.8 2.0 %collective-permute-start.12 = (bf16[4,32,1024]{2,1,0:T(8,128)(2,1)S(1)}, bf16[4,32,1024]{2,1,0:T(8,128)(2,1)S(1)}, u32[]{:S(2)}, u32[]{:S(2)}) collective-permute-start(bf16[4,32,1024]{2,1,0:T(8,128)(2,1)S(1)} %shard_map.112.after_ref.refs_0_), channel_id=1, source_target_pairs={{0,2},{1,3},{2,0},{3,1},{4,6},{5,7},{6,4},{7,5},{8,10},{9,11},{10,... | collective-permute-start | bytes 786440 | tf_op jit(solution)/shard_map/ppermute | solution.py:577
  29.8 1.0 %shard_map.114 = (f32[2,128,512]{2,1,0:T(8,128)S(1)}, bf16[2,3,16,512]{3,2,1,0:T(8,128)(2,1)S(1)}, bf16[2,3,16,512]{3,2,1,0:T(8,128)(2,1)S(1)}, bf16[2,1,16,512]...) custom-call(bf16[4,32,1024]{2,1,0:T(8,128)(2,1)S(1)} %shard_map.112.after_ref.refs_0_, ...), custom_call_target="tpu_custom_call" | custom-call | flops 1000000 | bytes 10000 | tf_op jit(solution)/shard_map/pallas_call | solution.py:468
  30.8 0.1 collective-permute-start.10
  30.9 0.0 collective-permute-done.7.core_in
  30.9 3.8 %collective-permute-start.9 = (bf16[2,3,16,512]{3,2,1,0:T(8,128)(2,1)S(1)}, bf16[2,3,16,512]{3,2,1,0:T(8,128)(2,1)S(1)}, u32[]{:S(2)}, u32[]{:S(2)}) collective-permute-start(bf16[2,3,16,512]{3,2,1,0:T(8,128)(2,1)S(1)} %get-tuple-element.109), channel_id=1, source_target_pairs={{0,12},{1,13},{2,14},{3,15},{4,0},{5,1},{6,2},{7,3},{8,4},{9,5},{1... | collective-permute-start | bytes 294920 | tf_op jit(solution)/shard_map/ppermute | solution.py:28
  34.7 0.1 shard_map.113
  34.8 0.1 collective-permute-start.11
  34.9 3.5 %collective-permute-done.10.minus_ref = bf16[2,3,16,512]{3,2,1,0:T(8,128)(2,1)S(1)} collective-permute-done((bf16[2,3,16,512]{3,2,1,0:T(8,128)(2,1)S(1)}, bf16[2,3,16,512]{3,2,1,0:T(8,128)(2,1)S(1)}, u32[]{:S(2)}, u32[]{:S(2)}) %collective-permute-start.10) | collective-permute-done | bytes 98336 | tf_op jit(solution)/shard_map/ppermute | solution.py:28
  38.3 0.0 collective-permute-done.9.plus_ref
  38.4 1.4 %collective-permute-done.11.refs_2_ = bf16[6,32,256]{2,1,0:T(8,128)(2,1)S(1)} collective-permute-done((bf16[6,32,256]{2,1,0:T(8,128)(2,1)S(1)}, bf16[6,32,256]{2,1,0:T(8,128)(2,1)S(1)}, u32[]{:S(2)}, u32[]{:S(2)}) %collective-permute-start.11) | collective-permute-done | bytes 98336 | tf_op jit(solution)/shard_map/ppermute | solution.py:587
  39.8 0.0 collective-permute-done.12.refs_4_
  39.8 0.1 shard_map.116
  39.9 0.0 copy-start
  39.9 2.5 %collective-permute-start.17 = (bf16[8,32,256]{2,1,0:T(8,128)(2,1)S(1)}, bf16[8,32,256]{2,1,0:T(8,128)(2,1)S(1)}, u32[]{:S(2)}, u32[]{:S(2)}) collective-permute-start(bf16[8,32,256]{2,1,0:T(8,128)(2,1)S(1)} %get-tuple-element.122), channel_id=1, source_target_pairs={{0,12},{1,13},{2,14},{3,15},{4,8},{5,9},{6,10},{7,11},{8,4},{9,5},... | collective-permute-start | bytes 393224 | tf_op jit(solution)/shard_map/ppermute | solution.py:587
  42.4 2.1 %collective-permute-start.15 = (bf16[2,3,16,512]{3,2,1,0:T(8,128)(2,1)S(1)}, bf16[2,3,16,512]{3,2,1,0:T(8,128)(2,1)S(1)}, u32[]{:S(2)}, u32[]{:S(2)}) collective-permute-start(bf16[2,3,16,512]{3,2,1,0:T(8,128)(2,1)S(1)} %get-tuple-element.119), channel_id=1, source_target_pairs={{0,15},{1,2},{2,1},{3,4},{4,3},{5,6},{6,5},{7,8},{8,7},{9,10},{10,... | collective-permute-start | bytes 294920 | tf_op jit(solution)/shard_map/ppermute | solution.py:43
  44.5 1.3 %collective-permute-start.16 = (bf16[5,32,256]{2,1,0:T(8,128)(2,1)S(1)}, bf16[5,32,256]{2,1,0:T(8,128)(2,1)S(1)}, u32[]{:S(2)}, u32[]{:S(2)}) collective-permute-start(bf16[5,32,256]{2,1,0:T(8,128)(2,1)S(1)} %get-tuple-element.117.after_ref), channel_id=1, source_target_pairs={{0,4},{1,5},{2,6},{3,7},{4,0},{5,1},{6,2},{7,3},{8,12},{9,13},{10,... | collective-permute-start | bytes 245768 | tf_op jit(solution)/shard_map/ppermute | solution.py:587
  45.8 3.6 %collective-permute-done.15.second_in = bf16[2,3,16,512]{3,2,1,0:T(8,128)(2,1)S(1)} collective-permute-done((bf16[2,3,16,512]{3,2,1,0:T(8,128)(2,1)S(1)}, bf16[2,3,16,512]{3,2,1,0:T(8,128)(2,1)S(1)}, u32[]{:S(2)}, u32[]{:S(2)}) %collective-permute-start.15) | collective-permute-done | bytes 98336 | tf_op jit(solution)/shard_map/ppermute | solution.py:43
  49.4 1.0 %shard_map.117.after_ref = bf16[2,128,512]{2,1,0:T(8,128)(2,1)} custom-call(s32[1]{0:T(128)} %bitcast.me_ref, bf16[5,32,256]{2,1,0:T(8,128)(2,1)S(1)} %get-tuple-element.117.after_ref, s32[1,8,16]{2,1,0:T(8,128)S(1)} %copy-done, f32[2,128,512]{2,1,0:T(8,128)S(1)} %get-tuple-element.118.node_ref, bf16[2,3,16,512]{3,2,1,0:T(8,128)(2,1)S(1)} %collective-permute-done.9.plus_ref, ...), custom_call_target="tpu_custom_call" | custom-call | flops 1000000 | bytes 10000 | tf_op jit(solution)/shard_map/pallas_call | solution.py:468
  50.4 0.6 %collective-permute-done.16.refs_0_ = bf16[5,32,256]{2,1,0:T(8,128)(2,1)S(1)} collective-permute-done((bf16[5,32,256]{2,1,0:T(8,128)(2,1)S(1)}, bf16[5,32,256]{2,1,0:T(8,128)(2,1)S(1)}, u32[]{:S(2)}, u32[]{:S(2)}) %collective-permute-start.16) | collective-permute-done | bytes 81952 | tf_op jit(solution)/shard_map/ppermute | solution.py:587
  51.0 1.5 %collective-permute-done.18.refs_2_ = bf16[5,32,256]{2,1,0:T(8,128)(2,1)S(1)} collective-permute-done((bf16[5,32,256]{2,1,0:T(8,128)(2,1)S(1)}, bf16[5,32,256]{2,1,0:T(8,128)(2,1)S(1)}, u32[]{:S(2)}, u32[]{:S(2)}) %collective-permute-start.18) | collective-permute-done | bytes 81952 | tf_op jit(solution)/shard_map/ppermute | solution.py:587
  52.5 0.0 collective-permute-done.17.refs_1_
  52.5 0.8 %shard_map.118 = f32[32,2048]{1,0:T(8,128)} custom-call(bf16[2,128,512]{2,1,0:T(8,128)(2,1)} %shard_map.117.after_ref, f32[32,768]{1,0:T(8,128)S(1)} %get-tuple-element.120.own_a, f32[32,1280]{1,0:T(8,128)S(1)} %get-tuple-element.121.own_b, bf16[5,32,256]{2,1,0:T(8,128)(2,1)S(1)} %collective-permute-done.16.refs_0_, ...), custom_call_target="tpu_custom_call" | custom-call | flops 1000000 | bytes 10000 | tf_op jit(solution)/shard_map/pallas_call | solution.py:468
  (8 shorter events, 0.1 us)
Async XLA Ops:
  1.8 8.6 %collective-permute-start = (bf16[2,3,16,512]{3,2,1,0:T(8,128)(2,1)S(1)}, bf16[2,3,16,512]{3,2,1,0:T(8,128)(2,1)S(1)}, u32[]{:S(2)}, u32[]{:S(2)}) collective-permute-start(bf16[2,3,16,512]{3,2,1,0:T(8,128)(2,1)S(1)} %get-tuple-element.66), channel_id=1, source_target_pairs={{0,4},{1,5},{2,6},{3,7},{4,8},{5,9},{6,10},{7,11},{8,12},{9,13},{1... | collective-permute-start | bytes 294920 | tf_op jit(solution)/shard_map/ppermute | solution.py:28
  4.9 6.4 %collective-permute-start.1 = (bf16[2,3,16,512]{3,2,1,0:T(8,128)(2,1)S(1)}, bf16[2,3,16,512]{3,2,1,0:T(8,128)(2,1)S(1)}, u32[]{:S(2)}, u32[]{:S(2)}) collective-permute-start(bf16[2,3,16,512]{3,2,1,0:T(8,128)(2,1)S(1)} %get-tuple-element.67), channel_id=1, source_target_pairs={{0,12},{1,13},{2,14},{3,15},{4,0},{5,1},{6,2},{7,3},{8,4},{9,5},{1... | collective-permute-start | bytes 294920 | tf_op jit(solution)/shard_map/ppermute | solution.py:28
  11.3 5.0 %collective-permute-start.2 = (bf16[2,3,16,512]{3,2,1,0:T(8,128)(2,1)S(1)}, bf16[2,3,16,512]{3,2,1,0:T(8,128)(2,1)S(1)}, u32[]{:S(2)}, u32[]{:S(2)}) collective-permute-start(bf16[2,3,16,512]{3,2,1,0:T(8,128)(2,1)S(1)} %get-tuple-element.70.after_ref), channel_id=1, source_target_pairs={{0,1},{1,0},{2,3},{3,2},{4,5},{5,4},{6,7},{7,6},{8,9},{9,8},{10,11... | collective-permute-start | bytes 294920 | tf_op jit(solution)/shard_map/ppermute | solution.py:43
  11.4 6.8 %collective-permute-start.3 = (bf16[2,3,16,512]{3,2,1,0:T(8,128)(2,1)S(1)}, bf16[2,3,16,512]{3,2,1,0:T(8,128)(2,1)S(1)}, u32[]{:S(2)}, u32[]{:S(2)}) collective-permute-start(bf16[2,3,16,512]{3,2,1,0:T(8,128)(2,1)S(1)} %get-tuple-element.71), channel_id=1, source_target_pairs={{0,15},{1,2},{2,1},{3,4},{4,3},{5,6},{6,5},{7,8},{8,7},{9,10},{10,... | collective-permute-start | bytes 294920 | tf_op jit(solution)/shard_map/ppermute | solution.py:43
  22.0 2.4 %collective-permute-start.4 = (bf16[4,32,1024]{2,1,0:T(8,128)(2,1)S(1)}, bf16[4,32,1024]{2,1,0:T(8,128)(2,1)S(1)}, u32[]{:S(2)}, u32[]{:S(2)}) collective-permute-start(bf16[4,32,1024]{2,1,0:T(8,128)(2,1)S(1)} %get-tuple-element.85), channel_id=1, source_target_pairs={{0,1},{1,0},{2,3},{3,2},{4,5},{5,4},{6,7},{7,6},{8,9},{9,8},{10,11... | collective-permute-start | bytes 786440 | tf_op jit(solution)/shard_map/ppermute | solution.py:560
  23.7 3.1 %collective-permute-start.5 = (bf16[2,4,32,512]{3,2,1,0:T(8,128)(2,1)S(1)}, bf16[2,4,32,512]{3,2,1,0:T(8,128)(2,1)S(1)}, u32[]{:S(2)}, u32[]{:S(2)}) collective-permute-start(bf16[2,4,32,512]{3,2,1,0:T(8,128)(2,1)S(1)} %get-tuple-element.89), channel_id=1, source_target_pairs={{0,1},{1,0},{2,3},{3,2},{4,5},{5,4},{6,7},{7,6},{8,9},{9,8},{10,11... | collective-permute-start | bytes 786440 | tf_op jit(solution)/shard_map/ppermute | solution.py:560
  24.3 6.6 %collective-permute-start.7 = (bf16[4,32,1024]{2,1,0:T(8,128)(2,1)S(1)}, bf16[4,32,1024]{2,1,0:T(8,128)(2,1)S(1)}, u32[]{:S(2)}, u32[]{:S(2)}) collective-permute-start(bf16[4,32,1024]{2,1,0:T(8,128)(2,1)S(1)} %get-tuple-element.92), channel_id=1, source_target_pairs={{0,1},{1,0},{2,3},{3,2},{4,5},{5,4},{6,7},{7,6},{8,9},{9,8},{10,11... | collective-permute-start | bytes 786440 | tf_op jit(solution)/shard_map/ppermute | solution.py:560
  24.5 10.2 %collective-permute-start.8 = (bf16[4,32,1024]{2,1,0:T(8,128)(2,1)S(1)}, bf16[4,32,1024]{2,1,0:T(8,128)(2,1)S(1)}, u32[]{:S(2)}, u32[]{:S(2)}) collective-permute-start(bf16[4,32,1024]{2,1,0:T(8,128)(2,1)S(1)} %add_convert_fusion.refs_0_), channel_id=1, source_target_pairs={{0,2},{1,3},{2,0},{3,1},{4,6},{5,7},{6,4},{7,5},{8,10},{9,11},{10,... | collective-permute-start | bytes 786440 | tf_op jit(solution)/shard_map/ppermute | solution.py:567
  26.3 1.4 %collective-permute-start.6 = (bf16[4,32,512]{2,1,0:T(8,128)(2,1)S(1)}, bf16[4,32,512]{2,1,0:T(8,128)(2,1)S(1)}, u32[]{:S(2)}, u32[]{:S(2)}) collective-permute-start(bf16[4,32,512]{2,1,0:T(8,128)(2,1)S(1)} %get-tuple-element.90), channel_id=1, source_target_pairs={{0,1},{1,0},{2,3},{3,2},{4,5},{5,4},{6,7},{7,6},{8,9},{9,8},{10,11... | collective-permute-start | bytes 393224 | tf_op jit(solution)/shard_map/ppermute | solution.py:560
  26.7 11.6 %collective-permute-start.13 = (bf16[4,32,512]{2,1,0:T(8,128)(2,1)S(1)}, bf16[4,32,512]{2,1,0:T(8,128)(2,1)S(1)}, u32[]{:S(2)}, u32[]{:S(2)}) collective-permute-start(bf16[4,32,512]{2,1,0:T(8,128)(2,1)S(1)} %get-tuple-element.116), channel_id=1, source_target_pairs={{0,1},{1,0},{2,3},{3,2},{4,5},{5,4},{6,7},{7,6},{8,9},{9,8},{10,11... | collective-permute-start | bytes 393224 | tf_op jit(solution)/shard_map/ppermute | solution.py:560
  27.8 12.0 %collective-permute-start.12 = (bf16[4,32,1024]{2,1,0:T(8,128)(2,1)S(1)}, bf16[4,32,1024]{2,1,0:T(8,128)(2,1)S(1)}, u32[]{:S(2)}, u32[]{:S(2)}) collective-permute-start(bf16[4,32,1024]{2,1,0:T(8,128)(2,1)S(1)} %shard_map.112.after_ref.refs_0_), channel_id=1, source_target_pairs={{0,2},{1,3},{2,0},{3,1},{4,6},{5,7},{6,4},{7,5},{8,10},{9,11},{10,... | collective-permute-start | bytes 786440 | tf_op jit(solution)/shard_map/ppermute | solution.py:577
  30.8 7.5 %collective-permute-start.10 = (bf16[2,3,16,512]{3,2,1,0:T(8,128)(2,1)S(1)}, bf16[2,3,16,512]{3,2,1,0:T(8,128)(2,1)S(1)}, u32[]{:S(2)}, u32[]{:S(2)}) collective-permute-start(bf16[2,3,16,512]{3,2,1,0:T(8,128)(2,1)S(1)} %get-tuple-element.110), channel_id=1, source_target_pairs={{0,4},{1,5},{2,6},{3,7},{4,8},{5,9},{6,10},{7,11},{8,12},{9,13},{1... | collective-permute-start | bytes 294920 | tf_op jit(solution)/shard_map/ppermute | solution.py:28
  30.9 7.5 %collective-permute-start.9 = (bf16[2,3,16,512]{3,2,1,0:T(8,128)(2,1)S(1)}, bf16[2,3,16,512]{3,2,1,0:T(8,128)(2,1)S(1)}, u32[]{:S(2)}, u32[]{:S(2)}) collective-permute-start(bf16[2,3,16,512]{3,2,1,0:T(8,128)(2,1)S(1)} %get-tuple-element.109), channel_id=1, source_target_pairs={{0,12},{1,13},{2,14},{3,15},{4,0},{5,1},{6,2},{7,3},{8,4},{9,5},{1... | collective-permute-start | bytes 294920 | tf_op jit(solution)/shard_map/ppermute | solution.py:28
  34.8 5.0 %collective-permute-start.11 = (bf16[6,32,256]{2,1,0:T(8,128)(2,1)S(1)}, bf16[6,32,256]{2,1,0:T(8,128)(2,1)S(1)}, u32[]{:S(2)}, u32[]{:S(2)}) collective-permute-start(bf16[6,32,256]{2,1,0:T(8,128)(2,1)S(1)} %get-tuple-element.93.after_ref), channel_id=1, source_target_pairs={{0,4},{1,5},{2,6},{3,7},{4,0},{5,1},{6,2},{7,3},{8,12},{9,13},{10,... | collective-permute-start | bytes 294920 | tf_op jit(solution)/shard_map/ppermute | solution.py:587
  39.9 9.4 %copy-start = (s32[1,8,16]{2,1,0:T(8,128)S(1)}, s32[1,8,16]{2,1,0:T(8,128)}, u32[]{:S(2)}) copy-start(s32[1,8,16]{2,1,0:T(8,128)} %send_ref.1) | copy-start | bytes 1540
  39.9 12.5 %collective-permute-start.17 = (bf16[8,32,256]{2,1,0:T(8,128)(2,1)S(1)}, bf16[8,32,256]{2,1,0:T(8,128)(2,1)S(1)}, u32[]{:S(2)}, u32[]{:S(2)}) collective-permute-start(bf16[8,32,256]{2,1,0:T(8,128)(2,1)S(1)} %get-tuple-element.122), channel_id=1, source_target_pairs={{0,12},{1,13},{2,14},{3,15},{4,8},{5,9},{6,10},{7,11},{8,4},{9,5},... | collective-permute-start | bytes 393224 | tf_op jit(solution)/shard_map/ppermute | solution.py:587
  42.4 3.4 %collective-permute-start.14 = (bf16[2,3,16,512]{3,2,1,0:T(8,128)(2,1)S(1)}, bf16[2,3,16,512]{3,2,1,0:T(8,128)(2,1)S(1)}, u32[]{:S(2)}, u32[]{:S(2)}) collective-permute-start(bf16[2,3,16,512]{3,2,1,0:T(8,128)(2,1)S(1)} %get-tuple-element.111.refs_0_), channel_id=1, source_target_pairs={{0,1},{1,0},{2,3},{3,2},{4,5},{5,4},{6,7},{7,6},{8,9},{9,8},{10,11... | collective-permute-start | bytes 294920 | tf_op jit(solution)/shard_map/ppermute | solution.py:43
  42.4 7.0 %collective-permute-start.15 = (bf16[2,3,16,512]{3,2,1,0:T(8,128)(2,1)S(1)}, bf16[2,3,16,512]{3,2,1,0:T(8,128)(2,1)S(1)}, u32[]{:S(2)}, u32[]{:S(2)}) collective-permute-start(bf16[2,3,16,512]{3,2,1,0:T(8,128)(2,1)S(1)} %get-tuple-element.119), channel_id=1, source_target_pairs={{0,15},{1,2},{2,1},{3,4},{4,3},{5,6},{6,5},{7,8},{8,7},{9,10},{10,... | collective-permute-start | bytes 294920 | tf_op jit(solution)/shard_map/ppermute | solution.py:43
  44.5 6.5 %collective-permute-start.16 = (bf16[5,32,256]{2,1,0:T(8,128)(2,1)S(1)}, bf16[5,32,256]{2,1,0:T(8,128)(2,1)S(1)}, u32[]{:S(2)}, u32[]{:S(2)}) collective-permute-start(bf16[5,32,256]{2,1,0:T(8,128)(2,1)S(1)} %get-tuple-element.117.after_ref), channel_id=1, source_target_pairs={{0,4},{1,5},{2,6},{3,7},{4,0},{5,1},{6,2},{7,3},{8,12},{9,13},{10,... | collective-permute-start | bytes 245768 | tf_op jit(solution)/shard_map/ppermute | solution.py:587
  45.8 6.7 %collective-permute-start.18 = (bf16[5,32,256]{2,1,0:T(8,128)(2,1)S(1)}, bf16[5,32,256]{2,1,0:T(8,128)(2,1)S(1)}, u32[]{:S(2)}, u32[]{:S(2)}) collective-permute-start(bf16[5,32,256]{2,1,0:T(8,128)(2,1)S(1)} %get-tuple-element.123), channel_id=1, source_target_pairs={{0,8},{1,9},{2,10},{3,11},{4,12},{5,13},{6,14},{7,15},{8,0},{9,1},... | collective-permute-start | bytes 245768 | tf_op jit(solution)/shard_map/ppermute | solution.py:587

commit v9 on v8

--- a/solution.py
+++ b/solution.py
@@ -575,14 +575,6 @@
         (*other_b, *core_other_b),
     )
     y_b = lax.ppermute(y_sent, "patch", flop)
-    node, to_plus, to_minus, own_right, own_left = call(
-        functools.partial(node_kernel, groups, 1),
-        [((members, node_rows, width), f32), three, three, one, one],
-        (y_sent, *grads[0::3], *grads[1::3], *grads[2::3], wq, wk, wv),
-        specs=[pl.ANY],
-    )
-    from_plus = shifted(to_minus, -row_width)
-    from_minus = shifted(to_plus, row_width)
     def exchange(sent, distance):
         return lax.ppermute(sent, "patch", along_z(count, distance))
 
@@ -596,22 +588,30 @@
         (y_sent, own_a, core_own, y_a), specs=[pl.ANY], flops=2 * 10**10,
     )
     in_a = exchange(sent_a, 1)
-    outgoing = call(
-        relay_kernel, [three, three],
-        (place, sent_a, own_right, own_left, from_plus, from_minus),
-        specs=[pltpu.SMEM, pl.ANY], scratch=[trio],
-    )
-    back = swap(outgoing, 1)
+    node, to_plus, to_minus, own_right, own_left = call(
+        functools.partial(node_kernel, groups, 1),
+        [((members, node_rows, width), f32), three, three, one, one],
+        (sent_a, *grads[0::3], *grads[1::3], *grads[2::3], wq, wk, wv),
+        specs=[pl.ANY],
+    )
+    from_plus = shifted(to_minus, -row_width)
+    from_minus = shifted(to_plus, row_width)
     more, blocks = wide // 256, (wide + width) // 256
     own_a, own_b, *sent = call(
         functools.partial(second_kernel, 1, len(later)),
         [((rows, wide), f32), ((rows, wide + width), f32)]
         + [((blocks + (0 if k % 2 else more), rows, 256), bf16) for k in range(1, planes)],
-        (place, outgoing[0], kept_a, in_a, out_a, y_b, *own_b, *core_own_b),
+        (place, node, kept_a, in_a, out_a, y_b, *own_b, *core_own_b),
         specs=[pltpu.SMEM, pl.ANY],
         scratch=[pltpu.VMEM((planes, rows, width), f32)],
     )
     received = [exchange(shard, k) for k, shard in enumerate(sent, 1)]
+    outgoing = call(
+        relay_kernel, [three, three],
+        (place, sent[0], own_right, own_left, from_plus, from_minus),
+        specs=[pltpu.SMEM, pl.ANY], scratch=[trio],
+    )
+    back = swap(outgoing, 1)
     (node_grad,) = call(
         finish_kernel, [((members, node_rows, width), bf16)],
         (place, sent[0], send_rows, node, from_plus, from_minus, *back),

time: 53.4 us -> 54.9 us (1.028)
  starting transfers between devices: 21.9 us -> 22.9 us
    ppermute x1, waiting for transfers between devices: 0.01 us -> 3.83 us  [body(): y_a = lax.ppermute(y_sent, 'patch', flop)]
    ppermute x4, starting transfers between devices: 5.6 us -> 7.37 us  [swap(): lax.ppermute(shard, 'patch', perm)]
    ppermute x4, waiting for transfers between devices: 5.51 us -> 3.74 us  [swap(): lax.ppermute(shard, 'patch', perm)]
    ppermute x4, waiting for transfers between devices: 5.1 us -> 3.34 us  [shifted(): lax.ppermute(shard, 'patch', [(i, (i + by) % count) for i in range(count)])]
    ppermute x4, starting transfers between devices: 9.03 us -> 7.41 us  [shifted(): lax.ppermute(shard, 'patch', [(i, (i + by) % count) for i in range(count)])]
    ppermute x4, starting transfers between devices: 3.82 us -> 4.71 us  [exchange(): return lax.ppermute(sent, 'patch', along_z(count, distance))]
  transfers between devices with their start and end apart: 19 -> 19, of which waited for: 9 -> 10; matrix products, arithmetic and copies ran while one was open for 0% -> 0% of each run, Pallas kernels for 18% -> 18%
where the time goes in v9:
time: 54.9 us; the launch traced here: 54.7 us
  starting transfers between devices  22.9 us (42%)
  Pallas kernels  15.6 us (28%)
  waiting for transfers between devices  15.5 us (28%)
  between operations  0.77 us (1%)
    pallas_call x15, Pallas kernels, call(): pl.pallas_call(kernel, out_shape=[jax.ShapeDtypeStruct(*o) if final else...  15.6 us
    ppermute x4, starting transfers between devices, shifted(): lax.ppermute(shard, 'patch', [(i, (i + by) % count) for i in range(count)])  7.41 us
    ppermute x4, starting transfers between devices, swap(): lax.ppermute(shard, 'patch', perm)  7.37 us
    ppermute x4, starting transfers between devices, exchange(): return lax.ppermute(sent, 'patch', along_z(count, distance))  4.71 us
    ppermute x1, waiting for transfers between devices, body(): y_a = lax.ppermute(y_sent, 'patch', flop)  3.83 us
    ppermute x4, waiting for transfers between devices, swap(): lax.ppermute(shard, 'patch', perm)  3.74 us
    ppermute x4, waiting for transfers between devices, exchange(): return lax.ppermute(sent, 'patch', along_z(count, distance))  3.68 us
    ppermute x4, waiting for transfers between devices, shifted(): lax.ppermute(shard, 'patch', [(i, (i + by) % count) for i in range(count)])  3.34 us
  transfers between devices with their start and end apart: 19, of which 10 were waited for; matrix products, arithmetic and copies ran while one was open for 0% of the time, Pallas kernels for 18%

profile of v9, /device:TPU:0, one launch (start us, length us, event | category | flops | bytes accessed | tf_op | source)
XLA Modules:
  0.0 54.7 jit_solution(915860545708693099)
XLA Ops:
  0.6 1.2 %shard_map.104 = (bf16[2,3,16,512]{3,2,1,0:T(8,128)(2,1)S(1)}, bf16[2,3,16,512]{3,2,1,0:T(8,128)(2,1)S(1)}, bf16[2,1,16,512]{3,2,1,0:T(8,128)(2,1)S(1)}, bf16[2,...) custom-call(s32[1,8,16]{2,1,0:T(8,128)} %send_ref.1, bf16[2,128,512]{2,1,0:T(8,128)(2,1)} %x_hbm.1), custom_call_target="tpu_custom_call" | custom-call | flops 1000000 | bytes 10000 | tf_op jit(solution)/shard_map/pallas_call | solution.py:468
  1.8 3.1 %collective-permute-start = (bf16[2,3,16,512]{3,2,1,0:T(8,128)(2,1)S(1)}, bf16[2,3,16,512]{3,2,1,0:T(8,128)(2,1)S(1)}, u32[]{:S(2)}, u32[]{:S(2)}) collective-permute-start(bf16[2,3,16,512]{3,2,1,0:T(8,128)(2,1)S(1)} %get-tuple-element.66), channel_id=1, source_target_pairs={{0,4},{1,5},{2,6},{3,7},{4,8},{5,9},{6,10},{7,11},{8,12},{9,13},{1... | collective-permute-start | bytes 294920 | tf_op jit(solution)/shard_map/ppermute | solution.py:28
  4.9 2.1 %collective-permute-start.1 = (bf16[2,3,16,512]{3,2,1,0:T(8,128)(2,1)S(1)}, bf16[2,3,16,512]{3,2,1,0:T(8,128)(2,1)S(1)}, u32[]{:S(2)}, u32[]{:S(2)}) collective-permute-start(bf16[2,3,16,512]{3,2,1,0:T(8,128)(2,1)S(1)} %get-tuple-element.67), channel_id=1, source_target_pairs={{0,12},{1,13},{2,14},{3,15},{4,0},{5,1},{6,2},{7,3},{8,4},{9,5},{1... | collective-permute-start | bytes 294920 | tf_op jit(solution)/shard_map/ppermute | solution.py:28
  7.0 2.6 %shard_map.105 = (bf16[8,2,128,128]{3,2,1,0:T(8,128)(2,1)S(1)}, bf16[8,2,128,128]{3,2,1,0:T(8,128)(2,1)S(1)}, bf16[8,2,128,128]{3,2,1,0:T(8,128)(2,1)S(1)}, bf16...) custom-call(bf16[2,1,16,512]{3,2,1,0:T(8,128)(2,1)S(1)} %get-tuple-e, ...), custom_call_target="tpu_custom_call" | custom-call | flops 1000000 | bytes 10000 | tf_op jit(solution)/shard_map/pallas_call | solution.py:468
  9.7 0.8 %collective-permute-done.plus_ref = bf16[2,3,16,512]{3,2,1,0:T(8,128)(2,1)S(1)} collective-permute-done((bf16[2,3,16,512]{3,2,1,0:T(8,128)(2,1)S(1)}, bf16[2,3,16,512]{3,2,1,0:T(8,128)(2,1)S(1)}, u32[]{:S(2)}, u32[]{:S(2)}) %collective-permute-start) | collective-permute-done | bytes 98336 | tf_op jit(solution)/shard_map/ppermute | solution.py:28
  10.4 0.8 %collective-permute-done.1.minus_ref = bf16[2,3,16,512]{3,2,1,0:T(8,128)(2,1)S(1)} collective-permute-done((bf16[2,3,16,512]{3,2,1,0:T(8,128)(2,1)S(1)}, bf16[2,3,16,512]{3,2,1,0:T(8,128)(2,1)S(1)}, u32[]{:S(2)}, u32[]{:S(2)}) %collective-permute-start.1) | collective-permute-done | bytes 98336 | tf_op jit(solution)/shard_map/ppermute | solution.py:28
  11.3 0.1 collective-permute-start.2
  11.4 3.4 %collective-permute-start.3 = (bf16[2,3,16,512]{3,2,1,0:T(8,128)(2,1)S(1)}, bf16[2,3,16,512]{3,2,1,0:T(8,128)(2,1)S(1)}, u32[]{:S(2)}, u32[]{:S(2)}) collective-permute-start(bf16[2,3,16,512]{3,2,1,0:T(8,128)(2,1)S(1)} %get-tuple-element.71), channel_id=1, source_target_pairs={{0,15},{1,2},{2,1},{3,4},{4,3},{5,6},{6,5},{7,8},{8,7},{9,10},{10,... | collective-permute-start | bytes 294920 | tf_op jit(solution)/shard_map/ppermute | solution.py:43
  14.8 1.4 %shard_map.108.refs_2_.refs_4_.refs_3_ = f32[256,128]{1,0:T(8,128)S(1)} custom-call(bf16[2,3,16,512]{3,2,1,0:T(8,128)(2,1)S(1)} %get-tuple-element.70.after_ref, s32[128,256]{1,0:T(8,128)S(1)} %get-tuple-element.76.neigh_ref, s32[1,128]{1,0:T(1,128)S(1)} %get-tuple-element.77.count_ref), custom_call_target="tpu_custom_call" | custom-call | flops 1000000 | bytes 10000 | tf_op jit(solution)/shard_map/pallas_call | solution.py:468
  16.3 0.0 collective-permute-done.2.first_in
  16.3 1.9 %collective-permute-done.3.second_in = bf16[2,3,16,512]{3,2,1,0:T(8,128)(2,1)S(1)} collective-permute-done((bf16[2,3,16,512]{3,2,1,0:T(8,128)(2,1)S(1)}, bf16[2,3,16,512]{3,2,1,0:T(8,128)(2,1)S(1)}, u32[]{:S(2)}, u32[]{:S(2)}) %collective-permute-start.3) | collective-permute-done | bytes 98336 | tf_op jit(solution)/shard_map/ppermute | solution.py:43
  18.2 0.6 %shard_map.107 = (bf16[4,2,128,128]{3,2,1,0:T(8,128)(2,1)S(1)}, bf16[4,2,128,128]{3,2,1,0:T(8,128)(2,1)S(1)}, bf16[4,2,128,128]{3,2,1,0:T(8,128)(2,1)S(1)}, bf16...) custom-call(s32[1]{0:T(128)} %bitcast.me_ref, bf16[2,3,16,512]{3,2,1,0:T(8,128)(2,1)S(1)} %collective-permute-done.plus_ref, ...), custom_call_target="tpu_custom_call" | custom-call | flops 1000000 | bytes 10000 | tf_op jit(solution)/shard_map/pallas_call | solution.py:468
  18.8 3.1 %shard_map.110 = (f32[4,32,1024]{2,1,0:T(8,128)S(1)}, f32[4,32,1024]{2,1,0:T(8,128)S(1)}, bf16[4,32,1024]{2,1,0:T(8,128)(2,1)S(1)}, bf16[4,32,1024]{2,1,0:T(8,12...) custom-call(s32[1]{0:T(128)} %bitcast.me_ref, ...), custom_call_target="tpu_custom_call" | custom-call | flops 1000000 | bytes 10000 | tf_op jit(solution)/shard_map/pallas_call | solution.py:468
  22.0 0.1 collective-permute-start.4
  22.0 1.7 %shard_map.109 = (f32[4,32,512]{2,1,0:T(8,128)S(1)}, f32[4,32,512]{2,1,0:T(8,128)S(1)}, bf16[2,4,32,512]{3,2,1,0:T(8,128)(2,1)S(1)}, bf16[2,128,128]{2,1,0:T(8,1...) custom-call(s32[1]{0:T(128)} %bitcast.me_ref, ...), custom_call_target="tpu_custom_call" | custom-call | flops 1000000 | bytes 10000 | tf_op jit(solution)/shard_map/pallas_call | solution.py:468
  23.7 0.6 %collective-permute-start.5 = (bf16[2,4,32,512]{3,2,1,0:T(8,128)(2,1)S(1)}, bf16[2,4,32,512]{3,2,1,0:T(8,128)(2,1)S(1)}, u32[]{:S(2)}, u32[]{:S(2)}) collective-permute-start(bf16[2,4,32,512]{3,2,1,0:T(8,128)(2,1)S(1)} %get-tuple-element.89), channel_id=1, source_target_pairs={{0,1},{1,0},{2,3},{3,2},{4,5},{5,4},{6,7},{7,6},{8,9},{9,8},{10,11... | collective-permute-start | bytes 786440 | tf_op jit(solution)/shard_map/ppermute | solution.py:560
  24.3 0.1 collective-permute-start.7
  24.4 0.1 add_convert_fusion.refs_0_
  24.5 0.1 collective-permute-start.8
  24.6 1.7 %shard_map.111 = (f32[4,32,512]{2,1,0:T(8,128)S(1)}, f32[4,32,512]{2,1,0:T(8,128)S(1)}, bf16[4,32,512]{2,1,0:T(8,128)(2,1)S(1)}, bf16[4,32,512]{2,1,0:T(8,128)(2...) custom-call(s32[1]{0:T(128)} %bitcast.me_ref, ...), custom_call_target="tpu_custom_call" | custom-call | flops 1000000 | bytes 10000 | tf_op jit(solution)/shard_map/pallas_call | solution.py:468
  26.3 0.5 collective-permute-start.6
  26.7 0.1 collective-permute-start.11
  26.9 0.9 %collective-permute-done.6.refs_3_ = bf16[4,32,512]{2,1,0:T(8,128)(2,1)S(1)} collective-permute-done((bf16[4,32,512]{2,1,0:T(8,128)(2,1)S(1)}, bf16[4,32,512]{2,1,0:T(8,128)(2,1)S(1)}, u32[]{:S(2)}, u32[]{:S(2)}) %collective-permute-start.6) | collective-permute-done | bytes 131104 | tf_op jit(solution)/shard_map/ppermute | solution.py:560
  27.7 0.1 shard_map.112.after_ref
  27.8 2.0 %collective-permute-start.10 = (bf16[4,32,1024]{2,1,0:T(8,128)(2,1)S(1)}, bf16[4,32,1024]{2,1,0:T(8,128)(2,1)S(1)}, u32[]{:S(2)}, u32[]{:S(2)}) collective-permute-start(bf16[4,32,1024]{2,1,0:T(8,128)(2,1)S(1)} %shard_map.112.after_ref), channel_id=1, source_target_pairs={{0,2},{1,3},{2,0},{3,1},{4,6},{5,7},{6,4},{7,5},{8,10},{9,11},{10,... | collective-permute-start | bytes 786440 | tf_op jit(solution)/shard_map/ppermute | solution.py:577
  29.8 0.0 collective-permute-done.7.core_in
  29.8 3.8 %collective-permute-done.8.y_in = bf16[4,32,1024]{2,1,0:T(8,128)(2,1)S(1)} collective-permute-done((bf16[4,32,1024]{2,1,0:T(8,128)(2,1)S(1)}, bf16[4,32,1024]{2,1,0:T(8,128)(2,1)S(1)}, u32[]{:S(2)}, u32[]{:S(2)}) %collective-permute-start.8) | collective-permute-done | bytes 262176 | tf_op jit(solution)/shard_map/ppermute | solution.py:567
  33.6 0.1 shard_map.113
  33.7 0.1 collective-permute-start.9
  33.8 1.0 %shard_map.114 = (f32[2,128,512]{2,1,0:T(8,128)S(1)}, bf16[2,3,16,512]{3,2,1,0:T(8,128)(2,1)S(1)}, bf16[2,3,16,512]{3,2,1,0:T(8,128)(2,1)S(1)}, bf16[2,1,16,512]...) custom-call(bf16[6,32,256]{2,1,0:T(8,128)(2,1)S(1)} %get-tuple-element.93.refs_0_, ...), custom_call_target="tpu_custom_call" | custom-call | flops 1000000 | bytes 10000 | tf_op jit(solution)/shard_map/pallas_call | solution.py:468
  34.8 2.2 %collective-permute-start.12 = (bf16[2,3,16,512]{3,2,1,0:T(8,128)(2,1)S(1)}, bf16[2,3,16,512]{3,2,1,0:T(8,128)(2,1)S(1)}, u32[]{:S(2)}, u32[]{:S(2)}) collective-permute-start(bf16[2,3,16,512]{3,2,1,0:T(8,128)(2,1)S(1)} %get-tuple-element.114), channel_id=1, source_target_pairs={{0,12},{1,13},{2,14},{3,15},{4,0},{5,1},{6,2},{7,3},{8,4},{9,5},{1... | collective-permute-start | bytes 294920 | tf_op jit(solution)/shard_map/ppermute | solution.py:28
  37.1 0.0 collective-permute-start.13
  37.1 1.7 %collective-permute-done.9.refs_2_ = bf16[6,32,256]{2,1,0:T(8,128)(2,1)S(1)} collective-permute-done((bf16[6,32,256]{2,1,0:T(8,128)(2,1)S(1)}, bf16[6,32,256]{2,1,0:T(8,128)(2,1)S(1)}, u32[]{:S(2)}, u32[]{:S(2)}) %collective-permute-start.9) | collective-permute-done | bytes 98336 | tf_op jit(solution)/shard_map/ppermute | solution.py:579
  38.8 0.1 shard_map.115
  38.9 3.4 %collective-permute-start.17 = (bf16[8,32,256]{2,1,0:T(8,128)(2,1)S(1)}, bf16[8,32,256]{2,1,0:T(8,128)(2,1)S(1)}, u32[]{:S(2)}, u32[]{:S(2)}) collective-permute-start(bf16[8,32,256]{2,1,0:T(8,128)(2,1)S(1)} %get-tuple-element.122), channel_id=1, source_target_pairs={{0,12},{1,13},{2,14},{3,15},{4,8},{5,9},{6,10},{7,11},{8,4},{9,5},... | collective-permute-start | bytes 393224 | tf_op jit(solution)/shard_map/ppermute | solution.py:579
  42.3 0.0 collective-permute-done.12.plus_ref
  42.3 1.7 %collective-permute-done.13.minus_ref = bf16[2,3,16,512]{3,2,1,0:T(8,128)(2,1)S(1)} collective-permute-done((bf16[2,3,16,512]{3,2,1,0:T(8,128)(2,1)S(1)}, bf16[2,3,16,512]{3,2,1,0:T(8,128)(2,1)S(1)}, u32[]{:S(2)}, u32[]{:S(2)}) %collective-permute-start.13) | collective-permute-done | bytes 98336 | tf_op jit(solution)/shard_map/ppermute | solution.py:28
  44.1 0.0 copy-start
  44.1 0.1 collective-permute-start.14
  44.2 3.8 %collective-permute-start.15 = (bf16[2,3,16,512]{3,2,1,0:T(8,128)(2,1)S(1)}, bf16[2,3,16,512]{3,2,1,0:T(8,128)(2,1)S(1)}, u32[]{:S(2)}, u32[]{:S(2)}) collective-permute-start(bf16[2,3,16,512]{3,2,1,0:T(8,128)(2,1)S(1)} %get-tuple-element.119), channel_id=1, source_target_pairs={{0,15},{1,2},{2,1},{3,4},{4,3},{5,6},{6,5},{7,8},{8,7},{9,10},{10,... | collective-permute-start | bytes 294920 | tf_op jit(solution)/shard_map/ppermute | solution.py:43
  47.9 0.2 collective-permute-start.16
  48.1 1.1 %collective-permute-start.18 = (bf16[5,32,256]{2,1,0:T(8,128)(2,1)S(1)}, bf16[5,32,256]{2,1,0:T(8,128)(2,1)S(1)}, u32[]{:S(2)}, u32[]{:S(2)}) collective-permute-start(bf16[5,32,256]{2,1,0:T(8,128)(2,1)S(1)} %get-tuple-element.123), channel_id=1, source_target_pairs={{0,8},{1,9},{2,10},{3,11},{4,12},{5,13},{6,14},{7,15},{8,0},{9,1},... | collective-permute-start | bytes 245768 | tf_op jit(solution)/shard_map/ppermute | solution.py:579
  49.2 0.0 collective-permute-done.14.first_in
  49.2 1.8 %collective-permute-done.15.second_in = bf16[2,3,16,512]{3,2,1,0:T(8,128)(2,1)S(1)} collective-permute-done((bf16[2,3,16,512]{3,2,1,0:T(8,128)(2,1)S(1)}, bf16[2,3,16,512]{3,2,1,0:T(8,128)(2,1)S(1)}, u32[]{:S(2)}, u32[]{:S(2)}) %collective-permute-start.15) | collective-permute-done | bytes 98336 | tf_op jit(solution)/shard_map/ppermute | solution.py:43
  51.0 1.0 %shard_map.117.after_ref = bf16[2,128,512]{2,1,0:T(8,128)(2,1)} custom-call(s32[1]{0:T(128)} %bitcast.me_ref, bf16[5,32,256]{2,1,0:T(8,128)(2,1)S(1)} %get-tuple-element.113.after_ref, s32[1,8,16]{2,1,0:T(8,128)S(1)} %copy-done, f32[2,128,512]{2,1,0:T(8,128)S(1)} %get-tuple-element.107.refs_0_.node_ref, ...), custom_call_target="tpu_custom_call" | custom-call | flops 1000000 | bytes 10000 | tf_op jit(solution)/shard_map/pallas_call | solution.py:468
  52.0 1.2 %collective-permute-done.16.refs_0_ = bf16[5,32,256]{2,1,0:T(8,128)(2,1)S(1)} collective-permute-done((bf16[5,32,256]{2,1,0:T(8,128)(2,1)S(1)}, bf16[5,32,256]{2,1,0:T(8,128)(2,1)S(1)}, u32[]{:S(2)}, u32[]{:S(2)}) %collective-permute-start.16) | collective-permute-done | bytes 81952 | tf_op jit(solution)/shard_map/ppermute | solution.py:579
  53.2 0.8 %collective-permute-done.18.refs_2_ = bf16[5,32,256]{2,1,0:T(8,128)(2,1)S(1)} collective-permute-done((bf16[5,32,256]{2,1,0:T(8,128)(2,1)S(1)}, bf16[5,32,256]{2,1,0:T(8,128)(2,1)S(1)}, u32[]{:S(2)}, u32[]{:S(2)}) %collective-permute-start.18) | collective-permute-done | bytes 81952 | tf_op jit(solution)/shard_map/ppermute | solution.py:579
  54.0 0.8 %shard_map.118 = f32[32,2048]{1,0:T(8,128)} custom-call(bf16[2,128,512]{2,1,0:T(8,128)(2,1)} %shard_map.117.after_ref, f32[32,768]{1,0:T(8,128)S(1)} %get-tuple-element.120.own_a, f32[32,1280]{1,0:T(8,128)S(1)} %get-tuple-element.121.own_b, bf16[5,32,256]{2,1,0:T(8,128)(2,1)S(1)} %collective-permute-done.16.refs_0_, ...), custom_call_target="tpu_custom_call" | custom-call | flops 1000000 | bytes 10000 | tf_op jit(solution)/shard_map/pallas_call | solution.py:468
  (8 shorter events, 0.1 us)
Async XLA Ops:
  1.8 8.6 %collective-permute-start = (bf16[2,3,16,512]{3,2,1,0:T(8,128)(2,1)S(1)}, bf16[2,3,16,512]{3,2,1,0:T(8,128)(2,1)S(1)}, u32[]{:S(2)}, u32[]{:S(2)}) collective-permute-start(bf16[2,3,16,512]{3,2,1,0:T(8,128)(2,1)S(1)} %get-tuple-element.66), channel_id=1, source_target_pairs={{0,4},{1,5},{2,6},{3,7},{4,8},{5,9},{6,10},{7,11},{8,12},{9,13},{1... | collective-permute-start | bytes 294920 | tf_op jit(solution)/shard_map/ppermute | solution.py:28
  4.9 6.4 %collective-permute-start.1 = (bf16[2,3,16,512]{3,2,1,0:T(8,128)(2,1)S(1)}, bf16[2,3,16,512]{3,2,1,0:T(8,128)(2,1)S(1)}, u32[]{:S(2)}, u32[]{:S(2)}) collective-permute-start(bf16[2,3,16,512]{3,2,1,0:T(8,128)(2,1)S(1)} %get-tuple-element.67), channel_id=1, source_target_pairs={{0,12},{1,13},{2,14},{3,15},{4,0},{5,1},{6,2},{7,3},{8,4},{9,5},{1... | collective-permute-start | bytes 294920 | tf_op jit(solution)/shard_map/ppermute | solution.py:28
  11.3 5.0 %collective-permute-start.2 = (bf16[2,3,16,512]{3,2,1,0:T(8,128)(2,1)S(1)}, bf16[2,3,16,512]{3,2,1,0:T(8,128)(2,1)S(1)}, u32[]{:S(2)}, u32[]{:S(2)}) collective-permute-start(bf16[2,3,16,512]{3,2,1,0:T(8,128)(2,1)S(1)} %get-tuple-element.70.after_ref), channel_id=1, source_target_pairs={{0,1},{1,0},{2,3},{3,2},{4,5},{5,4},{6,7},{7,6},{8,9},{9,8},{10,11... | collective-permute-start | bytes 294920 | tf_op jit(solution)/shard_map/ppermute | solution.py:43
  11.4 6.8 %collective-permute-start.3 = (bf16[2,3,16,512]{3,2,1,0:T(8,128)(2,1)S(1)}, bf16[2,3,16,512]{3,2,1,0:T(8,128)(2,1)S(1)}, u32[]{:S(2)}, u32[]{:S(2)}) collective-permute-start(bf16[2,3,16,512]{3,2,1,0:T(8,128)(2,1)S(1)} %get-tuple-element.71), channel_id=1, source_target_pairs={{0,15},{1,2},{2,1},{3,4},{4,3},{5,6},{6,5},{7,8},{8,7},{9,10},{10,... | collective-permute-start | bytes 294920 | tf_op jit(solution)/shard_map/ppermute | solution.py:43
  22.0 2.4 %collective-permute-start.4 = (bf16[4,32,1024]{2,1,0:T(8,128)(2,1)S(1)}, bf16[4,32,1024]{2,1,0:T(8,128)(2,1)S(1)}, u32[]{:S(2)}, u32[]{:S(2)}) collective-permute-start(bf16[4,32,1024]{2,1,0:T(8,128)(2,1)S(1)} %get-tuple-element.85), channel_id=1, source_target_pairs={{0,1},{1,0},{2,3},{3,2},{4,5},{5,4},{6,7},{7,6},{8,9},{9,8},{10,11... | collective-permute-start | bytes 786440 | tf_op jit(solution)/shard_map/ppermute | solution.py:560
  23.7 3.1 %collective-permute-start.5 = (bf16[2,4,32,512]{3,2,1,0:T(8,128)(2,1)S(1)}, bf16[2,4,32,512]{3,2,1,0:T(8,128)(2,1)S(1)}, u32[]{:S(2)}, u32[]{:S(2)}) collective-permute-start(bf16[2,4,32,512]{3,2,1,0:T(8,128)(2,1)S(1)} %get-tuple-element.89), channel_id=1, source_target_pairs={{0,1},{1,0},{2,3},{3,2},{4,5},{5,4},{6,7},{7,6},{8,9},{9,8},{10,11... | collective-permute-start | bytes 786440 | tf_op jit(solution)/shard_map/ppermute | solution.py:560
  24.3 5.5 %collective-permute-start.7 = (bf16[4,32,1024]{2,1,0:T(8,128)(2,1)S(1)}, bf16[4,32,1024]{2,1,0:T(8,128)(2,1)S(1)}, u32[]{:S(2)}, u32[]{:S(2)}) collective-permute-start(bf16[4,32,1024]{2,1,0:T(8,128)(2,1)S(1)} %get-tuple-element.92), channel_id=1, source_target_pairs={{0,1},{1,0},{2,3},{3,2},{4,5},{5,4},{6,7},{7,6},{8,9},{9,8},{10,11... | collective-permute-start | bytes 786440 | tf_op jit(solution)/shard_map/ppermute | solution.py:560
  24.5 9.2 %collective-permute-start.8 = (bf16[4,32,1024]{2,1,0:T(8,128)(2,1)S(1)}, bf16[4,32,1024]{2,1,0:T(8,128)(2,1)S(1)}, u32[]{:S(2)}, u32[]{:S(2)}) collective-permute-start(bf16[4,32,1024]{2,1,0:T(8,128)(2,1)S(1)} %add_convert_fusion.refs_0_), channel_id=1, source_target_pairs={{0,2},{1,3},{2,0},{3,1},{4,6},{5,7},{6,4},{7,5},{8,10},{9,11},{10,... | collective-permute-start | bytes 786440 | tf_op jit(solution)/shard_map/ppermute | solution.py:567
  26.3 1.4 %collective-permute-start.6 = (bf16[4,32,512]{2,1,0:T(8,128)(2,1)S(1)}, bf16[4,32,512]{2,1,0:T(8,128)(2,1)S(1)}, u32[]{:S(2)}, u32[]{:S(2)}) collective-permute-start(bf16[4,32,512]{2,1,0:T(8,128)(2,1)S(1)} %get-tuple-element.90), channel_id=1, source_target_pairs={{0,1},{1,0},{2,3},{3,2},{4,5},{5,4},{6,7},{7,6},{8,9},{9,8},{10,11... | collective-permute-start | bytes 393224 | tf_op jit(solution)/shard_map/ppermute | solution.py:560
  26.7 10.3 %collective-permute-start.11 = (bf16[4,32,512]{2,1,0:T(8,128)(2,1)S(1)}, bf16[4,32,512]{2,1,0:T(8,128)(2,1)S(1)}, u32[]{:S(2)}, u32[]{:S(2)}) collective-permute-start(bf16[4,32,512]{2,1,0:T(8,128)(2,1)S(1)} %get-tuple-element.112), channel_id=1, source_target_pairs={{0,1},{1,0},{2,3},{3,2},{4,5},{5,4},{6,7},{7,6},{8,9},{9,8},{10,11... | collective-permute-start | bytes 393224 | tf_op jit(solution)/shard_map/ppermute | solution.py:560
  27.8 11.0 %collective-permute-start.10 = (bf16[4,32,1024]{2,1,0:T(8,128)(2,1)S(1)}, bf16[4,32,1024]{2,1,0:T(8,128)(2,1)S(1)}, u32[]{:S(2)}, u32[]{:S(2)}) collective-permute-start(bf16[4,32,1024]{2,1,0:T(8,128)(2,1)S(1)} %shard_map.112.after_ref), channel_id=1, source_target_pairs={{0,2},{1,3},{2,0},{3,1},{4,6},{5,7},{6,4},{7,5},{8,10},{9,11},{10,... | collective-permute-start | bytes 786440 | tf_op jit(solution)/shard_map/ppermute | solution.py:577
  33.7 5.1 %collective-permute-start.9 = (bf16[6,32,256]{2,1,0:T(8,128)(2,1)S(1)}, bf16[6,32,256]{2,1,0:T(8,128)(2,1)S(1)}, u32[]{:S(2)}, u32[]{:S(2)}) collective-permute-start(bf16[6,32,256]{2,1,0:T(8,128)(2,1)S(1)} %get-tuple-element.93.refs_0_), channel_id=1, source_target_pairs={{0,4},{1,5},{2,6},{3,7},{4,0},{5,1},{6,2},{7,3},{8,12},{9,13},{10,... | collective-permute-start | bytes 294920 | tf_op jit(solution)/shard_map/ppermute | solution.py:579
  34.8 7.5 %collective-permute-start.12 = (bf16[2,3,16,512]{3,2,1,0:T(8,128)(2,1)S(1)}, bf16[2,3,16,512]{3,2,1,0:T(8,128)(2,1)S(1)}, u32[]{:S(2)}, u32[]{:S(2)}) collective-permute-start(bf16[2,3,16,512]{3,2,1,0:T(8,128)(2,1)S(1)} %get-tuple-element.114), channel_id=1, source_target_pairs={{0,12},{1,13},{2,14},{3,15},{4,0},{5,1},{6,2},{7,3},{8,4},{9,5},{1... | collective-permute-start | bytes 294920 | tf_op jit(solution)/shard_map/ppermute | solution.py:28
  37.1 7.0 %collective-permute-start.13 = (bf16[2,3,16,512]{3,2,1,0:T(8,128)(2,1)S(1)}, bf16[2,3,16,512]{3,2,1,0:T(8,128)(2,1)S(1)}, u32[]{:S(2)}, u32[]{:S(2)}) collective-permute-start(bf16[2,3,16,512]{3,2,1,0:T(8,128)(2,1)S(1)} %get-tuple-element.115), channel_id=1, source_target_pairs={{0,4},{1,5},{2,6},{3,7},{4,8},{5,9},{6,10},{7,11},{8,12},{9,13},{1... | collective-permute-start | bytes 294920 | tf_op jit(solution)/shard_map/ppermute | solution.py:28
  38.9 15.1 %collective-permute-start.17 = (bf16[8,32,256]{2,1,0:T(8,128)(2,1)S(1)}, bf16[8,32,256]{2,1,0:T(8,128)(2,1)S(1)}, u32[]{:S(2)}, u32[]{:S(2)}) collective-permute-start(bf16[8,32,256]{2,1,0:T(8,128)(2,1)S(1)} %get-tuple-element.122), channel_id=1, source_target_pairs={{0,12},{1,13},{2,14},{3,15},{4,8},{5,9},{6,10},{7,11},{8,4},{9,5},... | collective-permute-start | bytes 393224 | tf_op jit(solution)/shard_map/ppermute | solution.py:579
  44.1 7.0 %copy-start = (s32[1,8,16]{2,1,0:T(8,128)S(1)}, s32[1,8,16]{2,1,0:T(8,128)}, u32[]{:S(2)}) copy-start(s32[1,8,16]{2,1,0:T(8,128)} %send_ref.1) | copy-start | bytes 1540
  44.1 5.1 %collective-permute-start.14 = (bf16[2,3,16,512]{3,2,1,0:T(8,128)(2,1)S(1)}, bf16[2,3,16,512]{3,2,1,0:T(8,128)(2,1)S(1)}, u32[]{:S(2)}, u32[]{:S(2)}) collective-permute-start(bf16[2,3,16,512]{3,2,1,0:T(8,128)(2,1)S(1)} %get-tuple-element.118), channel_id=1, source_target_pairs={{0,1},{1,0},{2,3},{3,2},{4,5},{5,4},{6,7},{7,6},{8,9},{9,8},{10,11... | collective-permute-start | bytes 294920 | tf_op jit(solution)/shard_map/ppermute | solution.py:43
  44.2 6.9 %collective-permute-start.15 = (bf16[2,3,16,512]{3,2,1,0:T(8,128)(2,1)S(1)}, bf16[2,3,16,512]{3,2,1,0:T(8,128)(2,1)S(1)}, u32[]{:S(2)}, u32[]{:S(2)}) collective-permute-start(bf16[2,3,16,512]{3,2,1,0:T(8,128)(2,1)S(1)} %get-tuple-element.119), channel_id=1, source_target_pairs={{0,15},{1,2},{2,1},{3,4},{4,3},{5,6},{6,5},{7,8},{8,7},{9,10},{10,... | collective-permute-start | bytes 294920 | tf_op jit(solution)/shard_map/ppermute | solution.py:43
  47.9 5.3 %collective-permute-start.16 = (bf16[5,32,256]{2,1,0:T(8,128)(2,1)S(1)}, bf16[5,32,256]{2,1,0:T(8,128)(2,1)S(1)}, u32[]{:S(2)}, u32[]{:S(2)}) collective-permute-start(bf16[5,32,256]{2,1,0:T(8,128)(2,1)S(1)} %get-tuple-element.113.after_ref), channel_id=1, source_target_pairs={{0,4},{1,5},{2,6},{3,7},{4,0},{5,1},{6,2},{7,3},{8,12},{9,13},{10,... | collective-permute-start | bytes 245768 | tf_op jit(solution)/shard_map/ppermute | solution.py:579
  48.1 5.9 %collective-permute-start.18 = (bf16[5,32,256]{2,1,0:T(8,128)(2,1)S(1)}, bf16[5,32,256]{2,1,0:T(8,128)(2,1)S(1)}, u32[]{:S(2)}, u32[]{:S(2)}) collective-permute-start(bf16[5,32,256]{2,1,0:T(8,128)(2,1)S(1)} %get-tuple-element.123), channel_id=1, source_target_pairs={{0,8},{1,9},{2,10},{3,11},{4,12},{5,13},{6,14},{7,15},{8,0},{9,1},... | collective-permute-start | bytes 245768 | tf_op jit(solution)/shard_map/ppermute | solution.py:579

commit v10 on v8

--- a/solution.py
+++ b/solution.py
@@ -39,10 +39,9 @@
 
 
 def swap(pair, stride):
-    return [
-        lax.ppermute(shard, "patch", perm)
-        for shard, perm in zip(pair, neighbours_apart(lax.axis_size("patch"), stride))
-    ]
+    first, second = neighbours_apart(lax.axis_size("patch"), stride)
+    later = lax.ppermute(pair[1], "patch", second)
+    return [lax.ppermute(pair[0], "patch", first), later]
 
 
 def to_swaps(both, odd, first_ref, second_ref):
@@ -169,7 +168,7 @@
 
 
 def halo_kernel(
-    me_ref, plus_ref, minus_ref, first_in, second_in, xt_ref, wk_ref, wv_ref, *refs
+    me_ref, second_in, first_in, plus_ref, minus_ref, xt_ref, wk_ref, wv_ref, *refs
 ):
     halo_refs, xtf_ref, both = refs[:-2], refs[-2], refs[-1]
     members, _, node_rows = xt_ref.shape
@@ -425,7 +424,7 @@
 
 
 def finish_kernel(
-    me_ref, after_ref, send_ref, node_ref, plus_ref, minus_ref, first_in, second_in, out_ref, came
+    me_ref, after_ref, second_in, first_in, send_ref, node_ref, plus_ref, minus_ref, out_ref, came
 ):
     members, node_rows, _ = node_ref.shape
     pick = sent_selector(send_ref[0], node_rows).astype(bf16)
@@ -517,12 +516,12 @@
     )
     arrived = swap(outgoing, 1)
     (mask,) = call(
-        mask_kernel, [((table, node_rows), f32)], (outgoing[0], neigh, counts), specs=[pl.ANY]
+        mask_kernel, [((table, node_rows), f32)], (outgoing[1], neigh, counts), specs=[pl.ANY]
     )
     *halo, xtf = call(
         halo_kernel,
         [((4, members, node_rows, 128), bf16)] * groups + [((members, width, table), bf16)],
-        (place, plus, minus, *arrived, xt, wk, wv), specs=[pltpu.SMEM], scratch=[trio],
+        (place, *arrived[::-1], plus, minus, xt, wk, wv), specs=[pltpu.SMEM], scratch=[trio],
     )
 
     planes, rows = count // 4, width // count
@@ -614,7 +613,7 @@
     received = [exchange(shard, k) for k, shard in enumerate(sent, 1)]
     (node_grad,) = call(
         finish_kernel, [((members, node_rows, width), bf16)],
-        (place, sent[0], send_rows, node, from_plus, from_minus, *back),
+        (place, sent[0], *back[::-1], send_rows, node, from_plus, from_minus),
         specs=[pltpu.SMEM, pl.ANY], scratch=[trio], final=True,
     )
     (weight_grad,) = call(

time: 53.4 us -> 53.3 us (level)
  starting transfers between devices: 21.9 us -> 19.7 us
  waiting for transfers between devices: 15 us -> 17.1 us
    ppermute x4, starting transfers between devices: 5.6 us -> 2.35 us  [the longest x2 2.32 us: swap(): later = lax.ppermute(pair[1], 'patch', second)]
    ppermute x4, waiting for transfers between devices: 5.51 us -> 7.5 us  [the longest x2 7.5 us: swap(): later = lax.ppermute(pair[1], 'patch', second)]
    ppermute x4, starting transfers between devices: 3.82 us -> 4.93 us  [exchange(): return lax.ppermute(sent, 'patch', along_z(count, distance))]
  transfers between devices with their start and end apart: 19 -> 19, of which waited for: 9 -> 8; matrix products, arithmetic and copies ran while one was open for 0% -> 0% of each run, Pallas kernels for 18% -> 18%
where the time goes in v10:
time: 53.3 us; the launch traced here: 53.1 us
  starting transfers between devices  19.7 us (37%)
  waiting for transfers between devices  17.1 us (32%)
  Pallas kernels  15.5 us (29%)
  between operations  0.78 us (1%)
    pallas_call x15, Pallas kernels, call(): pl.pallas_call(kernel, out_shape=[jax.ShapeDtypeStruct(*o) if final else...  15.5 us
    ppermute x4, starting transfers between devices, shifted(): lax.ppermute(shard, 'patch', [(i, (i + by) % count) for i in range(count)])  9.03 us
    ppermute x2, waiting for transfers between devices, swap(): later = lax.ppermute(pair[1], 'patch', second)  7.5 us
    ppermute x4, waiting for transfers between devices, shifted(): lax.ppermute(shard, 'patch', [(i, (i + by) % count) for i in range(count)])  5.1 us
    ppermute x4, starting transfers between devices, exchange(): return lax.ppermute(sent, 'patch', along_z(count, distance))  4.93 us
    ppermute x4, waiting for transfers between devices, exchange(): return lax.ppermute(sent, 'patch', along_z(count, distance))  3.56 us
    ppermute x2, starting transfers between devices, swap(): later = lax.ppermute(pair[1], 'patch', second)  2.32 us
    ppermute x1, starting transfers between devices, body(): y_b = lax.ppermute(y_sent, 'patch', flop)  2.01 us
  transfers between devices with their start and end apart: 19, of which 8 were waited for; matrix products, arithmetic and copies ran while one was open for 0% of the time, Pallas kernels for 18%

profile of v10, /device:TPU:0, one launch (start us, length us, event | category | flops | bytes accessed | tf_op | source)
XLA Modules:
  0.0 53.1 jit_solution(1677514827216516099)
XLA Ops:
  0.6 1.2 %shard_map.104 = (bf16[2,3,16,512]{3,2,1,0:T(8,128)(2,1)S(1)}, bf16[2,3,16,512]{3,2,1,0:T(8,128)(2,1)S(1)}, bf16[2,1,16,512]{3,2,1,0:T(8,128)(2,1)S(1)}, bf16[2,...) custom-call(s32[1,8,16]{2,1,0:T(8,128)} %send_ref.1, bf16[2,128,512]{2,1,0:T(8,128)(2,1)} %x_hbm.1), custom_call_target="tpu_custom_call" | custom-call | flops 1000000 | bytes 10000 | tf_op jit(solution)/shard_map/pallas_call | solution.py:467
  1.8 3.1 %collective-permute-start = (bf16[2,3,16,512]{3,2,1,0:T(8,128)(2,1)S(1)}, bf16[2,3,16,512]{3,2,1,0:T(8,128)(2,1)S(1)}, u32[]{:S(2)}, u32[]{:S(2)}) collective-permute-start(bf16[2,3,16,512]{3,2,1,0:T(8,128)(2,1)S(1)} %get-tuple-element.68), channel_id=1, source_target_pairs={{0,4},{1,5},{2,6},{3,7},{4,8},{5,9},{6,10},{7,11},{8,12},{9,13},{1... | collective-permute-start | bytes 294920 | tf_op jit(solution)/shard_map/ppermute | solution.py:28
  4.9 2.1 %collective-permute-start.1 = (bf16[2,3,16,512]{3,2,1,0:T(8,128)(2,1)S(1)}, bf16[2,3,16,512]{3,2,1,0:T(8,128)(2,1)S(1)}, u32[]{:S(2)}, u32[]{:S(2)}) collective-permute-start(bf16[2,3,16,512]{3,2,1,0:T(8,128)(2,1)S(1)} %get-tuple-element.69), channel_id=1, source_target_pairs={{0,12},{1,13},{2,14},{3,15},{4,0},{5,1},{6,2},{7,3},{8,4},{9,5},{1... | collective-permute-start | bytes 294920 | tf_op jit(solution)/shard_map/ppermute | solution.py:28
  7.0 2.6 %shard_map.105 = (bf16[8,2,128,128]{3,2,1,0:T(8,128)(2,1)S(1)}, bf16[8,2,128,128]{3,2,1,0:T(8,128)(2,1)S(1)}, bf16[8,2,128,128]{3,2,1,0:T(8,128)(2,1)S(1)}, bf16...) custom-call(bf16[2,1,16,512]{3,2,1,0:T(8,128)(2,1)S(1)} %get-tuple-e, ...), custom_call_target="tpu_custom_call" | custom-call | flops 1000000 | bytes 10000 | tf_op jit(solution)/shard_map/pallas_call | solution.py:467
  9.7 0.8 %collective-permute-done.plus_ref = bf16[2,3,16,512]{3,2,1,0:T(8,128)(2,1)S(1)} collective-permute-done((bf16[2,3,16,512]{3,2,1,0:T(8,128)(2,1)S(1)}, bf16[2,3,16,512]{3,2,1,0:T(8,128)(2,1)S(1)}, u32[]{:S(2)}, u32[]{:S(2)}) %collective-permute-start) | collective-permute-done | bytes 98336 | tf_op jit(solution)/shard_map/ppermute | solution.py:28
  10.4 0.8 %collective-permute-done.1.minus_ref = bf16[2,3,16,512]{3,2,1,0:T(8,128)(2,1)S(1)} collective-permute-done((bf16[2,3,16,512]{3,2,1,0:T(8,128)(2,1)S(1)}, bf16[2,3,16,512]{3,2,1,0:T(8,128)(2,1)S(1)}, u32[]{:S(2)}, u32[]{:S(2)}) %collective-permute-start.1) | collective-permute-done | bytes 98336 | tf_op jit(solution)/shard_map/ppermute | solution.py:28
  11.3 1.7 %collective-permute-start.2 = (bf16[2,3,16,512]{3,2,1,0:T(8,128)(2,1)S(1)}, bf16[2,3,16,512]{3,2,1,0:T(8,128)(2,1)S(1)}, u32[]{:S(2)}, u32[]{:S(2)}) collective-permute-start(bf16[2,3,16,512]{3,2,1,0:T(8,128)(2,1)S(1)} %get-tuple-element.70.after_ref), channel_id=1, source_target_pairs={{0,15},{1,2},{2,1},{3,4},{4,3},{5,6},{6,5},{7,8},{8,7},{9,10},{10,... | collective-permute-start | bytes 294920 | tf_op jit(solution)/shard_map/ppermute | solution.py:43
  13.0 0.0 collective-permute-start.3
  13.0 1.4 %shard_map.108.refs_2_.refs_4_.refs_3_ = f32[256,128]{1,0:T(8,128)S(1)} custom-call(bf16[2,3,16,512]{3,2,1,0:T(8,128)(2,1)S(1)} %get-tuple-element.70.after_ref, s32[128,256]{1,0:T(8,128)S(1)} %get-tuple-element.76.neigh_ref, s32[1,128]{1,0:T(1,128)S(1)} %get-tuple-element.77.count_ref), custom_call_target="tpu_custom_call" | custom-call | flops 1000000 | bytes 10000 | tf_op jit(solution)/shard_map/pallas_call | solution.py:467
  14.5 3.7 %collective-permute-done.2.second_in = bf16[2,3,16,512]{3,2,1,0:T(8,128)(2,1)S(1)} collective-permute-done((bf16[2,3,16,512]{3,2,1,0:T(8,128)(2,1)S(1)}, bf16[2,3,16,512]{3,2,1,0:T(8,128)(2,1)S(1)}, u32[]{:S(2)}, u32[]{:S(2)}) %collective-permute-start.2) | collective-permute-done | bytes 98336 | tf_op jit(solution)/shard_map/ppermute | solution.py:43
  18.1 0.0 collective-permute-done.3.first_in
  18.1 0.6 %shard_map.107 = (bf16[4,2,128,128]{3,2,1,0:T(8,128)(2,1)S(1)}, bf16[4,2,128,128]{3,2,1,0:T(8,128)(2,1)S(1)}, bf16[4,2,128,128]{3,2,1,0:T(8,128)(2,1)S(1)}, bf16...) custom-call(s32[1]{0:T(128)} %bitcast.me_ref, bf16[2,3,16,512]{3,2,1,0:T(8,128)(2,1)S(1)} %collective-permute-done.2.second_in, ...), custom_call_target="tpu_custom_call" | custom-call | flops 1000000 | bytes 10000 | tf_op jit(solution)/shard_map/pallas_call | solution.py:467
  18.7 3.1 %shard_map.110 = (f32[4,32,1024]{2,1,0:T(8,128)S(1)}, f32[4,32,1024]{2,1,0:T(8,128)S(1)}, bf16[4,32,1024]{2,1,0:T(8,128)(2,1)S(1)}, bf16[4,32,1024]{2,1,0:T(8,12...) custom-call(s32[1]{0:T(128)} %bitcast.me_ref, ...), custom_call_target="tpu_custom_call" | custom-call | flops 1000000 | bytes 10000 | tf_op jit(solution)/shard_map/pallas_call | solution.py:467
  21.9 0.1 collective-permute-start.4
  22.0 1.7 %shard_map.109 = (f32[4,32,512]{2,1,0:T(8,128)S(1)}, f32[4,32,512]{2,1,0:T(8,128)S(1)}, bf16[2,4,32,512]{3,2,1,0:T(8,128)(2,1)S(1)}, bf16[2,128,128]{2,1,0:T(8,1...) custom-call(s32[1]{0:T(128)} %bitcast.me_ref, ...), custom_call_target="tpu_custom_call" | custom-call | flops 1000000 | bytes 10000 | tf_op jit(solution)/shard_map/pallas_call | solution.py:467
  23.7 0.6 %collective-permute-start.5 = (bf16[2,4,32,512]{3,2,1,0:T(8,128)(2,1)S(1)}, bf16[2,4,32,512]{3,2,1,0:T(8,128)(2,1)S(1)}, u32[]{:S(2)}, u32[]{:S(2)}) collective-permute-start(bf16[2,4,32,512]{3,2,1,0:T(8,128)(2,1)S(1)} %get-tuple-element.89), channel_id=1, source_target_pairs={{0,1},{1,0},{2,3},{3,2},{4,5},{5,4},{6,7},{7,6},{8,9},{9,8},{10,11... | collective-permute-start | bytes 786440 | tf_op jit(solution)/shard_map/ppermute | solution.py:559
  24.2 0.1 collective-permute-start.7
  24.3 0.0 collective-permute-done.4
  24.3 0.1 add_convert_fusion.refs_0_
  24.4 0.1 collective-permute-start.8
  24.4 1.7 %shard_map.111 = (f32[4,32,512]{2,1,0:T(8,128)S(1)}, f32[4,32,512]{2,1,0:T(8,128)S(1)}, bf16[4,32,512]{2,1,0:T(8,128)(2,1)S(1)}, bf16[4,32,512]{2,1,0:T(8,128)(2...) custom-call(s32[1]{0:T(128)} %bitcast.me_ref, ...), custom_call_target="tpu_custom_call" | custom-call | flops 1000000 | bytes 10000 | tf_op jit(solution)/shard_map/pallas_call | solution.py:467
  26.2 0.5 collective-permute-start.6
  26.6 0.1 collective-permute-start.13
  26.7 0.0 collective-permute-done.5.refs_2_.refs_7_
  26.7 0.9 %collective-permute-done.6.refs_3_ = bf16[4,32,512]{2,1,0:T(8,128)(2,1)S(1)} collective-permute-done((bf16[4,32,512]{2,1,0:T(8,128)(2,1)S(1)}, bf16[4,32,512]{2,1,0:T(8,128)(2,1)S(1)}, u32[]{:S(2)}, u32[]{:S(2)}) %collective-permute-start.6) | collective-permute-done | bytes 131104 | tf_op jit(solution)/shard_map/ppermute | solution.py:559
  27.6 0.1 shard_map.112.after_ref.refs_0_
  27.7 2.0 %collective-permute-start.12 = (bf16[4,32,1024]{2,1,0:T(8,128)(2,1)S(1)}, bf16[4,32,1024]{2,1,0:T(8,128)(2,1)S(1)}, u32[]{:S(2)}, u32[]{:S(2)}) collective-permute-start(bf16[4,32,1024]{2,1,0:T(8,128)(2,1)S(1)} %shard_map.112.after_ref.refs_0_), channel_id=1, source_target_pairs={{0,2},{1,3},{2,0},{3,1},{4,6},{5,7},{6,4},{7,5},{8,10},{9,11},{10,... | collective-permute-start | bytes 786440 | tf_op jit(solution)/shard_map/ppermute | solution.py:576
  29.7 1.0 %shard_map.114 = (f32[2,128,512]{2,1,0:T(8,128)S(1)}, bf16[2,3,16,512]{3,2,1,0:T(8,128)(2,1)S(1)}, bf16[2,3,16,512]{3,2,1,0:T(8,128)(2,1)S(1)}, bf16[2,1,16,512]...) custom-call(bf16[4,32,1024]{2,1,0:T(8,128)(2,1)S(1)} %shard_map.112.after_ref.refs_0_, ...), custom_call_target="tpu_custom_call" | custom-call | flops 1000000 | bytes 10000 | tf_op jit(solution)/shard_map/pallas_call | solution.py:467
  30.7 0.1 collective-permute-start.10
  30.8 0.0 collective-permute-done.7.core_in
  30.8 3.8 %collective-permute-start.9 = (bf16[2,3,16,512]{3,2,1,0:T(8,128)(2,1)S(1)}, bf16[2,3,16,512]{3,2,1,0:T(8,128)(2,1)S(1)}, u32[]{:S(2)}, u32[]{:S(2)}) collective-permute-start(bf16[2,3,16,512]{3,2,1,0:T(8,128)(2,1)S(1)} %get-tuple-element.109), channel_id=1, source_target_pairs={{0,12},{1,13},{2,14},{3,15},{4,0},{5,1},{6,2},{7,3},{8,4},{9,5},{1... | collective-permute-start | bytes 294920 | tf_op jit(solution)/shard_map/ppermute | solution.py:28
  34.6 0.0 collective-permute-done.8.y_in
  34.6 0.1 shard_map.113
  34.7 0.1 collective-permute-start.11
  34.8 3.5 %collective-permute-done.10.minus_ref = bf16[2,3,16,512]{3,2,1,0:T(8,128)(2,1)S(1)} collective-permute-done((bf16[2,3,16,512]{3,2,1,0:T(8,128)(2,1)S(1)}, bf16[2,3,16,512]{3,2,1,0:T(8,128)(2,1)S(1)}, u32[]{:S(2)}, u32[]{:S(2)}) %collective-permute-start.10) | collective-permute-done | bytes 98336 | tf_op jit(solution)/shard_map/ppermute | solution.py:28
  38.3 0.0 collective-permute-done.13.refs_8_
  38.3 1.4 %collective-permute-done.11.refs_2_ = bf16[6,32,256]{2,1,0:T(8,128)(2,1)S(1)} collective-permute-done((bf16[6,32,256]{2,1,0:T(8,128)(2,1)S(1)}, bf16[6,32,256]{2,1,0:T(8,128)(2,1)S(1)}, u32[]{:S(2)}, u32[]{:S(2)}) %collective-permute-start.11) | collective-permute-done | bytes 98336 | tf_op jit(solution)/shard_map/ppermute | solution.py:586
  39.7 0.1 shard_map.116
  39.8 0.0 copy-start
  39.8 2.2 %collective-permute-start.17 = (bf16[8,32,256]{2,1,0:T(8,128)(2,1)S(1)}, bf16[8,32,256]{2,1,0:T(8,128)(2,1)S(1)}, u32[]{:S(2)}, u32[]{:S(2)}) collective-permute-start(bf16[8,32,256]{2,1,0:T(8,128)(2,1)S(1)} %get-tuple-element.122), channel_id=1, source_target_pairs={{0,12},{1,13},{2,14},{3,15},{4,8},{5,9},{6,10},{7,11},{8,4},{9,5},... | collective-permute-start | bytes 393224 | tf_op jit(solution)/shard_map/ppermute | solution.py:586
  42.1 0.7 %collective-permute-start.14 = (bf16[2,3,16,512]{3,2,1,0:T(8,128)(2,1)S(1)}, bf16[2,3,16,512]{3,2,1,0:T(8,128)(2,1)S(1)}, u32[]{:S(2)}, u32[]{:S(2)}) collective-permute-start(bf16[2,3,16,512]{3,2,1,0:T(8,128)(2,1)S(1)} %get-tuple-element.118), channel_id=1, source_target_pairs={{0,15},{1,2},{2,1},{3,4},{4,3},{5,6},{6,5},{7,8},{8,7},{9,10},{10,... | collective-permute-start | bytes 294920 | tf_op jit(solution)/shard_map/ppermute | solution.py:43
  42.7 0.5 collective-permute-start.16
  43.2 2.2 %collective-permute-start.18 = (bf16[5,32,256]{2,1,0:T(8,128)(2,1)S(1)}, bf16[5,32,256]{2,1,0:T(8,128)(2,1)S(1)}, u32[]{:S(2)}, u32[]{:S(2)}) collective-permute-start(bf16[5,32,256]{2,1,0:T(8,128)(2,1)S(1)} %get-tuple-element.123), channel_id=1, source_target_pairs={{0,8},{1,9},{2,10},{3,11},{4,12},{5,13},{6,14},{7,15},{8,0},{9,1},... | collective-permute-start | bytes 245768 | tf_op jit(solution)/shard_map/ppermute | solution.py:586
  45.4 3.8 %collective-permute-done.14.second_in = bf16[2,3,16,512]{3,2,1,0:T(8,128)(2,1)S(1)} collective-permute-done((bf16[2,3,16,512]{3,2,1,0:T(8,128)(2,1)S(1)}, bf16[2,3,16,512]{3,2,1,0:T(8,128)(2,1)S(1)}, u32[]{:S(2)}, u32[]{:S(2)}) %collective-permute-start.14) | collective-permute-done | bytes 98336 | tf_op jit(solution)/shard_map/ppermute | solution.py:43
  49.2 1.0 %shard_map.117.after_ref = bf16[2,128,512]{2,1,0:T(8,128)(2,1)} custom-call(s32[1]{0:T(128)} %bitcast.me_ref, bf16[5,32,256]{2,1,0:T(8,128)(2,1)S(1)} %get-tuple-element.117.after_ref, bf16[2,3,16,512]{3,2,1,0:T(8,128)(2,1)S(1)} %collective-permute-done.14.second_in, bf16[2,3,16,512]{3,2,1,0:T(8,128)(2,1)S(1)} %collective-permute-done.15.first_in, ...), custom_call_target="tpu_custom_call" | custom-call | flops 1000000 | bytes 10000 | tf_op jit(solution)/shard_map/pallas_call | solution.py:467
  50.2 0.0 collective-permute-done.16.refs_0_
  50.2 2.2 %collective-permute-done.18.refs_2_ = bf16[5,32,256]{2,1,0:T(8,128)(2,1)S(1)} collective-permute-done((bf16[5,32,256]{2,1,0:T(8,128)(2,1)S(1)}, bf16[5,32,256]{2,1,0:T(8,128)(2,1)S(1)}, u32[]{:S(2)}, u32[]{:S(2)}) %collective-permute-start.18) | collective-permute-done | bytes 81952 | tf_op jit(solution)/shard_map/ppermute | solution.py:586
  52.4 0.8 %shard_map.118 = f32[32,2048]{1,0:T(8,128)} custom-call(bf16[2,128,512]{2,1,0:T(8,128)(2,1)} %shard_map.117.after_ref, f32[32,768]{1,0:T(8,128)S(1)} %get-tuple-element.120.own_a, f32[32,1280]{1,0:T(8,128)S(1)} %get-tuple-element.121.own_b, bf16[5,32,256]{2,1,0:T(8,128)(2,1)S(1)} %collective-permute-done.16.refs_0_, ...), custom_call_target="tpu_custom_call" | custom-call | flops 1000000 | bytes 10000 | tf_op jit(solution)/shard_map/pallas_call | solution.py:467
  (8 shorter events, 0.1 us)
Async XLA Ops:
  1.8 8.6 %collective-permute-start = (bf16[2,3,16,512]{3,2,1,0:T(8,128)(2,1)S(1)}, bf16[2,3,16,512]{3,2,1,0:T(8,128)(2,1)S(1)}, u32[]{:S(2)}, u32[]{:S(2)}) collective-permute-start(bf16[2,3,16,512]{3,2,1,0:T(8,128)(2,1)S(1)} %get-tuple-element.68), channel_id=1, source_target_pairs={{0,4},{1,5},{2,6},{3,7},{4,8},{5,9},{6,10},{7,11},{8,12},{9,13},{1... | collective-permute-start | bytes 294920 | tf_op jit(solution)/shard_map/ppermute | solution.py:28
  4.9 6.4 %collective-permute-start.1 = (bf16[2,3,16,512]{3,2,1,0:T(8,128)(2,1)S(1)}, bf16[2,3,16,512]{3,2,1,0:T(8,128)(2,1)S(1)}, u32[]{:S(2)}, u32[]{:S(2)}) collective-permute-start(bf16[2,3,16,512]{3,2,1,0:T(8,128)(2,1)S(1)} %get-tuple-element.69), channel_id=1, source_target_pairs={{0,12},{1,13},{2,14},{3,15},{4,0},{5,1},{6,2},{7,3},{8,4},{9,5},{1... | collective-permute-start | bytes 294920 | tf_op jit(solution)/shard_map/ppermute | solution.py:28
  11.3 6.8 %collective-permute-start.2 = (bf16[2,3,16,512]{3,2,1,0:T(8,128)(2,1)S(1)}, bf16[2,3,16,512]{3,2,1,0:T(8,128)(2,1)S(1)}, u32[]{:S(2)}, u32[]{:S(2)}) collective-permute-start(bf16[2,3,16,512]{3,2,1,0:T(8,128)(2,1)S(1)} %get-tuple-element.70.after_ref), channel_id=1, source_target_pairs={{0,15},{1,2},{2,1},{3,4},{4,3},{5,6},{6,5},{7,8},{8,7},{9,10},{10,... | collective-permute-start | bytes 294920 | tf_op jit(solution)/shard_map/ppermute | solution.py:43
  13.0 5.1 %collective-permute-start.3 = (bf16[2,3,16,512]{3,2,1,0:T(8,128)(2,1)S(1)}, bf16[2,3,16,512]{3,2,1,0:T(8,128)(2,1)S(1)}, u32[]{:S(2)}, u32[]{:S(2)}) collective-permute-start(bf16[2,3,16,512]{3,2,1,0:T(8,128)(2,1)S(1)} %get-tuple-element.71), channel_id=1, source_target_pairs={{0,1},{1,0},{2,3},{3,2},{4,5},{5,4},{6,7},{7,6},{8,9},{9,8},{10,11... | collective-permute-start | bytes 294920 | tf_op jit(solution)/shard_map/ppermute | solution.py:44
  21.9 2.4 %collective-permute-start.4 = (bf16[4,32,1024]{2,1,0:T(8,128)(2,1)S(1)}, bf16[4,32,1024]{2,1,0:T(8,128)(2,1)S(1)}, u32[]{:S(2)}, u32[]{:S(2)}) collective-permute-start(bf16[4,32,1024]{2,1,0:T(8,128)(2,1)S(1)} %get-tuple-element.85), channel_id=1, source_target_pairs={{0,1},{1,0},{2,3},{3,2},{4,5},{5,4},{6,7},{7,6},{8,9},{9,8},{10,11... | collective-permute-start | bytes 786440 | tf_op jit(solution)/shard_map/ppermute | solution.py:559
  23.7 3.1 %collective-permute-start.5 = (bf16[2,4,32,512]{3,2,1,0:T(8,128)(2,1)S(1)}, bf16[2,4,32,512]{3,2,1,0:T(8,128)(2,1)S(1)}, u32[]{:S(2)}, u32[]{:S(2)}) collective-permute-start(bf16[2,4,32,512]{3,2,1,0:T(8,128)(2,1)S(1)} %get-tuple-element.89), channel_id=1, source_target_pairs={{0,1},{1,0},{2,3},{3,2},{4,5},{5,4},{6,7},{7,6},{8,9},{9,8},{10,11... | collective-permute-start | bytes 786440 | tf_op jit(solution)/shard_map/ppermute | solution.py:559
  24.2 6.6 %collective-permute-start.7 = (bf16[4,32,1024]{2,1,0:T(8,128)(2,1)S(1)}, bf16[4,32,1024]{2,1,0:T(8,128)(2,1)S(1)}, u32[]{:S(2)}, u32[]{:S(2)}) collective-permute-start(bf16[4,32,1024]{2,1,0:T(8,128)(2,1)S(1)} %get-tuple-element.92), channel_id=1, source_target_pairs={{0,1},{1,0},{2,3},{3,2},{4,5},{5,4},{6,7},{7,6},{8,9},{9,8},{10,11... | collective-permute-start | bytes 786440 | tf_op jit(solution)/shard_map/ppermute | solution.py:559
  24.4 10.2 %collective-permute-start.8 = (bf16[4,32,1024]{2,1,0:T(8,128)(2,1)S(1)}, bf16[4,32,1024]{2,1,0:T(8,128)(2,1)S(1)}, u32[]{:S(2)}, u32[]{:S(2)}) collective-permute-start(bf16[4,32,1024]{2,1,0:T(8,128)(2,1)S(1)} %add_convert_fusion.refs_0_), channel_id=1, source_target_pairs={{0,2},{1,3},{2,0},{3,1},{4,6},{5,7},{6,4},{7,5},{8,10},{9,11},{10,... | collective-permute-start | bytes 786440 | tf_op jit(solution)/shard_map/ppermute | solution.py:566
  26.2 1.5 %collective-permute-start.6 = (bf16[4,32,512]{2,1,0:T(8,128)(2,1)S(1)}, bf16[4,32,512]{2,1,0:T(8,128)(2,1)S(1)}, u32[]{:S(2)}, u32[]{:S(2)}) collective-permute-start(bf16[4,32,512]{2,1,0:T(8,128)(2,1)S(1)} %get-tuple-element.90), channel_id=1, source_target_pairs={{0,1},{1,0},{2,3},{3,2},{4,5},{5,4},{6,7},{7,6},{8,9},{9,8},{10,11... | collective-permute-start | bytes 393224 | tf_op jit(solution)/shard_map/ppermute | solution.py:559
  26.6 11.7 %collective-permute-start.13 = (bf16[4,32,512]{2,1,0:T(8,128)(2,1)S(1)}, bf16[4,32,512]{2,1,0:T(8,128)(2,1)S(1)}, u32[]{:S(2)}, u32[]{:S(2)}) collective-permute-start(bf16[4,32,512]{2,1,0:T(8,128)(2,1)S(1)} %get-tuple-element.116), channel_id=1, source_target_pairs={{0,1},{1,0},{2,3},{3,2},{4,5},{5,4},{6,7},{7,6},{8,9},{9,8},{10,11... | collective-permute-start | bytes 393224 | tf_op jit(solution)/shard_map/ppermute | solution.py:559
  27.7 12.0 %collective-permute-start.12 = (bf16[4,32,1024]{2,1,0:T(8,128)(2,1)S(1)}, bf16[4,32,1024]{2,1,0:T(8,128)(2,1)S(1)}, u32[]{:S(2)}, u32[]{:S(2)}) collective-permute-start(bf16[4,32,1024]{2,1,0:T(8,128)(2,1)S(1)} %shard_map.112.after_ref.refs_0_), channel_id=1, source_target_pairs={{0,2},{1,3},{2,0},{3,1},{4,6},{5,7},{6,4},{7,5},{8,10},{9,11},{10,... | collective-permute-start | bytes 786440 | tf_op jit(solution)/shard_map/ppermute | solution.py:576
  30.7 7.5 %collective-permute-start.10 = (bf16[2,3,16,512]{3,2,1,0:T(8,128)(2,1)S(1)}, bf16[2,3,16,512]{3,2,1,0:T(8,128)(2,1)S(1)}, u32[]{:S(2)}, u32[]{:S(2)}) collective-permute-start(bf16[2,3,16,512]{3,2,1,0:T(8,128)(2,1)S(1)} %get-tuple-element.110), channel_id=1, source_target_pairs={{0,4},{1,5},{2,6},{3,7},{4,8},{5,9},{6,10},{7,11},{8,12},{9,13},{1... | collective-permute-start | bytes 294920 | tf_op jit(solution)/shard_map/ppermute | solution.py:28
  30.8 7.5 %collective-permute-start.9 = (bf16[2,3,16,512]{3,2,1,0:T(8,128)(2,1)S(1)}, bf16[2,3,16,512]{3,2,1,0:T(8,128)(2,1)S(1)}, u32[]{:S(2)}, u32[]{:S(2)}) collective-permute-start(bf16[2,3,16,512]{3,2,1,0:T(8,128)(2,1)S(1)} %get-tuple-element.109), channel_id=1, source_target_pairs={{0,12},{1,13},{2,14},{3,15},{4,0},{5,1},{6,2},{7,3},{8,4},{9,5},{1... | collective-permute-start | bytes 294920 | tf_op jit(solution)/shard_map/ppermute | solution.py:28
  34.7 5.0 %collective-permute-start.11 = (bf16[6,32,256]{2,1,0:T(8,128)(2,1)S(1)}, bf16[6,32,256]{2,1,0:T(8,128)(2,1)S(1)}, u32[]{:S(2)}, u32[]{:S(2)}) collective-permute-start(bf16[6,32,256]{2,1,0:T(8,128)(2,1)S(1)} %get-tuple-element.93.after_ref), channel_id=1, source_target_pairs={{0,4},{1,5},{2,6},{3,7},{4,0},{5,1},{6,2},{7,3},{8,12},{9,13},{10,... | collective-permute-start | bytes 294920 | tf_op jit(solution)/shard_map/ppermute | solution.py:586
  39.8 9.4 %copy-start = (s32[1,8,16]{2,1,0:T(8,128)S(1)}, s32[1,8,16]{2,1,0:T(8,128)}, u32[]{:S(2)}) copy-start(s32[1,8,16]{2,1,0:T(8,128)} %send_ref.1) | copy-start | bytes 1540
  39.8 12.5 %collective-permute-start.17 = (bf16[8,32,256]{2,1,0:T(8,128)(2,1)S(1)}, bf16[8,32,256]{2,1,0:T(8,128)(2,1)S(1)}, u32[]{:S(2)}, u32[]{:S(2)}) collective-permute-start(bf16[8,32,256]{2,1,0:T(8,128)(2,1)S(1)} %get-tuple-element.122), channel_id=1, source_target_pairs={{0,12},{1,13},{2,14},{3,15},{4,8},{5,9},{6,10},{7,11},{8,4},{9,5},... | collective-permute-start | bytes 393224 | tf_op jit(solution)/shard_map/ppermute | solution.py:586
  42.1 7.1 %collective-permute-start.14 = (bf16[2,3,16,512]{3,2,1,0:T(8,128)(2,1)S(1)}, bf16[2,3,16,512]{3,2,1,0:T(8,128)(2,1)S(1)}, u32[]{:S(2)}, u32[]{:S(2)}) collective-permute-start(bf16[2,3,16,512]{3,2,1,0:T(8,128)(2,1)S(1)} %get-tuple-element.118), channel_id=1, source_target_pairs={{0,15},{1,2},{2,1},{3,4},{4,3},{5,6},{6,5},{7,8},{8,7},{9,10},{10,... | collective-permute-start | bytes 294920 | tf_op jit(solution)/shard_map/ppermute | solution.py:43
  42.7 6.5 %collective-permute-start.15 = (bf16[2,3,16,512]{3,2,1,0:T(8,128)(2,1)S(1)}, bf16[2,3,16,512]{3,2,1,0:T(8,128)(2,1)S(1)}, u32[]{:S(2)}, u32[]{:S(2)}) collective-permute-start(bf16[2,3,16,512]{3,2,1,0:T(8,128)(2,1)S(1)} %get-tuple-element.111.refs_0_), channel_id=1, source_target_pairs={{0,1},{1,0},{2,3},{3,2},{4,5},{5,4},{6,7},{7,6},{8,9},{9,8},{10,11... | collective-permute-start | bytes 294920 | tf_op jit(solution)/shard_map/ppermute | solution.py:44
  42.7 7.5 %collective-permute-start.16 = (bf16[5,32,256]{2,1,0:T(8,128)(2,1)S(1)}, bf16[5,32,256]{2,1,0:T(8,128)(2,1)S(1)}, u32[]{:S(2)}, u32[]{:S(2)}) collective-permute-start(bf16[5,32,256]{2,1,0:T(8,128)(2,1)S(1)} %get-tuple-element.117.after_ref), channel_id=1, source_target_pairs={{0,4},{1,5},{2,6},{3,7},{4,0},{5,1},{6,2},{7,3},{8,12},{9,13},{10,... | collective-permute-start | bytes 245768 | tf_op jit(solution)/shard_map/ppermute | solution.py:586
  43.2 9.2 %collective-permute-start.18 = (bf16[5,32,256]{2,1,0:T(8,128)(2,1)S(1)}, bf16[5,32,256]{2,1,0:T(8,128)(2,1)S(1)}, u32[]{:S(2)}, u32[]{:S(2)}) collective-permute-start(bf16[5,32,256]{2,1,0:T(8,128)(2,1)S(1)} %get-tuple-element.123), channel_id=1, source_target_pairs={{0,8},{1,9},{2,10},{3,11},{4,12},{5,13},{6,14},{7,15},{8,0},{9,1},... | collective-permute-start | bytes 245768 | tf_op jit(solution)/shard_map/ppermute | solution.py:586

commit v11 on v10

--- a/solution.py
+++ b/solution.py
@@ -366,14 +366,14 @@
         if i % 2 == 0:
             kept_ref[i // 2] = row
             continue
-        pieces = row.shape[1] // 256
+        pieces = row.shape[1] // 128
         for n in range(pieces):
-            sent_ref[i // 2 * pieces + n] = row[:, n * 256 : (n + 1) * 256].astype(bf16)
+            sent_ref[i // 2 * pieces + n] = row[:, n * 128 : (n + 1) * 128].astype(bf16)
 
 
 def add_received(kept_ref, received_ref):
     planes, _, wide = kept_ref.shape
-    pieces = wide // 256
+    pieces = wide // 128
     return [
         kept_ref[i]
         + jnp.concatenate([received_ref[i * pieces + n] for n in range(pieces)], axis=1).astype(f32)
@@ -392,15 +392,15 @@
 
 
 def put(row, ref, at):
-    for n in range(row.shape[1] // 256):
-        ref[at + n] = row[:, n * 256 : (n + 1) * 256].astype(bf16)
+    for n in range(row.shape[1] // 128):
+        ref[at + n] = row[:, n * 128 : (n + 1) * 128].astype(bf16)
 
 
 def second_kernel(skip, pieces, me_ref, *refs):
     refs = refs[skip:]
-    kept_a, in_a, first_ref, y_in = refs[:4]
-    owns, core_in = refs[4 : 4 + pieces], refs[4 + pieces : 4 + 2 * pieces]
-    own_a, own_b, *sent = refs[4 + 2 * pieces : -1]
+    first_ref, y_in = refs[:2]
+    owns, core_in = refs[2 : 2 + pieces], refs[2 + pieces : 2 + 2 * pieces]
+    own_b, *sent = refs[2 + 2 * pieces : -1]
     projection_ref = refs[-1]
     done = first_ref.shape[0]
     planes = projection_ref.shape[0]
@@ -410,17 +410,23 @@
         parts = sums(owns, core_in, y_in, k)
         gather_projection(parts, k, planes, projection_ref, done)
         held.append(jnp.concatenate([part[:, :384] for part in parts], axis=1))
-    first = add_received(kept_a, in_a)
-    own_a[...] = first[0]
     z = me_ref[0] // 4
     for k in range(planes):
         row = jnp.concatenate([held[k], projection_ref[plane_of(gray(z) ^ k)]], axis=1)
-        if k == 0:
+        if k:
+            put(row, sent[k - 1], 0)
+        else:
             own_b[...] = row
-            continue
-        put(row, sent[k - 1], 0)
-        if k % 2 == 0:
-            put(first[k // 2], sent[k - 1], row.shape[1] // 256)
+
+
+def join_kernel(kept_a, in_a, *refs):
+    count = (len(refs) - 1) // 2
+    blocks, own_a, sent = refs[:count], refs[count], refs[count + 1 :]
+    first = add_received(kept_a, in_a)
+    own_a[...] = first[0]
+    for i, ref in enumerate(sent):
+        ref[: blocks[i].shape[0]] = blocks[i][...]
+        put(first[i + 1], ref, blocks[i].shape[0])
 
 
 def finish_kernel(
@@ -442,19 +448,20 @@
 def weight_kernel(after_ref, own_a, own_b, *refs):
     received, out_ref = refs[:-1], refs[-1]
     a, b = own_a[...], own_b[...]
-    blocks, more = b.shape[1] // 256, a.shape[1] // 256
+    blocks, more = b.shape[1] // 128, a.shape[1] // 128
     for k, ref in enumerate(received, 1):
         b = b + jnp.concatenate([ref[n] for n in range(blocks)], axis=1).astype(f32)
         if k % 2 == 0:
             a = a + jnp.concatenate([ref[blocks + n] for n in range(more)], axis=1).astype(f32)
-    half = a.shape[1] // 384
-    width = 256 * half
-    for i, part in enumerate((a, b)):
-        for j in range(half):
+    width = out_ref.shape[1] // 4
+    group = 0
+    for part, wide in ((a, a.shape[1]), (b, b.shape[1] - width)):
+        for j in range(0, wide, 384):
             for n in range(3):
-                at = n * width + (i * half + j) * 128
-                out_ref[:, at : at + 128] = part[:, j * 384 + n * 128 : j * 384 + (n + 1) * 128]
-    out_ref[:, 3 * width :] = b[:, 384 * half :]
+                at = n * width + group * 128
+                out_ref[:, at : at + 128] = part[:, j + n * 128 : j + (n + 1) * 128]
+            group += 1
+    out_ref[:, 3 * width :] = b[:, b.shape[1] - width :]
 
 
 def call(kernel, outs, operands, specs=None, scratch=(), limit=12, final=False, flops=10**6):
@@ -552,25 +559,22 @@
                 pltpu.VMEM((planes, 2, 2, rows, 384), f32),
                 pltpu.VMEM((inner_planes, 2, 2, rows, width), f32),
             ],
-            limit=24,
+            limit=32,
         )
         sent = outs[2 : 2 + len(sends)]
         grads.extend(outs[2 + len(sends) :])
         arrived = [lax.ppermute(shard, "patch", flip) for shard in sent]
         return outs[0], outs[1], arrived[0], arrived[-1]
 
-    half = groups // 2
+    half = groups - 1
     wide = 384 * half
     own_a, other, core_other, core_own = attention((), range(half), False)
     y_sent = (other + core_other.astype(f32)).astype(bf16)
     y_a = lax.ppermute(y_sent, "patch", flop)
-    later = []
-    for g in range(half, groups):
-        last = g == groups - 1
-        later.append(attention((y_sent,) if last else (), range(g, g + 1), not last))
+    later = [attention((), range(half, groups), False)]
     own_b, other_b, core_other_b, core_own_b = zip(*later)
     (y_sent,) = call(
-        functools.partial(pack_kernel, len(later)), [(y_sent.shape, bf16)],
+        functools.partial(pack_kernel, len(later)), [(other_b[0].shape, bf16)],
         (*other_b, *core_other_b),
     )
     y_b = lax.ppermute(y_sent, "patch", flop)
@@ -590,9 +594,9 @@
         [
             ((planes // 2, rows, wide), f32),
             ((half * inner_planes, rows, width), f32),
-            ((planes // 2 * wide // 256, rows, 256), bf16),
+            ((planes // 2 * wide // 128, rows, 128), bf16),
         ],
-        (y_sent, own_a, core_own, y_a), specs=[pl.ANY], flops=2 * 10**10,
+        (node, own_a, core_own, y_a), specs=[pl.ANY], flops=2 * 10**10,
     )
     in_a = exchange(sent_a, 1)
     outgoing = call(
@@ -601,14 +605,19 @@
         specs=[pltpu.SMEM, pl.ANY], scratch=[trio],
     )
     back = swap(outgoing, 1)
-    more, blocks = wide // 256, (wide + width) // 256
-    own_a, own_b, *sent = call(
+    last = 384 * (groups - half) + width
+    more, blocks = wide // 128, last // 128
+    own_b, *sent = call(
         functools.partial(second_kernel, 1, len(later)),
-        [((rows, wide), f32), ((rows, wide + width), f32)]
-        + [((blocks + (0 if k % 2 else more), rows, 256), bf16) for k in range(1, planes)],
-        (place, outgoing[0], kept_a, in_a, out_a, y_b, *own_b, *core_own_b),
+        [((rows, last), f32)] + [((blocks, rows, 128), bf16)] * (planes - 1),
+        (place, outgoing[0], out_a, y_b, *own_b, *core_own_b),
         specs=[pltpu.SMEM, pl.ANY],
-        scratch=[pltpu.VMEM((planes, rows, width), f32)],
+        scratch=[pltpu.VMEM((planes, rows, width), f32)], flops=4 * 10**9,
+    )
+    own_a, *sent[1::2] = call(
+        join_kernel,
+        [((rows, wide), f32)] + [((blocks + more, rows, 128), bf16)] * (planes // 2 - 1),
+        (kept_a, in_a, *sent[1::2]),
     )
     received = [exchange(shard, k) for k, shard in enumerate(sent, 1)]
     (node_grad,) = call(

time: 53.3 us -> 53 us (level)
  starting transfers between devices: 19.7 us -> 17.6 us
  waiting for transfers between devices: 17.1 us -> 19.1 us
    ppermute x1, waiting for transfers between devices: 0.01 us -> 3.62 us  [body(): y_a = lax.ppermute(y_sent, 'patch', flop)]
    ppermute x4, starting transfers between devices: 9.03 us -> 7.25 us  [shifted(): lax.ppermute(shard, 'patch', [(i, (i + by) % count) for i in range(count)])]
    ppermute x4, starting transfers between devices: 4.93 us -> 3.48 us  [exchange(): return lax.ppermute(sent, 'patch', along_z(count, distance))]
    ppermute x2, starting transfers between devices: 2.32 us -> 3.6 us  [swap(): later = lax.ppermute(pair[1], 'patch', second)]
    ppermute x4, waiting for transfers between devices: 5.1 us -> 3.92 us  [shifted(): lax.ppermute(shard, 'patch', [(i, (i + by) % count) for i in range(count)])]
    ppermute x5 -> x4, waiting for transfers between devices: 0.91 us -> 2.05 us  [attention(): arrived = [lax.ppermute(shard, 'patch', flip) for shard in sent]]
    ppermute x2, waiting for transfers between devices: 7.5 us -> 6.52 us  [swap(): later = lax.ppermute(pair[1], 'patch', second)]
    ppermute x5 -> x4, starting transfers between devices: 1.27 us -> 1.14 us  [attention(): arrived = [lax.ppermute(shard, 'patch', flip) for shard in sent]]
  transfers between devices with their start and end apart: 19 -> 18, of which waited for: 8 -> 10; matrix products, arithmetic and copies ran while one was open for 0% -> 0% of each run, Pallas kernels for 18% -> 15%
where the time goes in v11:
time: 53 us; the launch traced here: 52.8 us
  waiting for transfers between devices  19.1 us (36%)
  starting transfers between devices  17.6 us (33%)
  Pallas kernels  15.2 us (29%)
  between operations  0.77 us (1%)
    pallas_call x15, Pallas kernels, call(): pl.pallas_call(kernel, out_shape=[jax.ShapeDtypeStruct(*o) if final else...  15.2 us
    ppermute x4, starting transfers between devices, shifted(): lax.ppermute(shard, 'patch', [(i, (i + by) % count) for i in range(count)])  7.25 us
    ppermute x2, waiting for transfers between devices, swap(): later = lax.ppermute(pair[1], 'patch', second)  6.52 us
    ppermute x4, waiting for transfers between devices, shifted(): lax.ppermute(shard, 'patch', [(i, (i + by) % count) for i in range(count)])  3.92 us
    ppermute x1, waiting for transfers between devices, body(): y_a = lax.ppermute(y_sent, 'patch', flop)  3.62 us
    ppermute x2, starting transfers between devices, swap(): later = lax.ppermute(pair[1], 'patch', second)  3.6 us
    ppermute x4, starting transfers between devices, exchange(): return lax.ppermute(sent, 'patch', along_z(count, distance))  3.48 us
    ppermute x4, waiting for transfers between devices, exchange(): return lax.ppermute(sent, 'patch', along_z(count, distance))  3.03 us
  transfers between devices with their start and end apart: 18, of which 10 were waited for; matrix products, arithmetic and copies ran while one was open for 0% of the time, Pallas kernels for 15%

profile of v11, /device:TPU:0, one launch (start us, length us, event | category | flops | bytes accessed | tf_op | source)
XLA Modules:
  0.0 52.8 jit_solution(15038757958576311238)
XLA Ops:
  0.6 1.2 %shard_map.104 = (bf16[2,3,16,512]{3,2,1,0:T(8,128)(2,1)S(1)}, bf16[2,3,16,512]{3,2,1,0:T(8,128)(2,1)S(1)}, bf16[2,1,16,512]{3,2,1,0:T(8,128)(2,1)S(1)}, bf16[2,...) custom-call(s32[1,8,16]{2,1,0:T(8,128)} %send_ref.1, bf16[2,128,512]{2,1,0:T(8,128)(2,1)} %x_hbm.1), custom_call_target="tpu_custom_call" | custom-call | flops 1000000 | bytes 10000 | tf_op jit(solution)/shard_map/pallas_call | solution.py:474
  1.8 3.1 %collective-permute-start = (bf16[2,3,16,512]{3,2,1,0:T(8,128)(2,1)S(1)}, bf16[2,3,16,512]{3,2,1,0:T(8,128)(2,1)S(1)}, u32[]{:S(2)}, u32[]{:S(2)}) collective-permute-start(bf16[2,3,16,512]{3,2,1,0:T(8,128)(2,1)S(1)} %get-tuple-element.66), channel_id=1, source_target_pairs={{0,4},{1,5},{2,6},{3,7},{4,8},{5,9},{6,10},{7,11},{8,12},{9,13},{1... | collective-permute-start | bytes 294920 | tf_op jit(solution)/shard_map/ppermute | solution.py:28
  4.9 2.1 %collective-permute-start.1 = (bf16[2,3,16,512]{3,2,1,0:T(8,128)(2,1)S(1)}, bf16[2,3,16,512]{3,2,1,0:T(8,128)(2,1)S(1)}, u32[]{:S(2)}, u32[]{:S(2)}) collective-permute-start(bf16[2,3,16,512]{3,2,1,0:T(8,128)(2,1)S(1)} %get-tuple-element.67), channel_id=1, source_target_pairs={{0,12},{1,13},{2,14},{3,15},{4,0},{5,1},{6,2},{7,3},{8,4},{9,5},{1... | collective-permute-start | bytes 294920 | tf_op jit(solution)/shard_map/ppermute | solution.py:28
  7.0 2.6 %shard_map.105 = (bf16[8,2,128,128]{3,2,1,0:T(8,128)(2,1)S(1)}, bf16[8,2,128,128]{3,2,1,0:T(8,128)(2,1)S(1)}, bf16[8,2,128,128]{3,2,1,0:T(8,128)(2,1)S(1)}, bf16...) custom-call(bf16[2,1,16,512]{3,2,1,0:T(8,128)(2,1)S(1)} %get-tuple-e, ...), custom_call_target="tpu_custom_call" | custom-call | flops 1000000 | bytes 10000 | tf_op jit(solution)/shard_map/pallas_call | solution.py:474
  9.7 0.8 %collective-permute-done.plus_ref = bf16[2,3,16,512]{3,2,1,0:T(8,128)(2,1)S(1)} collective-permute-done((bf16[2,3,16,512]{3,2,1,0:T(8,128)(2,1)S(1)}, bf16[2,3,16,512]{3,2,1,0:T(8,128)(2,1)S(1)}, u32[]{:S(2)}, u32[]{:S(2)}) %collective-permute-start) | collective-permute-done | bytes 98336 | tf_op jit(solution)/shard_map/ppermute | solution.py:28
  10.4 0.8 %collective-permute-done.1.minus_ref = bf16[2,3,16,512]{3,2,1,0:T(8,128)(2,1)S(1)} collective-permute-done((bf16[2,3,16,512]{3,2,1,0:T(8,128)(2,1)S(1)}, bf16[2,3,16,512]{3,2,1,0:T(8,128)(2,1)S(1)}, u32[]{:S(2)}, u32[]{:S(2)}) %collective-permute-start.1) | collective-permute-done | bytes 98336 | tf_op jit(solution)/shard_map/ppermute | solution.py:28
  11.3 1.7 %collective-permute-start.2 = (bf16[2,3,16,512]{3,2,1,0:T(8,128)(2,1)S(1)}, bf16[2,3,16,512]{3,2,1,0:T(8,128)(2,1)S(1)}, u32[]{:S(2)}, u32[]{:S(2)}) collective-permute-start(bf16[2,3,16,512]{3,2,1,0:T(8,128)(2,1)S(1)} %get-tuple-element.68.after_ref), channel_id=1, source_target_pairs={{0,15},{1,2},{2,1},{3,4},{4,3},{5,6},{6,5},{7,8},{8,7},{9,10},{10,... | collective-permute-start | bytes 294920 | tf_op jit(solution)/shard_map/ppermute | solution.py:43
  13.0 0.0 collective-permute-start.3
  13.0 1.4 %shard_map.108.refs_2_.refs_6_ = f32[256,128]{1,0:T(8,128)S(1)} custom-call(bf16[2,3,16,512]{3,2,1,0:T(8,128)(2,1)S(1)} %get-tuple-element.68.after_ref, s32[128,256]{1,0:T(8,128)S(1)} %get-tuple-element.74.neigh_ref, s32[1,128]{1,0:T(1,128)S(1)} %get-tuple-element.75.count_ref), custom_call_target="tpu_custom_call" | custom-call | flops 1000000 | bytes 10000 | tf_op jit(solution)/shard_map/pallas_call | solution.py:474
  14.5 3.7 %collective-permute-done.2.second_in = bf16[2,3,16,512]{3,2,1,0:T(8,128)(2,1)S(1)} collective-permute-done((bf16[2,3,16,512]{3,2,1,0:T(8,128)(2,1)S(1)}, bf16[2,3,16,512]{3,2,1,0:T(8,128)(2,1)S(1)}, u32[]{:S(2)}, u32[]{:S(2)}) %collective-permute-start.2) | collective-permute-done | bytes 98336 | tf_op jit(solution)/shard_map/ppermute | solution.py:43
  18.1 0.0 collective-permute-done.3.first_in
  18.1 0.6 %shard_map.107 = (bf16[4,2,128,128]{3,2,1,0:T(8,128)(2,1)S(1)}, bf16[4,2,128,128]{3,2,1,0:T(8,128)(2,1)S(1)}, bf16[4,2,128,128]{3,2,1,0:T(8,128)(2,1)S(1)}, bf16...) custom-call(s32[1]{0:T(128)} %bitcast.me_ref, bf16[2,3,16,512]{3,2,1,0:T(8,128)(2,1)S(1)} %collective-permute-done.2.second_in, ...), custom_call_target="tpu_custom_call" | custom-call | flops 1000000 | bytes 10000 | tf_op jit(solution)/shard_map/pallas_call | solution.py:474
  18.7 4.5 %shard_map.111 = (f32[4,32,1536]{2,1,0:T(8,128)S(1)}, f32[4,32,1536]{2,1,0:T(8,128)S(1)}, bf16[4,32,1536]{2,1,0:T(8,128)(2,1)S(1)}, bf16[4,32,1536]{2,1,0:T(8,12...) custom-call(s32[1]{0:T(128)} %bitcast.me_ref, ...), custom_call_target="tpu_custom_call" | custom-call | flops 1000000 | bytes 10000 | tf_op jit(solution)/shard_map/pallas_call | solution.py:474
  23.2 0.1 collective-permute-start.6
  23.3 0.5 collective-permute-start.5
  23.8 1.2 %collective-permute-done.6 = bf16[4,32,1536]{2,1,0:T(8,128)(2,1)S(1)} collective-permute-done((bf16[4,32,1536]{2,1,0:T(8,128)(2,1)S(1)}, bf16[4,32,1536]{2,1,0:T(8,128)(2,1)S(1)}, u32[]{:S(2)}, u32[]{:S(2)}) %collective-permute-start.6) | collective-permute-done | bytes 393248 | tf_op jit(solution)/shard_map/ppermute | solution.py:566
  25.0 0.1 add_convert_fusion
  25.1 0.1 collective-permute-start.7
  25.2 1.7 %shard_map.109 = (f32[4,32,512]{2,1,0:T(8,128)S(1)}, f32[4,32,512]{2,1,0:T(8,128)S(1)}, bf16[4,32,512]{2,1,0:T(8,128)(2,1)S(1)}, bf16[4,32,512]{2,1,0:T(8,128)(2...) custom-call(s32[1]{0:T(128)} %bitcast.me_ref, ...), custom_call_target="tpu_custom_call" | custom-call | flops 1000000 | bytes 10000 | tf_op jit(solution)/shard_map/pallas_call | solution.py:474
  26.9 0.2 collective-permute-start.4
  27.1 0.4 collective-permute-start.11
  27.5 0.8 %collective-permute-done.4.refs_1_ = bf16[4,32,512]{2,1,0:T(8,128)(2,1)S(1)} collective-permute-done((bf16[4,32,512]{2,1,0:T(8,128)(2,1)S(1)}, bf16[4,32,512]{2,1,0:T(8,128)(2,1)S(1)}, u32[]{:S(2)}, u32[]{:S(2)}) %collective-permute-start.4) | collective-permute-done | bytes 131104 | tf_op jit(solution)/shard_map/ppermute | solution.py:566
  28.3 2.1 %collective-permute-start.10 = (bf16[4,32,512]{2,1,0:T(8,128)(2,1)S(1)}, bf16[4,32,512]{2,1,0:T(8,128)(2,1)S(1)}, u32[]{:S(2)}, u32[]{:S(2)}) collective-permute-start(bf16[4,32,512]{2,1,0:T(8,128)(2,1)S(1)} %shard_map.110.refs_0_), channel_id=1, source_target_pairs={{0,2},{1,3},{2,0},{3,1},{4,6},{5,7},{6,4},{7,5},{8,10},{9,11},{10,... | collective-permute-start | bytes 393224 | tf_op jit(solution)/shard_map/ppermute | solution.py:580
  30.4 1.0 %shard_map.112 = (f32[2,128,512]{2,1,0:T(8,128)S(1)}, bf16[2,3,16,512]{3,2,1,0:T(8,128)(2,1)S(1)}, bf16[2,3,16,512]{3,2,1,0:T(8,128)(2,1)S(1)}, bf16[2,1,16,512]...) custom-call(bf16[4,32,512]{2,1,0:T(8,128)(2,1)S(1)} %shard_map.110.refs_0_, ...), custom_call_target="tpu_custom_call" | custom-call | flops 1000000 | bytes 10000 | tf_op jit(solution)/shard_map/pallas_call | solution.py:474
  31.4 0.8 %collective-permute-start.8 = (bf16[2,3,16,512]{3,2,1,0:T(8,128)(2,1)S(1)}, bf16[2,3,16,512]{3,2,1,0:T(8,128)(2,1)S(1)}, u32[]{:S(2)}, u32[]{:S(2)}) collective-permute-start(bf16[2,3,16,512]{3,2,1,0:T(8,128)(2,1)S(1)} %get-tuple-element.106), channel_id=1, source_target_pairs={{0,12},{1,13},{2,14},{3,15},{4,0},{5,1},{6,2},{7,3},{8,4},{9,5},{1... | collective-permute-start | bytes 294920 | tf_op jit(solution)/shard_map/ppermute | solution.py:28
  32.2 0.0 collective-permute-done.5.core_in
  32.2 1.3 %collective-permute-start.9 = (bf16[2,3,16,512]{3,2,1,0:T(8,128)(2,1)S(1)}, bf16[2,3,16,512]{3,2,1,0:T(8,128)(2,1)S(1)}, u32[]{:S(2)}, u32[]{:S(2)}) collective-permute-start(bf16[2,3,16,512]{3,2,1,0:T(8,128)(2,1)S(1)} %get-tuple-element.107), channel_id=1, source_target_pairs={{0,4},{1,5},{2,6},{3,7},{4,8},{5,9},{6,10},{7,11},{8,12},{9,13},{1... | collective-permute-start | bytes 294920 | tf_op jit(solution)/shard_map/ppermute | solution.py:28
  33.5 3.6 %collective-permute-done.7.y_in = bf16[4,32,1536]{2,1,0:T(8,128)(2,1)S(1)} collective-permute-done((bf16[4,32,1536]{2,1,0:T(8,128)(2,1)S(1)}, bf16[4,32,1536]{2,1,0:T(8,128)(2,1)S(1)}, u32[]{:S(2)}, u32[]{:S(2)}) %collective-permute-start.7) | collective-permute-done | bytes 393248 | tf_op jit(solution)/shard_map/ppermute | solution.py:573
  37.1 0.1 shard_map.113
  37.3 0.1 collective-permute-start.14
  37.4 0.0 collective-permute-done.8.plus_ref
  37.4 2.3 %collective-permute-done.9.minus_ref = bf16[2,3,16,512]{3,2,1,0:T(8,128)(2,1)S(1)} collective-permute-done((bf16[2,3,16,512]{3,2,1,0:T(8,128)(2,1)S(1)}, bf16[2,3,16,512]{3,2,1,0:T(8,128)(2,1)S(1)}, u32[]{:S(2)}, u32[]{:S(2)}) %collective-permute-start.9) | collective-permute-done | bytes 98336 | tf_op jit(solution)/shard_map/ppermute | solution.py:28
  39.7 0.0 collective-permute-done.11.refs_4_
  39.7 0.0 collective-permute-done.10.refs_2_
  39.7 0.1 shard_map.115
  39.8 2.7 %collective-permute-done.14.in_a = bf16[18,32,128]{2,1,0:T(8,128)(2,1)S(1)} collective-permute-done((bf16[18,32,128]{2,1,0:T(8,128)(2,1)S(1)}, bf16[18,32,128]{2,1,0:T(8,128)(2,1)S(1)}, u32[]{:S(2)}, u32[]{:S(2)}) %collective-permute-start.14) | collective-permute-done | bytes 147488 | tf_op jit(solution)/shard_map/ppermute | solution.py:590
  42.5 0.0 copy-start
  42.5 0.8 %collective-permute-start.16 = (bf16[16,32,128]{2,1,0:T(8,128)(2,1)S(1)}, bf16[16,32,128]{2,1,0:T(8,128)(2,1)S(1)}, u32[]{:S(2)}, u32[]{:S(2)}) collective-permute-start(bf16[16,32,128]{2,1,0:T(8,128)(2,1)S(1)} %get-tuple-element.118), channel_id=1, source_target_pairs={{0,12},{1,13},{2,14},{3,15},{4,8},{5,9},{6,10},{7,11},{8,4},{9,5},... | collective-permute-start | bytes 393224 | tf_op jit(solution)/shard_map/ppermute | solution.py:590
  43.3 1.9 %collective-permute-start.12 = (bf16[2,3,16,512]{3,2,1,0:T(8,128)(2,1)S(1)}, bf16[2,3,16,512]{3,2,1,0:T(8,128)(2,1)S(1)}, u32[]{:S(2)}, u32[]{:S(2)}) collective-permute-start(bf16[2,3,16,512]{3,2,1,0:T(8,128)(2,1)S(1)} %get-tuple-element.113), channel_id=1, source_target_pairs={{0,15},{1,2},{2,1},{3,4},{4,3},{5,6},{6,5},{7,8},{8,7},{9,10},{10,... | collective-permute-start | bytes 294920 | tf_op jit(solution)/shard_map/ppermute | solution.py:43
  45.2 0.0 collective-permute-start.13
  45.2 0.0 collective-permute-start.15
  45.2 2.6 %collective-permute-start.17 = (bf16[7,32,128]{2,1,0:T(8,128)(2,1)S(1)}, bf16[7,32,128]{2,1,0:T(8,128)(2,1)S(1)}, u32[]{:S(2)}, u32[]{:S(2)}) collective-permute-start(bf16[7,32,128]{2,1,0:T(8,128)(2,1)S(1)} %get-tuple-element.119), channel_id=1, source_target_pairs={{0,8},{1,9},{2,10},{3,11},{4,12},{5,13},{6,14},{7,15},{8,0},{9,1},... | collective-permute-start | bytes 172040 | tf_op jit(solution)/shard_map/ppermute | solution.py:590
  47.9 2.9 %collective-permute-done.12.second_in = bf16[2,3,16,512]{3,2,1,0:T(8,128)(2,1)S(1)} collective-permute-done((bf16[2,3,16,512]{3,2,1,0:T(8,128)(2,1)S(1)}, bf16[2,3,16,512]{3,2,1,0:T(8,128)(2,1)S(1)}, u32[]{:S(2)}, u32[]{:S(2)}) %collective-permute-start.12) | collective-permute-done | bytes 98336 | tf_op jit(solution)/shard_map/ppermute | solution.py:43
  50.8 1.0 %shard_map.116.after_ref = bf16[2,128,512]{2,1,0:T(8,128)(2,1)} custom-call(s32[1]{0:T(128)} %bitcast.me_ref, bf16[7,32,128]{2,1,0:T(8,128)(2,1)S(1)} %get-tuple-element.112.after_ref, bf16[2,3,16,512]{3,2,1,0:T(8,128)(2,1)S(1)} %collective-permute-done.12.second_in, bf16[2,3,16,512]{3,2,1,0:T(8,128)(2,1)S(1)} %collective-permute-done.13.first_in, ...), custom_call_target="tpu_custom_call" | custom-call | flops 1000000 | bytes 10000 | tf_op jit(solution)/shard_map/pallas_call | solution.py:474
  51.7 0.0 collective-permute-done.15.refs_0_
  51.7 0.3 collective-permute-done.17.refs_2_
  52.1 0.0 collective-permute-done.16.refs_1_
  52.1 0.7 %shard_map.118 = f32[32,2048]{1,0:T(8,128)} custom-call(bf16[2,128,512]{2,1,0:T(8,128)(2,1)} %shard_map.116.after_ref, f32[32,1152]{1,0:T(8,128)S(1)} %get-tuple-element.116.own_a, f32[32,896]{1,0:T(8,128)S(1)} %get-tuple-element.117.own_b, bf16[7,32,128]{2,1,0:T(8,128)(2,1)S(1)} %collective-permute-done.15.refs_0_, ...), custom_call_target="tpu_custom_call" | custom-call | flops 1000000 | bytes 10000 | tf_op jit(solution)/shard_map/pallas_call | solution.py:474
  (6 shorter events, 0.1 us)
Async XLA Ops:
  1.8 8.6 %collective-permute-start = (bf16[2,3,16,512]{3,2,1,0:T(8,128)(2,1)S(1)}, bf16[2,3,16,512]{3,2,1,0:T(8,128)(2,1)S(1)}, u32[]{:S(2)}, u32[]{:S(2)}) collective-permute-start(bf16[2,3,16,512]{3,2,1,0:T(8,128)(2,1)S(1)} %get-tuple-element.66), channel_id=1, source_target_pairs={{0,4},{1,5},{2,6},{3,7},{4,8},{5,9},{6,10},{7,11},{8,12},{9,13},{1... | collective-permute-start | bytes 294920 | tf_op jit(solution)/shard_map/ppermute | solution.py:28
  4.9 6.4 %collective-permute-start.1 = (bf16[2,3,16,512]{3,2,1,0:T(8,128)(2,1)S(1)}, bf16[2,3,16,512]{3,2,1,0:T(8,128)(2,1)S(1)}, u32[]{:S(2)}, u32[]{:S(2)}) collective-permute-start(bf16[2,3,16,512]{3,2,1,0:T(8,128)(2,1)S(1)} %get-tuple-element.67), channel_id=1, source_target_pairs={{0,12},{1,13},{2,14},{3,15},{4,0},{5,1},{6,2},{7,3},{8,4},{9,5},{1... | collective-permute-start | bytes 294920 | tf_op jit(solution)/shard_map/ppermute | solution.py:28
  11.3 6.8 %collective-permute-start.2 = (bf16[2,3,16,512]{3,2,1,0:T(8,128)(2,1)S(1)}, bf16[2,3,16,512]{3,2,1,0:T(8,128)(2,1)S(1)}, u32[]{:S(2)}, u32[]{:S(2)}) collective-permute-start(bf16[2,3,16,512]{3,2,1,0:T(8,128)(2,1)S(1)} %get-tuple-element.68.after_ref), channel_id=1, source_target_pairs={{0,15},{1,2},{2,1},{3,4},{4,3},{5,6},{6,5},{7,8},{8,7},{9,10},{10,... | collective-permute-start | bytes 294920 | tf_op jit(solution)/shard_map/ppermute | solution.py:43
  13.0 5.1 %collective-permute-start.3 = (bf16[2,3,16,512]{3,2,1,0:T(8,128)(2,1)S(1)}, bf16[2,3,16,512]{3,2,1,0:T(8,128)(2,1)S(1)}, u32[]{:S(2)}, u32[]{:S(2)}) collective-permute-start(bf16[2,3,16,512]{3,2,1,0:T(8,128)(2,1)S(1)} %get-tuple-element.69), channel_id=1, source_target_pairs={{0,1},{1,0},{2,3},{3,2},{4,5},{5,4},{6,7},{7,6},{8,9},{9,8},{10,11... | collective-permute-start | bytes 294920 | tf_op jit(solution)/shard_map/ppermute | solution.py:44
  23.2 1.8 %collective-permute-start.6 = (bf16[4,32,1536]{2,1,0:T(8,128)(2,1)S(1)}, bf16[4,32,1536]{2,1,0:T(8,128)(2,1)S(1)}, u32[]{:S(2)}, u32[]{:S(2)}) collective-permute-start(bf16[4,32,1536]{2,1,0:T(8,128)(2,1)S(1)} %get-tuple-element.102), channel_id=1, source_target_pairs={{0,1},{1,0},{2,3},{3,2},{4,5},{5,4},{6,7},{7,6},{8,9},{9,8},{10,11... | collective-permute-start | bytes 1179656 | tf_op jit(solution)/shard_map/ppermute | solution.py:566
  23.3 8.9 %collective-permute-start.5 = (bf16[4,32,1536]{2,1,0:T(8,128)(2,1)S(1)}, bf16[4,32,1536]{2,1,0:T(8,128)(2,1)S(1)}, u32[]{:S(2)}, u32[]{:S(2)}) collective-permute-start(bf16[4,32,1536]{2,1,0:T(8,128)(2,1)S(1)} %get-tuple-element.100), channel_id=1, source_target_pairs={{0,1},{1,0},{2,3},{3,2},{4,5},{5,4},{6,7},{7,6},{8,9},{9,8},{10,11... | collective-permute-start | bytes 1179656 | tf_op jit(solution)/shard_map/ppermute | solution.py:566
  25.1 12.0 %collective-permute-start.7 = (bf16[4,32,1536]{2,1,0:T(8,128)(2,1)S(1)}, bf16[4,32,1536]{2,1,0:T(8,128)(2,1)S(1)}, u32[]{:S(2)}, u32[]{:S(2)}) collective-permute-start(bf16[4,32,1536]{2,1,0:T(8,128)(2,1)S(1)} %add_convert_fusion), channel_id=1, source_target_pairs={{0,2},{1,3},{2,0},{3,1},{4,6},{5,7},{6,4},{7,5},{8,10},{9,11},{10,... | collective-permute-start | bytes 1179656 | tf_op jit(solution)/shard_map/ppermute | solution.py:573
  26.9 1.4 %collective-permute-start.4 = (bf16[4,32,512]{2,1,0:T(8,128)(2,1)S(1)}, bf16[4,32,512]{2,1,0:T(8,128)(2,1)S(1)}, u32[]{:S(2)}, u32[]{:S(2)}) collective-permute-start(bf16[4,32,512]{2,1,0:T(8,128)(2,1)S(1)} %get-tuple-element.79), channel_id=1, source_target_pairs={{0,1},{1,0},{2,3},{3,2},{4,5},{5,4},{6,7},{7,6},{8,9},{9,8},{10,11... | collective-permute-start | bytes 393224 | tf_op jit(solution)/shard_map/ppermute | solution.py:566
  27.1 12.6 %collective-permute-start.11 = (bf16[4,32,512]{2,1,0:T(8,128)(2,1)S(1)}, bf16[4,32,512]{2,1,0:T(8,128)(2,1)S(1)}, u32[]{:S(2)}, u32[]{:S(2)}) collective-permute-start(bf16[4,32,512]{2,1,0:T(8,128)(2,1)S(1)} %get-tuple-element.111), channel_id=1, source_target_pairs={{0,1},{1,0},{2,3},{3,2},{4,5},{5,4},{6,7},{7,6},{8,9},{9,8},{10,11... | collective-permute-start | bytes 393224 | tf_op jit(solution)/shard_map/ppermute | solution.py:566
  28.3 11.4 %collective-permute-start.10 = (bf16[4,32,512]{2,1,0:T(8,128)(2,1)S(1)}, bf16[4,32,512]{2,1,0:T(8,128)(2,1)S(1)}, u32[]{:S(2)}, u32[]{:S(2)}) collective-permute-start(bf16[4,32,512]{2,1,0:T(8,128)(2,1)S(1)} %shard_map.110.refs_0_), channel_id=1, source_target_pairs={{0,2},{1,3},{2,0},{3,1},{4,6},{5,7},{6,4},{7,5},{8,10},{9,11},{10,... | collective-permute-start | bytes 393224 | tf_op jit(solution)/shard_map/ppermute | solution.py:580
  31.4 5.9 %collective-permute-start.8 = (bf16[2,3,16,512]{3,2,1,0:T(8,128)(2,1)S(1)}, bf16[2,3,16,512]{3,2,1,0:T(8,128)(2,1)S(1)}, u32[]{:S(2)}, u32[]{:S(2)}) collective-permute-start(bf16[2,3,16,512]{3,2,1,0:T(8,128)(2,1)S(1)} %get-tuple-element.106), channel_id=1, source_target_pairs={{0,12},{1,13},{2,14},{3,15},{4,0},{5,1},{6,2},{7,3},{8,4},{9,5},{1... | collective-permute-start | bytes 294920 | tf_op jit(solution)/shard_map/ppermute | solution.py:28
  32.2 7.5 %collective-permute-start.9 = (bf16[2,3,16,512]{3,2,1,0:T(8,128)(2,1)S(1)}, bf16[2,3,16,512]{3,2,1,0:T(8,128)(2,1)S(1)}, u32[]{:S(2)}, u32[]{:S(2)}) collective-permute-start(bf16[2,3,16,512]{3,2,1,0:T(8,128)(2,1)S(1)} %get-tuple-element.107), channel_id=1, source_target_pairs={{0,4},{1,5},{2,6},{3,7},{4,8},{5,9},{6,10},{7,11},{8,12},{9,13},{1... | collective-permute-start | bytes 294920 | tf_op jit(solution)/shard_map/ppermute | solution.py:28
  37.3 5.2 %collective-permute-start.14 = (bf16[18,32,128]{2,1,0:T(8,128)(2,1)S(1)}, bf16[18,32,128]{2,1,0:T(8,128)(2,1)S(1)}, u32[]{:S(2)}, u32[]{:S(2)}) collective-permute-start(bf16[18,32,128]{2,1,0:T(8,128)(2,1)S(1)} %get-tuple-element.103.after_ref), channel_id=1, source_target_pairs={{0,4},{1,5},{2,6},{3,7},{4,0},{5,1},{6,2},{7,3},{8,12},{9,13},{10,... | collective-permute-start | bytes 442376 | tf_op jit(solution)/shard_map/ppermute | solution.py:590
  42.5 8.2 %copy-start = (s32[1,8,16]{2,1,0:T(8,128)S(1)}, s32[1,8,16]{2,1,0:T(8,128)}, u32[]{:S(2)}) copy-start(s32[1,8,16]{2,1,0:T(8,128)} %send_ref.1) | copy-start | bytes 1540
  42.5 9.5 %collective-permute-start.16 = (bf16[16,32,128]{2,1,0:T(8,128)(2,1)S(1)}, bf16[16,32,128]{2,1,0:T(8,128)(2,1)S(1)}, u32[]{:S(2)}, u32[]{:S(2)}) collective-permute-start(bf16[16,32,128]{2,1,0:T(8,128)(2,1)S(1)} %get-tuple-element.118), channel_id=1, source_target_pairs={{0,12},{1,13},{2,14},{3,15},{4,8},{5,9},{6,10},{7,11},{8,4},{9,5},... | collective-permute-start | bytes 393224 | tf_op jit(solution)/shard_map/ppermute | solution.py:590
  43.3 7.4 %collective-permute-start.12 = (bf16[2,3,16,512]{3,2,1,0:T(8,128)(2,1)S(1)}, bf16[2,3,16,512]{3,2,1,0:T(8,128)(2,1)S(1)}, u32[]{:S(2)}, u32[]{:S(2)}) collective-permute-start(bf16[2,3,16,512]{3,2,1,0:T(8,128)(2,1)S(1)} %get-tuple-element.113), channel_id=1, source_target_pairs={{0,15},{1,2},{2,1},{3,4},{4,3},{5,6},{6,5},{7,8},{8,7},{9,10},{10,... | collective-permute-start | bytes 294920 | tf_op jit(solution)/shard_map/ppermute | solution.py:43
  45.2 5.5 %collective-permute-start.13 = (bf16[2,3,16,512]{3,2,1,0:T(8,128)(2,1)S(1)}, bf16[2,3,16,512]{3,2,1,0:T(8,128)(2,1)S(1)}, u32[]{:S(2)}, u32[]{:S(2)}) collective-permute-start(bf16[2,3,16,512]{3,2,1,0:T(8,128)(2,1)S(1)} %get-tuple-element.108.refs_0_), channel_id=1, source_target_pairs={{0,1},{1,0},{2,3},{3,2},{4,5},{5,4},{6,7},{7,6},{8,9},{9,8},{10,11... | collective-permute-start | bytes 294920 | tf_op jit(solution)/shard_map/ppermute | solution.py:44
  45.2 6.5 %collective-permute-start.15 = (bf16[7,32,128]{2,1,0:T(8,128)(2,1)S(1)}, bf16[7,32,128]{2,1,0:T(8,128)(2,1)S(1)}, u32[]{:S(2)}, u32[]{:S(2)}) collective-permute-start(bf16[7,32,128]{2,1,0:T(8,128)(2,1)S(1)} %get-tuple-element.112.after_ref), channel_id=1, source_target_pairs={{0,4},{1,5},{2,6},{3,7},{4,0},{5,1},{6,2},{7,3},{8,12},{9,13},{10,... | collective-permute-start | bytes 172040 | tf_op jit(solution)/shard_map/ppermute | solution.py:590
  45.2 6.8 %collective-permute-start.17 = (bf16[7,32,128]{2,1,0:T(8,128)(2,1)S(1)}, bf16[7,32,128]{2,1,0:T(8,128)(2,1)S(1)}, u32[]{:S(2)}, u32[]{:S(2)}) collective-permute-start(bf16[7,32,128]{2,1,0:T(8,128)(2,1)S(1)} %get-tuple-element.119), channel_id=1, source_target_pairs={{0,8},{1,9},{2,10},{3,11},{4,12},{5,13},{6,14},{7,15},{8,0},{9,1},... | collective-permute-start | bytes 172040 | tf_op jit(solution)/shard_map/ppermute | solution.py:590

commit v12 on v11

--- a/solution.py
+++ b/solution.py
@@ -191,9 +191,63 @@
                 ref[kind + 2, m] = block.T
 
 
+STRIP = 64
+
+
+def by_head_t(block, head):
+    row_head = lax.broadcasted_iota(jnp.int32, block.shape, 0) // head
+    zero = jnp.zeros_like(block)
+    return jnp.concatenate(
+        [jnp.where(row_head == h, block, zero) for h in range(block.shape[0] // head)], axis=1
+    )
+
+
+def by_head_n(block, head):
+    lane_head = lax.broadcasted_iota(jnp.int32, block.shape, 1) // head
+    zero = jnp.zeros_like(block)
+    return jnp.concatenate(
+        [jnp.where(lane_head == h, block, zero) for h in range(block.shape[1] // head)], axis=0
+    )
+
+
+def unnormalised(scale, score, grad, slope, m, lanes, mask_ref, start):
+    columns, node_rows = score.shape[1], mask_ref.shape[1]
+    den = jnp.zeros((8, node_rows), f32)
+    inner = jnp.zeros((8, node_rows), f32)
+    for c in range(0, columns, STRIP):
+        box = (m, slice(c, c + STRIP), lanes)
+        t = jnp.tanh(score[box] * (scale / score_cap))
+        e = jnp.exp2(t * (score_cap / math.log(2.0))) * mask_ref[start + c : start + c + STRIP]
+        den = den + jnp.sum(e.reshape(STRIP // 8, 8, node_rows), axis=0)
+        inner = inner + jnp.sum((e * grad[box]).reshape(STRIP // 8, 8, node_rows), axis=0)
+        score[box] = e
+        slope[box] = e * (scale - scale * (t * t))
+    return den, inner
+
+
+def own_kernel(groups, *refs):
+    locs, mask_ref, outs = refs[:groups], refs[groups], refs[groups + 1 :]
+    _, members, node_rows, _ = locs[0].shape
+    head = 128 * groups // HEADS
+    scale = 1.0 / math.sqrt(head)
+    for g, loc in enumerate(locs):
+        own, totals = outs[2 * g : 2 * g + 2]
+        score, grad, slope = own.at[0], own.at[1], own.at[2]
+        for m in range(members):
+            score[m] = nn(loc[K, m], by_head_t(loc[QT, m], head))
+            grad[m] = nn(loc[V, m], by_head_t(loc[GT, m], head))
+        for m in range(members):
+            for h in range(128 // head):
+                lanes = slice(h * node_rows, (h + 1) * node_rows)
+                den, inner = unnormalised(scale, score, grad, slope, m, lanes, mask_ref, 0)
+                totals[0, m, :, lanes] = den
+                totals[1, m, :, lanes] = inner
+
+
 def attention_kernel(extra, here, me_ref, *refs):
     refs = refs[extra:]
-    locs, halos, refs = refs[:here], refs[here : 2 * here], refs[2 * here :]
+    locs, halos, owns = refs[:here], refs[here : 2 * here], refs[2 * here : 4 * here]
+    refs = refs[4 * here :]
     mask_ref, xtf, og_ref = refs[:3]
     split = 7 if len(refs) == 15 + 3 * (here - 1) else 6
     outs, grads, scratch = refs[3:split], refs[split : split + 3 * here], refs[split + 3 * here :]
@@ -201,12 +255,12 @@
         outs = (*outs[:2], outs[2].at[0], outs[2].at[1])
     for i in range(here):
         attend(
-            me_ref, locs[i], halos[i], mask_ref, xtf, og_ref, outs, 512 * i,
+            me_ref, locs[i], halos[i], owns[2 * i : 2 * i + 2], mask_ref, xtf, og_ref, outs, 512 * i,
             grads[3 * i : 3 * i + 3], scratch,
         )
 
 
-def attend(me_ref, loc, halo, mask_ref, xtf, og_ref, out_refs, at, grad_refs, scratch):
+def attend(me_ref, loc, halo, own, mask_ref, xtf, og_ref, out_refs, at, grad_refs, scratch):
     own_ref, other_ref, send_other, send_own = out_refs
     dq_ref, dk_ref, dv_ref = grad_refs
     score, grad, slope, dw, wos = scratch
@@ -217,23 +271,10 @@
     per = 128 // head
     scale = 1.0 / math.sqrt(head)
 
-    row_head = lax.broadcasted_iota(jnp.int32, (128, node_rows), 0) // head
-    lane_head = lax.broadcasted_iota(jnp.int32, (node_rows, 128), 1) // head
-
-    def spread_t(block):
-        zero = jnp.zeros_like(block)
-        return jnp.concatenate([jnp.where(row_head == h, block, zero) for h in range(per)], axis=1)
-
-    def spread_n(block):
-        zero = jnp.zeros_like(block)
-        return jnp.concatenate([jnp.where(lane_head == h, block, zero) for h in range(per)], axis=0)
-
-    strip = 64
+    own, totals = own
     for m in range(members):
-        kg = jnp.concatenate([loc[K, m], halo[0, m]], axis=0)
-        vg = jnp.concatenate([loc[V, m], halo[1, m]], axis=0)
-        score[m] = nn(kg, spread_t(loc[QT, m]))
-        grad[m] = nn(vg, spread_t(loc[GT, m]))
+        score[m] = nn(halo[0, m], by_head_t(loc[QT, m], head))
+        grad[m] = nn(halo[1, m], by_head_t(loc[GT, m], head))
 
     wo_total = None
     kv_total = None
@@ -242,24 +283,16 @@
         probs = []
         for h in range(per):
             lanes = slice(h * node_rows, (h + 1) * node_rows)
-            den = jnp.zeros((8, node_rows), f32)
-            inner = jnp.zeros((8, node_rows), f32)
-            for c in range(0, table, strip):
-                box = (m, slice(c, c + strip), lanes)
-                t = jnp.tanh(score[box] * (scale / score_cap))
-                e = jnp.exp2(t * (score_cap / math.log(2.0))) * mask_ref[c : c + strip]
-                den = den + jnp.sum(e.reshape(strip // 8, 8, node_rows), axis=0)
-                inner = inner + jnp.sum((e * grad[box]).reshape(strip // 8, 8, node_rows), axis=0)
-                score[box] = e
-                slope[box] = e * (scale - scale * (t * t))
-            r = 1.0 / jnp.sum(den, axis=0, keepdims=True)
-            inner = jnp.sum(inner, axis=0, keepdims=True) * r
+            den, inner = unnormalised(scale, score, grad, slope, m, lanes, mask_ref, node_rows)
+            r = 1.0 / jnp.sum(den + totals[0, m, :, lanes], axis=0, keepdims=True)
+            inner = jnp.sum(inner + totals[1, m, :, lanes], axis=0, keepdims=True) * r
             column = []
             scores = []
-            for c in range(0, table, strip):
-                box = (m, slice(c, c + strip), lanes)
-                column.append((score[box] * r).astype(bf16))
-                scores.append(((slope[box] * r) * (grad[box] - inner)).astype(bf16))
+            for e, g, w in ((own.at[0], own.at[1], own.at[2]), (score, grad, slope)):
+                for c in range(0, e.shape[1], STRIP):
+                    box = (m, slice(c, c + STRIP), lanes)
+                    column.append((e[box] * r).astype(bf16))
+                    scores.append(((w[box] * r) * (g[box] - inner)).astype(bf16))
             probs.append((jnp.concatenate(column, axis=0), jnp.concatenate(scores, axis=0)))
         pb = jnp.concatenate([p for p, _ in probs], axis=1)
         ds = jnp.concatenate([s for _, s in probs], axis=1)
@@ -277,8 +310,8 @@
                 dqt.append(b[inside].astype(bf16))
         att = jnp.concatenate(att, axis=0)
         dq = jnp.concatenate(dqt, axis=0).T
-        dk = nn(ds, spread_n(loc[Q, m])).astype(bf16)
-        dv = nn(pb, spread_n(loc[G, m])).astype(bf16)
+        dk = nn(ds, by_head_n(loc[Q, m], head)).astype(bf16)
+        dv = nn(pb, by_head_n(loc[G, m], head)).astype(bf16)
         dq_ref[m], dk_ref[m], dv_ref[m] = dq, dk, dv
         wo_term = nn(att, og_ref[m])
         kv_term = nn(xtf[m], jnp.concatenate([dk, dv], axis=1))
@@ -525,6 +558,15 @@
     (mask,) = call(
         mask_kernel, [((table, node_rows), f32)], (outgoing[1], neigh, counts), specs=[pl.ANY]
     )
+    own_part = call(
+        functools.partial(own_kernel, groups),
+        [
+            ((3, members, node_rows, 4 * node_rows), f32),
+            ((2, members, 8, 4 * node_rows), f32),
+        ]
+        * groups,
+        (*loc, mask),
+    )
     *halo, xtf = call(
         halo_kernel,
         [((4, members, node_rows, 128), bf16)] * groups + [((members, width, table), bf16)],
@@ -551,10 +593,11 @@
             ]
             * len(which),
             (
-                place, *extra, *[loc[g] for g in which], *[halo[g] for g in which], mask, xtf, og,
+                place, *extra, *[loc[g] for g in which], *[halo[g] for g in which],
+                *[part for g in which for part in own_part[2 * g : 2 * g + 2]], mask, xtf, og,
             ),
             specs=[pltpu.SMEM] + [pl.ANY] * len(extra),
-            scratch=[pltpu.VMEM((members, table, 512), f32)] * 3
+            scratch=[pltpu.VMEM((members, table - node_rows, 512), f32)] * 3
             + [
                 pltpu.VMEM((planes, 2, 2, rows, 384), f32),
                 pltpu.VMEM((inner_planes, 2, 2, rows, width), f32),

time: 53 us -> 52.2 us (0.985)
  waiting for transfers between devices: 19.1 us -> 18 us
    ppermute x2, waiting for transfers between devices: 6.52 us -> 5.16 us  [swap(): later = lax.ppermute(pair[1], 'patch', second)]
    pallas_call x15 -> x16, Pallas kernels: 15.2 us -> 15.7 us  [call(): pl.pallas_call(kernel, out_shape=[jax.ShapeDtypeStruct(*o) if final else...]
  transfers between devices with their start and end apart: 18 -> 18, of which waited for: 10 -> 10; matrix products, arithmetic and copies ran while one was open for 0% -> 0% of each run, Pallas kernels for 15% -> 18%
where the time goes in v12:
time: 52.2 us; the launch traced here: 52 us
  waiting for transfers between devices  18 us (34%)
  starting transfers between devices  17.5 us (34%)
  Pallas kernels  15.7 us (30%)
  between operations  0.78 us (1%)
    pallas_call x16, Pallas kernels, call(): pl.pallas_call(kernel, out_shape=[jax.ShapeDtypeStruct(*o) if final else...  15.7 us
    ppermute x4, starting transfers between devices, shifted(): lax.ppermute(shard, 'patch', [(i, (i + by) % count) for i in range(count)])  7.25 us
    ppermute x2, waiting for transfers between devices, swap(): later = lax.ppermute(pair[1], 'patch', second)  5.16 us
    ppermute x1, waiting for transfers between devices, body(): y_a = lax.ppermute(y_sent, 'patch', flop)  3.75 us
    ppermute x4, waiting for transfers between devices, shifted(): lax.ppermute(shard, 'patch', [(i, (i + by) % count) for i in range(count)])  3.75 us
    ppermute x4, starting transfers between devices, exchange(): return lax.ppermute(sent, 'patch', along_z(count, distance))  3.61 us
    ppermute x2, starting transfers between devices, swap(): later = lax.ppermute(pair[1], 'patch', second)  3.34 us
    ppermute x4, waiting for transfers between devices, exchange(): return lax.ppermute(sent, 'patch', along_z(count, distance))  3.23 us
  transfers between devices with their start and end apart: 18, of which 10 were waited for; matrix products, arithmetic and copies ran while one was open for 0% of the time, Pallas kernels for 18%

profile of v12, /device:TPU:0, one launch (start us, length us, event | category | flops | bytes accessed | tf_op | source)
XLA Modules:
  0.0 52.0 jit_solution(3128924253889233904)
XLA Ops:
  0.6 1.2 %shard_map.104 = (bf16[2,3,16,512]{3,2,1,0:T(8,128)(2,1)S(1)}, bf16[2,3,16,512]{3,2,1,0:T(8,128)(2,1)S(1)}, bf16[2,1,16,512]{3,2,1,0:T(8,128)(2,1)S(1)}, bf16[2,...) custom-call(s32[1,8,16]{2,1,0:T(8,128)} %send_ref.1, bf16[2,128,512]{2,1,0:T(8,128)(2,1)} %x_hbm.1), custom_call_target="tpu_custom_call" | custom-call | flops 1000000 | bytes 10000 | tf_op jit(solution)/shard_map/pallas_call | solution.py:507
  1.8 3.1 %collective-permute-start = (bf16[2,3,16,512]{3,2,1,0:T(8,128)(2,1)S(1)}, bf16[2,3,16,512]{3,2,1,0:T(8,128)(2,1)S(1)}, u32[]{:S(2)}, u32[]{:S(2)}) collective-permute-start(bf16[2,3,16,512]{3,2,1,0:T(8,128)(2,1)S(1)} %get-tuple-element.74), channel_id=1, source_target_pairs={{0,4},{1,5},{2,6},{3,7},{4,8},{5,9},{6,10},{7,11},{8,12},{9,13},{1... | collective-permute-start | bytes 294920 | tf_op jit(solution)/shard_map/ppermute | solution.py:28
  4.9 2.1 %collective-permute-start.1 = (bf16[2,3,16,512]{3,2,1,0:T(8,128)(2,1)S(1)}, bf16[2,3,16,512]{3,2,1,0:T(8,128)(2,1)S(1)}, u32[]{:S(2)}, u32[]{:S(2)}) collective-permute-start(bf16[2,3,16,512]{3,2,1,0:T(8,128)(2,1)S(1)} %get-tuple-element.75), channel_id=1, source_target_pairs={{0,12},{1,13},{2,14},{3,15},{4,0},{5,1},{6,2},{7,3},{8,4},{9,5},{1... | collective-permute-start | bytes 294920 | tf_op jit(solution)/shard_map/ppermute | solution.py:28
  7.0 2.6 %shard_map.105 = (bf16[8,2,128,128]{3,2,1,0:T(8,128)(2,1)S(1)}, bf16[8,2,128,128]{3,2,1,0:T(8,128)(2,1)S(1)}, bf16[8,2,128,128]{3,2,1,0:T(8,128)(2,1)S(1)}, bf16...) custom-call(bf16[2,1,16,512]{3,2,1,0:T(8,128)(2,1)S(1)} %get-tuple-e, ...), custom_call_target="tpu_custom_call" | custom-call | flops 1000000 | bytes 10000 | tf_op jit(solution)/shard_map/pallas_call | solution.py:507
  9.7 0.8 %collective-permute-done.plus_ref = bf16[2,3,16,512]{3,2,1,0:T(8,128)(2,1)S(1)} collective-permute-done((bf16[2,3,16,512]{3,2,1,0:T(8,128)(2,1)S(1)}, bf16[2,3,16,512]{3,2,1,0:T(8,128)(2,1)S(1)}, u32[]{:S(2)}, u32[]{:S(2)}) %collective-permute-start) | collective-permute-done | bytes 98336 | tf_op jit(solution)/shard_map/ppermute | solution.py:28
  10.4 0.8 %collective-permute-done.1.minus_ref = bf16[2,3,16,512]{3,2,1,0:T(8,128)(2,1)S(1)} collective-permute-done((bf16[2,3,16,512]{3,2,1,0:T(8,128)(2,1)S(1)}, bf16[2,3,16,512]{3,2,1,0:T(8,128)(2,1)S(1)}, u32[]{:S(2)}, u32[]{:S(2)}) %collective-permute-start.1) | collective-permute-done | bytes 98336 | tf_op jit(solution)/shard_map/ppermute | solution.py:28
  11.3 1.7 %collective-permute-start.2 = (bf16[2,3,16,512]{3,2,1,0:T(8,128)(2,1)S(1)}, bf16[2,3,16,512]{3,2,1,0:T(8,128)(2,1)S(1)}, u32[]{:S(2)}, u32[]{:S(2)}) collective-permute-start(bf16[2,3,16,512]{3,2,1,0:T(8,128)(2,1)S(1)} %get-tuple-element.76.after_ref), channel_id=1, source_target_pairs={{0,15},{1,2},{2,1},{3,4},{4,3},{5,6},{6,5},{7,8},{8,7},{9,10},{10,... | collective-permute-start | bytes 294920 | tf_op jit(solution)/shard_map/ppermute | solution.py:43
  13.0 0.0 collective-permute-start.3
  13.0 1.4 %shard_map.108.refs_4_.refs_12_ = f32[256,128]{1,0:T(8,128)S(1)} custom-call(bf16[2,3,16,512]{3,2,1,0:T(8,128)(2,1)S(1)} %get-tuple-element.76.after_ref, s32[128,256]{1,0:T(8,128)S(1)} %get-tuple-element.84.neigh_ref, s32[1,128]{1,0:T(1,128)S(1)} %get-tuple-element.85.count_ref), custom_call_target="tpu_custom_call" | custom-call | flops 1000000 | bytes 10000 | tf_op jit(solution)/shard_map/pallas_call | solution.py:507
  14.5 1.4 %shard_map.109 = (f32[3,2,128,512]{3,2,1,0:T(8,128)S(1)}, f32[2,2,8,512]{3,2,1,0:T(8,128)S(1)}, f32[3,2,128,512]{3,2,1,0:T(8,128)S(1)}, f32[2,2,8,512]{3,2,1,0:T...) custom-call(bf16[8,2,128,128]{3,2,1,0:T(8,128)(2,1)S(1)} %get-tuple-, ...), custom_call_target="tpu_custom_call" | custom-call | flops 1000000 | bytes 10000 | tf_op jit(solution)/shard_map/pallas_call | solution.py:507
  15.8 2.3 %collective-permute-done.2.second_in = bf16[2,3,16,512]{3,2,1,0:T(8,128)(2,1)S(1)} collective-permute-done((bf16[2,3,16,512]{3,2,1,0:T(8,128)(2,1)S(1)}, bf16[2,3,16,512]{3,2,1,0:T(8,128)(2,1)S(1)}, u32[]{:S(2)}, u32[]{:S(2)}) %collective-permute-start.2) | collective-permute-done | bytes 98336 | tf_op jit(solution)/shard_map/ppermute | solution.py:43
  18.1 0.0 collective-permute-done.3.first_in
  18.1 0.6 %shard_map.107 = (bf16[4,2,128,128]{3,2,1,0:T(8,128)(2,1)S(1)}, bf16[4,2,128,128]{3,2,1,0:T(8,128)(2,1)S(1)}, bf16[4,2,128,128]{3,2,1,0:T(8,128)(2,1)S(1)}, bf16...) custom-call(s32[1]{0:T(128)} %bitcast.me_ref, bf16[2,3,16,512]{3,2,1,0:T(8,128)(2,1)S(1)} %collective-permute-done.2.second_in, ...), custom_call_target="tpu_custom_call" | custom-call | flops 1000000 | bytes 10000 | tf_op jit(solution)/shard_map/pallas_call | solution.py:507
  18.7 3.8 %shard_map.112 = (f32[4,32,1536]{2,1,0:T(8,128)S(1)}, f32[4,32,1536]{2,1,0:T(8,128)S(1)}, bf16[4,32,1536]{2,1,0:T(8,128)(2,1)S(1)}, bf16[4,32,1536]{2,1,0:T(8,12...) custom-call(s32[1]{0:T(128)} %bitcast.me_ref, ...), custom_call_target="tpu_custom_call" | custom-call | flops 1000000 | bytes 10000 | tf_op jit(solution)/shard_map/pallas_call | solution.py:507
  22.5 0.1 collective-permute-start.6
  22.6 0.5 collective-permute-start.5
  23.1 1.2 %collective-permute-done.6 = bf16[4,32,1536]{2,1,0:T(8,128)(2,1)S(1)} collective-permute-done((bf16[4,32,1536]{2,1,0:T(8,128)(2,1)S(1)}, bf16[4,32,1536]{2,1,0:T(8,128)(2,1)S(1)}, u32[]{:S(2)}, u32[]{:S(2)}) %collective-permute-start.6) | collective-permute-done | bytes 393248 | tf_op jit(solution)/shard_map/ppermute | solution.py:609
  24.3 0.1 add_convert_fusion
  24.4 0.1 collective-permute-start.7
  24.5 1.5 %shard_map.110 = (f32[4,32,512]{2,1,0:T(8,128)S(1)}, f32[4,32,512]{2,1,0:T(8,128)S(1)}, bf16[4,32,512]{2,1,0:T(8,128)(2,1)S(1)}, bf16[4,32,512]{2,1,0:T(8,128)(2...) custom-call(s32[1]{0:T(128)} %bitcast.me_ref, ...), custom_call_target="tpu_custom_call" | custom-call | flops 1000000 | bytes 10000 | tf_op jit(solution)/shard_map/pallas_call | solution.py:507
  26.0 0.2 collective-permute-start.4
  26.2 0.4 collective-permute-start.11
  26.6 0.8 %collective-permute-done.4.refs_1_ = bf16[4,32,512]{2,1,0:T(8,128)(2,1)S(1)} collective-permute-done((bf16[4,32,512]{2,1,0:T(8,128)(2,1)S(1)}, bf16[4,32,512]{2,1,0:T(8,128)(2,1)S(1)}, u32[]{:S(2)}, u32[]{:S(2)}) %collective-permute-start.4) | collective-permute-done | bytes 131104 | tf_op jit(solution)/shard_map/ppermute | solution.py:609
  27.5 2.1 %collective-permute-start.10 = (bf16[4,32,512]{2,1,0:T(8,128)(2,1)S(1)}, bf16[4,32,512]{2,1,0:T(8,128)(2,1)S(1)}, u32[]{:S(2)}, u32[]{:S(2)}) collective-permute-start(bf16[4,32,512]{2,1,0:T(8,128)(2,1)S(1)} %shard_map.111.refs_0_), channel_id=1, source_target_pairs={{0,2},{1,3},{2,0},{3,1},{4,6},{5,7},{6,4},{7,5},{8,10},{9,11},{10,... | collective-permute-start | bytes 393224 | tf_op jit(solution)/shard_map/ppermute | solution.py:623
  29.6 1.0 %shard_map.113 = (f32[2,128,512]{2,1,0:T(8,128)S(1)}, bf16[2,3,16,512]{3,2,1,0:T(8,128)(2,1)S(1)}, bf16[2,3,16,512]{3,2,1,0:T(8,128)(2,1)S(1)}, bf16[2,1,16,512]...) custom-call(bf16[4,32,512]{2,1,0:T(8,128)(2,1)S(1)} %shard_map.111.refs_0_, ...), custom_call_target="tpu_custom_call" | custom-call | flops 1000000 | bytes 10000 | tf_op jit(solution)/shard_map/pallas_call | solution.py:507
  30.6 0.8 %collective-permute-start.8 = (bf16[2,3,16,512]{3,2,1,0:T(8,128)(2,1)S(1)}, bf16[2,3,16,512]{3,2,1,0:T(8,128)(2,1)S(1)}, u32[]{:S(2)}, u32[]{:S(2)}) collective-permute-start(bf16[2,3,16,512]{3,2,1,0:T(8,128)(2,1)S(1)} %get-tuple-element.122), channel_id=1, source_target_pairs={{0,12},{1,13},{2,14},{3,15},{4,0},{5,1},{6,2},{7,3},{8,4},{9,5},{1... | collective-permute-start | bytes 294920 | tf_op jit(solution)/shard_map/ppermute | solution.py:28
  31.3 1.3 %collective-permute-start.9 = (bf16[2,3,16,512]{3,2,1,0:T(8,128)(2,1)S(1)}, bf16[2,3,16,512]{3,2,1,0:T(8,128)(2,1)S(1)}, u32[]{:S(2)}, u32[]{:S(2)}) collective-permute-start(bf16[2,3,16,512]{3,2,1,0:T(8,128)(2,1)S(1)} %get-tuple-element.123), channel_id=1, source_target_pairs={{0,4},{1,5},{2,6},{3,7},{4,8},{5,9},{6,10},{7,11},{8,12},{9,13},{1... | collective-permute-start | bytes 294920 | tf_op jit(solution)/shard_map/ppermute | solution.py:28
  32.7 3.8 %collective-permute-done.7.y_in = bf16[4,32,1536]{2,1,0:T(8,128)(2,1)S(1)} collective-permute-done((bf16[4,32,1536]{2,1,0:T(8,128)(2,1)S(1)}, bf16[4,32,1536]{2,1,0:T(8,128)(2,1)S(1)}, u32[]{:S(2)}, u32[]{:S(2)}) %collective-permute-start.7) | collective-permute-done | bytes 393248 | tf_op jit(solution)/shard_map/ppermute | solution.py:616
  36.4 0.1 shard_map.114
  36.6 0.1 collective-permute-start.14
  36.6 0.0 collective-permute-done.8.plus_ref
  36.6 2.1 %collective-permute-done.9.minus_ref = bf16[2,3,16,512]{3,2,1,0:T(8,128)(2,1)S(1)} collective-permute-done((bf16[2,3,16,512]{3,2,1,0:T(8,128)(2,1)S(1)}, bf16[2,3,16,512]{3,2,1,0:T(8,128)(2,1)S(1)}, u32[]{:S(2)}, u32[]{:S(2)}) %collective-permute-start.9) | collective-permute-done | bytes 98336 | tf_op jit(solution)/shard_map/ppermute | solution.py:28
  38.8 0.0 collective-permute-done.11.refs_4_
  38.8 0.0 collective-permute-done.10.refs_2_
  38.8 0.0 copy-start
  38.8 0.1 shard_map.116
  38.9 2.8 %collective-permute-done.14.in_a = bf16[18,32,128]{2,1,0:T(8,128)(2,1)S(1)} collective-permute-done((bf16[18,32,128]{2,1,0:T(8,128)(2,1)S(1)}, bf16[18,32,128]{2,1,0:T(8,128)(2,1)S(1)}, u32[]{:S(2)}, u32[]{:S(2)}) %collective-permute-start.14) | collective-permute-done | bytes 147488 | tf_op jit(solution)/shard_map/ppermute | solution.py:633
  41.8 0.8 %collective-permute-start.16 = (bf16[16,32,128]{2,1,0:T(8,128)(2,1)S(1)}, bf16[16,32,128]{2,1,0:T(8,128)(2,1)S(1)}, u32[]{:S(2)}, u32[]{:S(2)}) collective-permute-start(bf16[16,32,128]{2,1,0:T(8,128)(2,1)S(1)} %get-tuple-element.134), channel_id=1, source_target_pairs={{0,12},{1,13},{2,14},{3,15},{4,8},{5,9},{6,10},{7,11},{8,4},{9,5},... | collective-permute-start | bytes 393224 | tf_op jit(solution)/shard_map/ppermute | solution.py:633
  42.6 1.7 %collective-permute-start.12 = (bf16[2,3,16,512]{3,2,1,0:T(8,128)(2,1)S(1)}, bf16[2,3,16,512]{3,2,1,0:T(8,128)(2,1)S(1)}, u32[]{:S(2)}, u32[]{:S(2)}) collective-permute-start(bf16[2,3,16,512]{3,2,1,0:T(8,128)(2,1)S(1)} %get-tuple-element.129), channel_id=1, source_target_pairs={{0,15},{1,2},{2,1},{3,4},{4,3},{5,6},{6,5},{7,8},{8,7},{9,10},{10,... | collective-permute-start | bytes 294920 | tf_op jit(solution)/shard_map/ppermute | solution.py:43
  44.2 0.0 collective-permute-start.13
  44.2 0.0 collective-permute-start.15
  44.2 2.8 %collective-permute-start.17 = (bf16[7,32,128]{2,1,0:T(8,128)(2,1)S(1)}, bf16[7,32,128]{2,1,0:T(8,128)(2,1)S(1)}, u32[]{:S(2)}, u32[]{:S(2)}) collective-permute-start(bf16[7,32,128]{2,1,0:T(8,128)(2,1)S(1)} %get-tuple-element.135), channel_id=1, source_target_pairs={{0,8},{1,9},{2,10},{3,11},{4,12},{5,13},{6,14},{7,15},{8,0},{9,1},... | collective-permute-start | bytes 172040 | tf_op jit(solution)/shard_map/ppermute | solution.py:633
  47.0 2.9 %collective-permute-done.12.second_in = bf16[2,3,16,512]{3,2,1,0:T(8,128)(2,1)S(1)} collective-permute-done((bf16[2,3,16,512]{3,2,1,0:T(8,128)(2,1)S(1)}, bf16[2,3,16,512]{3,2,1,0:T(8,128)(2,1)S(1)}, u32[]{:S(2)}, u32[]{:S(2)}) %collective-permute-start.12) | collective-permute-done | bytes 98336 | tf_op jit(solution)/shard_map/ppermute | solution.py:43
  49.9 1.0 %shard_map.117.after_ref = bf16[2,128,512]{2,1,0:T(8,128)(2,1)} custom-call(s32[1]{0:T(128)} %bitcast.me_ref, bf16[7,32,128]{2,1,0:T(8,128)(2,1)S(1)} %get-tuple-element.128.after_ref, bf16[2,3,16,512]{3,2,1,0:T(8,128)(2,1)S(1)} %collective-permute-done.12.second_in, bf16[2,3,16,512]{3,2,1,0:T(8,128)(2,1)S(1)} %collective-permute-done.13.first_in, ...), custom_call_target="tpu_custom_call" | custom-call | flops 1000000 | bytes 10000 | tf_op jit(solution)/shard_map/pallas_call | solution.py:507
  50.9 0.0 collective-permute-done.15.refs_0_
  50.9 0.4 collective-permute-done.17.refs_2_
  51.3 0.0 collective-permute-done.16.refs_1_
  51.3 0.7 %shard_map.119 = f32[32,2048]{1,0:T(8,128)} custom-call(bf16[2,128,512]{2,1,0:T(8,128)(2,1)} %shard_map.117.after_ref, f32[32,1152]{1,0:T(8,128)S(1)} %get-tuple-element.132.own_a, f32[32,896]{1,0:T(8,128)S(1)} %get-tuple-element.133.own_b, bf16[7,32,128]{2,1,0:T(8,128)(2,1)S(1)} %collective-permute-done.15.refs_0_, ...), custom_call_target="tpu_custom_call" | custom-call | flops 1000000 | bytes 10000 | tf_op jit(solution)/shard_map/pallas_call | solution.py:507
  (7 shorter events, 0.1 us)
Async XLA Ops:
  1.8 8.6 %collective-permute-start = (bf16[2,3,16,512]{3,2,1,0:T(8,128)(2,1)S(1)}, bf16[2,3,16,512]{3,2,1,0:T(8,128)(2,1)S(1)}, u32[]{:S(2)}, u32[]{:S(2)}) collective-permute-start(bf16[2,3,16,512]{3,2,1,0:T(8,128)(2,1)S(1)} %get-tuple-element.74), channel_id=1, source_target_pairs={{0,4},{1,5},{2,6},{3,7},{4,8},{5,9},{6,10},{7,11},{8,12},{9,13},{1... | collective-permute-start | bytes 294920 | tf_op jit(solution)/shard_map/ppermute | solution.py:28
  4.9 6.4 %collective-permute-start.1 = (bf16[2,3,16,512]{3,2,1,0:T(8,128)(2,1)S(1)}, bf16[2,3,16,512]{3,2,1,0:T(8,128)(2,1)S(1)}, u32[]{:S(2)}, u32[]{:S(2)}) collective-permute-start(bf16[2,3,16,512]{3,2,1,0:T(8,128)(2,1)S(1)} %get-tuple-element.75), channel_id=1, source_target_pairs={{0,12},{1,13},{2,14},{3,15},{4,0},{5,1},{6,2},{7,3},{8,4},{9,5},{1... | collective-permute-start | bytes 294920 | tf_op jit(solution)/shard_map/ppermute | solution.py:28
  11.3 6.8 %collective-permute-start.2 = (bf16[2,3,16,512]{3,2,1,0:T(8,128)(2,1)S(1)}, bf16[2,3,16,512]{3,2,1,0:T(8,128)(2,1)S(1)}, u32[]{:S(2)}, u32[]{:S(2)}) collective-permute-start(bf16[2,3,16,512]{3,2,1,0:T(8,128)(2,1)S(1)} %get-tuple-element.76.after_ref), channel_id=1, source_target_pairs={{0,15},{1,2},{2,1},{3,4},{4,3},{5,6},{6,5},{7,8},{8,7},{9,10},{10,... | collective-permute-start | bytes 294920 | tf_op jit(solution)/shard_map/ppermute | solution.py:43
  13.0 5.1 %collective-permute-start.3 = (bf16[2,3,16,512]{3,2,1,0:T(8,128)(2,1)S(1)}, bf16[2,3,16,512]{3,2,1,0:T(8,128)(2,1)S(1)}, u32[]{:S(2)}, u32[]{:S(2)}) collective-permute-start(bf16[2,3,16,512]{3,2,1,0:T(8,128)(2,1)S(1)} %get-tuple-element.77), channel_id=1, source_target_pairs={{0,1},{1,0},{2,3},{3,2},{4,5},{5,4},{6,7},{7,6},{8,9},{9,8},{10,11... | collective-permute-start | bytes 294920 | tf_op jit(solution)/shard_map/ppermute | solution.py:44
  22.5 1.8 %collective-permute-start.6 = (bf16[4,32,1536]{2,1,0:T(8,128)(2,1)S(1)}, bf16[4,32,1536]{2,1,0:T(8,128)(2,1)S(1)}, u32[]{:S(2)}, u32[]{:S(2)}) collective-permute-start(bf16[4,32,1536]{2,1,0:T(8,128)(2,1)S(1)} %get-tuple-element.118), channel_id=1, source_target_pairs={{0,1},{1,0},{2,3},{3,2},{4,5},{5,4},{6,7},{7,6},{8,9},{9,8},{10,11... | collective-permute-start | bytes 1179656 | tf_op jit(solution)/shard_map/ppermute | solution.py:609
  22.6 8.7 %collective-permute-start.5 = (bf16[4,32,1536]{2,1,0:T(8,128)(2,1)S(1)}, bf16[4,32,1536]{2,1,0:T(8,128)(2,1)S(1)}, u32[]{:S(2)}, u32[]{:S(2)}) collective-permute-start(bf16[4,32,1536]{2,1,0:T(8,128)(2,1)S(1)} %get-tuple-element.116), channel_id=1, source_target_pairs={{0,1},{1,0},{2,3},{3,2},{4,5},{5,4},{6,7},{7,6},{8,9},{9,8},{10,11... | collective-permute-start | bytes 1179656 | tf_op jit(solution)/shard_map/ppermute | solution.py:609
  24.4 12.0 %collective-permute-start.7 = (bf16[4,32,1536]{2,1,0:T(8,128)(2,1)S(1)}, bf16[4,32,1536]{2,1,0:T(8,128)(2,1)S(1)}, u32[]{:S(2)}, u32[]{:S(2)}) collective-permute-start(bf16[4,32,1536]{2,1,0:T(8,128)(2,1)S(1)} %add_convert_fusion), channel_id=1, source_target_pairs={{0,2},{1,3},{2,0},{3,1},{4,6},{5,7},{6,4},{7,5},{8,10},{9,11},{10,... | collective-permute-start | bytes 1179656 | tf_op jit(solution)/shard_map/ppermute | solution.py:616
  26.0 1.4 %collective-permute-start.4 = (bf16[4,32,512]{2,1,0:T(8,128)(2,1)S(1)}, bf16[4,32,512]{2,1,0:T(8,128)(2,1)S(1)}, u32[]{:S(2)}, u32[]{:S(2)}) collective-permute-start(bf16[4,32,512]{2,1,0:T(8,128)(2,1)S(1)} %get-tuple-element.91), channel_id=1, source_target_pairs={{0,1},{1,0},{2,3},{3,2},{4,5},{5,4},{6,7},{7,6},{8,9},{9,8},{10,11... | collective-permute-start | bytes 393224 | tf_op jit(solution)/shard_map/ppermute | solution.py:609
  26.2 12.6 %collective-permute-start.11 = (bf16[4,32,512]{2,1,0:T(8,128)(2,1)S(1)}, bf16[4,32,512]{2,1,0:T(8,128)(2,1)S(1)}, u32[]{:S(2)}, u32[]{:S(2)}) collective-permute-start(bf16[4,32,512]{2,1,0:T(8,128)(2,1)S(1)} %get-tuple-element.127), channel_id=1, source_target_pairs={{0,1},{1,0},{2,3},{3,2},{4,5},{5,4},{6,7},{7,6},{8,9},{9,8},{10,11... | collective-permute-start | bytes 393224 | tf_op jit(solution)/shard_map/ppermute | solution.py:609
  27.5 11.3 %collective-permute-start.10 = (bf16[4,32,512]{2,1,0:T(8,128)(2,1)S(1)}, bf16[4,32,512]{2,1,0:T(8,128)(2,1)S(1)}, u32[]{:S(2)}, u32[]{:S(2)}) collective-permute-start(bf16[4,32,512]{2,1,0:T(8,128)(2,1)S(1)} %shard_map.111.refs_0_), channel_id=1, source_target_pairs={{0,2},{1,3},{2,0},{3,1},{4,6},{5,7},{6,4},{7,5},{8,10},{9,11},{10,... | collective-permute-start | bytes 393224 | tf_op jit(solution)/shard_map/ppermute | solution.py:623
  30.6 6.1 %collective-permute-start.8 = (bf16[2,3,16,512]{3,2,1,0:T(8,128)(2,1)S(1)}, bf16[2,3,16,512]{3,2,1,0:T(8,128)(2,1)S(1)}, u32[]{:S(2)}, u32[]{:S(2)}) collective-permute-start(bf16[2,3,16,512]{3,2,1,0:T(8,128)(2,1)S(1)} %get-tuple-element.122), channel_id=1, source_target_pairs={{0,12},{1,13},{2,14},{3,15},{4,0},{5,1},{6,2},{7,3},{8,4},{9,5},{1... | collective-permute-start | bytes 294920 | tf_op jit(solution)/shard_map/ppermute | solution.py:28
  31.3 7.4 %collective-permute-start.9 = (bf16[2,3,16,512]{3,2,1,0:T(8,128)(2,1)S(1)}, bf16[2,3,16,512]{3,2,1,0:T(8,128)(2,1)S(1)}, u32[]{:S(2)}, u32[]{:S(2)}) collective-permute-start(bf16[2,3,16,512]{3,2,1,0:T(8,128)(2,1)S(1)} %get-tuple-element.123), channel_id=1, source_target_pairs={{0,4},{1,5},{2,6},{3,7},{4,8},{5,9},{6,10},{7,11},{8,12},{9,13},{1... | collective-permute-start | bytes 294920 | tf_op jit(solution)/shard_map/ppermute | solution.py:28
  36.6 5.2 %collective-permute-start.14 = (bf16[18,32,128]{2,1,0:T(8,128)(2,1)S(1)}, bf16[18,32,128]{2,1,0:T(8,128)(2,1)S(1)}, u32[]{:S(2)}, u32[]{:S(2)}) collective-permute-start(bf16[18,32,128]{2,1,0:T(8,128)(2,1)S(1)} %get-tuple-element.119.after_ref), channel_id=1, source_target_pairs={{0,4},{1,5},{2,6},{3,7},{4,0},{5,1},{6,2},{7,3},{8,12},{9,13},{10,... | collective-permute-start | bytes 442376 | tf_op jit(solution)/shard_map/ppermute | solution.py:633
  38.8 11.1 %copy-start = (s32[1,8,16]{2,1,0:T(8,128)S(1)}, s32[1,8,16]{2,1,0:T(8,128)}, u32[]{:S(2)}) copy-start(s32[1,8,16]{2,1,0:T(8,128)} %send_ref.1) | copy-start | bytes 1540
  41.8 9.5 %collective-permute-start.16 = (bf16[16,32,128]{2,1,0:T(8,128)(2,1)S(1)}, bf16[16,32,128]{2,1,0:T(8,128)(2,1)S(1)}, u32[]{:S(2)}, u32[]{:S(2)}) collective-permute-start(bf16[16,32,128]{2,1,0:T(8,128)(2,1)S(1)} %get-tuple-element.134), channel_id=1, source_target_pairs={{0,12},{1,13},{2,14},{3,15},{4,8},{5,9},{6,10},{7,11},{8,4},{9,5},... | collective-permute-start | bytes 393224 | tf_op jit(solution)/shard_map/ppermute | solution.py:633
  42.6 7.3 %collective-permute-start.12 = (bf16[2,3,16,512]{3,2,1,0:T(8,128)(2,1)S(1)}, bf16[2,3,16,512]{3,2,1,0:T(8,128)(2,1)S(1)}, u32[]{:S(2)}, u32[]{:S(2)}) collective-permute-start(bf16[2,3,16,512]{3,2,1,0:T(8,128)(2,1)S(1)} %get-tuple-element.129), channel_id=1, source_target_pairs={{0,15},{1,2},{2,1},{3,4},{4,3},{5,6},{6,5},{7,8},{8,7},{9,10},{10,... | collective-permute-start | bytes 294920 | tf_op jit(solution)/shard_map/ppermute | solution.py:43
  44.2 5.6 %collective-permute-start.13 = (bf16[2,3,16,512]{3,2,1,0:T(8,128)(2,1)S(1)}, bf16[2,3,16,512]{3,2,1,0:T(8,128)(2,1)S(1)}, u32[]{:S(2)}, u32[]{:S(2)}) collective-permute-start(bf16[2,3,16,512]{3,2,1,0:T(8,128)(2,1)S(1)} %get-tuple-element.124.refs_0_), channel_id=1, source_target_pairs={{0,1},{1,0},{2,3},{3,2},{4,5},{5,4},{6,7},{7,6},{8,9},{9,8},{10,11... | collective-permute-start | bytes 294920 | tf_op jit(solution)/shard_map/ppermute | solution.py:44
  44.2 6.6 %collective-permute-start.15 = (bf16[7,32,128]{2,1,0:T(8,128)(2,1)S(1)}, bf16[7,32,128]{2,1,0:T(8,128)(2,1)S(1)}, u32[]{:S(2)}, u32[]{:S(2)}) collective-permute-start(bf16[7,32,128]{2,1,0:T(8,128)(2,1)S(1)} %get-tuple-element.128.after_ref), channel_id=1, source_target_pairs={{0,4},{1,5},{2,6},{3,7},{4,0},{5,1},{6,2},{7,3},{8,12},{9,13},{10,... | collective-permute-start | bytes 172040 | tf_op jit(solution)/shard_map/ppermute | solution.py:633
  44.2 7.0 %collective-permute-start.17 = (bf16[7,32,128]{2,1,0:T(8,128)(2,1)S(1)}, bf16[7,32,128]{2,1,0:T(8,128)(2,1)S(1)}, u32[]{:S(2)}, u32[]{:S(2)}) collective-permute-start(bf16[7,32,128]{2,1,0:T(8,128)(2,1)S(1)} %get-tuple-element.135), channel_id=1, source_target_pairs={{0,8},{1,9},{2,10},{3,11},{4,12},{5,13},{6,14},{7,15},{8,0},{9,1},... | collective-permute-start | bytes 172040 | tf_op jit(solution)/shard_map/ppermute | solution.py:633

commit v13 on v12

--- a/solution.py
+++ b/solution.py
@@ -609,15 +609,19 @@
         arrived = [lax.ppermute(shard, "patch", flip) for shard in sent]
         return outs[0], outs[1], arrived[0], arrived[-1]
 
-    half = groups - 1
+    half = groups // 2
     wide = 384 * half
     own_a, other, core_other, core_own = attention((), range(half), False)
     y_sent = (other + core_other.astype(f32)).astype(bf16)
     y_a = lax.ppermute(y_sent, "patch", flop)
-    later = [attention((), range(half, groups), False)]
+    later = []
+    for g in range(half, groups):
+        last = g == groups - 1
+        later.append(attention((y_sent,) if last else (), range(g, g + 1), not last))
     own_b, other_b, core_other_b, core_own_b = zip(*later)
     (y_sent,) = call(
-        functools.partial(pack_kernel, len(later)), [(other_b[0].shape, bf16)],
+        functools.partial(pack_kernel, len(later)),
+        [((planes, rows, 512 * (groups - half)), bf16)],
         (*other_b, *core_other_b),
     )
     y_b = lax.ppermute(y_sent, "patch", flop)

time: 52.2 us -> 53.9 us (1.033)
  starting transfers between devices: 17.5 us -> 20.8 us
  waiting for transfers between devices: 18 us -> 16 us
    ppermute x4, waiting for transfers between devices: 3.75 us -> 8.22 us  [shifted(): lax.ppermute(shard, 'patch', [(i, (i + by) % count) for i in range(count)])]
    ppermute x1, waiting for transfers between devices: 3.75 us -> 0.64 us  [body(): y_a = lax.ppermute(y_sent, 'patch', flop)]
    ppermute x2, waiting for transfers between devices: 5.16 us -> 3.66 us  [swap(): later = lax.ppermute(pair[1], 'patch', second)]
    ppermute x4 -> x5, waiting for transfers between devices: 2.05 us -> 0.87 us  [attention(): arrived = [lax.ppermute(shard, 'patch', flip) for shard in sent]]
    ppermute x2, starting transfers between devices: 0.04 us -> 1.19 us  [swap(): return [lax.ppermute(pair[0], 'patch', first), later]]
    ppermute x2, starting transfers between devices: 3.34 us -> 4.22 us  [swap(): later = lax.ppermute(pair[1], 'patch', second)]
    ppermute x4, starting transfers between devices: 3.61 us -> 4.48 us  [exchange(): return lax.ppermute(sent, 'patch', along_z(count, distance))]
    ppermute x4, waiting for transfers between devices: 3.23 us -> 2.55 us  [exchange(): return lax.ppermute(sent, 'patch', along_z(count, distance))]
  transfers between devices with their start and end apart: 18 -> 19, of which waited for: 10 -> 9; matrix products, arithmetic and copies ran while one was open for 0% -> 0% of each run, Pallas kernels for 18% -> 20%
where the time goes in v13:
time: 53.9 us; the launch traced here: 53.7 us
  starting transfers between devices  20.8 us (39%)
  Pallas kernels  16.1 us (30%)
  waiting for transfers between devices  16 us (30%)
  between operations  0.8 us (1%)
    pallas_call x17, Pallas kernels, call(): pl.pallas_call(kernel, out_shape=[jax.ShapeDtypeStruct(*o) if final else...  16.1 us
    ppermute x4, waiting for transfers between devices, shifted(): lax.ppermute(shard, 'patch', [(i, (i + by) % count) for i in range(count)])  8.22 us
    ppermute x4, starting transfers between devices, shifted(): lax.ppermute(shard, 'patch', [(i, (i + by) % count) for i in range(count)])  7.48 us
    ppermute x4, starting transfers between devices, exchange(): return lax.ppermute(sent, 'patch', along_z(count, distance))  4.48 us
    ppermute x2, starting transfers between devices, swap(): later = lax.ppermute(pair[1], 'patch', second)  4.22 us
    ppermute x2, waiting for transfers between devices, swap(): later = lax.ppermute(pair[1], 'patch', second)  3.66 us
    ppermute x4, waiting for transfers between devices, exchange(): return lax.ppermute(sent, 'patch', along_z(count, distance))  2.55 us
    ppermute x1, starting transfers between devices, body(): y_b = lax.ppermute(y_sent, 'patch', flop)  2 us
  transfers between devices with their start and end apart: 19, of which 9 were waited for; matrix products, arithmetic and copies ran while one was open for 0% of the time, Pallas kernels for 20%

profile of v13, /device:TPU:0, one launch (start us, length us, event | category | flops | bytes accessed | tf_op | source)
XLA Modules:
  0.0 53.7 jit_solution(16023936643924443771)
XLA Ops:
  0.6 1.2 %shard_map.104 = (bf16[2,3,16,512]{3,2,1,0:T(8,128)(2,1)S(1)}, bf16[2,3,16,512]{3,2,1,0:T(8,128)(2,1)S(1)}, bf16[2,1,16,512]{3,2,1,0:T(8,128)(2,1)S(1)}, bf16[2,...) custom-call(s32[1,8,16]{2,1,0:T(8,128)} %send_ref.1, bf16[2,128,512]{2,1,0:T(8,128)(2,1)} %x_hbm.1), custom_call_target="tpu_custom_call" | custom-call | flops 1000000 | bytes 10000 | tf_op jit(solution)/shard_map/pallas_call | solution.py:507
  1.8 3.1 %collective-permute-start = (bf16[2,3,16,512]{3,2,1,0:T(8,128)(2,1)S(1)}, bf16[2,3,16,512]{3,2,1,0:T(8,128)(2,1)S(1)}, u32[]{:S(2)}, u32[]{:S(2)}) collective-permute-start(bf16[2,3,16,512]{3,2,1,0:T(8,128)(2,1)S(1)} %get-tuple-element.77), channel_id=1, source_target_pairs={{0,4},{1,5},{2,6},{3,7},{4,8},{5,9},{6,10},{7,11},{8,12},{9,13},{1... | collective-permute-start | bytes 294920 | tf_op jit(solution)/shard_map/ppermute | solution.py:28
  4.9 2.1 %collective-permute-start.1 = (bf16[2,3,16,512]{3,2,1,0:T(8,128)(2,1)S(1)}, bf16[2,3,16,512]{3,2,1,0:T(8,128)(2,1)S(1)}, u32[]{:S(2)}, u32[]{:S(2)}) collective-permute-start(bf16[2,3,16,512]{3,2,1,0:T(8,128)(2,1)S(1)} %get-tuple-element.78), channel_id=1, source_target_pairs={{0,12},{1,13},{2,14},{3,15},{4,0},{5,1},{6,2},{7,3},{8,4},{9,5},{1... | collective-permute-start | bytes 294920 | tf_op jit(solution)/shard_map/ppermute | solution.py:28
  7.0 2.6 %shard_map.105 = (bf16[8,2,128,128]{3,2,1,0:T(8,128)(2,1)S(1)}, bf16[8,2,128,128]{3,2,1,0:T(8,128)(2,1)S(1)}, bf16[8,2,128,128]{3,2,1,0:T(8,128)(2,1)S(1)}, bf16...) custom-call(bf16[2,1,16,512]{3,2,1,0:T(8,128)(2,1)S(1)} %get-tuple-e, ...), custom_call_target="tpu_custom_call" | custom-call | flops 1000000 | bytes 10000 | tf_op jit(solution)/shard_map/pallas_call | solution.py:507
  9.7 0.8 %collective-permute-done.plus_ref = bf16[2,3,16,512]{3,2,1,0:T(8,128)(2,1)S(1)} collective-permute-done((bf16[2,3,16,512]{3,2,1,0:T(8,128)(2,1)S(1)}, bf16[2,3,16,512]{3,2,1,0:T(8,128)(2,1)S(1)}, u32[]{:S(2)}, u32[]{:S(2)}) %collective-permute-start) | collective-permute-done | bytes 98336 | tf_op jit(solution)/shard_map/ppermute | solution.py:28
  10.4 0.8 %collective-permute-done.1.minus_ref = bf16[2,3,16,512]{3,2,1,0:T(8,128)(2,1)S(1)} collective-permute-done((bf16[2,3,16,512]{3,2,1,0:T(8,128)(2,1)S(1)}, bf16[2,3,16,512]{3,2,1,0:T(8,128)(2,1)S(1)}, u32[]{:S(2)}, u32[]{:S(2)}) %collective-permute-start.1) | collective-permute-done | bytes 98336 | tf_op jit(solution)/shard_map/ppermute | solution.py:28
  11.3 0.1 collective-permute-start.3
  11.4 3.4 %collective-permute-start.2 = (bf16[2,3,16,512]{3,2,1,0:T(8,128)(2,1)S(1)}, bf16[2,3,16,512]{3,2,1,0:T(8,128)(2,1)S(1)}, u32[]{:S(2)}, u32[]{:S(2)}) collective-permute-start(bf16[2,3,16,512]{3,2,1,0:T(8,128)(2,1)S(1)} %get-tuple-element.79.after_ref), channel_id=1, source_target_pairs={{0,15},{1,2},{2,1},{3,4},{4,3},{5,6},{6,5},{7,8},{8,7},{9,10},{10,... | collective-permute-start | bytes 294920 | tf_op jit(solution)/shard_map/ppermute | solution.py:43
  14.8 1.4 %shard_map.108.refs_4_.refs_8_.refs_5_ = f32[256,128]{1,0:T(8,128)S(1)} custom-call(bf16[2,3,16,512]{3,2,1,0:T(8,128)(2,1)S(1)} %get-tuple-element.79.after_ref, s32[128,256]{1,0:T(8,128)S(1)} %get-tuple-element.87.neigh_ref, s32[1,128]{1,0:T(1,128)S(1)} %get-tuple-element.88.count_ref), custom_call_target="tpu_custom_call" | custom-call | flops 1000000 | bytes 10000 | tf_op jit(solution)/shard_map/pallas_call | solution.py:507
  16.3 1.3 %shard_map.109 = (f32[3,2,128,512]{3,2,1,0:T(8,128)S(1)}, f32[2,2,8,512]{3,2,1,0:T(8,128)S(1)}, f32[3,2,128,512]{3,2,1,0:T(8,128)S(1)}, f32[2,2,8,512]{3,2,1,0:T...) custom-call(bf16[8,2,128,128]{3,2,1,0:T(8,128)(2,1)S(1)} %get-tuple-, ...), custom_call_target="tpu_custom_call" | custom-call | flops 1000000 | bytes 10000 | tf_op jit(solution)/shard_map/pallas_call | solution.py:507
  17.6 0.0 collective-permute-done.3.first_in
  17.6 0.5 %collective-permute-done.2.second_in = bf16[2,3,16,512]{3,2,1,0:T(8,128)(2,1)S(1)} collective-permute-done((bf16[2,3,16,512]{3,2,1,0:T(8,128)(2,1)S(1)}, bf16[2,3,16,512]{3,2,1,0:T(8,128)(2,1)S(1)}, u32[]{:S(2)}, u32[]{:S(2)}) %collective-permute-start.2) | collective-permute-done | bytes 98336 | tf_op jit(solution)/shard_map/ppermute | solution.py:43
  18.2 0.6 %shard_map.107 = (bf16[4,2,128,128]{3,2,1,0:T(8,128)(2,1)S(1)}, bf16[4,2,128,128]{3,2,1,0:T(8,128)(2,1)S(1)}, bf16[4,2,128,128]{3,2,1,0:T(8,128)(2,1)S(1)}, bf16...) custom-call(s32[1]{0:T(128)} %bitcast.me_ref, bf16[2,3,16,512]{3,2,1,0:T(8,128)(2,1)S(1)} %collective-permute-done.2.second_in, ...), custom_call_target="tpu_custom_call" | custom-call | flops 1000000 | bytes 10000 | tf_op jit(solution)/shard_map/pallas_call | solution.py:507
  18.8 2.7 %shard_map.111 = (f32[4,32,1024]{2,1,0:T(8,128)S(1)}, f32[4,32,1024]{2,1,0:T(8,128)S(1)}, bf16[4,32,1024]{2,1,0:T(8,128)(2,1)S(1)}, bf16[4,32,1024]{2,1,0:T(8,12...) custom-call(s32[1]{0:T(128)} %bitcast.me_ref, ...), custom_call_target="tpu_custom_call" | custom-call | flops 1000000 | bytes 10000 | tf_op jit(solution)/shard_map/pallas_call | solution.py:507
  21.5 0.1 collective-permute-start.4
  21.6 1.5 %shard_map.110 = (f32[4,32,512]{2,1,0:T(8,128)S(1)}, f32[4,32,512]{2,1,0:T(8,128)S(1)}, bf16[2,4,32,512]{3,2,1,0:T(8,128)(2,1)S(1)}, bf16[2,128,128]{2,1,0:T(8,1...) custom-call(s32[1]{0:T(128)} %bitcast.me_ref, ...), custom_call_target="tpu_custom_call" | custom-call | flops 1000000 | bytes 10000 | tf_op jit(solution)/shard_map/pallas_call | solution.py:507
  23.1 0.6 %collective-permute-start.5 = (bf16[2,4,32,512]{3,2,1,0:T(8,128)(2,1)S(1)}, bf16[2,4,32,512]{3,2,1,0:T(8,128)(2,1)S(1)}, u32[]{:S(2)}, u32[]{:S(2)}) collective-permute-start(bf16[2,4,32,512]{3,2,1,0:T(8,128)(2,1)S(1)} %get-tuple-element.106), channel_id=1, source_target_pairs={{0,1},{1,0},{2,3},{3,2},{4,5},{5,4},{6,7},{7,6},{8,9},{9,8},{10,11... | collective-permute-start | bytes 786440 | tf_op jit(solution)/shard_map/ppermute | solution.py:609
  23.7 0.1 collective-permute-start.7
  23.8 0.0 collective-permute-done.4
  23.8 0.1 add_convert_fusion.refs_0_
  23.8 0.1 collective-permute-start.8
  24.0 1.5 %shard_map.112 = (f32[4,32,512]{2,1,0:T(8,128)S(1)}, f32[4,32,512]{2,1,0:T(8,128)S(1)}, bf16[4,32,512]{2,1,0:T(8,128)(2,1)S(1)}, bf16[4,32,512]{2,1,0:T(8,128)(2...) custom-call(s32[1]{0:T(128)} %bitcast.me_ref, ...), custom_call_target="tpu_custom_call" | custom-call | flops 1000000 | bytes 10000 | tf_op jit(solution)/shard_map/pallas_call | solution.py:507
  25.5 0.5 collective-permute-start.6
  26.0 0.1 collective-permute-start.12
  26.1 0.9 %collective-permute-done.6.refs_3_ = bf16[4,32,512]{2,1,0:T(8,128)(2,1)S(1)} collective-permute-done((bf16[4,32,512]{2,1,0:T(8,128)(2,1)S(1)}, bf16[4,32,512]{2,1,0:T(8,128)(2,1)S(1)}, u32[]{:S(2)}, u32[]{:S(2)}) %collective-permute-start.6) | collective-permute-done | bytes 131104 | tf_op jit(solution)/shard_map/ppermute | solution.py:609
  27.0 0.1 shard_map.113.refs_0_
  27.0 2.0 %collective-permute-start.11 = (bf16[4,32,1024]{2,1,0:T(8,128)(2,1)S(1)}, bf16[4,32,1024]{2,1,0:T(8,128)(2,1)S(1)}, u32[]{:S(2)}, u32[]{:S(2)}) collective-permute-start(bf16[4,32,1024]{2,1,0:T(8,128)(2,1)S(1)} %shard_map.113.refs_0_), channel_id=1, source_target_pairs={{0,2},{1,3},{2,0},{3,1},{4,6},{5,7},{6,4},{7,5},{8,10},{9,11},{10,... | collective-permute-start | bytes 786440 | tf_op jit(solution)/shard_map/ppermute | solution.py:627
  29.0 1.0 %shard_map.114 = (f32[2,128,512]{2,1,0:T(8,128)S(1)}, bf16[2,3,16,512]{3,2,1,0:T(8,128)(2,1)S(1)}, bf16[2,3,16,512]{3,2,1,0:T(8,128)(2,1)S(1)}, bf16[2,1,16,512]...) custom-call(bf16[4,32,1024]{2,1,0:T(8,128)(2,1)S(1)} %shard_map.113.refs_0_, ...), custom_call_target="tpu_custom_call" | custom-call | flops 1000000 | bytes 10000 | tf_op jit(solution)/shard_map/pallas_call | solution.py:507
  30.0 2.3 %collective-permute-start.9 = (bf16[2,3,16,512]{3,2,1,0:T(8,128)(2,1)S(1)}, bf16[2,3,16,512]{3,2,1,0:T(8,128)(2,1)S(1)}, u32[]{:S(2)}, u32[]{:S(2)}) collective-permute-start(bf16[2,3,16,512]{3,2,1,0:T(8,128)(2,1)S(1)} %get-tuple-element.127), channel_id=1, source_target_pairs={{0,12},{1,13},{2,14},{3,15},{4,0},{5,1},{6,2},{7,3},{8,4},{9,5},{1... | collective-permute-start | bytes 294920 | tf_op jit(solution)/shard_map/ppermute | solution.py:28
  32.4 0.6 %collective-permute-done.8.y_in = bf16[4,32,1024]{2,1,0:T(8,128)(2,1)S(1)} collective-permute-done((bf16[4,32,1024]{2,1,0:T(8,128)(2,1)S(1)}, bf16[4,32,1024]{2,1,0:T(8,128)(2,1)S(1)}, u32[]{:S(2)}, u32[]{:S(2)}) %collective-permute-start.8) | collective-permute-done | bytes 262176 | tf_op jit(solution)/shard_map/ppermute | solution.py:616
  33.0 0.1 shard_map.115
  33.1 0.1 collective-permute-start.15
  33.2 2.4 %collective-permute-done.9.plus_ref = bf16[2,3,16,512]{3,2,1,0:T(8,128)(2,1)S(1)} collective-permute-done((bf16[2,3,16,512]{3,2,1,0:T(8,128)(2,1)S(1)}, bf16[2,3,16,512]{3,2,1,0:T(8,128)(2,1)S(1)}, u32[]{:S(2)}, u32[]{:S(2)}) %collective-permute-start.9) | collective-permute-done | bytes 98336 | tf_op jit(solution)/shard_map/ppermute | solution.py:28
  35.6 4.2 %collective-permute-done.10.minus_ref = bf16[2,3,16,512]{3,2,1,0:T(8,128)(2,1)S(1)} collective-permute-done((bf16[2,3,16,512]{3,2,1,0:T(8,128)(2,1)S(1)}, bf16[2,3,16,512]{3,2,1,0:T(8,128)(2,1)S(1)}, u32[]{:S(2)}, u32[]{:S(2)}) %collective-permute-start.10) | collective-permute-done | bytes 98336 | tf_op jit(solution)/shard_map/ppermute | solution.py:28
  39.8 0.0 copy-start
  39.8 0.1 shard_map.117
  40.0 0.0 collective-permute-done.15.in_a
  40.0 1.6 %collective-permute-start.17 = (bf16[16,32,128]{2,1,0:T(8,128)(2,1)S(1)}, bf16[16,32,128]{2,1,0:T(8,128)(2,1)S(1)}, u32[]{:S(2)}, u32[]{:S(2)}) collective-permute-start(bf16[16,32,128]{2,1,0:T(8,128)(2,1)S(1)} %get-tuple-element.140), channel_id=1, source_target_pairs={{0,12},{1,13},{2,14},{3,15},{4,8},{5,9},{6,10},{7,11},{8,4},{9,5},... | collective-permute-start | bytes 393224 | tf_op jit(solution)/shard_map/ppermute | solution.py:637
  41.6 0.8 %collective-permute-start.13 = (bf16[2,3,16,512]{3,2,1,0:T(8,128)(2,1)S(1)}, bf16[2,3,16,512]{3,2,1,0:T(8,128)(2,1)S(1)}, u32[]{:S(2)}, u32[]{:S(2)}) collective-permute-start(bf16[2,3,16,512]{3,2,1,0:T(8,128)(2,1)S(1)} %get-tuple-element.135), channel_id=1, source_target_pairs={{0,15},{1,2},{2,1},{3,4},{4,3},{5,6},{6,5},{7,8},{8,7},{9,10},{10,... | collective-permute-start | bytes 294920 | tf_op jit(solution)/shard_map/ppermute | solution.py:43
  42.4 1.1 %collective-permute-start.14 = (bf16[2,3,16,512]{3,2,1,0:T(8,128)(2,1)S(1)}, bf16[2,3,16,512]{3,2,1,0:T(8,128)(2,1)S(1)}, u32[]{:S(2)}, u32[]{:S(2)}) collective-permute-start(bf16[2,3,16,512]{3,2,1,0:T(8,128)(2,1)S(1)} %get-tuple-element.129.refs_0_), channel_id=1, source_target_pairs={{0,1},{1,0},{2,3},{3,2},{4,5},{5,4},{6,7},{7,6},{8,9},{9,8},{10,11... | collective-permute-start | bytes 294920 | tf_op jit(solution)/shard_map/ppermute | solution.py:44
  43.5 1.3 %collective-permute-start.18 = (bf16[10,32,128]{2,1,0:T(8,128)(2,1)S(1)}, bf16[10,32,128]{2,1,0:T(8,128)(2,1)S(1)}, u32[]{:S(2)}, u32[]{:S(2)}) collective-permute-start(bf16[10,32,128]{2,1,0:T(8,128)(2,1)S(1)} %get-tuple-element.141), channel_id=1, source_target_pairs={{0,8},{1,9},{2,10},{3,11},{4,12},{5,13},{6,14},{7,15},{8,0},{9,1},... | collective-permute-start | bytes 245768 | tf_op jit(solution)/shard_map/ppermute | solution.py:637
  44.8 1.5 %collective-permute-start.16 = (bf16[10,32,128]{2,1,0:T(8,128)(2,1)S(1)}, bf16[10,32,128]{2,1,0:T(8,128)(2,1)S(1)}, u32[]{:S(2)}, u32[]{:S(2)}) collective-permute-start(bf16[10,32,128]{2,1,0:T(8,128)(2,1)S(1)} %get-tuple-element.134.after_ref), channel_id=1, source_target_pairs={{0,4},{1,5},{2,6},{3,7},{4,0},{5,1},{6,2},{7,3},{8,12},{9,13},{10,... | collective-permute-start | bytes 245768 | tf_op jit(solution)/shard_map/ppermute | solution.py:637
  46.3 3.1 %collective-permute-done.13.second_in = bf16[2,3,16,512]{3,2,1,0:T(8,128)(2,1)S(1)} collective-permute-done((bf16[2,3,16,512]{3,2,1,0:T(8,128)(2,1)S(1)}, bf16[2,3,16,512]{3,2,1,0:T(8,128)(2,1)S(1)}, u32[]{:S(2)}, u32[]{:S(2)}) %collective-permute-start.13) | collective-permute-done | bytes 98336 | tf_op jit(solution)/shard_map/ppermute | solution.py:43
  49.4 1.0 %shard_map.118.after_ref = bf16[2,128,512]{2,1,0:T(8,128)(2,1)} custom-call(s32[1]{0:T(128)} %bitcast.me_ref, bf16[10,32,128]{2,1,0:T(8,128)(2,1)S(1)} %get-tuple-element.134.after_ref, bf16[2,3,16,512]{3,2,1,0:T(8,128)(2,1)S(1)} %collective-permute-done.13.second_in, bf16[2,3,16,512]{3,2,1,0:T(8,128)(2,1)S(1)} %collective-permute-done.14.first_in, ...), custom_call_target="tpu_custom_call" | custom-call | flops 1000000 | bytes 10000 | tf_op jit(solution)/shard_map/pallas_call | solution.py:507
  50.4 2.5 %collective-permute-done.18.refs_2_ = bf16[10,32,128]{2,1,0:T(8,128)(2,1)S(1)} collective-permute-done((bf16[10,32,128]{2,1,0:T(8,128)(2,1)S(1)}, bf16[10,32,128]{2,1,0:T(8,128)(2,1)S(1)}, u32[]{:S(2)}, u32[]{:S(2)}) %collective-permute-start.18) | collective-permute-done | bytes 81952 | tf_op jit(solution)/shard_map/ppermute | solution.py:637
  53.0 0.0 collective-permute-done.16.refs_0_
  53.0 0.0 collective-permute-done.17.refs_1_
  53.0 0.8 %shard_map.120 = f32[32,2048]{1,0:T(8,128)} custom-call(bf16[2,128,512]{2,1,0:T(8,128)(2,1)} %shard_map.118.after_ref, f32[32,768]{1,0:T(8,128)S(1)} %get-tuple-element.138.own_a, f32[32,1280]{1,0:T(8,128)S(1)} %get-tuple-element.139.own_b, bf16[10,32,128]{2,1,0:T(8,128)(2,1)S(1)} %collective-permute-done.16.refs_0_, ...), custom_call_target="tpu_custom_call" | custom-call | flops 1000000 | bytes 10000 | tf_op jit(solution)/shard_map/pallas_call | solution.py:507
  (10 shorter events, 0.1 us)
Async XLA Ops:
  1.8 8.6 %collective-permute-start = (bf16[2,3,16,512]{3,2,1,0:T(8,128)(2,1)S(1)}, bf16[2,3,16,512]{3,2,1,0:T(8,128)(2,1)S(1)}, u32[]{:S(2)}, u32[]{:S(2)}) collective-permute-start(bf16[2,3,16,512]{3,2,1,0:T(8,128)(2,1)S(1)} %get-tuple-element.77), channel_id=1, source_target_pairs={{0,4},{1,5},{2,6},{3,7},{4,8},{5,9},{6,10},{7,11},{8,12},{9,13},{1... | collective-permute-start | bytes 294920 | tf_op jit(solution)/shard_map/ppermute | solution.py:28
  4.9 6.4 %collective-permute-start.1 = (bf16[2,3,16,512]{3,2,1,0:T(8,128)(2,1)S(1)}, bf16[2,3,16,512]{3,2,1,0:T(8,128)(2,1)S(1)}, u32[]{:S(2)}, u32[]{:S(2)}) collective-permute-start(bf16[2,3,16,512]{3,2,1,0:T(8,128)(2,1)S(1)} %get-tuple-element.78), channel_id=1, source_target_pairs={{0,12},{1,13},{2,14},{3,15},{4,0},{5,1},{6,2},{7,3},{8,4},{9,5},{1... | collective-permute-start | bytes 294920 | tf_op jit(solution)/shard_map/ppermute | solution.py:28
  11.3 6.3 %collective-permute-start.3 = (bf16[2,3,16,512]{3,2,1,0:T(8,128)(2,1)S(1)}, bf16[2,3,16,512]{3,2,1,0:T(8,128)(2,1)S(1)}, u32[]{:S(2)}, u32[]{:S(2)}) collective-permute-start(bf16[2,3,16,512]{3,2,1,0:T(8,128)(2,1)S(1)} %get-tuple-element.80), channel_id=1, source_target_pairs={{0,1},{1,0},{2,3},{3,2},{4,5},{5,4},{6,7},{7,6},{8,9},{9,8},{10,11... | collective-permute-start | bytes 294920 | tf_op jit(solution)/shard_map/ppermute | solution.py:44
  11.4 6.8 %collective-permute-start.2 = (bf16[2,3,16,512]{3,2,1,0:T(8,128)(2,1)S(1)}, bf16[2,3,16,512]{3,2,1,0:T(8,128)(2,1)S(1)}, u32[]{:S(2)}, u32[]{:S(2)}) collective-permute-start(bf16[2,3,16,512]{3,2,1,0:T(8,128)(2,1)S(1)} %get-tuple-element.79.after_ref), channel_id=1, source_target_pairs={{0,15},{1,2},{2,1},{3,4},{4,3},{5,6},{6,5},{7,8},{8,7},{9,10},{10,... | collective-permute-start | bytes 294920 | tf_op jit(solution)/shard_map/ppermute | solution.py:43
  21.5 2.3 %collective-permute-start.4 = (bf16[4,32,1024]{2,1,0:T(8,128)(2,1)S(1)}, bf16[4,32,1024]{2,1,0:T(8,128)(2,1)S(1)}, u32[]{:S(2)}, u32[]{:S(2)}) collective-permute-start(bf16[4,32,1024]{2,1,0:T(8,128)(2,1)S(1)} %get-tuple-element.101), channel_id=1, source_target_pairs={{0,1},{1,0},{2,3},{3,2},{4,5},{5,4},{6,7},{7,6},{8,9},{9,8},{10,11... | collective-permute-start | bytes 786440 | tf_op jit(solution)/shard_map/ppermute | solution.py:609
  23.1 3.0 %collective-permute-start.5 = (bf16[2,4,32,512]{3,2,1,0:T(8,128)(2,1)S(1)}, bf16[2,4,32,512]{3,2,1,0:T(8,128)(2,1)S(1)}, u32[]{:S(2)}, u32[]{:S(2)}) collective-permute-start(bf16[2,4,32,512]{3,2,1,0:T(8,128)(2,1)S(1)} %get-tuple-element.106), channel_id=1, source_target_pairs={{0,1},{1,0},{2,3},{3,2},{4,5},{5,4},{6,7},{7,6},{8,9},{9,8},{10,11... | collective-permute-start | bytes 786440 | tf_op jit(solution)/shard_map/ppermute | solution.py:609
  23.7 8.7 %collective-permute-start.7 = (bf16[4,32,1024]{2,1,0:T(8,128)(2,1)S(1)}, bf16[4,32,1024]{2,1,0:T(8,128)(2,1)S(1)}, u32[]{:S(2)}, u32[]{:S(2)}) collective-permute-start(bf16[4,32,1024]{2,1,0:T(8,128)(2,1)S(1)} %get-tuple-element.123), channel_id=1, source_target_pairs={{0,1},{1,0},{2,3},{3,2},{4,5},{5,4},{6,7},{7,6},{8,9},{9,8},{10,11... | collective-permute-start | bytes 786440 | tf_op jit(solution)/shard_map/ppermute | solution.py:609
  23.8 9.2 %collective-permute-start.8 = (bf16[4,32,1024]{2,1,0:T(8,128)(2,1)S(1)}, bf16[4,32,1024]{2,1,0:T(8,128)(2,1)S(1)}, u32[]{:S(2)}, u32[]{:S(2)}) collective-permute-start(bf16[4,32,1024]{2,1,0:T(8,128)(2,1)S(1)} %add_convert_fusion.refs_0_), channel_id=1, source_target_pairs={{0,2},{1,3},{2,0},{3,1},{4,6},{5,7},{6,4},{7,5},{8,10},{9,11},{10,... | collective-permute-start | bytes 786440 | tf_op jit(solution)/shard_map/ppermute | solution.py:616
  25.5 1.4 %collective-permute-start.6 = (bf16[4,32,512]{2,1,0:T(8,128)(2,1)S(1)}, bf16[4,32,512]{2,1,0:T(8,128)(2,1)S(1)}, u32[]{:S(2)}, u32[]{:S(2)}) collective-permute-start(bf16[4,32,512]{2,1,0:T(8,128)(2,1)S(1)} %get-tuple-element.107), channel_id=1, source_target_pairs={{0,1},{1,0},{2,3},{3,2},{4,5},{5,4},{6,7},{7,6},{8,9},{9,8},{10,11... | collective-permute-start | bytes 393224 | tf_op jit(solution)/shard_map/ppermute | solution.py:609
  26.0 13.8 %collective-permute-start.12 = (bf16[4,32,512]{2,1,0:T(8,128)(2,1)S(1)}, bf16[4,32,512]{2,1,0:T(8,128)(2,1)S(1)}, u32[]{:S(2)}, u32[]{:S(2)}) collective-permute-start(bf16[4,32,512]{2,1,0:T(8,128)(2,1)S(1)} %get-tuple-element.133), channel_id=1, source_target_pairs={{0,1},{1,0},{2,3},{3,2},{4,5},{5,4},{6,7},{7,6},{8,9},{9,8},{10,11... | collective-permute-start | bytes 393224 | tf_op jit(solution)/shard_map/ppermute | solution.py:609
  27.0 12.8 %collective-permute-start.11 = (bf16[4,32,1024]{2,1,0:T(8,128)(2,1)S(1)}, bf16[4,32,1024]{2,1,0:T(8,128)(2,1)S(1)}, u32[]{:S(2)}, u32[]{:S(2)}) collective-permute-start(bf16[4,32,1024]{2,1,0:T(8,128)(2,1)S(1)} %shard_map.113.refs_0_), channel_id=1, source_target_pairs={{0,2},{1,3},{2,0},{3,1},{4,6},{5,7},{6,4},{7,5},{8,10},{9,11},{10,... | collective-permute-start | bytes 786440 | tf_op jit(solution)/shard_map/ppermute | solution.py:627
  30.0 5.5 %collective-permute-start.9 = (bf16[2,3,16,512]{3,2,1,0:T(8,128)(2,1)S(1)}, bf16[2,3,16,512]{3,2,1,0:T(8,128)(2,1)S(1)}, u32[]{:S(2)}, u32[]{:S(2)}) collective-permute-start(bf16[2,3,16,512]{3,2,1,0:T(8,128)(2,1)S(1)} %get-tuple-element.127), channel_id=1, source_target_pairs={{0,12},{1,13},{2,14},{3,15},{4,0},{5,1},{6,2},{7,3},{8,4},{9,5},{1... | collective-permute-start | bytes 294920 | tf_op jit(solution)/shard_map/ppermute | solution.py:28
  32.4 7.4 %collective-permute-start.10 = (bf16[2,3,16,512]{3,2,1,0:T(8,128)(2,1)S(1)}, bf16[2,3,16,512]{3,2,1,0:T(8,128)(2,1)S(1)}, u32[]{:S(2)}, u32[]{:S(2)}) collective-permute-start(bf16[2,3,16,512]{3,2,1,0:T(8,128)(2,1)S(1)} %get-tuple-element.128), channel_id=1, source_target_pairs={{0,4},{1,5},{2,6},{3,7},{4,8},{5,9},{6,10},{7,11},{8,12},{9,13},{1... | collective-permute-start | bytes 294920 | tf_op jit(solution)/shard_map/ppermute | solution.py:28
  33.1 6.9 %collective-permute-start.15 = (bf16[12,32,128]{2,1,0:T(8,128)(2,1)S(1)}, bf16[12,32,128]{2,1,0:T(8,128)(2,1)S(1)}, u32[]{:S(2)}, u32[]{:S(2)}) collective-permute-start(bf16[12,32,128]{2,1,0:T(8,128)(2,1)S(1)} %get-tuple-element.124.after_ref), channel_id=1, source_target_pairs={{0,4},{1,5},{2,6},{3,7},{4,0},{5,1},{6,2},{7,3},{8,12},{9,13},{10,... | collective-permute-start | bytes 294920 | tf_op jit(solution)/shard_map/ppermute | solution.py:637
  39.8 9.6 %copy-start = (s32[1,8,16]{2,1,0:T(8,128)S(1)}, s32[1,8,16]{2,1,0:T(8,128)}, u32[]{:S(2)}) copy-start(s32[1,8,16]{2,1,0:T(8,128)} %send_ref.1) | copy-start | bytes 1540
  40.0 13.0 %collective-permute-start.17 = (bf16[16,32,128]{2,1,0:T(8,128)(2,1)S(1)}, bf16[16,32,128]{2,1,0:T(8,128)(2,1)S(1)}, u32[]{:S(2)}, u32[]{:S(2)}) collective-permute-start(bf16[16,32,128]{2,1,0:T(8,128)(2,1)S(1)} %get-tuple-element.140), channel_id=1, source_target_pairs={{0,12},{1,13},{2,14},{3,15},{4,8},{5,9},{6,10},{7,11},{8,4},{9,5},... | collective-permute-start | bytes 393224 | tf_op jit(solution)/shard_map/ppermute | solution.py:637
  41.6 7.8 %collective-permute-start.13 = (bf16[2,3,16,512]{3,2,1,0:T(8,128)(2,1)S(1)}, bf16[2,3,16,512]{3,2,1,0:T(8,128)(2,1)S(1)}, u32[]{:S(2)}, u32[]{:S(2)}) collective-permute-start(bf16[2,3,16,512]{3,2,1,0:T(8,128)(2,1)S(1)} %get-tuple-element.135), channel_id=1, source_target_pairs={{0,15},{1,2},{2,1},{3,4},{4,3},{5,6},{6,5},{7,8},{8,7},{9,10},{10,... | collective-permute-start | bytes 294920 | tf_op jit(solution)/shard_map/ppermute | solution.py:43
  42.4 7.1 %collective-permute-start.14 = (bf16[2,3,16,512]{3,2,1,0:T(8,128)(2,1)S(1)}, bf16[2,3,16,512]{3,2,1,0:T(8,128)(2,1)S(1)}, u32[]{:S(2)}, u32[]{:S(2)}) collective-permute-start(bf16[2,3,16,512]{3,2,1,0:T(8,128)(2,1)S(1)} %get-tuple-element.129.refs_0_), channel_id=1, source_target_pairs={{0,1},{1,0},{2,3},{3,2},{4,5},{5,4},{6,7},{7,6},{8,9},{9,8},{10,11... | collective-permute-start | bytes 294920 | tf_op jit(solution)/shard_map/ppermute | solution.py:44
  43.5 9.5 %collective-permute-start.18 = (bf16[10,32,128]{2,1,0:T(8,128)(2,1)S(1)}, bf16[10,32,128]{2,1,0:T(8,128)(2,1)S(1)}, u32[]{:S(2)}, u32[]{:S(2)}) collective-permute-start(bf16[10,32,128]{2,1,0:T(8,128)(2,1)S(1)} %get-tuple-element.141), channel_id=1, source_target_pairs={{0,8},{1,9},{2,10},{3,11},{4,12},{5,13},{6,14},{7,15},{8,0},{9,1},... | collective-permute-start | bytes 245768 | tf_op jit(solution)/shard_map/ppermute | solution.py:637
  44.8 8.1 %collective-permute-start.16 = (bf16[10,32,128]{2,1,0:T(8,128)(2,1)S(1)}, bf16[10,32,128]{2,1,0:T(8,128)(2,1)S(1)}, u32[]{:S(2)}, u32[]{:S(2)}) collective-permute-start(bf16[10,32,128]{2,1,0:T(8,128)(2,1)S(1)} %get-tuple-element.134.after_ref), channel_id=1, source_target_pairs={{0,4},{1,5},{2,6},{3,7},{4,0},{5,1},{6,2},{7,3},{8,12},{9,13},{10,... | collective-permute-start | bytes 245768 | tf_op jit(solution)/shard_map/ppermute | solution.py:637

commit v14 on v12

--- a/solution.py
+++ b/solution.py
@@ -388,7 +388,7 @@
         projection_ref[plane, :, quarter * 128 : (quarter + 1) * 128] = part[:, 384:]
 
 
-def pack_kernel(pieces, *refs):
+def pack_kernel(pieces, after_ref, *refs):
     for i, (ref, core) in enumerate(zip(refs[:pieces], refs[pieces:-1])):
         arrived = core[0] if len(core.shape) == 4 else core[...]
         refs[-1][:, :, i * 512 : (i + 1) * 512] = (ref[...] + arrived.astype(f32)).astype(bf16)
@@ -616,17 +616,16 @@
     y_a = lax.ppermute(y_sent, "patch", flop)
     later = [attention((), range(half, groups), False)]
     own_b, other_b, core_other_b, core_own_b = zip(*later)
+    node, to_plus, to_minus, own_right, own_left = call(
+        functools.partial(node_kernel, groups, 0),
+        [((members, node_rows, width), f32), three, three, one, one],
+        (*grads[0::3], *grads[1::3], *grads[2::3], wq, wk, wv),
+    )
     (y_sent,) = call(
         functools.partial(pack_kernel, len(later)), [(other_b[0].shape, bf16)],
-        (*other_b, *core_other_b),
+        (node, *other_b, *core_other_b), specs=[pl.ANY],
     )
     y_b = lax.ppermute(y_sent, "patch", flop)
-    node, to_plus, to_minus, own_right, own_left = call(
-        functools.partial(node_kernel, groups, 1),
-        [((members, node_rows, width), f32), three, three, one, one],
-        (y_sent, *grads[0::3], *grads[1::3], *grads[2::3], wq, wk, wv),
-        specs=[pl.ANY],
-    )
     from_plus = shifted(to_minus, -row_width)
     from_minus = shifted(to_plus, row_width)
     def exchange(sent, distance):
@@ -639,7 +638,7 @@
             ((half * inner_planes, rows, width), f32),
             ((planes // 2 * wide // 128, rows, 128), bf16),
         ],
-        (node, own_a, core_own, y_a), specs=[pl.ANY], flops=2 * 10**10,
+        (y_sent, own_a, core_own, y_a), specs=[pl.ANY], flops=2 * 10**10,
     )
     in_a = exchange(sent_a, 1)
     outgoing = call(

time: 52.2 us -> 53.2 us (1.019)
  starting transfers between devices: 17.5 us -> 18.7 us
    ppermute x2, starting transfers between devices: 0.04 us -> 2.07 us  [swap(): return [lax.ppermute(pair[0], 'patch', first), later]]
    ppermute x4, starting transfers between devices: 7.25 us -> 9.13 us  [shifted(): lax.ppermute(shard, 'patch', [(i, (i + by) % count) for i in range(count)])]
    ppermute x1, starting transfers between devices: 2.07 us -> 0.21 us  [body(): y_b = lax.ppermute(y_sent, 'patch', flop)]
    ppermute x1, waiting for transfers between devices: 3.75 us -> 4.77 us  [body(): y_a = lax.ppermute(y_sent, 'patch', flop)]
    ppermute x4, waiting for transfers between devices: 3.75 us -> 2.86 us  [shifted(): lax.ppermute(shard, 'patch', [(i, (i + by) % count) for i in range(count)])]
    ppermute x4, waiting for transfers between devices: 2.05 us -> 1.22 us  [attention(): arrived = [lax.ppermute(shard, 'patch', flip) for shard in sent]]
    ppermute x4, starting transfers between devices: 3.61 us -> 2.85 us  [exchange(): return lax.ppermute(sent, 'patch', along_z(count, distance))]
  transfers between devices with their start and end apart: 18 -> 18, of which waited for: 10 -> 9; matrix products, arithmetic and copies ran while one was open for 0% -> 0% of each run, Pallas kernels for 18% -> 17%
where the time goes in v14:
time: 53.2 us; the launch traced here: 53 us
  starting transfers between devices  18.7 us (35%)
  waiting for transfers between devices  17.8 us (33%)
  Pallas kernels  15.7 us (30%)
  between operations  0.79 us (1%)
    pallas_call x16, Pallas kernels, call(): pl.pallas_call(kernel, out_shape=[jax.ShapeDtypeStruct(*o) if final else...  15.7 us
    ppermute x4, starting transfers between devices, shifted(): lax.ppermute(shard, 'patch', [(i, (i + by) % count) for i in range(count)])  9.13 us
    ppermute x2, waiting for transfers between devices, swap(): later = lax.ppermute(pair[1], 'patch', second)  5.14 us
    ppermute x1, waiting for transfers between devices, body(): y_a = lax.ppermute(y_sent, 'patch', flop)  4.77 us
    ppermute x2, starting transfers between devices, swap(): later = lax.ppermute(pair[1], 'patch', second)  3.45 us
    ppermute x4, waiting for transfers between devices, exchange(): return lax.ppermute(sent, 'patch', along_z(count, distance))  3.26 us
    ppermute x4, waiting for transfers between devices, shifted(): lax.ppermute(shard, 'patch', [(i, (i + by) % count) for i in range(count)])  2.86 us
    ppermute x4, starting transfers between devices, exchange(): return lax.ppermute(sent, 'patch', along_z(count, distance))  2.85 us
  transfers between devices with their start and end apart: 18, of which 9 were waited for; matrix products, arithmetic and copies ran while one was open for 0% of the time, Pallas kernels for 17%

profile of v14, /device:TPU:0, one launch (start us, length us, event | category | flops | bytes accessed | tf_op | source)
XLA Modules:
  0.0 53.0 jit_solution(7225357759802678136)
XLA Ops:
  0.6 1.2 %shard_map.104 = (bf16[2,3,16,512]{3,2,1,0:T(8,128)(2,1)S(1)}, bf16[2,3,16,512]{3,2,1,0:T(8,128)(2,1)S(1)}, bf16[2,1,16,512]{3,2,1,0:T(8,128)(2,1)S(1)}, bf16[2,...) custom-call(s32[1,8,16]{2,1,0:T(8,128)} %send_ref.1, bf16[2,128,512]{2,1,0:T(8,128)(2,1)} %x_hbm.1), custom_call_target="tpu_custom_call" | custom-call | flops 1000000 | bytes 10000 | tf_op jit(solution)/shard_map/pallas_call | solution.py:507
  1.8 3.1 %collective-permute-start = (bf16[2,3,16,512]{3,2,1,0:T(8,128)(2,1)S(1)}, bf16[2,3,16,512]{3,2,1,0:T(8,128)(2,1)S(1)}, u32[]{:S(2)}, u32[]{:S(2)}) collective-permute-start(bf16[2,3,16,512]{3,2,1,0:T(8,128)(2,1)S(1)} %get-tuple-element.75), channel_id=1, source_target_pairs={{0,4},{1,5},{2,6},{3,7},{4,8},{5,9},{6,10},{7,11},{8,12},{9,13},{1... | collective-permute-start | bytes 294920 | tf_op jit(solution)/shard_map/ppermute | solution.py:28
  4.9 2.1 %collective-permute-start.1 = (bf16[2,3,16,512]{3,2,1,0:T(8,128)(2,1)S(1)}, bf16[2,3,16,512]{3,2,1,0:T(8,128)(2,1)S(1)}, u32[]{:S(2)}, u32[]{:S(2)}) collective-permute-start(bf16[2,3,16,512]{3,2,1,0:T(8,128)(2,1)S(1)} %get-tuple-element.76), channel_id=1, source_target_pairs={{0,12},{1,13},{2,14},{3,15},{4,0},{5,1},{6,2},{7,3},{8,4},{9,5},{1... | collective-permute-start | bytes 294920 | tf_op jit(solution)/shard_map/ppermute | solution.py:28
  7.0 2.6 %shard_map.105 = (bf16[8,2,128,128]{3,2,1,0:T(8,128)(2,1)S(1)}, bf16[8,2,128,128]{3,2,1,0:T(8,128)(2,1)S(1)}, bf16[8,2,128,128]{3,2,1,0:T(8,128)(2,1)S(1)}, bf16...) custom-call(bf16[2,1,16,512]{3,2,1,0:T(8,128)(2,1)S(1)} %get-tuple-e, ...), custom_call_target="tpu_custom_call" | custom-call | flops 1000000 | bytes 10000 | tf_op jit(solution)/shard_map/pallas_call | solution.py:507
  9.7 0.8 %collective-permute-done.plus_ref = bf16[2,3,16,512]{3,2,1,0:T(8,128)(2,1)S(1)} collective-permute-done((bf16[2,3,16,512]{3,2,1,0:T(8,128)(2,1)S(1)}, bf16[2,3,16,512]{3,2,1,0:T(8,128)(2,1)S(1)}, u32[]{:S(2)}, u32[]{:S(2)}) %collective-permute-start) | collective-permute-done | bytes 98336 | tf_op jit(solution)/shard_map/ppermute | solution.py:28
  10.4 0.8 %collective-permute-done.1.minus_ref = bf16[2,3,16,512]{3,2,1,0:T(8,128)(2,1)S(1)} collective-permute-done((bf16[2,3,16,512]{3,2,1,0:T(8,128)(2,1)S(1)}, bf16[2,3,16,512]{3,2,1,0:T(8,128)(2,1)S(1)}, u32[]{:S(2)}, u32[]{:S(2)}) %collective-permute-start.1) | collective-permute-done | bytes 98336 | tf_op jit(solution)/shard_map/ppermute | solution.py:28
  11.3 0.1 collective-permute-start.3
  11.4 3.4 %collective-permute-start.2 = (bf16[2,3,16,512]{3,2,1,0:T(8,128)(2,1)S(1)}, bf16[2,3,16,512]{3,2,1,0:T(8,128)(2,1)S(1)}, u32[]{:S(2)}, u32[]{:S(2)}) collective-permute-start(bf16[2,3,16,512]{3,2,1,0:T(8,128)(2,1)S(1)} %get-tuple-element.77.after_ref), channel_id=1, source_target_pairs={{0,15},{1,2},{2,1},{3,4},{4,3},{5,6},{6,5},{7,8},{8,7},{9,10},{10,... | collective-permute-start | bytes 294920 | tf_op jit(solution)/shard_map/ppermute | solution.py:43
  14.8 1.4 %shard_map.108.refs_4_.refs_12_ = f32[256,128]{1,0:T(8,128)S(1)} custom-call(bf16[2,3,16,512]{3,2,1,0:T(8,128)(2,1)S(1)} %get-tuple-element.77.after_ref, s32[128,256]{1,0:T(8,128)S(1)} %get-tuple-element.86.neigh_ref, s32[1,128]{1,0:T(1,128)S(1)} %get-tuple-element.87.count_ref), custom_call_target="tpu_custom_call" | custom-call | flops 1000000 | bytes 10000 | tf_op jit(solution)/shard_map/pallas_call | solution.py:507
  16.3 1.3 %shard_map.109 = (f32[3,2,128,512]{3,2,1,0:T(8,128)S(1)}, f32[2,2,8,512]{3,2,1,0:T(8,128)S(1)}, f32[3,2,128,512]{3,2,1,0:T(8,128)S(1)}, f32[2,2,8,512]{3,2,1,0:T...) custom-call(bf16[8,2,128,128]{3,2,1,0:T(8,128)(2,1)S(1)} %get-tuple-, ...), custom_call_target="tpu_custom_call" | custom-call | flops 1000000 | bytes 10000 | tf_op jit(solution)/shard_map/pallas_call | solution.py:507
  17.6 0.0 collective-permute-done.3.first_in
  17.6 0.5 %collective-permute-done.2.second_in = bf16[2,3,16,512]{3,2,1,0:T(8,128)(2,1)S(1)} collective-permute-done((bf16[2,3,16,512]{3,2,1,0:T(8,128)(2,1)S(1)}, bf16[2,3,16,512]{3,2,1,0:T(8,128)(2,1)S(1)}, u32[]{:S(2)}, u32[]{:S(2)}) %collective-permute-start.2) | collective-permute-done | bytes 98336 | tf_op jit(solution)/shard_map/ppermute | solution.py:43
  18.2 0.6 %shard_map.107 = (bf16[4,2,128,128]{3,2,1,0:T(8,128)(2,1)S(1)}, bf16[4,2,128,128]{3,2,1,0:T(8,128)(2,1)S(1)}, bf16[4,2,128,128]{3,2,1,0:T(8,128)(2,1)S(1)}, bf16...) custom-call(s32[1]{0:T(128)} %bitcast.me_ref, bf16[2,3,16,512]{3,2,1,0:T(8,128)(2,1)S(1)} %collective-permute-done.2.second_in, ...), custom_call_target="tpu_custom_call" | custom-call | flops 1000000 | bytes 10000 | tf_op jit(solution)/shard_map/pallas_call | solution.py:507
  18.8 3.8 %shard_map.110 = (f32[4,32,1536]{2,1,0:T(8,128)S(1)}, f32[4,32,1536]{2,1,0:T(8,128)S(1)}, bf16[4,32,1536]{2,1,0:T(8,128)(2,1)S(1)}, bf16[4,32,1536]{2,1,0:T(8,12...) custom-call(s32[1]{0:T(128)} %bitcast.me_ref, ...), custom_call_target="tpu_custom_call" | custom-call | flops 1000000 | bytes 10000 | tf_op jit(solution)/shard_map/pallas_call | solution.py:507
  22.6 0.1 collective-permute-start.6
  22.7 0.5 collective-permute-start.5
  23.2 1.2 %collective-permute-done.6 = bf16[4,32,1536]{2,1,0:T(8,128)(2,1)S(1)} collective-permute-done((bf16[4,32,1536]{2,1,0:T(8,128)(2,1)S(1)}, bf16[4,32,1536]{2,1,0:T(8,128)(2,1)S(1)}, u32[]{:S(2)}, u32[]{:S(2)}) %collective-permute-start.6) | collective-permute-done | bytes 393248 | tf_op jit(solution)/shard_map/ppermute | solution.py:609
  24.4 0.1 add_convert_fusion
  24.5 0.1 collective-permute-start.7
  24.6 1.5 %shard_map.111 = (f32[4,32,512]{2,1,0:T(8,128)S(1)}, f32[4,32,512]{2,1,0:T(8,128)S(1)}, bf16[4,32,512]{2,1,0:T(8,128)(2,1)S(1)}, bf16[4,32,512]{2,1,0:T(8,128)(2...) custom-call(s32[1]{0:T(128)} %bitcast.me_ref, ...), custom_call_target="tpu_custom_call" | custom-call | flops 1000000 | bytes 10000 | tf_op jit(solution)/shard_map/pallas_call | solution.py:507
  26.1 0.2 collective-permute-start.4
  26.3 1.0 %shard_map.112 = (f32[2,128,512]{2,1,0:T(8,128)S(1)}, bf16[2,3,16,512]{3,2,1,0:T(8,128)(2,1)S(1)}, bf16[2,3,16,512]{3,2,1,0:T(8,128)(2,1)S(1)}, bf16[2,1,16,512]...) custom-call(bf16[2,128,128]{2,1,0:T(8,128)(2,1)S(1)} %get-tuple-element.96.refs_0_, ...), custom_call_target="tpu_custom_call" | custom-call | flops 1000000 | bytes 10000 | tf_op jit(solution)/shard_map/pallas_call | solution.py:507
  27.3 4.0 %collective-permute-start.8 = (bf16[2,3,16,512]{3,2,1,0:T(8,128)(2,1)S(1)}, bf16[2,3,16,512]{3,2,1,0:T(8,128)(2,1)S(1)}, u32[]{:S(2)}, u32[]{:S(2)}) collective-permute-start(bf16[2,3,16,512]{3,2,1,0:T(8,128)(2,1)S(1)} %get-tuple-element.122), channel_id=1, source_target_pairs={{0,12},{1,13},{2,14},{3,15},{4,0},{5,1},{6,2},{7,3},{8,4},{9,5},{1... | collective-permute-start | bytes 294920 | tf_op jit(solution)/shard_map/ppermute | solution.py:28
  31.3 0.0 collective-permute-start.9
  31.3 0.0 collective-permute-done.4.refs_1_
  31.3 0.2 collective-permute-start.11
  31.5 0.0 collective-permute-done.5.core_in
  31.5 0.2 collective-permute-start.10
  31.7 4.8 %collective-permute-done.7.y_in = bf16[4,32,1536]{2,1,0:T(8,128)(2,1)S(1)} collective-permute-done((bf16[4,32,1536]{2,1,0:T(8,128)(2,1)S(1)}, bf16[4,32,1536]{2,1,0:T(8,128)(2,1)S(1)}, u32[]{:S(2)}, u32[]{:S(2)}) %collective-permute-start.7) | collective-permute-done | bytes 393248 | tf_op jit(solution)/shard_map/ppermute | solution.py:616
  36.5 0.1 shard_map.114
  36.6 0.1 collective-permute-start.14
  36.7 0.0 collective-permute-done.8.plus_ref
  36.7 1.2 %collective-permute-done.9.minus_ref = bf16[2,3,16,512]{3,2,1,0:T(8,128)(2,1)S(1)} collective-permute-done((bf16[2,3,16,512]{3,2,1,0:T(8,128)(2,1)S(1)}, bf16[2,3,16,512]{3,2,1,0:T(8,128)(2,1)S(1)}, u32[]{:S(2)}, u32[]{:S(2)}) %collective-permute-start.9) | collective-permute-done | bytes 98336 | tf_op jit(solution)/shard_map/ppermute | solution.py:28
  38.0 0.0 collective-permute-done.11.refs_4_
  38.0 0.5 collective-permute-done.10.refs_2_
  38.5 0.1 shard_map.116
  38.6 3.3 %collective-permute-done.14.in_a = bf16[18,32,128]{2,1,0:T(8,128)(2,1)S(1)} collective-permute-done((bf16[18,32,128]{2,1,0:T(8,128)(2,1)S(1)}, bf16[18,32,128]{2,1,0:T(8,128)(2,1)S(1)}, u32[]{:S(2)}, u32[]{:S(2)}) %collective-permute-start.14) | collective-permute-done | bytes 147488 | tf_op jit(solution)/shard_map/ppermute | solution.py:632
  41.9 2.1 %collective-permute-start.16 = (bf16[16,32,128]{2,1,0:T(8,128)(2,1)S(1)}, bf16[16,32,128]{2,1,0:T(8,128)(2,1)S(1)}, u32[]{:S(2)}, u32[]{:S(2)}) collective-permute-start(bf16[16,32,128]{2,1,0:T(8,128)(2,1)S(1)} %get-tuple-element.134), channel_id=1, source_target_pairs={{0,12},{1,13},{2,14},{3,15},{4,8},{5,9},{6,10},{7,11},{8,4},{9,5},... | collective-permute-start | bytes 393224 | tf_op jit(solution)/shard_map/ppermute | solution.py:632
  44.0 0.0 collective-permute-start.12
  44.0 2.0 %collective-permute-start.13 = (bf16[2,3,16,512]{3,2,1,0:T(8,128)(2,1)S(1)}, bf16[2,3,16,512]{3,2,1,0:T(8,128)(2,1)S(1)}, u32[]{:S(2)}, u32[]{:S(2)}) collective-permute-start(bf16[2,3,16,512]{3,2,1,0:T(8,128)(2,1)S(1)} %get-tuple-element.124.refs_0_), channel_id=1, source_target_pairs={{0,1},{1,0},{2,3},{3,2},{4,5},{5,4},{6,7},{7,6},{8,9},{9,8},{10,11... | collective-permute-start | bytes 294920 | tf_op jit(solution)/shard_map/ppermute | solution.py:44
  46.0 0.0 collective-permute-start.17
  46.0 0.6 %collective-permute-start.15 = (bf16[7,32,128]{2,1,0:T(8,128)(2,1)S(1)}, bf16[7,32,128]{2,1,0:T(8,128)(2,1)S(1)}, u32[]{:S(2)}, u32[]{:S(2)}) collective-permute-start(bf16[7,32,128]{2,1,0:T(8,128)(2,1)S(1)} %get-tuple-element.128.after_ref), channel_id=1, source_target_pairs={{0,4},{1,5},{2,6},{3,7},{4,0},{5,1},{6,2},{7,3},{8,12},{9,13},{10,... | collective-permute-start | bytes 172040 | tf_op jit(solution)/shard_map/ppermute | solution.py:632
  46.7 4.6 %collective-permute-done.12.second_in = bf16[2,3,16,512]{3,2,1,0:T(8,128)(2,1)S(1)} collective-permute-done((bf16[2,3,16,512]{3,2,1,0:T(8,128)(2,1)S(1)}, bf16[2,3,16,512]{3,2,1,0:T(8,128)(2,1)S(1)}, u32[]{:S(2)}, u32[]{:S(2)}) %collective-permute-start.12) | collective-permute-done | bytes 98336 | tf_op jit(solution)/shard_map/ppermute | solution.py:43
  51.3 1.0 %shard_map.117.after_ref = bf16[2,128,512]{2,1,0:T(8,128)(2,1)} custom-call(s32[1]{0:T(128)} %bitcast.me_ref, bf16[7,32,128]{2,1,0:T(8,128)(2,1)S(1)} %get-tuple-element.128.after_ref, bf16[2,3,16,512]{3,2,1,0:T(8,128)(2,1)S(1)} %collective-permute-done.12.second_in, bf16[2,3,16,512]{3,2,1,0:T(8,128)(2,1)S(1)} %collective-permute-done.13.first_in, ...), custom_call_target="tpu_custom_call" | custom-call | flops 1000000 | bytes 10000 | tf_op jit(solution)/shard_map/pallas_call | solution.py:507
  52.2 0.0 collective-permute-done.17.refs_2_
  52.3 0.0 collective-permute-done.15.refs_0_
  52.3 0.0 collective-permute-done.16.refs_1_
  52.3 0.7 %shard_map.119 = f32[32,2048]{1,0:T(8,128)} custom-call(bf16[2,128,512]{2,1,0:T(8,128)(2,1)} %shard_map.117.after_ref, f32[32,1152]{1,0:T(8,128)S(1)} %get-tuple-element.132.own_a, f32[32,896]{1,0:T(8,128)S(1)} %get-tuple-element.133.own_b, bf16[7,32,128]{2,1,0:T(8,128)(2,1)S(1)} %collective-permute-done.15.refs_0_, ...), custom_call_target="tpu_custom_call" | custom-call | flops 1000000 | bytes 10000 | tf_op jit(solution)/shard_map/pallas_call | solution.py:507
  (7 shorter events, 0.1 us)
Async XLA Ops:
  1.8 8.6 %collective-permute-start = (bf16[2,3,16,512]{3,2,1,0:T(8,128)(2,1)S(1)}, bf16[2,3,16,512]{3,2,1,0:T(8,128)(2,1)S(1)}, u32[]{:S(2)}, u32[]{:S(2)}) collective-permute-start(bf16[2,3,16,512]{3,2,1,0:T(8,128)(2,1)S(1)} %get-tuple-element.75), channel_id=1, source_target_pairs={{0,4},{1,5},{2,6},{3,7},{4,8},{5,9},{6,10},{7,11},{8,12},{9,13},{1... | collective-permute-start | bytes 294920 | tf_op jit(solution)/shard_map/ppermute | solution.py:28
  4.9 6.4 %collective-permute-start.1 = (bf16[2,3,16,512]{3,2,1,0:T(8,128)(2,1)S(1)}, bf16[2,3,16,512]{3,2,1,0:T(8,128)(2,1)S(1)}, u32[]{:S(2)}, u32[]{:S(2)}) collective-permute-start(bf16[2,3,16,512]{3,2,1,0:T(8,128)(2,1)S(1)} %get-tuple-element.76), channel_id=1, source_target_pairs={{0,12},{1,13},{2,14},{3,15},{4,0},{5,1},{6,2},{7,3},{8,4},{9,5},{1... | collective-permute-start | bytes 294920 | tf_op jit(solution)/shard_map/ppermute | solution.py:28
  11.3 6.3 %collective-permute-start.3 = (bf16[2,3,16,512]{3,2,1,0:T(8,128)(2,1)S(1)}, bf16[2,3,16,512]{3,2,1,0:T(8,128)(2,1)S(1)}, u32[]{:S(2)}, u32[]{:S(2)}) collective-permute-start(bf16[2,3,16,512]{3,2,1,0:T(8,128)(2,1)S(1)} %get-tuple-element.78), channel_id=1, source_target_pairs={{0,1},{1,0},{2,3},{3,2},{4,5},{5,4},{6,7},{7,6},{8,9},{9,8},{10,11... | collective-permute-start | bytes 294920 | tf_op jit(solution)/shard_map/ppermute | solution.py:44
  11.4 6.8 %collective-permute-start.2 = (bf16[2,3,16,512]{3,2,1,0:T(8,128)(2,1)S(1)}, bf16[2,3,16,512]{3,2,1,0:T(8,128)(2,1)S(1)}, u32[]{:S(2)}, u32[]{:S(2)}) collective-permute-start(bf16[2,3,16,512]{3,2,1,0:T(8,128)(2,1)S(1)} %get-tuple-element.77.after_ref), channel_id=1, source_target_pairs={{0,15},{1,2},{2,1},{3,4},{4,3},{5,6},{6,5},{7,8},{8,7},{9,10},{10,... | collective-permute-start | bytes 294920 | tf_op jit(solution)/shard_map/ppermute | solution.py:43
  22.6 1.8 %collective-permute-start.6 = (bf16[4,32,1536]{2,1,0:T(8,128)(2,1)S(1)}, bf16[4,32,1536]{2,1,0:T(8,128)(2,1)S(1)}, u32[]{:S(2)}, u32[]{:S(2)}) collective-permute-start(bf16[4,32,1536]{2,1,0:T(8,128)(2,1)S(1)} %get-tuple-element.118), channel_id=1, source_target_pairs={{0,1},{1,0},{2,3},{3,2},{4,5},{5,4},{6,7},{7,6},{8,9},{9,8},{10,11... | collective-permute-start | bytes 1179656 | tf_op jit(solution)/shard_map/ppermute | solution.py:609
  22.7 8.8 %collective-permute-start.5 = (bf16[4,32,1536]{2,1,0:T(8,128)(2,1)S(1)}, bf16[4,32,1536]{2,1,0:T(8,128)(2,1)S(1)}, u32[]{:S(2)}, u32[]{:S(2)}) collective-permute-start(bf16[4,32,1536]{2,1,0:T(8,128)(2,1)S(1)} %get-tuple-element.116), channel_id=1, source_target_pairs={{0,1},{1,0},{2,3},{3,2},{4,5},{5,4},{6,7},{7,6},{8,9},{9,8},{10,11... | collective-permute-start | bytes 1179656 | tf_op jit(solution)/shard_map/ppermute | solution.py:609
  24.5 12.0 %collective-permute-start.7 = (bf16[4,32,1536]{2,1,0:T(8,128)(2,1)S(1)}, bf16[4,32,1536]{2,1,0:T(8,128)(2,1)S(1)}, u32[]{:S(2)}, u32[]{:S(2)}) collective-permute-start(bf16[4,32,1536]{2,1,0:T(8,128)(2,1)S(1)} %add_convert_fusion), channel_id=1, source_target_pairs={{0,2},{1,3},{2,0},{3,1},{4,6},{5,7},{6,4},{7,5},{8,10},{9,11},{10,... | collective-permute-start | bytes 1179656 | tf_op jit(solution)/shard_map/ppermute | solution.py:616
  26.1 5.2 %collective-permute-start.4 = (bf16[4,32,512]{2,1,0:T(8,128)(2,1)S(1)}, bf16[4,32,512]{2,1,0:T(8,128)(2,1)S(1)}, u32[]{:S(2)}, u32[]{:S(2)}) collective-permute-start(bf16[4,32,512]{2,1,0:T(8,128)(2,1)S(1)} %get-tuple-element.114), channel_id=1, source_target_pairs={{0,1},{1,0},{2,3},{3,2},{4,5},{5,4},{6,7},{7,6},{8,9},{9,8},{10,11... | collective-permute-start | bytes 393224 | tf_op jit(solution)/shard_map/ppermute | solution.py:609
  27.3 9.4 %collective-permute-start.8 = (bf16[2,3,16,512]{3,2,1,0:T(8,128)(2,1)S(1)}, bf16[2,3,16,512]{3,2,1,0:T(8,128)(2,1)S(1)}, u32[]{:S(2)}, u32[]{:S(2)}) collective-permute-start(bf16[2,3,16,512]{3,2,1,0:T(8,128)(2,1)S(1)} %get-tuple-element.122), channel_id=1, source_target_pairs={{0,12},{1,13},{2,14},{3,15},{4,0},{5,1},{6,2},{7,3},{8,4},{9,5},{1... | collective-permute-start | bytes 294920 | tf_op jit(solution)/shard_map/ppermute | solution.py:28
  31.3 6.7 %collective-permute-start.9 = (bf16[2,3,16,512]{3,2,1,0:T(8,128)(2,1)S(1)}, bf16[2,3,16,512]{3,2,1,0:T(8,128)(2,1)S(1)}, u32[]{:S(2)}, u32[]{:S(2)}) collective-permute-start(bf16[2,3,16,512]{3,2,1,0:T(8,128)(2,1)S(1)} %get-tuple-element.123), channel_id=1, source_target_pairs={{0,4},{1,5},{2,6},{3,7},{4,8},{5,9},{6,10},{7,11},{8,12},{9,13},{1... | collective-permute-start | bytes 294920 | tf_op jit(solution)/shard_map/ppermute | solution.py:28
  31.3 6.7 %collective-permute-start.11 = (bf16[4,32,512]{2,1,0:T(8,128)(2,1)S(1)}, bf16[4,32,512]{2,1,0:T(8,128)(2,1)S(1)}, u32[]{:S(2)}, u32[]{:S(2)}) collective-permute-start(bf16[4,32,512]{2,1,0:T(8,128)(2,1)S(1)} %get-tuple-element.127), channel_id=1, source_target_pairs={{0,1},{1,0},{2,3},{3,2},{4,5},{5,4},{6,7},{7,6},{8,9},{9,8},{10,11... | collective-permute-start | bytes 393224 | tf_op jit(solution)/shard_map/ppermute | solution.py:609
  31.5 7.0 %collective-permute-start.10 = (bf16[4,32,512]{2,1,0:T(8,128)(2,1)S(1)}, bf16[4,32,512]{2,1,0:T(8,128)(2,1)S(1)}, u32[]{:S(2)}, u32[]{:S(2)}) collective-permute-start(bf16[4,32,512]{2,1,0:T(8,128)(2,1)S(1)} %shard_map.113.after_ref), channel_id=1, source_target_pairs={{0,2},{1,3},{2,0},{3,1},{4,6},{5,7},{6,4},{7,5},{8,10},{9,11},{10,... | collective-permute-start | bytes 393224 | tf_op jit(solution)/shard_map/ppermute | solution.py:628
  36.6 5.2 %collective-permute-start.14 = (bf16[18,32,128]{2,1,0:T(8,128)(2,1)S(1)}, bf16[18,32,128]{2,1,0:T(8,128)(2,1)S(1)}, u32[]{:S(2)}, u32[]{:S(2)}) collective-permute-start(bf16[18,32,128]{2,1,0:T(8,128)(2,1)S(1)} %get-tuple-element.119.after_ref), channel_id=1, source_target_pairs={{0,4},{1,5},{2,6},{3,7},{4,0},{5,1},{6,2},{7,3},{8,12},{9,13},{10,... | collective-permute-start | bytes 442376 | tf_op jit(solution)/shard_map/ppermute | solution.py:632
  38.5 12.7 %copy-start = (s32[1,8,16]{2,1,0:T(8,128)S(1)}, s32[1,8,16]{2,1,0:T(8,128)}, u32[]{:S(2)}) copy-start(s32[1,8,16]{2,1,0:T(8,128)} %send_ref.1) | copy-start | bytes 1540
  41.9 10.4 %collective-permute-start.16 = (bf16[16,32,128]{2,1,0:T(8,128)(2,1)S(1)}, bf16[16,32,128]{2,1,0:T(8,128)(2,1)S(1)}, u32[]{:S(2)}, u32[]{:S(2)}) collective-permute-start(bf16[16,32,128]{2,1,0:T(8,128)(2,1)S(1)} %get-tuple-element.134), channel_id=1, source_target_pairs={{0,12},{1,13},{2,14},{3,15},{4,8},{5,9},{6,10},{7,11},{8,4},{9,5},... | collective-permute-start | bytes 393224 | tf_op jit(solution)/shard_map/ppermute | solution.py:632
  44.0 7.2 %collective-permute-start.12 = (bf16[2,3,16,512]{3,2,1,0:T(8,128)(2,1)S(1)}, bf16[2,3,16,512]{3,2,1,0:T(8,128)(2,1)S(1)}, u32[]{:S(2)}, u32[]{:S(2)}) collective-permute-start(bf16[2,3,16,512]{3,2,1,0:T(8,128)(2,1)S(1)} %get-tuple-element.129), channel_id=1, source_target_pairs={{0,15},{1,2},{2,1},{3,4},{4,3},{5,6},{6,5},{7,8},{8,7},{9,10},{10,... | collective-permute-start | bytes 294920 | tf_op jit(solution)/shard_map/ppermute | solution.py:43
  44.0 7.2 %collective-permute-start.13 = (bf16[2,3,16,512]{3,2,1,0:T(8,128)(2,1)S(1)}, bf16[2,3,16,512]{3,2,1,0:T(8,128)(2,1)S(1)}, u32[]{:S(2)}, u32[]{:S(2)}) collective-permute-start(bf16[2,3,16,512]{3,2,1,0:T(8,128)(2,1)S(1)} %get-tuple-element.124.refs_0_), channel_id=1, source_target_pairs={{0,1},{1,0},{2,3},{3,2},{4,5},{5,4},{6,7},{7,6},{8,9},{9,8},{10,11... | collective-permute-start | bytes 294920 | tf_op jit(solution)/shard_map/ppermute | solution.py:44
  46.0 6.2 %collective-permute-start.17 = (bf16[7,32,128]{2,1,0:T(8,128)(2,1)S(1)}, bf16[7,32,128]{2,1,0:T(8,128)(2,1)S(1)}, u32[]{:S(2)}, u32[]{:S(2)}) collective-permute-start(bf16[7,32,128]{2,1,0:T(8,128)(2,1)S(1)} %get-tuple-element.135), channel_id=1, source_target_pairs={{0,8},{1,9},{2,10},{3,11},{4,12},{5,13},{6,14},{7,15},{8,0},{9,1},... | collective-permute-start | bytes 172040 | tf_op jit(solution)/shard_map/ppermute | solution.py:632
  46.0 6.2 %collective-permute-start.15 = (bf16[7,32,128]{2,1,0:T(8,128)(2,1)S(1)}, bf16[7,32,128]{2,1,0:T(8,128)(2,1)S(1)}, u32[]{:S(2)}, u32[]{:S(2)}) collective-permute-start(bf16[7,32,128]{2,1,0:T(8,128)(2,1)S(1)} %get-tuple-element.128.after_ref), channel_id=1, source_target_pairs={{0,4},{1,5},{2,6},{3,7},{4,0},{5,1},{6,2},{7,3},{8,12},{9,13},{10,... | collective-permute-start | bytes 172040 | tf_op jit(solution)/shard_map/ppermute | solution.py:632

commit v15 on v12

--- a/solution.py
+++ b/solution.py
@@ -660,13 +660,13 @@
     own_a, *sent[1::2] = call(
         join_kernel,
         [((rows, wide), f32)] + [((blocks + more, rows, 128), bf16)] * (planes // 2 - 1),
-        (kept_a, in_a, *sent[1::2]),
+        (kept_a, in_a, *sent[1::2]), flops=2 * 10**10,
     )
     received = [exchange(shard, k) for k, shard in enumerate(sent, 1)]
     (node_grad,) = call(
         finish_kernel, [((members, node_rows, width), bf16)],
         (place, sent[0], *back[::-1], send_rows, node, from_plus, from_minus),
-        specs=[pltpu.SMEM, pl.ANY], scratch=[trio], final=True,
+        specs=[pltpu.SMEM, pl.ANY], scratch=[trio], final=True, flops=2 * 10**10,
     )
     (weight_grad,) = call(
         weight_kernel, [((rows, 4 * width), f32)], (node_grad, own_a, own_b, *received),

time: 52.2 us -> 51.3 us (0.983)
  waiting for transfers between devices: 18 us -> 17 us
    ppermute x2, waiting for transfers between devices: 5.16 us -> 3.35 us  [swap(): later = lax.ppermute(pair[1], 'patch', second)]
    ppermute x2, starting transfers between devices: 3.34 us -> 1.73 us  [swap(): later = lax.ppermute(pair[1], 'patch', second)]
    ppermute x2, starting transfers between devices: 0.04 us -> 1.29 us  [swap(): return [lax.ppermute(pair[0], 'patch', first), later]]
    ppermute x4, waiting for transfers between devices: 3.23 us -> 4.08 us  [exchange(): return lax.ppermute(sent, 'patch', along_z(count, distance))]
where the time goes in v15:
time: 51.3 us; the launch traced here: 51.1 us
  starting transfers between devices  17.6 us (34%)
  waiting for transfers between devices  17 us (33%)
  Pallas kernels  15.7 us (31%)
  between operations  0.76 us (1%)
    pallas_call x16, Pallas kernels, call(): pl.pallas_call(kernel, out_shape=[jax.ShapeDtypeStruct(*o) if final else...  15.7 us
    ppermute x4, starting transfers between devices, shifted(): lax.ppermute(shard, 'patch', [(i, (i + by) % count) for i in range(count)])  7.25 us
    ppermute x4, waiting for transfers between devices, exchange(): return lax.ppermute(sent, 'patch', along_z(count, distance))  4.08 us
    ppermute x4, starting transfers between devices, exchange(): return lax.ppermute(sent, 'patch', along_z(count, distance))  4.05 us
    ppermute x1, waiting for transfers between devices, body(): y_a = lax.ppermute(y_sent, 'patch', flop)  3.75 us
    ppermute x4, waiting for transfers between devices, shifted(): lax.ppermute(shard, 'patch', [(i, (i + by) % count) for i in range(count)])  3.75 us
    ppermute x2, waiting for transfers between devices, swap(): later = lax.ppermute(pair[1], 'patch', second)  3.35 us
    ppermute x1, starting transfers between devices, body(): y_b = lax.ppermute(y_sent, 'patch', flop)  2.07 us
  transfers between devices with their start and end apart: 18, of which 10 were waited for; matrix products, arithmetic and copies ran while one was open for 0% of the time, Pallas kernels for 18%

profile of v15, /device:TPU:0, one launch (start us, length us, event | category | flops | bytes accessed | tf_op | source)
XLA Modules:
  0.0 51.1 jit_solution(13886876078817346134)
XLA Ops:
  0.6 1.2 %shard_map.104 = (bf16[2,3,16,512]{3,2,1,0:T(8,128)(2,1)S(1)}, bf16[2,3,16,512]{3,2,1,0:T(8,128)(2,1)S(1)}, bf16[2,1,16,512]{3,2,1,0:T(8,128)(2,1)S(1)}, bf16[2,...) custom-call(s32[1,8,16]{2,1,0:T(8,128)} %send_ref.1, bf16[2,128,512]{2,1,0:T(8,128)(2,1)} %x_hbm.1), custom_call_target="tpu_custom_call" | custom-call | flops 1000000 | bytes 10000 | tf_op jit(solution)/shard_map/pallas_call | solution.py:507
  1.8 3.1 %collective-permute-start = (bf16[2,3,16,512]{3,2,1,0:T(8,128)(2,1)S(1)}, bf16[2,3,16,512]{3,2,1,0:T(8,128)(2,1)S(1)}, u32[]{:S(2)}, u32[]{:S(2)}) collective-permute-start(bf16[2,3,16,512]{3,2,1,0:T(8,128)(2,1)S(1)} %get-tuple-element.74), channel_id=1, source_target_pairs={{0,4},{1,5},{2,6},{3,7},{4,8},{5,9},{6,10},{7,11},{8,12},{9,13},{1... | collective-permute-start | bytes 294920 | tf_op jit(solution)/shard_map/ppermute | solution.py:28
  4.9 2.1 %collective-permute-start.1 = (bf16[2,3,16,512]{3,2,1,0:T(8,128)(2,1)S(1)}, bf16[2,3,16,512]{3,2,1,0:T(8,128)(2,1)S(1)}, u32[]{:S(2)}, u32[]{:S(2)}) collective-permute-start(bf16[2,3,16,512]{3,2,1,0:T(8,128)(2,1)S(1)} %get-tuple-element.75), channel_id=1, source_target_pairs={{0,12},{1,13},{2,14},{3,15},{4,0},{5,1},{6,2},{7,3},{8,4},{9,5},{1... | collective-permute-start | bytes 294920 | tf_op jit(solution)/shard_map/ppermute | solution.py:28
  7.0 2.6 %shard_map.105 = (bf16[8,2,128,128]{3,2,1,0:T(8,128)(2,1)S(1)}, bf16[8,2,128,128]{3,2,1,0:T(8,128)(2,1)S(1)}, bf16[8,2,128,128]{3,2,1,0:T(8,128)(2,1)S(1)}, bf16...) custom-call(bf16[2,1,16,512]{3,2,1,0:T(8,128)(2,1)S(1)} %get-tuple-e, ...), custom_call_target="tpu_custom_call" | custom-call | flops 1000000 | bytes 10000 | tf_op jit(solution)/shard_map/pallas_call | solution.py:507
  9.7 0.8 %collective-permute-done.plus_ref = bf16[2,3,16,512]{3,2,1,0:T(8,128)(2,1)S(1)} collective-permute-done((bf16[2,3,16,512]{3,2,1,0:T(8,128)(2,1)S(1)}, bf16[2,3,16,512]{3,2,1,0:T(8,128)(2,1)S(1)}, u32[]{:S(2)}, u32[]{:S(2)}) %collective-permute-start) | collective-permute-done | bytes 98336 | tf_op jit(solution)/shard_map/ppermute | solution.py:28
  10.4 0.8 %collective-permute-done.1.minus_ref = bf16[2,3,16,512]{3,2,1,0:T(8,128)(2,1)S(1)} collective-permute-done((bf16[2,3,16,512]{3,2,1,0:T(8,128)(2,1)S(1)}, bf16[2,3,16,512]{3,2,1,0:T(8,128)(2,1)S(1)}, u32[]{:S(2)}, u32[]{:S(2)}) %collective-permute-start.1) | collective-permute-done | bytes 98336 | tf_op jit(solution)/shard_map/ppermute | solution.py:28
  11.3 1.7 %collective-permute-start.2 = (bf16[2,3,16,512]{3,2,1,0:T(8,128)(2,1)S(1)}, bf16[2,3,16,512]{3,2,1,0:T(8,128)(2,1)S(1)}, u32[]{:S(2)}, u32[]{:S(2)}) collective-permute-start(bf16[2,3,16,512]{3,2,1,0:T(8,128)(2,1)S(1)} %get-tuple-element.76.after_ref), channel_id=1, source_target_pairs={{0,15},{1,2},{2,1},{3,4},{4,3},{5,6},{6,5},{7,8},{8,7},{9,10},{10,... | collective-permute-start | bytes 294920 | tf_op jit(solution)/shard_map/ppermute | solution.py:43
  13.0 0.0 collective-permute-start.3
  13.0 1.4 %shard_map.108.refs_4_.refs_12_ = f32[256,128]{1,0:T(8,128)S(1)} custom-call(bf16[2,3,16,512]{3,2,1,0:T(8,128)(2,1)S(1)} %get-tuple-element.76.after_ref, s32[128,256]{1,0:T(8,128)S(1)} %get-tuple-element.84.neigh_ref, s32[1,128]{1,0:T(1,128)S(1)} %get-tuple-element.85.count_ref), custom_call_target="tpu_custom_call" | custom-call | flops 1000000 | bytes 10000 | tf_op jit(solution)/shard_map/pallas_call | solution.py:507
  14.5 1.4 %shard_map.109 = (f32[3,2,128,512]{3,2,1,0:T(8,128)S(1)}, f32[2,2,8,512]{3,2,1,0:T(8,128)S(1)}, f32[3,2,128,512]{3,2,1,0:T(8,128)S(1)}, f32[2,2,8,512]{3,2,1,0:T...) custom-call(bf16[8,2,128,128]{3,2,1,0:T(8,128)(2,1)S(1)} %get-tuple-, ...), custom_call_target="tpu_custom_call" | custom-call | flops 1000000 | bytes 10000 | tf_op jit(solution)/shard_map/pallas_call | solution.py:507
  15.8 2.3 %collective-permute-done.2.second_in = bf16[2,3,16,512]{3,2,1,0:T(8,128)(2,1)S(1)} collective-permute-done((bf16[2,3,16,512]{3,2,1,0:T(8,128)(2,1)S(1)}, bf16[2,3,16,512]{3,2,1,0:T(8,128)(2,1)S(1)}, u32[]{:S(2)}, u32[]{:S(2)}) %collective-permute-start.2) | collective-permute-done | bytes 98336 | tf_op jit(solution)/shard_map/ppermute | solution.py:43
  18.1 0.0 collective-permute-done.3.first_in
  18.1 0.6 %shard_map.107 = (bf16[4,2,128,128]{3,2,1,0:T(8,128)(2,1)S(1)}, bf16[4,2,128,128]{3,2,1,0:T(8,128)(2,1)S(1)}, bf16[4,2,128,128]{3,2,1,0:T(8,128)(2,1)S(1)}, bf16...) custom-call(s32[1]{0:T(128)} %bitcast.me_ref, bf16[2,3,16,512]{3,2,1,0:T(8,128)(2,1)S(1)} %collective-permute-done.2.second_in, ...), custom_call_target="tpu_custom_call" | custom-call | flops 1000000 | bytes 10000 | tf_op jit(solution)/shard_map/pallas_call | solution.py:507
  18.7 3.8 %shard_map.112 = (f32[4,32,1536]{2,1,0:T(8,128)S(1)}, f32[4,32,1536]{2,1,0:T(8,128)S(1)}, bf16[4,32,1536]{2,1,0:T(8,128)(2,1)S(1)}, bf16[4,32,1536]{2,1,0:T(8,12...) custom-call(s32[1]{0:T(128)} %bitcast.me_ref, ...), custom_call_target="tpu_custom_call" | custom-call | flops 1000000 | bytes 10000 | tf_op jit(solution)/shard_map/pallas_call | solution.py:507
  22.5 0.1 collective-permute-start.6
  22.6 0.5 collective-permute-start.5
  23.1 1.2 %collective-permute-done.6 = bf16[4,32,1536]{2,1,0:T(8,128)(2,1)S(1)} collective-permute-done((bf16[4,32,1536]{2,1,0:T(8,128)(2,1)S(1)}, bf16[4,32,1536]{2,1,0:T(8,128)(2,1)S(1)}, u32[]{:S(2)}, u32[]{:S(2)}) %collective-permute-start.6) | collective-permute-done | bytes 393248 | tf_op jit(solution)/shard_map/ppermute | solution.py:609
  24.3 0.1 add_convert_fusion
  24.4 0.1 collective-permute-start.7
  24.5 1.5 %shard_map.110 = (f32[4,32,512]{2,1,0:T(8,128)S(1)}, f32[4,32,512]{2,1,0:T(8,128)S(1)}, bf16[4,32,512]{2,1,0:T(8,128)(2,1)S(1)}, bf16[4,32,512]{2,1,0:T(8,128)(2...) custom-call(s32[1]{0:T(128)} %bitcast.me_ref, ...), custom_call_target="tpu_custom_call" | custom-call | flops 1000000 | bytes 10000 | tf_op jit(solution)/shard_map/pallas_call | solution.py:507
  26.0 0.2 collective-permute-start.4
  26.2 0.4 collective-permute-start.11
  26.6 0.8 %collective-permute-done.4.refs_1_ = bf16[4,32,512]{2,1,0:T(8,128)(2,1)S(1)} collective-permute-done((bf16[4,32,512]{2,1,0:T(8,128)(2,1)S(1)}, bf16[4,32,512]{2,1,0:T(8,128)(2,1)S(1)}, u32[]{:S(2)}, u32[]{:S(2)}) %collective-permute-start.4) | collective-permute-done | bytes 131104 | tf_op jit(solution)/shard_map/ppermute | solution.py:609
  27.5 2.1 %collective-permute-start.10 = (bf16[4,32,512]{2,1,0:T(8,128)(2,1)S(1)}, bf16[4,32,512]{2,1,0:T(8,128)(2,1)S(1)}, u32[]{:S(2)}, u32[]{:S(2)}) collective-permute-start(bf16[4,32,512]{2,1,0:T(8,128)(2,1)S(1)} %shard_map.111.refs_0_), channel_id=1, source_target_pairs={{0,2},{1,3},{2,0},{3,1},{4,6},{5,7},{6,4},{7,5},{8,10},{9,11},{10,... | collective-permute-start | bytes 393224 | tf_op jit(solution)/shard_map/ppermute | solution.py:623
  29.6 1.0 %shard_map.113 = (f32[2,128,512]{2,1,0:T(8,128)S(1)}, bf16[2,3,16,512]{3,2,1,0:T(8,128)(2,1)S(1)}, bf16[2,3,16,512]{3,2,1,0:T(8,128)(2,1)S(1)}, bf16[2,1,16,512]...) custom-call(bf16[4,32,512]{2,1,0:T(8,128)(2,1)S(1)} %shard_map.111.refs_0_, ...), custom_call_target="tpu_custom_call" | custom-call | flops 1000000 | bytes 10000 | tf_op jit(solution)/shard_map/pallas_call | solution.py:507
  30.6 0.8 %collective-permute-start.8 = (bf16[2,3,16,512]{3,2,1,0:T(8,128)(2,1)S(1)}, bf16[2,3,16,512]{3,2,1,0:T(8,128)(2,1)S(1)}, u32[]{:S(2)}, u32[]{:S(2)}) collective-permute-start(bf16[2,3,16,512]{3,2,1,0:T(8,128)(2,1)S(1)} %get-tuple-element.122), channel_id=1, source_target_pairs={{0,12},{1,13},{2,14},{3,15},{4,0},{5,1},{6,2},{7,3},{8,4},{9,5},{1... | collective-permute-start | bytes 294920 | tf_op jit(solution)/shard_map/ppermute | solution.py:28
  31.3 0.0 collective-permute-done.5.core_in
  31.3 1.3 %collective-permute-start.9 = (bf16[2,3,16,512]{3,2,1,0:T(8,128)(2,1)S(1)}, bf16[2,3,16,512]{3,2,1,0:T(8,128)(2,1)S(1)}, u32[]{:S(2)}, u32[]{:S(2)}) collective-permute-start(bf16[2,3,16,512]{3,2,1,0:T(8,128)(2,1)S(1)} %get-tuple-element.123), channel_id=1, source_target_pairs={{0,4},{1,5},{2,6},{3,7},{4,8},{5,9},{6,10},{7,11},{8,12},{9,13},{1... | collective-permute-start | bytes 294920 | tf_op jit(solution)/shard_map/ppermute | solution.py:28
  32.7 3.8 %collective-permute-done.7.y_in = bf16[4,32,1536]{2,1,0:T(8,128)(2,1)S(1)} collective-permute-done((bf16[4,32,1536]{2,1,0:T(8,128)(2,1)S(1)}, bf16[4,32,1536]{2,1,0:T(8,128)(2,1)S(1)}, u32[]{:S(2)}, u32[]{:S(2)}) %collective-permute-start.7) | collective-permute-done | bytes 393248 | tf_op jit(solution)/shard_map/ppermute | solution.py:616
  36.4 0.1 shard_map.114
  36.6 0.1 collective-permute-start.14
  36.6 0.0 collective-permute-done.8.plus_ref
  36.6 2.1 %collective-permute-done.9.minus_ref = bf16[2,3,16,512]{3,2,1,0:T(8,128)(2,1)S(1)} collective-permute-done((bf16[2,3,16,512]{3,2,1,0:T(8,128)(2,1)S(1)}, bf16[2,3,16,512]{3,2,1,0:T(8,128)(2,1)S(1)}, u32[]{:S(2)}, u32[]{:S(2)}) %collective-permute-start.9) | collective-permute-done | bytes 98336 | tf_op jit(solution)/shard_map/ppermute | solution.py:28
  38.8 0.1 collective-permute-start.12
  38.9 1.2 %collective-permute-start.13 = (bf16[2,3,16,512]{3,2,1,0:T(8,128)(2,1)S(1)}, bf16[2,3,16,512]{3,2,1,0:T(8,128)(2,1)S(1)}, u32[]{:S(2)}, u32[]{:S(2)}) collective-permute-start(bf16[2,3,16,512]{3,2,1,0:T(8,128)(2,1)S(1)} %get-tuple-element.124.refs_0_), channel_id=1, source_target_pairs={{0,1},{1,0},{2,3},{3,2},{4,5},{5,4},{6,7},{7,6},{8,9},{9,8},{10,11... | collective-permute-start | bytes 294920 | tf_op jit(solution)/shard_map/ppermute | solution.py:44
  40.1 0.0 collective-permute-done.11.refs_4_
  40.1 0.0 collective-permute-done.10.refs_2_
  40.1 0.1 shard_map.116
  40.2 0.4 collective-permute-start.15
  40.7 0.6 %collective-permute-start.17 = (bf16[7,32,128]{2,1,0:T(8,128)(2,1)S(1)}, bf16[7,32,128]{2,1,0:T(8,128)(2,1)S(1)}, u32[]{:S(2)}, u32[]{:S(2)}) collective-permute-start(bf16[7,32,128]{2,1,0:T(8,128)(2,1)S(1)} %get-tuple-element.135), channel_id=1, source_target_pairs={{0,8},{1,9},{2,10},{3,11},{4,12},{5,13},{6,14},{7,15},{8,0},{9,1},... | collective-permute-start | bytes 172040 | tf_op jit(solution)/shard_map/ppermute | solution.py:633
  41.2 0.5 %collective-permute-done.14.in_a = bf16[18,32,128]{2,1,0:T(8,128)(2,1)S(1)} collective-permute-done((bf16[18,32,128]{2,1,0:T(8,128)(2,1)S(1)}, bf16[18,32,128]{2,1,0:T(8,128)(2,1)S(1)}, u32[]{:S(2)}, u32[]{:S(2)}) %collective-permute-start.14) | collective-permute-done | bytes 147488 | tf_op jit(solution)/shard_map/ppermute | solution.py:633
  41.8 3.0 %collective-permute-start.16 = (bf16[16,32,128]{2,1,0:T(8,128)(2,1)S(1)}, bf16[16,32,128]{2,1,0:T(8,128)(2,1)S(1)}, u32[]{:S(2)}, u32[]{:S(2)}) collective-permute-start(bf16[16,32,128]{2,1,0:T(8,128)(2,1)S(1)} %get-tuple-element.134), channel_id=1, source_target_pairs={{0,12},{1,13},{2,14},{3,15},{4,8},{5,9},{6,10},{7,11},{8,4},{9,5},... | collective-permute-start | bytes 393224 | tf_op jit(solution)/shard_map/ppermute | solution.py:633
  44.8 1.1 %collective-permute-done.12.second_in = bf16[2,3,16,512]{3,2,1,0:T(8,128)(2,1)S(1)} collective-permute-done((bf16[2,3,16,512]{3,2,1,0:T(8,128)(2,1)S(1)}, bf16[2,3,16,512]{3,2,1,0:T(8,128)(2,1)S(1)}, u32[]{:S(2)}, u32[]{:S(2)}) %collective-permute-start.12) | collective-permute-done | bytes 98336 | tf_op jit(solution)/shard_map/ppermute | solution.py:43
  45.8 0.0 collective-permute-done.13.first_in
  45.9 1.0 %shard_map.117.after_ref = bf16[2,128,512]{2,1,0:T(8,128)(2,1)} custom-call(s32[1]{0:T(128)} %bitcast.me_ref, bf16[7,32,128]{2,1,0:T(8,128)(2,1)S(1)} %get-tuple-element.128.after_ref, bf16[2,3,16,512]{3,2,1,0:T(8,128)(2,1)S(1)} %collective-permute-done.12.second_in, bf16[2,3,16,512]{3,2,1,0:T(8,128)(2,1)S(1)} %collective-permute-done.13.first_in, ...), custom_call_target="tpu_custom_call" | custom-call | flops 20000000000 | bytes 10000 | tf_op jit(solution)/shard_map/pallas_call | solution.py:507
  46.8 3.5 %collective-permute-done.17.refs_2_ = bf16[7,32,128]{2,1,0:T(8,128)(2,1)S(1)} collective-permute-done((bf16[7,32,128]{2,1,0:T(8,128)(2,1)S(1)}, bf16[7,32,128]{2,1,0:T(8,128)(2,1)S(1)}, u32[]{:S(2)}, u32[]{:S(2)}) %collective-permute-start.17) | collective-permute-done | bytes 57376 | tf_op jit(solution)/shard_map/ppermute | solution.py:633
  50.4 0.0 collective-permute-done.16.refs_1_
  50.4 0.7 %shard_map.119 = f32[32,2048]{1,0:T(8,128)} custom-call(bf16[2,128,512]{2,1,0:T(8,128)(2,1)} %shard_map.117.after_ref, f32[32,1152]{1,0:T(8,128)S(1)} %get-tuple-element.132.own_a, f32[32,896]{1,0:T(8,128)S(1)} %get-tuple-element.133.own_b, bf16[7,32,128]{2,1,0:T(8,128)(2,1)S(1)} %collective-permute-done.15.refs_0_, ...), custom_call_target="tpu_custom_call" | custom-call | flops 1000000 | bytes 10000 | tf_op jit(solution)/shard_map/pallas_call | solution.py:507
  (7 shorter events, 0.1 us)
Async XLA Ops:
  1.8 8.6 %collective-permute-start = (bf16[2,3,16,512]{3,2,1,0:T(8,128)(2,1)S(1)}, bf16[2,3,16,512]{3,2,1,0:T(8,128)(2,1)S(1)}, u32[]{:S(2)}, u32[]{:S(2)}) collective-permute-start(bf16[2,3,16,512]{3,2,1,0:T(8,128)(2,1)S(1)} %get-tuple-element.74), channel_id=1, source_target_pairs={{0,4},{1,5},{2,6},{3,7},{4,8},{5,9},{6,10},{7,11},{8,12},{9,13},{1... | collective-permute-start | bytes 294920 | tf_op jit(solution)/shard_map/ppermute | solution.py:28
  4.9 6.4 %collective-permute-start.1 = (bf16[2,3,16,512]{3,2,1,0:T(8,128)(2,1)S(1)}, bf16[2,3,16,512]{3,2,1,0:T(8,128)(2,1)S(1)}, u32[]{:S(2)}, u32[]{:S(2)}) collective-permute-start(bf16[2,3,16,512]{3,2,1,0:T(8,128)(2,1)S(1)} %get-tuple-element.75), channel_id=1, source_target_pairs={{0,12},{1,13},{2,14},{3,15},{4,0},{5,1},{6,2},{7,3},{8,4},{9,5},{1... | collective-permute-start | bytes 294920 | tf_op jit(solution)/shard_map/ppermute | solution.py:28
  11.3 6.8 %collective-permute-start.2 = (bf16[2,3,16,512]{3,2,1,0:T(8,128)(2,1)S(1)}, bf16[2,3,16,512]{3,2,1,0:T(8,128)(2,1)S(1)}, u32[]{:S(2)}, u32[]{:S(2)}) collective-permute-start(bf16[2,3,16,512]{3,2,1,0:T(8,128)(2,1)S(1)} %get-tuple-element.76.after_ref), channel_id=1, source_target_pairs={{0,15},{1,2},{2,1},{3,4},{4,3},{5,6},{6,5},{7,8},{8,7},{9,10},{10,... | collective-permute-start | bytes 294920 | tf_op jit(solution)/shard_map/ppermute | solution.py:43
  13.0 5.1 %collective-permute-start.3 = (bf16[2,3,16,512]{3,2,1,0:T(8,128)(2,1)S(1)}, bf16[2,3,16,512]{3,2,1,0:T(8,128)(2,1)S(1)}, u32[]{:S(2)}, u32[]{:S(2)}) collective-permute-start(bf16[2,3,16,512]{3,2,1,0:T(8,128)(2,1)S(1)} %get-tuple-element.77), channel_id=1, source_target_pairs={{0,1},{1,0},{2,3},{3,2},{4,5},{5,4},{6,7},{7,6},{8,9},{9,8},{10,11... | collective-permute-start | bytes 294920 | tf_op jit(solution)/shard_map/ppermute | solution.py:44
  22.5 1.8 %collective-permute-start.6 = (bf16[4,32,1536]{2,1,0:T(8,128)(2,1)S(1)}, bf16[4,32,1536]{2,1,0:T(8,128)(2,1)S(1)}, u32[]{:S(2)}, u32[]{:S(2)}) collective-permute-start(bf16[4,32,1536]{2,1,0:T(8,128)(2,1)S(1)} %get-tuple-element.118), channel_id=1, source_target_pairs={{0,1},{1,0},{2,3},{3,2},{4,5},{5,4},{6,7},{7,6},{8,9},{9,8},{10,11... | collective-permute-start | bytes 1179656 | tf_op jit(solution)/shard_map/ppermute | solution.py:609
  22.6 8.7 %collective-permute-start.5 = (bf16[4,32,1536]{2,1,0:T(8,128)(2,1)S(1)}, bf16[4,32,1536]{2,1,0:T(8,128)(2,1)S(1)}, u32[]{:S(2)}, u32[]{:S(2)}) collective-permute-start(bf16[4,32,1536]{2,1,0:T(8,128)(2,1)S(1)} %get-tuple-element.116), channel_id=1, source_target_pairs={{0,1},{1,0},{2,3},{3,2},{4,5},{5,4},{6,7},{7,6},{8,9},{9,8},{10,11... | collective-permute-start | bytes 1179656 | tf_op jit(solution)/shard_map/ppermute | solution.py:609
  24.4 12.0 %collective-permute-start.7 = (bf16[4,32,1536]{2,1,0:T(8,128)(2,1)S(1)}, bf16[4,32,1536]{2,1,0:T(8,128)(2,1)S(1)}, u32[]{:S(2)}, u32[]{:S(2)}) collective-permute-start(bf16[4,32,1536]{2,1,0:T(8,128)(2,1)S(1)} %add_convert_fusion), channel_id=1, source_target_pairs={{0,2},{1,3},{2,0},{3,1},{4,6},{5,7},{6,4},{7,5},{8,10},{9,11},{10,... | collective-permute-start | bytes 1179656 | tf_op jit(solution)/shard_map/ppermute | solution.py:616
  26.0 1.4 %collective-permute-start.4 = (bf16[4,32,512]{2,1,0:T(8,128)(2,1)S(1)}, bf16[4,32,512]{2,1,0:T(8,128)(2,1)S(1)}, u32[]{:S(2)}, u32[]{:S(2)}) collective-permute-start(bf16[4,32,512]{2,1,0:T(8,128)(2,1)S(1)} %get-tuple-element.91), channel_id=1, source_target_pairs={{0,1},{1,0},{2,3},{3,2},{4,5},{5,4},{6,7},{7,6},{8,9},{9,8},{10,11... | collective-permute-start | bytes 393224 | tf_op jit(solution)/shard_map/ppermute | solution.py:609
  26.2 13.9 %collective-permute-start.11 = (bf16[4,32,512]{2,1,0:T(8,128)(2,1)S(1)}, bf16[4,32,512]{2,1,0:T(8,128)(2,1)S(1)}, u32[]{:S(2)}, u32[]{:S(2)}) collective-permute-start(bf16[4,32,512]{2,1,0:T(8,128)(2,1)S(1)} %get-tuple-element.127), channel_id=1, source_target_pairs={{0,1},{1,0},{2,3},{3,2},{4,5},{5,4},{6,7},{7,6},{8,9},{9,8},{10,11... | collective-permute-start | bytes 393224 | tf_op jit(solution)/shard_map/ppermute | solution.py:609
  27.5 12.7 %collective-permute-start.10 = (bf16[4,32,512]{2,1,0:T(8,128)(2,1)S(1)}, bf16[4,32,512]{2,1,0:T(8,128)(2,1)S(1)}, u32[]{:S(2)}, u32[]{:S(2)}) collective-permute-start(bf16[4,32,512]{2,1,0:T(8,128)(2,1)S(1)} %shard_map.111.refs_0_), channel_id=1, source_target_pairs={{0,2},{1,3},{2,0},{3,1},{4,6},{5,7},{6,4},{7,5},{8,10},{9,11},{10,... | collective-permute-start | bytes 393224 | tf_op jit(solution)/shard_map/ppermute | solution.py:623
  30.6 6.1 %collective-permute-start.8 = (bf16[2,3,16,512]{3,2,1,0:T(8,128)(2,1)S(1)}, bf16[2,3,16,512]{3,2,1,0:T(8,128)(2,1)S(1)}, u32[]{:S(2)}, u32[]{:S(2)}) collective-permute-start(bf16[2,3,16,512]{3,2,1,0:T(8,128)(2,1)S(1)} %get-tuple-element.122), channel_id=1, source_target_pairs={{0,12},{1,13},{2,14},{3,15},{4,0},{5,1},{6,2},{7,3},{8,4},{9,5},{1... | collective-permute-start | bytes 294920 | tf_op jit(solution)/shard_map/ppermute | solution.py:28
  31.3 7.4 %collective-permute-start.9 = (bf16[2,3,16,512]{3,2,1,0:T(8,128)(2,1)S(1)}, bf16[2,3,16,512]{3,2,1,0:T(8,128)(2,1)S(1)}, u32[]{:S(2)}, u32[]{:S(2)}) collective-permute-start(bf16[2,3,16,512]{3,2,1,0:T(8,128)(2,1)S(1)} %get-tuple-element.123), channel_id=1, source_target_pairs={{0,4},{1,5},{2,6},{3,7},{4,8},{5,9},{6,10},{7,11},{8,12},{9,13},{1... | collective-permute-start | bytes 294920 | tf_op jit(solution)/shard_map/ppermute | solution.py:28
  36.6 5.2 %collective-permute-start.14 = (bf16[18,32,128]{2,1,0:T(8,128)(2,1)S(1)}, bf16[18,32,128]{2,1,0:T(8,128)(2,1)S(1)}, u32[]{:S(2)}, u32[]{:S(2)}) collective-permute-start(bf16[18,32,128]{2,1,0:T(8,128)(2,1)S(1)} %get-tuple-element.119.after_ref), channel_id=1, source_target_pairs={{0,4},{1,5},{2,6},{3,7},{4,0},{5,1},{6,2},{7,3},{8,12},{9,13},{10,... | collective-permute-start | bytes 442376 | tf_op jit(solution)/shard_map/ppermute | solution.py:633
  38.8 7.0 %collective-permute-start.12 = (bf16[2,3,16,512]{3,2,1,0:T(8,128)(2,1)S(1)}, bf16[2,3,16,512]{3,2,1,0:T(8,128)(2,1)S(1)}, u32[]{:S(2)}, u32[]{:S(2)}) collective-permute-start(bf16[2,3,16,512]{3,2,1,0:T(8,128)(2,1)S(1)} %get-tuple-element.129), channel_id=1, source_target_pairs={{0,15},{1,2},{2,1},{3,4},{4,3},{5,6},{6,5},{7,8},{8,7},{9,10},{10,... | collective-permute-start | bytes 294920 | tf_op jit(solution)/shard_map/ppermute | solution.py:43
  38.9 7.0 %collective-permute-start.13 = (bf16[2,3,16,512]{3,2,1,0:T(8,128)(2,1)S(1)}, bf16[2,3,16,512]{3,2,1,0:T(8,128)(2,1)S(1)}, u32[]{:S(2)}, u32[]{:S(2)}) collective-permute-start(bf16[2,3,16,512]{3,2,1,0:T(8,128)(2,1)S(1)} %get-tuple-element.124.refs_0_), channel_id=1, source_target_pairs={{0,1},{1,0},{2,3},{3,2},{4,5},{5,4},{6,7},{7,6},{8,9},{9,8},{10,11... | collective-permute-start | bytes 294920 | tf_op jit(solution)/shard_map/ppermute | solution.py:44
  40.2 6.6 %collective-permute-start.15 = (bf16[7,32,128]{2,1,0:T(8,128)(2,1)S(1)}, bf16[7,32,128]{2,1,0:T(8,128)(2,1)S(1)}, u32[]{:S(2)}, u32[]{:S(2)}) collective-permute-start(bf16[7,32,128]{2,1,0:T(8,128)(2,1)S(1)} %get-tuple-element.128.after_ref), channel_id=1, source_target_pairs={{0,4},{1,5},{2,6},{3,7},{4,0},{5,1},{6,2},{7,3},{8,12},{9,13},{10,... | collective-permute-start | bytes 172040 | tf_op jit(solution)/shard_map/ppermute | solution.py:633
  40.7 9.7 %collective-permute-start.17 = (bf16[7,32,128]{2,1,0:T(8,128)(2,1)S(1)}, bf16[7,32,128]{2,1,0:T(8,128)(2,1)S(1)}, u32[]{:S(2)}, u32[]{:S(2)}) collective-permute-start(bf16[7,32,128]{2,1,0:T(8,128)(2,1)S(1)} %get-tuple-element.135), channel_id=1, source_target_pairs={{0,8},{1,9},{2,10},{3,11},{4,12},{5,13},{6,14},{7,15},{8,0},{9,1},... | collective-permute-start | bytes 172040 | tf_op jit(solution)/shard_map/ppermute | solution.py:633
  41.8 4.1 %copy-start = (s32[1,8,16]{2,1,0:T(8,128)S(1)}, s32[1,8,16]{2,1,0:T(8,128)}, u32[]{:S(2)}) copy-start(s32[1,8,16]{2,1,0:T(8,128)} %send_ref.1) | copy-start | bytes 1540
  41.8 8.6 %collective-permute-start.16 = (bf16[16,32,128]{2,1,0:T(8,128)(2,1)S(1)}, bf16[16,32,128]{2,1,0:T(8,128)(2,1)S(1)}, u32[]{:S(2)}, u32[]{:S(2)}) collective-permute-start(bf16[16,32,128]{2,1,0:T(8,128)(2,1)S(1)} %get-tuple-element.134), channel_id=1, source_target_pairs={{0,12},{1,13},{2,14},{3,15},{4,8},{5,9},{6,10},{7,11},{8,4},{9,5},... | collective-permute-start | bytes 393224 | tf_op jit(solution)/shard_map/ppermute | solution.py:633

commit v16 on v15

--- a/solution.py
+++ b/solution.py
@@ -93,7 +93,7 @@
 
 
 def relay_kernel(
-    me_ref, after_ref, own_right, own_left, plus_ref, minus_ref, first_ref, second_ref, both
+    me_ref, after_ref, minus_ref, plus_ref, own_right, own_left, first_ref, second_ref, both
 ):
     for side, own in enumerate((own_right, own_left)):
         both[side, :, 0:1] = own[...]
@@ -470,7 +470,7 @@
     from_swaps(came, me_ref[0] % 2, first_in, second_in)
     for m in range(members):
         pieces = [None] * 8
-        for side, order in enumerate(((1, 4, 7), (0, 6, 5))):
+        for side, order in enumerate(((1, 7, 4), (0, 5, 6))):
             for i, k in enumerate(order):
                 pieces[k] = came[side, m, i]
         pieces[2], pieces[3] = plus_ref[m, 0], minus_ref[m, 0]
@@ -551,7 +551,7 @@
         limit=16,
     )
     outgoing = call(
-        relay_kernel, [three, three], (place, loc[0], own_right, own_left, plus, minus),
+        relay_kernel, [three, three], (place, loc[0], minus, plus, own_right, own_left),
         specs=[pltpu.SMEM, pl.ANY], scratch=[trio],
     )
     arrived = swap(outgoing, 1)
@@ -644,7 +644,7 @@
     in_a = exchange(sent_a, 1)
     outgoing = call(
         relay_kernel, [three, three],
-        (place, sent_a, own_right, own_left, from_plus, from_minus),
+        (place, sent_a, from_plus, from_minus, own_right, own_left),
         specs=[pltpu.SMEM, pl.ANY], scratch=[trio],
     )
     back = swap(outgoing, 1)

time: 51.3 us -> 52.8 us (1.029)
  waiting for transfers between devices: 17 us -> 19 us
    ppermute x2, starting transfers between devices: 1.29 us -> 3.13 us  [swap(): return [lax.ppermute(pair[0], 'patch', first), later]]
    ppermute x2, starting transfers between devices: 1.73 us -> 0.14 us  [swap(): later = lax.ppermute(pair[1], 'patch', second)]
    ppermute x4, waiting for transfers between devices: 3.75 us -> 5.3 us  [shifted(): lax.ppermute(shard, 'patch', [(i, (i + by) % count) for i in range(count)])]
    ppermute x4, starting transfers between devices: 4.05 us -> 3.33 us  [exchange(): return lax.ppermute(sent, 'patch', along_z(count, distance))]
    ppermute x4, waiting for transfers between devices: 4.08 us -> 4.7 us  [exchange(): return lax.ppermute(sent, 'patch', along_z(count, distance))]
where the time goes in v16:
time: 52.8 us; the launch traced here: 52.6 us
  waiting for transfers between devices  19 us (36%)
  starting transfers between devices  17.1 us (32%)
  Pallas kernels  15.7 us (30%)
  between operations  0.79 us (1%)
    pallas_call x16, Pallas kernels, call(): pl.pallas_call(kernel, out_shape=[jax.ShapeDtypeStruct(*o) if final else...  15.7 us
    ppermute x4, starting transfers between devices, shifted(): lax.ppermute(shard, 'patch', [(i, (i + by) % count) for i in range(count)])  7.17 us
    ppermute x4, waiting for transfers between devices, shifted(): lax.ppermute(shard, 'patch', [(i, (i + by) % count) for i in range(count)])  5.3 us
    ppermute x4, waiting for transfers between devices, exchange(): return lax.ppermute(sent, 'patch', along_z(count, distance))  4.7 us
    ppermute x1, waiting for transfers between devices, body(): y_a = lax.ppermute(y_sent, 'patch', flop)  3.75 us
    ppermute x4, starting transfers between devices, exchange(): return lax.ppermute(sent, 'patch', along_z(count, distance))  3.33 us
    ppermute x2, waiting for transfers between devices, swap(): later = lax.ppermute(pair[1], 'patch', second)  3.16 us
    ppermute x2, starting transfers between devices, swap(): return [lax.ppermute(pair[0], 'patch', first), later]  3.13 us
  transfers between devices with their start and end apart: 18, of which 10 were waited for; matrix products, arithmetic and copies ran while one was open for 0% of the time, Pallas kernels for 18%

profile of v16, /device:TPU:0, one launch (start us, length us, event | category | flops | bytes accessed | tf_op | source)
XLA Modules:
  0.0 52.6 jit_solution(14236624818069840920)
XLA Ops:
  0.6 1.2 %shard_map.104 = (bf16[2,3,16,512]{3,2,1,0:T(8,128)(2,1)S(1)}, bf16[2,3,16,512]{3,2,1,0:T(8,128)(2,1)S(1)}, bf16[2,1,16,512]{3,2,1,0:T(8,128)(2,1)S(1)}, bf16[2,...) custom-call(s32[1,8,16]{2,1,0:T(8,128)} %send_ref.1, bf16[2,128,512]{2,1,0:T(8,128)(2,1)} %x_hbm.1), custom_call_target="tpu_custom_call" | custom-call | flops 1000000 | bytes 10000 | tf_op jit(solution)/shard_map/pallas_call | solution.py:507
  1.8 5.1 %collective-permute-start = (bf16[2,3,16,512]{3,2,1,0:T(8,128)(2,1)S(1)}, bf16[2,3,16,512]{3,2,1,0:T(8,128)(2,1)S(1)}, u32[]{:S(2)}, u32[]{:S(2)}) collective-permute-start(bf16[2,3,16,512]{3,2,1,0:T(8,128)(2,1)S(1)} %get-tuple-element.73), channel_id=1, source_target_pairs={{0,12},{1,13},{2,14},{3,15},{4,0},{5,1},{6,2},{7,3},{8,4},{9,5},{1... | collective-permute-start | bytes 294920 | tf_op jit(solution)/shard_map/ppermute | solution.py:28
  6.9 0.0 collective-permute-start.1
  6.9 2.6 %shard_map.105 = (bf16[8,2,128,128]{3,2,1,0:T(8,128)(2,1)S(1)}, bf16[8,2,128,128]{3,2,1,0:T(8,128)(2,1)S(1)}, bf16[8,2,128,128]{3,2,1,0:T(8,128)(2,1)S(1)}, bf16...) custom-call(bf16[2,1,16,512]{3,2,1,0:T(8,128)(2,1)S(1)} %get-tuple-e, ...), custom_call_target="tpu_custom_call" | custom-call | flops 1000000 | bytes 10000 | tf_op jit(solution)/shard_map/pallas_call | solution.py:507
  9.6 0.5 collective-permute-done.minus_ref
  10.1 3.2 %collective-permute-done.1.plus_ref = bf16[2,3,16,512]{3,2,1,0:T(8,128)(2,1)S(1)} collective-permute-done((bf16[2,3,16,512]{3,2,1,0:T(8,128)(2,1)S(1)}, bf16[2,3,16,512]{3,2,1,0:T(8,128)(2,1)S(1)}, u32[]{:S(2)}, u32[]{:S(2)}) %collective-permute-start.1) | collective-permute-done | bytes 98336 | tf_op jit(solution)/shard_map/ppermute | solution.py:28
  13.4 0.1 collective-permute-start.2
  13.5 1.6 %collective-permute-start.3 = (bf16[2,3,16,512]{3,2,1,0:T(8,128)(2,1)S(1)}, bf16[2,3,16,512]{3,2,1,0:T(8,128)(2,1)S(1)}, u32[]{:S(2)}, u32[]{:S(2)}) collective-permute-start(bf16[2,3,16,512]{3,2,1,0:T(8,128)(2,1)S(1)} %get-tuple-element.77), channel_id=1, source_target_pairs={{0,1},{1,0},{2,3},{3,2},{4,5},{5,4},{6,7},{7,6},{8,9},{9,8},{10,11... | collective-permute-start | bytes 294920 | tf_op jit(solution)/shard_map/ppermute | solution.py:44
  15.1 1.4 %shard_map.108.refs_4_.refs_12_ = f32[256,128]{1,0:T(8,128)S(1)} custom-call(bf16[2,3,16,512]{3,2,1,0:T(8,128)(2,1)S(1)} %get-tuple-element.76.after_ref, s32[128,256]{1,0:T(8,128)S(1)} %get-tuple-element.84.neigh_ref, s32[1,128]{1,0:T(1,128)S(1)} %get-tuple-element.85.count_ref), custom_call_target="tpu_custom_call" | custom-call | flops 1000000 | bytes 10000 | tf_op jit(solution)/shard_map/pallas_call | solution.py:507
  16.5 1.3 %shard_map.109 = (f32[3,2,128,512]{3,2,1,0:T(8,128)S(1)}, f32[2,2,8,512]{3,2,1,0:T(8,128)S(1)}, f32[3,2,128,512]{3,2,1,0:T(8,128)S(1)}, f32[2,2,8,512]{3,2,1,0:T...) custom-call(bf16[8,2,128,128]{3,2,1,0:T(8,128)(2,1)S(1)} %get-tuple-, ...), custom_call_target="tpu_custom_call" | custom-call | flops 1000000 | bytes 10000 | tf_op jit(solution)/shard_map/pallas_call | solution.py:507
  17.9 2.3 %collective-permute-done.2.second_in = bf16[2,3,16,512]{3,2,1,0:T(8,128)(2,1)S(1)} collective-permute-done((bf16[2,3,16,512]{3,2,1,0:T(8,128)(2,1)S(1)}, bf16[2,3,16,512]{3,2,1,0:T(8,128)(2,1)S(1)}, u32[]{:S(2)}, u32[]{:S(2)}) %collective-permute-start.2) | collective-permute-done | bytes 98336 | tf_op jit(solution)/shard_map/ppermute | solution.py:43
  20.2 0.0 collective-permute-done.3.first_in
  20.2 0.6 %shard_map.107 = (bf16[4,2,128,128]{3,2,1,0:T(8,128)(2,1)S(1)}, bf16[4,2,128,128]{3,2,1,0:T(8,128)(2,1)S(1)}, bf16[4,2,128,128]{3,2,1,0:T(8,128)(2,1)S(1)}, bf16...) custom-call(s32[1]{0:T(128)} %bitcast.me_ref, bf16[2,3,16,512]{3,2,1,0:T(8,128)(2,1)S(1)} %collective-permute-done.2.second_in, ...), custom_call_target="tpu_custom_call" | custom-call | flops 1000000 | bytes 10000 | tf_op jit(solution)/shard_map/pallas_call | solution.py:507
  20.8 3.8 %shard_map.112 = (f32[4,32,1536]{2,1,0:T(8,128)S(1)}, f32[4,32,1536]{2,1,0:T(8,128)S(1)}, bf16[4,32,1536]{2,1,0:T(8,128)(2,1)S(1)}, bf16[4,32,1536]{2,1,0:T(8,12...) custom-call(s32[1]{0:T(128)} %bitcast.me_ref, ...), custom_call_target="tpu_custom_call" | custom-call | flops 1000000 | bytes 10000 | tf_op jit(solution)/shard_map/pallas_call | solution.py:507
  24.6 0.1 collective-permute-start.6
  24.7 0.5 collective-permute-start.5
  25.2 1.2 %collective-permute-done.6 = bf16[4,32,1536]{2,1,0:T(8,128)(2,1)S(1)} collective-permute-done((bf16[4,32,1536]{2,1,0:T(8,128)(2,1)S(1)}, bf16[4,32,1536]{2,1,0:T(8,128)(2,1)S(1)}, u32[]{:S(2)}, u32[]{:S(2)}) %collective-permute-start.6) | collective-permute-done | bytes 393248 | tf_op jit(solution)/shard_map/ppermute | solution.py:609
  26.4 0.1 add_convert_fusion
  26.5 0.1 collective-permute-start.7
  26.6 1.5 %shard_map.110 = (f32[4,32,512]{2,1,0:T(8,128)S(1)}, f32[4,32,512]{2,1,0:T(8,128)S(1)}, bf16[4,32,512]{2,1,0:T(8,128)(2,1)S(1)}, bf16[4,32,512]{2,1,0:T(8,128)(2...) custom-call(s32[1]{0:T(128)} %bitcast.me_ref, ...), custom_call_target="tpu_custom_call" | custom-call | flops 1000000 | bytes 10000 | tf_op jit(solution)/shard_map/pallas_call | solution.py:507
  28.1 0.2 collective-permute-start.4
  28.3 0.4 collective-permute-start.11
  28.7 0.8 %collective-permute-done.4.refs_1_ = bf16[4,32,512]{2,1,0:T(8,128)(2,1)S(1)} collective-permute-done((bf16[4,32,512]{2,1,0:T(8,128)(2,1)S(1)}, bf16[4,32,512]{2,1,0:T(8,128)(2,1)S(1)}, u32[]{:S(2)}, u32[]{:S(2)}) %collective-permute-start.4) | collective-permute-done | bytes 131104 | tf_op jit(solution)/shard_map/ppermute | solution.py:609
  29.6 2.1 %collective-permute-start.10 = (bf16[4,32,512]{2,1,0:T(8,128)(2,1)S(1)}, bf16[4,32,512]{2,1,0:T(8,128)(2,1)S(1)}, u32[]{:S(2)}, u32[]{:S(2)}) collective-permute-start(bf16[4,32,512]{2,1,0:T(8,128)(2,1)S(1)} %shard_map.111.refs_0_), channel_id=1, source_target_pairs={{0,2},{1,3},{2,0},{3,1},{4,6},{5,7},{6,4},{7,5},{8,10},{9,11},{10,... | collective-permute-start | bytes 393224 | tf_op jit(solution)/shard_map/ppermute | solution.py:623
  31.6 1.0 %shard_map.113 = (f32[2,128,512]{2,1,0:T(8,128)S(1)}, bf16[2,3,16,512]{3,2,1,0:T(8,128)(2,1)S(1)}, bf16[2,3,16,512]{3,2,1,0:T(8,128)(2,1)S(1)}, bf16[2,1,16,512]...) custom-call(bf16[4,32,512]{2,1,0:T(8,128)(2,1)S(1)} %shard_map.111.refs_0_, ...), custom_call_target="tpu_custom_call" | custom-call | flops 1000000 | bytes 10000 | tf_op jit(solution)/shard_map/pallas_call | solution.py:507
  32.7 0.1 collective-permute-start.8
  32.7 0.0 collective-permute-done.5.core_in
  32.7 2.0 %collective-permute-start.9 = (bf16[2,3,16,512]{3,2,1,0:T(8,128)(2,1)S(1)}, bf16[2,3,16,512]{3,2,1,0:T(8,128)(2,1)S(1)}, u32[]{:S(2)}, u32[]{:S(2)}) collective-permute-start(bf16[2,3,16,512]{3,2,1,0:T(8,128)(2,1)S(1)} %get-tuple-element.121), channel_id=1, source_target_pairs={{0,4},{1,5},{2,6},{3,7},{4,8},{5,9},{6,10},{7,11},{8,12},{9,13},{1... | collective-permute-start | bytes 294920 | tf_op jit(solution)/shard_map/ppermute | solution.py:28
  34.8 3.8 %collective-permute-done.7.y_in = bf16[4,32,1536]{2,1,0:T(8,128)(2,1)S(1)} collective-permute-done((bf16[4,32,1536]{2,1,0:T(8,128)(2,1)S(1)}, bf16[4,32,1536]{2,1,0:T(8,128)(2,1)S(1)}, u32[]{:S(2)}, u32[]{:S(2)}) %collective-permute-start.7) | collective-permute-done | bytes 393248 | tf_op jit(solution)/shard_map/ppermute | solution.py:616
  38.5 0.1 shard_map.114
  38.6 0.1 collective-permute-start.14
  38.7 0.0 collective-permute-done.8.minus_ref.plus_ref
  38.7 1.5 %collective-permute-done.9.plus_ref.minus_ref = bf16[2,3,16,512]{3,2,1,0:T(8,128)(2,1)S(1)} collective-permute-done((bf16[2,3,16,512]{3,2,1,0:T(8,128)(2,1)S(1)}, bf16[2,3,16,512]{3,2,1,0:T(8,128)(2,1)S(1)}, u32[]{:S(2)}, u32[]{:S(2)}) %collective-permute-start.9) | collective-permute-done | bytes 98336 | tf_op jit(solution)/shard_map/ppermute | solution.py:28
  40.3 0.1 collective-permute-start.12
  40.4 1.5 %collective-permute-start.13 = (bf16[2,3,16,512]{3,2,1,0:T(8,128)(2,1)S(1)}, bf16[2,3,16,512]{3,2,1,0:T(8,128)(2,1)S(1)}, u32[]{:S(2)}, u32[]{:S(2)}) collective-permute-start(bf16[2,3,16,512]{3,2,1,0:T(8,128)(2,1)S(1)} %get-tuple-element.124.refs_0_), channel_id=1, source_target_pairs={{0,1},{1,0},{2,3},{3,2},{4,5},{5,4},{6,7},{7,6},{8,9},{9,8},{10,11... | collective-permute-start | bytes 294920 | tf_op jit(solution)/shard_map/ppermute | solution.py:44
  41.9 0.0 collective-permute-done.11.refs_4_
  41.9 0.0 collective-permute-done.10.refs_2_
  41.9 0.1 shard_map.116
  42.0 0.1 collective-permute-start.15
  42.0 0.6 %collective-permute-start.17 = (bf16[7,32,128]{2,1,0:T(8,128)(2,1)S(1)}, bf16[7,32,128]{2,1,0:T(8,128)(2,1)S(1)}, u32[]{:S(2)}, u32[]{:S(2)}) collective-permute-start(bf16[7,32,128]{2,1,0:T(8,128)(2,1)S(1)} %get-tuple-element.135), channel_id=1, source_target_pairs={{0,8},{1,9},{2,10},{3,11},{4,12},{5,13},{6,14},{7,15},{8,0},{9,1},... | collective-permute-start | bytes 172040 | tf_op jit(solution)/shard_map/ppermute | solution.py:633
  42.6 1.3 %collective-permute-done.14.in_a = bf16[18,32,128]{2,1,0:T(8,128)(2,1)S(1)} collective-permute-done((bf16[18,32,128]{2,1,0:T(8,128)(2,1)S(1)}, bf16[18,32,128]{2,1,0:T(8,128)(2,1)S(1)}, u32[]{:S(2)}, u32[]{:S(2)}) %collective-permute-start.14) | collective-permute-done | bytes 147488 | tf_op jit(solution)/shard_map/ppermute | solution.py:633
  43.9 2.6 %collective-permute-start.16 = (bf16[16,32,128]{2,1,0:T(8,128)(2,1)S(1)}, bf16[16,32,128]{2,1,0:T(8,128)(2,1)S(1)}, u32[]{:S(2)}, u32[]{:S(2)}) collective-permute-start(bf16[16,32,128]{2,1,0:T(8,128)(2,1)S(1)} %get-tuple-element.134), channel_id=1, source_target_pairs={{0,12},{1,13},{2,14},{3,15},{4,8},{5,9},{6,10},{7,11},{8,4},{9,5},... | collective-permute-start | bytes 393224 | tf_op jit(solution)/shard_map/ppermute | solution.py:633
  46.5 0.9 %collective-permute-done.12.second_in = bf16[2,3,16,512]{3,2,1,0:T(8,128)(2,1)S(1)} collective-permute-done((bf16[2,3,16,512]{3,2,1,0:T(8,128)(2,1)S(1)}, bf16[2,3,16,512]{3,2,1,0:T(8,128)(2,1)S(1)}, u32[]{:S(2)}, u32[]{:S(2)}) %collective-permute-start.12) | collective-permute-done | bytes 98336 | tf_op jit(solution)/shard_map/ppermute | solution.py:43
  47.4 0.0 collective-permute-done.13.first_in
  47.4 1.0 %shard_map.117.after_ref = bf16[2,128,512]{2,1,0:T(8,128)(2,1)} custom-call(s32[1]{0:T(128)} %bitcast.me_ref, bf16[7,32,128]{2,1,0:T(8,128)(2,1)S(1)} %get-tuple-element.128.after_ref, bf16[2,3,16,512]{3,2,1,0:T(8,128)(2,1)S(1)} %collective-permute-done.12.second_in, bf16[2,3,16,512]{3,2,1,0:T(8,128)(2,1)S(1)} %collective-permute-done.13.first_in, ...), custom_call_target="tpu_custom_call" | custom-call | flops 20000000000 | bytes 10000 | tf_op jit(solution)/shard_map/pallas_call | solution.py:507
  48.4 3.4 %collective-permute-done.17.refs_2_ = bf16[7,32,128]{2,1,0:T(8,128)(2,1)S(1)} collective-permute-done((bf16[7,32,128]{2,1,0:T(8,128)(2,1)S(1)}, bf16[7,32,128]{2,1,0:T(8,128)(2,1)S(1)}, u32[]{:S(2)}, u32[]{:S(2)}) %collective-permute-start.17) | collective-permute-done | bytes 57376 | tf_op jit(solution)/shard_map/ppermute | solution.py:633
  51.8 0.0 collective-permute-done.16.refs_1_
  51.8 0.7 %shard_map.119 = f32[32,2048]{1,0:T(8,128)} custom-call(bf16[2,128,512]{2,1,0:T(8,128)(2,1)} %shard_map.117.after_ref, f32[32,1152]{1,0:T(8,128)S(1)} %get-tuple-element.132.own_a, f32[32,896]{1,0:T(8,128)S(1)} %get-tuple-element.133.own_b, bf16[7,32,128]{2,1,0:T(8,128)(2,1)S(1)} %collective-permute-done.15.refs_0_, ...), custom_call_target="tpu_custom_call" | custom-call | flops 1000000 | bytes 10000 | tf_op jit(solution)/shard_map/pallas_call | solution.py:507
  (7 shorter events, 0.1 us)
Async XLA Ops:
  1.8 8.3 %collective-permute-start = (bf16[2,3,16,512]{3,2,1,0:T(8,128)(2,1)S(1)}, bf16[2,3,16,512]{3,2,1,0:T(8,128)(2,1)S(1)}, u32[]{:S(2)}, u32[]{:S(2)}) collective-permute-start(bf16[2,3,16,512]{3,2,1,0:T(8,128)(2,1)S(1)} %get-tuple-element.73), channel_id=1, source_target_pairs={{0,12},{1,13},{2,14},{3,15},{4,0},{5,1},{6,2},{7,3},{8,4},{9,5},{1... | collective-permute-start | bytes 294920 | tf_op jit(solution)/shard_map/ppermute | solution.py:28
  6.9 6.4 %collective-permute-start.1 = (bf16[2,3,16,512]{3,2,1,0:T(8,128)(2,1)S(1)}, bf16[2,3,16,512]{3,2,1,0:T(8,128)(2,1)S(1)}, u32[]{:S(2)}, u32[]{:S(2)}) collective-permute-start(bf16[2,3,16,512]{3,2,1,0:T(8,128)(2,1)S(1)} %get-tuple-element.74), channel_id=1, source_target_pairs={{0,4},{1,5},{2,6},{3,7},{4,8},{5,9},{6,10},{7,11},{8,12},{9,13},{1... | collective-permute-start | bytes 294920 | tf_op jit(solution)/shard_map/ppermute | solution.py:28
  13.4 6.8 %collective-permute-start.2 = (bf16[2,3,16,512]{3,2,1,0:T(8,128)(2,1)S(1)}, bf16[2,3,16,512]{3,2,1,0:T(8,128)(2,1)S(1)}, u32[]{:S(2)}, u32[]{:S(2)}) collective-permute-start(bf16[2,3,16,512]{3,2,1,0:T(8,128)(2,1)S(1)} %get-tuple-element.76.after_ref), channel_id=1, source_target_pairs={{0,15},{1,2},{2,1},{3,4},{4,3},{5,6},{6,5},{7,8},{8,7},{9,10},{10,... | collective-permute-start | bytes 294920 | tf_op jit(solution)/shard_map/ppermute | solution.py:43
  13.5 6.7 %collective-permute-start.3 = (bf16[2,3,16,512]{3,2,1,0:T(8,128)(2,1)S(1)}, bf16[2,3,16,512]{3,2,1,0:T(8,128)(2,1)S(1)}, u32[]{:S(2)}, u32[]{:S(2)}) collective-permute-start(bf16[2,3,16,512]{3,2,1,0:T(8,128)(2,1)S(1)} %get-tuple-element.77), channel_id=1, source_target_pairs={{0,1},{1,0},{2,3},{3,2},{4,5},{5,4},{6,7},{7,6},{8,9},{9,8},{10,11... | collective-permute-start | bytes 294920 | tf_op jit(solution)/shard_map/ppermute | solution.py:44
  24.6 1.8 %collective-permute-start.6 = (bf16[4,32,1536]{2,1,0:T(8,128)(2,1)S(1)}, bf16[4,32,1536]{2,1,0:T(8,128)(2,1)S(1)}, u32[]{:S(2)}, u32[]{:S(2)}) collective-permute-start(bf16[4,32,1536]{2,1,0:T(8,128)(2,1)S(1)} %get-tuple-element.118), channel_id=1, source_target_pairs={{0,1},{1,0},{2,3},{3,2},{4,5},{5,4},{6,7},{7,6},{8,9},{9,8},{10,11... | collective-permute-start | bytes 1179656 | tf_op jit(solution)/shard_map/ppermute | solution.py:609
  24.7 8.0 %collective-permute-start.5 = (bf16[4,32,1536]{2,1,0:T(8,128)(2,1)S(1)}, bf16[4,32,1536]{2,1,0:T(8,128)(2,1)S(1)}, u32[]{:S(2)}, u32[]{:S(2)}) collective-permute-start(bf16[4,32,1536]{2,1,0:T(8,128)(2,1)S(1)} %get-tuple-element.116), channel_id=1, source_target_pairs={{0,1},{1,0},{2,3},{3,2},{4,5},{5,4},{6,7},{7,6},{8,9},{9,8},{10,11... | collective-permute-start | bytes 1179656 | tf_op jit(solution)/shard_map/ppermute | solution.py:609
  26.5 12.0 %collective-permute-start.7 = (bf16[4,32,1536]{2,1,0:T(8,128)(2,1)S(1)}, bf16[4,32,1536]{2,1,0:T(8,128)(2,1)S(1)}, u32[]{:S(2)}, u32[]{:S(2)}) collective-permute-start(bf16[4,32,1536]{2,1,0:T(8,128)(2,1)S(1)} %add_convert_fusion), channel_id=1, source_target_pairs={{0,2},{1,3},{2,0},{3,1},{4,6},{5,7},{6,4},{7,5},{8,10},{9,11},{10,... | collective-permute-start | bytes 1179656 | tf_op jit(solution)/shard_map/ppermute | solution.py:616
  28.1 1.4 %collective-permute-start.4 = (bf16[4,32,512]{2,1,0:T(8,128)(2,1)S(1)}, bf16[4,32,512]{2,1,0:T(8,128)(2,1)S(1)}, u32[]{:S(2)}, u32[]{:S(2)}) collective-permute-start(bf16[4,32,512]{2,1,0:T(8,128)(2,1)S(1)} %get-tuple-element.91), channel_id=1, source_target_pairs={{0,1},{1,0},{2,3},{3,2},{4,5},{5,4},{6,7},{7,6},{8,9},{9,8},{10,11... | collective-permute-start | bytes 393224 | tf_op jit(solution)/shard_map/ppermute | solution.py:609
  28.3 13.6 %collective-permute-start.11 = (bf16[4,32,512]{2,1,0:T(8,128)(2,1)S(1)}, bf16[4,32,512]{2,1,0:T(8,128)(2,1)S(1)}, u32[]{:S(2)}, u32[]{:S(2)}) collective-permute-start(bf16[4,32,512]{2,1,0:T(8,128)(2,1)S(1)} %get-tuple-element.127), channel_id=1, source_target_pairs={{0,1},{1,0},{2,3},{3,2},{4,5},{5,4},{6,7},{7,6},{8,9},{9,8},{10,11... | collective-permute-start | bytes 393224 | tf_op jit(solution)/shard_map/ppermute | solution.py:609
  29.6 12.3 %collective-permute-start.10 = (bf16[4,32,512]{2,1,0:T(8,128)(2,1)S(1)}, bf16[4,32,512]{2,1,0:T(8,128)(2,1)S(1)}, u32[]{:S(2)}, u32[]{:S(2)}) collective-permute-start(bf16[4,32,512]{2,1,0:T(8,128)(2,1)S(1)} %shard_map.111.refs_0_), channel_id=1, source_target_pairs={{0,2},{1,3},{2,0},{3,1},{4,6},{5,7},{6,4},{7,5},{8,10},{9,11},{10,... | collective-permute-start | bytes 393224 | tf_op jit(solution)/shard_map/ppermute | solution.py:623
  32.7 6.1 %collective-permute-start.8 = (bf16[2,3,16,512]{3,2,1,0:T(8,128)(2,1)S(1)}, bf16[2,3,16,512]{3,2,1,0:T(8,128)(2,1)S(1)}, u32[]{:S(2)}, u32[]{:S(2)}) collective-permute-start(bf16[2,3,16,512]{3,2,1,0:T(8,128)(2,1)S(1)} %get-tuple-element.120), channel_id=1, source_target_pairs={{0,12},{1,13},{2,14},{3,15},{4,0},{5,1},{6,2},{7,3},{8,4},{9,5},{1... | collective-permute-start | bytes 294920 | tf_op jit(solution)/shard_map/ppermute | solution.py:28
  32.7 7.5 %collective-permute-start.9 = (bf16[2,3,16,512]{3,2,1,0:T(8,128)(2,1)S(1)}, bf16[2,3,16,512]{3,2,1,0:T(8,128)(2,1)S(1)}, u32[]{:S(2)}, u32[]{:S(2)}) collective-permute-start(bf16[2,3,16,512]{3,2,1,0:T(8,128)(2,1)S(1)} %get-tuple-element.121), channel_id=1, source_target_pairs={{0,4},{1,5},{2,6},{3,7},{4,8},{5,9},{6,10},{7,11},{8,12},{9,13},{1... | collective-permute-start | bytes 294920 | tf_op jit(solution)/shard_map/ppermute | solution.py:28
  38.6 5.2 %collective-permute-start.14 = (bf16[18,32,128]{2,1,0:T(8,128)(2,1)S(1)}, bf16[18,32,128]{2,1,0:T(8,128)(2,1)S(1)}, u32[]{:S(2)}, u32[]{:S(2)}) collective-permute-start(bf16[18,32,128]{2,1,0:T(8,128)(2,1)S(1)} %get-tuple-element.119.after_ref), channel_id=1, source_target_pairs={{0,4},{1,5},{2,6},{3,7},{4,0},{5,1},{6,2},{7,3},{8,12},{9,13},{10,... | collective-permute-start | bytes 442376 | tf_op jit(solution)/shard_map/ppermute | solution.py:633
  40.3 7.1 %collective-permute-start.12 = (bf16[2,3,16,512]{3,2,1,0:T(8,128)(2,1)S(1)}, bf16[2,3,16,512]{3,2,1,0:T(8,128)(2,1)S(1)}, u32[]{:S(2)}, u32[]{:S(2)}) collective-permute-start(bf16[2,3,16,512]{3,2,1,0:T(8,128)(2,1)S(1)} %get-tuple-element.129), channel_id=1, source_target_pairs={{0,15},{1,2},{2,1},{3,4},{4,3},{5,6},{6,5},{7,8},{8,7},{9,10},{10,... | collective-permute-start | bytes 294920 | tf_op jit(solution)/shard_map/ppermute | solution.py:43
  40.4 7.0 %collective-permute-start.13 = (bf16[2,3,16,512]{3,2,1,0:T(8,128)(2,1)S(1)}, bf16[2,3,16,512]{3,2,1,0:T(8,128)(2,1)S(1)}, u32[]{:S(2)}, u32[]{:S(2)}) collective-permute-start(bf16[2,3,16,512]{3,2,1,0:T(8,128)(2,1)S(1)} %get-tuple-element.124.refs_0_), channel_id=1, source_target_pairs={{0,1},{1,0},{2,3},{3,2},{4,5},{5,4},{6,7},{7,6},{8,9},{9,8},{10,11... | collective-permute-start | bytes 294920 | tf_op jit(solution)/shard_map/ppermute | solution.py:44
  42.0 6.4 %collective-permute-start.15 = (bf16[7,32,128]{2,1,0:T(8,128)(2,1)S(1)}, bf16[7,32,128]{2,1,0:T(8,128)(2,1)S(1)}, u32[]{:S(2)}, u32[]{:S(2)}) collective-permute-start(bf16[7,32,128]{2,1,0:T(8,128)(2,1)S(1)} %get-tuple-element.128.after_ref), channel_id=1, source_target_pairs={{0,4},{1,5},{2,6},{3,7},{4,0},{5,1},{6,2},{7,3},{8,12},{9,13},{10,... | collective-permute-start | bytes 172040 | tf_op jit(solution)/shard_map/ppermute | solution.py:633
  42.0 9.8 %collective-permute-start.17 = (bf16[7,32,128]{2,1,0:T(8,128)(2,1)S(1)}, bf16[7,32,128]{2,1,0:T(8,128)(2,1)S(1)}, u32[]{:S(2)}, u32[]{:S(2)}) collective-permute-start(bf16[7,32,128]{2,1,0:T(8,128)(2,1)S(1)} %get-tuple-element.135), channel_id=1, source_target_pairs={{0,8},{1,9},{2,10},{3,11},{4,12},{5,13},{6,14},{7,15},{8,0},{9,1},... | collective-permute-start | bytes 172040 | tf_op jit(solution)/shard_map/ppermute | solution.py:633
  43.8 3.6 %copy-start = (s32[1,8,16]{2,1,0:T(8,128)S(1)}, s32[1,8,16]{2,1,0:T(8,128)}, u32[]{:S(2)}) copy-start(s32[1,8,16]{2,1,0:T(8,128)} %send_ref.1) | copy-start | bytes 1540
  43.9 7.9 %collective-permute-start.16 = (bf16[16,32,128]{2,1,0:T(8,128)(2,1)S(1)}, bf16[16,32,128]{2,1,0:T(8,128)(2,1)S(1)}, u32[]{:S(2)}, u32[]{:S(2)}) collective-permute-start(bf16[16,32,128]{2,1,0:T(8,128)(2,1)S(1)} %get-tuple-element.134), channel_id=1, source_target_pairs={{0,12},{1,13},{2,14},{3,15},{4,8},{5,9},{6,10},{7,11},{8,4},{9,5},... | collective-permute-start | bytes 393224 | tf_op jit(solution)/shard_map/ppermute | solution.py:633

commit v17 on v15

--- a/solution.py
+++ b/solution.py
@@ -395,13 +395,12 @@
 
 
 def halve(rows, kept_ref, sent_ref):
+    half = len(rows) // 2
     for i, row in enumerate(rows):
-        if i % 2 == 0:
-            kept_ref[i // 2] = row
-            continue
-        pieces = row.shape[1] // 128
-        for n in range(pieces):
-            sent_ref[i // 2 * pieces + n] = row[:, n * 128 : (n + 1) * 128].astype(bf16)
+        if i < half:
+            kept_ref[i] = row
+        else:
+            put(row, sent_ref, (i - half) * row.shape[1] // 128)
 
 
 def add_received(kept_ref, received_ref):
@@ -484,7 +483,7 @@
     blocks, more = b.shape[1] // 128, a.shape[1] // 128
     for k, ref in enumerate(received, 1):
         b = b + jnp.concatenate([ref[n] for n in range(blocks)], axis=1).astype(f32)
-        if k % 2 == 0:
+        if k <= len(received) // 2:
             a = a + jnp.concatenate([ref[blocks + n] for n in range(more)], axis=1).astype(f32)
     width = out_ref.shape[1] // 4
     group = 0
@@ -641,7 +640,7 @@
         ],
         (node, own_a, core_own, y_a), specs=[pl.ANY], flops=2 * 10**10,
     )
-    in_a = exchange(sent_a, 1)
+    in_a = exchange(sent_a, planes // 2)
     outgoing = call(
         relay_kernel, [three, three],
         (place, sent_a, own_right, own_left, from_plus, from_minus),
@@ -657,10 +656,11 @@
         specs=[pltpu.SMEM, pl.ANY],
         scratch=[pltpu.VMEM((planes, rows, width), f32)], flops=4 * 10**9,
     )
-    own_a, *sent[1::2] = call(
+    riding = planes // 2 - 1
+    own_a, *sent[:riding] = call(
         join_kernel,
-        [((rows, wide), f32)] + [((blocks + more, rows, 128), bf16)] * (planes // 2 - 1),
-        (kept_a, in_a, *sent[1::2]), flops=2 * 10**10,
+        [((rows, wide), f32)] + [((blocks + more, rows, 128), bf16)] * riding,
+        (kept_a, in_a, *sent[:riding]), flops=2 * 10**10,
     )
     received = [exchange(shard, k) for k, shard in enumerate(sent, 1)]
     (node_grad,) = call(

time: 51.3 us -> 52.1 us (1.016)
  starting transfers between devices: 17.6 us -> 20.2 us
  waiting for transfers between devices: 17 us -> 15.1 us
    ppermute x4, starting transfers between devices: 4.05 us -> 6.27 us  [exchange(): return lax.ppermute(sent, 'patch', along_z(count, distance))]
    ppermute x4, waiting for transfers between devices: 3.75 us -> 2.16 us  [shifted(): lax.ppermute(shard, 'patch', [(i, (i + by) % count) for i in range(count)])]
    ppermute x2, waiting for transfers between devices: 3.35 us -> 2.3 us  [swap(): later = lax.ppermute(pair[1], 'patch', second)]
    ppermute x4, waiting for transfers between devices: 4.08 us -> 4.86 us  [exchange(): return lax.ppermute(sent, 'patch', along_z(count, distance))]
where the time goes in v17:
time: 52.1 us; the launch traced here: 51.8 us
  starting transfers between devices  20.2 us (39%)
  Pallas kernels  15.7 us (30%)
  waiting for transfers between devices  15.1 us (29%)
  between operations  0.75 us (1%)
    pallas_call x16, Pallas kernels, call(): pl.pallas_call(kernel, out_shape=[jax.ShapeDtypeStruct(*o) if final else...  15.7 us
    ppermute x4, starting transfers between devices, shifted(): lax.ppermute(shard, 'patch', [(i, (i + by) % count) for i in range(count)])  7.25 us
    ppermute x4, starting transfers between devices, exchange(): return lax.ppermute(sent, 'patch', along_z(count, distance))  6.27 us
    ppermute x4, waiting for transfers between devices, exchange(): return lax.ppermute(sent, 'patch', along_z(count, distance))  4.86 us
    ppermute x1, waiting for transfers between devices, body(): y_a = lax.ppermute(y_sent, 'patch', flop)  3.75 us
    ppermute x2, waiting for transfers between devices, swap(): later = lax.ppermute(pair[1], 'patch', second)  2.3 us
    ppermute x2, starting transfers between devices, swap(): later = lax.ppermute(pair[1], 'patch', second)  2.19 us
    ppermute x4, waiting for transfers between devices, shifted(): lax.ppermute(shard, 'patch', [(i, (i + by) % count) for i in range(count)])  2.16 us
  transfers between devices with their start and end apart: 18, of which 10 were waited for; matrix products, arithmetic and copies ran while one was open for 0% of the time, Pallas kernels for 18%

profile of v17, /device:TPU:0, one launch (start us, length us, event | category | flops | bytes accessed | tf_op | source)
XLA Modules:
  0.0 51.8 jit_solution(14747140945570245725)
XLA Ops:
  0.6 1.2 %shard_map.104 = (bf16[2,3,16,512]{3,2,1,0:T(8,128)(2,1)S(1)}, bf16[2,3,16,512]{3,2,1,0:T(8,128)(2,1)S(1)}, bf16[2,1,16,512]{3,2,1,0:T(8,128)(2,1)S(1)}, bf16[2,...) custom-call(s32[1,8,16]{2,1,0:T(8,128)} %send_ref.1, bf16[2,128,512]{2,1,0:T(8,128)(2,1)} %x_hbm.1), custom_call_target="tpu_custom_call" | custom-call | flops 1000000 | bytes 10000 | tf_op jit(solution)/shard_map/pallas_call | solution.py:506
  1.8 3.1 %collective-permute-start = (bf16[2,3,16,512]{3,2,1,0:T(8,128)(2,1)S(1)}, bf16[2,3,16,512]{3,2,1,0:T(8,128)(2,1)S(1)}, u32[]{:S(2)}, u32[]{:S(2)}) collective-permute-start(bf16[2,3,16,512]{3,2,1,0:T(8,128)(2,1)S(1)} %get-tuple-element.74), channel_id=1, source_target_pairs={{0,4},{1,5},{2,6},{3,7},{4,8},{5,9},{6,10},{7,11},{8,12},{9,13},{1... | collective-permute-start | bytes 294920 | tf_op jit(solution)/shard_map/ppermute | solution.py:28
  4.9 2.1 %collective-permute-start.1 = (bf16[2,3,16,512]{3,2,1,0:T(8,128)(2,1)S(1)}, bf16[2,3,16,512]{3,2,1,0:T(8,128)(2,1)S(1)}, u32[]{:S(2)}, u32[]{:S(2)}) collective-permute-start(bf16[2,3,16,512]{3,2,1,0:T(8,128)(2,1)S(1)} %get-tuple-element.75), channel_id=1, source_target_pairs={{0,12},{1,13},{2,14},{3,15},{4,0},{5,1},{6,2},{7,3},{8,4},{9,5},{1... | collective-permute-start | bytes 294920 | tf_op jit(solution)/shard_map/ppermute | solution.py:28
  7.0 2.6 %shard_map.105 = (bf16[8,2,128,128]{3,2,1,0:T(8,128)(2,1)S(1)}, bf16[8,2,128,128]{3,2,1,0:T(8,128)(2,1)S(1)}, bf16[8,2,128,128]{3,2,1,0:T(8,128)(2,1)S(1)}, bf16...) custom-call(bf16[2,1,16,512]{3,2,1,0:T(8,128)(2,1)S(1)} %get-tuple-e, ...), custom_call_target="tpu_custom_call" | custom-call | flops 1000000 | bytes 10000 | tf_op jit(solution)/shard_map/pallas_call | solution.py:506
  9.7 0.8 %collective-permute-done.plus_ref = bf16[2,3,16,512]{3,2,1,0:T(8,128)(2,1)S(1)} collective-permute-done((bf16[2,3,16,512]{3,2,1,0:T(8,128)(2,1)S(1)}, bf16[2,3,16,512]{3,2,1,0:T(8,128)(2,1)S(1)}, u32[]{:S(2)}, u32[]{:S(2)}) %collective-permute-start) | collective-permute-done | bytes 98336 | tf_op jit(solution)/shard_map/ppermute | solution.py:28
  10.4 0.8 %collective-permute-done.1.minus_ref = bf16[2,3,16,512]{3,2,1,0:T(8,128)(2,1)S(1)} collective-permute-done((bf16[2,3,16,512]{3,2,1,0:T(8,128)(2,1)S(1)}, bf16[2,3,16,512]{3,2,1,0:T(8,128)(2,1)S(1)}, u32[]{:S(2)}, u32[]{:S(2)}) %collective-permute-start.1) | collective-permute-done | bytes 98336 | tf_op jit(solution)/shard_map/ppermute | solution.py:28
  11.3 1.7 %collective-permute-start.2 = (bf16[2,3,16,512]{3,2,1,0:T(8,128)(2,1)S(1)}, bf16[2,3,16,512]{3,2,1,0:T(8,128)(2,1)S(1)}, u32[]{:S(2)}, u32[]{:S(2)}) collective-permute-start(bf16[2,3,16,512]{3,2,1,0:T(8,128)(2,1)S(1)} %get-tuple-element.76.after_ref), channel_id=1, source_target_pairs={{0,15},{1,2},{2,1},{3,4},{4,3},{5,6},{6,5},{7,8},{8,7},{9,10},{10,... | collective-permute-start | bytes 294920 | tf_op jit(solution)/shard_map/ppermute | solution.py:43
  13.0 0.0 collective-permute-start.3
  13.0 1.4 %shard_map.108.refs_4_.refs_12_ = f32[256,128]{1,0:T(8,128)S(1)} custom-call(bf16[2,3,16,512]{3,2,1,0:T(8,128)(2,1)S(1)} %get-tuple-element.76.after_ref, s32[128,256]{1,0:T(8,128)S(1)} %get-tuple-element.84.neigh_ref, s32[1,128]{1,0:T(1,128)S(1)} %get-tuple-element.85.count_ref), custom_call_target="tpu_custom_call" | custom-call | flops 1000000 | bytes 10000 | tf_op jit(solution)/shard_map/pallas_call | solution.py:506
  14.5 1.4 %shard_map.109 = (f32[3,2,128,512]{3,2,1,0:T(8,128)S(1)}, f32[2,2,8,512]{3,2,1,0:T(8,128)S(1)}, f32[3,2,128,512]{3,2,1,0:T(8,128)S(1)}, f32[2,2,8,512]{3,2,1,0:T...) custom-call(bf16[8,2,128,128]{3,2,1,0:T(8,128)(2,1)S(1)} %get-tuple-, ...), custom_call_target="tpu_custom_call" | custom-call | flops 1000000 | bytes 10000 | tf_op jit(solution)/shard_map/pallas_call | solution.py:506
  15.8 2.3 %collective-permute-done.2.second_in = bf16[2,3,16,512]{3,2,1,0:T(8,128)(2,1)S(1)} collective-permute-done((bf16[2,3,16,512]{3,2,1,0:T(8,128)(2,1)S(1)}, bf16[2,3,16,512]{3,2,1,0:T(8,128)(2,1)S(1)}, u32[]{:S(2)}, u32[]{:S(2)}) %collective-permute-start.2) | collective-permute-done | bytes 98336 | tf_op jit(solution)/shard_map/ppermute | solution.py:43
  18.1 0.0 collective-permute-done.3.first_in
  18.1 0.6 %shard_map.107 = (bf16[4,2,128,128]{3,2,1,0:T(8,128)(2,1)S(1)}, bf16[4,2,128,128]{3,2,1,0:T(8,128)(2,1)S(1)}, bf16[4,2,128,128]{3,2,1,0:T(8,128)(2,1)S(1)}, bf16...) custom-call(s32[1]{0:T(128)} %bitcast.me_ref, bf16[2,3,16,512]{3,2,1,0:T(8,128)(2,1)S(1)} %collective-permute-done.2.second_in, ...), custom_call_target="tpu_custom_call" | custom-call | flops 1000000 | bytes 10000 | tf_op jit(solution)/shard_map/pallas_call | solution.py:506
  18.7 3.8 %shard_map.112 = (f32[4,32,1536]{2,1,0:T(8,128)S(1)}, f32[4,32,1536]{2,1,0:T(8,128)S(1)}, bf16[4,32,1536]{2,1,0:T(8,128)(2,1)S(1)}, bf16[4,32,1536]{2,1,0:T(8,12...) custom-call(s32[1]{0:T(128)} %bitcast.me_ref, ...), custom_call_target="tpu_custom_call" | custom-call | flops 1000000 | bytes 10000 | tf_op jit(solution)/shard_map/pallas_call | solution.py:506
  22.5 0.1 collective-permute-start.6
  22.6 0.5 collective-permute-start.5
  23.1 1.2 %collective-permute-done.6 = bf16[4,32,1536]{2,1,0:T(8,128)(2,1)S(1)} collective-permute-done((bf16[4,32,1536]{2,1,0:T(8,128)(2,1)S(1)}, bf16[4,32,1536]{2,1,0:T(8,128)(2,1)S(1)}, u32[]{:S(2)}, u32[]{:S(2)}) %collective-permute-start.6) | collective-permute-done | bytes 393248 | tf_op jit(solution)/shard_map/ppermute | solution.py:608
  24.3 0.1 add_convert_fusion
  24.4 0.1 collective-permute-start.7
  24.5 1.5 %shard_map.110 = (f32[4,32,512]{2,1,0:T(8,128)S(1)}, f32[4,32,512]{2,1,0:T(8,128)S(1)}, bf16[4,32,512]{2,1,0:T(8,128)(2,1)S(1)}, bf16[4,32,512]{2,1,0:T(8,128)(2...) custom-call(s32[1]{0:T(128)} %bitcast.me_ref, ...), custom_call_target="tpu_custom_call" | custom-call | flops 1000000 | bytes 10000 | tf_op jit(solution)/shard_map/pallas_call | solution.py:506
  26.0 0.2 collective-permute-start.4
  26.2 0.4 collective-permute-start.12
  26.6 0.8 %collective-permute-done.4.refs_1_ = bf16[4,32,512]{2,1,0:T(8,128)(2,1)S(1)} collective-permute-done((bf16[4,32,512]{2,1,0:T(8,128)(2,1)S(1)}, bf16[4,32,512]{2,1,0:T(8,128)(2,1)S(1)}, u32[]{:S(2)}, u32[]{:S(2)}) %collective-permute-start.4) | collective-permute-done | bytes 131104 | tf_op jit(solution)/shard_map/ppermute | solution.py:608
  27.5 2.1 %collective-permute-start.11 = (bf16[4,32,512]{2,1,0:T(8,128)(2,1)S(1)}, bf16[4,32,512]{2,1,0:T(8,128)(2,1)S(1)}, u32[]{:S(2)}, u32[]{:S(2)}) collective-permute-start(bf16[4,32,512]{2,1,0:T(8,128)(2,1)S(1)} %shard_map.111.refs_0_), channel_id=1, source_target_pairs={{0,2},{1,3},{2,0},{3,1},{4,6},{5,7},{6,4},{7,5},{8,10},{9,11},{10,... | collective-permute-start | bytes 393224 | tf_op jit(solution)/shard_map/ppermute | solution.py:622
  29.6 1.0 %shard_map.113 = (f32[2,128,512]{2,1,0:T(8,128)S(1)}, bf16[2,3,16,512]{3,2,1,0:T(8,128)(2,1)S(1)}, bf16[2,3,16,512]{3,2,1,0:T(8,128)(2,1)S(1)}, bf16[2,1,16,512]...) custom-call(bf16[4,32,512]{2,1,0:T(8,128)(2,1)S(1)} %shard_map.111.refs_0_, ...), custom_call_target="tpu_custom_call" | custom-call | flops 1000000 | bytes 10000 | tf_op jit(solution)/shard_map/pallas_call | solution.py:506
  30.6 0.8 %collective-permute-start.9 = (bf16[2,3,16,512]{3,2,1,0:T(8,128)(2,1)S(1)}, bf16[2,3,16,512]{3,2,1,0:T(8,128)(2,1)S(1)}, u32[]{:S(2)}, u32[]{:S(2)}) collective-permute-start(bf16[2,3,16,512]{3,2,1,0:T(8,128)(2,1)S(1)} %get-tuple-element.123), channel_id=1, source_target_pairs={{0,12},{1,13},{2,14},{3,15},{4,0},{5,1},{6,2},{7,3},{8,4},{9,5},{1... | collective-permute-start | bytes 294920 | tf_op jit(solution)/shard_map/ppermute | solution.py:28
  31.3 0.0 collective-permute-done.5.core_in
  31.3 1.3 %collective-permute-start.10 = (bf16[2,3,16,512]{3,2,1,0:T(8,128)(2,1)S(1)}, bf16[2,3,16,512]{3,2,1,0:T(8,128)(2,1)S(1)}, u32[]{:S(2)}, u32[]{:S(2)}) collective-permute-start(bf16[2,3,16,512]{3,2,1,0:T(8,128)(2,1)S(1)} %get-tuple-element.124), channel_id=1, source_target_pairs={{0,4},{1,5},{2,6},{3,7},{4,8},{5,9},{6,10},{7,11},{8,12},{9,13},{1... | collective-permute-start | bytes 294920 | tf_op jit(solution)/shard_map/ppermute | solution.py:28
  32.7 3.8 %collective-permute-done.7.y_in = bf16[4,32,1536]{2,1,0:T(8,128)(2,1)S(1)} collective-permute-done((bf16[4,32,1536]{2,1,0:T(8,128)(2,1)S(1)}, bf16[4,32,1536]{2,1,0:T(8,128)(2,1)S(1)}, u32[]{:S(2)}, u32[]{:S(2)}) %collective-permute-start.7) | collective-permute-done | bytes 393248 | tf_op jit(solution)/shard_map/ppermute | solution.py:615
  36.4 0.1 shard_map.114
  36.6 0.8 %collective-permute-start.8 = (bf16[18,32,128]{2,1,0:T(8,128)(2,1)S(1)}, bf16[18,32,128]{2,1,0:T(8,128)(2,1)S(1)}, u32[]{:S(2)}, u32[]{:S(2)}) collective-permute-start(bf16[18,32,128]{2,1,0:T(8,128)(2,1)S(1)} %get-tuple-element.120.after_ref), channel_id=1, source_target_pairs={{0,12},{1,13},{2,14},{3,15},{4,8},{5,9},{6,10},{7,11},{8,4},{9,5},... | collective-permute-start | bytes 442376 | tf_op jit(solution)/shard_map/ppermute | solution.py:632
  37.3 0.0 collective-permute-done.9.plus_ref
  37.3 0.5 %collective-permute-done.10.minus_ref = bf16[2,3,16,512]{3,2,1,0:T(8,128)(2,1)S(1)} collective-permute-done((bf16[2,3,16,512]{3,2,1,0:T(8,128)(2,1)S(1)}, bf16[2,3,16,512]{3,2,1,0:T(8,128)(2,1)S(1)}, u32[]{:S(2)}, u32[]{:S(2)}) %collective-permute-start.10) | collective-permute-done | bytes 98336 | tf_op jit(solution)/shard_map/ppermute | solution.py:28
  37.9 0.5 %collective-permute-start.13 = (bf16[2,3,16,512]{3,2,1,0:T(8,128)(2,1)S(1)}, bf16[2,3,16,512]{3,2,1,0:T(8,128)(2,1)S(1)}, u32[]{:S(2)}, u32[]{:S(2)}) collective-permute-start(bf16[2,3,16,512]{3,2,1,0:T(8,128)(2,1)S(1)} %get-tuple-element.131), channel_id=1, source_target_pairs={{0,15},{1,2},{2,1},{3,4},{4,3},{5,6},{6,5},{7,8},{8,7},{9,10},{10,... | collective-permute-start | bytes 294920 | tf_op jit(solution)/shard_map/ppermute | solution.py:43
  38.4 1.1 %collective-permute-start.14 = (bf16[2,3,16,512]{3,2,1,0:T(8,128)(2,1)S(1)}, bf16[2,3,16,512]{3,2,1,0:T(8,128)(2,1)S(1)}, u32[]{:S(2)}, u32[]{:S(2)}) collective-permute-start(bf16[2,3,16,512]{3,2,1,0:T(8,128)(2,1)S(1)} %get-tuple-element.125.refs_0_), channel_id=1, source_target_pairs={{0,1},{1,0},{2,3},{3,2},{4,5},{5,4},{6,7},{7,6},{8,9},{9,8},{10,11... | collective-permute-start | bytes 294920 | tf_op jit(solution)/shard_map/ppermute | solution.py:44
  39.6 0.0 collective-permute-done.12.refs_4_
  39.6 0.0 collective-permute-done.11.refs_2_
  39.6 0.1 shard_map.116
  39.7 1.2 %collective-permute-start.16 = (bf16[7,32,128]{2,1,0:T(8,128)(2,1)S(1)}, bf16[7,32,128]{2,1,0:T(8,128)(2,1)S(1)}, u32[]{:S(2)}, u32[]{:S(2)}) collective-permute-start(bf16[7,32,128]{2,1,0:T(8,128)(2,1)S(1)} %get-tuple-element.134), channel_id=1, source_target_pairs={{0,12},{1,13},{2,14},{3,15},{4,8},{5,9},{6,10},{7,11},{8,4},{9,5},... | collective-permute-start | bytes 172040 | tf_op jit(solution)/shard_map/ppermute | solution.py:632
  40.8 0.6 %collective-permute-start.17 = (bf16[7,32,128]{2,1,0:T(8,128)(2,1)S(1)}, bf16[7,32,128]{2,1,0:T(8,128)(2,1)S(1)}, u32[]{:S(2)}, u32[]{:S(2)}) collective-permute-start(bf16[7,32,128]{2,1,0:T(8,128)(2,1)S(1)} %get-tuple-element.135), channel_id=1, source_target_pairs={{0,8},{1,9},{2,10},{3,11},{4,12},{5,13},{6,14},{7,15},{8,0},{9,1},... | collective-permute-start | bytes 172040 | tf_op jit(solution)/shard_map/ppermute | solution.py:632
  41.4 2.3 %collective-permute-done.8.in_a = bf16[18,32,128]{2,1,0:T(8,128)(2,1)S(1)} collective-permute-done((bf16[18,32,128]{2,1,0:T(8,128)(2,1)S(1)}, bf16[18,32,128]{2,1,0:T(8,128)(2,1)S(1)}, u32[]{:S(2)}, u32[]{:S(2)}) %collective-permute-start.8) | collective-permute-done | bytes 147488 | tf_op jit(solution)/shard_map/ppermute | solution.py:632
  43.7 3.8 %collective-permute-start.15 = (bf16[16,32,128]{2,1,0:T(8,128)(2,1)S(1)}, bf16[16,32,128]{2,1,0:T(8,128)(2,1)S(1)}, u32[]{:S(2)}, u32[]{:S(2)}) collective-permute-start(bf16[16,32,128]{2,1,0:T(8,128)(2,1)S(1)} %get-tuple-element.130.after_ref), channel_id=1, source_target_pairs={{0,4},{1,5},{2,6},{3,7},{4,0},{5,1},{6,2},{7,3},{8,12},{9,13},{10,... | collective-permute-start | bytes 393224 | tf_op jit(solution)/shard_map/ppermute | solution.py:632
  47.5 0.0 collective-permute-done.13.second_in
  47.5 1.0 %shard_map.118.after_ref = bf16[2,128,512]{2,1,0:T(8,128)(2,1)} custom-call(s32[1]{0:T(128)} %bitcast.me_ref, bf16[16,32,128]{2,1,0:T(8,128)(2,1)S(1)} %get-tuple-element.130.after_ref, bf16[2,3,16,512]{3,2,1,0:T(8,128)(2,1)S(1)} %collective-permute-done.13.second_in, bf16[2,3,16,512]{3,2,1,0:T(8,128)(2,1)S(1)} %collective-permute-done.14.first_in, ...), custom_call_target="tpu_custom_call" | custom-call | flops 20000000000 | bytes 10000 | tf_op jit(solution)/shard_map/pallas_call | solution.py:506
  48.5 0.0 collective-permute-done.16.refs_1_
  48.5 1.5 %collective-permute-done.17.refs_2_ = bf16[7,32,128]{2,1,0:T(8,128)(2,1)S(1)} collective-permute-done((bf16[7,32,128]{2,1,0:T(8,128)(2,1)S(1)}, bf16[7,32,128]{2,1,0:T(8,128)(2,1)S(1)}, u32[]{:S(2)}, u32[]{:S(2)}) %collective-permute-start.17) | collective-permute-done | bytes 57376 | tf_op jit(solution)/shard_map/ppermute | solution.py:632
  50.1 1.0 %collective-permute-done.15.refs_0_ = bf16[16,32,128]{2,1,0:T(8,128)(2,1)S(1)} collective-permute-done((bf16[16,32,128]{2,1,0:T(8,128)(2,1)S(1)}, bf16[16,32,128]{2,1,0:T(8,128)(2,1)S(1)}, u32[]{:S(2)}, u32[]{:S(2)}) %collective-permute-start.15) | collective-permute-done | bytes 131104 | tf_op jit(solution)/shard_map/ppermute | solution.py:632
  51.1 0.7 %shard_map.119 = f32[32,2048]{1,0:T(8,128)} custom-call(bf16[2,128,512]{2,1,0:T(8,128)(2,1)} %shard_map.118.after_ref, f32[32,1152]{1,0:T(8,128)S(1)} %get-tuple-element.132.own_a, f32[32,896]{1,0:T(8,128)S(1)} %get-tuple-element.133.own_b, bf16[16,32,128]{2,1,0:T(8,128)(2,1)S(1)} %collective-permute-done.15.refs_0_, ...), custom_call_target="tpu_custom_call" | custom-call | flops 1000000 | bytes 10000 | tf_op jit(solution)/shard_map/pallas_call | solution.py:506
  (7 shorter events, 0.1 us)
Async XLA Ops:
  1.8 8.6 %collective-permute-start = (bf16[2,3,16,512]{3,2,1,0:T(8,128)(2,1)S(1)}, bf16[2,3,16,512]{3,2,1,0:T(8,128)(2,1)S(1)}, u32[]{:S(2)}, u32[]{:S(2)}) collective-permute-start(bf16[2,3,16,512]{3,2,1,0:T(8,128)(2,1)S(1)} %get-tuple-element.74), channel_id=1, source_target_pairs={{0,4},{1,5},{2,6},{3,7},{4,8},{5,9},{6,10},{7,11},{8,12},{9,13},{1... | collective-permute-start | bytes 294920 | tf_op jit(solution)/shard_map/ppermute | solution.py:28
  4.9 6.4 %collective-permute-start.1 = (bf16[2,3,16,512]{3,2,1,0:T(8,128)(2,1)S(1)}, bf16[2,3,16,512]{3,2,1,0:T(8,128)(2,1)S(1)}, u32[]{:S(2)}, u32[]{:S(2)}) collective-permute-start(bf16[2,3,16,512]{3,2,1,0:T(8,128)(2,1)S(1)} %get-tuple-element.75), channel_id=1, source_target_pairs={{0,12},{1,13},{2,14},{3,15},{4,0},{5,1},{6,2},{7,3},{8,4},{9,5},{1... | collective-permute-start | bytes 294920 | tf_op jit(solution)/shard_map/ppermute | solution.py:28
  11.3 6.8 %collective-permute-start.2 = (bf16[2,3,16,512]{3,2,1,0:T(8,128)(2,1)S(1)}, bf16[2,3,16,512]{3,2,1,0:T(8,128)(2,1)S(1)}, u32[]{:S(2)}, u32[]{:S(2)}) collective-permute-start(bf16[2,3,16,512]{3,2,1,0:T(8,128)(2,1)S(1)} %get-tuple-element.76.after_ref), channel_id=1, source_target_pairs={{0,15},{1,2},{2,1},{3,4},{4,3},{5,6},{6,5},{7,8},{8,7},{9,10},{10,... | collective-permute-start | bytes 294920 | tf_op jit(solution)/shard_map/ppermute | solution.py:43
  13.0 5.1 %collective-permute-start.3 = (bf16[2,3,16,512]{3,2,1,0:T(8,128)(2,1)S(1)}, bf16[2,3,16,512]{3,2,1,0:T(8,128)(2,1)S(1)}, u32[]{:S(2)}, u32[]{:S(2)}) collective-permute-start(bf16[2,3,16,512]{3,2,1,0:T(8,128)(2,1)S(1)} %get-tuple-element.77), channel_id=1, source_target_pairs={{0,1},{1,0},{2,3},{3,2},{4,5},{5,4},{6,7},{7,6},{8,9},{9,8},{10,11... | collective-permute-start | bytes 294920 | tf_op jit(solution)/shard_map/ppermute | solution.py:44
  22.5 1.8 %collective-permute-start.6 = (bf16[4,32,1536]{2,1,0:T(8,128)(2,1)S(1)}, bf16[4,32,1536]{2,1,0:T(8,128)(2,1)S(1)}, u32[]{:S(2)}, u32[]{:S(2)}) collective-permute-start(bf16[4,32,1536]{2,1,0:T(8,128)(2,1)S(1)} %get-tuple-element.118), channel_id=1, source_target_pairs={{0,1},{1,0},{2,3},{3,2},{4,5},{5,4},{6,7},{7,6},{8,9},{9,8},{10,11... | collective-permute-start | bytes 1179656 | tf_op jit(solution)/shard_map/ppermute | solution.py:608
  22.6 8.7 %collective-permute-start.5 = (bf16[4,32,1536]{2,1,0:T(8,128)(2,1)S(1)}, bf16[4,32,1536]{2,1,0:T(8,128)(2,1)S(1)}, u32[]{:S(2)}, u32[]{:S(2)}) collective-permute-start(bf16[4,32,1536]{2,1,0:T(8,128)(2,1)S(1)} %get-tuple-element.116), channel_id=1, source_target_pairs={{0,1},{1,0},{2,3},{3,2},{4,5},{5,4},{6,7},{7,6},{8,9},{9,8},{10,11... | collective-permute-start | bytes 1179656 | tf_op jit(solution)/shard_map/ppermute | solution.py:608
  24.4 12.0 %collective-permute-start.7 = (bf16[4,32,1536]{2,1,0:T(8,128)(2,1)S(1)}, bf16[4,32,1536]{2,1,0:T(8,128)(2,1)S(1)}, u32[]{:S(2)}, u32[]{:S(2)}) collective-permute-start(bf16[4,32,1536]{2,1,0:T(8,128)(2,1)S(1)} %add_convert_fusion), channel_id=1, source_target_pairs={{0,2},{1,3},{2,0},{3,1},{4,6},{5,7},{6,4},{7,5},{8,10},{9,11},{10,... | collective-permute-start | bytes 1179656 | tf_op jit(solution)/shard_map/ppermute | solution.py:615
  26.0 1.4 %collective-permute-start.4 = (bf16[4,32,512]{2,1,0:T(8,128)(2,1)S(1)}, bf16[4,32,512]{2,1,0:T(8,128)(2,1)S(1)}, u32[]{:S(2)}, u32[]{:S(2)}) collective-permute-start(bf16[4,32,512]{2,1,0:T(8,128)(2,1)S(1)} %get-tuple-element.91), channel_id=1, source_target_pairs={{0,1},{1,0},{2,3},{3,2},{4,5},{5,4},{6,7},{7,6},{8,9},{9,8},{10,11... | collective-permute-start | bytes 393224 | tf_op jit(solution)/shard_map/ppermute | solution.py:608
  26.2 13.3 %collective-permute-start.12 = (bf16[4,32,512]{2,1,0:T(8,128)(2,1)S(1)}, bf16[4,32,512]{2,1,0:T(8,128)(2,1)S(1)}, u32[]{:S(2)}, u32[]{:S(2)}) collective-permute-start(bf16[4,32,512]{2,1,0:T(8,128)(2,1)S(1)} %get-tuple-element.128), channel_id=1, source_target_pairs={{0,1},{1,0},{2,3},{3,2},{4,5},{5,4},{6,7},{7,6},{8,9},{9,8},{10,11... | collective-permute-start | bytes 393224 | tf_op jit(solution)/shard_map/ppermute | solution.py:608
  27.5 12.1 %collective-permute-start.11 = (bf16[4,32,512]{2,1,0:T(8,128)(2,1)S(1)}, bf16[4,32,512]{2,1,0:T(8,128)(2,1)S(1)}, u32[]{:S(2)}, u32[]{:S(2)}) collective-permute-start(bf16[4,32,512]{2,1,0:T(8,128)(2,1)S(1)} %shard_map.111.refs_0_), channel_id=1, source_target_pairs={{0,2},{1,3},{2,0},{3,1},{4,6},{5,7},{6,4},{7,5},{8,10},{9,11},{10,... | collective-permute-start | bytes 393224 | tf_op jit(solution)/shard_map/ppermute | solution.py:622
  30.6 6.7 %collective-permute-start.9 = (bf16[2,3,16,512]{3,2,1,0:T(8,128)(2,1)S(1)}, bf16[2,3,16,512]{3,2,1,0:T(8,128)(2,1)S(1)}, u32[]{:S(2)}, u32[]{:S(2)}) collective-permute-start(bf16[2,3,16,512]{3,2,1,0:T(8,128)(2,1)S(1)} %get-tuple-element.123), channel_id=1, source_target_pairs={{0,12},{1,13},{2,14},{3,15},{4,0},{5,1},{6,2},{7,3},{8,4},{9,5},{1... | collective-permute-start | bytes 294920 | tf_op jit(solution)/shard_map/ppermute | solution.py:28
  31.3 6.5 %collective-permute-start.10 = (bf16[2,3,16,512]{3,2,1,0:T(8,128)(2,1)S(1)}, bf16[2,3,16,512]{3,2,1,0:T(8,128)(2,1)S(1)}, u32[]{:S(2)}, u32[]{:S(2)}) collective-permute-start(bf16[2,3,16,512]{3,2,1,0:T(8,128)(2,1)S(1)} %get-tuple-element.124), channel_id=1, source_target_pairs={{0,4},{1,5},{2,6},{3,7},{4,8},{5,9},{6,10},{7,11},{8,12},{9,13},{1... | collective-permute-start | bytes 294920 | tf_op jit(solution)/shard_map/ppermute | solution.py:28
  36.6 7.1 %collective-permute-start.8 = (bf16[18,32,128]{2,1,0:T(8,128)(2,1)S(1)}, bf16[18,32,128]{2,1,0:T(8,128)(2,1)S(1)}, u32[]{:S(2)}, u32[]{:S(2)}) collective-permute-start(bf16[18,32,128]{2,1,0:T(8,128)(2,1)S(1)} %get-tuple-element.120.after_ref), channel_id=1, source_target_pairs={{0,12},{1,13},{2,14},{3,15},{4,8},{5,9},{6,10},{7,11},{8,4},{9,5},... | collective-permute-start | bytes 442376 | tf_op jit(solution)/shard_map/ppermute | solution.py:632
  37.9 9.6 %collective-permute-start.13 = (bf16[2,3,16,512]{3,2,1,0:T(8,128)(2,1)S(1)}, bf16[2,3,16,512]{3,2,1,0:T(8,128)(2,1)S(1)}, u32[]{:S(2)}, u32[]{:S(2)}) collective-permute-start(bf16[2,3,16,512]{3,2,1,0:T(8,128)(2,1)S(1)} %get-tuple-element.131), channel_id=1, source_target_pairs={{0,15},{1,2},{2,1},{3,4},{4,3},{5,6},{6,5},{7,8},{8,7},{9,10},{10,... | collective-permute-start | bytes 294920 | tf_op jit(solution)/shard_map/ppermute | solution.py:43
  38.4 9.1 %collective-permute-start.14 = (bf16[2,3,16,512]{3,2,1,0:T(8,128)(2,1)S(1)}, bf16[2,3,16,512]{3,2,1,0:T(8,128)(2,1)S(1)}, u32[]{:S(2)}, u32[]{:S(2)}) collective-permute-start(bf16[2,3,16,512]{3,2,1,0:T(8,128)(2,1)S(1)} %get-tuple-element.125.refs_0_), channel_id=1, source_target_pairs={{0,1},{1,0},{2,3},{3,2},{4,5},{5,4},{6,7},{7,6},{8,9},{9,8},{10,11... | collective-permute-start | bytes 294920 | tf_op jit(solution)/shard_map/ppermute | solution.py:44
  39.7 8.9 %collective-permute-start.16 = (bf16[7,32,128]{2,1,0:T(8,128)(2,1)S(1)}, bf16[7,32,128]{2,1,0:T(8,128)(2,1)S(1)}, u32[]{:S(2)}, u32[]{:S(2)}) collective-permute-start(bf16[7,32,128]{2,1,0:T(8,128)(2,1)S(1)} %get-tuple-element.134), channel_id=1, source_target_pairs={{0,12},{1,13},{2,14},{3,15},{4,8},{5,9},{6,10},{7,11},{8,4},{9,5},... | collective-permute-start | bytes 172040 | tf_op jit(solution)/shard_map/ppermute | solution.py:632
  40.8 9.2 %collective-permute-start.17 = (bf16[7,32,128]{2,1,0:T(8,128)(2,1)S(1)}, bf16[7,32,128]{2,1,0:T(8,128)(2,1)S(1)}, u32[]{:S(2)}, u32[]{:S(2)}) collective-permute-start(bf16[7,32,128]{2,1,0:T(8,128)(2,1)S(1)} %get-tuple-element.135), channel_id=1, source_target_pairs={{0,8},{1,9},{2,10},{3,11},{4,12},{5,13},{6,14},{7,15},{8,0},{9,1},... | collective-permute-start | bytes 172040 | tf_op jit(solution)/shard_map/ppermute | solution.py:632
  43.7 3.8 %copy-start = (s32[1,8,16]{2,1,0:T(8,128)S(1)}, s32[1,8,16]{2,1,0:T(8,128)}, u32[]{:S(2)}) copy-start(s32[1,8,16]{2,1,0:T(8,128)} %send_ref.1) | copy-start | bytes 1540
  43.7 7.3 %collective-permute-start.15 = (bf16[16,32,128]{2,1,0:T(8,128)(2,1)S(1)}, bf16[16,32,128]{2,1,0:T(8,128)(2,1)S(1)}, u32[]{:S(2)}, u32[]{:S(2)}) collective-permute-start(bf16[16,32,128]{2,1,0:T(8,128)(2,1)S(1)} %get-tuple-element.130.after_ref), channel_id=1, source_target_pairs={{0,4},{1,5},{2,6},{3,7},{4,0},{5,1},{6,2},{7,3},{8,12},{9,13},{10,... | collective-permute-start | bytes 393224 | tf_op jit(solution)/shard_map/ppermute | solution.py:632

commit v18 on v17

--- a/solution.py
+++ b/solution.py
@@ -396,11 +396,10 @@
 
 def halve(rows, kept_ref, sent_ref):
     half = len(rows) // 2
-    for i, row in enumerate(rows):
-        if i < half:
-            kept_ref[i] = row
-        else:
-            put(row, sent_ref, (i - half) * row.shape[1] // 128)
+    for i in range(half):
+        kept_ref[i] = rows[i]
+        row = rows[i ^ (len(rows) - 1)]
+        put(row, sent_ref, i * row.shape[1] // 128)
 
 
 def add_received(kept_ref, received_ref):
@@ -640,7 +639,7 @@
         ],
         (node, own_a, core_own, y_a), specs=[pl.ANY], flops=2 * 10**10,
     )
-    in_a = exchange(sent_a, planes // 2)
+    in_a = exchange(sent_a, planes - 1)
     outgoing = call(
         relay_kernel, [three, three],
         (place, sent_a, own_right, own_left, from_plus, from_minus),

time: 52.1 us -> 53.4 us (1.025)
  waiting for transfers between devices: 15.1 us -> 19.7 us
  starting transfers between devices: 20.2 us -> 16.3 us
  local copies, waits for them, and re-layouts: 0.01 us -> 0.55 us
    ppermute x4, starting transfers between devices: 6.27 us -> 2.49 us  [exchange(): return lax.ppermute(sent, 'patch', along_z(count, distance))]
    ppermute x4, waiting for transfers between devices: 4.86 us -> 8.63 us  [exchange(): return lax.ppermute(sent, 'patch', along_z(count, distance))]
    ppermute x4, waiting for transfers between devices: 2.16 us -> 3 us  [shifted(): lax.ppermute(shard, 'patch', [(i, (i + by) % count) for i in range(count)])]
    unnamed x2, local copies, waits for them, and re-layouts: 0.01 us -> 0.55 us
  transfers between devices with their start and end apart: 18 -> 18, of which waited for: 10 -> 10; matrix products, arithmetic and copies ran while one was open for 0% -> 0% of each run, Pallas kernels for 18% -> 17%
where the time goes in v18:
time: 53.4 us; the launch traced here: 53.2 us
  waiting for transfers between devices  19.7 us (37%)
  starting transfers between devices  16.3 us (31%)
  Pallas kernels  15.7 us (29%)
  between operations  0.79 us (1%)
  local copies, waits for them, and re-layouts  0.55 us (1%)
    pallas_call x16, Pallas kernels, call(): pl.pallas_call(kernel, out_shape=[jax.ShapeDtypeStruct(*o) if final else...  15.7 us
    ppermute x4, waiting for transfers between devices, exchange(): return lax.ppermute(sent, 'patch', along_z(count, distance))  8.63 us
    ppermute x4, starting transfers between devices, shifted(): lax.ppermute(shard, 'patch', [(i, (i + by) % count) for i in range(count)])  7.25 us
    ppermute x1, waiting for transfers between devices, body(): y_a = lax.ppermute(y_sent, 'patch', flop)  3.75 us
    ppermute x4, waiting for transfers between devices, shifted(): lax.ppermute(shard, 'patch', [(i, (i + by) % count) for i in range(count)])  3 us
    ppermute x4, starting transfers between devices, exchange(): return lax.ppermute(sent, 'patch', along_z(count, distance))  2.49 us
    ppermute x2, waiting for transfers between devices, swap(): later = lax.ppermute(pair[1], 'patch', second)  2.3 us
    ppermute x1, starting transfers between devices, body(): y_b = lax.ppermute(y_sent, 'patch', flop)  2.07 us
  transfers between devices with their start and end apart: 18, of which 10 were waited for; matrix products, arithmetic and copies ran while one was open for 0% of the time, Pallas kernels for 17%

profile of v18, /device:TPU:0, one launch (start us, length us, event | category | flops | bytes accessed | tf_op | source)
XLA Modules:
  0.0 53.2 jit_solution(5161620501225611329)
XLA Ops:
  0.6 1.2 %shard_map.104 = (bf16[2,3,16,512]{3,2,1,0:T(8,128)(2,1)S(1)}, bf16[2,3,16,512]{3,2,1,0:T(8,128)(2,1)S(1)}, bf16[2,1,16,512]{3,2,1,0:T(8,128)(2,1)S(1)}, bf16[2,...) custom-call(s32[1,8,16]{2,1,0:T(8,128)} %send_ref.1, bf16[2,128,512]{2,1,0:T(8,128)(2,1)} %x_hbm.1), custom_call_target="tpu_custom_call" | custom-call | flops 1000000 | bytes 10000 | tf_op jit(solution)/shard_map/pallas_call | solution.py:505
  1.8 3.1 %collective-permute-start = (bf16[2,3,16,512]{3,2,1,0:T(8,128)(2,1)S(1)}, bf16[2,3,16,512]{3,2,1,0:T(8,128)(2,1)S(1)}, u32[]{:S(2)}, u32[]{:S(2)}) collective-permute-start(bf16[2,3,16,512]{3,2,1,0:T(8,128)(2,1)S(1)} %get-tuple-element.74), channel_id=1, source_target_pairs={{0,4},{1,5},{2,6},{3,7},{4,8},{5,9},{6,10},{7,11},{8,12},{9,13},{1... | collective-permute-start | bytes 294920 | tf_op jit(solution)/shard_map/ppermute | solution.py:28
  4.9 2.1 %collective-permute-start.1 = (bf16[2,3,16,512]{3,2,1,0:T(8,128)(2,1)S(1)}, bf16[2,3,16,512]{3,2,1,0:T(8,128)(2,1)S(1)}, u32[]{:S(2)}, u32[]{:S(2)}) collective-permute-start(bf16[2,3,16,512]{3,2,1,0:T(8,128)(2,1)S(1)} %get-tuple-element.75), channel_id=1, source_target_pairs={{0,12},{1,13},{2,14},{3,15},{4,0},{5,1},{6,2},{7,3},{8,4},{9,5},{1... | collective-permute-start | bytes 294920 | tf_op jit(solution)/shard_map/ppermute | solution.py:28
  7.0 2.6 %shard_map.105 = (bf16[8,2,128,128]{3,2,1,0:T(8,128)(2,1)S(1)}, bf16[8,2,128,128]{3,2,1,0:T(8,128)(2,1)S(1)}, bf16[8,2,128,128]{3,2,1,0:T(8,128)(2,1)S(1)}, bf16...) custom-call(bf16[2,1,16,512]{3,2,1,0:T(8,128)(2,1)S(1)} %get-tuple-e, ...), custom_call_target="tpu_custom_call" | custom-call | flops 1000000 | bytes 10000 | tf_op jit(solution)/shard_map/pallas_call | solution.py:505
  9.7 0.8 %collective-permute-done.plus_ref = bf16[2,3,16,512]{3,2,1,0:T(8,128)(2,1)S(1)} collective-permute-done((bf16[2,3,16,512]{3,2,1,0:T(8,128)(2,1)S(1)}, bf16[2,3,16,512]{3,2,1,0:T(8,128)(2,1)S(1)}, u32[]{:S(2)}, u32[]{:S(2)}) %collective-permute-start) | collective-permute-done | bytes 98336 | tf_op jit(solution)/shard_map/ppermute | solution.py:28
  10.4 0.8 %collective-permute-done.1.minus_ref = bf16[2,3,16,512]{3,2,1,0:T(8,128)(2,1)S(1)} collective-permute-done((bf16[2,3,16,512]{3,2,1,0:T(8,128)(2,1)S(1)}, bf16[2,3,16,512]{3,2,1,0:T(8,128)(2,1)S(1)}, u32[]{:S(2)}, u32[]{:S(2)}) %collective-permute-start.1) | collective-permute-done | bytes 98336 | tf_op jit(solution)/shard_map/ppermute | solution.py:28
  11.3 1.7 %collective-permute-start.2 = (bf16[2,3,16,512]{3,2,1,0:T(8,128)(2,1)S(1)}, bf16[2,3,16,512]{3,2,1,0:T(8,128)(2,1)S(1)}, u32[]{:S(2)}, u32[]{:S(2)}) collective-permute-start(bf16[2,3,16,512]{3,2,1,0:T(8,128)(2,1)S(1)} %get-tuple-element.76.after_ref), channel_id=1, source_target_pairs={{0,15},{1,2},{2,1},{3,4},{4,3},{5,6},{6,5},{7,8},{8,7},{9,10},{10,... | collective-permute-start | bytes 294920 | tf_op jit(solution)/shard_map/ppermute | solution.py:43
  13.0 0.0 collective-permute-start.3
  13.0 1.4 %shard_map.108.refs_4_.refs_12_ = f32[256,128]{1,0:T(8,128)S(1)} custom-call(bf16[2,3,16,512]{3,2,1,0:T(8,128)(2,1)S(1)} %get-tuple-element.76.after_ref, s32[128,256]{1,0:T(8,128)S(1)} %get-tuple-element.84.neigh_ref, s32[1,128]{1,0:T(1,128)S(1)} %get-tuple-element.85.count_ref), custom_call_target="tpu_custom_call" | custom-call | flops 1000000 | bytes 10000 | tf_op jit(solution)/shard_map/pallas_call | solution.py:505
  14.5 1.4 %shard_map.109 = (f32[3,2,128,512]{3,2,1,0:T(8,128)S(1)}, f32[2,2,8,512]{3,2,1,0:T(8,128)S(1)}, f32[3,2,128,512]{3,2,1,0:T(8,128)S(1)}, f32[2,2,8,512]{3,2,1,0:T...) custom-call(bf16[8,2,128,128]{3,2,1,0:T(8,128)(2,1)S(1)} %get-tuple-, ...), custom_call_target="tpu_custom_call" | custom-call | flops 1000000 | bytes 10000 | tf_op jit(solution)/shard_map/pallas_call | solution.py:505
  15.8 2.3 %collective-permute-done.2.second_in = bf16[2,3,16,512]{3,2,1,0:T(8,128)(2,1)S(1)} collective-permute-done((bf16[2,3,16,512]{3,2,1,0:T(8,128)(2,1)S(1)}, bf16[2,3,16,512]{3,2,1,0:T(8,128)(2,1)S(1)}, u32[]{:S(2)}, u32[]{:S(2)}) %collective-permute-start.2) | collective-permute-done | bytes 98336 | tf_op jit(solution)/shard_map/ppermute | solution.py:43
  18.1 0.0 collective-permute-done.3.first_in
  18.1 0.6 %shard_map.107 = (bf16[4,2,128,128]{3,2,1,0:T(8,128)(2,1)S(1)}, bf16[4,2,128,128]{3,2,1,0:T(8,128)(2,1)S(1)}, bf16[4,2,128,128]{3,2,1,0:T(8,128)(2,1)S(1)}, bf16...) custom-call(s32[1]{0:T(128)} %bitcast.me_ref, bf16[2,3,16,512]{3,2,1,0:T(8,128)(2,1)S(1)} %collective-permute-done.2.second_in, ...), custom_call_target="tpu_custom_call" | custom-call | flops 1000000 | bytes 10000 | tf_op jit(solution)/shard_map/pallas_call | solution.py:505
  18.7 3.8 %shard_map.112 = (f32[4,32,1536]{2,1,0:T(8,128)S(1)}, f32[4,32,1536]{2,1,0:T(8,128)S(1)}, bf16[4,32,1536]{2,1,0:T(8,128)(2,1)S(1)}, bf16[4,32,1536]{2,1,0:T(8,12...) custom-call(s32[1]{0:T(128)} %bitcast.me_ref, ...), custom_call_target="tpu_custom_call" | custom-call | flops 1000000 | bytes 10000 | tf_op jit(solution)/shard_map/pallas_call | solution.py:505
  22.5 0.1 collective-permute-start.6
  22.6 0.5 collective-permute-start.5
  23.1 1.2 %collective-permute-done.6 = bf16[4,32,1536]{2,1,0:T(8,128)(2,1)S(1)} collective-permute-done((bf16[4,32,1536]{2,1,0:T(8,128)(2,1)S(1)}, bf16[4,32,1536]{2,1,0:T(8,128)(2,1)S(1)}, u32[]{:S(2)}, u32[]{:S(2)}) %collective-permute-start.6) | collective-permute-done | bytes 393248 | tf_op jit(solution)/shard_map/ppermute | solution.py:607
  24.3 0.1 add_convert_fusion
  24.4 0.1 collective-permute-start.7
  24.5 1.5 %shard_map.110 = (f32[4,32,512]{2,1,0:T(8,128)S(1)}, f32[4,32,512]{2,1,0:T(8,128)S(1)}, bf16[4,32,512]{2,1,0:T(8,128)(2,1)S(1)}, bf16[4,32,512]{2,1,0:T(8,128)(2...) custom-call(s32[1]{0:T(128)} %bitcast.me_ref, ...), custom_call_target="tpu_custom_call" | custom-call | flops 1000000 | bytes 10000 | tf_op jit(solution)/shard_map/pallas_call | solution.py:505
  26.0 0.2 collective-permute-start.4
  26.2 0.4 collective-permute-start.12
  26.6 0.8 %collective-permute-done.4.refs_1_ = bf16[4,32,512]{2,1,0:T(8,128)(2,1)S(1)} collective-permute-done((bf16[4,32,512]{2,1,0:T(8,128)(2,1)S(1)}, bf16[4,32,512]{2,1,0:T(8,128)(2,1)S(1)}, u32[]{:S(2)}, u32[]{:S(2)}) %collective-permute-start.4) | collective-permute-done | bytes 131104 | tf_op jit(solution)/shard_map/ppermute | solution.py:607
  27.5 2.1 %collective-permute-start.11 = (bf16[4,32,512]{2,1,0:T(8,128)(2,1)S(1)}, bf16[4,32,512]{2,1,0:T(8,128)(2,1)S(1)}, u32[]{:S(2)}, u32[]{:S(2)}) collective-permute-start(bf16[4,32,512]{2,1,0:T(8,128)(2,1)S(1)} %shard_map.111.refs_0_), channel_id=1, source_target_pairs={{0,2},{1,3},{2,0},{3,1},{4,6},{5,7},{6,4},{7,5},{8,10},{9,11},{10,... | collective-permute-start | bytes 393224 | tf_op jit(solution)/shard_map/ppermute | solution.py:621
  29.6 1.0 %shard_map.113 = (f32[2,128,512]{2,1,0:T(8,128)S(1)}, bf16[2,3,16,512]{3,2,1,0:T(8,128)(2,1)S(1)}, bf16[2,3,16,512]{3,2,1,0:T(8,128)(2,1)S(1)}, bf16[2,1,16,512]...) custom-call(bf16[4,32,512]{2,1,0:T(8,128)(2,1)S(1)} %shard_map.111.refs_0_, ...), custom_call_target="tpu_custom_call" | custom-call | flops 1000000 | bytes 10000 | tf_op jit(solution)/shard_map/pallas_call | solution.py:505
  30.6 0.8 %collective-permute-start.9 = (bf16[2,3,16,512]{3,2,1,0:T(8,128)(2,1)S(1)}, bf16[2,3,16,512]{3,2,1,0:T(8,128)(2,1)S(1)}, u32[]{:S(2)}, u32[]{:S(2)}) collective-permute-start(bf16[2,3,16,512]{3,2,1,0:T(8,128)(2,1)S(1)} %get-tuple-element.123), channel_id=1, source_target_pairs={{0,12},{1,13},{2,14},{3,15},{4,0},{5,1},{6,2},{7,3},{8,4},{9,5},{1... | collective-permute-start | bytes 294920 | tf_op jit(solution)/shard_map/ppermute | solution.py:28
  31.3 0.0 collective-permute-done.5.core_in
  31.3 1.3 %collective-permute-start.10 = (bf16[2,3,16,512]{3,2,1,0:T(8,128)(2,1)S(1)}, bf16[2,3,16,512]{3,2,1,0:T(8,128)(2,1)S(1)}, u32[]{:S(2)}, u32[]{:S(2)}) collective-permute-start(bf16[2,3,16,512]{3,2,1,0:T(8,128)(2,1)S(1)} %get-tuple-element.124), channel_id=1, source_target_pairs={{0,4},{1,5},{2,6},{3,7},{4,8},{5,9},{6,10},{7,11},{8,12},{9,13},{1... | collective-permute-start | bytes 294920 | tf_op jit(solution)/shard_map/ppermute | solution.py:28
  32.7 3.8 %collective-permute-done.7.y_in = bf16[4,32,1536]{2,1,0:T(8,128)(2,1)S(1)} collective-permute-done((bf16[4,32,1536]{2,1,0:T(8,128)(2,1)S(1)}, bf16[4,32,1536]{2,1,0:T(8,128)(2,1)S(1)}, u32[]{:S(2)}, u32[]{:S(2)}) %collective-permute-start.7) | collective-permute-done | bytes 393248 | tf_op jit(solution)/shard_map/ppermute | solution.py:614
  36.4 0.1 shard_map.114
  36.6 0.1 collective-permute-start.8
  36.6 0.0 collective-permute-done.9.plus_ref
  36.7 1.4 %collective-permute-done.10.minus_ref = bf16[2,3,16,512]{3,2,1,0:T(8,128)(2,1)S(1)} collective-permute-done((bf16[2,3,16,512]{3,2,1,0:T(8,128)(2,1)S(1)}, bf16[2,3,16,512]{3,2,1,0:T(8,128)(2,1)S(1)}, u32[]{:S(2)}, u32[]{:S(2)}) %collective-permute-start.10) | collective-permute-done | bytes 98336 | tf_op jit(solution)/shard_map/ppermute | solution.py:28
  38.1 0.1 collective-permute-start.13
  38.1 1.5 %collective-permute-start.14 = (bf16[2,3,16,512]{3,2,1,0:T(8,128)(2,1)S(1)}, bf16[2,3,16,512]{3,2,1,0:T(8,128)(2,1)S(1)}, u32[]{:S(2)}, u32[]{:S(2)}) collective-permute-start(bf16[2,3,16,512]{3,2,1,0:T(8,128)(2,1)S(1)} %get-tuple-element.125.refs_0_), channel_id=1, source_target_pairs={{0,1},{1,0},{2,3},{3,2},{4,5},{5,4},{6,7},{7,6},{8,9},{9,8},{10,11... | collective-permute-start | bytes 294920 | tf_op jit(solution)/shard_map/ppermute | solution.py:44
  39.7 0.0 collective-permute-done.12.refs_4_
  39.7 0.0 collective-permute-done.11.refs_2_
  39.7 0.1 shard_map.116
  39.8 0.9 %collective-permute-start.16 = (bf16[7,32,128]{2,1,0:T(8,128)(2,1)S(1)}, bf16[7,32,128]{2,1,0:T(8,128)(2,1)S(1)}, u32[]{:S(2)}, u32[]{:S(2)}) collective-permute-start(bf16[7,32,128]{2,1,0:T(8,128)(2,1)S(1)} %get-tuple-element.134), channel_id=1, source_target_pairs={{0,12},{1,13},{2,14},{3,15},{4,8},{5,9},{6,10},{7,11},{8,4},{9,5},... | collective-permute-start | bytes 172040 | tf_op jit(solution)/shard_map/ppermute | solution.py:631
  40.7 1.5 %collective-permute-start.17 = (bf16[7,32,128]{2,1,0:T(8,128)(2,1)S(1)}, bf16[7,32,128]{2,1,0:T(8,128)(2,1)S(1)}, u32[]{:S(2)}, u32[]{:S(2)}) collective-permute-start(bf16[7,32,128]{2,1,0:T(8,128)(2,1)S(1)} %get-tuple-element.135), channel_id=1, source_target_pairs={{0,8},{1,9},{2,10},{3,11},{4,12},{5,13},{6,14},{7,15},{8,0},{9,1},... | collective-permute-start | bytes 172040 | tf_op jit(solution)/shard_map/ppermute | solution.py:631
  42.1 5.2 %collective-permute-done.8.in_a = bf16[18,32,128]{2,1,0:T(8,128)(2,1)S(1)} collective-permute-done((bf16[18,32,128]{2,1,0:T(8,128)(2,1)S(1)}, bf16[18,32,128]{2,1,0:T(8,128)(2,1)S(1)}, u32[]{:S(2)}, u32[]{:S(2)}) %collective-permute-start.8) | collective-permute-done | bytes 147488 | tf_op jit(solution)/shard_map/ppermute | solution.py:631
  47.4 0.1 collective-permute-start.15
  47.5 0.0 collective-permute-done.13.second_in
  47.5 0.5 %copy-done = s32[1,8,16]{2,1,0:T(8,128)S(1)} copy-done((s32[1,8,16]{2,1,0:T(8,128)S(1)}, s32[1,8,16]{2,1,0:T(8,128)}, u32[]{:S(2)}) %copy-start) | copy-done | bytes 536
  48.0 1.0 %shard_map.118.after_ref = bf16[2,128,512]{2,1,0:T(8,128)(2,1)} custom-call(s32[1]{0:T(128)} %bitcast.me_ref, bf16[16,32,128]{2,1,0:T(8,128)(2,1)S(1)} %get-tuple-element.130.after_ref, bf16[2,3,16,512]{3,2,1,0:T(8,128)(2,1)S(1)} %collective-permute-done.13.second_in, bf16[2,3,16,512]{3,2,1,0:T(8,128)(2,1)S(1)} %collective-permute-done.14.first_in, ...), custom_call_target="tpu_custom_call" | custom-call | flops 20000000000 | bytes 10000 | tf_op jit(solution)/shard_map/pallas_call | solution.py:505
  49.0 1.0 %collective-permute-done.17.refs_2_ = bf16[7,32,128]{2,1,0:T(8,128)(2,1)S(1)} collective-permute-done((bf16[7,32,128]{2,1,0:T(8,128)(2,1)S(1)}, bf16[7,32,128]{2,1,0:T(8,128)(2,1)S(1)}, u32[]{:S(2)}, u32[]{:S(2)}) %collective-permute-start.17) | collective-permute-done | bytes 57376 | tf_op jit(solution)/shard_map/ppermute | solution.py:631
  50.0 2.4 %collective-permute-done.15.refs_0_ = bf16[16,32,128]{2,1,0:T(8,128)(2,1)S(1)} collective-permute-done((bf16[16,32,128]{2,1,0:T(8,128)(2,1)S(1)}, bf16[16,32,128]{2,1,0:T(8,128)(2,1)S(1)}, u32[]{:S(2)}, u32[]{:S(2)}) %collective-permute-start.15) | collective-permute-done | bytes 131104 | tf_op jit(solution)/shard_map/ppermute | solution.py:631
  52.4 0.7 %shard_map.119 = f32[32,2048]{1,0:T(8,128)} custom-call(bf16[2,128,512]{2,1,0:T(8,128)(2,1)} %shard_map.118.after_ref, f32[32,1152]{1,0:T(8,128)S(1)} %get-tuple-element.132.own_a, f32[32,896]{1,0:T(8,128)S(1)} %get-tuple-element.133.own_b, bf16[16,32,128]{2,1,0:T(8,128)(2,1)S(1)} %collective-permute-done.15.refs_0_, ...), custom_call_target="tpu_custom_call" | custom-call | flops 1000000 | bytes 10000 | tf_op jit(solution)/shard_map/pallas_call | solution.py:505
  (7 shorter events, 0.1 us)
Async XLA Ops:
  1.8 8.6 %collective-permute-start = (bf16[2,3,16,512]{3,2,1,0:T(8,128)(2,1)S(1)}, bf16[2,3,16,512]{3,2,1,0:T(8,128)(2,1)S(1)}, u32[]{:S(2)}, u32[]{:S(2)}) collective-permute-start(bf16[2,3,16,512]{3,2,1,0:T(8,128)(2,1)S(1)} %get-tuple-element.74), channel_id=1, source_target_pairs={{0,4},{1,5},{2,6},{3,7},{4,8},{5,9},{6,10},{7,11},{8,12},{9,13},{1... | collective-permute-start | bytes 294920 | tf_op jit(solution)/shard_map/ppermute | solution.py:28
  4.9 6.4 %collective-permute-start.1 = (bf16[2,3,16,512]{3,2,1,0:T(8,128)(2,1)S(1)}, bf16[2,3,16,512]{3,2,1,0:T(8,128)(2,1)S(1)}, u32[]{:S(2)}, u32[]{:S(2)}) collective-permute-start(bf16[2,3,16,512]{3,2,1,0:T(8,128)(2,1)S(1)} %get-tuple-element.75), channel_id=1, source_target_pairs={{0,12},{1,13},{2,14},{3,15},{4,0},{5,1},{6,2},{7,3},{8,4},{9,5},{1... | collective-permute-start | bytes 294920 | tf_op jit(solution)/shard_map/ppermute | solution.py:28
  11.3 6.8 %collective-permute-start.2 = (bf16[2,3,16,512]{3,2,1,0:T(8,128)(2,1)S(1)}, bf16[2,3,16,512]{3,2,1,0:T(8,128)(2,1)S(1)}, u32[]{:S(2)}, u32[]{:S(2)}) collective-permute-start(bf16[2,3,16,512]{3,2,1,0:T(8,128)(2,1)S(1)} %get-tuple-element.76.after_ref), channel_id=1, source_target_pairs={{0,15},{1,2},{2,1},{3,4},{4,3},{5,6},{6,5},{7,8},{8,7},{9,10},{10,... | collective-permute-start | bytes 294920 | tf_op jit(solution)/shard_map/ppermute | solution.py:43
  13.0 5.1 %collective-permute-start.3 = (bf16[2,3,16,512]{3,2,1,0:T(8,128)(2,1)S(1)}, bf16[2,3,16,512]{3,2,1,0:T(8,128)(2,1)S(1)}, u32[]{:S(2)}, u32[]{:S(2)}) collective-permute-start(bf16[2,3,16,512]{3,2,1,0:T(8,128)(2,1)S(1)} %get-tuple-element.77), channel_id=1, source_target_pairs={{0,1},{1,0},{2,3},{3,2},{4,5},{5,4},{6,7},{7,6},{8,9},{9,8},{10,11... | collective-permute-start | bytes 294920 | tf_op jit(solution)/shard_map/ppermute | solution.py:44
  22.5 1.8 %collective-permute-start.6 = (bf16[4,32,1536]{2,1,0:T(8,128)(2,1)S(1)}, bf16[4,32,1536]{2,1,0:T(8,128)(2,1)S(1)}, u32[]{:S(2)}, u32[]{:S(2)}) collective-permute-start(bf16[4,32,1536]{2,1,0:T(8,128)(2,1)S(1)} %get-tuple-element.118), channel_id=1, source_target_pairs={{0,1},{1,0},{2,3},{3,2},{4,5},{5,4},{6,7},{7,6},{8,9},{9,8},{10,11... | collective-permute-start | bytes 1179656 | tf_op jit(solution)/shard_map/ppermute | solution.py:607
  22.6 8.7 %collective-permute-start.5 = (bf16[4,32,1536]{2,1,0:T(8,128)(2,1)S(1)}, bf16[4,32,1536]{2,1,0:T(8,128)(2,1)S(1)}, u32[]{:S(2)}, u32[]{:S(2)}) collective-permute-start(bf16[4,32,1536]{2,1,0:T(8,128)(2,1)S(1)} %get-tuple-element.116), channel_id=1, source_target_pairs={{0,1},{1,0},{2,3},{3,2},{4,5},{5,4},{6,7},{7,6},{8,9},{9,8},{10,11... | collective-permute-start | bytes 1179656 | tf_op jit(solution)/shard_map/ppermute | solution.py:607
  24.4 12.0 %collective-permute-start.7 = (bf16[4,32,1536]{2,1,0:T(8,128)(2,1)S(1)}, bf16[4,32,1536]{2,1,0:T(8,128)(2,1)S(1)}, u32[]{:S(2)}, u32[]{:S(2)}) collective-permute-start(bf16[4,32,1536]{2,1,0:T(8,128)(2,1)S(1)} %add_convert_fusion), channel_id=1, source_target_pairs={{0,2},{1,3},{2,0},{3,1},{4,6},{5,7},{6,4},{7,5},{8,10},{9,11},{10,... | collective-permute-start | bytes 1179656 | tf_op jit(solution)/shard_map/ppermute | solution.py:614
  26.0 1.4 %collective-permute-start.4 = (bf16[4,32,512]{2,1,0:T(8,128)(2,1)S(1)}, bf16[4,32,512]{2,1,0:T(8,128)(2,1)S(1)}, u32[]{:S(2)}, u32[]{:S(2)}) collective-permute-start(bf16[4,32,512]{2,1,0:T(8,128)(2,1)S(1)} %get-tuple-element.91), channel_id=1, source_target_pairs={{0,1},{1,0},{2,3},{3,2},{4,5},{5,4},{6,7},{7,6},{8,9},{9,8},{10,11... | collective-permute-start | bytes 393224 | tf_op jit(solution)/shard_map/ppermute | solution.py:607
  26.2 13.5 %collective-permute-start.12 = (bf16[4,32,512]{2,1,0:T(8,128)(2,1)S(1)}, bf16[4,32,512]{2,1,0:T(8,128)(2,1)S(1)}, u32[]{:S(2)}, u32[]{:S(2)}) collective-permute-start(bf16[4,32,512]{2,1,0:T(8,128)(2,1)S(1)} %get-tuple-element.128), channel_id=1, source_target_pairs={{0,1},{1,0},{2,3},{3,2},{4,5},{5,4},{6,7},{7,6},{8,9},{9,8},{10,11... | collective-permute-start | bytes 393224 | tf_op jit(solution)/shard_map/ppermute | solution.py:607
  27.5 12.2 %collective-permute-start.11 = (bf16[4,32,512]{2,1,0:T(8,128)(2,1)S(1)}, bf16[4,32,512]{2,1,0:T(8,128)(2,1)S(1)}, u32[]{:S(2)}, u32[]{:S(2)}) collective-permute-start(bf16[4,32,512]{2,1,0:T(8,128)(2,1)S(1)} %shard_map.111.refs_0_), channel_id=1, source_target_pairs={{0,2},{1,3},{2,0},{3,1},{4,6},{5,7},{6,4},{7,5},{8,10},{9,11},{10,... | collective-permute-start | bytes 393224 | tf_op jit(solution)/shard_map/ppermute | solution.py:621
  30.6 6.1 %collective-permute-start.9 = (bf16[2,3,16,512]{3,2,1,0:T(8,128)(2,1)S(1)}, bf16[2,3,16,512]{3,2,1,0:T(8,128)(2,1)S(1)}, u32[]{:S(2)}, u32[]{:S(2)}) collective-permute-start(bf16[2,3,16,512]{3,2,1,0:T(8,128)(2,1)S(1)} %get-tuple-element.123), channel_id=1, source_target_pairs={{0,12},{1,13},{2,14},{3,15},{4,0},{5,1},{6,2},{7,3},{8,4},{9,5},{1... | collective-permute-start | bytes 294920 | tf_op jit(solution)/shard_map/ppermute | solution.py:28
  31.3 6.7 %collective-permute-start.10 = (bf16[2,3,16,512]{3,2,1,0:T(8,128)(2,1)S(1)}, bf16[2,3,16,512]{3,2,1,0:T(8,128)(2,1)S(1)}, u32[]{:S(2)}, u32[]{:S(2)}) collective-permute-start(bf16[2,3,16,512]{3,2,1,0:T(8,128)(2,1)S(1)} %get-tuple-element.124), channel_id=1, source_target_pairs={{0,4},{1,5},{2,6},{3,7},{4,8},{5,9},{6,10},{7,11},{8,12},{9,13},{1... | collective-permute-start | bytes 294920 | tf_op jit(solution)/shard_map/ppermute | solution.py:28
  36.6 10.8 %collective-permute-start.8 = (bf16[18,32,128]{2,1,0:T(8,128)(2,1)S(1)}, bf16[18,32,128]{2,1,0:T(8,128)(2,1)S(1)}, u32[]{:S(2)}, u32[]{:S(2)}) collective-permute-start(bf16[18,32,128]{2,1,0:T(8,128)(2,1)S(1)} %get-tuple-element.120.after_ref), channel_id=1, source_target_pairs={{0,8},{1,9},{2,10},{3,11},{4,12},{5,13},{6,14},{7,15},{8,0},{9,1},... | collective-permute-start | bytes 442376 | tf_op jit(solution)/shard_map/ppermute | solution.py:631
  38.1 9.4 %collective-permute-start.13 = (bf16[2,3,16,512]{3,2,1,0:T(8,128)(2,1)S(1)}, bf16[2,3,16,512]{3,2,1,0:T(8,128)(2,1)S(1)}, u32[]{:S(2)}, u32[]{:S(2)}) collective-permute-start(bf16[2,3,16,512]{3,2,1,0:T(8,128)(2,1)S(1)} %get-tuple-element.131), channel_id=1, source_target_pairs={{0,15},{1,2},{2,1},{3,4},{4,3},{5,6},{6,5},{7,8},{8,7},{9,10},{10,... | collective-permute-start | bytes 294920 | tf_op jit(solution)/shard_map/ppermute | solution.py:43
  38.1 9.3 %collective-permute-start.14 = (bf16[2,3,16,512]{3,2,1,0:T(8,128)(2,1)S(1)}, bf16[2,3,16,512]{3,2,1,0:T(8,128)(2,1)S(1)}, u32[]{:S(2)}, u32[]{:S(2)}) collective-permute-start(bf16[2,3,16,512]{3,2,1,0:T(8,128)(2,1)S(1)} %get-tuple-element.125.refs_0_), channel_id=1, source_target_pairs={{0,1},{1,0},{2,3},{3,2},{4,5},{5,4},{6,7},{7,6},{8,9},{9,8},{10,11... | collective-permute-start | bytes 294920 | tf_op jit(solution)/shard_map/ppermute | solution.py:44
  39.8 9.2 %collective-permute-start.16 = (bf16[7,32,128]{2,1,0:T(8,128)(2,1)S(1)}, bf16[7,32,128]{2,1,0:T(8,128)(2,1)S(1)}, u32[]{:S(2)}, u32[]{:S(2)}) collective-permute-start(bf16[7,32,128]{2,1,0:T(8,128)(2,1)S(1)} %get-tuple-element.134), channel_id=1, source_target_pairs={{0,12},{1,13},{2,14},{3,15},{4,8},{5,9},{6,10},{7,11},{8,4},{9,5},... | collective-permute-start | bytes 172040 | tf_op jit(solution)/shard_map/ppermute | solution.py:631
  40.7 9.4 %collective-permute-start.17 = (bf16[7,32,128]{2,1,0:T(8,128)(2,1)S(1)}, bf16[7,32,128]{2,1,0:T(8,128)(2,1)S(1)}, u32[]{:S(2)}, u32[]{:S(2)}) collective-permute-start(bf16[7,32,128]{2,1,0:T(8,128)(2,1)S(1)} %get-tuple-element.135), channel_id=1, source_target_pairs={{0,8},{1,9},{2,10},{3,11},{4,12},{5,13},{6,14},{7,15},{8,0},{9,1},... | collective-permute-start | bytes 172040 | tf_op jit(solution)/shard_map/ppermute | solution.py:631
  47.3 0.7 %copy-start = (s32[1,8,16]{2,1,0:T(8,128)S(1)}, s32[1,8,16]{2,1,0:T(8,128)}, u32[]{:S(2)}) copy-start(s32[1,8,16]{2,1,0:T(8,128)} %send_ref.1) | copy-start | bytes 1540
  47.4 5.0 %collective-permute-start.15 = (bf16[16,32,128]{2,1,0:T(8,128)(2,1)S(1)}, bf16[16,32,128]{2,1,0:T(8,128)(2,1)S(1)}, u32[]{:S(2)}, u32[]{:S(2)}) collective-permute-start(bf16[16,32,128]{2,1,0:T(8,128)(2,1)S(1)} %get-tuple-element.130.after_ref), channel_id=1, source_target_pairs={{0,4},{1,5},{2,6},{3,7},{4,0},{5,1},{6,2},{7,3},{8,12},{9,13},{10,... | collective-permute-start | bytes 393224 | tf_op jit(solution)/shard_map/ppermute | solution.py:631

commit v19 on v15

--- a/solution.py
+++ b/solution.py
@@ -479,7 +479,7 @@
 
 
 def weight_kernel(after_ref, own_a, own_b, *refs):
-    received, out_ref = refs[:-1], refs[-1]
+    received, out_ref = refs[-2::-1], refs[-1]
     a, b = own_a[...], own_b[...]
     blocks, more = b.shape[1] // 128, a.shape[1] // 128
     for k, ref in enumerate(received, 1):
@@ -669,7 +669,7 @@
         specs=[pltpu.SMEM, pl.ANY], scratch=[trio], final=True, flops=2 * 10**10,
     )
     (weight_grad,) = call(
-        weight_kernel, [((rows, 4 * width), f32)], (node_grad, own_a, own_b, *received),
+        weight_kernel, [((rows, 4 * width), f32)], (node_grad, own_a, own_b, *received[::-1]),
         specs=[pltpu.HBM], final=True,
     )
     return (node_grad, weight_grad)

time: 51.3 us -> 50.4 us (0.982)
  waiting for transfers between devices: 17 us -> 15.9 us
    ppermute x4, waiting for transfers between devices: 4.08 us -> 2.87 us  [exchange(): return lax.ppermute(sent, 'patch', along_z(count, distance))]
  transfers between devices with their start and end apart: 18 -> 18, of which waited for: 10 -> 11; matrix products, arithmetic and copies ran while one was open for 0% -> 0% of each run, Pallas kernels for 18% -> 19%
where the time goes in v19:
time: 50.4 us; the launch traced here: 50 us
  starting transfers between devices  17.6 us (35%)
  waiting for transfers between devices  15.9 us (32%)
  Pallas kernels  15.7 us (31%)
  between operations  0.77 us (2%)
    pallas_call x16, Pallas kernels, call(): pl.pallas_call(kernel, out_shape=[jax.ShapeDtypeStruct(*o) if final else...  15.7 us
    ppermute x4, starting transfers between devices, shifted(): lax.ppermute(shard, 'patch', [(i, (i + by) % count) for i in range(count)])  7.25 us
    ppermute x4, starting transfers between devices, exchange(): return lax.ppermute(sent, 'patch', along_z(count, distance))  4.05 us
    ppermute x1, waiting for transfers between devices, body(): y_a = lax.ppermute(y_sent, 'patch', flop)  3.75 us
    ppermute x4, waiting for transfers between devices, shifted(): lax.ppermute(shard, 'patch', [(i, (i + by) % count) for i in range(count)])  3.75 us
    ppermute x2, waiting for transfers between devices, swap(): later = lax.ppermute(pair[1], 'patch', second)  3.46 us
    ppermute x4, waiting for transfers between devices, exchange(): return lax.ppermute(sent, 'patch', along_z(count, distance))  2.87 us
    ppermute x1, starting transfers between devices, body(): y_b = lax.ppermute(y_sent, 'patch', flop)  2.07 us
  transfers between devices with their start and end apart: 18, of which 11 were waited for; matrix products, arithmetic and copies ran while one was open for 0% of the time, Pallas kernels for 19%

profile of v19, /device:TPU:0, one launch (start us, length us, event | category | flops | bytes accessed | tf_op | source)
XLA Modules:
  0.0 50.0 jit_solution(15281102334262351549)
XLA Ops:
  0.6 1.2 %shard_map.104 = (bf16[2,3,16,512]{3,2,1,0:T(8,128)(2,1)S(1)}, bf16[2,3,16,512]{3,2,1,0:T(8,128)(2,1)S(1)}, bf16[2,1,16,512]{3,2,1,0:T(8,128)(2,1)S(1)}, bf16[2,...) custom-call(s32[1,8,16]{2,1,0:T(8,128)} %send_ref.1, bf16[2,128,512]{2,1,0:T(8,128)(2,1)} %x_hbm.1), custom_call_target="tpu_custom_call" | custom-call | flops 1000000 | bytes 10000 | tf_op jit(solution)/shard_map/pallas_call | solution.py:507
  1.8 3.1 %collective-permute-start = (bf16[2,3,16,512]{3,2,1,0:T(8,128)(2,1)S(1)}, bf16[2,3,16,512]{3,2,1,0:T(8,128)(2,1)S(1)}, u32[]{:S(2)}, u32[]{:S(2)}) collective-permute-start(bf16[2,3,16,512]{3,2,1,0:T(8,128)(2,1)S(1)} %get-tuple-element.74), channel_id=1, source_target_pairs={{0,4},{1,5},{2,6},{3,7},{4,8},{5,9},{6,10},{7,11},{8,12},{9,13},{1... | collective-permute-start | bytes 294920 | tf_op jit(solution)/shard_map/ppermute | solution.py:28
  4.9 2.1 %collective-permute-start.1 = (bf16[2,3,16,512]{3,2,1,0:T(8,128)(2,1)S(1)}, bf16[2,3,16,512]{3,2,1,0:T(8,128)(2,1)S(1)}, u32[]{:S(2)}, u32[]{:S(2)}) collective-permute-start(bf16[2,3,16,512]{3,2,1,0:T(8,128)(2,1)S(1)} %get-tuple-element.75), channel_id=1, source_target_pairs={{0,12},{1,13},{2,14},{3,15},{4,0},{5,1},{6,2},{7,3},{8,4},{9,5},{1... | collective-permute-start | bytes 294920 | tf_op jit(solution)/shard_map/ppermute | solution.py:28
  7.0 2.6 %shard_map.105 = (bf16[8,2,128,128]{3,2,1,0:T(8,128)(2,1)S(1)}, bf16[8,2,128,128]{3,2,1,0:T(8,128)(2,1)S(1)}, bf16[8,2,128,128]{3,2,1,0:T(8,128)(2,1)S(1)}, bf16...) custom-call(bf16[2,1,16,512]{3,2,1,0:T(8,128)(2,1)S(1)} %get-tuple-e, ...), custom_call_target="tpu_custom_call" | custom-call | flops 1000000 | bytes 10000 | tf_op jit(solution)/shard_map/pallas_call | solution.py:507
  9.7 0.8 %collective-permute-done.plus_ref = bf16[2,3,16,512]{3,2,1,0:T(8,128)(2,1)S(1)} collective-permute-done((bf16[2,3,16,512]{3,2,1,0:T(8,128)(2,1)S(1)}, bf16[2,3,16,512]{3,2,1,0:T(8,128)(2,1)S(1)}, u32[]{:S(2)}, u32[]{:S(2)}) %collective-permute-start) | collective-permute-done | bytes 98336 | tf_op jit(solution)/shard_map/ppermute | solution.py:28
  10.4 0.8 %collective-permute-done.1.minus_ref = bf16[2,3,16,512]{3,2,1,0:T(8,128)(2,1)S(1)} collective-permute-done((bf16[2,3,16,512]{3,2,1,0:T(8,128)(2,1)S(1)}, bf16[2,3,16,512]{3,2,1,0:T(8,128)(2,1)S(1)}, u32[]{:S(2)}, u32[]{:S(2)}) %collective-permute-start.1) | collective-permute-done | bytes 98336 | tf_op jit(solution)/shard_map/ppermute | solution.py:28
  11.3 1.7 %collective-permute-start.2 = (bf16[2,3,16,512]{3,2,1,0:T(8,128)(2,1)S(1)}, bf16[2,3,16,512]{3,2,1,0:T(8,128)(2,1)S(1)}, u32[]{:S(2)}, u32[]{:S(2)}) collective-permute-start(bf16[2,3,16,512]{3,2,1,0:T(8,128)(2,1)S(1)} %get-tuple-element.76.after_ref), channel_id=1, source_target_pairs={{0,15},{1,2},{2,1},{3,4},{4,3},{5,6},{6,5},{7,8},{8,7},{9,10},{10,... | collective-permute-start | bytes 294920 | tf_op jit(solution)/shard_map/ppermute | solution.py:43
  13.0 0.0 collective-permute-start.3
  13.0 1.4 %shard_map.108.refs_4_.refs_12_ = f32[256,128]{1,0:T(8,128)S(1)} custom-call(bf16[2,3,16,512]{3,2,1,0:T(8,128)(2,1)S(1)} %get-tuple-element.76.after_ref, s32[128,256]{1,0:T(8,128)S(1)} %get-tuple-element.84.neigh_ref, s32[1,128]{1,0:T(1,128)S(1)} %get-tuple-element.85.count_ref), custom_call_target="tpu_custom_call" | custom-call | flops 1000000 | bytes 10000 | tf_op jit(solution)/shard_map/pallas_call | solution.py:507
  14.5 1.4 %shard_map.109 = (f32[3,2,128,512]{3,2,1,0:T(8,128)S(1)}, f32[2,2,8,512]{3,2,1,0:T(8,128)S(1)}, f32[3,2,128,512]{3,2,1,0:T(8,128)S(1)}, f32[2,2,8,512]{3,2,1,0:T...) custom-call(bf16[8,2,128,128]{3,2,1,0:T(8,128)(2,1)S(1)} %get-tuple-, ...), custom_call_target="tpu_custom_call" | custom-call | flops 1000000 | bytes 10000 | tf_op jit(solution)/shard_map/pallas_call | solution.py:507
  15.8 2.3 %collective-permute-done.2.second_in = bf16[2,3,16,512]{3,2,1,0:T(8,128)(2,1)S(1)} collective-permute-done((bf16[2,3,16,512]{3,2,1,0:T(8,128)(2,1)S(1)}, bf16[2,3,16,512]{3,2,1,0:T(8,128)(2,1)S(1)}, u32[]{:S(2)}, u32[]{:S(2)}) %collective-permute-start.2) | collective-permute-done | bytes 98336 | tf_op jit(solution)/shard_map/ppermute | solution.py:43
  18.1 0.0 collective-permute-done.3.first_in
  18.1 0.6 %shard_map.107 = (bf16[4,2,128,128]{3,2,1,0:T(8,128)(2,1)S(1)}, bf16[4,2,128,128]{3,2,1,0:T(8,128)(2,1)S(1)}, bf16[4,2,128,128]{3,2,1,0:T(8,128)(2,1)S(1)}, bf16...) custom-call(s32[1]{0:T(128)} %bitcast.me_ref, bf16[2,3,16,512]{3,2,1,0:T(8,128)(2,1)S(1)} %collective-permute-done.2.second_in, ...), custom_call_target="tpu_custom_call" | custom-call | flops 1000000 | bytes 10000 | tf_op jit(solution)/shard_map/pallas_call | solution.py:507
  18.7 3.8 %shard_map.112 = (f32[4,32,1536]{2,1,0:T(8,128)S(1)}, f32[4,32,1536]{2,1,0:T(8,128)S(1)}, bf16[4,32,1536]{2,1,0:T(8,128)(2,1)S(1)}, bf16[4,32,1536]{2,1,0:T(8,12...) custom-call(s32[1]{0:T(128)} %bitcast.me_ref, ...), custom_call_target="tpu_custom_call" | custom-call | flops 1000000 | bytes 10000 | tf_op jit(solution)/shard_map/pallas_call | solution.py:507
  22.5 0.1 collective-permute-start.6
  22.6 0.5 collective-permute-start.5
  23.1 1.2 %collective-permute-done.6 = bf16[4,32,1536]{2,1,0:T(8,128)(2,1)S(1)} collective-permute-done((bf16[4,32,1536]{2,1,0:T(8,128)(2,1)S(1)}, bf16[4,32,1536]{2,1,0:T(8,128)(2,1)S(1)}, u32[]{:S(2)}, u32[]{:S(2)}) %collective-permute-start.6) | collective-permute-done | bytes 393248 | tf_op jit(solution)/shard_map/ppermute | solution.py:609
  24.3 0.1 add_convert_fusion
  24.4 0.1 collective-permute-start.7
  24.5 1.5 %shard_map.110 = (f32[4,32,512]{2,1,0:T(8,128)S(1)}, f32[4,32,512]{2,1,0:T(8,128)S(1)}, bf16[4,32,512]{2,1,0:T(8,128)(2,1)S(1)}, bf16[4,32,512]{2,1,0:T(8,128)(2...) custom-call(s32[1]{0:T(128)} %bitcast.me_ref, ...), custom_call_target="tpu_custom_call" | custom-call | flops 1000000 | bytes 10000 | tf_op jit(solution)/shard_map/pallas_call | solution.py:507
  26.0 0.2 collective-permute-start.4
  26.2 0.4 collective-permute-start.11
  26.6 0.8 %collective-permute-done.4.refs_1_ = bf16[4,32,512]{2,1,0:T(8,128)(2,1)S(1)} collective-permute-done((bf16[4,32,512]{2,1,0:T(8,128)(2,1)S(1)}, bf16[4,32,512]{2,1,0:T(8,128)(2,1)S(1)}, u32[]{:S(2)}, u32[]{:S(2)}) %collective-permute-start.4) | collective-permute-done | bytes 131104 | tf_op jit(solution)/shard_map/ppermute | solution.py:609
  27.5 2.1 %collective-permute-start.10 = (bf16[4,32,512]{2,1,0:T(8,128)(2,1)S(1)}, bf16[4,32,512]{2,1,0:T(8,128)(2,1)S(1)}, u32[]{:S(2)}, u32[]{:S(2)}) collective-permute-start(bf16[4,32,512]{2,1,0:T(8,128)(2,1)S(1)} %shard_map.111.refs_0_), channel_id=1, source_target_pairs={{0,2},{1,3},{2,0},{3,1},{4,6},{5,7},{6,4},{7,5},{8,10},{9,11},{10,... | collective-permute-start | bytes 393224 | tf_op jit(solution)/shard_map/ppermute | solution.py:623
  29.6 1.0 %shard_map.113 = (f32[2,128,512]{2,1,0:T(8,128)S(1)}, bf16[2,3,16,512]{3,2,1,0:T(8,128)(2,1)S(1)}, bf16[2,3,16,512]{3,2,1,0:T(8,128)(2,1)S(1)}, bf16[2,1,16,512]...) custom-call(bf16[4,32,512]{2,1,0:T(8,128)(2,1)S(1)} %shard_map.111.refs_0_, ...), custom_call_target="tpu_custom_call" | custom-call | flops 1000000 | bytes 10000 | tf_op jit(solution)/shard_map/pallas_call | solution.py:507
  30.6 0.8 %collective-permute-start.8 = (bf16[2,3,16,512]{3,2,1,0:T(8,128)(2,1)S(1)}, bf16[2,3,16,512]{3,2,1,0:T(8,128)(2,1)S(1)}, u32[]{:S(2)}, u32[]{:S(2)}) collective-permute-start(bf16[2,3,16,512]{3,2,1,0:T(8,128)(2,1)S(1)} %get-tuple-element.122), channel_id=1, source_target_pairs={{0,12},{1,13},{2,14},{3,15},{4,0},{5,1},{6,2},{7,3},{8,4},{9,5},{1... | collective-permute-start | bytes 294920 | tf_op jit(solution)/shard_map/ppermute | solution.py:28
  31.3 0.0 collective-permute-done.5.core_in
  31.3 1.3 %collective-permute-start.9 = (bf16[2,3,16,512]{3,2,1,0:T(8,128)(2,1)S(1)}, bf16[2,3,16,512]{3,2,1,0:T(8,128)(2,1)S(1)}, u32[]{:S(2)}, u32[]{:S(2)}) collective-permute-start(bf16[2,3,16,512]{3,2,1,0:T(8,128)(2,1)S(1)} %get-tuple-element.123), channel_id=1, source_target_pairs={{0,4},{1,5},{2,6},{3,7},{4,8},{5,9},{6,10},{7,11},{8,12},{9,13},{1... | collective-permute-start | bytes 294920 | tf_op jit(solution)/shard_map/ppermute | solution.py:28
  32.7 3.8 %collective-permute-done.7.y_in = bf16[4,32,1536]{2,1,0:T(8,128)(2,1)S(1)} collective-permute-done((bf16[4,32,1536]{2,1,0:T(8,128)(2,1)S(1)}, bf16[4,32,1536]{2,1,0:T(8,128)(2,1)S(1)}, u32[]{:S(2)}, u32[]{:S(2)}) %collective-permute-start.7) | collective-permute-done | bytes 393248 | tf_op jit(solution)/shard_map/ppermute | solution.py:616
  36.4 0.1 shard_map.114
  36.6 0.1 collective-permute-start.14
  36.6 0.0 collective-permute-done.8.plus_ref
  36.6 2.1 %collective-permute-done.9.minus_ref = bf16[2,3,16,512]{3,2,1,0:T(8,128)(2,1)S(1)} collective-permute-done((bf16[2,3,16,512]{3,2,1,0:T(8,128)(2,1)S(1)}, bf16[2,3,16,512]{3,2,1,0:T(8,128)(2,1)S(1)}, u32[]{:S(2)}, u32[]{:S(2)}) %collective-permute-start.9) | collective-permute-done | bytes 98336 | tf_op jit(solution)/shard_map/ppermute | solution.py:28
  38.8 0.1 collective-permute-start.12
  38.9 1.2 %collective-permute-start.13 = (bf16[2,3,16,512]{3,2,1,0:T(8,128)(2,1)S(1)}, bf16[2,3,16,512]{3,2,1,0:T(8,128)(2,1)S(1)}, u32[]{:S(2)}, u32[]{:S(2)}) collective-permute-start(bf16[2,3,16,512]{3,2,1,0:T(8,128)(2,1)S(1)} %get-tuple-element.124.refs_0_), channel_id=1, source_target_pairs={{0,1},{1,0},{2,3},{3,2},{4,5},{5,4},{6,7},{7,6},{8,9},{9,8},{10,11... | collective-permute-start | bytes 294920 | tf_op jit(solution)/shard_map/ppermute | solution.py:44
  40.1 0.0 collective-permute-done.11.refs_4_
  40.1 0.1 shard_map.116
  40.2 0.1 collective-permute-start.15
  40.3 0.9 %collective-permute-start.17 = (bf16[7,32,128]{2,1,0:T(8,128)(2,1)S(1)}, bf16[7,32,128]{2,1,0:T(8,128)(2,1)S(1)}, u32[]{:S(2)}, u32[]{:S(2)}) collective-permute-start(bf16[7,32,128]{2,1,0:T(8,128)(2,1)S(1)} %get-tuple-element.128.after_ref), channel_id=1, source_target_pairs={{0,4},{1,5},{2,6},{3,7},{4,0},{5,1},{6,2},{7,3},{8,12},{9,13},{10,... | collective-permute-start | bytes 172040 | tf_op jit(solution)/shard_map/ppermute | solution.py:633
  41.2 0.5 %collective-permute-done.14.in_a = bf16[18,32,128]{2,1,0:T(8,128)(2,1)S(1)} collective-permute-done((bf16[18,32,128]{2,1,0:T(8,128)(2,1)S(1)}, bf16[18,32,128]{2,1,0:T(8,128)(2,1)S(1)}, u32[]{:S(2)}, u32[]{:S(2)}) %collective-permute-start.14) | collective-permute-done | bytes 147488 | tf_op jit(solution)/shard_map/ppermute | solution.py:633
  41.8 3.0 %collective-permute-start.16 = (bf16[16,32,128]{2,1,0:T(8,128)(2,1)S(1)}, bf16[16,32,128]{2,1,0:T(8,128)(2,1)S(1)}, u32[]{:S(2)}, u32[]{:S(2)}) collective-permute-start(bf16[16,32,128]{2,1,0:T(8,128)(2,1)S(1)} %get-tuple-element.135), channel_id=1, source_target_pairs={{0,12},{1,13},{2,14},{3,15},{4,8},{5,9},{6,10},{7,11},{8,4},{9,5},... | collective-permute-start | bytes 393224 | tf_op jit(solution)/shard_map/ppermute | solution.py:633
  44.8 1.2 %collective-permute-done.12.second_in = bf16[2,3,16,512]{3,2,1,0:T(8,128)(2,1)S(1)} collective-permute-done((bf16[2,3,16,512]{3,2,1,0:T(8,128)(2,1)S(1)}, bf16[2,3,16,512]{3,2,1,0:T(8,128)(2,1)S(1)}, u32[]{:S(2)}, u32[]{:S(2)}) %collective-permute-start.12) | collective-permute-done | bytes 98336 | tf_op jit(solution)/shard_map/ppermute | solution.py:43
  45.9 0.0 collective-permute-done.13.first_in
  46.0 1.0 %shard_map.117.after_ref = bf16[2,128,512]{2,1,0:T(8,128)(2,1)} custom-call(s32[1]{0:T(128)} %bitcast.me_ref, bf16[7,32,128]{2,1,0:T(8,128)(2,1)S(1)} %get-tuple-element.128.after_ref, bf16[2,3,16,512]{3,2,1,0:T(8,128)(2,1)S(1)} %collective-permute-done.12.second_in, bf16[2,3,16,512]{3,2,1,0:T(8,128)(2,1)S(1)} %collective-permute-done.13.first_in, ...), custom_call_target="tpu_custom_call" | custom-call | flops 20000000000 | bytes 10000 | tf_op jit(solution)/shard_map/pallas_call | solution.py:507
  46.9 0.5 %collective-permute-done.15.refs_0_ = bf16[7,32,128]{2,1,0:T(8,128)(2,1)S(1)} collective-permute-done((bf16[7,32,128]{2,1,0:T(8,128)(2,1)S(1)}, bf16[7,32,128]{2,1,0:T(8,128)(2,1)S(1)}, u32[]{:S(2)}, u32[]{:S(2)}) %collective-permute-start.15) | collective-permute-done | bytes 57376 | tf_op jit(solution)/shard_map/ppermute | solution.py:633
  47.5 0.0 collective-permute-done.17.refs_2_
  47.5 1.8 %collective-permute-done.16.refs_1_ = bf16[16,32,128]{2,1,0:T(8,128)(2,1)S(1)} collective-permute-done((bf16[16,32,128]{2,1,0:T(8,128)(2,1)S(1)}, bf16[16,32,128]{2,1,0:T(8,128)(2,1)S(1)}, u32[]{:S(2)}, u32[]{:S(2)}) %collective-permute-start.16) | collective-permute-done | bytes 131104 | tf_op jit(solution)/shard_map/ppermute | solution.py:633
  49.3 0.7 %shard_map.119 = f32[32,2048]{1,0:T(8,128)} custom-call(bf16[2,128,512]{2,1,0:T(8,128)(2,1)} %shard_map.117.after_ref, f32[32,1152]{1,0:T(8,128)S(1)} %get-tuple-element.132.own_a, f32[32,896]{1,0:T(8,128)S(1)} %get-tuple-element.133.own_b, bf16[7,32,128]{2,1,0:T(8,128)(2,1)S(1)} %collective-permute-done.15.refs_0_, ...), custom_call_target="tpu_custom_call" | custom-call | flops 1000000 | bytes 10000 | tf_op jit(solution)/shard_map/pallas_call | solution.py:507
  (7 shorter events, 0.1 us)
Async XLA Ops:
  1.8 8.6 %collective-permute-start = (bf16[2,3,16,512]{3,2,1,0:T(8,128)(2,1)S(1)}, bf16[2,3,16,512]{3,2,1,0:T(8,128)(2,1)S(1)}, u32[]{:S(2)}, u32[]{:S(2)}) collective-permute-start(bf16[2,3,16,512]{3,2,1,0:T(8,128)(2,1)S(1)} %get-tuple-element.74), channel_id=1, source_target_pairs={{0,4},{1,5},{2,6},{3,7},{4,8},{5,9},{6,10},{7,11},{8,12},{9,13},{1... | collective-permute-start | bytes 294920 | tf_op jit(solution)/shard_map/ppermute | solution.py:28
  4.9 6.4 %collective-permute-start.1 = (bf16[2,3,16,512]{3,2,1,0:T(8,128)(2,1)S(1)}, bf16[2,3,16,512]{3,2,1,0:T(8,128)(2,1)S(1)}, u32[]{:S(2)}, u32[]{:S(2)}) collective-permute-start(bf16[2,3,16,512]{3,2,1,0:T(8,128)(2,1)S(1)} %get-tuple-element.75), channel_id=1, source_target_pairs={{0,12},{1,13},{2,14},{3,15},{4,0},{5,1},{6,2},{7,3},{8,4},{9,5},{1... | collective-permute-start | bytes 294920 | tf_op jit(solution)/shard_map/ppermute | solution.py:28
  11.3 6.8 %collective-permute-start.2 = (bf16[2,3,16,512]{3,2,1,0:T(8,128)(2,1)S(1)}, bf16[2,3,16,512]{3,2,1,0:T(8,128)(2,1)S(1)}, u32[]{:S(2)}, u32[]{:S(2)}) collective-permute-start(bf16[2,3,16,512]{3,2,1,0:T(8,128)(2,1)S(1)} %get-tuple-element.76.after_ref), channel_id=1, source_target_pairs={{0,15},{1,2},{2,1},{3,4},{4,3},{5,6},{6,5},{7,8},{8,7},{9,10},{10,... | collective-permute-start | bytes 294920 | tf_op jit(solution)/shard_map/ppermute | solution.py:43
  13.0 5.1 %collective-permute-start.3 = (bf16[2,3,16,512]{3,2,1,0:T(8,128)(2,1)S(1)}, bf16[2,3,16,512]{3,2,1,0:T(8,128)(2,1)S(1)}, u32[]{:S(2)}, u32[]{:S(2)}) collective-permute-start(bf16[2,3,16,512]{3,2,1,0:T(8,128)(2,1)S(1)} %get-tuple-element.77), channel_id=1, source_target_pairs={{0,1},{1,0},{2,3},{3,2},{4,5},{5,4},{6,7},{7,6},{8,9},{9,8},{10,11... | collective-permute-start | bytes 294920 | tf_op jit(solution)/shard_map/ppermute | solution.py:44
  22.5 1.8 %collective-permute-start.6 = (bf16[4,32,1536]{2,1,0:T(8,128)(2,1)S(1)}, bf16[4,32,1536]{2,1,0:T(8,128)(2,1)S(1)}, u32[]{:S(2)}, u32[]{:S(2)}) collective-permute-start(bf16[4,32,1536]{2,1,0:T(8,128)(2,1)S(1)} %get-tuple-element.118), channel_id=1, source_target_pairs={{0,1},{1,0},{2,3},{3,2},{4,5},{5,4},{6,7},{7,6},{8,9},{9,8},{10,11... | collective-permute-start | bytes 1179656 | tf_op jit(solution)/shard_map/ppermute | solution.py:609
  22.6 8.7 %collective-permute-start.5 = (bf16[4,32,1536]{2,1,0:T(8,128)(2,1)S(1)}, bf16[4,32,1536]{2,1,0:T(8,128)(2,1)S(1)}, u32[]{:S(2)}, u32[]{:S(2)}) collective-permute-start(bf16[4,32,1536]{2,1,0:T(8,128)(2,1)S(1)} %get-tuple-element.116), channel_id=1, source_target_pairs={{0,1},{1,0},{2,3},{3,2},{4,5},{5,4},{6,7},{7,6},{8,9},{9,8},{10,11... | collective-permute-start | bytes 1179656 | tf_op jit(solution)/shard_map/ppermute | solution.py:609
  24.4 12.0 %collective-permute-start.7 = (bf16[4,32,1536]{2,1,0:T(8,128)(2,1)S(1)}, bf16[4,32,1536]{2,1,0:T(8,128)(2,1)S(1)}, u32[]{:S(2)}, u32[]{:S(2)}) collective-permute-start(bf16[4,32,1536]{2,1,0:T(8,128)(2,1)S(1)} %add_convert_fusion), channel_id=1, source_target_pairs={{0,2},{1,3},{2,0},{3,1},{4,6},{5,7},{6,4},{7,5},{8,10},{9,11},{10,... | collective-permute-start | bytes 1179656 | tf_op jit(solution)/shard_map/ppermute | solution.py:616
  26.0 1.4 %collective-permute-start.4 = (bf16[4,32,512]{2,1,0:T(8,128)(2,1)S(1)}, bf16[4,32,512]{2,1,0:T(8,128)(2,1)S(1)}, u32[]{:S(2)}, u32[]{:S(2)}) collective-permute-start(bf16[4,32,512]{2,1,0:T(8,128)(2,1)S(1)} %get-tuple-element.91), channel_id=1, source_target_pairs={{0,1},{1,0},{2,3},{3,2},{4,5},{5,4},{6,7},{7,6},{8,9},{9,8},{10,11... | collective-permute-start | bytes 393224 | tf_op jit(solution)/shard_map/ppermute | solution.py:609
  26.2 13.9 %collective-permute-start.11 = (bf16[4,32,512]{2,1,0:T(8,128)(2,1)S(1)}, bf16[4,32,512]{2,1,0:T(8,128)(2,1)S(1)}, u32[]{:S(2)}, u32[]{:S(2)}) collective-permute-start(bf16[4,32,512]{2,1,0:T(8,128)(2,1)S(1)} %get-tuple-element.127), channel_id=1, source_target_pairs={{0,1},{1,0},{2,3},{3,2},{4,5},{5,4},{6,7},{7,6},{8,9},{9,8},{10,11... | collective-permute-start | bytes 393224 | tf_op jit(solution)/shard_map/ppermute | solution.py:609
  27.5 12.7 %collective-permute-start.10 = (bf16[4,32,512]{2,1,0:T(8,128)(2,1)S(1)}, bf16[4,32,512]{2,1,0:T(8,128)(2,1)S(1)}, u32[]{:S(2)}, u32[]{:S(2)}) collective-permute-start(bf16[4,32,512]{2,1,0:T(8,128)(2,1)S(1)} %shard_map.111.refs_0_), channel_id=1, source_target_pairs={{0,2},{1,3},{2,0},{3,1},{4,6},{5,7},{6,4},{7,5},{8,10},{9,11},{10,... | collective-permute-start | bytes 393224 | tf_op jit(solution)/shard_map/ppermute | solution.py:623
  30.6 6.1 %collective-permute-start.8 = (bf16[2,3,16,512]{3,2,1,0:T(8,128)(2,1)S(1)}, bf16[2,3,16,512]{3,2,1,0:T(8,128)(2,1)S(1)}, u32[]{:S(2)}, u32[]{:S(2)}) collective-permute-start(bf16[2,3,16,512]{3,2,1,0:T(8,128)(2,1)S(1)} %get-tuple-element.122), channel_id=1, source_target_pairs={{0,12},{1,13},{2,14},{3,15},{4,0},{5,1},{6,2},{7,3},{8,4},{9,5},{1... | collective-permute-start | bytes 294920 | tf_op jit(solution)/shard_map/ppermute | solution.py:28
  31.3 7.4 %collective-permute-start.9 = (bf16[2,3,16,512]{3,2,1,0:T(8,128)(2,1)S(1)}, bf16[2,3,16,512]{3,2,1,0:T(8,128)(2,1)S(1)}, u32[]{:S(2)}, u32[]{:S(2)}) collective-permute-start(bf16[2,3,16,512]{3,2,1,0:T(8,128)(2,1)S(1)} %get-tuple-element.123), channel_id=1, source_target_pairs={{0,4},{1,5},{2,6},{3,7},{4,8},{5,9},{6,10},{7,11},{8,12},{9,13},{1... | collective-permute-start | bytes 294920 | tf_op jit(solution)/shard_map/ppermute | solution.py:28
  36.6 5.2 %collective-permute-start.14 = (bf16[18,32,128]{2,1,0:T(8,128)(2,1)S(1)}, bf16[18,32,128]{2,1,0:T(8,128)(2,1)S(1)}, u32[]{:S(2)}, u32[]{:S(2)}) collective-permute-start(bf16[18,32,128]{2,1,0:T(8,128)(2,1)S(1)} %get-tuple-element.119.after_ref), channel_id=1, source_target_pairs={{0,4},{1,5},{2,6},{3,7},{4,0},{5,1},{6,2},{7,3},{8,12},{9,13},{10,... | collective-permute-start | bytes 442376 | tf_op jit(solution)/shard_map/ppermute | solution.py:633
  38.8 7.1 %collective-permute-start.12 = (bf16[2,3,16,512]{3,2,1,0:T(8,128)(2,1)S(1)}, bf16[2,3,16,512]{3,2,1,0:T(8,128)(2,1)S(1)}, u32[]{:S(2)}, u32[]{:S(2)}) collective-permute-start(bf16[2,3,16,512]{3,2,1,0:T(8,128)(2,1)S(1)} %get-tuple-element.129), channel_id=1, source_target_pairs={{0,15},{1,2},{2,1},{3,4},{4,3},{5,6},{6,5},{7,8},{8,7},{9,10},{10,... | collective-permute-start | bytes 294920 | tf_op jit(solution)/shard_map/ppermute | solution.py:43
  38.9 7.1 %collective-permute-start.13 = (bf16[2,3,16,512]{3,2,1,0:T(8,128)(2,1)S(1)}, bf16[2,3,16,512]{3,2,1,0:T(8,128)(2,1)S(1)}, u32[]{:S(2)}, u32[]{:S(2)}) collective-permute-start(bf16[2,3,16,512]{3,2,1,0:T(8,128)(2,1)S(1)} %get-tuple-element.124.refs_0_), channel_id=1, source_target_pairs={{0,1},{1,0},{2,3},{3,2},{4,5},{5,4},{6,7},{7,6},{8,9},{9,8},{10,11... | collective-permute-start | bytes 294920 | tf_op jit(solution)/shard_map/ppermute | solution.py:44
  40.2 7.2 %collective-permute-start.15 = (bf16[7,32,128]{2,1,0:T(8,128)(2,1)S(1)}, bf16[7,32,128]{2,1,0:T(8,128)(2,1)S(1)}, u32[]{:S(2)}, u32[]{:S(2)}) collective-permute-start(bf16[7,32,128]{2,1,0:T(8,128)(2,1)S(1)} %get-tuple-element.134), channel_id=1, source_target_pairs={{0,8},{1,9},{2,10},{3,11},{4,12},{5,13},{6,14},{7,15},{8,0},{9,1},... | collective-permute-start | bytes 172040 | tf_op jit(solution)/shard_map/ppermute | solution.py:633
  40.3 7.2 %collective-permute-start.17 = (bf16[7,32,128]{2,1,0:T(8,128)(2,1)S(1)}, bf16[7,32,128]{2,1,0:T(8,128)(2,1)S(1)}, u32[]{:S(2)}, u32[]{:S(2)}) collective-permute-start(bf16[7,32,128]{2,1,0:T(8,128)(2,1)S(1)} %get-tuple-element.128.after_ref), channel_id=1, source_target_pairs={{0,4},{1,5},{2,6},{3,7},{4,0},{5,1},{6,2},{7,3},{8,12},{9,13},{10,... | collective-permute-start | bytes 172040 | tf_op jit(solution)/shard_map/ppermute | solution.py:633
  41.8 4.2 %copy-start = (s32[1,8,16]{2,1,0:T(8,128)S(1)}, s32[1,8,16]{2,1,0:T(8,128)}, u32[]{:S(2)}) copy-start(s32[1,8,16]{2,1,0:T(8,128)} %send_ref.1) | copy-start | bytes 1540
  41.8 7.5 %collective-permute-start.16 = (bf16[16,32,128]{2,1,0:T(8,128)(2,1)S(1)}, bf16[16,32,128]{2,1,0:T(8,128)(2,1)S(1)}, u32[]{:S(2)}, u32[]{:S(2)}) collective-permute-start(bf16[16,32,128]{2,1,0:T(8,128)(2,1)S(1)} %get-tuple-element.135), channel_id=1, source_target_pairs={{0,12},{1,13},{2,14},{3,15},{4,8},{5,9},{6,10},{7,11},{8,4},{9,5},... | collective-permute-start | bytes 393224 | tf_op jit(solution)/shard_map/ppermute | solution.py:633

commit v20 on v19

--- a/solution.py
+++ b/solution.py
@@ -452,9 +452,10 @@
             own_b[...] = row
 
 
-def join_kernel(kept_a, in_a, *refs):
-    count = (len(refs) - 1) // 2
-    blocks, own_a, sent = refs[:count], refs[count], refs[count + 1 :]
+def join_kernel(kept_a, in_a, near, *refs):
+    count = (len(refs) - 2) // 2
+    blocks, own_a, near_out, sent = refs[:count], refs[count], refs[count + 1], refs[count + 2 :]
+    near_out[...] = near[...]
     first = add_received(kept_a, in_a)
     own_a[...] = first[0]
     for i, ref in enumerate(sent):
@@ -657,10 +658,11 @@
         specs=[pltpu.SMEM, pl.ANY],
         scratch=[pltpu.VMEM((planes, rows, width), f32)], flops=4 * 10**9,
     )
-    own_a, *sent[1::2] = call(
+    own_a, sent[0], *sent[1::2] = call(
         join_kernel,
-        [((rows, wide), f32)] + [((blocks + more, rows, 128), bf16)] * (planes // 2 - 1),
-        (kept_a, in_a, *sent[1::2]), flops=2 * 10**10,
+        [((rows, wide), f32), ((blocks, rows, 128), bf16)]
+        + [((blocks + more, rows, 128), bf16)] * (planes // 2 - 1),
+        (kept_a, in_a, sent[0], *sent[1::2]), flops=2 * 10**10,
     )
     received = [exchange(shard, k) for k, shard in enumerate(sent, 1)]
     (node_grad,) = call(

time: 50.4 us -> 50.9 us (level)
  waiting for transfers between devices: 15.9 us -> 18.4 us
  starting transfers between devices: 17.6 us -> 15.8 us
    ppermute x4, starting transfers between devices: 4.05 us -> 2.22 us  [exchange(): return lax.ppermute(sent, 'patch', along_z(count, distance))]
    ppermute x4, waiting for transfers between devices: 2.87 us -> 4.46 us  [exchange(): return lax.ppermute(sent, 'patch', along_z(count, distance))]
    ppermute x2, waiting for transfers between devices: 3.46 us -> 4.35 us  [swap(): later = lax.ppermute(pair[1], 'patch', second)]
  transfers between devices with their start and end apart: 18 -> 18, of which waited for: 11 -> 11; matrix products, arithmetic and copies ran while one was open for 0% -> 0% of each run, Pallas kernels for 19% -> 18%
where the time goes in v20:
time: 50.9 us; the launch traced here: 50.7 us
  waiting for transfers between devices  18.4 us (36%)
  starting transfers between devices  15.8 us (31%)
  Pallas kernels  15.7 us (31%)
  between operations  0.77 us (2%)
    pallas_call x16, Pallas kernels, call(): pl.pallas_call(kernel, out_shape=[jax.ShapeDtypeStruct(*o) if final else...  15.7 us
    ppermute x4, starting transfers between devices, shifted(): lax.ppermute(shard, 'patch', [(i, (i + by) % count) for i in range(count)])  7.25 us
    ppermute x4, waiting for transfers between devices, exchange(): return lax.ppermute(sent, 'patch', along_z(count, distance))  4.46 us
    ppermute x2, waiting for transfers between devices, swap(): later = lax.ppermute(pair[1], 'patch', second)  4.35 us
    ppermute x1, waiting for transfers between devices, body(): y_a = lax.ppermute(y_sent, 'patch', flop)  3.75 us
    ppermute x4, waiting for transfers between devices, shifted(): lax.ppermute(shard, 'patch', [(i, (i + by) % count) for i in range(count)])  3.75 us
    ppermute x4, starting transfers between devices, exchange(): return lax.ppermute(sent, 'patch', along_z(count, distance))  2.22 us
    ppermute x1, starting transfers between devices, body(): y_b = lax.ppermute(y_sent, 'patch', flop)  2.07 us
  transfers between devices with their start and end apart: 18, of which 11 were waited for; matrix products, arithmetic and copies ran while one was open for 0% of the time, Pallas kernels for 18%

profile of v20, /device:TPU:0, one launch (start us, length us, event | category | flops | bytes accessed | tf_op | source)
XLA Modules:
  0.0 50.7 jit_solution(18221768554130131922)
XLA Ops:
  0.6 1.2 %shard_map.104 = (bf16[2,3,16,512]{3,2,1,0:T(8,128)(2,1)S(1)}, bf16[2,3,16,512]{3,2,1,0:T(8,128)(2,1)S(1)}, bf16[2,1,16,512]{3,2,1,0:T(8,128)(2,1)S(1)}, bf16[2,...) custom-call(s32[1,8,16]{2,1,0:T(8,128)} %send_ref.1, bf16[2,128,512]{2,1,0:T(8,128)(2,1)} %x_hbm.1), custom_call_target="tpu_custom_call" | custom-call | flops 1000000 | bytes 10000 | tf_op jit(solution)/shard_map/pallas_call | solution.py:508
  1.8 3.1 %collective-permute-start = (bf16[2,3,16,512]{3,2,1,0:T(8,128)(2,1)S(1)}, bf16[2,3,16,512]{3,2,1,0:T(8,128)(2,1)S(1)}, u32[]{:S(2)}, u32[]{:S(2)}) collective-permute-start(bf16[2,3,16,512]{3,2,1,0:T(8,128)(2,1)S(1)} %get-tuple-element.75), channel_id=1, source_target_pairs={{0,4},{1,5},{2,6},{3,7},{4,8},{5,9},{6,10},{7,11},{8,12},{9,13},{1... | collective-permute-start | bytes 294920 | tf_op jit(solution)/shard_map/ppermute | solution.py:28
  4.9 2.1 %collective-permute-start.1 = (bf16[2,3,16,512]{3,2,1,0:T(8,128)(2,1)S(1)}, bf16[2,3,16,512]{3,2,1,0:T(8,128)(2,1)S(1)}, u32[]{:S(2)}, u32[]{:S(2)}) collective-permute-start(bf16[2,3,16,512]{3,2,1,0:T(8,128)(2,1)S(1)} %get-tuple-element.76), channel_id=1, source_target_pairs={{0,12},{1,13},{2,14},{3,15},{4,0},{5,1},{6,2},{7,3},{8,4},{9,5},{1... | collective-permute-start | bytes 294920 | tf_op jit(solution)/shard_map/ppermute | solution.py:28
  7.0 2.6 %shard_map.105 = (bf16[8,2,128,128]{3,2,1,0:T(8,128)(2,1)S(1)}, bf16[8,2,128,128]{3,2,1,0:T(8,128)(2,1)S(1)}, bf16[8,2,128,128]{3,2,1,0:T(8,128)(2,1)S(1)}, bf16...) custom-call(bf16[2,1,16,512]{3,2,1,0:T(8,128)(2,1)S(1)} %get-tuple-e, ...), custom_call_target="tpu_custom_call" | custom-call | flops 1000000 | bytes 10000 | tf_op jit(solution)/shard_map/pallas_call | solution.py:508
  9.7 0.8 %collective-permute-done.plus_ref = bf16[2,3,16,512]{3,2,1,0:T(8,128)(2,1)S(1)} collective-permute-done((bf16[2,3,16,512]{3,2,1,0:T(8,128)(2,1)S(1)}, bf16[2,3,16,512]{3,2,1,0:T(8,128)(2,1)S(1)}, u32[]{:S(2)}, u32[]{:S(2)}) %collective-permute-start) | collective-permute-done | bytes 98336 | tf_op jit(solution)/shard_map/ppermute | solution.py:28
  10.4 0.8 %collective-permute-done.1.minus_ref = bf16[2,3,16,512]{3,2,1,0:T(8,128)(2,1)S(1)} collective-permute-done((bf16[2,3,16,512]{3,2,1,0:T(8,128)(2,1)S(1)}, bf16[2,3,16,512]{3,2,1,0:T(8,128)(2,1)S(1)}, u32[]{:S(2)}, u32[]{:S(2)}) %collective-permute-start.1) | collective-permute-done | bytes 98336 | tf_op jit(solution)/shard_map/ppermute | solution.py:28
  11.3 1.7 %collective-permute-start.2 = (bf16[2,3,16,512]{3,2,1,0:T(8,128)(2,1)S(1)}, bf16[2,3,16,512]{3,2,1,0:T(8,128)(2,1)S(1)}, u32[]{:S(2)}, u32[]{:S(2)}) collective-permute-start(bf16[2,3,16,512]{3,2,1,0:T(8,128)(2,1)S(1)} %get-tuple-element.77.after_ref), channel_id=1, source_target_pairs={{0,15},{1,2},{2,1},{3,4},{4,3},{5,6},{6,5},{7,8},{8,7},{9,10},{10,... | collective-permute-start | bytes 294920 | tf_op jit(solution)/shard_map/ppermute | solution.py:43
  13.0 0.0 collective-permute-start.3
  13.0 1.4 %shard_map.108.refs_4_.refs_12_ = f32[256,128]{1,0:T(8,128)S(1)} custom-call(bf16[2,3,16,512]{3,2,1,0:T(8,128)(2,1)S(1)} %get-tuple-element.77.after_ref, s32[128,256]{1,0:T(8,128)S(1)} %get-tuple-element.85.neigh_ref, s32[1,128]{1,0:T(1,128)S(1)} %get-tuple-element.86.count_ref), custom_call_target="tpu_custom_call" | custom-call | flops 1000000 | bytes 10000 | tf_op jit(solution)/shard_map/pallas_call | solution.py:508
  14.5 1.4 %shard_map.109 = (f32[3,2,128,512]{3,2,1,0:T(8,128)S(1)}, f32[2,2,8,512]{3,2,1,0:T(8,128)S(1)}, f32[3,2,128,512]{3,2,1,0:T(8,128)S(1)}, f32[2,2,8,512]{3,2,1,0:T...) custom-call(bf16[8,2,128,128]{3,2,1,0:T(8,128)(2,1)S(1)} %get-tuple-, ...), custom_call_target="tpu_custom_call" | custom-call | flops 1000000 | bytes 10000 | tf_op jit(solution)/shard_map/pallas_call | solution.py:508
  15.8 2.3 %collective-permute-done.2.second_in = bf16[2,3,16,512]{3,2,1,0:T(8,128)(2,1)S(1)} collective-permute-done((bf16[2,3,16,512]{3,2,1,0:T(8,128)(2,1)S(1)}, bf16[2,3,16,512]{3,2,1,0:T(8,128)(2,1)S(1)}, u32[]{:S(2)}, u32[]{:S(2)}) %collective-permute-start.2) | collective-permute-done | bytes 98336 | tf_op jit(solution)/shard_map/ppermute | solution.py:43
  18.1 0.0 collective-permute-done.3.first_in
  18.1 0.6 %shard_map.107 = (bf16[4,2,128,128]{3,2,1,0:T(8,128)(2,1)S(1)}, bf16[4,2,128,128]{3,2,1,0:T(8,128)(2,1)S(1)}, bf16[4,2,128,128]{3,2,1,0:T(8,128)(2,1)S(1)}, bf16...) custom-call(s32[1]{0:T(128)} %bitcast.me_ref, bf16[2,3,16,512]{3,2,1,0:T(8,128)(2,1)S(1)} %collective-permute-done.2.second_in, ...), custom_call_target="tpu_custom_call" | custom-call | flops 1000000 | bytes 10000 | tf_op jit(solution)/shard_map/pallas_call | solution.py:508
  18.7 3.8 %shard_map.112 = (f32[4,32,1536]{2,1,0:T(8,128)S(1)}, f32[4,32,1536]{2,1,0:T(8,128)S(1)}, bf16[4,32,1536]{2,1,0:T(8,128)(2,1)S(1)}, bf16[4,32,1536]{2,1,0:T(8,12...) custom-call(s32[1]{0:T(128)} %bitcast.me_ref, ...), custom_call_target="tpu_custom_call" | custom-call | flops 1000000 | bytes 10000 | tf_op jit(solution)/shard_map/pallas_call | solution.py:508
  22.5 0.1 collective-permute-start.6
  22.6 0.5 collective-permute-start.5
  23.1 1.2 %collective-permute-done.6 = bf16[4,32,1536]{2,1,0:T(8,128)(2,1)S(1)} collective-permute-done((bf16[4,32,1536]{2,1,0:T(8,128)(2,1)S(1)}, bf16[4,32,1536]{2,1,0:T(8,128)(2,1)S(1)}, u32[]{:S(2)}, u32[]{:S(2)}) %collective-permute-start.6) | collective-permute-done | bytes 393248 | tf_op jit(solution)/shard_map/ppermute | solution.py:610
  24.3 0.1 add_convert_fusion
  24.4 0.1 collective-permute-start.7
  24.5 1.5 %shard_map.110 = (f32[4,32,512]{2,1,0:T(8,128)S(1)}, f32[4,32,512]{2,1,0:T(8,128)S(1)}, bf16[4,32,512]{2,1,0:T(8,128)(2,1)S(1)}, bf16[4,32,512]{2,1,0:T(8,128)(2...) custom-call(s32[1]{0:T(128)} %bitcast.me_ref, ...), custom_call_target="tpu_custom_call" | custom-call | flops 1000000 | bytes 10000 | tf_op jit(solution)/shard_map/pallas_call | solution.py:508
  26.0 0.2 collective-permute-start.4
  26.2 0.4 collective-permute-start.12
  26.6 0.8 %collective-permute-done.4.refs_1_ = bf16[4,32,512]{2,1,0:T(8,128)(2,1)S(1)} collective-permute-done((bf16[4,32,512]{2,1,0:T(8,128)(2,1)S(1)}, bf16[4,32,512]{2,1,0:T(8,128)(2,1)S(1)}, u32[]{:S(2)}, u32[]{:S(2)}) %collective-permute-start.4) | collective-permute-done | bytes 131104 | tf_op jit(solution)/shard_map/ppermute | solution.py:610
  27.5 2.1 %collective-permute-start.11 = (bf16[4,32,512]{2,1,0:T(8,128)(2,1)S(1)}, bf16[4,32,512]{2,1,0:T(8,128)(2,1)S(1)}, u32[]{:S(2)}, u32[]{:S(2)}) collective-permute-start(bf16[4,32,512]{2,1,0:T(8,128)(2,1)S(1)} %shard_map.111.refs_0_), channel_id=1, source_target_pairs={{0,2},{1,3},{2,0},{3,1},{4,6},{5,7},{6,4},{7,5},{8,10},{9,11},{10,... | collective-permute-start | bytes 393224 | tf_op jit(solution)/shard_map/ppermute | solution.py:624
  29.6 1.0 %shard_map.113 = (f32[2,128,512]{2,1,0:T(8,128)S(1)}, bf16[2,3,16,512]{3,2,1,0:T(8,128)(2,1)S(1)}, bf16[2,3,16,512]{3,2,1,0:T(8,128)(2,1)S(1)}, bf16[2,1,16,512]...) custom-call(bf16[4,32,512]{2,1,0:T(8,128)(2,1)S(1)} %shard_map.111.refs_0_, ...), custom_call_target="tpu_custom_call" | custom-call | flops 1000000 | bytes 10000 | tf_op jit(solution)/shard_map/pallas_call | solution.py:508
  30.6 0.8 %collective-permute-start.9 = (bf16[2,3,16,512]{3,2,1,0:T(8,128)(2,1)S(1)}, bf16[2,3,16,512]{3,2,1,0:T(8,128)(2,1)S(1)}, u32[]{:S(2)}, u32[]{:S(2)}) collective-permute-start(bf16[2,3,16,512]{3,2,1,0:T(8,128)(2,1)S(1)} %get-tuple-element.124), channel_id=1, source_target_pairs={{0,12},{1,13},{2,14},{3,15},{4,0},{5,1},{6,2},{7,3},{8,4},{9,5},{1... | collective-permute-start | bytes 294920 | tf_op jit(solution)/shard_map/ppermute | solution.py:28
  31.3 0.0 collective-permute-done.5.core_in
  31.3 1.3 %collective-permute-start.10 = (bf16[2,3,16,512]{3,2,1,0:T(8,128)(2,1)S(1)}, bf16[2,3,16,512]{3,2,1,0:T(8,128)(2,1)S(1)}, u32[]{:S(2)}, u32[]{:S(2)}) collective-permute-start(bf16[2,3,16,512]{3,2,1,0:T(8,128)(2,1)S(1)} %get-tuple-element.125), channel_id=1, source_target_pairs={{0,4},{1,5},{2,6},{3,7},{4,8},{5,9},{6,10},{7,11},{8,12},{9,13},{1... | collective-permute-start | bytes 294920 | tf_op jit(solution)/shard_map/ppermute | solution.py:28
  32.7 3.8 %collective-permute-done.7.y_in = bf16[4,32,1536]{2,1,0:T(8,128)(2,1)S(1)} collective-permute-done((bf16[4,32,1536]{2,1,0:T(8,128)(2,1)S(1)}, bf16[4,32,1536]{2,1,0:T(8,128)(2,1)S(1)}, u32[]{:S(2)}, u32[]{:S(2)}) %collective-permute-start.7) | collective-permute-done | bytes 393248 | tf_op jit(solution)/shard_map/ppermute | solution.py:617
  36.4 0.1 shard_map.114
  36.6 0.1 collective-permute-start.8
  36.6 0.0 collective-permute-done.9.plus_ref
  36.6 2.1 %collective-permute-done.10.minus_ref = bf16[2,3,16,512]{3,2,1,0:T(8,128)(2,1)S(1)} collective-permute-done((bf16[2,3,16,512]{3,2,1,0:T(8,128)(2,1)S(1)}, bf16[2,3,16,512]{3,2,1,0:T(8,128)(2,1)S(1)}, u32[]{:S(2)}, u32[]{:S(2)}) %collective-permute-start.10) | collective-permute-done | bytes 98336 | tf_op jit(solution)/shard_map/ppermute | solution.py:28
  38.8 0.1 collective-permute-start.13
  38.9 1.2 %collective-permute-start.14 = (bf16[2,3,16,512]{3,2,1,0:T(8,128)(2,1)S(1)}, bf16[2,3,16,512]{3,2,1,0:T(8,128)(2,1)S(1)}, u32[]{:S(2)}, u32[]{:S(2)}) collective-permute-start(bf16[2,3,16,512]{3,2,1,0:T(8,128)(2,1)S(1)} %get-tuple-element.126.refs_0_), channel_id=1, source_target_pairs={{0,1},{1,0},{2,3},{3,2},{4,5},{5,4},{6,7},{7,6},{8,9},{9,8},{10,11... | collective-permute-start | bytes 294920 | tf_op jit(solution)/shard_map/ppermute | solution.py:44
  40.1 0.0 collective-permute-done.12.refs_4_
  40.1 0.0 collective-permute-done.11.refs_2_
  40.1 0.1 shard_map.116
  40.2 0.1 collective-permute-start.15
  40.3 1.5 %collective-permute-done.8.in_a = bf16[18,32,128]{2,1,0:T(8,128)(2,1)S(1)} collective-permute-done((bf16[18,32,128]{2,1,0:T(8,128)(2,1)S(1)}, bf16[18,32,128]{2,1,0:T(8,128)(2,1)S(1)}, u32[]{:S(2)}, u32[]{:S(2)}) %collective-permute-start.8) | collective-permute-done | bytes 147488 | tf_op jit(solution)/shard_map/ppermute | solution.py:634
  41.8 1.3 %collective-permute-start.16 = (bf16[16,32,128]{2,1,0:T(8,128)(2,1)S(1)}, bf16[16,32,128]{2,1,0:T(8,128)(2,1)S(1)}, u32[]{:S(2)}, u32[]{:S(2)}) collective-permute-start(bf16[16,32,128]{2,1,0:T(8,128)(2,1)S(1)} %get-tuple-element.137), channel_id=1, source_target_pairs={{0,12},{1,13},{2,14},{3,15},{4,8},{5,9},{6,10},{7,11},{8,4},{9,5},... | collective-permute-start | bytes 393224 | tf_op jit(solution)/shard_map/ppermute | solution.py:634
  43.1 0.7 %collective-permute-start.17 = (bf16[7,32,128]{2,1,0:T(8,128)(2,1)S(1)}, bf16[7,32,128]{2,1,0:T(8,128)(2,1)S(1)}, u32[]{:S(2)}, u32[]{:S(2)}) collective-permute-start(bf16[7,32,128]{2,1,0:T(8,128)(2,1)S(1)} %get-tuple-element.132.after_ref), channel_id=1, source_target_pairs={{0,4},{1,5},{2,6},{3,7},{4,0},{5,1},{6,2},{7,3},{8,12},{9,13},{10,... | collective-permute-start | bytes 172040 | tf_op jit(solution)/shard_map/ppermute | solution.py:634
  43.9 2.1 %collective-permute-done.13.second_in = bf16[2,3,16,512]{3,2,1,0:T(8,128)(2,1)S(1)} collective-permute-done((bf16[2,3,16,512]{3,2,1,0:T(8,128)(2,1)S(1)}, bf16[2,3,16,512]{3,2,1,0:T(8,128)(2,1)S(1)}, u32[]{:S(2)}, u32[]{:S(2)}) %collective-permute-start.13) | collective-permute-done | bytes 98336 | tf_op jit(solution)/shard_map/ppermute | solution.py:43
  45.9 0.0 collective-permute-done.14.first_in
  46.0 1.0 %shard_map.118.after_ref = bf16[2,128,512]{2,1,0:T(8,128)(2,1)} custom-call(s32[1]{0:T(128)} %bitcast.me_ref, bf16[7,32,128]{2,1,0:T(8,128)(2,1)S(1)} %get-tuple-element.132.after_ref, bf16[2,3,16,512]{3,2,1,0:T(8,128)(2,1)S(1)} %collective-permute-done.13.second_in, bf16[2,3,16,512]{3,2,1,0:T(8,128)(2,1)S(1)} %collective-permute-done.14.first_in, ...), custom_call_target="tpu_custom_call" | custom-call | flops 20000000000 | bytes 10000 | tf_op jit(solution)/shard_map/pallas_call | solution.py:508
  46.9 2.3 %collective-permute-done.15.refs_0_ = bf16[7,32,128]{2,1,0:T(8,128)(2,1)S(1)} collective-permute-done((bf16[7,32,128]{2,1,0:T(8,128)(2,1)S(1)}, bf16[7,32,128]{2,1,0:T(8,128)(2,1)S(1)}, u32[]{:S(2)}, u32[]{:S(2)}) %collective-permute-start.15) | collective-permute-done | bytes 57376 | tf_op jit(solution)/shard_map/ppermute | solution.py:634
  49.3 0.7 %collective-permute-done.17.refs_2_ = bf16[7,32,128]{2,1,0:T(8,128)(2,1)S(1)} collective-permute-done((bf16[7,32,128]{2,1,0:T(8,128)(2,1)S(1)}, bf16[7,32,128]{2,1,0:T(8,128)(2,1)S(1)}, u32[]{:S(2)}, u32[]{:S(2)}) %collective-permute-start.17) | collective-permute-done | bytes 57376 | tf_op jit(solution)/shard_map/ppermute | solution.py:634
  49.9 0.7 %shard_map.119 = f32[32,2048]{1,0:T(8,128)} custom-call(bf16[2,128,512]{2,1,0:T(8,128)(2,1)} %shard_map.118.after_ref, f32[32,1152]{1,0:T(8,128)S(1)} %get-tuple-element.134.own_a, f32[32,896]{1,0:T(8,128)S(1)} %get-tuple-element.135.own_b, bf16[7,32,128]{2,1,0:T(8,128)(2,1)S(1)} %collective-permute-done.15.refs_0_, ...), custom_call_target="tpu_custom_call" | custom-call | flops 1000000 | bytes 10000 | tf_op jit(solution)/shard_map/pallas_call | solution.py:508
  (7 shorter events, 0.1 us)
Async XLA Ops:
  1.8 8.6 %collective-permute-start = (bf16[2,3,16,512]{3,2,1,0:T(8,128)(2,1)S(1)}, bf16[2,3,16,512]{3,2,1,0:T(8,128)(2,1)S(1)}, u32[]{:S(2)}, u32[]{:S(2)}) collective-permute-start(bf16[2,3,16,512]{3,2,1,0:T(8,128)(2,1)S(1)} %get-tuple-element.75), channel_id=1, source_target_pairs={{0,4},{1,5},{2,6},{3,7},{4,8},{5,9},{6,10},{7,11},{8,12},{9,13},{1... | collective-permute-start | bytes 294920 | tf_op jit(solution)/shard_map/ppermute | solution.py:28
  4.9 6.4 %collective-permute-start.1 = (bf16[2,3,16,512]{3,2,1,0:T(8,128)(2,1)S(1)}, bf16[2,3,16,512]{3,2,1,0:T(8,128)(2,1)S(1)}, u32[]{:S(2)}, u32[]{:S(2)}) collective-permute-start(bf16[2,3,16,512]{3,2,1,0:T(8,128)(2,1)S(1)} %get-tuple-element.76), channel_id=1, source_target_pairs={{0,12},{1,13},{2,14},{3,15},{4,0},{5,1},{6,2},{7,3},{8,4},{9,5},{1... | collective-permute-start | bytes 294920 | tf_op jit(solution)/shard_map/ppermute | solution.py:28
  11.3 6.8 %collective-permute-start.2 = (bf16[2,3,16,512]{3,2,1,0:T(8,128)(2,1)S(1)}, bf16[2,3,16,512]{3,2,1,0:T(8,128)(2,1)S(1)}, u32[]{:S(2)}, u32[]{:S(2)}) collective-permute-start(bf16[2,3,16,512]{3,2,1,0:T(8,128)(2,1)S(1)} %get-tuple-element.77.after_ref), channel_id=1, source_target_pairs={{0,15},{1,2},{2,1},{3,4},{4,3},{5,6},{6,5},{7,8},{8,7},{9,10},{10,... | collective-permute-start | bytes 294920 | tf_op jit(solution)/shard_map/ppermute | solution.py:43
  13.0 5.1 %collective-permute-start.3 = (bf16[2,3,16,512]{3,2,1,0:T(8,128)(2,1)S(1)}, bf16[2,3,16,512]{3,2,1,0:T(8,128)(2,1)S(1)}, u32[]{:S(2)}, u32[]{:S(2)}) collective-permute-start(bf16[2,3,16,512]{3,2,1,0:T(8,128)(2,1)S(1)} %get-tuple-element.78), channel_id=1, source_target_pairs={{0,1},{1,0},{2,3},{3,2},{4,5},{5,4},{6,7},{7,6},{8,9},{9,8},{10,11... | collective-permute-start | bytes 294920 | tf_op jit(solution)/shard_map/ppermute | solution.py:44
  22.5 1.8 %collective-permute-start.6 = (bf16[4,32,1536]{2,1,0:T(8,128)(2,1)S(1)}, bf16[4,32,1536]{2,1,0:T(8,128)(2,1)S(1)}, u32[]{:S(2)}, u32[]{:S(2)}) collective-permute-start(bf16[4,32,1536]{2,1,0:T(8,128)(2,1)S(1)} %get-tuple-element.119), channel_id=1, source_target_pairs={{0,1},{1,0},{2,3},{3,2},{4,5},{5,4},{6,7},{7,6},{8,9},{9,8},{10,11... | collective-permute-start | bytes 1179656 | tf_op jit(solution)/shard_map/ppermute | solution.py:610
  22.6 8.7 %collective-permute-start.5 = (bf16[4,32,1536]{2,1,0:T(8,128)(2,1)S(1)}, bf16[4,32,1536]{2,1,0:T(8,128)(2,1)S(1)}, u32[]{:S(2)}, u32[]{:S(2)}) collective-permute-start(bf16[4,32,1536]{2,1,0:T(8,128)(2,1)S(1)} %get-tuple-element.117), channel_id=1, source_target_pairs={{0,1},{1,0},{2,3},{3,2},{4,5},{5,4},{6,7},{7,6},{8,9},{9,8},{10,11... | collective-permute-start | bytes 1179656 | tf_op jit(solution)/shard_map/ppermute | solution.py:610
  24.4 12.0 %collective-permute-start.7 = (bf16[4,32,1536]{2,1,0:T(8,128)(2,1)S(1)}, bf16[4,32,1536]{2,1,0:T(8,128)(2,1)S(1)}, u32[]{:S(2)}, u32[]{:S(2)}) collective-permute-start(bf16[4,32,1536]{2,1,0:T(8,128)(2,1)S(1)} %add_convert_fusion), channel_id=1, source_target_pairs={{0,2},{1,3},{2,0},{3,1},{4,6},{5,7},{6,4},{7,5},{8,10},{9,11},{10,... | collective-permute-start | bytes 1179656 | tf_op jit(solution)/shard_map/ppermute | solution.py:617
  26.0 1.4 %collective-permute-start.4 = (bf16[4,32,512]{2,1,0:T(8,128)(2,1)S(1)}, bf16[4,32,512]{2,1,0:T(8,128)(2,1)S(1)}, u32[]{:S(2)}, u32[]{:S(2)}) collective-permute-start(bf16[4,32,512]{2,1,0:T(8,128)(2,1)S(1)} %get-tuple-element.92), channel_id=1, source_target_pairs={{0,1},{1,0},{2,3},{3,2},{4,5},{5,4},{6,7},{7,6},{8,9},{9,8},{10,11... | collective-permute-start | bytes 393224 | tf_op jit(solution)/shard_map/ppermute | solution.py:610
  26.2 13.9 %collective-permute-start.12 = (bf16[4,32,512]{2,1,0:T(8,128)(2,1)S(1)}, bf16[4,32,512]{2,1,0:T(8,128)(2,1)S(1)}, u32[]{:S(2)}, u32[]{:S(2)}) collective-permute-start(bf16[4,32,512]{2,1,0:T(8,128)(2,1)S(1)} %get-tuple-element.129), channel_id=1, source_target_pairs={{0,1},{1,0},{2,3},{3,2},{4,5},{5,4},{6,7},{7,6},{8,9},{9,8},{10,11... | collective-permute-start | bytes 393224 | tf_op jit(solution)/shard_map/ppermute | solution.py:610
  27.5 12.7 %collective-permute-start.11 = (bf16[4,32,512]{2,1,0:T(8,128)(2,1)S(1)}, bf16[4,32,512]{2,1,0:T(8,128)(2,1)S(1)}, u32[]{:S(2)}, u32[]{:S(2)}) collective-permute-start(bf16[4,32,512]{2,1,0:T(8,128)(2,1)S(1)} %shard_map.111.refs_0_), channel_id=1, source_target_pairs={{0,2},{1,3},{2,0},{3,1},{4,6},{5,7},{6,4},{7,5},{8,10},{9,11},{10,... | collective-permute-start | bytes 393224 | tf_op jit(solution)/shard_map/ppermute | solution.py:624
  30.6 6.1 %collective-permute-start.9 = (bf16[2,3,16,512]{3,2,1,0:T(8,128)(2,1)S(1)}, bf16[2,3,16,512]{3,2,1,0:T(8,128)(2,1)S(1)}, u32[]{:S(2)}, u32[]{:S(2)}) collective-permute-start(bf16[2,3,16,512]{3,2,1,0:T(8,128)(2,1)S(1)} %get-tuple-element.124), channel_id=1, source_target_pairs={{0,12},{1,13},{2,14},{3,15},{4,0},{5,1},{6,2},{7,3},{8,4},{9,5},{1... | collective-permute-start | bytes 294920 | tf_op jit(solution)/shard_map/ppermute | solution.py:28
  31.3 7.4 %collective-permute-start.10 = (bf16[2,3,16,512]{3,2,1,0:T(8,128)(2,1)S(1)}, bf16[2,3,16,512]{3,2,1,0:T(8,128)(2,1)S(1)}, u32[]{:S(2)}, u32[]{:S(2)}) collective-permute-start(bf16[2,3,16,512]{3,2,1,0:T(8,128)(2,1)S(1)} %get-tuple-element.125), channel_id=1, source_target_pairs={{0,4},{1,5},{2,6},{3,7},{4,8},{5,9},{6,10},{7,11},{8,12},{9,13},{1... | collective-permute-start | bytes 294920 | tf_op jit(solution)/shard_map/ppermute | solution.py:28
  36.6 5.2 %collective-permute-start.8 = (bf16[18,32,128]{2,1,0:T(8,128)(2,1)S(1)}, bf16[18,32,128]{2,1,0:T(8,128)(2,1)S(1)}, u32[]{:S(2)}, u32[]{:S(2)}) collective-permute-start(bf16[18,32,128]{2,1,0:T(8,128)(2,1)S(1)} %get-tuple-element.121.after_ref), channel_id=1, source_target_pairs={{0,4},{1,5},{2,6},{3,7},{4,0},{5,1},{6,2},{7,3},{8,12},{9,13},{10,... | collective-permute-start | bytes 442376 | tf_op jit(solution)/shard_map/ppermute | solution.py:634
  38.8 7.1 %collective-permute-start.13 = (bf16[2,3,16,512]{3,2,1,0:T(8,128)(2,1)S(1)}, bf16[2,3,16,512]{3,2,1,0:T(8,128)(2,1)S(1)}, u32[]{:S(2)}, u32[]{:S(2)}) collective-permute-start(bf16[2,3,16,512]{3,2,1,0:T(8,128)(2,1)S(1)} %get-tuple-element.133), channel_id=1, source_target_pairs={{0,15},{1,2},{2,1},{3,4},{4,3},{5,6},{6,5},{7,8},{8,7},{9,10},{10,... | collective-permute-start | bytes 294920 | tf_op jit(solution)/shard_map/ppermute | solution.py:43
  38.9 7.1 %collective-permute-start.14 = (bf16[2,3,16,512]{3,2,1,0:T(8,128)(2,1)S(1)}, bf16[2,3,16,512]{3,2,1,0:T(8,128)(2,1)S(1)}, u32[]{:S(2)}, u32[]{:S(2)}) collective-permute-start(bf16[2,3,16,512]{3,2,1,0:T(8,128)(2,1)S(1)} %get-tuple-element.126.refs_0_), channel_id=1, source_target_pairs={{0,1},{1,0},{2,3},{3,2},{4,5},{5,4},{6,7},{7,6},{8,9},{9,8},{10,11... | collective-permute-start | bytes 294920 | tf_op jit(solution)/shard_map/ppermute | solution.py:44
  40.2 9.0 %collective-permute-start.15 = (bf16[7,32,128]{2,1,0:T(8,128)(2,1)S(1)}, bf16[7,32,128]{2,1,0:T(8,128)(2,1)S(1)}, u32[]{:S(2)}, u32[]{:S(2)}) collective-permute-start(bf16[7,32,128]{2,1,0:T(8,128)(2,1)S(1)} %get-tuple-element.136), channel_id=1, source_target_pairs={{0,8},{1,9},{2,10},{3,11},{4,12},{5,13},{6,14},{7,15},{8,0},{9,1},... | collective-permute-start | bytes 172040 | tf_op jit(solution)/shard_map/ppermute | solution.py:634
  41.8 4.2 %copy-start = (s32[1,8,16]{2,1,0:T(8,128)S(1)}, s32[1,8,16]{2,1,0:T(8,128)}, u32[]{:S(2)}) copy-start(s32[1,8,16]{2,1,0:T(8,128)} %send_ref.1) | copy-start | bytes 1540
  41.8 8.1 %collective-permute-start.16 = (bf16[16,32,128]{2,1,0:T(8,128)(2,1)S(1)}, bf16[16,32,128]{2,1,0:T(8,128)(2,1)S(1)}, u32[]{:S(2)}, u32[]{:S(2)}) collective-permute-start(bf16[16,32,128]{2,1,0:T(8,128)(2,1)S(1)} %get-tuple-element.137), channel_id=1, source_target_pairs={{0,12},{1,13},{2,14},{3,15},{4,8},{5,9},{6,10},{7,11},{8,4},{9,5},... | collective-permute-start | bytes 393224 | tf_op jit(solution)/shard_map/ppermute | solution.py:634
  43.1 6.8 %collective-permute-start.17 = (bf16[7,32,128]{2,1,0:T(8,128)(2,1)S(1)}, bf16[7,32,128]{2,1,0:T(8,128)(2,1)S(1)}, u32[]{:S(2)}, u32[]{:S(2)}) collective-permute-start(bf16[7,32,128]{2,1,0:T(8,128)(2,1)S(1)} %get-tuple-element.132.after_ref), channel_id=1, source_target_pairs={{0,4},{1,5},{2,6},{3,7},{4,0},{5,1},{6,2},{7,3},{8,12},{9,13},{10,... | collective-permute-start | bytes 172040 | tf_op jit(solution)/shard_map/ppermute | solution.py:634

commit v21 on v19

--- a/solution.py
+++ b/solution.py
@@ -71,15 +71,17 @@
 ):
     copies = [
         pltpu.make_async_copy(send_hbm, send_ref, sem.at[0]),
-        pltpu.make_async_copy(x_hbm, x_ref, sem.at[1]),
+    ]
+    members, node_rows, _ = x_ref.shape
+    copies += [
+        pltpu.make_async_copy(x_hbm.at[m], x_ref.at[m], sem.at[1 + m]) for m in range(members)
     ]
     for copy in copies:
         copy.start()
     copies[0].wait()
-    members, node_rows, _ = x_ref.shape
     pick = sent_selector(send_ref[0], node_rows).T.astype(bf16)
-    copies[1].wait()
     for m in range(members):
+        copies[1 + m].wait()
         rows = nn(pick, x_ref[m]).astype(bf16)
 
         def part(k):
@@ -168,10 +170,10 @@
 
 
 def halo_kernel(
-    me_ref, second_in, first_in, plus_ref, minus_ref, xt_ref, wk_ref, wv_ref, *refs
+    me_ref, second_in, first_in, plus_ref, minus_ref, wk_ref, wv_ref, *refs
 ):
     halo_refs, xtf_ref, both = refs[:-2], refs[-2], refs[-1]
-    members, _, node_rows = xt_ref.shape
+    members = plus_ref.shape[0]
     from_swaps(both, me_ref[0] % 2, first_in, second_in)
     for m in range(members):
         pieces = [None] * 8
@@ -181,8 +183,7 @@
         pieces[2] = plus_ref[m, 0]
         pieces[3] = minus_ref[m, 0]
         halo = jnp.concatenate(pieces, axis=0)
-        xtf_ref[m, :, :node_rows] = xt_ref[m]
-        xtf_ref[m, :, node_rows:] = halo.T
+        xtf_ref[m] = halo.T
         for kind, w_ref in enumerate((wk_ref, wv_ref)):
             rows = nn(halo, w_ref[...]).astype(bf16)
             for g, ref in enumerate(halo_refs):
@@ -248,7 +249,9 @@
     refs = refs[extra:]
     locs, halos, owns = refs[:here], refs[here : 2 * here], refs[2 * here : 4 * here]
     refs = refs[4 * here :]
-    mask_ref, xtf, og_ref = refs[:3]
+    mask_ref, xt, xth, og_ref = refs[:4]
+    refs = refs[1:]
+    xtf = (xt, xth)
     split = 7 if len(refs) == 15 + 3 * (here - 1) else 6
     outs, grads, scratch = refs[3:split], refs[split : split + 3 * here], refs[split + 3 * here :]
     if split == 6:
@@ -314,8 +317,8 @@
         dv = nn(pb, by_head_n(loc[G, m], head)).astype(bf16)
         dq_ref[m], dk_ref[m], dv_ref[m] = dq, dk, dv
         wo_term = nn(att, og_ref[m])
-        kv_term = nn(xtf[m], jnp.concatenate([dk, dv], axis=1))
-        q_term = nn(xtf[m, :, :node_rows], dq)
+        kv_term = nn(jnp.concatenate([xtf[0][m], xtf[1][m]], axis=1), jnp.concatenate([dk, dv], axis=1))
+        q_term = nn(xtf[0][m], dq)
         wo_total = wo_term if m == 0 else wo_total + wo_term
         kv_total = kv_term if m == 0 else kv_total + kv_term
         q_total = q_term if m == 0 else q_total + q_term
@@ -534,7 +537,7 @@
         [three, three, one, one, (node_features.shape, bf16)],
         (send_rows, node_features),
         specs=[pltpu.HBM] * 2,
-        scratch=[pltpu.VMEM(send_rows.shape, jnp.int32), pltpu.SemaphoreType.DMA((2,))],
+        scratch=[pltpu.VMEM(send_rows.shape, jnp.int32), pltpu.SemaphoreType.DMA((1 + members,))],
     )
     plus = shifted(to_plus, row_width)
     minus = shifted(to_minus, -row_width)
@@ -569,8 +572,9 @@
     )
     *halo, xtf = call(
         halo_kernel,
-        [((4, members, node_rows, 128), bf16)] * groups + [((members, width, table), bf16)],
-        (place, *arrived[::-1], plus, minus, xt, wk, wv), specs=[pltpu.SMEM], scratch=[trio],
+        [((4, members, node_rows, 128), bf16)] * groups
+        + [((members, width, table - node_rows), bf16)],
+        (place, *arrived[::-1], plus, minus, wk, wv), specs=[pltpu.SMEM], scratch=[trio],
     )
 
     planes, rows = count // 4, width // count
@@ -594,7 +598,7 @@
             * len(which),
             (
                 place, *extra, *[loc[g] for g in which], *[halo[g] for g in which],
-                *[part for g in which for part in own_part[2 * g : 2 * g + 2]], mask, xtf, og,
+                *[part for g in which for part in own_part[2 * g : 2 * g + 2]], mask, xt, xtf, og,
             ),
             specs=[pltpu.SMEM] + [pl.ANY] * len(extra),
             scratch=[pltpu.VMEM((members, table - node_rows, 512), f32)] * 3

time: 50.4 us -> 50.4 us (level)
  no operation moved by 1% of the time
where the time goes in v21:
time: 50.4 us; the launch traced here: 50.1 us
  starting transfers between devices  17.6 us (35%)
  waiting for transfers between devices  15.9 us (32%)
  Pallas kernels  15.7 us (31%)
  between operations  0.77 us (2%)
    pallas_call x16, Pallas kernels, call(): pl.pallas_call(kernel, out_shape=[jax.ShapeDtypeStruct(*o) if final else...  15.7 us
    ppermute x4, starting transfers between devices, shifted(): lax.ppermute(shard, 'patch', [(i, (i + by) % count) for i in range(count)])  7.25 us
    ppermute x4, starting transfers between devices, exchange(): return lax.ppermute(sent, 'patch', along_z(count, distance))  4.06 us
    ppermute x4, waiting for transfers between devices, shifted(): lax.ppermute(shard, 'patch', [(i, (i + by) % count) for i in range(count)])  3.76 us
    ppermute x1, waiting for transfers between devices, body(): y_a = lax.ppermute(y_sent, 'patch', flop)  3.75 us
    ppermute x2, waiting for transfers between devices, swap(): later = lax.ppermute(pair[1], 'patch', second)  3.44 us
    ppermute x4, waiting for transfers between devices, exchange(): return lax.ppermute(sent, 'patch', along_z(count, distance))  2.89 us
    ppermute x1, starting transfers between devices, body(): y_b = lax.ppermute(y_sent, 'patch', flop)  2.07 us
  transfers between devices with their start and end apart: 18, of which 11 were waited for; matrix products, arithmetic and copies ran while one was open for 0% of the time, Pallas kernels for 19%

profile of v21, /device:TPU:0, one launch (start us, length us, event | category | flops | bytes accessed | tf_op | source)
XLA Modules:
  0.0 50.1 jit_solution(18291402140901388019)
XLA Ops:
  0.6 1.3 %shard_map.104 = (bf16[2,3,16,512]{3,2,1,0:T(8,128)(2,1)S(1)}, bf16[2,3,16,512]{3,2,1,0:T(8,128)(2,1)S(1)}, bf16[2,1,16,512]{3,2,1,0:T(8,128)(2,1)S(1)}, bf16[2,...) custom-call(s32[1,8,16]{2,1,0:T(8,128)} %send_ref.1, bf16[2,128,512]{2,1,0:T(8,128)(2,1)} %x_hbm.1), custom_call_target="tpu_custom_call" | custom-call | flops 1000000 | bytes 10000 | tf_op jit(solution)/shard_map/pallas_call | solution.py:510
  1.9 3.1 %collective-permute-start = (bf16[2,3,16,512]{3,2,1,0:T(8,128)(2,1)S(1)}, bf16[2,3,16,512]{3,2,1,0:T(8,128)(2,1)S(1)}, u32[]{:S(2)}, u32[]{:S(2)}) collective-permute-start(bf16[2,3,16,512]{3,2,1,0:T(8,128)(2,1)S(1)} %get-tuple-element.74), channel_id=1, source_target_pairs={{0,4},{1,5},{2,6},{3,7},{4,8},{5,9},{6,10},{7,11},{8,12},{9,13},{1... | collective-permute-start | bytes 294920 | tf_op jit(solution)/shard_map/ppermute | solution.py:28
  5.0 2.1 %collective-permute-start.1 = (bf16[2,3,16,512]{3,2,1,0:T(8,128)(2,1)S(1)}, bf16[2,3,16,512]{3,2,1,0:T(8,128)(2,1)S(1)}, u32[]{:S(2)}, u32[]{:S(2)}) collective-permute-start(bf16[2,3,16,512]{3,2,1,0:T(8,128)(2,1)S(1)} %get-tuple-element.75), channel_id=1, source_target_pairs={{0,12},{1,13},{2,14},{3,15},{4,0},{5,1},{6,2},{7,3},{8,4},{9,5},{1... | collective-permute-start | bytes 294920 | tf_op jit(solution)/shard_map/ppermute | solution.py:28
  7.1 2.6 %shard_map.105 = (bf16[8,2,128,128]{3,2,1,0:T(8,128)(2,1)S(1)}, bf16[8,2,128,128]{3,2,1,0:T(8,128)(2,1)S(1)}, bf16[8,2,128,128]{3,2,1,0:T(8,128)(2,1)S(1)}, bf16...) custom-call(bf16[2,1,16,512]{3,2,1,0:T(8,128)(2,1)S(1)} %get-tuple-e, ...), custom_call_target="tpu_custom_call" | custom-call | flops 1000000 | bytes 10000 | tf_op jit(solution)/shard_map/pallas_call | solution.py:510
  9.8 0.8 %collective-permute-done.plus_ref = bf16[2,3,16,512]{3,2,1,0:T(8,128)(2,1)S(1)} collective-permute-done((bf16[2,3,16,512]{3,2,1,0:T(8,128)(2,1)S(1)}, bf16[2,3,16,512]{3,2,1,0:T(8,128)(2,1)S(1)}, u32[]{:S(2)}, u32[]{:S(2)}) %collective-permute-start) | collective-permute-done | bytes 98336 | tf_op jit(solution)/shard_map/ppermute | solution.py:28
  10.5 0.8 %collective-permute-done.1.minus_ref = bf16[2,3,16,512]{3,2,1,0:T(8,128)(2,1)S(1)} collective-permute-done((bf16[2,3,16,512]{3,2,1,0:T(8,128)(2,1)S(1)}, bf16[2,3,16,512]{3,2,1,0:T(8,128)(2,1)S(1)}, u32[]{:S(2)}, u32[]{:S(2)}) %collective-permute-start.1) | collective-permute-done | bytes 98336 | tf_op jit(solution)/shard_map/ppermute | solution.py:28
  11.4 1.7 %collective-permute-start.2 = (bf16[2,3,16,512]{3,2,1,0:T(8,128)(2,1)S(1)}, bf16[2,3,16,512]{3,2,1,0:T(8,128)(2,1)S(1)}, u32[]{:S(2)}, u32[]{:S(2)}) collective-permute-start(bf16[2,3,16,512]{3,2,1,0:T(8,128)(2,1)S(1)} %get-tuple-element.76.after_ref), channel_id=1, source_target_pairs={{0,15},{1,2},{2,1},{3,4},{4,3},{5,6},{6,5},{7,8},{8,7},{9,10},{10,... | collective-permute-start | bytes 294920 | tf_op jit(solution)/shard_map/ppermute | solution.py:43
  13.1 0.0 collective-permute-start.3
  13.1 1.4 %shard_map.108.refs_4_.refs_12_ = f32[256,128]{1,0:T(8,128)S(1)} custom-call(bf16[2,3,16,512]{3,2,1,0:T(8,128)(2,1)S(1)} %get-tuple-element.76.after_ref, s32[128,256]{1,0:T(8,128)S(1)} %get-tuple-element.83.neigh_ref, s32[1,128]{1,0:T(1,128)S(1)} %get-tuple-element.84.count_ref), custom_call_target="tpu_custom_call" | custom-call | flops 1000000 | bytes 10000 | tf_op jit(solution)/shard_map/pallas_call | solution.py:510
  14.6 1.4 %shard_map.109 = (f32[3,2,128,512]{3,2,1,0:T(8,128)S(1)}, f32[2,2,8,512]{3,2,1,0:T(8,128)S(1)}, f32[3,2,128,512]{3,2,1,0:T(8,128)S(1)}, f32[2,2,8,512]{3,2,1,0:T...) custom-call(bf16[8,2,128,128]{3,2,1,0:T(8,128)(2,1)S(1)} %get-tuple-, ...), custom_call_target="tpu_custom_call" | custom-call | flops 1000000 | bytes 10000 | tf_op jit(solution)/shard_map/pallas_call | solution.py:510
  15.9 2.3 %collective-permute-done.2.second_in = bf16[2,3,16,512]{3,2,1,0:T(8,128)(2,1)S(1)} collective-permute-done((bf16[2,3,16,512]{3,2,1,0:T(8,128)(2,1)S(1)}, bf16[2,3,16,512]{3,2,1,0:T(8,128)(2,1)S(1)}, u32[]{:S(2)}, u32[]{:S(2)}) %collective-permute-start.2) | collective-permute-done | bytes 98336 | tf_op jit(solution)/shard_map/ppermute | solution.py:43
  18.2 0.0 collective-permute-done.3.first_in
  18.2 0.5 %shard_map.107 = (bf16[4,2,128,128]{3,2,1,0:T(8,128)(2,1)S(1)}, bf16[4,2,128,128]{3,2,1,0:T(8,128)(2,1)S(1)}, bf16[4,2,128,128]{3,2,1,0:T(8,128)(2,1)S(1)}, bf16...) custom-call(s32[1]{0:T(128)} %bitcast.me_ref, bf16[2,3,16,512]{3,2,1,0:T(8,128)(2,1)S(1)} %collective-permute-done.2.second_in, ...), custom_call_target="tpu_custom_call" | custom-call | flops 1000000 | bytes 10000 | tf_op jit(solution)/shard_map/pallas_call | solution.py:510
  18.8 3.8 %shard_map.112 = (f32[4,32,1536]{2,1,0:T(8,128)S(1)}, f32[4,32,1536]{2,1,0:T(8,128)S(1)}, bf16[4,32,1536]{2,1,0:T(8,128)(2,1)S(1)}, bf16[4,32,1536]{2,1,0:T(8,12...) custom-call(s32[1]{0:T(128)} %bitcast.me_ref, ...), custom_call_target="tpu_custom_call" | custom-call | flops 1000000 | bytes 10000 | tf_op jit(solution)/shard_map/pallas_call | solution.py:510
  22.6 0.1 collective-permute-start.6
  22.7 0.5 collective-permute-start.5
  23.2 1.2 %collective-permute-done.6 = bf16[4,32,1536]{2,1,0:T(8,128)(2,1)S(1)} collective-permute-done((bf16[4,32,1536]{2,1,0:T(8,128)(2,1)S(1)}, bf16[4,32,1536]{2,1,0:T(8,128)(2,1)S(1)}, u32[]{:S(2)}, u32[]{:S(2)}) %collective-permute-start.6) | collective-permute-done | bytes 393248 | tf_op jit(solution)/shard_map/ppermute | solution.py:613
  24.4 0.1 add_convert_fusion
  24.4 0.1 collective-permute-start.7
  24.5 1.5 %shard_map.110 = (f32[4,32,512]{2,1,0:T(8,128)S(1)}, f32[4,32,512]{2,1,0:T(8,128)S(1)}, bf16[4,32,512]{2,1,0:T(8,128)(2,1)S(1)}, bf16[4,32,512]{2,1,0:T(8,128)(2...) custom-call(s32[1]{0:T(128)} %bitcast.me_ref, ...), custom_call_target="tpu_custom_call" | custom-call | flops 1000000 | bytes 10000 | tf_op jit(solution)/shard_map/pallas_call | solution.py:510
  26.1 0.2 collective-permute-start.4
  26.3 0.4 collective-permute-start.11
  26.6 0.8 %collective-permute-done.4.refs_1_ = bf16[4,32,512]{2,1,0:T(8,128)(2,1)S(1)} collective-permute-done((bf16[4,32,512]{2,1,0:T(8,128)(2,1)S(1)}, bf16[4,32,512]{2,1,0:T(8,128)(2,1)S(1)}, u32[]{:S(2)}, u32[]{:S(2)}) %collective-permute-start.4) | collective-permute-done | bytes 131104 | tf_op jit(solution)/shard_map/ppermute | solution.py:613
  27.5 2.1 %collective-permute-start.10 = (bf16[4,32,512]{2,1,0:T(8,128)(2,1)S(1)}, bf16[4,32,512]{2,1,0:T(8,128)(2,1)S(1)}, u32[]{:S(2)}, u32[]{:S(2)}) collective-permute-start(bf16[4,32,512]{2,1,0:T(8,128)(2,1)S(1)} %shard_map.111.refs_0_), channel_id=1, source_target_pairs={{0,2},{1,3},{2,0},{3,1},{4,6},{5,7},{6,4},{7,5},{8,10},{9,11},{10,... | collective-permute-start | bytes 393224 | tf_op jit(solution)/shard_map/ppermute | solution.py:627
  29.6 1.0 %shard_map.113 = (f32[2,128,512]{2,1,0:T(8,128)S(1)}, bf16[2,3,16,512]{3,2,1,0:T(8,128)(2,1)S(1)}, bf16[2,3,16,512]{3,2,1,0:T(8,128)(2,1)S(1)}, bf16[2,1,16,512]...) custom-call(bf16[4,32,512]{2,1,0:T(8,128)(2,1)S(1)} %shard_map.111.refs_0_, ...), custom_call_target="tpu_custom_call" | custom-call | flops 1000000 | bytes 10000 | tf_op jit(solution)/shard_map/pallas_call | solution.py:510
  30.6 0.8 %collective-permute-start.8 = (bf16[2,3,16,512]{3,2,1,0:T(8,128)(2,1)S(1)}, bf16[2,3,16,512]{3,2,1,0:T(8,128)(2,1)S(1)}, u32[]{:S(2)}, u32[]{:S(2)}) collective-permute-start(bf16[2,3,16,512]{3,2,1,0:T(8,128)(2,1)S(1)} %get-tuple-element.122), channel_id=1, source_target_pairs={{0,12},{1,13},{2,14},{3,15},{4,0},{5,1},{6,2},{7,3},{8,4},{9,5},{1... | collective-permute-start | bytes 294920 | tf_op jit(solution)/shard_map/ppermute | solution.py:28
  31.4 0.0 collective-permute-done.5.core_in
  31.4 1.3 %collective-permute-start.9 = (bf16[2,3,16,512]{3,2,1,0:T(8,128)(2,1)S(1)}, bf16[2,3,16,512]{3,2,1,0:T(8,128)(2,1)S(1)}, u32[]{:S(2)}, u32[]{:S(2)}) collective-permute-start(bf16[2,3,16,512]{3,2,1,0:T(8,128)(2,1)S(1)} %get-tuple-element.123), channel_id=1, source_target_pairs={{0,4},{1,5},{2,6},{3,7},{4,8},{5,9},{6,10},{7,11},{8,12},{9,13},{1... | collective-permute-start | bytes 294920 | tf_op jit(solution)/shard_map/ppermute | solution.py:28
  32.7 3.8 %collective-permute-done.7.y_in = bf16[4,32,1536]{2,1,0:T(8,128)(2,1)S(1)} collective-permute-done((bf16[4,32,1536]{2,1,0:T(8,128)(2,1)S(1)}, bf16[4,32,1536]{2,1,0:T(8,128)(2,1)S(1)}, u32[]{:S(2)}, u32[]{:S(2)}) %collective-permute-start.7) | collective-permute-done | bytes 393248 | tf_op jit(solution)/shard_map/ppermute | solution.py:620
  36.5 0.1 shard_map.114
  36.6 0.1 collective-permute-start.14
  36.7 0.0 collective-permute-done.8.plus_ref
  36.7 2.1 %collective-permute-done.9.minus_ref = bf16[2,3,16,512]{3,2,1,0:T(8,128)(2,1)S(1)} collective-permute-done((bf16[2,3,16,512]{3,2,1,0:T(8,128)(2,1)S(1)}, bf16[2,3,16,512]{3,2,1,0:T(8,128)(2,1)S(1)}, u32[]{:S(2)}, u32[]{:S(2)}) %collective-permute-start.9) | collective-permute-done | bytes 98336 | tf_op jit(solution)/shard_map/ppermute | solution.py:28
  38.9 0.1 collective-permute-start.12
  38.9 1.3 %collective-permute-start.13 = (bf16[2,3,16,512]{3,2,1,0:T(8,128)(2,1)S(1)}, bf16[2,3,16,512]{3,2,1,0:T(8,128)(2,1)S(1)}, u32[]{:S(2)}, u32[]{:S(2)}) collective-permute-start(bf16[2,3,16,512]{3,2,1,0:T(8,128)(2,1)S(1)} %get-tuple-element.124.refs_0_), channel_id=1, source_target_pairs={{0,1},{1,0},{2,3},{3,2},{4,5},{5,4},{6,7},{7,6},{8,9},{9,8},{10,11... | collective-permute-start | bytes 294920 | tf_op jit(solution)/shard_map/ppermute | solution.py:44
  40.2 0.0 collective-permute-done.11.refs_4_
  40.2 0.0 collective-permute-done.10.refs_2_
  40.2 0.1 shard_map.116
  40.3 0.1 collective-permute-start.15
  40.4 0.9 %collective-permute-start.17 = (bf16[7,32,128]{2,1,0:T(8,128)(2,1)S(1)}, bf16[7,32,128]{2,1,0:T(8,128)(2,1)S(1)}, u32[]{:S(2)}, u32[]{:S(2)}) collective-permute-start(bf16[7,32,128]{2,1,0:T(8,128)(2,1)S(1)} %get-tuple-element.128.after_ref), channel_id=1, source_target_pairs={{0,4},{1,5},{2,6},{3,7},{4,0},{5,1},{6,2},{7,3},{8,12},{9,13},{10,... | collective-permute-start | bytes 172040 | tf_op jit(solution)/shard_map/ppermute | solution.py:637
  41.3 0.5 %collective-permute-done.14.in_a = bf16[18,32,128]{2,1,0:T(8,128)(2,1)S(1)} collective-permute-done((bf16[18,32,128]{2,1,0:T(8,128)(2,1)S(1)}, bf16[18,32,128]{2,1,0:T(8,128)(2,1)S(1)}, u32[]{:S(2)}, u32[]{:S(2)}) %collective-permute-start.14) | collective-permute-done | bytes 147488 | tf_op jit(solution)/shard_map/ppermute | solution.py:637
  41.8 3.0 %collective-permute-start.16 = (bf16[16,32,128]{2,1,0:T(8,128)(2,1)S(1)}, bf16[16,32,128]{2,1,0:T(8,128)(2,1)S(1)}, u32[]{:S(2)}, u32[]{:S(2)}) collective-permute-start(bf16[16,32,128]{2,1,0:T(8,128)(2,1)S(1)} %get-tuple-element.135), channel_id=1, source_target_pairs={{0,12},{1,13},{2,14},{3,15},{4,8},{5,9},{6,10},{7,11},{8,4},{9,5},... | collective-permute-start | bytes 393224 | tf_op jit(solution)/shard_map/ppermute | solution.py:637
  44.8 1.1 %collective-permute-done.12.second_in = bf16[2,3,16,512]{3,2,1,0:T(8,128)(2,1)S(1)} collective-permute-done((bf16[2,3,16,512]{3,2,1,0:T(8,128)(2,1)S(1)}, bf16[2,3,16,512]{3,2,1,0:T(8,128)(2,1)S(1)}, u32[]{:S(2)}, u32[]{:S(2)}) %collective-permute-start.12) | collective-permute-done | bytes 98336 | tf_op jit(solution)/shard_map/ppermute | solution.py:43
  46.0 1.0 %shard_map.117.after_ref = bf16[2,128,512]{2,1,0:T(8,128)(2,1)} custom-call(s32[1]{0:T(128)} %bitcast.me_ref, bf16[7,32,128]{2,1,0:T(8,128)(2,1)S(1)} %get-tuple-element.128.after_ref, bf16[2,3,16,512]{3,2,1,0:T(8,128)(2,1)S(1)} %collective-permute-done.12.second_in, bf16[2,3,16,512]{3,2,1,0:T(8,128)(2,1)S(1)} %collective-permute-done.13.first_in, ...), custom_call_target="tpu_custom_call" | custom-call | flops 20000000000 | bytes 10000 | tf_op jit(solution)/shard_map/pallas_call | solution.py:510
  47.0 0.5 %collective-permute-done.15.refs_0_ = bf16[7,32,128]{2,1,0:T(8,128)(2,1)S(1)} collective-permute-done((bf16[7,32,128]{2,1,0:T(8,128)(2,1)S(1)}, bf16[7,32,128]{2,1,0:T(8,128)(2,1)S(1)}, u32[]{:S(2)}, u32[]{:S(2)}) %collective-permute-start.15) | collective-permute-done | bytes 57376 | tf_op jit(solution)/shard_map/ppermute | solution.py:637
  47.5 0.0 collective-permute-done.17.refs_2_
  47.5 1.8 %collective-permute-done.16.refs_1_ = bf16[16,32,128]{2,1,0:T(8,128)(2,1)S(1)} collective-permute-done((bf16[16,32,128]{2,1,0:T(8,128)(2,1)S(1)}, bf16[16,32,128]{2,1,0:T(8,128)(2,1)S(1)}, u32[]{:S(2)}, u32[]{:S(2)}) %collective-permute-start.16) | collective-permute-done | bytes 131104 | tf_op jit(solution)/shard_map/ppermute | solution.py:637
  49.3 0.7 %shard_map.119 = f32[32,2048]{1,0:T(8,128)} custom-call(bf16[2,128,512]{2,1,0:T(8,128)(2,1)} %shard_map.117.after_ref, f32[32,1152]{1,0:T(8,128)S(1)} %get-tuple-element.132.own_a, f32[32,896]{1,0:T(8,128)S(1)} %get-tuple-element.133.own_b, bf16[7,32,128]{2,1,0:T(8,128)(2,1)S(1)} %collective-permute-done.15.refs_0_, ...), custom_call_target="tpu_custom_call" | custom-call | flops 1000000 | bytes 10000 | tf_op jit(solution)/shard_map/pallas_call | solution.py:510
  (7 shorter events, 0.1 us)
Async XLA Ops:
  1.9 8.6 %collective-permute-start = (bf16[2,3,16,512]{3,2,1,0:T(8,128)(2,1)S(1)}, bf16[2,3,16,512]{3,2,1,0:T(8,128)(2,1)S(1)}, u32[]{:S(2)}, u32[]{:S(2)}) collective-permute-start(bf16[2,3,16,512]{3,2,1,0:T(8,128)(2,1)S(1)} %get-tuple-element.74), channel_id=1, source_target_pairs={{0,4},{1,5},{2,6},{3,7},{4,8},{5,9},{6,10},{7,11},{8,12},{9,13},{1... | collective-permute-start | bytes 294920 | tf_op jit(solution)/shard_map/ppermute | solution.py:28
  5.0 6.4 %collective-permute-start.1 = (bf16[2,3,16,512]{3,2,1,0:T(8,128)(2,1)S(1)}, bf16[2,3,16,512]{3,2,1,0:T(8,128)(2,1)S(1)}, u32[]{:S(2)}, u32[]{:S(2)}) collective-permute-start(bf16[2,3,16,512]{3,2,1,0:T(8,128)(2,1)S(1)} %get-tuple-element.75), channel_id=1, source_target_pairs={{0,12},{1,13},{2,14},{3,15},{4,0},{5,1},{6,2},{7,3},{8,4},{9,5},{1... | collective-permute-start | bytes 294920 | tf_op jit(solution)/shard_map/ppermute | solution.py:28
  11.4 6.8 %collective-permute-start.2 = (bf16[2,3,16,512]{3,2,1,0:T(8,128)(2,1)S(1)}, bf16[2,3,16,512]{3,2,1,0:T(8,128)(2,1)S(1)}, u32[]{:S(2)}, u32[]{:S(2)}) collective-permute-start(bf16[2,3,16,512]{3,2,1,0:T(8,128)(2,1)S(1)} %get-tuple-element.76.after_ref), channel_id=1, source_target_pairs={{0,15},{1,2},{2,1},{3,4},{4,3},{5,6},{6,5},{7,8},{8,7},{9,10},{10,... | collective-permute-start | bytes 294920 | tf_op jit(solution)/shard_map/ppermute | solution.py:43
  13.1 5.1 %collective-permute-start.3 = (bf16[2,3,16,512]{3,2,1,0:T(8,128)(2,1)S(1)}, bf16[2,3,16,512]{3,2,1,0:T(8,128)(2,1)S(1)}, u32[]{:S(2)}, u32[]{:S(2)}) collective-permute-start(bf16[2,3,16,512]{3,2,1,0:T(8,128)(2,1)S(1)} %get-tuple-element.77), channel_id=1, source_target_pairs={{0,1},{1,0},{2,3},{3,2},{4,5},{5,4},{6,7},{7,6},{8,9},{9,8},{10,11... | collective-permute-start | bytes 294920 | tf_op jit(solution)/shard_map/ppermute | solution.py:44
  22.6 1.8 %collective-permute-start.6 = (bf16[4,32,1536]{2,1,0:T(8,128)(2,1)S(1)}, bf16[4,32,1536]{2,1,0:T(8,128)(2,1)S(1)}, u32[]{:S(2)}, u32[]{:S(2)}) collective-permute-start(bf16[4,32,1536]{2,1,0:T(8,128)(2,1)S(1)} %get-tuple-element.118), channel_id=1, source_target_pairs={{0,1},{1,0},{2,3},{3,2},{4,5},{5,4},{6,7},{7,6},{8,9},{9,8},{10,11... | collective-permute-start | bytes 1179656 | tf_op jit(solution)/shard_map/ppermute | solution.py:613
  22.7 8.7 %collective-permute-start.5 = (bf16[4,32,1536]{2,1,0:T(8,128)(2,1)S(1)}, bf16[4,32,1536]{2,1,0:T(8,128)(2,1)S(1)}, u32[]{:S(2)}, u32[]{:S(2)}) collective-permute-start(bf16[4,32,1536]{2,1,0:T(8,128)(2,1)S(1)} %get-tuple-element.116), channel_id=1, source_target_pairs={{0,1},{1,0},{2,3},{3,2},{4,5},{5,4},{6,7},{7,6},{8,9},{9,8},{10,11... | collective-permute-start | bytes 1179656 | tf_op jit(solution)/shard_map/ppermute | solution.py:613
  24.4 12.0 %collective-permute-start.7 = (bf16[4,32,1536]{2,1,0:T(8,128)(2,1)S(1)}, bf16[4,32,1536]{2,1,0:T(8,128)(2,1)S(1)}, u32[]{:S(2)}, u32[]{:S(2)}) collective-permute-start(bf16[4,32,1536]{2,1,0:T(8,128)(2,1)S(1)} %add_convert_fusion), channel_id=1, source_target_pairs={{0,2},{1,3},{2,0},{3,1},{4,6},{5,7},{6,4},{7,5},{8,10},{9,11},{10,... | collective-permute-start | bytes 1179656 | tf_op jit(solution)/shard_map/ppermute | solution.py:620
  26.1 1.4 %collective-permute-start.4 = (bf16[4,32,512]{2,1,0:T(8,128)(2,1)S(1)}, bf16[4,32,512]{2,1,0:T(8,128)(2,1)S(1)}, u32[]{:S(2)}, u32[]{:S(2)}) collective-permute-start(bf16[4,32,512]{2,1,0:T(8,128)(2,1)S(1)} %get-tuple-element.91), channel_id=1, source_target_pairs={{0,1},{1,0},{2,3},{3,2},{4,5},{5,4},{6,7},{7,6},{8,9},{9,8},{10,11... | collective-permute-start | bytes 393224 | tf_op jit(solution)/shard_map/ppermute | solution.py:613
  26.3 13.9 %collective-permute-start.11 = (bf16[4,32,512]{2,1,0:T(8,128)(2,1)S(1)}, bf16[4,32,512]{2,1,0:T(8,128)(2,1)S(1)}, u32[]{:S(2)}, u32[]{:S(2)}) collective-permute-start(bf16[4,32,512]{2,1,0:T(8,128)(2,1)S(1)} %get-tuple-element.127), channel_id=1, source_target_pairs={{0,1},{1,0},{2,3},{3,2},{4,5},{5,4},{6,7},{7,6},{8,9},{9,8},{10,11... | collective-permute-start | bytes 393224 | tf_op jit(solution)/shard_map/ppermute | solution.py:613
  27.5 12.7 %collective-permute-start.10 = (bf16[4,32,512]{2,1,0:T(8,128)(2,1)S(1)}, bf16[4,32,512]{2,1,0:T(8,128)(2,1)S(1)}, u32[]{:S(2)}, u32[]{:S(2)}) collective-permute-start(bf16[4,32,512]{2,1,0:T(8,128)(2,1)S(1)} %shard_map.111.refs_0_), channel_id=1, source_target_pairs={{0,2},{1,3},{2,0},{3,1},{4,6},{5,7},{6,4},{7,5},{8,10},{9,11},{10,... | collective-permute-start | bytes 393224 | tf_op jit(solution)/shard_map/ppermute | solution.py:627
  30.6 6.1 %collective-permute-start.8 = (bf16[2,3,16,512]{3,2,1,0:T(8,128)(2,1)S(1)}, bf16[2,3,16,512]{3,2,1,0:T(8,128)(2,1)S(1)}, u32[]{:S(2)}, u32[]{:S(2)}) collective-permute-start(bf16[2,3,16,512]{3,2,1,0:T(8,128)(2,1)S(1)} %get-tuple-element.122), channel_id=1, source_target_pairs={{0,12},{1,13},{2,14},{3,15},{4,0},{5,1},{6,2},{7,3},{8,4},{9,5},{1... | collective-permute-start | bytes 294920 | tf_op jit(solution)/shard_map/ppermute | solution.py:28
  31.4 7.4 %collective-permute-start.9 = (bf16[2,3,16,512]{3,2,1,0:T(8,128)(2,1)S(1)}, bf16[2,3,16,512]{3,2,1,0:T(8,128)(2,1)S(1)}, u32[]{:S(2)}, u32[]{:S(2)}) collective-permute-start(bf16[2,3,16,512]{3,2,1,0:T(8,128)(2,1)S(1)} %get-tuple-element.123), channel_id=1, source_target_pairs={{0,4},{1,5},{2,6},{3,7},{4,8},{5,9},{6,10},{7,11},{8,12},{9,13},{1... | collective-permute-start | bytes 294920 | tf_op jit(solution)/shard_map/ppermute | solution.py:28
  36.6 5.2 %collective-permute-start.14 = (bf16[18,32,128]{2,1,0:T(8,128)(2,1)S(1)}, bf16[18,32,128]{2,1,0:T(8,128)(2,1)S(1)}, u32[]{:S(2)}, u32[]{:S(2)}) collective-permute-start(bf16[18,32,128]{2,1,0:T(8,128)(2,1)S(1)} %get-tuple-element.119.after_ref), channel_id=1, source_target_pairs={{0,4},{1,5},{2,6},{3,7},{4,0},{5,1},{6,2},{7,3},{8,12},{9,13},{10,... | collective-permute-start | bytes 442376 | tf_op jit(solution)/shard_map/ppermute | solution.py:637
  38.9 7.1 %collective-permute-start.12 = (bf16[2,3,16,512]{3,2,1,0:T(8,128)(2,1)S(1)}, bf16[2,3,16,512]{3,2,1,0:T(8,128)(2,1)S(1)}, u32[]{:S(2)}, u32[]{:S(2)}) collective-permute-start(bf16[2,3,16,512]{3,2,1,0:T(8,128)(2,1)S(1)} %get-tuple-element.129), channel_id=1, source_target_pairs={{0,15},{1,2},{2,1},{3,4},{4,3},{5,6},{6,5},{7,8},{8,7},{9,10},{10,... | collective-permute-start | bytes 294920 | tf_op jit(solution)/shard_map/ppermute | solution.py:43
  38.9 7.1 %collective-permute-start.13 = (bf16[2,3,16,512]{3,2,1,0:T(8,128)(2,1)S(1)}, bf16[2,3,16,512]{3,2,1,0:T(8,128)(2,1)S(1)}, u32[]{:S(2)}, u32[]{:S(2)}) collective-permute-start(bf16[2,3,16,512]{3,2,1,0:T(8,128)(2,1)S(1)} %get-tuple-element.124.refs_0_), channel_id=1, source_target_pairs={{0,1},{1,0},{2,3},{3,2},{4,5},{5,4},{6,7},{7,6},{8,9},{9,8},{10,11... | collective-permute-start | bytes 294920 | tf_op jit(solution)/shard_map/ppermute | solution.py:44
  40.3 7.2 %collective-permute-start.15 = (bf16[7,32,128]{2,1,0:T(8,128)(2,1)S(1)}, bf16[7,32,128]{2,1,0:T(8,128)(2,1)S(1)}, u32[]{:S(2)}, u32[]{:S(2)}) collective-permute-start(bf16[7,32,128]{2,1,0:T(8,128)(2,1)S(1)} %get-tuple-element.134), channel_id=1, source_target_pairs={{0,8},{1,9},{2,10},{3,11},{4,12},{5,13},{6,14},{7,15},{8,0},{9,1},... | collective-permute-start | bytes 172040 | tf_op jit(solution)/shard_map/ppermute | solution.py:637
  40.4 7.2 %collective-permute-start.17 = (bf16[7,32,128]{2,1,0:T(8,128)(2,1)S(1)}, bf16[7,32,128]{2,1,0:T(8,128)(2,1)S(1)}, u32[]{:S(2)}, u32[]{:S(2)}) collective-permute-start(bf16[7,32,128]{2,1,0:T(8,128)(2,1)S(1)} %get-tuple-element.128.after_ref), channel_id=1, source_target_pairs={{0,4},{1,5},{2,6},{3,7},{4,0},{5,1},{6,2},{7,3},{8,12},{9,13},{10,... | collective-permute-start | bytes 172040 | tf_op jit(solution)/shard_map/ppermute | solution.py:637
  41.8 4.2 %copy-start = (s32[1,8,16]{2,1,0:T(8,128)S(1)}, s32[1,8,16]{2,1,0:T(8,128)}, u32[]{:S(2)}) copy-start(s32[1,8,16]{2,1,0:T(8,128)} %send_ref.1) | copy-start | bytes 1540
  41.8 7.5 %collective-permute-start.16 = (bf16[16,32,128]{2,1,0:T(8,128)(2,1)S(1)}, bf16[16,32,128]{2,1,0:T(8,128)(2,1)S(1)}, u32[]{:S(2)}, u32[]{:S(2)}) collective-permute-start(bf16[16,32,128]{2,1,0:T(8,128)(2,1)S(1)} %get-tuple-element.135), channel_id=1, source_target_pairs={{0,12},{1,13},{2,14},{3,15},{4,8},{5,9},{6,10},{7,11},{8,4},{9,5},... | collective-permute-start | bytes 393224 | tf_op jit(solution)/shard_map/ppermute | solution.py:637
